TPU v7x, 32 devices: a whole 2x2x4 slice. The times are simulated.
32 devices in a mesh: grp: 2 (over y), frm: 4 (over z), row: 2 (over x), sub: 2 (over core).
Axes of the slice: x: 2, y: 2, z: 4, core: 2. Of those that a mesh axis runs over, the one named last changes fastest.
Arguments:
- signal: bfloat16 [64, 65536], P('row', ('grp', 'frm', 'sub')), parts along dimension 1, may hold values from -6 to 6
- w_start: float32 [2560, 32], P('row'), may hold values from 0.02 to 0.4
- h_start: float32 [32, 65536], P(None, ('grp', 'frm', 'sub')), parts along dimension 1, may hold values from 0.02 to 0.4
Outputs:
- synergies: float32 [5120, 32], P(('grp', 'row')), parts along dimension 0
- activations: float32 [32, 65536], P(None, ('grp', 'frm', 'sub')), parts along dimension 1
There are 2 independent parts, one for each index of `grp`. A program takes and returns all parts, laid end to end along the dimension named above; an argument that names none is the same for every part. Nothing has to cross between parts.
All inputs are finite; a program needn't handle non-finite values.
Results may differ from a plain program's by a relative error of at most 0.0019.
Values may be sent and summed in bfloat16 or wider, within the bound.
No kernel may reach another device: no remote copies, remote signals or barrier semaphores. Data moves between devices by JAX's collectives and lax.ppermute only.
A program may use at most 128 MiB of HBM per device.

v0:
```python
import functools
import math

import jax
import jax.numpy as jnp
import ml_dtypes
import numpy as np
from jax import lax
from jax.experimental import pallas as pl
from jax.experimental.pallas import tpu as pltpu
from jax.sharding import PartitionSpec as P

NF = 40
TAPS = 128
HALF = TAPS // 2
GROUP = 4
GROUPS = NF // GROUP
F32 = jnp.float32
BF16 = jnp.bfloat16
HIGH = lax.Precision.HIGHEST
NT = (((1,), (1,)), ((), ()))
VMEM_LIMIT = 56 * 1024 * 1024


def wavelets():
    f = np.float32
    level = np.arange(NF, dtype=f) / f(NF - 1)
    freq = f(2.0) * np.power(f(12.0), level)
    sigma = f(7.0) / (f(2.0 * math.pi) * freq)
    times = (np.arange(TAPS, dtype=f) - f(HALF)) / f(50.0)
    env = np.exp(-(times[None, :] ** 2) / (f(2.0) * sigma[:, None] ** 2))
    scale = f(1.0) / np.sqrt(np.sum(env * env, axis=1))
    env = env * scale[:, None]
    phase = f(2.0 * math.pi) * freq[:, None] * times[None, :]
    return np.stack([env * np.cos(phase), env * np.sin(phase)]).astype(ml_dtypes.bfloat16)


def toeplitz():
    kernel = wavelets()
    table = np.zeros((NF, 2 * TAPS, 2 * TAPS), ml_dtypes.bfloat16)
    for at in range(TAPS):
        for part in range(2):
            table[:, at : at + TAPS, part * TAPS + at] = kernel[part]
    return table


def split_two(value):
    top = value.astype(BF16)
    return top, (value - top.astype(F32)).astype(BF16)


def joined(message, at, rank):
    return message[:, at : at + rank].astype(F32) + message[:, at + rank : at + 2 * rank].astype(F32)


def pack(out_ref, main, gram):
    rank, size = main.shape
    top, rest = split_two(gram)
    out_ref[:, :size] = main.astype(BF16)
    out_ref[:, size : size + rank] = top
    out_ref[:, size + rank : size + 2 * rank] = rest


def prepare_kernel(w_ref, msg_ref, gram_ref):
    w = w_ref[...]
    gram = lax.dot_general(w, w, NT, precision=HIGH, preferred_element_type=F32)
    gram_ref[...] = gram
    pack(msg_ref, w, gram)


def group_rows(s_scr, g, pair, rows, cl):
    halves = []
    for blk in (2 * pair, 2 * pair + 1):
        parts = [
            s_scr[pl.ds(g * GROUP, GROUP), blk, x * cl : (x + 1) * cl, :].reshape(GROUP * cl, TAPS)
            for x in range(rows)
        ]
        halves.append(jnp.concatenate(parts, axis=0))
    return jnp.concatenate(halves, axis=1)


def add_crossed(s_scr, wg, num_scr, g, pairs, rows, cl):
    for pair in range(pairs):
        cols = slice(2 * TAPS * pair, 2 * TAPS * (pair + 1))
        num_scr[:, cols] += jnp.dot(wg, group_rows(s_scr, g, pair, rows, cl), preferred_element_type=F32)


def finish_update(old, gram, num_scr, s_scr, p_scr, h_out, own_ref, own_gram_ref, msg_refs, rows, subs, cl):
    rank, frames = old.shape
    pairs = frames // (2 * TAPS)
    per_sub = GROUPS // subs
    new = old * num_scr[...] / jnp.dot(gram, old, precision=HIGH, preferred_element_type=F32)
    h_out[...] = new
    low = new.astype(BF16)
    h_gram = lax.dot_general(new, new, NT, precision=HIGH, preferred_element_type=F32)
    wide = GROUP * cl
    for g in range(GROUPS):
        acc = jnp.zeros((rank, rows * wide), F32)
        for pair in range(pairs):
            cols = slice(2 * TAPS * pair, 2 * TAPS * (pair + 1))
            acc = acc + lax.dot_general(
                low[:, cols], group_rows(s_scr, g, pair, rows, cl), NT, preferred_element_type=F32
            )
        at = (g % per_sub) * wide
        for x in range(rows):
            p_scr[x, g // per_sub, :, at : at + wide] = acc[:, x * wide : (x + 1) * wide]
    x_me, c_me = lax.axis_index("row"), lax.axis_index("sub")
    own_ref[...] = p_scr[x_me, c_me]
    own_gram_ref[...] = h_gram
    at = 0
    for dx in range(rows):
        for dc in range(subs):
            if dx or dc:
                pack(msg_refs[at], p_scr[lax.rem(x_me + dx, rows), lax.rem(c_me + dc, subs)], h_gram)
                at += 1


def first_kernel(rows, subs, cl, blocks, *refs):
    refs = list(refs)
    sig_refs = [refs.pop(0) for _ in range(rows)]
    halo_refs = [refs.pop(0) for _ in range(rows)]
    w_refs = [refs.pop(0) for _ in range(rows)]
    gram_ref, h_ref, tab_ref = refs.pop(0), refs.pop(0), refs.pop(0)
    s_hbm, h_out, own_ref, own_gram_ref = (refs.pop(0) for _ in range(4))
    msg_refs = [refs.pop(0) for _ in range(rows * subs - 1)]
    xp_scr, x_scr, w_scr, s_scr, num_scr, p_scr, sems = refs
    rank = h_ref.shape[0]
    frames = blocks * TAPS
    wide = GROUP * cl
    g = pl.program_id(0)
    x_me = lax.axis_index("row")

    @pl.when(g == 0)
    def _():
        for shift in range(rows):
            owner = lax.rem(x_me + rows - shift, rows)
            xp_scr[owner] = sig_refs[shift][...]
            for at in range(GROUPS):
                w_scr[at, owner] = w_refs[shift][:, at * wide : (at + 1) * wide]

        @pl.when(x_me == 0)
        def _():
            for at in range(rows):
                xp_scr[at, :, :HALF] = halo_refs[at][...]

        @pl.when(x_me == rows - 1)
        def _():
            for at in range(rows):
                xp_scr[rows - 1 - at, :, frames + HALF :] = halo_refs[at][...]

        for blk in range(blocks):
            for x in range(rows):
                x_scr[blk, x * cl : (x + 1) * cl, :] = xp_scr[x, :, blk * TAPS : (blk + 2) * TAPS]
        num_scr[...] = jnp.zeros_like(num_scr)

    for at in range(GROUP):
        co = jnp.dot(x_scr[...].reshape(blocks * rows * cl, 2 * TAPS), tab_ref[at], preferred_element_type=F32)
        power = co[:, :TAPS] * co[:, :TAPS] + co[:, TAPS:] * co[:, TAPS:]
        s_scr[g * GROUP + at] = power.astype(BF16).reshape(blocks, rows * cl, TAPS)

    def copy_out(at):
        span = pl.ds(at * GROUP, GROUP)
        return pltpu.make_async_copy(s_scr.at[span], s_hbm.at[span], sems.at[at])

    copy_out(g).start()
    wg = jnp.concatenate([w_scr[g, x] for x in range(rows)], axis=1)
    add_crossed(s_scr, wg, num_scr, g, blocks // 2, rows, cl)

    @pl.when(g == GROUPS - 1)
    def _():
        gram = gram_ref[...]
        for shift in range(1, rows):
            gram = gram + joined(w_refs[shift], NF * cl, rank)
        old = h_ref[:, pl.ds(pl.multiple_of(x_me * frames, TAPS), frames)]
        finish_update(old, gram, num_scr, s_scr, p_scr, h_out, own_ref, own_gram_ref, msg_refs, rows, subs, cl)
        for at in range(GROUPS):
            copy_out(at).wait()


def later_kernel(rows, subs, cl, blocks, *refs):
    refs = list(refs)
    w_refs = [refs.pop(0) for _ in range(rows * subs)]
    h_ref, s_hbm = refs.pop(0), refs.pop(0)
    h_out, own_ref, own_gram_ref = (refs.pop(0) for _ in range(3))
    msg_refs = [refs.pop(0) for _ in range(rows * subs - 1)]
    w_scr, s_scr, num_scr, p_scr, sems = refs
    rank = h_ref.shape[0]
    per_sub = GROUPS // subs
    wide = GROUP * cl
    x_me, c_me = lax.axis_index("row"), lax.axis_index("sub")

    def copy_in(at):
        span = pl.ds(at * GROUP, GROUP)
        return pltpu.make_async_copy(s_hbm.at[span], s_scr.at[span], sems.at[at])

    for at in range(GROUPS):
        copy_in(at).start()
    gram = jnp.zeros((rank, rank), F32)
    at = 0
    for dx in range(rows):
        for dc in range(subs):
            x_of, c_of = lax.rem(x_me + rows - dx, rows), lax.rem(c_me + subs - dc, subs)
            for part in range(per_sub):
                w_scr[c_of, part, x_of] = w_refs[at][:, part * wide : (part + 1) * wide]
            gram = gram + joined(w_refs[at], per_sub * wide, rank)
            at += 1
    num_scr[...] = jnp.zeros_like(num_scr)
    for g in range(GROUPS):
        copy_in(g).wait()
        wg = jnp.concatenate([w_scr[g // per_sub, g % per_sub, x] for x in range(rows)], axis=1)
        add_crossed(s_scr, wg, num_scr, g, blocks // 2, rows, cl)
    finish_update(h_ref[...], gram, num_scr, s_scr, p_scr, h_out, own_ref, own_gram_ref, msg_refs, rows, subs, cl)


def partial_kernel(*refs):
    own_ref, own_gram_ref, *msg_refs, out_ref = refs
    rank, size = own_ref.shape
    total, gram = own_ref[...], own_gram_ref[...]
    for ref in msg_refs:
        total = total + ref[:, :size].astype(F32)
        gram = gram + joined(ref, size, rank)
    pack(out_ref, total, gram)


def update_kernel(count, w_ref, *refs):
    msg_refs, (new_ref, out_ref, scr) = refs[:count], refs[count:]
    rank, size = new_ref.shape
    z_me = lax.axis_index("frm")
    for shift in range(count):
        scr[lax.rem(z_me + count - shift, count)] = msg_refs[shift][...]
    total, gram = scr[0, :, :size].astype(F32), joined(scr[0], size, rank)
    for at in range(1, count):
        total = total + scr[at, :, :size].astype(F32)
        gram = gram + joined(scr[at], size, rank)
    w = w_ref[lax.axis_index("sub")] if len(w_ref.shape) == 3 else w_ref[...]
    new = w * total / jnp.dot(gram, w, precision=HIGH, preferred_element_type=F32)
    new_ref[...] = new
    pack(out_ref, new, lax.dot_general(new, new, NT, precision=HIGH, preferred_element_type=F32))


def call(kernel, args, outs, scratch=(), grid=None, in_specs=None, out_specs=None):
    whole = pl.BlockSpec(memory_space=pltpu.VMEM)
    extra = {} if grid is None else {"grid": grid}
    return pl.pallas_call(
        kernel,
        out_shape=[jax.ShapeDtypeStruct(*out) for out in outs],
        in_specs=in_specs or [whole] * len(args),
        out_specs=out_specs or [whole] * len(outs),
        scratch_shapes=list(scratch),
        compiler_params=pltpu.CompilerParams(vmem_limit_bytes=VMEM_LIMIT),
        **extra,
    )(*args)


def shards(signal, w_start, h_start):
    rows, subs, frms = (lax.axis_size(axis) for axis in ("row", "sub", "frm"))
    x_me = lax.axis_index("row")
    cl, window = signal.shape
    rank = w_start.shape[1]
    frames = window // rows
    blocks = frames // TAPS
    chans = rows * cl
    size = NF * cl // subs
    line = frms * subs

    def row_shift(value, shift):
        return lax.ppermute(value, "row", [(i, (i + shift) % rows) for i in range(rows)])

    def quad_shift(value, dx, dc):
        pairs = [
            (x * subs + c, ((x + dx) % rows) * subs + (c + dc) % subs) for x in range(rows) for c in range(subs)
        ]
        return lax.ppermute(value, ("row", "sub"), pairs)

    def place(x, at):
        return (at // subs * rows + x) * subs + at % subs

    others = [(dx, dc) for dx in range(rows) for dc in range(subs) if dx or dc]

    padded = jnp.pad(signal, ((0, 0), (HALF, HALF)))

    def part_for(target):
        return lax.dynamic_slice_in_dim(padded, target * frames, frames + TAPS, 1)

    sig = [part_for(x_me)]
    for shift in range(1, rows):
        sig.append(row_shift(part_for((x_me + shift) % rows), shift))
    tail, head = signal[:, window - HALF :], signal[:, :HALF]
    halos = []
    for at in range(rows):
        to_next = [(place(at, i), place(0, i + 1)) for i in range(line - 1)]
        to_prev = [(place(rows - 1 - at, i + 1), place(rows - 1, i)) for i in range(line - 1)]
        halos.append(lax.ppermute(jnp.where(x_me == at, tail, head), ("frm", "row", "sub"), to_next + to_prev))

    w_cols = w_start.reshape(cl, NF, rank).transpose(2, 1, 0).reshape(rank, NF * cl)
    w_msg, w_gram = call(
        prepare_kernel, [w_cols], [((rank, NF * cl + 2 * rank), BF16), ((rank, rank), F32)]
    )
    w_msgs = [w_msg] + [row_shift(w_msg, shift) for shift in range(1, rows)]
    w_own = w_cols.reshape(rank, subs, size).transpose(1, 0, 2)

    msg = ((rank, size + 2 * rank), BF16)
    tail_outs = [((rank, frames), F32), ((rank, size), F32), ((rank, rank), F32)] + [msg] * len(others)
    s_shape = (NF, blocks, chans, TAPS)

    def fixed(shape):
        return pl.BlockSpec(shape, lambda g: (0,) * len(shape))

    table = jnp.asarray(toeplitz())
    args = sig + halos + w_msgs + [w_gram, h_start]
    spec = [fixed(a.shape) for a in args] + [pl.BlockSpec((GROUP, 2 * TAPS, 2 * TAPS), lambda g: (g, 0, 0))]
    tail_scratch = [
        pltpu.VMEM(s_shape, BF16),
        pltpu.VMEM((rank, frames), F32),
        pltpu.VMEM((rows, subs, rank, size), F32),
        pltpu.SemaphoreType.DMA((GROUPS,)),
    ]
    spectra, activations, own, own_gram, *msgs = call(
        functools.partial(first_kernel, rows, subs, cl, blocks),
        args + [table],
        [(s_shape, BF16)] + tail_outs,
        [
            pltpu.VMEM((rows, cl, frames + TAPS), BF16),
            pltpu.VMEM((blocks, chans, 2 * TAPS), BF16),
            pltpu.VMEM((GROUPS, rows, rank, GROUP * cl), BF16),
        ]
        + tail_scratch,
        (GROUPS,),
        spec,
        [pl.BlockSpec(memory_space=pl.ANY)] + [fixed(out[0]) for out in tail_outs],
    )

    def reduced(own, own_gram, msgs, w):
        got = [quad_shift(m, dx, dc) for m, (dx, dc) in zip(msgs, others)]
        (part,) = call(partial_kernel, [own, own_gram] + got, [msg])
        parts = [part] + [
            lax.ppermute(part, "frm", [(i, (i + shift) % frms) for i in range(frms)]) for shift in range(1, frms)
        ]
        return call(
            functools.partial(update_kernel, frms),
            [w] + parts,
            [((rank, size), F32), msg],
            [pltpu.VMEM((frms,) + msg[0], BF16)],
        )

    w_piece, w_msg = reduced(own, own_gram, msgs, w_own)
    w_msgs = [w_msg] + [quad_shift(w_msg, dx, dc) for dx, dc in others]
    whole = pl.BlockSpec(memory_space=pltpu.VMEM)
    activations, own, own_gram, *msgs = call(
        functools.partial(later_kernel, rows, subs, cl, blocks),
        w_msgs + [activations, spectra],
        tail_outs,
        [pltpu.VMEM((subs, GROUPS // subs, rows, rank, GROUP * cl), BF16)] + tail_scratch,
        in_specs=[whole] * (len(w_msgs) + 1) + [pl.BlockSpec(memory_space=pl.ANY)],
    )
    w_piece, _ = reduced(own, own_gram, msgs, w_piece)

    c_me = lax.axis_index("sub")
    full = jnp.zeros((subs, rank, size), F32)
    for dc in range(subs):
        got = w_piece if dc == 0 else lax.ppermute(w_piece, "sub", [(i, (i + dc) % subs) for i in range(subs)])
        full = lax.dynamic_update_slice(full, got[None], ((c_me + subs - dc) % subs, 0, 0))
    synergies = full.reshape(subs, rank, NF // subs, cl).transpose(3, 0, 2, 1).reshape(NF * cl, rank)

    wide = jnp.zeros((rank, window), F32)
    for shift in range(rows):
        got = activations if shift == 0 else row_shift(activations, shift)
        wide = lax.dynamic_update_slice(wide, got, (0, (x_me + rows - shift) % rows * frames))
    return (synergies, wide)


def solution(mesh):
    placed = (P("row", ("grp", "frm", "sub")), P("row", None), P(None, ("grp", "frm", "sub")))
    return jax.shard_map(
        shards,
        mesh=mesh,
        in_specs=placed,
        out_specs=(P(("grp", "row"), None), P(None, ("grp", "frm", "sub"))),
        check_vma=False,
    )
```

profile of v0, /device:TPU:0, one launch (start us, length us, event | category | flops | bytes accessed | tf_op | source)
XLA Modules:
  0.0 95.6 jit_solution(753421236121553292)
XLA Ops:
  0.6 1.8 %pad_dynamic-slice_fusion = (bf16[32,2176]{1,0:T(8,128)(2,1)S(1)}, bf16[32,2176]{1,0:T(8,128)(2,1)}) fusion(s32[]{:T(128)S(6)} %select_n.55, bf16[32,4096]{1,0:T(8,128)(2,1)} %param.4, s32[]{:T(128)S(6)} %select_n.53), kind=kLoop, calls=%fused_computation | loop fusion | bytes 540680 | tf_op jit(solution)/shard_map/dynamic_slice | solution.py:283
  2.4 2.9 %collective-permute-start = (bf16[32,2176]{1,0:T(8,128)(2,1)S(1)}, bf16[32,2176]{1,0:T(8,128)(2,1)S(1)}, u32[]{:S(2)}, u32[]{:S(2)}) collective-permute-start(bf16[32,2176]{1,0:T(8,128)(2,1)S(1)} %get-tuple-element.40), channel_id=1, source_target_pairs={{0,2},{2,0},{1,3},{3,1},{4,6},{6,4},{5,7},{7,5},{8,10},{10,8},{9,1... | collective-permute-start | bytes 417800 | tf_op jit(solution)/shard_map/ppermute | solution.py:267
  5.4 1.3 %reshape.16 = f32[32,40,32]{1,0,2:T(8,128)S(1)} reshape(f32[1280,32]{0,1:T(8,128)} %param.5) | data formatting | bytes 327680 | tf_op jit(solution)/shard_map/reshape | solution.py:295
  6.7 0.3 copy.7
  6.9 0.9 reshape.17.w_ref
  7.8 1.9 %shard_map.59 = (bf16[32,1344]{1,0:T(8,128)(2,1)}, f32[32,32]{1,0:T(8,128)}) custom-call(f32[32,1280]{1,0:T(8,128)} %reshape.17.w_ref), custom_call_target="tpu_custom_call" | custom-call | tf_op jit(solution)/shard_map/pallas_call | solution.py:244
  9.7 0.0 collective-permute-start.3
  9.7 0.8 broadcast_select_fusion
  10.5 1.4 %collective-permute-start.1 = (bf16[32,64]{1,0:T(8,128)(2,1)S(1)}, bf16[32,64]{1,0:T(8,128)(2,1)S(1)}, u32[]{:S(2)}, u32[]{:S(2)}) collective-permute-start(bf16[32,64]{1,0:T(8,128)(2,1)S(1)} %get-tuple-element.39), channel_id=1, source_target_pairs={{0,1},{1,4},{4,5},{5,8},{8,9},{9,12},{12,13},{3,2},{6,3},{7,6},{10... | collective-permute-start | bytes 12296 | tf_op jit(solution)/shard_map/ppermute | solution.py:293
  11.9 0.7 collective-permute-start.2
  12.6 0.1 collective-permute-done.1.refs_2_
  12.8 0.0 collective-permute-done.2.refs_3_
  12.8 1.7 %collective-permute-done.3.refs_5_ = bf16[32,1344]{1,0:T(8,128)(2,1)S(1)} collective-permute-done((bf16[32,1344]{1,0:T(8,128)(2,1)}, bf16[32,1344]{1,0:T(8,128)(2,1)S(1)}, u32[]{:S(2)}, u32[]{:S(2)}) %collective-permute-start.3) | collective-permute-done | bytes 86048 | tf_op jit(solution)/shard_map/ppermute | solution.py:267
  14.5 0.6 copy-done.2
  15.1 0.0 copy-done.1
  15.1 16.7 %shard_map.60 = (bf16[40,16,64,128]{3,2,1,0:T(8,128)(2,1)}, f32[32,2048]{1,0:T(8,128)}, f32[32,640]{1,0:T(8,128)}, f32[32,32]{1,0:T(8,128)}, bf16[32,704]{1,0:T(...) custom-call(bf16[32,2176]{1,0:T(8,128)(2,1)} %get-tuple-element.41.refs_0_, bf16[32,2176]{1,0:T(8,128)(2,1)} %copy-done.1, ...), custom_call_target="tpu_custom_call" | custom-call | tf_op jit(solution)/shard_map/pallas_call | solution.py:244
  31.9 5.2 %collective-permute-start.4 = (bf16[32,704]{1,0:T(8,128)(2,1)}, bf16[32,704]{1,0:T(8,128)(2,1)S(1)}, u32[]{:S(2)}, u32[]{:S(2)}) collective-permute-start(bf16[32,704]{1,0:T(8,128)(2,1)} %get-tuple-element.24), channel_id=1, source_target_pairs={{0,1},{1,0},{2,3},{3,2},{4,5},{5,4},{6,7},{7,6},{8,9},{9,8},{10,11... | collective-permute-start | bytes 135176 | tf_op jit(solution)/shard_map/ppermute | solution.py:273
  37.1 1.3 %collective-permute-start.5 = (bf16[32,704]{1,0:T(8,128)(2,1)}, bf16[32,704]{1,0:T(8,128)(2,1)S(1)}, u32[]{:S(2)}, u32[]{:S(2)}) collective-permute-start(bf16[32,704]{1,0:T(8,128)(2,1)} %get-tuple-element.25), channel_id=1, source_target_pairs={{0,2},{1,3},{2,0},{3,1},{4,6},{5,7},{6,4},{7,5},{8,10},{9,11},{10,... | collective-permute-start | bytes 135176 | tf_op jit(solution)/shard_map/ppermute | solution.py:273
  38.4 0.1 collective-permute-start.6
  38.5 2.9 %collective-permute-done.5.refs_3_ = bf16[32,704]{1,0:T(8,128)(2,1)S(1)} collective-permute-done((bf16[32,704]{1,0:T(8,128)(2,1)}, bf16[32,704]{1,0:T(8,128)(2,1)S(1)}, u32[]{:S(2)}, u32[]{:S(2)}) %collective-permute-start.5) | collective-permute-done | bytes 45088 | tf_op jit(solution)/shard_map/ppermute | solution.py:273
  41.4 1.2 %collective-permute-done.6.refs_4_ = bf16[32,704]{1,0:T(8,128)(2,1)S(1)} collective-permute-done((bf16[32,704]{1,0:T(8,128)(2,1)}, bf16[32,704]{1,0:T(8,128)(2,1)S(1)}, u32[]{:S(2)}, u32[]{:S(2)}) %collective-permute-start.6) | collective-permute-done | bytes 45088 | tf_op jit(solution)/shard_map/ppermute | solution.py:273
  42.6 0.6 copy-done.11
  43.2 1.7 %shard_map.61.refs_0_ = bf16[32,704]{1,0:T(8,128)(2,1)} custom-call(f32[32,640]{1,0:T(8,128)} %get-tuple-element.22.refs_0_, f32[32,32]{1,0:T(8,128)} %get-tuple-element.23.refs_1_, bf16[32,704]{1,0:T(8,128)(2,1)} %copy-done.9, bf16[32,704]{1,0:T(8,128)(2,1)} %copy-done.10, bf16[32,704]{1,0:T(8,128)(2,1)} %copy-done.11), custom_call_target="tpu_custom_call" | custom-call | tf_op jit(solution)/shard_map/pallas_call | solution.py:244
  44.9 1.6 %collective-permute-start.7 = (bf16[32,704]{1,0:T(8,128)(2,1)}, bf16[32,704]{1,0:T(8,128)(2,1)S(1)}, u32[]{:S(2)}, u32[]{:S(2)}) collective-permute-start(bf16[32,704]{1,0:T(8,128)(2,1)} %shard_map.61.refs_0_), channel_id=1, source_target_pairs={{0,4},{4,8},{8,12},{12,0},{1,5},{5,9},{9,13},{13,1},{2,6},{6,10},{... | collective-permute-start | bytes 135176 | tf_op jit(solution)/shard_map/ppermute | solution.py:337
  46.5 1.3 %collective-permute-start.8 = (bf16[32,704]{1,0:T(8,128)(2,1)}, bf16[32,704]{1,0:T(8,128)(2,1)S(1)}, u32[]{:S(2)}, u32[]{:S(2)}) collective-permute-start(bf16[32,704]{1,0:T(8,128)(2,1)} %shard_map.61.refs_0_), channel_id=1, source_target_pairs={{0,8},{4,12},{8,0},{12,4},{1,9},{5,13},{9,1},{13,5},{2,10},{6,14},... | collective-permute-start | bytes 135176 | tf_op jit(solution)/shard_map/ppermute | solution.py:337
  47.8 2.7 %collective-permute-start.9 = (bf16[32,704]{1,0:T(8,128)(2,1)}, bf16[32,704]{1,0:T(8,128)(2,1)S(1)}, u32[]{:S(2)}, u32[]{:S(2)}) collective-permute-start(bf16[32,704]{1,0:T(8,128)(2,1)} %shard_map.61.refs_0_), channel_id=1, source_target_pairs={{0,12},{4,0},{8,4},{12,8},{1,13},{5,1},{9,5},{13,9},{2,14},{6,2},{... | collective-permute-start | bytes 135176 | tf_op jit(solution)/shard_map/ppermute | solution.py:337
  50.4 0.3 reshape_reshape.3
  50.8 0.7 copy.11
  51.5 1.7 %collective-permute-done.8.refs_2_ = bf16[32,704]{1,0:T(8,128)(2,1)S(1)} collective-permute-done((bf16[32,704]{1,0:T(8,128)(2,1)}, bf16[32,704]{1,0:T(8,128)(2,1)S(1)}, u32[]{:S(2)}, u32[]{:S(2)}) %collective-permute-start.8) | collective-permute-done | bytes 45088 | tf_op jit(solution)/shard_map/ppermute | solution.py:337
  53.2 0.6 copy-done.15
  53.7 0.0 copy-done.17
  53.8 2.2 %shard_map.62 = (f32[32,640]{1,0:T(8,128)}, bf16[32,704]{1,0:T(8,128)(2,1)}) custom-call(f32[2,32,640]{2,1,0:T(8,128)} %bitcast.16, bf16[32,704]{1,0:T(8,128)(2,1)} %shard_map.61.refs_0_, bf16[32,704]{1,0:T(8,128)(2,1)} %copy-done.13, bf16[32,704]{1,0:T(8,128)(2,1)} %copy-done.15, bf16[32,704]{1,0:T(8,128)(2,1)} %copy-done.17), custom_call_target="tpu_custom_call" | custom-call | tf_op jit(solution)/shard_map/pallas_call | solution.py:244
  56.0 0.8 collective-permute-start.11
  56.8 1.0 %collective-permute-start.12 = (bf16[32,704]{1,0:T(8,128)(2,1)}, bf16[32,704]{1,0:T(8,128)(2,1)S(1)}, u32[]{:S(2)}, u32[]{:S(2)}) collective-permute-start(bf16[32,704]{1,0:T(8,128)(2,1)} %get-tuple-element.28.refs_0_), channel_id=1, source_target_pairs={{0,3},{1,2},{2,1},{3,0},{4,7},{5,6},{6,5},{7,4},{8,11},{9,10},{10,... | collective-permute-start | bytes 135176 | tf_op jit(solution)/shard_map/ppermute | solution.py:273
  57.8 2.8 %collective-permute-done.11.refs_2_ = bf16[32,704]{1,0:T(8,128)(2,1)S(1)} collective-permute-done((bf16[32,704]{1,0:T(8,128)(2,1)}, bf16[32,704]{1,0:T(8,128)(2,1)S(1)}, u32[]{:S(2)}, u32[]{:S(2)}) %collective-permute-start.11) | collective-permute-done | bytes 45088 | tf_op jit(solution)/shard_map/ppermute | solution.py:273
  60.7 0.4 collective-permute-done.12.refs_3_
  61.1 0.2 copy-done.4
  61.3 0.4 copy-done.5
  61.7 9.6 %shard_map.63 = (f32[32,2048]{1,0:T(8,128)}, f32[32,640]{1,0:T(8,128)}, f32[32,32]{1,0:T(8,128)}, bf16[32,704]{1,0:T(8,128)(2,1)}, bf16[32,704]{1,0:T(8,128)(2,1)}, /*index=5*/bf16[32,704]{1,0:T(8,128)(2,1)}) custom-call(bf16[32,704]{1,0:T(8,128)(2,1)} %get-tuple-element.28.refs_0_, bf16[32,704]{1,0:T(8,128)(2,1)} %copy-done.3, bf16[32,704]{1,0:T(8,128)(2,1)} %copy-done.4, ...), custom_call_target="tpu_custom_call" | custom-call | tf_op jit(solution)/shard_map/pallas_call | solution.py:244
  71.3 0.2 collective-permute-start.13
  71.5 0.9 collective-permute-start.14
  72.4 0.8 collective-permute-start.15
  73.2 0.9 collective-permute-start.20
  74.1 2.0 %collective-permute-done.14.refs_3_ = bf16[32,704]{1,0:T(8,128)(2,1)S(1)} collective-permute-done((bf16[32,704]{1,0:T(8,128)(2,1)}, bf16[32,704]{1,0:T(8,128)(2,1)S(1)}, u32[]{:S(2)}, u32[]{:S(2)}) %collective-permute-start.14) | collective-permute-done | bytes 45088 | tf_op jit(solution)/shard_map/ppermute | solution.py:273
  76.0 0.6 collective-permute-done.15.refs_4_
  76.6 0.0 copy-done.7
  76.7 0.6 copy-done.8
  77.2 1.7 %shard_map.64.refs_0_ = bf16[32,704]{1,0:T(8,128)(2,1)} custom-call(f32[32,640]{1,0:T(8,128)} %get-tuple-element.31.refs_0_, f32[32,32]{1,0:T(8,128)} %get-tuple-element.32.refs_1_, bf16[32,704]{1,0:T(8,128)(2,1)} %copy-done.6, bf16[32,704]{1,0:T(8,128)(2,1)} %copy-done.7, bf16[32,704]{1,0:T(8,128)(2,1)} %copy-done.8), custom_call_target="tpu_custom_call" | custom-call | tf_op jit(solution)/shard_map/pallas_call | solution.py:244
  78.9 1.2 %collective-permute-start.16 = (bf16[32,704]{1,0:T(8,128)(2,1)}, bf16[32,704]{1,0:T(8,128)(2,1)S(1)}, u32[]{:S(2)}, u32[]{:S(2)}) collective-permute-start(bf16[32,704]{1,0:T(8,128)(2,1)} %shard_map.64.refs_0_), channel_id=1, source_target_pairs={{0,4},{4,8},{8,12},{12,0},{1,5},{5,9},{9,13},{13,1},{2,6},{6,10},{... | collective-permute-start | bytes 135176 | tf_op jit(solution)/shard_map/ppermute | solution.py:337
  80.2 2.7 %collective-permute-start.17 = (bf16[32,704]{1,0:T(8,128)(2,1)}, bf16[32,704]{1,0:T(8,128)(2,1)S(1)}, u32[]{:S(2)}, u32[]{:S(2)}) collective-permute-start(bf16[32,704]{1,0:T(8,128)(2,1)} %shard_map.64.refs_0_), channel_id=1, source_target_pairs={{0,8},{4,12},{8,0},{12,4},{1,9},{5,13},{9,1},{13,5},{2,10},{6,14},... | collective-permute-start | bytes 135176 | tf_op jit(solution)/shard_map/ppermute | solution.py:337
  82.9 1.0 %constant_dynamic-update-slice_fusion.1 = f32[32,4096]{1,0:T(8,128)S(1)} fusion(f32[32,4096]{1,0:T(8,128)S(1)} %broadcast_in_dim.15, f32[32,2048]{1,0:T(8,128)} %get-tuple-element.37, s32[]{:T(128)S(6)} %select_n.65), kind=kLoop, calls=%fused_computation.8 | loop fusion | bytes 524292 | tf_op jit(solution)/shard_map/dynamic_update_slice | solution.py:368
  83.9 1.7 %collective-permute-done.16.refs_1_ = bf16[32,704]{1,0:T(8,128)(2,1)S(1)} collective-permute-done((bf16[32,704]{1,0:T(8,128)(2,1)}, bf16[32,704]{1,0:T(8,128)(2,1)S(1)}, u32[]{:S(2)}, u32[]{:S(2)}) %collective-permute-start.16) | collective-permute-done | bytes 45088 | tf_op jit(solution)/shard_map/ppermute | solution.py:337
  85.6 1.5 %collective-permute-done.17.refs_2_ = bf16[32,704]{1,0:T(8,128)(2,1)S(1)} collective-permute-done((bf16[32,704]{1,0:T(8,128)(2,1)}, bf16[32,704]{1,0:T(8,128)(2,1)S(1)}, u32[]{:S(2)}, u32[]{:S(2)}) %collective-permute-start.17) | collective-permute-done | bytes 45088 | tf_op jit(solution)/shard_map/ppermute | solution.py:337
  87.1 0.4 collective-permute-done.18.refs_3_
  87.5 0.2 copy-done.14
  87.7 0.5 copy-done.16
  88.2 2.2 %shard_map.65 = (f32[32,640]{1,0:T(8,128)}, bf16[32,704]{1,0:T(8,128)(2,1)}) custom-call(f32[32,640]{1,0:T(8,128)} %get-tuple-element.27.w_ref, bf16[32,704]{1,0:T(8,128)(2,1)} %shard_map.64.refs_0_, bf16[32,704]{1,0:T(8,128)(2,1)} %copy-done.12, bf16[32,704]{1,0:T(8,128)(2,1)} %copy-done.14, bf16[32,704]{1,0:T(8,128)(2,1)} %copy-done.16), custom_call_target="tpu_custom_call" | custom-call | tf_op jit(solution)/shard_map/pallas_call | solution.py:244
  90.3 0.9 bitcast_dynamic-update-slice_fusion.1
  91.3 0.6 collective-permute-done.19
  91.8 0.2 reshape.18
  92.1 0.7 copy.9
  92.8 2.0 %reshape.19 = f32[1280,32]{0,1:T(8,128)} reshape(f32[32,2,20,32]{2,1,0,3:T(2,128)S(1)} %copy.9) | data formatting | bytes 327680 | tf_op jit(solution)/shard_map/reshape | solution.py:363
  94.8 0.0 copy-start
  94.8 0.8 copy-done
  (41 shorter events, 0.2 us)
Async XLA Ops:
  2.4 12.0 %collective-permute-start = (bf16[32,2176]{1,0:T(8,128)(2,1)S(1)}, bf16[32,2176]{1,0:T(8,128)(2,1)S(1)}, u32[]{:S(2)}, u32[]{:S(2)}) collective-permute-start(bf16[32,2176]{1,0:T(8,128)(2,1)S(1)} %get-tuple-element.40), channel_id=1, source_target_pairs={{0,2},{2,0},{1,3},{3,1},{4,6},{6,4},{5,7},{7,5},{8,10},{10,8},{9,1... | collective-permute-start | bytes 417800 | tf_op jit(solution)/shard_map/ppermute | solution.py:267
  9.7 4.7 %collective-permute-start.3 = (bf16[32,1344]{1,0:T(8,128)(2,1)}, bf16[32,1344]{1,0:T(8,128)(2,1)S(1)}, u32[]{:S(2)}, u32[]{:S(2)}) collective-permute-start(bf16[32,1344]{1,0:T(8,128)(2,1)} %get-tuple-element.20.refs_4_), channel_id=1, source_target_pairs={{0,2},{2,0},{1,3},{3,1},{4,6},{6,4},{5,7},{7,5},{8,10},{10,8},{9,1... | collective-permute-start | bytes 258056 | tf_op jit(solution)/shard_map/ppermute | solution.py:267
  10.5 2.3 %collective-permute-start.1 = (bf16[32,64]{1,0:T(8,128)(2,1)S(1)}, bf16[32,64]{1,0:T(8,128)(2,1)S(1)}, u32[]{:S(2)}, u32[]{:S(2)}) collective-permute-start(bf16[32,64]{1,0:T(8,128)(2,1)S(1)} %get-tuple-element.39), channel_id=1, source_target_pairs={{0,1},{1,4},{4,5},{5,8},{8,9},{9,12},{12,13},{3,2},{6,3},{7,6},{10... | collective-permute-start | bytes 12296 | tf_op jit(solution)/shard_map/ppermute | solution.py:293
  11.9 0.8 collective-permute-start.2
  12.8 1.7 %copy-start.18 = (bf16[32,64]{1,0:T(8,128)(2,1)}, bf16[32,64]{1,0:T(8,128)(2,1)S(1)}, u32[]{:S(2)}) copy-start(bf16[32,64]{1,0:T(8,128)(2,1)S(1)} %collective-permute-done.1.refs_2_) | copy-start | bytes 12292
  12.8 1.7 %copy-start.19 = (bf16[32,64]{1,0:T(8,128)(2,1)}, bf16[32,64]{1,0:T(8,128)(2,1)S(1)}, u32[]{:S(2)}) copy-start(bf16[32,64]{1,0:T(8,128)(2,1)S(1)} %collective-permute-done.2.refs_3_) | copy-start | bytes 12292
  14.4 0.6 copy-start.2
  14.4 0.7 copy-start.1
  31.9 6.7 %collective-permute-start.4 = (bf16[32,704]{1,0:T(8,128)(2,1)}, bf16[32,704]{1,0:T(8,128)(2,1)S(1)}, u32[]{:S(2)}, u32[]{:S(2)}) collective-permute-start(bf16[32,704]{1,0:T(8,128)(2,1)} %get-tuple-element.24), channel_id=1, source_target_pairs={{0,1},{1,0},{2,3},{3,2},{4,5},{5,4},{6,7},{7,6},{8,9},{9,8},{10,11... | collective-permute-start | bytes 135176 | tf_op jit(solution)/shard_map/ppermute | solution.py:273
  37.1 4.3 %collective-permute-start.5 = (bf16[32,704]{1,0:T(8,128)(2,1)}, bf16[32,704]{1,0:T(8,128)(2,1)S(1)}, u32[]{:S(2)}, u32[]{:S(2)}) collective-permute-start(bf16[32,704]{1,0:T(8,128)(2,1)} %get-tuple-element.25), channel_id=1, source_target_pairs={{0,2},{1,3},{2,0},{3,1},{4,6},{5,7},{6,4},{7,5},{8,10},{9,11},{10,... | collective-permute-start | bytes 135176 | tf_op jit(solution)/shard_map/ppermute | solution.py:273
  38.4 4.2 %collective-permute-start.6 = (bf16[32,704]{1,0:T(8,128)(2,1)}, bf16[32,704]{1,0:T(8,128)(2,1)S(1)}, u32[]{:S(2)}, u32[]{:S(2)}) collective-permute-start(bf16[32,704]{1,0:T(8,128)(2,1)} %get-tuple-element.26), channel_id=1, source_target_pairs={{0,3},{1,2},{2,1},{3,0},{4,7},{5,6},{6,5},{7,4},{8,11},{9,10},{10,... | collective-permute-start | bytes 135176 | tf_op jit(solution)/shard_map/ppermute | solution.py:273
  38.5 4.1 %copy-start.9 = (bf16[32,704]{1,0:T(8,128)(2,1)}, bf16[32,704]{1,0:T(8,128)(2,1)S(1)}, u32[]{:S(2)}) copy-start(bf16[32,704]{1,0:T(8,128)(2,1)S(1)} %collective-permute-done.4.refs_2_) | copy-start | bytes 135172
  41.4 1.2 %copy-start.10 = (bf16[32,704]{1,0:T(8,128)(2,1)}, bf16[32,704]{1,0:T(8,128)(2,1)S(1)}, u32[]{:S(2)}) copy-start(bf16[32,704]{1,0:T(8,128)(2,1)S(1)} %collective-permute-done.5.refs_3_) | copy-start | bytes 135172
  42.6 0.6 copy-start.11
  44.9 6.5 %collective-permute-start.7 = (bf16[32,704]{1,0:T(8,128)(2,1)}, bf16[32,704]{1,0:T(8,128)(2,1)S(1)}, u32[]{:S(2)}, u32[]{:S(2)}) collective-permute-start(bf16[32,704]{1,0:T(8,128)(2,1)} %shard_map.61.refs_0_), channel_id=1, source_target_pairs={{0,4},{4,8},{8,12},{12,0},{1,5},{5,9},{9,13},{13,1},{2,6},{6,10},{... | collective-permute-start | bytes 135176 | tf_op jit(solution)/shard_map/ppermute | solution.py:337
  46.5 6.7 %collective-permute-start.8 = (bf16[32,704]{1,0:T(8,128)(2,1)}, bf16[32,704]{1,0:T(8,128)(2,1)S(1)}, u32[]{:S(2)}, u32[]{:S(2)}) collective-permute-start(bf16[32,704]{1,0:T(8,128)(2,1)} %shard_map.61.refs_0_), channel_id=1, source_target_pairs={{0,8},{4,12},{8,0},{12,4},{1,9},{5,13},{9,1},{13,5},{2,10},{6,14},... | collective-permute-start | bytes 135176 | tf_op jit(solution)/shard_map/ppermute | solution.py:337
  47.8 5.4 %collective-permute-start.9 = (bf16[32,704]{1,0:T(8,128)(2,1)}, bf16[32,704]{1,0:T(8,128)(2,1)S(1)}, u32[]{:S(2)}, u32[]{:S(2)}) collective-permute-start(bf16[32,704]{1,0:T(8,128)(2,1)} %shard_map.61.refs_0_), channel_id=1, source_target_pairs={{0,12},{4,0},{8,4},{12,8},{1,13},{5,1},{9,5},{13,9},{2,14},{6,2},{... | collective-permute-start | bytes 135176 | tf_op jit(solution)/shard_map/ppermute | solution.py:337
  51.5 1.7 %copy-start.13 = (bf16[32,704]{1,0:T(8,128)(2,1)}, bf16[32,704]{1,0:T(8,128)(2,1)S(1)}, u32[]{:S(2)}) copy-start(bf16[32,704]{1,0:T(8,128)(2,1)S(1)} %collective-permute-done.7.refs_1_) | copy-start | bytes 135172
  53.1 0.6 copy-start.15
  53.1 0.6 copy-start.17
  56.0 1.9 %collective-permute-start.10 = (bf16[32,704]{1,0:T(8,128)(2,1)}, bf16[32,704]{1,0:T(8,128)(2,1)S(1)}, u32[]{:S(2)}, u32[]{:S(2)}) collective-permute-start(bf16[32,704]{1,0:T(8,128)(2,1)} %get-tuple-element.28.refs_0_), channel_id=1, source_target_pairs={{0,1},{1,0},{2,3},{3,2},{4,5},{5,4},{6,7},{7,6},{8,9},{9,8},{10,11... | collective-permute-start | bytes 135176 | tf_op jit(solution)/shard_map/ppermute | solution.py:273
  56.0 4.7 %collective-permute-start.11 = (bf16[32,704]{1,0:T(8,128)(2,1)}, bf16[32,704]{1,0:T(8,128)(2,1)S(1)}, u32[]{:S(2)}, u32[]{:S(2)}) collective-permute-start(bf16[32,704]{1,0:T(8,128)(2,1)} %get-tuple-element.28.refs_0_), channel_id=1, source_target_pairs={{0,2},{1,3},{2,0},{3,1},{4,6},{5,7},{6,4},{7,5},{8,10},{9,11},{10,... | collective-permute-start | bytes 135176 | tf_op jit(solution)/shard_map/ppermute | solution.py:273
  56.8 4.2 %collective-permute-start.12 = (bf16[32,704]{1,0:T(8,128)(2,1)}, bf16[32,704]{1,0:T(8,128)(2,1)S(1)}, u32[]{:S(2)}, u32[]{:S(2)}) collective-permute-start(bf16[32,704]{1,0:T(8,128)(2,1)} %get-tuple-element.28.refs_0_), channel_id=1, source_target_pairs={{0,3},{1,2},{2,1},{3,0},{4,7},{5,6},{6,5},{7,4},{8,11},{9,10},{10,... | collective-permute-start | bytes 135176 | tf_op jit(solution)/shard_map/ppermute | solution.py:273
  57.8 3.2 %copy-start.3 = (bf16[32,704]{1,0:T(8,128)(2,1)}, bf16[32,704]{1,0:T(8,128)(2,1)S(1)}, u32[]{:S(2)}) copy-start(bf16[32,704]{1,0:T(8,128)(2,1)S(1)} %collective-permute-done.10.refs_1_) | copy-start | bytes 135172
  60.7 0.6 copy-start.4
  61.1 0.6 copy-start.5
  71.3 2.8 %collective-permute-start.13 = (bf16[32,704]{1,0:T(8,128)(2,1)}, bf16[32,704]{1,0:T(8,128)(2,1)S(1)}, u32[]{:S(2)}, u32[]{:S(2)}) collective-permute-start(bf16[32,704]{1,0:T(8,128)(2,1)} %get-tuple-element.33), channel_id=1, source_target_pairs={{0,1},{1,0},{2,3},{3,2},{4,5},{5,4},{6,7},{7,6},{8,9},{9,8},{10,11... | collective-permute-start | bytes 135176 | tf_op jit(solution)/shard_map/ppermute | solution.py:273
  71.5 4.6 %collective-permute-start.14 = (bf16[32,704]{1,0:T(8,128)(2,1)}, bf16[32,704]{1,0:T(8,128)(2,1)S(1)}, u32[]{:S(2)}, u32[]{:S(2)}) collective-permute-start(bf16[32,704]{1,0:T(8,128)(2,1)} %get-tuple-element.34), channel_id=1, source_target_pairs={{0,2},{1,3},{2,0},{3,1},{4,6},{5,7},{6,4},{7,5},{8,10},{9,11},{10,... | collective-permute-start | bytes 135176 | tf_op jit(solution)/shard_map/ppermute | solution.py:273
  72.4 4.2 %collective-permute-start.15 = (bf16[32,704]{1,0:T(8,128)(2,1)}, bf16[32,704]{1,0:T(8,128)(2,1)S(1)}, u32[]{:S(2)}, u32[]{:S(2)}) collective-permute-start(bf16[32,704]{1,0:T(8,128)(2,1)} %get-tuple-element.35), channel_id=1, source_target_pairs={{0,3},{1,2},{2,1},{3,0},{4,7},{5,6},{6,5},{7,4},{8,11},{9,10},{10,... | collective-permute-start | bytes 135176 | tf_op jit(solution)/shard_map/ppermute | solution.py:273
  73.2 21.6 %collective-permute-start.20 = (f32[32,2048]{1,0:T(8,128)}, f32[32,2048]{1,0:T(8,128)S(1)}, u32[]{:S(2)}, u32[]{:S(2)}) collective-permute-start(f32[32,2048]{1,0:T(8,128)} %get-tuple-element.37), channel_id=1, source_target_pairs={{0,2},{2,0},{1,3},{3,1},{4,6},{6,4},{5,7},{7,5},{8,10},{10,8},{9,1... | collective-permute-start | bytes 786440 | tf_op jit(solution)/shard_map/ppermute | solution.py:267
  74.1 2.6 %copy-start.6 = (bf16[32,704]{1,0:T(8,128)(2,1)}, bf16[32,704]{1,0:T(8,128)(2,1)S(1)}, u32[]{:S(2)}) copy-start(bf16[32,704]{1,0:T(8,128)(2,1)S(1)} %collective-permute-done.13.refs_2_) | copy-start | bytes 135172
  76.0 0.6 copy-start.7
  76.6 0.6 copy-start.8
  78.9 6.7 %collective-permute-start.16 = (bf16[32,704]{1,0:T(8,128)(2,1)}, bf16[32,704]{1,0:T(8,128)(2,1)S(1)}, u32[]{:S(2)}, u32[]{:S(2)}) collective-permute-start(bf16[32,704]{1,0:T(8,128)(2,1)} %shard_map.64.refs_0_), channel_id=1, source_target_pairs={{0,4},{4,8},{8,12},{12,0},{1,5},{5,9},{9,13},{13,1},{2,6},{6,10},{... | collective-permute-start | bytes 135176 | tf_op jit(solution)/shard_map/ppermute | solution.py:337
  80.2 6.9 %collective-permute-start.17 = (bf16[32,704]{1,0:T(8,128)(2,1)}, bf16[32,704]{1,0:T(8,128)(2,1)S(1)}, u32[]{:S(2)}, u32[]{:S(2)}) collective-permute-start(bf16[32,704]{1,0:T(8,128)(2,1)} %shard_map.64.refs_0_), channel_id=1, source_target_pairs={{0,8},{4,12},{8,0},{12,4},{1,9},{5,13},{9,1},{13,5},{2,10},{6,14},... | collective-permute-start | bytes 135176 | tf_op jit(solution)/shard_map/ppermute | solution.py:337
  82.9 4.7 %collective-permute-start.18 = (bf16[32,704]{1,0:T(8,128)(2,1)}, bf16[32,704]{1,0:T(8,128)(2,1)S(1)}, u32[]{:S(2)}, u32[]{:S(2)}) collective-permute-start(bf16[32,704]{1,0:T(8,128)(2,1)} %shard_map.64.refs_0_), channel_id=1, source_target_pairs={{0,12},{4,0},{8,4},{12,8},{1,13},{5,1},{9,5},{13,9},{2,14},{6,2},{... | collective-permute-start | bytes 135176 | tf_op jit(solution)/shard_map/ppermute | solution.py:337
  85.6 1.9 %copy-start.12 = (bf16[32,704]{1,0:T(8,128)(2,1)}, bf16[32,704]{1,0:T(8,128)(2,1)S(1)}, u32[]{:S(2)}) copy-start(bf16[32,704]{1,0:T(8,128)(2,1)S(1)} %collective-permute-done.16.refs_1_) | copy-start | bytes 135172
  87.1 0.6 copy-start.14
  87.5 0.6 copy-start.16
  90.3 1.5 %collective-permute-start.19 = (f32[32,640]{1,0:T(8,128)}, f32[32,640]{1,0:T(8,128)S(1)}, u32[]{:S(2)}, u32[]{:S(2)}) collective-permute-start(f32[32,640]{1,0:T(8,128)} %get-tuple-element.36), channel_id=1, source_target_pairs={{0,1},{1,0},{2,3},{3,2},{4,5},{5,4},{6,7},{7,6},{8,9},{9,8},{10,11... | collective-permute-start | bytes 245768 | tf_op jit(solution)/shard_map/ppermute | solution.py:361
  94.8 0.8 copy-start
where the time goes:
time: 96.4 us; the launch traced here: 95.6 us
  Pallas kernels  36 us (37%)
  starting transfers between devices  25.8 us (27%)
  waiting for transfers between devices  17.6 us (18%)
  local copies, waits for them, and re-layouts  14.7 us (15%)
    pallas_call x7, Pallas kernels, call(): pl.pallas_call(kernel, out_shape=[jax.ShapeDtypeStruct(*out) for out in o...  36 us
    ppermute x9, starting transfers between devices, quad_shift(): return lax.ppermute(value, ('row', 'sub'), pairs)  10.4 us
    ppermute x9, waiting for transfers between devices, quad_shift(): return lax.ppermute(value, ('row', 'sub'), pairs)  9.85 us
    ppermute x6, starting transfers between devices, reduced(): lax.ppermute(part, 'frm', [(i, (i + shift) % frms) for i in range(frms)])  9.45 us
    ppermute x6, waiting for transfers between devices, reduced(): lax.ppermute(part, 'frm', [(i, (i + shift) % frms) for i in range(frms)])  5.32 us
    unnamed x40, local copies, waits for them, and re-layouts  4.55 us
    ppermute x3, starting transfers between devices, row_shift(): lax.ppermute(value, 'row', [(i, (i + shift) % rows) for i in range(rows)])  3.8 us
    reshape x3, local copies, waits for them, and re-layouts, shards(): w_start.reshape(cl, NF, rank).transpose(2, 1, 0).reshape(rank, NF * cl)  2.43 us
  transfers between devices with their start and end apart: 21, of which 13 were waited for; matrix products, arithmetic and copies ran while one was open for 10% of the time, Pallas kernels for 6%

commit v1 on v0

--- a/solution.py
+++ b/solution.py
@@ -19,7 +19,7 @@
 BF16 = jnp.bfloat16
 HIGH = lax.Precision.HIGHEST
 NT = (((1,), (1,)), ((), ()))
-VMEM_LIMIT = 56 * 1024 * 1024
+MIB = 1024 * 1024
 
 
 def wavelets():
@@ -238,7 +238,7 @@
     pack(out_ref, new, lax.dot_general(new, new, NT, precision=HIGH, preferred_element_type=F32))
 
 
-def call(kernel, args, outs, scratch=(), grid=None, in_specs=None, out_specs=None):
+def call(kernel, args, outs, scratch=(), grid=None, in_specs=None, out_specs=None, limit=4):
     whole = pl.BlockSpec(memory_space=pltpu.VMEM)
     extra = {} if grid is None else {"grid": grid}
     return pl.pallas_call(
@@ -247,7 +247,7 @@
         in_specs=in_specs or [whole] * len(args),
         out_specs=out_specs or [whole] * len(outs),
         scratch_shapes=list(scratch),
-        compiler_params=pltpu.CompilerParams(vmem_limit_bytes=VMEM_LIMIT),
+        compiler_params=pltpu.CompilerParams(vmem_limit_bytes=limit * MIB),
         **extra,
     )(*args)
 
@@ -328,6 +328,7 @@
         (GROUPS,),
         spec,
         [pl.BlockSpec(memory_space=pl.ANY)] + [fixed(out[0]) for out in tail_outs],
+        limit=26,
     )
 
     def reduced(own, own_gram, msgs, w):
@@ -352,6 +353,7 @@
         tail_outs,
         [pltpu.VMEM((subs, GROUPS // subs, rows, rank, GROUP * cl), BF16)] + tail_scratch,
         in_specs=[whole] * (len(w_msgs) + 1) + [pl.BlockSpec(memory_space=pl.ANY)],
+        limit=20,
     )
     w_piece, _ = reduced(own, own_gram, msgs, w_piece)
 

time: 96.4 us -> 88.7 us (0.920)
  Pallas kernels: 36 us -> 23.5 us
  local copies, waits for them, and re-layouts: 14.7 us -> 18.6 us
  waiting for transfers between devices: 17.6 us -> 18.8 us
    pallas_call x7, Pallas kernels: 36 us -> 23.5 us  [call(): pl.pallas_call(kernel, out_shape=[jax.ShapeDtypeStruct(*out) for out in o...]
    unnamed x40 -> x10, local copies, waits for them, and re-layouts: 4.55 us -> 12.3 us
    ppermute x6, waiting for transfers between devices: 5.32 us -> 6.6 us  [reduced(): lax.ppermute(part, 'frm', [(i, (i + shift) % frms) for i in range(frms)])]
  transfers between devices with their start and end apart: 21 -> 21, of which waited for: 13 -> 14; matrix products, arithmetic and copies ran while one was open for 10% -> 7% of each run, Pallas kernels for 6% -> 2%
where the time goes in v1:
time: 88.7 us; the launch traced here: 88.3 us
  starting transfers between devices  25.9 us (29%)
  Pallas kernels  23.5 us (26%)
  waiting for transfers between devices  18.8 us (21%)
  local copies, waits for them, and re-layouts  18.6 us (21%)
    pallas_call x7, Pallas kernels, call(): pl.pallas_call(kernel, out_shape=[jax.ShapeDtypeStruct(*out) for out in o...  23.5 us
    unnamed x10, local copies, waits for them, and re-layouts  12.3 us
    ppermute x9, starting transfers between devices, quad_shift(): return lax.ppermute(value, ('row', 'sub'), pairs)  10.5 us
    ppermute x6, starting transfers between devices, reduced(): lax.ppermute(part, 'frm', [(i, (i + shift) % frms) for i in range(frms)])  9.37 us
    ppermute x9, waiting for transfers between devices, quad_shift(): return lax.ppermute(value, ('row', 'sub'), pairs)  9.35 us
    ppermute x6, waiting for transfers between devices, reduced(): lax.ppermute(part, 'frm', [(i, (i + shift) % frms) for i in range(frms)])  6.6 us
    ppermute x3, starting transfers between devices, row_shift(): lax.ppermute(value, 'row', [(i, (i + shift) % rows) for i in range(rows)])  3.89 us
    reshape x2, local copies, waits for them, and re-layouts, shards(): full.reshape(subs, rank, NF // subs, cl).transpose(3, 0, 2, 1)  2.27 us
  transfers between devices with their start and end apart: 21, of which 14 were waited for; matrix products, arithmetic and copies ran while one was open for 7% of the time, Pallas kernels for 2%

profile of v1, /device:TPU:0, one launch (start us, length us, event | category | flops | bytes accessed | tf_op | source)
XLA Modules:
  0.0 88.3 jit_solution(4140898621263958658)
XLA Ops:
  0.6 1.1 %pad_dynamic-slice_fusion = (bf16[32,2176]{1,0:T(8,128)(2,1)S(1)}, bf16[32,2176]{1,0:T(8,128)(2,1)S(1)}) fusion(s32[]{:T(128)S(6)} %select_n.55, bf16[32,4096]{1,0:T(8,128)(2,1)} %param.4, s32[]{:T(128)S(6)} %select_n.53), kind=kLoop, calls=%fused_computation | loop fusion | bytes 540680 | tf_op jit(solution)/shard_map/dynamic_slice | solution.py:283
  1.8 3.0 %collective-permute-start = (bf16[32,2176]{1,0:T(8,128)(2,1)S(1)}, bf16[32,2176]{1,0:T(8,128)(2,1)S(1)}, u32[]{:S(2)}, u32[]{:S(2)}) collective-permute-start(bf16[32,2176]{1,0:T(8,128)(2,1)S(1)} %get-tuple-element.40), channel_id=1, source_target_pairs={{0,2},{2,0},{1,3},{3,1},{4,6},{6,4},{5,7},{7,5},{8,10},{10,8},{9,1... | collective-permute-start | bytes 417800 | tf_op jit(solution)/shard_map/ppermute | solution.py:267
  4.8 1.3 %reshape.16 = f32[32,40,32]{1,0,2:T(8,128)S(1)} reshape(f32[1280,32]{0,1:T(8,128)} %param.5) | data formatting | bytes 327680 | tf_op jit(solution)/shard_map/reshape | solution.py:295
  6.1 0.3 copy.7
  6.4 0.2 reshape.17.w_ref
  6.6 0.3 shard_map.59
  6.9 0.0 collective-permute-start.3
  6.9 0.8 broadcast_select_fusion
  7.7 1.4 %collective-permute-start.1 = (bf16[32,64]{1,0:T(8,128)(2,1)S(1)}, bf16[32,64]{1,0:T(8,128)(2,1)S(1)}, u32[]{:S(2)}, u32[]{:S(2)}) collective-permute-start(bf16[32,64]{1,0:T(8,128)(2,1)S(1)} %get-tuple-element.39), channel_id=1, source_target_pairs={{0,1},{1,4},{4,5},{5,8},{8,9},{9,12},{12,13},{3,2},{6,3},{7,6},{10... | collective-permute-start | bytes 12296 | tf_op jit(solution)/shard_map/ppermute | solution.py:293
  9.2 0.7 collective-permute-start.2
  9.9 0.1 collective-permute-done.1.refs_2_
  10.0 0.0 collective-permute-done.2.refs_3_
  10.0 1.5 %collective-permute-done.3.refs_5_ = bf16[32,1344]{1,0:T(8,128)(2,1)S(1)} collective-permute-done((bf16[32,1344]{1,0:T(8,128)(2,1)S(1)}, bf16[32,1344]{1,0:T(8,128)(2,1)S(1)}, u32[]{:S(2)}, u32[]{:S(2)}) %collective-permute-start.3) | collective-permute-done | bytes 86048 | tf_op jit(solution)/shard_map/ppermute | solution.py:267
  11.5 0.0 collective-permute-done.refs_1_
  11.5 2.5 %copy-done.2 = bf16[40,256,256]{2,1,0:T(8,128)(2,1)S(1)} copy-done((bf16[40,256,256]{2,1,0:T(8,128)(2,1)S(1)}, bf16[40,256,256]{2,1,0:T(8,128)(2,1)}, u32[]{:S(2)}) %copy-start.2) | copy-done | bytes 5242904
  14.0 1.0 %copy-done.3 = f32[32,4096]{1,0:T(8,128)S(1)} copy-done((f32[32,4096]{1,0:T(8,128)S(1)}, f32[32,4096]{1,0:T(8,128)}, u32[]{:S(2)}) %copy-start.3) | copy-done | bytes 524312
  15.0 14.7 %shard_map.60 = (bf16[40,16,64,128]{3,2,1,0:T(8,128)(2,1)S(1)}, f32[32,2048]{1,0:T(8,128)S(1)}, f32[32,640]{1,0:T(8,128)S(1)}, f32[32,32]{1,0:T(8,128)S(1)}, bf1...) custom-call(bf16[32,2176]{1,0:T(8,128)(2,1)S(1)} %get-tuple-element.41.refs_0_, ...), custom_call_target="tpu_custom_call" | custom-call | tf_op jit(solution)/shard_map/pallas_call | solution.py:244
  29.7 4.0 %copy-done = bf16[40,16,64,128]{3,2,1,0:T(8,128)(2,1)} copy-done((bf16[40,16,64,128]{3,2,1,0:T(8,128)(2,1)}, bf16[40,16,64,128]{3,2,1,0:T(8,128)(2,1)S(1)}, u32[]{:S(2)}) %copy-start) | copy-done | bytes 10485784
  33.7 5.4 %collective-permute-start.4 = (bf16[32,704]{1,0:T(8,128)(2,1)S(1)}, bf16[32,704]{1,0:T(8,128)(2,1)S(1)}, u32[]{:S(2)}, u32[]{:S(2)}) collective-permute-start(bf16[32,704]{1,0:T(8,128)(2,1)S(1)} %get-tuple-element.24), channel_id=1, source_target_pairs={{0,1},{1,0},{2,3},{3,2},{4,5},{5,4},{6,7},{7,6},{8,9},{9,8},{10,11... | collective-permute-start | bytes 135176 | tf_op jit(solution)/shard_map/ppermute | solution.py:273
  39.0 1.3 %collective-permute-start.5 = (bf16[32,704]{1,0:T(8,128)(2,1)S(1)}, bf16[32,704]{1,0:T(8,128)(2,1)S(1)}, u32[]{:S(2)}, u32[]{:S(2)}) collective-permute-start(bf16[32,704]{1,0:T(8,128)(2,1)S(1)} %get-tuple-element.25), channel_id=1, source_target_pairs={{0,2},{1,3},{2,0},{3,1},{4,6},{5,7},{6,4},{7,5},{8,10},{9,11},{10,... | collective-permute-start | bytes 135176 | tf_op jit(solution)/shard_map/ppermute | solution.py:273
  40.3 0.1 collective-permute-start.6
  40.4 0.0 collective-permute-done.4.refs_2_
  40.4 2.7 %collective-permute-done.5.refs_3_ = bf16[32,704]{1,0:T(8,128)(2,1)S(1)} collective-permute-done((bf16[32,704]{1,0:T(8,128)(2,1)S(1)}, bf16[32,704]{1,0:T(8,128)(2,1)S(1)}, u32[]{:S(2)}, u32[]{:S(2)}) %collective-permute-start.5) | collective-permute-done | bytes 45088 | tf_op jit(solution)/shard_map/ppermute | solution.py:273
  43.1 1.1 %collective-permute-done.6.refs_4_ = bf16[32,704]{1,0:T(8,128)(2,1)S(1)} collective-permute-done((bf16[32,704]{1,0:T(8,128)(2,1)S(1)}, bf16[32,704]{1,0:T(8,128)(2,1)S(1)}, u32[]{:S(2)}, u32[]{:S(2)}) %collective-permute-start.6) | collective-permute-done | bytes 45088 | tf_op jit(solution)/shard_map/ppermute | solution.py:273
  44.3 0.2 shard_map.61.refs_0_
  44.4 1.6 %collective-permute-start.7 = (bf16[32,704]{1,0:T(8,128)(2,1)S(1)}, bf16[32,704]{1,0:T(8,128)(2,1)S(1)}, u32[]{:S(2)}, u32[]{:S(2)}) collective-permute-start(bf16[32,704]{1,0:T(8,128)(2,1)S(1)} %shard_map.61.refs_0_), channel_id=1, source_target_pairs={{0,4},{4,8},{8,12},{12,0},{1,5},{5,9},{9,13},{13,1},{2,6},{6,10},{... | collective-permute-start | bytes 135176 | tf_op jit(solution)/shard_map/ppermute | solution.py:338
  46.0 1.4 %collective-permute-start.8 = (bf16[32,704]{1,0:T(8,128)(2,1)S(1)}, bf16[32,704]{1,0:T(8,128)(2,1)S(1)}, u32[]{:S(2)}, u32[]{:S(2)}) collective-permute-start(bf16[32,704]{1,0:T(8,128)(2,1)S(1)} %shard_map.61.refs_0_), channel_id=1, source_target_pairs={{0,8},{4,12},{8,0},{12,4},{1,9},{5,13},{9,1},{13,5},{2,10},{6,14},... | collective-permute-start | bytes 135176 | tf_op jit(solution)/shard_map/ppermute | solution.py:338
  47.4 2.5 %collective-permute-start.9 = (bf16[32,704]{1,0:T(8,128)(2,1)S(1)}, bf16[32,704]{1,0:T(8,128)(2,1)S(1)}, u32[]{:S(2)}, u32[]{:S(2)}) collective-permute-start(bf16[32,704]{1,0:T(8,128)(2,1)S(1)} %shard_map.61.refs_0_), channel_id=1, source_target_pairs={{0,12},{4,0},{8,4},{12,8},{1,13},{5,1},{9,5},{13,9},{2,14},{6,2},{... | collective-permute-start | bytes 135176 | tf_op jit(solution)/shard_map/ppermute | solution.py:338
  50.0 0.3 reshape_reshape.3
  50.3 0.2 collective-permute-done.7.refs_1_
  50.5 2.0 %collective-permute-done.8.refs_2_ = bf16[32,704]{1,0:T(8,128)(2,1)S(1)} collective-permute-done((bf16[32,704]{1,0:T(8,128)(2,1)S(1)}, bf16[32,704]{1,0:T(8,128)(2,1)S(1)}, u32[]{:S(2)}, u32[]{:S(2)}) %collective-permute-start.8) | collective-permute-done | bytes 45088 | tf_op jit(solution)/shard_map/ppermute | solution.py:338
  52.5 0.0 collective-permute-done.9.refs_3_
  52.5 0.6 shard_map.62
  53.1 0.0 collective-permute-start.10
  53.1 1.0 %collective-permute-start.11 = (bf16[32,704]{1,0:T(8,128)(2,1)S(1)}, bf16[32,704]{1,0:T(8,128)(2,1)S(1)}, u32[]{:S(2)}, u32[]{:S(2)}) collective-permute-start(bf16[32,704]{1,0:T(8,128)(2,1)S(1)} %get-tuple-element.28.refs_0_), channel_id=1, source_target_pairs={{0,2},{1,3},{2,0},{3,1},{4,6},{5,7},{6,4},{7,5},{8,10},{9,11},{10,... | collective-permute-start | bytes 135176 | tf_op jit(solution)/shard_map/ppermute | solution.py:273
  54.1 0.9 %collective-permute-start.12 = (bf16[32,704]{1,0:T(8,128)(2,1)S(1)}, bf16[32,704]{1,0:T(8,128)(2,1)S(1)}, u32[]{:S(2)}, u32[]{:S(2)}) collective-permute-start(bf16[32,704]{1,0:T(8,128)(2,1)S(1)} %get-tuple-element.28.refs_0_), channel_id=1, source_target_pairs={{0,3},{1,2},{2,1},{3,0},{4,7},{5,6},{6,5},{7,4},{8,11},{9,10},{10,... | collective-permute-start | bytes 135176 | tf_op jit(solution)/shard_map/ppermute | solution.py:273
  54.9 0.0 collective-permute-done.10.refs_1_
  55.0 2.5 %collective-permute-done.11.refs_2_ = bf16[32,704]{1,0:T(8,128)(2,1)S(1)} collective-permute-done((bf16[32,704]{1,0:T(8,128)(2,1)S(1)}, bf16[32,704]{1,0:T(8,128)(2,1)S(1)}, u32[]{:S(2)}, u32[]{:S(2)}) %collective-permute-start.11) | collective-permute-done | bytes 45088 | tf_op jit(solution)/shard_map/ppermute | solution.py:273
  57.4 0.7 collective-permute-done.12.refs_3_
  58.1 4.0 %copy-done.1 = bf16[40,16,64,128]{3,2,1,0:T(8,128)(2,1)S(1)} copy-done((bf16[40,16,64,128]{3,2,1,0:T(8,128)(2,1)S(1)}, bf16[40,16,64,128]{3,2,1,0:T(8,128)(2,1)}, u32[]{:S(2)}) %copy-start.1) | copy-done | bytes 10485784
  62.1 6.3 %shard_map.63 = (f32[32,2048]{1,0:T(8,128)S(1)}, f32[32,640]{1,0:T(8,128)S(1)}, f32[32,32]{1,0:T(8,128)S(1)}, bf16[32,704]{1,0:T(8,128)(2,1)S(1)}, bf16[32,704]{...) custom-call(bf16[32,704]{1,0:T(8,128)(2,1)S(1)} %get-tuple-element.28.refs_0_, ...), custom_call_target="tpu_custom_call" | custom-call | tf_op jit(solution)/shard_map/pallas_call | solution.py:244
  68.4 0.2 collective-permute-start.13
  68.6 0.9 %collective-permute-start.14 = (bf16[32,704]{1,0:T(8,128)(2,1)S(1)}, bf16[32,704]{1,0:T(8,128)(2,1)S(1)}, u32[]{:S(2)}, u32[]{:S(2)}) collective-permute-start(bf16[32,704]{1,0:T(8,128)(2,1)S(1)} %get-tuple-element.34), channel_id=1, source_target_pairs={{0,2},{1,3},{2,0},{3,1},{4,6},{5,7},{6,4},{7,5},{8,10},{9,11},{10,... | collective-permute-start | bytes 135176 | tf_op jit(solution)/shard_map/ppermute | solution.py:273
  69.4 0.8 collective-permute-start.15
  70.3 0.9 collective-permute-start.20
  71.2 0.0 collective-permute-done.13.refs_2_
  71.2 1.7 %collective-permute-done.14.refs_3_ = bf16[32,704]{1,0:T(8,128)(2,1)S(1)} collective-permute-done((bf16[32,704]{1,0:T(8,128)(2,1)S(1)}, bf16[32,704]{1,0:T(8,128)(2,1)S(1)}, u32[]{:S(2)}, u32[]{:S(2)}) %collective-permute-start.14) | collective-permute-done | bytes 45088 | tf_op jit(solution)/shard_map/ppermute | solution.py:273
  72.9 0.6 collective-permute-done.15.refs_4_
  73.5 0.2 shard_map.64.refs_0_
  73.7 1.1 %collective-permute-start.16 = (bf16[32,704]{1,0:T(8,128)(2,1)S(1)}, bf16[32,704]{1,0:T(8,128)(2,1)S(1)}, u32[]{:S(2)}, u32[]{:S(2)}) collective-permute-start(bf16[32,704]{1,0:T(8,128)(2,1)S(1)} %shard_map.64.refs_0_), channel_id=1, source_target_pairs={{0,4},{4,8},{8,12},{12,0},{1,5},{5,9},{9,13},{13,1},{2,6},{6,10},{... | collective-permute-start | bytes 135176 | tf_op jit(solution)/shard_map/ppermute | solution.py:338
  74.8 2.7 %collective-permute-start.17 = (bf16[32,704]{1,0:T(8,128)(2,1)S(1)}, bf16[32,704]{1,0:T(8,128)(2,1)S(1)}, u32[]{:S(2)}, u32[]{:S(2)}) collective-permute-start(bf16[32,704]{1,0:T(8,128)(2,1)S(1)} %shard_map.64.refs_0_), channel_id=1, source_target_pairs={{0,8},{4,12},{8,0},{12,4},{1,9},{5,13},{9,1},{13,5},{2,10},{6,14},... | collective-permute-start | bytes 135176 | tf_op jit(solution)/shard_map/ppermute | solution.py:338
  77.5 0.0 collective-permute-start.18
  77.6 2.5 %collective-permute-done.16.refs_1_ = bf16[32,704]{1,0:T(8,128)(2,1)S(1)} collective-permute-done((bf16[32,704]{1,0:T(8,128)(2,1)S(1)}, bf16[32,704]{1,0:T(8,128)(2,1)S(1)}, u32[]{:S(2)}, u32[]{:S(2)}) %collective-permute-start.16) | collective-permute-done | bytes 45088 | tf_op jit(solution)/shard_map/ppermute | solution.py:338
  80.1 1.5 %collective-permute-done.17.refs_2_ = bf16[32,704]{1,0:T(8,128)(2,1)S(1)} collective-permute-done((bf16[32,704]{1,0:T(8,128)(2,1)S(1)}, bf16[32,704]{1,0:T(8,128)(2,1)S(1)}, u32[]{:S(2)}, u32[]{:S(2)}) %collective-permute-start.17) | collective-permute-done | bytes 45088 | tf_op jit(solution)/shard_map/ppermute | solution.py:338
  81.6 0.4 collective-permute-done.18.refs_3_
  82.0 1.2 %shard_map.65 = (f32[32,640]{1,0:T(8,128)S(1)}, bf16[32,704]{1,0:T(8,128)(2,1)}) custom-call(f32[32,640]{1,0:T(8,128)S(1)} %get-tuple-element.27.w_ref, bf16[32,704]{1,0:T(8,128)(2,1)S(1)} %shard_map.64.refs_0_, bf16[32,704]{1,0:T(8,128)(2,1)S(1)} %collective-permute-done.16.refs_1_, bf16[32,704]{1,0:T(8,128)(2,1)S(1)} %collective-permute-done.17.refs_2_, ...), custom_call_target="tpu_custom_call" | custom-call | tf_op jit(solution)/shard_map/pallas_call | solution.py:244
  83.3 0.0 collective-permute-start.19
  83.3 1.2 %collective-permute-done.19 = f32[32,640]{1,0:T(8,128)S(1)} collective-permute-done((f32[32,640]{1,0:T(8,128)S(1)}, f32[32,640]{1,0:T(8,128)S(1)}, u32[]{:S(2)}, u32[]{:S(2)}) %collective-permute-start.19) | collective-permute-done | bytes 81952 | tf_op jit(solution)/shard_map/ppermute | solution.py:363
  84.6 0.2 reshape.18
  84.8 0.7 copy.9
  85.5 2.0 %reshape.19 = f32[1280,32]{0,1:T(8,128)} reshape(f32[32,2,20,32]{2,1,0,3:T(2,128)S(1)} %copy.9) | data formatting | bytes 327680 | tf_op jit(solution)/shard_map/reshape | solution.py:365
  87.5 0.0 collective-permute-done.20
  87.5 0.0 copy-start.4
  87.6 0.8 copy-done.4
  (11 shorter events, 0.1 us)
Async XLA Ops:
  1.8 9.7 %collective-permute-start = (bf16[32,2176]{1,0:T(8,128)(2,1)S(1)}, bf16[32,2176]{1,0:T(8,128)(2,1)S(1)}, u32[]{:S(2)}, u32[]{:S(2)}) collective-permute-start(bf16[32,2176]{1,0:T(8,128)(2,1)S(1)} %get-tuple-element.40), channel_id=1, source_target_pairs={{0,2},{2,0},{1,3},{3,1},{4,6},{6,4},{5,7},{7,5},{8,10},{10,8},{9,1... | collective-permute-start | bytes 417800 | tf_op jit(solution)/shard_map/ppermute | solution.py:267
  6.9 4.5 %collective-permute-start.3 = (bf16[32,1344]{1,0:T(8,128)(2,1)S(1)}, bf16[32,1344]{1,0:T(8,128)(2,1)S(1)}, u32[]{:S(2)}, u32[]{:S(2)}) collective-permute-start(bf16[32,1344]{1,0:T(8,128)(2,1)S(1)} %get-tuple-element.20.refs_4_), channel_id=1, source_target_pairs={{0,2},{2,0},{1,3},{3,1},{4,6},{6,4},{5,7},{7,5},{8,10},{10,8},{9,1... | collective-permute-start | bytes 258056 | tf_op jit(solution)/shard_map/ppermute | solution.py:267
  7.7 2.3 %collective-permute-start.1 = (bf16[32,64]{1,0:T(8,128)(2,1)S(1)}, bf16[32,64]{1,0:T(8,128)(2,1)S(1)}, u32[]{:S(2)}, u32[]{:S(2)}) collective-permute-start(bf16[32,64]{1,0:T(8,128)(2,1)S(1)} %get-tuple-element.39), channel_id=1, source_target_pairs={{0,1},{1,4},{4,5},{5,8},{8,9},{9,12},{12,13},{3,2},{6,3},{7,6},{10... | collective-permute-start | bytes 12296 | tf_op jit(solution)/shard_map/ppermute | solution.py:293
  9.2 0.8 collective-permute-start.2
  11.5 2.5 %copy-start.2 = (bf16[40,256,256]{2,1,0:T(8,128)(2,1)S(1)}, bf16[40,256,256]{2,1,0:T(8,128)(2,1)}, u32[]{:S(2)}) copy-start(bf16[40,256,256]{2,1,0:T(8,128)(2,1)} %constant.54.clone.refs_8_) | copy-start | bytes 15728644
  13.9 1.0 %copy-start.3 = (f32[32,4096]{1,0:T(8,128)S(1)}, f32[32,4096]{1,0:T(8,128)}, u32[]{:S(2)}) copy-start(f32[32,4096]{1,0:T(8,128)} %refs_7_.1) | copy-start | bytes 1572868
  29.7 4.0 %copy-start = (bf16[40,16,64,128]{3,2,1,0:T(8,128)(2,1)}, bf16[40,16,64,128]{3,2,1,0:T(8,128)(2,1)S(1)}, u32[]{:S(2)}) copy-start(bf16[40,16,64,128]{3,2,1,0:T(8,128)(2,1)S(1)} %get-tuple-element.30.refs_5_) | copy-start | bytes 31457284
  33.7 6.7 %collective-permute-start.4 = (bf16[32,704]{1,0:T(8,128)(2,1)S(1)}, bf16[32,704]{1,0:T(8,128)(2,1)S(1)}, u32[]{:S(2)}, u32[]{:S(2)}) collective-permute-start(bf16[32,704]{1,0:T(8,128)(2,1)S(1)} %get-tuple-element.24), channel_id=1, source_target_pairs={{0,1},{1,0},{2,3},{3,2},{4,5},{5,4},{6,7},{7,6},{8,9},{9,8},{10,11... | collective-permute-start | bytes 135176 | tf_op jit(solution)/shard_map/ppermute | solution.py:273
  39.0 4.1 %collective-permute-start.5 = (bf16[32,704]{1,0:T(8,128)(2,1)S(1)}, bf16[32,704]{1,0:T(8,128)(2,1)S(1)}, u32[]{:S(2)}, u32[]{:S(2)}) collective-permute-start(bf16[32,704]{1,0:T(8,128)(2,1)S(1)} %get-tuple-element.25), channel_id=1, source_target_pairs={{0,2},{1,3},{2,0},{3,1},{4,6},{5,7},{6,4},{7,5},{8,10},{9,11},{10,... | collective-permute-start | bytes 135176 | tf_op jit(solution)/shard_map/ppermute | solution.py:273
  40.3 3.9 %collective-permute-start.6 = (bf16[32,704]{1,0:T(8,128)(2,1)S(1)}, bf16[32,704]{1,0:T(8,128)(2,1)S(1)}, u32[]{:S(2)}, u32[]{:S(2)}) collective-permute-start(bf16[32,704]{1,0:T(8,128)(2,1)S(1)} %get-tuple-element.26), channel_id=1, source_target_pairs={{0,3},{1,2},{2,1},{3,0},{4,7},{5,6},{6,5},{7,4},{8,11},{9,10},{10,... | collective-permute-start | bytes 135176 | tf_op jit(solution)/shard_map/ppermute | solution.py:273
  44.4 6.0 %collective-permute-start.7 = (bf16[32,704]{1,0:T(8,128)(2,1)S(1)}, bf16[32,704]{1,0:T(8,128)(2,1)S(1)}, u32[]{:S(2)}, u32[]{:S(2)}) collective-permute-start(bf16[32,704]{1,0:T(8,128)(2,1)S(1)} %shard_map.61.refs_0_), channel_id=1, source_target_pairs={{0,4},{4,8},{8,12},{12,0},{1,5},{5,9},{9,13},{13,1},{2,6},{6,10},{... | collective-permute-start | bytes 135176 | tf_op jit(solution)/shard_map/ppermute | solution.py:338
  46.0 6.4 %collective-permute-start.8 = (bf16[32,704]{1,0:T(8,128)(2,1)S(1)}, bf16[32,704]{1,0:T(8,128)(2,1)S(1)}, u32[]{:S(2)}, u32[]{:S(2)}) collective-permute-start(bf16[32,704]{1,0:T(8,128)(2,1)S(1)} %shard_map.61.refs_0_), channel_id=1, source_target_pairs={{0,8},{4,12},{8,0},{12,4},{1,9},{5,13},{9,1},{13,5},{2,10},{6,14},... | collective-permute-start | bytes 135176 | tf_op jit(solution)/shard_map/ppermute | solution.py:338
  47.4 5.1 %collective-permute-start.9 = (bf16[32,704]{1,0:T(8,128)(2,1)S(1)}, bf16[32,704]{1,0:T(8,128)(2,1)S(1)}, u32[]{:S(2)}, u32[]{:S(2)}) collective-permute-start(bf16[32,704]{1,0:T(8,128)(2,1)S(1)} %shard_map.61.refs_0_), channel_id=1, source_target_pairs={{0,12},{4,0},{8,4},{12,8},{1,13},{5,1},{9,5},{13,9},{2,14},{6,2},{... | collective-permute-start | bytes 135176 | tf_op jit(solution)/shard_map/ppermute | solution.py:338
  53.1 1.9 %collective-permute-start.10 = (bf16[32,704]{1,0:T(8,128)(2,1)S(1)}, bf16[32,704]{1,0:T(8,128)(2,1)S(1)}, u32[]{:S(2)}, u32[]{:S(2)}) collective-permute-start(bf16[32,704]{1,0:T(8,128)(2,1)S(1)} %get-tuple-element.28.refs_0_), channel_id=1, source_target_pairs={{0,1},{1,0},{2,3},{3,2},{4,5},{5,4},{6,7},{7,6},{8,9},{9,8},{10,11... | collective-permute-start | bytes 135176 | tf_op jit(solution)/shard_map/ppermute | solution.py:273
  53.1 4.4 %collective-permute-start.11 = (bf16[32,704]{1,0:T(8,128)(2,1)S(1)}, bf16[32,704]{1,0:T(8,128)(2,1)S(1)}, u32[]{:S(2)}, u32[]{:S(2)}) collective-permute-start(bf16[32,704]{1,0:T(8,128)(2,1)S(1)} %get-tuple-element.28.refs_0_), channel_id=1, source_target_pairs={{0,2},{1,3},{2,0},{3,1},{4,6},{5,7},{6,4},{7,5},{8,10},{9,11},{10,... | collective-permute-start | bytes 135176 | tf_op jit(solution)/shard_map/ppermute | solution.py:273
  54.1 4.0 %collective-permute-start.12 = (bf16[32,704]{1,0:T(8,128)(2,1)S(1)}, bf16[32,704]{1,0:T(8,128)(2,1)S(1)}, u32[]{:S(2)}, u32[]{:S(2)}) collective-permute-start(bf16[32,704]{1,0:T(8,128)(2,1)S(1)} %get-tuple-element.28.refs_0_), channel_id=1, source_target_pairs={{0,3},{1,2},{2,1},{3,0},{4,7},{5,6},{6,5},{7,4},{8,11},{9,10},{10,... | collective-permute-start | bytes 135176 | tf_op jit(solution)/shard_map/ppermute | solution.py:273
  58.1 4.0 %copy-start.1 = (bf16[40,16,64,128]{3,2,1,0:T(8,128)(2,1)S(1)}, bf16[40,16,64,128]{3,2,1,0:T(8,128)(2,1)}, u32[]{:S(2)}) copy-start(bf16[40,16,64,128]{3,2,1,0:T(8,128)(2,1)} %copy-done) | copy-start | bytes 31457284
  68.4 2.8 %collective-permute-start.13 = (bf16[32,704]{1,0:T(8,128)(2,1)S(1)}, bf16[32,704]{1,0:T(8,128)(2,1)S(1)}, u32[]{:S(2)}, u32[]{:S(2)}) collective-permute-start(bf16[32,704]{1,0:T(8,128)(2,1)S(1)} %get-tuple-element.33), channel_id=1, source_target_pairs={{0,1},{1,0},{2,3},{3,2},{4,5},{5,4},{6,7},{7,6},{8,9},{9,8},{10,11... | collective-permute-start | bytes 135176 | tf_op jit(solution)/shard_map/ppermute | solution.py:273
  68.6 4.4 %collective-permute-start.14 = (bf16[32,704]{1,0:T(8,128)(2,1)S(1)}, bf16[32,704]{1,0:T(8,128)(2,1)S(1)}, u32[]{:S(2)}, u32[]{:S(2)}) collective-permute-start(bf16[32,704]{1,0:T(8,128)(2,1)S(1)} %get-tuple-element.34), channel_id=1, source_target_pairs={{0,2},{1,3},{2,0},{3,1},{4,6},{5,7},{6,4},{7,5},{8,10},{9,11},{10,... | collective-permute-start | bytes 135176 | tf_op jit(solution)/shard_map/ppermute | solution.py:273
  69.4 4.0 %collective-permute-start.15 = (bf16[32,704]{1,0:T(8,128)(2,1)S(1)}, bf16[32,704]{1,0:T(8,128)(2,1)S(1)}, u32[]{:S(2)}, u32[]{:S(2)}) collective-permute-start(bf16[32,704]{1,0:T(8,128)(2,1)S(1)} %get-tuple-element.35), channel_id=1, source_target_pairs={{0,3},{1,2},{2,1},{3,0},{4,7},{5,6},{6,5},{7,4},{8,11},{9,10},{10,... | collective-permute-start | bytes 135176 | tf_op jit(solution)/shard_map/ppermute | solution.py:273
  70.3 17.2 %collective-permute-start.20 = (f32[32,2048]{1,0:T(8,128)S(1)}, f32[32,2048]{1,0:T(8,128)S(1)}, u32[]{:S(2)}, u32[]{:S(2)}) collective-permute-start(f32[32,2048]{1,0:T(8,128)S(1)} %get-tuple-element.37), channel_id=1, source_target_pairs={{0,2},{2,0},{1,3},{3,1},{4,6},{6,4},{5,7},{7,5},{8,10},{10,8},{9,1... | collective-permute-start | bytes 786440 | tf_op jit(solution)/shard_map/ppermute | solution.py:267
  73.7 6.5 %collective-permute-start.16 = (bf16[32,704]{1,0:T(8,128)(2,1)S(1)}, bf16[32,704]{1,0:T(8,128)(2,1)S(1)}, u32[]{:S(2)}, u32[]{:S(2)}) collective-permute-start(bf16[32,704]{1,0:T(8,128)(2,1)S(1)} %shard_map.64.refs_0_), channel_id=1, source_target_pairs={{0,4},{4,8},{8,12},{12,0},{1,5},{5,9},{9,13},{13,1},{2,6},{6,10},{... | collective-permute-start | bytes 135176 | tf_op jit(solution)/shard_map/ppermute | solution.py:338
  74.8 6.8 %collective-permute-start.17 = (bf16[32,704]{1,0:T(8,128)(2,1)S(1)}, bf16[32,704]{1,0:T(8,128)(2,1)S(1)}, u32[]{:S(2)}, u32[]{:S(2)}) collective-permute-start(bf16[32,704]{1,0:T(8,128)(2,1)S(1)} %shard_map.64.refs_0_), channel_id=1, source_target_pairs={{0,8},{4,12},{8,0},{12,4},{1,9},{5,13},{9,1},{13,5},{2,10},{6,14},... | collective-permute-start | bytes 135176 | tf_op jit(solution)/shard_map/ppermute | solution.py:338
  77.5 4.5 %collective-permute-start.18 = (bf16[32,704]{1,0:T(8,128)(2,1)S(1)}, bf16[32,704]{1,0:T(8,128)(2,1)S(1)}, u32[]{:S(2)}, u32[]{:S(2)}) collective-permute-start(bf16[32,704]{1,0:T(8,128)(2,1)S(1)} %shard_map.64.refs_0_), channel_id=1, source_target_pairs={{0,12},{4,0},{8,4},{12,8},{1,13},{5,1},{9,5},{13,9},{2,14},{6,2},{... | collective-permute-start | bytes 135176 | tf_op jit(solution)/shard_map/ppermute | solution.py:338
  83.3 1.3 %collective-permute-start.19 = (f32[32,640]{1,0:T(8,128)S(1)}, f32[32,640]{1,0:T(8,128)S(1)}, u32[]{:S(2)}, u32[]{:S(2)}) collective-permute-start(f32[32,640]{1,0:T(8,128)S(1)} %get-tuple-element.36), channel_id=1, source_target_pairs={{0,1},{1,0},{2,3},{3,2},{4,5},{5,4},{6,7},{7,6},{8,9},{9,8},{10,11... | collective-permute-start | bytes 245768 | tf_op jit(solution)/shard_map/ppermute | solution.py:363
  87.5 0.8 copy-start.4

commit v2 on v1

v2 whole, which is shorter than its diff:
```python
import functools
import math

import jax
import jax.numpy as jnp
import ml_dtypes
import numpy as np
from jax import lax
from jax.experimental import pallas as pl
from jax.experimental.pallas import tpu as pltpu
from jax.sharding import PartitionSpec as P

NF = 40
TAPS = 128
HALF = TAPS // 2
GROUP = 4
GROUPS = NF // GROUP
F32 = jnp.float32
BF16 = jnp.bfloat16
HIGH = lax.Precision.HIGHEST
NT = (((1,), (1,)), ((), ()))
MIB = 1024 * 1024


def wavelets():
    f = np.float32
    level = np.arange(NF, dtype=f) / f(NF - 1)
    freq = f(2.0) * np.power(f(12.0), level)
    sigma = f(7.0) / (f(2.0 * math.pi) * freq)
    times = (np.arange(TAPS, dtype=f) - f(HALF)) / f(50.0)
    env = np.exp(-(times[None, :] ** 2) / (f(2.0) * sigma[:, None] ** 2))
    scale = f(1.0) / np.sqrt(np.sum(env * env, axis=1))
    env = env * scale[:, None]
    phase = f(2.0 * math.pi) * freq[:, None] * times[None, :]
    return np.stack([env * np.cos(phase), env * np.sin(phase)]).astype(ml_dtypes.bfloat16)


def toeplitz():
    kernel = wavelets()
    table = np.zeros((NF, 2 * TAPS, 2 * TAPS), ml_dtypes.bfloat16)
    for at in range(TAPS):
        for part in range(2):
            table[:, at : at + TAPS, part * TAPS + at] = kernel[part]
    return table


def split_two(value):
    top = value.astype(BF16)
    return top, (value - top.astype(F32)).astype(BF16)


def joined(message, at, rank):
    return message[:, at : at + rank].astype(F32) + message[:, at + rank : at + 2 * rank].astype(F32)


def pack(out_ref, main, gram):
    rank, size = main.shape
    top, rest = split_two(gram)
    out_ref[:, :size] = main.astype(BF16)
    out_ref[:, size : size + rank] = top
    out_ref[:, size + rank : size + 2 * rank] = rest


def prepare_kernel(w_ref, msg_ref, gram_ref):
    w = w_ref[...]
    gram = lax.dot_general(w, w, NT, precision=HIGH, preferred_element_type=F32)
    gram_ref[...] = gram
    pack(msg_ref, w, gram)


def group_rows(s_ref, g, pair, rows, cl):
    halves = []
    for blk in (2 * pair, 2 * pair + 1):
        parts = [
            s_ref[g * GROUP : (g + 1) * GROUP, blk, x * cl : (x + 1) * cl, :].reshape(GROUP * cl, TAPS)
            for x in range(rows)
        ]
        halves.append(jnp.concatenate(parts, axis=0))
    return jnp.concatenate(halves, axis=1)


def finish_update(old, gram, w_scr, num_scr, s_ref, p_scr, h_out, own_ref, own_gram_ref, msg_refs, rows, subs, cl):
    rank, frames = old.shape
    pairs = frames // (2 * TAPS)
    per_sub = GROUPS // subs
    wide = GROUP * cl
    for pair in range(pairs):
        acc = jnp.zeros((rank, 2 * TAPS), F32)
        for g in range(GROUPS):
            wg = jnp.concatenate([w_scr[g // per_sub, g % per_sub, x] for x in range(rows)], axis=1)
            acc = acc + jnp.dot(wg, group_rows(s_ref, g, pair, rows, cl), preferred_element_type=F32)
        num_scr[:, 2 * TAPS * pair : 2 * TAPS * (pair + 1)] = acc
    new = old * num_scr[...] / jnp.dot(gram, old, precision=HIGH, preferred_element_type=F32)
    h_out[...] = new
    low = new.astype(BF16)
    h_gram = lax.dot_general(new, new, NT, precision=HIGH, preferred_element_type=F32)
    for g in range(GROUPS):
        acc = jnp.zeros((rank, rows * wide), F32)
        for pair in range(pairs):
            cols = slice(2 * TAPS * pair, 2 * TAPS * (pair + 1))
            acc = acc + lax.dot_general(
                low[:, cols], group_rows(s_ref, g, pair, rows, cl), NT, preferred_element_type=F32
            )
        at = (g % per_sub) * wide
        for x in range(rows):
            p_scr[g // per_sub, x, :, at : at + wide] = acc[:, x * wide : (x + 1) * wide]
    c_me = lax.axis_index("sub")
    size = per_sub * wide
    own_ref[...] = p_scr[c_me]
    own_gram_ref[...] = h_gram
    for dc in range(1, subs):
        ref = msg_refs[dc - 1]
        ref[:, :, :size] = p_scr[lax.rem(c_me + dc, subs)]
        for x in range(rows):
            ref[x, :, size:] = h_gram


def first_kernel(rows, subs, cl, blocks, *refs):
    refs = list(refs)
    sig_hbm, h_hbm, tab_hbm, order_hbm = (refs.pop(0) for _ in range(4))
    sig_refs = [refs.pop(0) for _ in range(rows - 1)]
    halo_ref, w_ref, gram_ref = (refs.pop(0) for _ in range(3))
    w_msgs = [refs.pop(0) for _ in range(rows - 1)]
    s_ref, w_out, h_out, own_ref, own_gram_ref = (refs.pop(0) for _ in range(5))
    msg_refs = [refs.pop(0) for _ in range(subs - 1)]
    sig_scr, old_scr, tab_scr, order_scr, xp_scr, x_scr, w_scr, num_scr, p_scr, sems, tab_sems = refs
    rank, frames = old_scr.shape
    window = sig_hbm.shape[1]
    width = sig_scr.shape[1]
    per_sub = GROUPS // subs
    wide = GROUP * cl
    x_me, c_me = lax.axis_index("row"), lax.axis_index("sub")
    depth = tab_scr.shape[0]

    def tab_copy(g):
        slot = lax.rem(g, depth)
        return pltpu.make_async_copy(tab_hbm.at[pl.ds(g * GROUP, GROUP)], tab_scr.at[slot], tab_sems.at[slot])

    begin = pl.multiple_of(jnp.clip(x_me * frames - TAPS, 0, window - width), TAPS)
    sig_copy = pltpu.make_async_copy(sig_hbm.at[:, pl.ds(begin, width)], sig_scr, sems.at[0])
    old_copy = pltpu.make_async_copy(
        h_hbm.at[:, pl.ds(pl.multiple_of(x_me * frames, TAPS), frames)], old_scr, sems.at[1]
    )
    order_copy = pltpu.make_async_copy(order_hbm, order_scr, sems.at[2])
    sig_copy.start()
    for g in range(depth - 1):
        tab_copy(g).start()
    old_copy.start()
    order_copy.start()
    sig_copy.wait()

    def place(source, owner):
        @pl.when(x_me == 0)
        def _():
            xp_scr[owner, :, HALF:] = source[:, : frames + HALF]

        @pl.when(x_me == rows - 1)
        def _():
            skip = width - frames - HALF
            xp_scr[owner, :, : frames + HALF] = source[:, skip:]

        if rows > 2:

            @pl.when((x_me > 0) & (x_me < rows - 1))
            def _():
                xp_scr[owner] = source[:, HALF : HALF + frames + TAPS]

    place(sig_scr, x_me)
    for shift in range(1, rows):
        place(sig_refs[shift - 1], lax.rem(x_me + rows - shift, rows))

    @pl.when(x_me == 0)
    def _():
        for at in range(rows):
            xp_scr[rows - 1 - at, :, :HALF] = halo_ref[at * cl : (at + 1) * cl, HALF:]

    @pl.when(x_me == rows - 1)
    def _():
        for at in range(rows):
            xp_scr[(rows - at) % rows, :, frames + HALF :] = halo_ref[at * cl : (at + 1) * cl, :HALF]

    for blk in range(blocks):
        for x in range(rows):
            x_scr[blk, x * cl : (x + 1) * cl, :] = xp_scr[x, :, blk * TAPS : (blk + 2) * TAPS]

    def convolve(g, carry):
        tab_copy(g).wait()

        @pl.when(g + depth - 1 < GROUPS)
        def _():
            tab_copy(g + depth - 1).start()

        for at in range(GROUP):
            co = jnp.dot(
                x_scr[...].reshape(blocks * rows * cl, 2 * TAPS),
                tab_scr[lax.rem(g, depth), at],
                preferred_element_type=F32,
            )
            power = co[:, :TAPS] * co[:, :TAPS] + co[:, TAPS:] * co[:, TAPS:]
            s_ref[g * GROUP + at] = power.astype(BF16).reshape(blocks, rows * cl, TAPS)
        return carry

    lax.fori_loop(0, GROUPS, convolve, 0)

    order_copy.wait()
    w = w_ref[...]
    top = w.astype(BF16)
    rest = w - top.astype(F32)
    middle = rest.astype(BF16)
    terms = [top, middle, (rest - middle.astype(F32)).astype(BF16)] + [ref[:, : NF * cl] for ref in w_msgs]
    moved = jnp.dot(jnp.concatenate(terms, axis=0), order_scr[...], preferred_element_type=F32)
    for at in range(GROUPS):
        cols = slice(at * wide, (at + 1) * wide)
        w_scr[at // per_sub, at % per_sub, x_me] = moved[:rank, cols].astype(BF16)
        for shift in range(1, rows):
            owner = lax.rem(x_me + rows - shift, rows)
            line = (shift + 2) * rank
            w_scr[at // per_sub, at % per_sub, owner] = moved[line : line + rank, cols].astype(BF16)
    whole = moved[:rank] + (moved[rank : 2 * rank] + moved[2 * rank : 3 * rank])
    size = per_sub * wide
    for c in range(subs):

        @pl.when(c_me == c)
        def _():
            w_out[...] = whole[:, c * size : (c + 1) * size]

    gram = gram_ref[...]
    for ref in w_msgs:
        gram = gram + joined(ref, NF * cl, rank)
    old_copy.wait()
    finish_update(
        old_scr[...], gram, w_scr, num_scr, s_ref, p_scr, h_out, own_ref, own_gram_ref, msg_refs, rows, subs, cl
    )


def later_kernel(rows, subs, cl, blocks, *refs):
    refs = list(refs)
    w_refs = [refs.pop(0) for _ in range(rows * subs)]
    h_ref, s_ref = refs.pop(0), refs.pop(0)
    h_out, own_ref, own_gram_ref = (refs.pop(0) for _ in range(3))
    msg_refs = [refs.pop(0) for _ in range(subs - 1)]
    w_scr, num_scr, p_scr = refs
    rank = h_ref.shape[0]
    per_sub = GROUPS // subs
    wide = GROUP * cl
    x_me, c_me = lax.axis_index("row"), lax.axis_index("sub")
    gram = jnp.zeros((rank, rank), F32)
    at = 0
    for dx in range(rows):
        for dc in range(subs):
            x_of, c_of = lax.rem(x_me + rows - dx, rows), lax.rem(c_me + subs - dc, subs)
            for part in range(per_sub):
                w_scr[c_of, part, x_of] = w_refs[at][:, part * wide : (part + 1) * wide]
            gram = gram + joined(w_refs[at], per_sub * wide, rank)
            at += 1
    finish_update(
        h_ref[...], gram, w_scr, num_scr, s_ref, p_scr, h_out, own_ref, own_gram_ref, msg_refs, rows, subs, cl
    )


def core_kernel(rows, subs, *refs):
    own_ref, own_gram_ref, *refs = refs
    msg_refs, refs = refs[: subs - 1], refs[subs - 1 :]
    out_ref, gram_ref, *out_msgs, scr = refs
    size = own_ref.shape[2]
    total, gram = own_ref[...], own_gram_ref[...]
    for ref in msg_refs:
        total = total + ref[:, :, :size]
        gram = gram + ref[0, :, size:]
    scr[...] = total
    gram_ref[...] = gram
    x_me = lax.axis_index("row")
    out_ref[...] = scr[x_me]
    for dx in range(1, rows):
        pack(out_msgs[dx - 1], scr[lax.rem(x_me + dx, rows)], gram)


def row_kernel(*refs):
    own_ref, own_gram_ref, *msg_refs, out_ref = refs
    rank, size = own_ref.shape
    total, gram = own_ref[...], own_gram_ref[...]
    for ref in msg_refs:
        total = total + ref[:, :size].astype(F32)
        gram = gram + joined(ref, size, rank)
    pack(out_ref, total, gram)


def summed(z_me, count, msg_refs, scr, rank, size):
    for shift in range(count):
        scr[partner(z_me, shift, count)] = msg_refs[shift][...]
    total, gram = scr[0, :, :size].astype(F32), joined(scr[0], size, rank)
    for at in range(1, count):
        total = total + scr[at, :, :size].astype(F32)
        gram = gram + joined(scr[at], size, rank)
    return total, gram


def partner(place, shift, count):
    if count & (count - 1):
        return (place + count - shift) % count
    return place ^ shift


def update_kernel(count, w_ref, *refs):
    msg_refs, (new_ref, out_ref, scr) = refs[:count], refs[count:]
    rank, size = new_ref.shape
    total, gram = summed(lax.axis_index("frm"), count, msg_refs, scr, rank, size)
    w = w_ref[...]
    new = w * total / jnp.dot(gram, w, precision=HIGH, preferred_element_type=F32)
    new_ref[...] = new
    pack(out_ref, new, lax.dot_general(new, new, NT, precision=HIGH, preferred_element_type=F32))


def last_kernel(count, w_ref, order_ref, *refs):
    msg_refs, (out_ref, scr) = refs[:count], refs[count:]
    rank, size = w_ref.shape
    total, gram = summed(lax.axis_index("frm"), count, msg_refs, scr, rank, size)
    w = w_ref[...]
    new = w * total / jnp.dot(gram, w, precision=HIGH, preferred_element_type=F32)
    top = new.astype(BF16)
    rest = new - top.astype(F32)
    middle = rest.astype(BF16)
    terms = jnp.concatenate([top, middle, (rest - middle.astype(F32)).astype(BF16)], axis=0)
    for c in range(order_ref.shape[1] // size):

        @pl.when(lax.axis_index("sub") == c)
        def _():
            moved = lax.dot_general(
                terms, order_ref[:, c * size : (c + 1) * size], NT, preferred_element_type=F32
            )
            out_ref[...] = moved[:rank] + (moved[rank : 2 * rank] + moved[2 * rank :])


def join_kernel(rows, *refs):
    own_refs, (out_ref, sems) = refs[:rows], refs[rows:]
    frames = own_refs[0].shape[1]
    x_me = lax.axis_index("row")
    copies = []
    for shift in range(rows):
        begin = pl.multiple_of(lax.rem(x_me + rows - shift, rows) * frames, TAPS)
        copies.append(pltpu.make_async_copy(own_refs[shift], out_ref.at[:, pl.ds(begin, frames)], sems.at[shift]))
    for copy in copies:
        copy.start()
    for copy in copies:
        copy.wait()


def call(kernel, args, outs, scratch=(), in_specs=None, out_specs=None, limit=4):
    whole = pl.BlockSpec(memory_space=pltpu.VMEM)
    return pl.pallas_call(
        kernel,
        out_shape=[jax.ShapeDtypeStruct(*out) if isinstance(out, tuple) else out for out in outs],
        in_specs=in_specs or [whole] * len(args),
        out_specs=out_specs or [whole] * len(outs),
        scratch_shapes=list(scratch),
        compiler_params=pltpu.CompilerParams(vmem_limit_bytes=limit * MIB),
    )(*args)


def reorder(cl):
    order = np.zeros((cl, NF, NF, cl), ml_dtypes.bfloat16)
    chans, freqs = np.meshgrid(np.arange(cl), np.arange(NF), indexing="ij")
    order[chans, freqs, freqs, chans] = 1
    return order.reshape(cl * NF, NF * cl)


def shards(signal, w_start, h_start):
    rows, subs, frms = (lax.axis_size(axis) for axis in ("row", "sub", "frm"))
    x_me = lax.axis_index("row")
    cl, window = signal.shape
    rank = w_start.shape[1]
    frames = window // rows
    blocks = frames // TAPS
    chans = rows * cl
    size = NF * cl // subs
    line = frms * subs
    width = frames + (TAPS if rows == 2 else 2 * TAPS)
    anywhere = pl.BlockSpec(memory_space=pl.ANY)
    whole = pl.BlockSpec(memory_space=pltpu.VMEM)

    def hbm(value):
        return pltpu.with_memory_space_constraint(value, pltpu.HBM)

    def vmem(value):
        return pltpu.with_memory_space_constraint(value, pltpu.VMEM)

    def row_shift(value, shift):
        return lax.ppermute(value, "row", [(i, (i + shift) % rows) for i in range(rows)])

    def sub_shift(value, shift):
        return lax.ppermute(value, "sub", [(i, (i + shift) % subs) for i in range(subs)])

    def frm_shift(value, shift):
        return lax.ppermute(value, "frm", [(partner(i, shift, frms), i) for i in range(frms)])

    def place(x, at):
        return (at // subs * rows + x) * subs + at % subs

    def begin(target):
        return jnp.clip(target * frames - TAPS, 0, window - width)

    sig = [
        row_shift(lax.dynamic_slice_in_dim(signal, begin((x_me + shift) % rows), width, 1), shift)
        for shift in range(1, rows)
    ]
    edge = jnp.where(x_me == 0, 0, window - TAPS)
    got_edge = jnp.where(x_me == 0, 0, width - TAPS)
    ends = [lax.dynamic_slice_in_dim(signal, edge, TAPS, 1)]
    ends += [lax.dynamic_slice_in_dim(part, got_edge, TAPS, 1) for part in sig]
    pairs = [(place(rows - 1, i), place(0, i + 1)) for i in range(line - 1)]
    halo = lax.ppermute(
        jnp.concatenate(ends, axis=0), ("frm", "row", "sub"), pairs + [(b, a) for a, b in pairs]
    )

    w_cols = w_start.T
    w_msg, w_gram = call(
        prepare_kernel, [w_cols], [((rank, NF * cl + 2 * rank), BF16), ((rank, rank), F32)]
    )
    w_msgs = [row_shift(w_msg, shift) for shift in range(1, rows)]

    msg = ((rank, size + 2 * rank), BF16)
    piece = ((rank, size), F32)
    tail_outs = [((rank, frames), F32), ((rows,) + piece[0], F32), ((rank, rank), F32)]
    tail_outs += [((rows, rank, size + rank), F32)] * (subs - 1)
    tail_scratch = [
        pltpu.VMEM((subs, GROUPS // subs, rows, rank, GROUP * cl), BF16),
        pltpu.VMEM((rank, frames), F32),
        pltpu.VMEM((subs, rows) + piece[0], F32),
    ]
    order = jnp.asarray(reorder(cl))
    held = [hbm(signal), hbm(h_start), hbm(jnp.asarray(toeplitz())), hbm(order)]
    rest = sig + [halo, w_cols, w_gram] + w_msgs
    spectra, w_piece, activations, own, own_gram, *msgs = call(
        functools.partial(first_kernel, rows, subs, cl, blocks),
        held + rest,
        [pltpu.VMEM((NF, blocks, chans, TAPS), BF16), piece] + tail_outs,
        [
            pltpu.VMEM((cl, width), BF16),
            pltpu.VMEM((rank, frames), F32),
            pltpu.VMEM((3, GROUP, 2 * TAPS, 2 * TAPS), BF16),
            pltpu.VMEM(order.shape, BF16),
            pltpu.VMEM((rows, cl, frames + TAPS), BF16),
            pltpu.VMEM((blocks, chans, 2 * TAPS), BF16),
        ]
        + tail_scratch
        + [pltpu.SemaphoreType.DMA((3,)), pltpu.SemaphoreType.DMA((3,))],
        in_specs=[anywhere] * len(held) + [whole] * len(rest),
        limit=24,
    )

    def gathered(own, own_gram, msgs):
        got = [sub_shift(m, dc + 1) for dc, m in enumerate(msgs)]
        part, gram, *outs = call(
            functools.partial(core_kernel, rows, subs),
            [own, own_gram] + got,
            [piece, ((rank, rank), F32)] + [msg] * (rows - 1),
            [pltpu.VMEM((rows,) + piece[0], F32)],
        )
        got = [row_shift(m, dx + 1) for dx, m in enumerate(outs)]
        (part,) = call(row_kernel, [part, gram] + got, [msg])
        return [part] + [frm_shift(part, shift) for shift in range(1, frms)]

    piled = [pltpu.VMEM((frms,) + msg[0], BF16)]
    w_piece, w_msg = call(
        functools.partial(update_kernel, frms), [w_piece] + gathered(own, own_gram, msgs), [piece, msg], piled
    )
    w_msgs = []
    for dx in range(rows):
        base = row_shift(w_msg, dx) if dx else w_msg
        w_msgs += [base] + [sub_shift(base, dc) for dc in range(1, subs)]
    activations, own, own_gram, *msgs = call(
        functools.partial(later_kernel, rows, subs, cl, blocks),
        w_msgs + [activations, vmem(spectra)],
        tail_outs,
        tail_scratch,
        limit=8,
    )
    (part,) = call(
        functools.partial(last_kernel, frms),
        [w_piece, vmem(order)] + gathered(own, own_gram, msgs),
        [((rank, NF * cl), F32)],
        piled,
    )
    synergies = part
    for dc in range(1, subs):
        synergies = synergies + sub_shift(part, dc)

    (wide,) = call(
        functools.partial(join_kernel, rows),
        [activations] + [row_shift(activations, shift) for shift in range(1, rows)],
        [pltpu.HBM((rank, window), F32)],
        [pltpu.SemaphoreType.DMA((rows,))],
        in_specs=[anywhere] * rows,
        out_specs=[anywhere],
    )
    return (synergies.T, wide)


def solution(mesh):
    placed = (P("row", ("grp", "frm", "sub")), P("row", None), P(None, ("grp", "frm", "sub")))
    return jax.shard_map(
        shards,
        mesh=mesh,
        in_specs=placed,
        out_specs=(P(("grp", "row"), None), P(None, ("grp", "frm", "sub"))),
        check_vma=False,
    )
```

time: 88.7 us -> 76.6 us (0.86)
  local copies, waits for them, and re-layouts: 18.6 us -> 3.56 us
  waiting for transfers between devices: 18.8 us -> 25.5 us
  starting transfers between devices: 25.9 us -> 23 us
    ppermute x3 -> x6, waiting for transfers between devices: 1.46 us -> 15.3 us  [row_shift(): lax.ppermute(value, 'row', [(i, (i + shift) % rows) for i in range(rows)])]
    unnamed x10 -> x6, local copies, waits for them, and re-layouts: 12.3 us -> 1.84 us
    ppermute x18 -> x12, starting transfers between devices: 22 us -> 14.5 us  [the longest x6 9.49 us: frm_shift(): lax.ppermute(value, 'frm', [(partner(i, shift, frms), i) for i in range(f...]
    ppermute x18 -> x12, waiting for transfers between devices: 17.3 us -> 10.2 us  [the longest x6 7.2 us: frm_shift(): lax.ppermute(value, 'frm', [(partner(i, shift, frms), i) for i in range(f...]
    ppermute x3 -> x6, starting transfers between devices: 3.89 us -> 8.48 us  [row_shift(): lax.ppermute(value, 'row', [(i, (i + shift) % rows) for i in range(rows)])]
    reshape x5 -> x0, local copies, waits for them, and re-layouts: 4.03 us -> none  [the longest x2 2.27 us: shards(): full.reshape(subs, rank, NF // subs, cl).transpose(3, 0, 2, 1)]
    pallas_call x7 -> x10, Pallas kernels: 23.5 us -> 22.9 us  [call(): pl.pallas_call(kernel, out_shape=[jax.ShapeDtypeStruct(*out) if isinstanc...]
  transfers between devices with their start and end apart: 21 -> 18, of which waited for: 14 -> 13; matrix products, arithmetic and copies ran while one was open for 7% -> 1% of each run, Pallas kernels for 2% -> 3%
where the time goes in v2:
time: 76.6 us; the launch traced here: 76.4 us
  waiting for transfers between devices  25.5 us (33%)
  starting transfers between devices  23 us (30%)
  Pallas kernels  22.9 us (30%)
  local copies, waits for them, and re-layouts  3.56 us (5%)
    pallas_call x10, Pallas kernels, call(): pl.pallas_call(kernel, out_shape=[jax.ShapeDtypeStruct(*out) if isinstanc...  22.9 us
    ppermute x6, waiting for transfers between devices, row_shift(): lax.ppermute(value, 'row', [(i, (i + shift) % rows) for i in range(rows)])  15.3 us
    ppermute x6, starting transfers between devices, frm_shift(): lax.ppermute(value, 'frm', [(partner(i, shift, frms), i) for i in range(f...  9.49 us
    ppermute x6, starting transfers between devices, row_shift(): lax.ppermute(value, 'row', [(i, (i + shift) % rows) for i in range(rows)])  8.48 us
    ppermute x6, waiting for transfers between devices, frm_shift(): lax.ppermute(value, 'frm', [(partner(i, shift, frms), i) for i in range(f...  7.2 us
    ppermute x5, starting transfers between devices, sub_shift(): lax.ppermute(value, 'sub', [(i, (i + shift) % subs) for i in range(subs)])  4.38 us
    ppermute x5, waiting for transfers between devices, sub_shift(): lax.ppermute(value, 'sub', [(i, (i + shift) % subs) for i in range(subs)])  2.99 us
    unnamed x6, local copies, waits for them, and re-layouts  1.84 us
  transfers between devices with their start and end apart: 18, of which 13 were waited for; matrix products, arithmetic and copies ran while one was open for 1% of the time, Pallas kernels for 3%

profile of v2, /device:TPU:0, one launch (start us, length us, event | category | flops | bytes accessed | tf_op | source)
XLA Modules:
  0.0 76.4 jit_solution(8477748208950716131)
XLA Ops:
  0.6 1.0 %constant_dynamic-slice_fusion.2 = bf16[32,2176]{1,0:T(8,128)(2,1)S(1)} fusion(bf16[32,4096]{1,0:T(8,128)(2,1)} %refs_0_.1, s32[]{:T(128)S(6)} %min.4), kind=kLoop, calls=%fused_computation.4 | loop fusion | bytes 278532 | tf_op jit(solution)/shard_map/dynamic_slice | solution.py:403
  1.7 3.0 %collective-permute-start = (bf16[32,2176]{1,0:T(8,128)(2,1)S(1)}, bf16[32,2176]{1,0:T(8,128)(2,1)S(1)}, u32[]{:S(2)}, u32[]{:S(2)}) collective-permute-start(bf16[32,2176]{1,0:T(8,128)(2,1)S(1)} %constant_dynamic-slice_fusion.2), channel_id=1, source_target_pairs={{0,2},{2,0},{1,3},{3,1},{4,6},{6,4},{5,7},{7,5},{8,10},{10,8},{9,1... | collective-permute-start | bytes 417800 | tf_op jit(solution)/shard_map/ppermute | solution.py:388
  4.7 0.0 copy-start.1
  4.7 0.9 %copy-done.1 = f32[1280,32]{0,1:T(8,128)S(1)} copy-done((f32[1280,32]{0,1:T(8,128)S(1)}, f32[1280,32]{0,1:T(8,128)}, u32[]{:S(2)}) %copy-start.1) | copy-done | bytes 163864
  5.6 0.3 shard_map.68
  5.9 0.0 collective-permute-start.2
  6.0 0.7 constant_dynamic-slice_fusion.1
  6.7 1.9 %collective-permute-done.refs_4_ = bf16[32,2176]{1,0:T(8,128)(2,1)S(1)} collective-permute-done((bf16[32,2176]{1,0:T(8,128)(2,1)S(1)}, bf16[32,2176]{1,0:T(8,128)(2,1)S(1)}, u32[]{:S(2)}, u32[]{:S(2)}) %collective-permute-start) | collective-permute-done | bytes 139296 | tf_op jit(solution)/shard_map/ppermute | solution.py:388
  8.6 0.7 collective-permute-start.1
  9.2 1.2 %collective-permute-done.2.refs_8_ = bf16[32,1344]{1,0:T(8,128)(2,1)S(1)} collective-permute-done((bf16[32,1344]{1,0:T(8,128)(2,1)S(1)}, bf16[32,1344]{1,0:T(8,128)(2,1)S(1)}, u32[]{:S(2)}, u32[]{:S(2)}) %collective-permute-start.2) | collective-permute-done | bytes 86048 | tf_op jit(solution)/shard_map/ppermute | solution.py:388
  10.5 0.0 collective-permute-done.1.refs_5_
  10.5 0.0 copy-start.2
  10.5 0.9 %copy-done.2 = f32[1280,32]{0,1:T(8,128)S(1)} copy-done((f32[1280,32]{0,1:T(8,128)S(1)}, f32[1280,32]{0,1:T(8,128)}, u32[]{:S(2)}) %copy-start.2) | copy-done | bytes 163864
  11.4 14.6 %shard_map.69 = (bf16[40,16,64,128]{3,2,1,0:T(8,128)(2,1)S(1)}, f32[32,640]{1,0:T(8,128)S(1)}, f32[32,2048]{1,0:T(8,128)S(1)}, f32[2,32,640]{2,1,0:T(8,128)S(1)}...) custom-call(bf16[32,4096]{1,0:T(8,128)(2,1)} %refs_0_.1, f32[32,4096]{1,0:T(8,128)} %refs_1_.1, ...), custom_call_target="tpu_custom_call" | custom-call | tf_op jit(solution)/shard_map/pallas_call | solution.py:350
  26.0 4.1 %collective-permute-start.3 = (f32[2,32,672]{2,1,0:T(8,128)S(1)}, f32[2,32,672]{2,1,0:T(8,128)S(1)}, u32[]{:S(2)}, u32[]{:S(2)}) collective-permute-start(f32[2,32,672]{2,1,0:T(8,128)S(1)} %get-tuple-element.27), channel_id=1, source_target_pairs={{0,1},{1,0},{2,3},{3,2},{4,5},{5,4},{6,7},{7,6},{8,9},{9,8},{10,11... | collective-permute-start | bytes 516104 | tf_op jit(solution)/shard_map/ppermute | solution.py:391
  30.1 1.1 %collective-permute-done.3.refs_2_ = f32[2,32,672]{2,1,0:T(8,128)S(1)} collective-permute-done((f32[2,32,672]{2,1,0:T(8,128)S(1)}, f32[2,32,672]{2,1,0:T(8,128)S(1)}, u32[]{:S(2)}, u32[]{:S(2)}) %collective-permute-start.3) | collective-permute-done | bytes 172064 | tf_op jit(solution)/shard_map/ppermute | solution.py:391
  31.1 0.1 shard_map.70
  31.2 2.0 %collective-permute-start.4 = (bf16[32,704]{1,0:T(8,128)(2,1)S(1)}, bf16[32,704]{1,0:T(8,128)(2,1)S(1)}, u32[]{:S(2)}, u32[]{:S(2)}) collective-permute-start(bf16[32,704]{1,0:T(8,128)(2,1)S(1)} %get-tuple-element.30), channel_id=1, source_target_pairs={{0,2},{2,0},{1,3},{3,1},{4,6},{6,4},{5,7},{7,5},{8,10},{10,8},{9,1... | collective-permute-start | bytes 135176 | tf_op jit(solution)/shard_map/ppermute | solution.py:388
  33.2 2.1 %collective-permute-done.4.refs_2_ = bf16[32,704]{1,0:T(8,128)(2,1)S(1)} collective-permute-done((bf16[32,704]{1,0:T(8,128)(2,1)S(1)}, bf16[32,704]{1,0:T(8,128)(2,1)S(1)}, u32[]{:S(2)}, u32[]{:S(2)}) %collective-permute-start.4) | collective-permute-done | bytes 45088 | tf_op jit(solution)/shard_map/ppermute | solution.py:388
  35.3 0.2 shard_map.71.refs_0_
  35.5 4.5 %collective-permute-start.7 = (bf16[32,704]{1,0:T(8,128)(2,1)S(1)}, bf16[32,704]{1,0:T(8,128)(2,1)S(1)}, u32[]{:S(2)}, u32[]{:S(2)}) collective-permute-start(bf16[32,704]{1,0:T(8,128)(2,1)S(1)} %shard_map.71.refs_0_), channel_id=1, source_target_pairs={{12,0},{8,4},{4,8},{0,12},{13,1},{9,5},{5,9},{1,13},{14,2},{10,6},... | collective-permute-start | bytes 135176 | tf_op jit(solution)/shard_map/ppermute | solution.py:394
  40.0 0.0 collective-permute-start.6
  40.0 0.6 collective-permute-start.5
  40.6 1.7 %collective-permute-done.7.refs_3_ = bf16[32,704]{1,0:T(8,128)(2,1)S(1)} collective-permute-done((bf16[32,704]{1,0:T(8,128)(2,1)S(1)}, bf16[32,704]{1,0:T(8,128)(2,1)S(1)}, u32[]{:S(2)}, u32[]{:S(2)}) %collective-permute-start.7) | collective-permute-done | bytes 45088 | tf_op jit(solution)/shard_map/ppermute | solution.py:394
  42.3 2.6 %collective-permute-done.6.refs_2_ = bf16[32,704]{1,0:T(8,128)(2,1)S(1)} collective-permute-done((bf16[32,704]{1,0:T(8,128)(2,1)S(1)}, bf16[32,704]{1,0:T(8,128)(2,1)S(1)}, u32[]{:S(2)}, u32[]{:S(2)}) %collective-permute-start.6) | collective-permute-done | bytes 45088 | tf_op jit(solution)/shard_map/ppermute | solution.py:394
  44.9 0.0 collective-permute-done.5.refs_1_
  44.9 0.6 shard_map.72
  45.6 1.1 %collective-permute-start.9 = (bf16[32,704]{1,0:T(8,128)(2,1)S(1)}, bf16[32,704]{1,0:T(8,128)(2,1)S(1)}, u32[]{:S(2)}, u32[]{:S(2)}) collective-permute-start(bf16[32,704]{1,0:T(8,128)(2,1)S(1)} %get-tuple-element.32.refs_0_), channel_id=1, source_target_pairs={{0,2},{2,0},{1,3},{3,1},{4,6},{6,4},{5,7},{7,5},{8,10},{10,8},{9,1... | collective-permute-start | bytes 135176 | tf_op jit(solution)/shard_map/ppermute | solution.py:388
  46.7 0.0 collective-permute-start.8
  46.7 3.0 %collective-permute-done.9.refs_2_ = bf16[32,704]{1,0:T(8,128)(2,1)S(1)} collective-permute-done((bf16[32,704]{1,0:T(8,128)(2,1)S(1)}, bf16[32,704]{1,0:T(8,128)(2,1)S(1)}, u32[]{:S(2)}, u32[]{:S(2)}) %collective-permute-start.9) | collective-permute-done | bytes 45088 | tf_op jit(solution)/shard_map/ppermute | solution.py:388
  49.7 0.0 collective-permute-start.10
  49.7 0.0 collective-permute-done.8.refs_1_
  49.7 1.2 %collective-permute-done.10.refs_3_ = bf16[32,704]{1,0:T(8,128)(2,1)S(1)} collective-permute-done((bf16[32,704]{1,0:T(8,128)(2,1)S(1)}, bf16[32,704]{1,0:T(8,128)(2,1)S(1)}, u32[]{:S(2)}, u32[]{:S(2)}) %collective-permute-start.10) | collective-permute-done | bytes 45088 | tf_op jit(solution)/shard_map/ppermute | solution.py:391
  50.9 0.0 copy-start
  50.9 5.2 %shard_map.73 = (f32[32,2048]{1,0:T(8,128)S(1)}, f32[2,32,640]{2,1,0:T(8,128)S(1)}, f32[32,32]{1,0:T(8,128)S(1)}, f32[2,32,672]{2,1,0:T(8,128)S(1)}) custom-call(bf16[32,704]{1,0:T(8,128)(2,1)S(1)} %get-tuple-element.32.refs_0_, bf16[32,704]{1,0:T(8,128)(2,1)S(1)} %collective-permute-done.8.refs_1_, bf16[32,704]{1,0:T(8,128)(2,1)S(1)} %collective-permute-done.9.refs_2_, ...), custom_call_target="tpu_custom_call" | custom-call | tf_op jit(solution)/shard_map/pallas_call | solution.py:350
  56.1 0.2 collective-permute-start.11
  56.3 1.1 %collective-permute-start.17 = (f32[32,2048]{1,0:T(8,128)S(1)}, f32[32,2048]{1,0:T(8,128)S(1)}, u32[]{:S(2)}, u32[]{:S(2)}) collective-permute-start(f32[32,2048]{1,0:T(8,128)S(1)} %get-tuple-element.41.refs_0_), channel_id=1, source_target_pairs={{0,2},{2,0},{1,3},{3,1},{4,6},{6,4},{5,7},{7,5},{8,10},{10,8},{9,1... | collective-permute-start | bytes 786440 | tf_op jit(solution)/shard_map/ppermute | solution.py:388
  57.4 0.1 collective-permute-done.11.refs_2_
  57.6 0.1 shard_map.74
  57.7 1.2 %collective-permute-start.12 = (bf16[32,704]{1,0:T(8,128)(2,1)S(1)}, bf16[32,704]{1,0:T(8,128)(2,1)S(1)}, u32[]{:S(2)}, u32[]{:S(2)}) collective-permute-start(bf16[32,704]{1,0:T(8,128)(2,1)S(1)} %get-tuple-element.40), channel_id=1, source_target_pairs={{0,2},{2,0},{1,3},{3,1},{4,6},{6,4},{5,7},{7,5},{8,10},{10,8},{9,1... | collective-permute-start | bytes 135176 | tf_op jit(solution)/shard_map/ppermute | solution.py:388
  58.8 7.1 %collective-permute-done.12.refs_2_ = bf16[32,704]{1,0:T(8,128)(2,1)S(1)} collective-permute-done((bf16[32,704]{1,0:T(8,128)(2,1)S(1)}, bf16[32,704]{1,0:T(8,128)(2,1)S(1)}, u32[]{:S(2)}, u32[]{:S(2)}) %collective-permute-start.12) | collective-permute-done | bytes 45088 | tf_op jit(solution)/shard_map/ppermute | solution.py:388
  65.9 0.2 shard_map.75.refs_0_
  66.1 1.6 %collective-permute-start.15 = (bf16[32,704]{1,0:T(8,128)(2,1)S(1)}, bf16[32,704]{1,0:T(8,128)(2,1)S(1)}, u32[]{:S(2)}, u32[]{:S(2)}) collective-permute-start(bf16[32,704]{1,0:T(8,128)(2,1)S(1)} %shard_map.75.refs_0_), channel_id=1, source_target_pairs={{12,0},{8,4},{4,8},{0,12},{13,1},{9,5},{5,9},{1,13},{14,2},{10,6},... | collective-permute-start | bytes 135176 | tf_op jit(solution)/shard_map/ppermute | solution.py:394
  67.6 0.5 collective-permute-start.14
  68.2 2.3 %collective-permute-start.13 = (bf16[32,704]{1,0:T(8,128)(2,1)S(1)}, bf16[32,704]{1,0:T(8,128)(2,1)S(1)}, u32[]{:S(2)}, u32[]{:S(2)}) collective-permute-start(bf16[32,704]{1,0:T(8,128)(2,1)S(1)} %shard_map.75.refs_0_), channel_id=1, source_target_pairs={{4,0},{0,4},{12,8},{8,12},{5,1},{1,5},{13,9},{9,13},{6,2},{2,6},{1... | collective-permute-start | bytes 135176 | tf_op jit(solution)/shard_map/ppermute | solution.py:394
  70.5 1.9 %collective-permute-done.15.refs_3_ = bf16[32,704]{1,0:T(8,128)(2,1)S(1)} collective-permute-done((bf16[32,704]{1,0:T(8,128)(2,1)S(1)}, bf16[32,704]{1,0:T(8,128)(2,1)S(1)}, u32[]{:S(2)}, u32[]{:S(2)}) %collective-permute-start.15) | collective-permute-done | bytes 45088 | tf_op jit(solution)/shard_map/ppermute | solution.py:394
  72.4 0.9 %collective-permute-done.14.refs_2_ = bf16[32,704]{1,0:T(8,128)(2,1)S(1)} collective-permute-done((bf16[32,704]{1,0:T(8,128)(2,1)S(1)}, bf16[32,704]{1,0:T(8,128)(2,1)S(1)}, u32[]{:S(2)}, u32[]{:S(2)}) %collective-permute-start.14) | collective-permute-done | bytes 45088 | tf_op jit(solution)/shard_map/ppermute | solution.py:394
  73.3 0.0 collective-permute-done.13.refs_1_
  73.3 0.0 copy-done
  73.3 0.9 %shard_map.76 = f32[32,1280]{1,0:T(8,128)S(1)} custom-call(f32[32,640]{1,0:T(8,128)S(1)} %get-tuple-element.31.w_ref, bf16[1280,1280]{1,0:T(8,128)(2,1)S(1)} %copy-done, bf16[32,704]{1,0:T(8,128)(2,1)S(1)} %shard_map.75.refs_0_, bf16[32,704]{1,0:T(8,128)(2,1)S(1)} %collective-permute-done.13.refs_1_, bf16[32,704]{1,0:T(8,128)(2,1)S(1)} %collective-permute-done.14.refs_2_, ...), custom_call_target="tpu_custom_call" | custom-call | tf_op jit(solution)/shard_map/pallas_call | solution.py:350
  74.2 0.1 collective-permute-start.16
  74.3 0.0 collective-permute-done.17.refs_1_
  74.3 0.8 %shard_map.77 = f32[32,4096]{1,0:T(8,128)} custom-call(f32[32,2048]{1,0:T(8,128)S(1)} %get-tuple-element.41.refs_0_, f32[32,2048]{1,0:T(8,128)S(1)} %collective-permute-done.17.refs_1_), custom_call_target="tpu_custom_call" | custom-call | tf_op jit(solution)/shard_map/pallas_call | solution.py:350
  75.2 0.5 collective-permute-done.16
  75.7 0.7 add_bitcast_fusion
  (2 shorter events, 0.0 us)
Async XLA Ops:
  1.7 6.9 %collective-permute-start = (bf16[32,2176]{1,0:T(8,128)(2,1)S(1)}, bf16[32,2176]{1,0:T(8,128)(2,1)S(1)}, u32[]{:S(2)}, u32[]{:S(2)}) collective-permute-start(bf16[32,2176]{1,0:T(8,128)(2,1)S(1)} %constant_dynamic-slice_fusion.2), channel_id=1, source_target_pairs={{0,2},{2,0},{1,3},{3,1},{4,6},{6,4},{5,7},{7,5},{8,10},{10,8},{9,1... | collective-permute-start | bytes 417800 | tf_op jit(solution)/shard_map/ppermute | solution.py:388
  4.7 0.9 %copy-start.1 = (f32[1280,32]{0,1:T(8,128)S(1)}, f32[1280,32]{0,1:T(8,128)}, u32[]{:S(2)}) copy-start(f32[1280,32]{0,1:T(8,128)} %param.6) | copy-start | bytes 491524
  5.9 4.5 %collective-permute-start.2 = (bf16[32,1344]{1,0:T(8,128)(2,1)S(1)}, bf16[32,1344]{1,0:T(8,128)(2,1)S(1)}, u32[]{:S(2)}, u32[]{:S(2)}) collective-permute-start(bf16[32,1344]{1,0:T(8,128)(2,1)S(1)} %get-tuple-element.23), channel_id=1, source_target_pairs={{0,2},{2,0},{1,3},{3,1},{4,6},{6,4},{5,7},{7,5},{8,10},{10,8},{9,1... | collective-permute-start | bytes 258056 | tf_op jit(solution)/shard_map/ppermute | solution.py:388
  8.6 1.9 %collective-permute-start.1 = (bf16[64,128]{1,0:T(8,128)(2,1)S(1)}, bf16[64,128]{1,0:T(8,128)(2,1)S(1)}, u32[]{:S(2)}, u32[]{:S(2)}) collective-permute-start(bf16[64,128]{1,0:T(8,128)(2,1)S(1)} %pad_maximum_fusion), channel_id=1, source_target_pairs={{2,1},{3,4},{6,5},{7,8},{10,9},{11,12},{14,13},{1,2},{4,3},{5,6},{... | collective-permute-start | bytes 49160 | tf_op jit(solution)/shard_map/ppermute | solution.py:411
  10.5 0.9 %copy-start.2 = (f32[1280,32]{0,1:T(8,128)S(1)}, f32[1280,32]{0,1:T(8,128)}, u32[]{:S(2)}) copy-start(f32[1280,32]{0,1:T(8,128)} %param.6) | copy-start | bytes 491524
  26.0 5.2 %collective-permute-start.3 = (f32[2,32,672]{2,1,0:T(8,128)S(1)}, f32[2,32,672]{2,1,0:T(8,128)S(1)}, u32[]{:S(2)}, u32[]{:S(2)}) collective-permute-start(f32[2,32,672]{2,1,0:T(8,128)S(1)} %get-tuple-element.27), channel_id=1, source_target_pairs={{0,1},{1,0},{2,3},{3,2},{4,5},{5,4},{6,7},{7,6},{8,9},{9,8},{10,11... | collective-permute-start | bytes 516104 | tf_op jit(solution)/shard_map/ppermute | solution.py:391
  31.2 4.1 %collective-permute-start.4 = (bf16[32,704]{1,0:T(8,128)(2,1)S(1)}, bf16[32,704]{1,0:T(8,128)(2,1)S(1)}, u32[]{:S(2)}, u32[]{:S(2)}) collective-permute-start(bf16[32,704]{1,0:T(8,128)(2,1)S(1)} %get-tuple-element.30), channel_id=1, source_target_pairs={{0,2},{2,0},{1,3},{3,1},{4,6},{6,4},{5,7},{7,5},{8,10},{10,8},{9,1... | collective-permute-start | bytes 135176 | tf_op jit(solution)/shard_map/ppermute | solution.py:388
  35.5 6.8 %collective-permute-start.7 = (bf16[32,704]{1,0:T(8,128)(2,1)S(1)}, bf16[32,704]{1,0:T(8,128)(2,1)S(1)}, u32[]{:S(2)}, u32[]{:S(2)}) collective-permute-start(bf16[32,704]{1,0:T(8,128)(2,1)S(1)} %shard_map.71.refs_0_), channel_id=1, source_target_pairs={{12,0},{8,4},{4,8},{0,12},{13,1},{9,5},{5,9},{1,13},{14,2},{10,6},... | collective-permute-start | bytes 135176 | tf_op jit(solution)/shard_map/ppermute | solution.py:394
  40.0 5.0 %collective-permute-start.6 = (bf16[32,704]{1,0:T(8,128)(2,1)S(1)}, bf16[32,704]{1,0:T(8,128)(2,1)S(1)}, u32[]{:S(2)}, u32[]{:S(2)}) collective-permute-start(bf16[32,704]{1,0:T(8,128)(2,1)S(1)} %shard_map.71.refs_0_), channel_id=1, source_target_pairs={{8,0},{12,4},{0,8},{4,12},{9,1},{13,5},{1,9},{5,13},{10,2},{14,6},... | collective-permute-start | bytes 135176 | tf_op jit(solution)/shard_map/ppermute | solution.py:394
  40.0 5.0 %collective-permute-start.5 = (bf16[32,704]{1,0:T(8,128)(2,1)S(1)}, bf16[32,704]{1,0:T(8,128)(2,1)S(1)}, u32[]{:S(2)}, u32[]{:S(2)}) collective-permute-start(bf16[32,704]{1,0:T(8,128)(2,1)S(1)} %shard_map.71.refs_0_), channel_id=1, source_target_pairs={{4,0},{0,4},{12,8},{8,12},{5,1},{1,5},{13,9},{9,13},{6,2},{2,6},{1... | collective-permute-start | bytes 135176 | tf_op jit(solution)/shard_map/ppermute | solution.py:394
  45.6 4.1 %collective-permute-start.9 = (bf16[32,704]{1,0:T(8,128)(2,1)S(1)}, bf16[32,704]{1,0:T(8,128)(2,1)S(1)}, u32[]{:S(2)}, u32[]{:S(2)}) collective-permute-start(bf16[32,704]{1,0:T(8,128)(2,1)S(1)} %get-tuple-element.32.refs_0_), channel_id=1, source_target_pairs={{0,2},{2,0},{1,3},{3,1},{4,6},{6,4},{5,7},{7,5},{8,10},{10,8},{9,1... | collective-permute-start | bytes 135176 | tf_op jit(solution)/shard_map/ppermute | solution.py:388
  46.7 3.0 %collective-permute-start.8 = (bf16[32,704]{1,0:T(8,128)(2,1)S(1)}, bf16[32,704]{1,0:T(8,128)(2,1)S(1)}, u32[]{:S(2)}, u32[]{:S(2)}) collective-permute-start(bf16[32,704]{1,0:T(8,128)(2,1)S(1)} %get-tuple-element.32.refs_0_), channel_id=1, source_target_pairs={{0,1},{1,0},{2,3},{3,2},{4,5},{5,4},{6,7},{7,6},{8,9},{9,8},{10,11... | collective-permute-start | bytes 135176 | tf_op jit(solution)/shard_map/ppermute | solution.py:391
  49.7 1.2 %collective-permute-start.10 = (bf16[32,704]{1,0:T(8,128)(2,1)S(1)}, bf16[32,704]{1,0:T(8,128)(2,1)S(1)}, u32[]{:S(2)}, u32[]{:S(2)}) collective-permute-start(bf16[32,704]{1,0:T(8,128)(2,1)S(1)} %collective-permute-done.9.refs_2_), channel_id=1, source_target_pairs={{0,1},{1,0},{2,3},{3,2},{4,5},{5,4},{6,7},{7,6},{8,9},{9,8},{10,11... | collective-permute-start | bytes 135176 | tf_op jit(solution)/shard_map/ppermute | solution.py:391
  50.9 22.4 %copy-start = (bf16[1280,1280]{1,0:T(8,128)(2,1)S(1)}, bf16[1280,1280]{1,0:T(8,128)(2,1)}, u32[]{:S(2)}) copy-start(bf16[1280,1280]{1,0:T(8,128)(2,1)} %constant.37.clone.refs_3_.order_ref) | copy-start | bytes 9830404
  56.1 1.5 %collective-permute-start.11 = (f32[2,32,672]{2,1,0:T(8,128)S(1)}, f32[2,32,672]{2,1,0:T(8,128)S(1)}, u32[]{:S(2)}, u32[]{:S(2)}) collective-permute-start(f32[2,32,672]{2,1,0:T(8,128)S(1)} %get-tuple-element.37), channel_id=1, source_target_pairs={{0,1},{1,0},{2,3},{3,2},{4,5},{5,4},{6,7},{7,6},{8,9},{9,8},{10,11... | collective-permute-start | bytes 516104 | tf_op jit(solution)/shard_map/ppermute | solution.py:391
  56.3 18.0 %collective-permute-start.17 = (f32[32,2048]{1,0:T(8,128)S(1)}, f32[32,2048]{1,0:T(8,128)S(1)}, u32[]{:S(2)}, u32[]{:S(2)}) collective-permute-start(f32[32,2048]{1,0:T(8,128)S(1)} %get-tuple-element.41.refs_0_), channel_id=1, source_target_pairs={{0,2},{2,0},{1,3},{3,1},{4,6},{6,4},{5,7},{7,5},{8,10},{10,8},{9,1... | collective-permute-start | bytes 786440 | tf_op jit(solution)/shard_map/ppermute | solution.py:388
  57.7 8.3 %collective-permute-start.12 = (bf16[32,704]{1,0:T(8,128)(2,1)S(1)}, bf16[32,704]{1,0:T(8,128)(2,1)S(1)}, u32[]{:S(2)}, u32[]{:S(2)}) collective-permute-start(bf16[32,704]{1,0:T(8,128)(2,1)S(1)} %get-tuple-element.40), channel_id=1, source_target_pairs={{0,2},{2,0},{1,3},{3,1},{4,6},{6,4},{5,7},{7,5},{8,10},{10,8},{9,1... | collective-permute-start | bytes 135176 | tf_op jit(solution)/shard_map/ppermute | solution.py:388
  66.1 6.3 %collective-permute-start.15 = (bf16[32,704]{1,0:T(8,128)(2,1)S(1)}, bf16[32,704]{1,0:T(8,128)(2,1)S(1)}, u32[]{:S(2)}, u32[]{:S(2)}) collective-permute-start(bf16[32,704]{1,0:T(8,128)(2,1)S(1)} %shard_map.75.refs_0_), channel_id=1, source_target_pairs={{12,0},{8,4},{4,8},{0,12},{13,1},{9,5},{5,9},{1,13},{14,2},{10,6},... | collective-permute-start | bytes 135176 | tf_op jit(solution)/shard_map/ppermute | solution.py:394
  67.6 5.7 %collective-permute-start.14 = (bf16[32,704]{1,0:T(8,128)(2,1)S(1)}, bf16[32,704]{1,0:T(8,128)(2,1)S(1)}, u32[]{:S(2)}, u32[]{:S(2)}) collective-permute-start(bf16[32,704]{1,0:T(8,128)(2,1)S(1)} %shard_map.75.refs_0_), channel_id=1, source_target_pairs={{8,0},{12,4},{0,8},{4,12},{9,1},{13,5},{1,9},{5,13},{10,2},{14,6},... | collective-permute-start | bytes 135176 | tf_op jit(solution)/shard_map/ppermute | solution.py:394
  68.2 5.2 %collective-permute-start.13 = (bf16[32,704]{1,0:T(8,128)(2,1)S(1)}, bf16[32,704]{1,0:T(8,128)(2,1)S(1)}, u32[]{:S(2)}, u32[]{:S(2)}) collective-permute-start(bf16[32,704]{1,0:T(8,128)(2,1)S(1)} %shard_map.75.refs_0_), channel_id=1, source_target_pairs={{4,0},{0,4},{12,8},{8,12},{5,1},{1,5},{13,9},{9,13},{6,2},{2,6},{1... | collective-permute-start | bytes 135176 | tf_op jit(solution)/shard_map/ppermute | solution.py:394
  74.2 1.5 %collective-permute-start.16 = (f32[32,1280]{1,0:T(8,128)S(1)}, f32[32,1280]{1,0:T(8,128)S(1)}, u32[]{:S(2)}, u32[]{:S(2)}) collective-permute-start(f32[32,1280]{1,0:T(8,128)S(1)} %shard_map.76), channel_id=1, source_target_pairs={{0,1},{1,0},{2,3},{3,2},{4,5},{5,4},{6,7},{7,6},{8,9},{9,8},{10,11... | collective-permute-start | bytes 491528 | tf_op jit(solution)/shard_map/ppermute | solution.py:391

commit v3 on v2

--- a/solution.py
+++ b/solution.py
@@ -61,7 +61,8 @@
     out_ref[:, size + rank : size + 2 * rank] = rest
 
 
-def prepare_kernel(w_ref, msg_ref, gram_ref):
+def prepare_kernel(w_ref, *refs):
+    msg_ref, gram_ref = refs[-2:]
     w = w_ref[...]
     gram = lax.dot_general(w, w, NT, precision=HIGH, preferred_element_type=F32)
     gram_ref[...] = gram
@@ -72,19 +73,30 @@
     halves = []
     for blk in (2 * pair, 2 * pair + 1):
         parts = [
-            s_ref[g * GROUP : (g + 1) * GROUP, blk, x * cl : (x + 1) * cl, :].reshape(GROUP * cl, TAPS)
+            s_ref[pl.ds(g * GROUP, GROUP), blk, x * cl : (x + 1) * cl, :].reshape(GROUP * cl, TAPS)
             for x in range(rows)
         ]
         halves.append(jnp.concatenate(parts, axis=0))
     return jnp.concatenate(halves, axis=1)
 
 
-def finish_update(old, gram, w_scr, num_scr, s_ref, p_scr, h_out, own_ref, own_gram_ref, msg_refs, rows, subs, cl):
-    rank, frames = old.shape
-    pairs = frames // (2 * TAPS)
+def crossed(low, s_ref, core, out_ref, rows, subs, cl):
     per_sub = GROUPS // subs
     wide = GROUP * cl
-    for pair in range(pairs):
+    for part in range(per_sub):
+        acc = jnp.zeros((low.shape[0], rows * wide), F32)
+        for pair in range(low.shape[1] // (2 * TAPS)):
+            cols = slice(2 * TAPS * pair, 2 * TAPS * (pair + 1))
+            spectra = group_rows(s_ref, core * per_sub + part, pair, rows, cl)
+            acc = acc + lax.dot_general(low[:, cols], spectra, NT, preferred_element_type=F32)
+        for x in range(rows):
+            out_ref[x, :, part * wide : (part + 1) * wide] = acc[:, x * wide : (x + 1) * wide]
+
+
+def new_activations(old, gram, w_scr, num_scr, s_ref, h_out, h_gram_ref, msg_refs, rows, subs, cl):
+    rank, frames = old.shape
+    per_sub = GROUPS // subs
+    for pair in range(frames // (2 * TAPS)):
         acc = jnp.zeros((rank, 2 * TAPS), F32)
         for g in range(GROUPS):
             wg = jnp.concatenate([w_scr[g // per_sub, g % per_sub, x] for x in range(rows)], axis=1)
@@ -92,44 +104,32 @@
         num_scr[:, 2 * TAPS * pair : 2 * TAPS * (pair + 1)] = acc
     new = old * num_scr[...] / jnp.dot(gram, old, precision=HIGH, preferred_element_type=F32)
     h_out[...] = new
-    low = new.astype(BF16)
     h_gram = lax.dot_general(new, new, NT, precision=HIGH, preferred_element_type=F32)
-    for g in range(GROUPS):
-        acc = jnp.zeros((rank, rows * wide), F32)
-        for pair in range(pairs):
-            cols = slice(2 * TAPS * pair, 2 * TAPS * (pair + 1))
-            acc = acc + lax.dot_general(
-                low[:, cols], group_rows(s_ref, g, pair, rows, cl), NT, preferred_element_type=F32
-            )
-        at = (g % per_sub) * wide
-        for x in range(rows):
-            p_scr[g // per_sub, x, :, at : at + wide] = acc[:, x * wide : (x + 1) * wide]
+    h_gram_ref[...] = h_gram
+    size = per_sub * GROUP * cl
     c_me = lax.axis_index("sub")
-    size = per_sub * wide
-    own_ref[...] = p_scr[c_me]
-    own_gram_ref[...] = h_gram
     for dc in range(1, subs):
         ref = msg_refs[dc - 1]
-        ref[:, :, :size] = p_scr[lax.rem(c_me + dc, subs)]
+        crossed(new.astype(BF16), s_ref, lax.rem(c_me + dc, subs), ref, rows, subs, cl)
         for x in range(rows):
             ref[x, :, size:] = h_gram
 
 
-def first_kernel(rows, subs, cl, blocks, *refs):
+def own_kernel(rows, subs, cl, h_ref, s_ref, out_ref):
+    crossed(h_ref[...].astype(BF16), s_ref, lax.axis_index("sub"), out_ref, rows, subs, cl)
+
+
+def spectra_kernel(rows, cl, blocks, *refs):
     refs = list(refs)
-    sig_hbm, h_hbm, tab_hbm, order_hbm = (refs.pop(0) for _ in range(4))
+    sig_hbm, h_hbm, w_hbm, tab_hbm, order_hbm = (refs.pop(0) for _ in range(5))
     sig_refs = [refs.pop(0) for _ in range(rows - 1)]
-    halo_ref, w_ref, gram_ref = (refs.pop(0) for _ in range(3))
-    w_msgs = [refs.pop(0) for _ in range(rows - 1)]
-    s_ref, w_out, h_out, own_ref, own_gram_ref = (refs.pop(0) for _ in range(5))
-    msg_refs = [refs.pop(0) for _ in range(subs - 1)]
-    sig_scr, old_scr, tab_scr, order_scr, xp_scr, x_scr, w_scr, num_scr, p_scr, sems, tab_sems = refs
-    rank, frames = old_scr.shape
+    halo_refs = [refs.pop(0) for _ in range(rows)]
+    s_ref, old_ref, w_ref, order_ref = (refs.pop(0) for _ in range(4))
+    sig_scr, tab_scr, xp_scr, x_scr, sems, tab_sems = refs
+    frames = old_ref.shape[1]
     window = sig_hbm.shape[1]
     width = sig_scr.shape[1]
-    per_sub = GROUPS // subs
-    wide = GROUP * cl
-    x_me, c_me = lax.axis_index("row"), lax.axis_index("sub")
+    x_me = lax.axis_index("row")
     depth = tab_scr.shape[0]
 
     def tab_copy(g):
@@ -138,16 +138,17 @@
 
     begin = pl.multiple_of(jnp.clip(x_me * frames - TAPS, 0, window - width), TAPS)
     sig_copy = pltpu.make_async_copy(sig_hbm.at[:, pl.ds(begin, width)], sig_scr, sems.at[0])
-    old_copy = pltpu.make_async_copy(
-        h_hbm.at[:, pl.ds(pl.multiple_of(x_me * frames, TAPS), frames)], old_scr, sems.at[1]
-    )
-    order_copy = pltpu.make_async_copy(order_hbm, order_scr, sems.at[2])
+    mine = pl.ds(pl.multiple_of(x_me * frames, TAPS), frames)
+    later = [
+        pltpu.make_async_copy(h_hbm.at[:, mine], old_ref, sems.at[1]),
+        pltpu.make_async_copy(w_hbm, w_ref, sems.at[2]),
+        pltpu.make_async_copy(order_hbm, order_ref, sems.at[3]),
+    ]
     sig_copy.start()
     for g in range(depth - 1):
         tab_copy(g).start()
-    old_copy.start()
-    order_copy.start()
-    sig_copy.wait()
+    for copy in later:
+        copy.start()
 
     def place(source, owner):
         @pl.when(x_me == 0)
@@ -165,19 +166,20 @@
             def _():
                 xp_scr[owner] = source[:, HALF : HALF + frames + TAPS]
 
-    place(sig_scr, x_me)
     for shift in range(1, rows):
         place(sig_refs[shift - 1], lax.rem(x_me + rows - shift, rows))
+    sig_copy.wait()
+    place(sig_scr, x_me)
 
     @pl.when(x_me == 0)
     def _():
         for at in range(rows):
-            xp_scr[rows - 1 - at, :, :HALF] = halo_ref[at * cl : (at + 1) * cl, HALF:]
+            xp_scr[at, :, :HALF] = halo_refs[at][:, HALF:]
 
     @pl.when(x_me == rows - 1)
     def _():
         for at in range(rows):
-            xp_scr[(rows - at) % rows, :, frames + HALF :] = halo_ref[at * cl : (at + 1) * cl, :HALF]
+            xp_scr[rows - 1 - at, :, frames + HALF :] = halo_refs[at][:, :HALF]
 
     for blk in range(blocks):
         for x in range(rows):
@@ -201,14 +203,27 @@
         return carry
 
     lax.fori_loop(0, GROUPS, convolve, 0)
-
-    order_copy.wait()
+    for copy in later:
+        copy.wait()
+
+
+def first_kernel(rows, subs, cl, *refs):
+    refs = list(refs)
+    w_ref, gram_ref = (refs.pop(0) for _ in range(2))
+    w_msgs = [refs.pop(0) for _ in range(rows - 1)]
+    order_ref, h_ref, s_ref = (refs.pop(0) for _ in range(3))
+    w_out, h_out, h_gram_ref = (refs.pop(0) for _ in range(3))
+    msg_refs, (w_scr, num_scr) = refs[: subs - 1], refs[subs - 1 :]
+    rank = h_ref.shape[0]
+    per_sub = GROUPS // subs
+    wide = GROUP * cl
+    x_me, c_me = lax.axis_index("row"), lax.axis_index("sub")
     w = w_ref[...]
     top = w.astype(BF16)
     rest = w - top.astype(F32)
     middle = rest.astype(BF16)
     terms = [top, middle, (rest - middle.astype(F32)).astype(BF16)] + [ref[:, : NF * cl] for ref in w_msgs]
-    moved = jnp.dot(jnp.concatenate(terms, axis=0), order_scr[...], preferred_element_type=F32)
+    moved = jnp.dot(jnp.concatenate(terms, axis=0), order_ref[...], preferred_element_type=F32)
     for at in range(GROUPS):
         cols = slice(at * wide, (at + 1) * wide)
         w_scr[at // per_sub, at % per_sub, x_me] = moved[:rank, cols].astype(BF16)
@@ -227,19 +242,15 @@
     gram = gram_ref[...]
     for ref in w_msgs:
         gram = gram + joined(ref, NF * cl, rank)
-    old_copy.wait()
-    finish_update(
-        old_scr[...], gram, w_scr, num_scr, s_ref, p_scr, h_out, own_ref, own_gram_ref, msg_refs, rows, subs, cl
-    )
-
-
-def later_kernel(rows, subs, cl, blocks, *refs):
+    new_activations(h_ref[...], gram, w_scr, num_scr, s_ref, h_out, h_gram_ref, msg_refs, rows, subs, cl)
+
+
+def later_kernel(rows, subs, cl, *refs):
     refs = list(refs)
     w_refs = [refs.pop(0) for _ in range(rows * subs)]
     h_ref, s_ref = refs.pop(0), refs.pop(0)
-    h_out, own_ref, own_gram_ref = (refs.pop(0) for _ in range(3))
-    msg_refs = [refs.pop(0) for _ in range(subs - 1)]
-    w_scr, num_scr, p_scr = refs
+    h_out, h_gram_ref = (refs.pop(0) for _ in range(2))
+    msg_refs, (w_scr, num_scr) = refs[: subs - 1], refs[subs - 1 :]
     rank = h_ref.shape[0]
     per_sub = GROUPS // subs
     wide = GROUP * cl
@@ -253,9 +264,7 @@
                 w_scr[c_of, part, x_of] = w_refs[at][:, part * wide : (part + 1) * wide]
             gram = gram + joined(w_refs[at], per_sub * wide, rank)
             at += 1
-    finish_update(
-        h_ref[...], gram, w_scr, num_scr, s_ref, p_scr, h_out, own_ref, own_gram_ref, msg_refs, rows, subs, cl
-    )
+    new_activations(h_ref[...], gram, w_scr, num_scr, s_ref, h_out, h_gram_ref, msg_refs, rows, subs, cl)
 
 
 def core_kernel(rows, subs, *refs):
@@ -331,22 +340,30 @@
             out_ref[...] = moved[:rank] + (moved[rank : 2 * rank] + moved[2 * rank :])
 
 
-def join_kernel(rows, *refs):
-    own_refs, (out_ref, sems) = refs[:rows], refs[rows:]
-    frames = own_refs[0].shape[1]
+def join_kernel(rows, subs, *refs):
+    act_refs, parts, (syn_ref, out_ref, scr, sems) = refs[:rows], refs[rows : rows + subs], refs[rows + subs :]
+    frames = act_refs[0].shape[1]
     x_me = lax.axis_index("row")
     copies = []
     for shift in range(rows):
         begin = pl.multiple_of(lax.rem(x_me + rows - shift, rows) * frames, TAPS)
-        copies.append(pltpu.make_async_copy(own_refs[shift], out_ref.at[:, pl.ds(begin, frames)], sems.at[shift]))
+        copies.append(pltpu.make_async_copy(act_refs[shift], out_ref.at[:, pl.ds(begin, frames)], sems.at[shift]))
     for copy in copies:
         copy.start()
+    total = parts[0][...]
+    for part in parts[1:]:
+        total = total + part[...]
+    scr[...] = total
+    copies.append(pltpu.make_async_copy(scr, syn_ref, sems.at[rows]))
+    copies[-1].start()
     for copy in copies:
         copy.wait()
 
 
-def call(kernel, args, outs, scratch=(), in_specs=None, out_specs=None, limit=4):
+def call(kernel, args, outs, scratch=(), in_specs=None, out_specs=None, limit=4, cost=None):
     whole = pl.BlockSpec(memory_space=pltpu.VMEM)
+    if cost is not None:
+        cost = pl.CostEstimate(flops=cost, bytes_accessed=0, transcendentals=0)
     return pl.pallas_call(
         kernel,
         out_shape=[jax.ShapeDtypeStruct(*out) if isinstance(out, tuple) else out for out in outs],
@@ -354,6 +371,7 @@
         out_specs=out_specs or [whole] * len(outs),
         scratch_shapes=list(scratch),
         compiler_params=pltpu.CompilerParams(vmem_limit_bytes=limit * MIB),
+        cost_estimate=cost,
     )(*args)
 
 
@@ -403,56 +421,67 @@
         row_shift(lax.dynamic_slice_in_dim(signal, begin((x_me + shift) % rows), width, 1), shift)
         for shift in range(1, rows)
     ]
-    edge = jnp.where(x_me == 0, 0, window - TAPS)
-    got_edge = jnp.where(x_me == 0, 0, width - TAPS)
-    ends = [lax.dynamic_slice_in_dim(signal, edge, TAPS, 1)]
-    ends += [lax.dynamic_slice_in_dim(part, got_edge, TAPS, 1) for part in sig]
-    pairs = [(place(rows - 1, i), place(0, i + 1)) for i in range(line - 1)]
-    halo = lax.ppermute(
-        jnp.concatenate(ends, axis=0), ("frm", "row", "sub"), pairs + [(b, a) for a, b in pairs]
-    )
+    tail, head = signal[:, window - TAPS :], signal[:, :TAPS]
+    halos = [None] * rows
+    for at in reversed(range(rows)):
+        to_next = [(place(at, i), place(0, i + 1)) for i in range(line - 1)]
+        to_prev = [(place(rows - 1 - at, i + 1), place(rows - 1, i)) for i in range(line - 1)]
+        halos[at] = lax.ppermute(jnp.where(x_me == at, tail, head), ("frm", "row", "sub"), to_next + to_prev)
 
     w_cols = w_start.T
     w_msg, w_gram = call(
-        prepare_kernel, [w_cols], [((rank, NF * cl + 2 * rank), BF16), ((rank, rank), F32)]
+        prepare_kernel,
+        [w_cols] + sig,
+        [((rank, NF * cl + 2 * rank), BF16), ((rank, rank), F32)],
+        in_specs=[whole] + [anywhere] * len(sig),
     )
     w_msgs = [row_shift(w_msg, shift) for shift in range(1, rows)]
 
     msg = ((rank, size + 2 * rank), BF16)
     piece = ((rank, size), F32)
-    tail_outs = [((rank, frames), F32), ((rows,) + piece[0], F32), ((rank, rank), F32)]
-    tail_outs += [((rows, rank, size + rank), F32)] * (subs - 1)
-    tail_scratch = [
+    update_outs = [((rank, frames), F32), ((rank, rank), F32)]
+    update_outs += [((rows, rank, size + rank), F32)] * (subs - 1)
+    update_scratch = [
         pltpu.VMEM((subs, GROUPS // subs, rows, rank, GROUP * cl), BF16),
         pltpu.VMEM((rank, frames), F32),
-        pltpu.VMEM((subs, rows) + piece[0], F32),
     ]
     order = jnp.asarray(reorder(cl))
-    held = [hbm(signal), hbm(h_start), hbm(jnp.asarray(toeplitz())), hbm(order)]
-    rest = sig + [halo, w_cols, w_gram] + w_msgs
-    spectra, w_piece, activations, own, own_gram, *msgs = call(
-        functools.partial(first_kernel, rows, subs, cl, blocks),
-        held + rest,
-        [pltpu.VMEM((NF, blocks, chans, TAPS), BF16), piece] + tail_outs,
+    held = [hbm(signal), hbm(h_start), hbm(w_cols), hbm(jnp.asarray(toeplitz())), hbm(order)]
+    macs = NF * chans * frames * rank
+    spectra, old, w_own, order = call(
+        functools.partial(spectra_kernel, rows, cl, blocks),
+        held + sig + halos,
+        [
+            pltpu.VMEM((NF, blocks, chans, TAPS), BF16),
+            pltpu.VMEM((rank, frames), F32),
+            pltpu.VMEM((rank, NF * cl), F32),
+            pltpu.VMEM(order.shape, BF16),
+        ],
         [
             pltpu.VMEM((cl, width), BF16),
-            pltpu.VMEM((rank, frames), F32),
             pltpu.VMEM((3, GROUP, 2 * TAPS, 2 * TAPS), BF16),
-            pltpu.VMEM(order.shape, BF16),
             pltpu.VMEM((rows, cl, frames + TAPS), BF16),
             pltpu.VMEM((blocks, chans, 2 * TAPS), BF16),
-        ]
-        + tail_scratch
-        + [pltpu.SemaphoreType.DMA((3,)), pltpu.SemaphoreType.DMA((3,))],
-        in_specs=[anywhere] * len(held) + [whole] * len(rest),
-        limit=24,
-    )
-
-    def gathered(own, own_gram, msgs):
+            pltpu.SemaphoreType.DMA((4,)),
+            pltpu.SemaphoreType.DMA((3,)),
+        ],
+        in_specs=[anywhere] * len(held) + [whole] * (len(sig) + len(halos)),
+        limit=12,
+        cost=2 * NF * chans * frames * 4 * TAPS,
+    )
+    spectra, order = vmem(spectra), vmem(order)
+
+    def gathered(activations, h_gram, msgs):
         got = [sub_shift(m, dc + 1) for dc, m in enumerate(msgs)]
+        (own,) = call(
+            functools.partial(own_kernel, rows, subs, cl),
+            [activations, spectra],
+            [((rows,) + piece[0], F32)],
+            cost=16 * macs // subs,
+        )
         part, gram, *outs = call(
             functools.partial(core_kernel, rows, subs),
-            [own, own_gram] + got,
+            [own, h_gram] + got,
             [piece, ((rank, rank), F32)] + [msg] * (rows - 1),
             [pltpu.VMEM((rows,) + piece[0], F32)],
         )
@@ -460,38 +489,44 @@
         (part,) = call(row_kernel, [part, gram] + got, [msg])
         return [part] + [frm_shift(part, shift) for shift in range(1, frms)]
 
+    w_piece, activations, h_gram, *msgs = call(
+        functools.partial(first_kernel, rows, subs, cl),
+        [vmem(w_own), w_gram] + w_msgs + [order, vmem(old), spectra],
+        [piece] + update_outs,
+        update_scratch,
+        limit=8,
+    )
     piled = [pltpu.VMEM((frms,) + msg[0], BF16)]
     w_piece, w_msg = call(
-        functools.partial(update_kernel, frms), [w_piece] + gathered(own, own_gram, msgs), [piece, msg], piled
+        functools.partial(update_kernel, frms),
+        [w_piece] + gathered(activations, h_gram, msgs),
+        [piece, msg],
+        piled,
     )
     w_msgs = []
     for dx in range(rows):
         base = row_shift(w_msg, dx) if dx else w_msg
         w_msgs += [base] + [sub_shift(base, dc) for dc in range(1, subs)]
-    activations, own, own_gram, *msgs = call(
-        functools.partial(later_kernel, rows, subs, cl, blocks),
-        w_msgs + [activations, vmem(spectra)],
-        tail_outs,
-        tail_scratch,
+    activations, h_gram, *msgs = call(
+        functools.partial(later_kernel, rows, subs, cl),
+        w_msgs + [activations, spectra],
+        update_outs,
+        update_scratch,
         limit=8,
     )
+    parts = gathered(activations, h_gram, msgs)
+    activations, parts[0] = lax.optimization_barrier((activations, parts[0]))
+    sides = [activations] + [row_shift(activations, shift) for shift in range(1, rows)]
     (part,) = call(
-        functools.partial(last_kernel, frms),
-        [w_piece, vmem(order)] + gathered(own, own_gram, msgs),
-        [((rank, NF * cl), F32)],
-        piled,
-    )
-    synergies = part
-    for dc in range(1, subs):
-        synergies = synergies + sub_shift(part, dc)
-
-    (wide,) = call(
-        functools.partial(join_kernel, rows),
-        [activations] + [row_shift(activations, shift) for shift in range(1, rows)],
-        [pltpu.HBM((rank, window), F32)],
-        [pltpu.SemaphoreType.DMA((rows,))],
-        in_specs=[anywhere] * rows,
-        out_specs=[anywhere],
+        functools.partial(last_kernel, frms), [w_piece, order] + parts, [((rank, NF * cl), F32)], piled
+    )
+    synergies, wide = call(
+        functools.partial(join_kernel, rows, subs),
+        sides + [part] + [sub_shift(part, dc) for dc in range(1, subs)],
+        [pltpu.HBM((rank, NF * cl), F32), pltpu.HBM((rank, window), F32)],
+        [pltpu.VMEM((rank, NF * cl), F32), pltpu.SemaphoreType.DMA((rows + 1,))],
+        in_specs=[anywhere] * rows + [whole] * subs,
+        out_specs=[anywhere] * 2,
     )
     return (synergies.T, wide)
 

time: 76.6 us -> 69 us (0.901)
  waiting for transfers between devices: 25.5 us -> 18.6 us
  local copies, waits for them, and re-layouts: 3.56 us -> 1.93 us
    ppermute x6, waiting for transfers between devices: 15.3 us -> 8.62 us  [row_shift(): lax.ppermute(value, 'row', [(i, (i + shift) % rows) for i in range(rows)])]
    ppermute x1 -> x2, starting transfers between devices: 0.65 us -> 3.94 us  [shards(): lax.ppermute(jnp.where(x_me == at, tail, head), ('frm', 'row', 'sub'), to...]
    ppermute x5, starting transfers between devices: 4.38 us -> 2.32 us  [sub_shift(): lax.ppermute(value, 'sub', [(i, (i + shift) % subs) for i in range(subs)])]
    unnamed x6 -> x2, local copies, waits for them, and re-layouts: 1.84 us -> 0.91 us
    pallas_call x10 -> x13, Pallas kernels: 22.9 us -> 23.1 us  [call(): pl.pallas_call(kernel, out_shape=[jax.ShapeDtypeStruct(*out) if isinstanc...]
  transfers between devices with their start and end apart: 18 -> 19, of which waited for: 13 -> 9; matrix products, arithmetic and copies ran while one was open for 1% -> 1% of each run, Pallas kernels for 3% -> 19%
where the time goes in v3:
time: 69 us; the launch traced here: 68.7 us
  starting transfers between devices  23.6 us (34%)
  Pallas kernels  23.1 us (33%)
  waiting for transfers between devices  18.6 us (27%)
  local copies, waits for them, and re-layouts  1.93 us (3%)
  between operations  0.77 us (1%)
  other arithmetic  0.72 us (1%)
    pallas_call x13, Pallas kernels, call(): pl.pallas_call(kernel, out_shape=[jax.ShapeDtypeStruct(*out) if isinstanc...  23.1 us
    ppermute x6, starting transfers between devices, frm_shift(): lax.ppermute(value, 'frm', [(partner(i, shift, frms), i) for i in range(f...  8.78 us
    ppermute x6, waiting for transfers between devices, row_shift(): lax.ppermute(value, 'row', [(i, (i + shift) % rows) for i in range(rows)])  8.62 us
    ppermute x6, starting transfers between devices, row_shift(): lax.ppermute(value, 'row', [(i, (i + shift) % rows) for i in range(rows)])  8.59 us
    ppermute x6, waiting for transfers between devices, frm_shift(): lax.ppermute(value, 'frm', [(partner(i, shift, frms), i) for i in range(f...  7.36 us
    ppermute x2, starting transfers between devices, shards(): lax.ppermute(jnp.where(x_me == at, tail, head), ('frm', 'row', 'sub'), to...  3.94 us
    ppermute x5, waiting for transfers between devices, sub_shift(): lax.ppermute(value, 'sub', [(i, (i + shift) % subs) for i in range(subs)])  2.61 us
    ppermute x5, starting transfers between devices, sub_shift(): lax.ppermute(value, 'sub', [(i, (i + shift) % subs) for i in range(subs)])  2.32 us
  transfers between devices with their start and end apart: 19, of which 9 were waited for; matrix products, arithmetic and copies ran while one was open for 1% of the time, Pallas kernels for 19%

profile of v3, /device:TPU:0, one launch (start us, length us, event | category | flops | bytes accessed | tf_op | source)
XLA Modules:
  0.0 68.7 jit_solution(8258676496152133369)
XLA Ops:
  0.6 1.0 %constant_dynamic-slice_fusion = bf16[32,2176]{1,0:T(8,128)(2,1)S(1)} fusion(bf16[32,4096]{1,0:T(8,128)(2,1)} %refs_0_.1, s32[]{:T(128)S(6)} %min.4), kind=kLoop, calls=%fused_computation.2 | loop fusion | bytes 278532 | tf_op jit(solution)/shard_map/dynamic_slice | solution.py:421
  1.7 3.0 %collective-permute-start = (bf16[32,2176]{1,0:T(8,128)(2,1)S(1)}, bf16[32,2176]{1,0:T(8,128)(2,1)S(1)}, u32[]{:S(2)}, u32[]{:S(2)}) collective-permute-start(bf16[32,2176]{1,0:T(8,128)(2,1)S(1)} %constant_dynamic-slice_fusion), channel_id=1, source_target_pairs={{0,2},{2,0},{1,3},{3,1},{4,6},{6,4},{5,7},{7,5},{8,10},{10,8},{9,1... | collective-permute-start | bytes 417800 | tf_op jit(solution)/shard_map/ppermute | solution.py:406
  4.7 0.7 %broadcast_select_fusion = (bf16[32,128]{1,0:T(8,128)(2,1)S(1)}, bf16[32,128]{1,0:T(8,128)(2,1)S(1)}) fusion(pred[]{:T(512)S(6)} %eq.9, bf16[32,4096]{1,0:T(8,128)(2,1)} %refs_0_.1, pred[]{:T(512)S(6)} %eq.8), kind=kLoop, calls=%fused_computation | loop fusion | flops 8192 | bytes 32770 | tf_op jit(solution)/shard_map/jit(_where)/select_n | solution.py:429
  5.4 0.6 collective-permute-start.2
  6.1 3.3 %collective-permute-start.1 = (bf16[32,128]{1,0:T(8,128)(2,1)S(1)}, bf16[32,128]{1,0:T(8,128)(2,1)S(1)}, u32[]{:S(2)}, u32[]{:S(2)}) collective-permute-start(bf16[32,128]{1,0:T(8,128)(2,1)S(1)} %get-tuple-element.53), channel_id=1, source_target_pairs={{0,1},{1,4},{4,5},{5,8},{8,9},{9,12},{12,13},{3,2},{6,3},{7,6},{10... | collective-permute-start | bytes 24584 | tf_op jit(solution)/shard_map/ppermute | solution.py:429
  9.3 0.0 collective-permute-done.refs_5_.refs_0_
  9.4 0.0 copy-start
  9.4 0.9 %copy-done = f32[1280,32]{0,1:T(8,128)S(1)} copy-done((f32[1280,32]{0,1:T(8,128)S(1)}, f32[1280,32]{0,1:T(8,128)}, u32[]{:S(2)}) %copy-start) | copy-done | bytes 163864
  10.3 0.3 shard_map.69
  10.6 0.7 %collective-permute-start.3 = (bf16[32,1344]{1,0:T(8,128)(2,1)S(1)}, bf16[32,1344]{1,0:T(8,128)(2,1)S(1)}, u32[]{:S(2)}, u32[]{:S(2)}) collective-permute-start(bf16[32,1344]{1,0:T(8,128)(2,1)S(1)} %get-tuple-element.29), channel_id=1, source_target_pairs={{0,2},{2,0},{1,3},{3,1},{4,6},{6,4},{5,7},{7,5},{8,10},{10,8},{9,1... | collective-permute-start | bytes 258056 | tf_op jit(solution)/shard_map/ppermute | solution.py:406
  11.4 0.0 collective-permute-done.2.refs_7_
  11.4 0.0 collective-permute-done.1.refs_6_
  11.4 8.6 %shard_map.68 = (bf16[40,16,64,128]{3,2,1,0:T(8,128)(2,1)S(1)}, f32[32,2048]{1,0:T(8,128)S(1)}, f32[32,1280]{1,0:T(8,128)S(1)}, bf16[1280,1280]{1,0:T(8,128)(2,1)S(1)}) custom-call(bf16[32,4096]{1,0:T(8,128)(2,1)} %refs_0_.1, f32[32,4096]{1,0:T(8,128)} %refs_1_.1, f32[32,1280]{1,0:T(8,128)} %bitcast.2, bf16[40,256,256]{2,1,0:T(8,128)(2,1)} %constant.33.clone.refs_3_, ...), custom_call_target="tpu_custom_call" | custom-call | flops 5368709120 | tf_op jit(solution)/shard_map/pallas_call | solution.py:367
  20.0 0.0 collective-permute-done.3.refs_2_
  20.0 4.3 %shard_map.70 = (f32[32,640]{1,0:T(8,128)S(1)}, f32[32,2048]{1,0:T(8,128)S(1)}, f32[32,32]{1,0:T(8,128)S(1)}, f32[2,32,672]{2,1,0:T(8,128)S(1)}) custom-call(f32[32,1280]{1,0:T(8,128)S(1)} %get-tuple-element.27.refs_0_, f32[32,32]{1,0:T(8,128)S(1)} %get-tuple-element.28.refs_1_, bf16[32,1344]{1,0:T(8,128)(2,1)S(1)} %collective-permute-done.3.refs_2_, ...), custom_call_target="tpu_custom_call" | custom-call | tf_op jit(solution)/shard_map/pallas_call | solution.py:367
  24.4 2.1 %collective-permute-start.4 = (f32[2,32,672]{2,1,0:T(8,128)S(1)}, f32[2,32,672]{2,1,0:T(8,128)S(1)}, u32[]{:S(2)}, u32[]{:S(2)}) collective-permute-start(f32[2,32,672]{2,1,0:T(8,128)S(1)} %get-tuple-element.36), channel_id=1, source_target_pairs={{0,1},{1,0},{2,3},{3,2},{4,5},{5,4},{6,7},{7,6},{8,9},{9,8},{10,11... | collective-permute-start | bytes 516104 | tf_op jit(solution)/shard_map/ppermute | solution.py:409
  26.4 1.6 %shard_map.71.refs_0_ = f32[2,32,640]{2,1,0:T(8,128)S(1)} custom-call(f32[32,2048]{1,0:T(8,128)S(1)} %get-tuple-element.34.h_ref.refs_4_, bf16[40,16,64,128]{3,2,1,0:T(8,128)(2,1)S(1)} %get-tuple-element.32.refs_5_.s_ref), custom_call_target="tpu_custom_call" | custom-call | flops 1342177280 | tf_op jit(solution)/shard_map/pallas_call | solution.py:367
  28.0 0.0 collective-permute-done.4.refs_2_
  28.1 0.1 shard_map.72
  28.1 2.4 %collective-permute-start.5 = (bf16[32,704]{1,0:T(8,128)(2,1)S(1)}, bf16[32,704]{1,0:T(8,128)(2,1)S(1)}, u32[]{:S(2)}, u32[]{:S(2)}) collective-permute-start(bf16[32,704]{1,0:T(8,128)(2,1)S(1)} %get-tuple-element.39), channel_id=1, source_target_pairs={{0,2},{2,0},{1,3},{3,1},{4,6},{6,4},{5,7},{7,5},{8,10},{10,8},{9,1... | collective-permute-start | bytes 135176 | tf_op jit(solution)/shard_map/ppermute | solution.py:406
  30.5 2.1 %collective-permute-done.5.refs_2_ = bf16[32,704]{1,0:T(8,128)(2,1)S(1)} collective-permute-done((bf16[32,704]{1,0:T(8,128)(2,1)S(1)}, bf16[32,704]{1,0:T(8,128)(2,1)S(1)}, u32[]{:S(2)}, u32[]{:S(2)}) %collective-permute-start.5) | collective-permute-done | bytes 45088 | tf_op jit(solution)/shard_map/ppermute | solution.py:406
  32.6 0.2 shard_map.73.refs_0_
  32.7 3.7 %collective-permute-start.8 = (bf16[32,704]{1,0:T(8,128)(2,1)S(1)}, bf16[32,704]{1,0:T(8,128)(2,1)S(1)}, u32[]{:S(2)}, u32[]{:S(2)}) collective-permute-start(bf16[32,704]{1,0:T(8,128)(2,1)S(1)} %shard_map.73.refs_0_), channel_id=1, source_target_pairs={{12,0},{8,4},{4,8},{0,12},{13,1},{9,5},{5,9},{1,13},{14,2},{10,6},... | collective-permute-start | bytes 135176 | tf_op jit(solution)/shard_map/ppermute | solution.py:412
  36.4 0.0 collective-permute-start.7
  36.4 0.7 %collective-permute-start.6 = (bf16[32,704]{1,0:T(8,128)(2,1)S(1)}, bf16[32,704]{1,0:T(8,128)(2,1)S(1)}, u32[]{:S(2)}, u32[]{:S(2)}) collective-permute-start(bf16[32,704]{1,0:T(8,128)(2,1)S(1)} %shard_map.73.refs_0_), channel_id=1, source_target_pairs={{4,0},{0,4},{12,8},{8,12},{5,1},{1,5},{13,9},{9,13},{6,2},{2,6},{1... | collective-permute-start | bytes 135176 | tf_op jit(solution)/shard_map/ppermute | solution.py:412
  37.1 1.8 %collective-permute-done.8.refs_3_ = bf16[32,704]{1,0:T(8,128)(2,1)S(1)} collective-permute-done((bf16[32,704]{1,0:T(8,128)(2,1)S(1)}, bf16[32,704]{1,0:T(8,128)(2,1)S(1)}, u32[]{:S(2)}, u32[]{:S(2)}) %collective-permute-start.8) | collective-permute-done | bytes 45088 | tf_op jit(solution)/shard_map/ppermute | solution.py:412
  38.9 2.5 %collective-permute-done.7.refs_2_ = bf16[32,704]{1,0:T(8,128)(2,1)S(1)} collective-permute-done((bf16[32,704]{1,0:T(8,128)(2,1)S(1)}, bf16[32,704]{1,0:T(8,128)(2,1)S(1)}, u32[]{:S(2)}, u32[]{:S(2)}) %collective-permute-start.7) | collective-permute-done | bytes 45088 | tf_op jit(solution)/shard_map/ppermute | solution.py:412
  41.4 0.0 collective-permute-done.6.refs_1_
  41.4 0.6 shard_map.74
  42.0 0.8 %collective-permute-start.10 = (bf16[32,704]{1,0:T(8,128)(2,1)S(1)}, bf16[32,704]{1,0:T(8,128)(2,1)S(1)}, u32[]{:S(2)}, u32[]{:S(2)}) collective-permute-start(bf16[32,704]{1,0:T(8,128)(2,1)S(1)} %get-tuple-element.40.refs_0_), channel_id=1, source_target_pairs={{0,2},{2,0},{1,3},{3,1},{4,6},{6,4},{5,7},{7,5},{8,10},{10,8},{9,1... | collective-permute-start | bytes 135176 | tf_op jit(solution)/shard_map/ppermute | solution.py:406
  42.8 0.0 collective-permute-start.9
  42.8 3.3 %collective-permute-done.10.refs_2_ = bf16[32,704]{1,0:T(8,128)(2,1)S(1)} collective-permute-done((bf16[32,704]{1,0:T(8,128)(2,1)S(1)}, bf16[32,704]{1,0:T(8,128)(2,1)S(1)}, u32[]{:S(2)}, u32[]{:S(2)}) %collective-permute-start.10) | collective-permute-done | bytes 45088 | tf_op jit(solution)/shard_map/ppermute | solution.py:406
  46.1 0.0 collective-permute-start.11
  46.1 0.0 collective-permute-done.9.refs_1_
  46.1 1.2 %collective-permute-done.11.refs_3_ = bf16[32,704]{1,0:T(8,128)(2,1)S(1)} collective-permute-done((bf16[32,704]{1,0:T(8,128)(2,1)S(1)}, bf16[32,704]{1,0:T(8,128)(2,1)S(1)}, u32[]{:S(2)}, u32[]{:S(2)}) %collective-permute-start.11) | collective-permute-done | bytes 45088 | tf_op jit(solution)/shard_map/ppermute | solution.py:409
  47.3 3.7 %shard_map.75 = (f32[32,2048]{1,0:T(8,128)S(1)}, f32[32,32]{1,0:T(8,128)S(1)}, f32[2,32,672]{2,1,0:T(8,128)S(1)}) custom-call(bf16[32,704]{1,0:T(8,128)(2,1)S(1)} %get-tuple-element.40.refs_0_, bf16[32,704]{1,0:T(8,128)(2,1)S(1)} %collective-permute-done.9.refs_1_, bf16[32,704]{1,0:T(8,128)(2,1)S(1)} %collective-permute-done.10.refs_2_, ...), custom_call_target="tpu_custom_call" | custom-call | tf_op jit(solution)/shard_map/pallas_call | solution.py:367
  51.0 0.2 collective-permute-start.12
  51.2 1.6 %shard_map.76.refs_0_ = f32[2,32,640]{2,1,0:T(8,128)S(1)} custom-call(f32[32,2048]{1,0:T(8,128)S(1)} %get-tuple-element.47.h_ref.refs_0_, bf16[40,16,64,128]{3,2,1,0:T(8,128)(2,1)S(1)} %get-tuple-element.32.refs_5_.s_ref), custom_call_target="tpu_custom_call" | custom-call | flops 1342177280 | tf_op jit(solution)/shard_map/pallas_call | solution.py:367
  52.8 0.0 collective-permute-done.12.refs_2_
  52.8 0.1 shard_map.77
  52.9 0.9 %collective-permute-start.13 = (bf16[32,704]{1,0:T(8,128)(2,1)S(1)}, bf16[32,704]{1,0:T(8,128)(2,1)S(1)}, u32[]{:S(2)}, u32[]{:S(2)}) collective-permute-start(bf16[32,704]{1,0:T(8,128)(2,1)S(1)} %get-tuple-element.46), channel_id=1, source_target_pairs={{0,2},{2,0},{1,3},{3,1},{4,6},{6,4},{5,7},{7,5},{8,10},{10,8},{9,1... | collective-permute-start | bytes 135176 | tf_op jit(solution)/shard_map/ppermute | solution.py:406
  53.8 3.3 %collective-permute-done.13.refs_2_ = bf16[32,704]{1,0:T(8,128)(2,1)S(1)} collective-permute-done((bf16[32,704]{1,0:T(8,128)(2,1)S(1)}, bf16[32,704]{1,0:T(8,128)(2,1)S(1)}, u32[]{:S(2)}, u32[]{:S(2)}) %collective-permute-start.13) | collective-permute-done | bytes 45088 | tf_op jit(solution)/shard_map/ppermute | solution.py:406
  57.0 0.2 shard_map.78.refs_0_
  57.2 0.8 %collective-permute-start.14 = (f32[32,2048]{1,0:T(8,128)S(1)}, f32[32,2048]{1,0:T(8,128)S(1)}, u32[]{:S(2)}, u32[]{:S(2)}) collective-permute-start(f32[32,2048]{1,0:T(8,128)S(1)} %get-tuple-element.47.h_ref.refs_0_), channel_id=1, source_target_pairs={{0,2},{2,0},{1,3},{3,1},{4,6},{6,4},{5,7},{7,5},{8,10},{10,8},{9,1... | collective-permute-start | bytes 786440 | tf_op jit(solution)/shard_map/ppermute | solution.py:406
  58.0 2.4 %collective-permute-start.17 = (bf16[32,704]{1,0:T(8,128)(2,1)S(1)}, bf16[32,704]{1,0:T(8,128)(2,1)S(1)}, u32[]{:S(2)}, u32[]{:S(2)}) collective-permute-start(bf16[32,704]{1,0:T(8,128)(2,1)S(1)} %shard_map.78.refs_0_), channel_id=1, source_target_pairs={{12,0},{8,4},{4,8},{0,12},{13,1},{9,5},{5,9},{1,13},{14,2},{10,6},... | collective-permute-start | bytes 135176 | tf_op jit(solution)/shard_map/ppermute | solution.py:412
  60.4 0.1 collective-permute-start.16
  60.5 1.9 %collective-permute-start.15 = (bf16[32,704]{1,0:T(8,128)(2,1)S(1)}, bf16[32,704]{1,0:T(8,128)(2,1)S(1)}, u32[]{:S(2)}, u32[]{:S(2)}) collective-permute-start(bf16[32,704]{1,0:T(8,128)(2,1)S(1)} %shard_map.78.refs_0_), channel_id=1, source_target_pairs={{4,0},{0,4},{12,8},{8,12},{5,1},{1,5},{13,9},{9,13},{6,2},{2,6},{1... | collective-permute-start | bytes 135176 | tf_op jit(solution)/shard_map/ppermute | solution.py:412
  62.4 1.7 %collective-permute-done.17.refs_3_ = bf16[32,704]{1,0:T(8,128)(2,1)S(1)} collective-permute-done((bf16[32,704]{1,0:T(8,128)(2,1)S(1)}, bf16[32,704]{1,0:T(8,128)(2,1)S(1)}, u32[]{:S(2)}, u32[]{:S(2)}) %collective-permute-start.17) | collective-permute-done | bytes 45088 | tf_op jit(solution)/shard_map/ppermute | solution.py:412
  64.1 1.4 %collective-permute-done.16.refs_2_ = bf16[32,704]{1,0:T(8,128)(2,1)S(1)} collective-permute-done((bf16[32,704]{1,0:T(8,128)(2,1)S(1)}, bf16[32,704]{1,0:T(8,128)(2,1)S(1)}, u32[]{:S(2)}, u32[]{:S(2)}) %collective-permute-start.16) | collective-permute-done | bytes 45088 | tf_op jit(solution)/shard_map/ppermute | solution.py:412
  65.5 0.0 collective-permute-done.15.refs_1_
  65.5 0.9 %shard_map.79.refs_2_ = f32[32,1280]{1,0:T(8,128)S(1)} custom-call(f32[32,640]{1,0:T(8,128)S(1)} %get-tuple-element.48.w_ref, bf16[1280,1280]{1,0:T(8,128)(2,1)S(1)} %get-tuple-element.30.refs_3_.order_ref, bf16[32,704]{1,0:T(8,128)(2,1)S(1)} %shard_map.78.refs_0_, bf16[32,704]{1,0:T(8,128)(2,1)S(1)} %collective-permute-done.15.refs_1_, ...), custom_call_target="tpu_custom_call" | custom-call | tf_op jit(solution)/shard_map/pallas_call | solution.py:367
  66.4 0.1 collective-permute-start.18
  66.5 1.4 %collective-permute-done.18.refs_3_ = f32[32,1280]{1,0:T(8,128)S(1)} collective-permute-done((f32[32,1280]{1,0:T(8,128)S(1)}, f32[32,1280]{1,0:T(8,128)S(1)}, u32[]{:S(2)}, u32[]{:S(2)}) %collective-permute-start.18) | collective-permute-done | bytes 163872 | tf_op jit(solution)/shard_map/ppermute | solution.py:409
  67.8 0.0 collective-permute-done.14.refs_1_
  67.9 0.9 %shard_map.80 = (f32[32,1280]{1,0:T(8,128)}, f32[32,4096]{1,0:T(8,128)}) custom-call(f32[32,2048]{1,0:T(8,128)S(1)} %get-tuple-element.47.h_ref.refs_0_, f32[32,2048]{1,0:T(8,128)S(1)} %collective-permute-done.14.refs_1_, f32[32,1280]{1,0:T(8,128)S(1)} %shard_map.79.refs_2_, f32[32,1280]{1,0:T(8,128)S(1)} %collective-permute-done.18.refs_3_), custom_call_target="tpu_custom_call" | custom-call | tf_op jit(solution)/shard_map/pallas_call | solution.py:367
Async XLA Ops:
  1.7 7.7 %collective-permute-start = (bf16[32,2176]{1,0:T(8,128)(2,1)S(1)}, bf16[32,2176]{1,0:T(8,128)(2,1)S(1)}, u32[]{:S(2)}, u32[]{:S(2)}) collective-permute-start(bf16[32,2176]{1,0:T(8,128)(2,1)S(1)} %constant_dynamic-slice_fusion), channel_id=1, source_target_pairs={{0,2},{2,0},{1,3},{3,1},{4,6},{6,4},{5,7},{7,5},{8,10},{10,8},{9,1... | collective-permute-start | bytes 417800 | tf_op jit(solution)/shard_map/ppermute | solution.py:406
  5.4 6.0 %collective-permute-start.2 = (bf16[32,128]{1,0:T(8,128)(2,1)S(1)}, bf16[32,128]{1,0:T(8,128)(2,1)S(1)}, u32[]{:S(2)}, u32[]{:S(2)}) collective-permute-start(bf16[32,128]{1,0:T(8,128)(2,1)S(1)} %get-tuple-element.52), channel_id=1, source_target_pairs={{2,1},{3,4},{6,5},{7,8},{10,9},{11,12},{14,13},{1,2},{4,3},{5,6},{... | collective-permute-start | bytes 24584 | tf_op jit(solution)/shard_map/ppermute | solution.py:429
  6.1 5.3 %collective-permute-start.1 = (bf16[32,128]{1,0:T(8,128)(2,1)S(1)}, bf16[32,128]{1,0:T(8,128)(2,1)S(1)}, u32[]{:S(2)}, u32[]{:S(2)}) collective-permute-start(bf16[32,128]{1,0:T(8,128)(2,1)S(1)} %get-tuple-element.53), channel_id=1, source_target_pairs={{0,1},{1,4},{4,5},{5,8},{8,9},{9,12},{12,13},{3,2},{6,3},{7,6},{10... | collective-permute-start | bytes 24584 | tf_op jit(solution)/shard_map/ppermute | solution.py:429
  9.4 0.9 %copy-start = (f32[1280,32]{0,1:T(8,128)S(1)}, f32[1280,32]{0,1:T(8,128)}, u32[]{:S(2)}) copy-start(f32[1280,32]{0,1:T(8,128)} %param.6) | copy-start | bytes 491524
  10.6 9.4 %collective-permute-start.3 = (bf16[32,1344]{1,0:T(8,128)(2,1)S(1)}, bf16[32,1344]{1,0:T(8,128)(2,1)S(1)}, u32[]{:S(2)}, u32[]{:S(2)}) collective-permute-start(bf16[32,1344]{1,0:T(8,128)(2,1)S(1)} %get-tuple-element.29), channel_id=1, source_target_pairs={{0,2},{2,0},{1,3},{3,1},{4,6},{6,4},{5,7},{7,5},{8,10},{10,8},{9,1... | collective-permute-start | bytes 258056 | tf_op jit(solution)/shard_map/ppermute | solution.py:406
  24.4 3.7 %collective-permute-start.4 = (f32[2,32,672]{2,1,0:T(8,128)S(1)}, f32[2,32,672]{2,1,0:T(8,128)S(1)}, u32[]{:S(2)}, u32[]{:S(2)}) collective-permute-start(f32[2,32,672]{2,1,0:T(8,128)S(1)} %get-tuple-element.36), channel_id=1, source_target_pairs={{0,1},{1,0},{2,3},{3,2},{4,5},{5,4},{6,7},{7,6},{8,9},{9,8},{10,11... | collective-permute-start | bytes 516104 | tf_op jit(solution)/shard_map/ppermute | solution.py:409
  28.1 4.4 %collective-permute-start.5 = (bf16[32,704]{1,0:T(8,128)(2,1)S(1)}, bf16[32,704]{1,0:T(8,128)(2,1)S(1)}, u32[]{:S(2)}, u32[]{:S(2)}) collective-permute-start(bf16[32,704]{1,0:T(8,128)(2,1)S(1)} %get-tuple-element.39), channel_id=1, source_target_pairs={{0,2},{2,0},{1,3},{3,1},{4,6},{6,4},{5,7},{7,5},{8,10},{10,8},{9,1... | collective-permute-start | bytes 135176 | tf_op jit(solution)/shard_map/ppermute | solution.py:406
  32.7 6.2 %collective-permute-start.8 = (bf16[32,704]{1,0:T(8,128)(2,1)S(1)}, bf16[32,704]{1,0:T(8,128)(2,1)S(1)}, u32[]{:S(2)}, u32[]{:S(2)}) collective-permute-start(bf16[32,704]{1,0:T(8,128)(2,1)S(1)} %shard_map.73.refs_0_), channel_id=1, source_target_pairs={{12,0},{8,4},{4,8},{0,12},{13,1},{9,5},{5,9},{1,13},{14,2},{10,6},... | collective-permute-start | bytes 135176 | tf_op jit(solution)/shard_map/ppermute | solution.py:412
  36.4 5.0 %collective-permute-start.7 = (bf16[32,704]{1,0:T(8,128)(2,1)S(1)}, bf16[32,704]{1,0:T(8,128)(2,1)S(1)}, u32[]{:S(2)}, u32[]{:S(2)}) collective-permute-start(bf16[32,704]{1,0:T(8,128)(2,1)S(1)} %shard_map.73.refs_0_), channel_id=1, source_target_pairs={{8,0},{12,4},{0,8},{4,12},{9,1},{13,5},{1,9},{5,13},{10,2},{14,6},... | collective-permute-start | bytes 135176 | tf_op jit(solution)/shard_map/ppermute | solution.py:412
  36.4 5.0 %collective-permute-start.6 = (bf16[32,704]{1,0:T(8,128)(2,1)S(1)}, bf16[32,704]{1,0:T(8,128)(2,1)S(1)}, u32[]{:S(2)}, u32[]{:S(2)}) collective-permute-start(bf16[32,704]{1,0:T(8,128)(2,1)S(1)} %shard_map.73.refs_0_), channel_id=1, source_target_pairs={{4,0},{0,4},{12,8},{8,12},{5,1},{1,5},{13,9},{9,13},{6,2},{2,6},{1... | collective-permute-start | bytes 135176 | tf_op jit(solution)/shard_map/ppermute | solution.py:412
  42.0 4.1 %collective-permute-start.10 = (bf16[32,704]{1,0:T(8,128)(2,1)S(1)}, bf16[32,704]{1,0:T(8,128)(2,1)S(1)}, u32[]{:S(2)}, u32[]{:S(2)}) collective-permute-start(bf16[32,704]{1,0:T(8,128)(2,1)S(1)} %get-tuple-element.40.refs_0_), channel_id=1, source_target_pairs={{0,2},{2,0},{1,3},{3,1},{4,6},{6,4},{5,7},{7,5},{8,10},{10,8},{9,1... | collective-permute-start | bytes 135176 | tf_op jit(solution)/shard_map/ppermute | solution.py:406
  42.8 3.3 %collective-permute-start.9 = (bf16[32,704]{1,0:T(8,128)(2,1)S(1)}, bf16[32,704]{1,0:T(8,128)(2,1)S(1)}, u32[]{:S(2)}, u32[]{:S(2)}) collective-permute-start(bf16[32,704]{1,0:T(8,128)(2,1)S(1)} %get-tuple-element.40.refs_0_), channel_id=1, source_target_pairs={{0,1},{1,0},{2,3},{3,2},{4,5},{5,4},{6,7},{7,6},{8,9},{9,8},{10,11... | collective-permute-start | bytes 135176 | tf_op jit(solution)/shard_map/ppermute | solution.py:409
  46.1 1.2 %collective-permute-start.11 = (bf16[32,704]{1,0:T(8,128)(2,1)S(1)}, bf16[32,704]{1,0:T(8,128)(2,1)S(1)}, u32[]{:S(2)}, u32[]{:S(2)}) collective-permute-start(bf16[32,704]{1,0:T(8,128)(2,1)S(1)} %collective-permute-done.10.refs_2_), channel_id=1, source_target_pairs={{0,1},{1,0},{2,3},{3,2},{4,5},{5,4},{6,7},{7,6},{8,9},{9,8},{10,11... | collective-permute-start | bytes 135176 | tf_op jit(solution)/shard_map/ppermute | solution.py:409
  51.0 1.8 %collective-permute-start.12 = (f32[2,32,672]{2,1,0:T(8,128)S(1)}, f32[2,32,672]{2,1,0:T(8,128)S(1)}, u32[]{:S(2)}, u32[]{:S(2)}) collective-permute-start(f32[2,32,672]{2,1,0:T(8,128)S(1)} %get-tuple-element.43), channel_id=1, source_target_pairs={{0,1},{1,0},{2,3},{3,2},{4,5},{5,4},{6,7},{7,6},{8,9},{9,8},{10,11... | collective-permute-start | bytes 516104 | tf_op jit(solution)/shard_map/ppermute | solution.py:409
  52.9 4.1 %collective-permute-start.13 = (bf16[32,704]{1,0:T(8,128)(2,1)S(1)}, bf16[32,704]{1,0:T(8,128)(2,1)S(1)}, u32[]{:S(2)}, u32[]{:S(2)}) collective-permute-start(bf16[32,704]{1,0:T(8,128)(2,1)S(1)} %get-tuple-element.46), channel_id=1, source_target_pairs={{0,2},{2,0},{1,3},{3,1},{4,6},{6,4},{5,7},{7,5},{8,10},{10,8},{9,1... | collective-permute-start | bytes 135176 | tf_op jit(solution)/shard_map/ppermute | solution.py:406
  57.2 10.7 %collective-permute-start.14 = (f32[32,2048]{1,0:T(8,128)S(1)}, f32[32,2048]{1,0:T(8,128)S(1)}, u32[]{:S(2)}, u32[]{:S(2)}) collective-permute-start(f32[32,2048]{1,0:T(8,128)S(1)} %get-tuple-element.47.h_ref.refs_0_), channel_id=1, source_target_pairs={{0,2},{2,0},{1,3},{3,1},{4,6},{6,4},{5,7},{7,5},{8,10},{10,8},{9,1... | collective-permute-start | bytes 786440 | tf_op jit(solution)/shard_map/ppermute | solution.py:406
  58.0 6.1 %collective-permute-start.17 = (bf16[32,704]{1,0:T(8,128)(2,1)S(1)}, bf16[32,704]{1,0:T(8,128)(2,1)S(1)}, u32[]{:S(2)}, u32[]{:S(2)}) collective-permute-start(bf16[32,704]{1,0:T(8,128)(2,1)S(1)} %shard_map.78.refs_0_), channel_id=1, source_target_pairs={{12,0},{8,4},{4,8},{0,12},{13,1},{9,5},{5,9},{1,13},{14,2},{10,6},... | collective-permute-start | bytes 135176 | tf_op jit(solution)/shard_map/ppermute | solution.py:412
  60.4 5.1 %collective-permute-start.16 = (bf16[32,704]{1,0:T(8,128)(2,1)S(1)}, bf16[32,704]{1,0:T(8,128)(2,1)S(1)}, u32[]{:S(2)}, u32[]{:S(2)}) collective-permute-start(bf16[32,704]{1,0:T(8,128)(2,1)S(1)} %shard_map.78.refs_0_), channel_id=1, source_target_pairs={{8,0},{12,4},{0,8},{4,12},{9,1},{13,5},{1,9},{5,13},{10,2},{14,6},... | collective-permute-start | bytes 135176 | tf_op jit(solution)/shard_map/ppermute | solution.py:412
  60.5 5.0 %collective-permute-start.15 = (bf16[32,704]{1,0:T(8,128)(2,1)S(1)}, bf16[32,704]{1,0:T(8,128)(2,1)S(1)}, u32[]{:S(2)}, u32[]{:S(2)}) collective-permute-start(bf16[32,704]{1,0:T(8,128)(2,1)S(1)} %shard_map.78.refs_0_), channel_id=1, source_target_pairs={{4,0},{0,4},{12,8},{8,12},{5,1},{1,5},{13,9},{9,13},{6,2},{2,6},{1... | collective-permute-start | bytes 135176 | tf_op jit(solution)/shard_map/ppermute | solution.py:412
  66.4 1.5 %collective-permute-start.18 = (f32[32,1280]{1,0:T(8,128)S(1)}, f32[32,1280]{1,0:T(8,128)S(1)}, u32[]{:S(2)}, u32[]{:S(2)}) collective-permute-start(f32[32,1280]{1,0:T(8,128)S(1)} %shard_map.79.refs_2_), channel_id=1, source_target_pairs={{0,1},{1,0},{2,3},{3,2},{4,5},{5,4},{6,7},{7,6},{8,9},{9,8},{10,11... | collective-permute-start | bytes 491528 | tf_op jit(solution)/shard_map/ppermute | solution.py:409

commit v4 on v3

--- a/solution.py
+++ b/solution.py
@@ -61,36 +61,79 @@
     out_ref[:, size + rank : size + 2 * rank] = rest
 
 
-def prepare_kernel(w_ref, *refs):
-    msg_ref, gram_ref = refs[-2:]
+def fetch_kernel(w_hbm, h_hbm, tab_hbm, order_hbm, *refs):
+    w_ref, old_ref, tab_ref, order_ref, msg_ref, gram_ref, sems = refs[-7:]
+    frames = old_ref.shape[1]
+    mine = pl.ds(pl.multiple_of(lax.axis_index("row") * frames, TAPS), frames)
+    copies = [
+        pltpu.make_async_copy(w_hbm, w_ref, sems.at[0]),
+        pltpu.make_async_copy(tab_hbm, tab_ref, sems.at[1]),
+        pltpu.make_async_copy(h_hbm.at[:, mine], old_ref, sems.at[2]),
+        pltpu.make_async_copy(order_hbm, order_ref, sems.at[3]),
+    ]
+    for copy in copies:
+        copy.start()
+    copies[0].wait()
     w = w_ref[...]
     gram = lax.dot_general(w, w, NT, precision=HIGH, preferred_element_type=F32)
     gram_ref[...] = gram
     pack(msg_ref, w, gram)
+    for copy in copies[1:]:
+        copy.wait()
+
+
+def cut_edges_kernel(rows, sig_hbm, *refs):
+    out_refs, sems = refs[:rows], refs[rows]
+    window, x_me = sig_hbm.shape[1], lax.axis_index("row")
+    copies = []
+    for at in range(rows):
+        begin = pl.multiple_of(jnp.where(x_me == at, window - TAPS, 0), TAPS)
+        copies.append(pltpu.make_async_copy(sig_hbm.at[:, pl.ds(begin, TAPS)], out_refs[at], sems.at[at]))
+    for copy in copies:
+        copy.start()
+    for copy in copies:
+        copy.wait()
+
+
+def cut_signal_kernel(rows, frames, sig_hbm, *refs):
+    out_refs, sems = refs[-rows - 1 : -1], refs[-1]
+    window, x_me = sig_hbm.shape[1], lax.axis_index("row")
+    width = out_refs[0].shape[1]
+    copies = []
+    for shift in range(rows):
+        target = lax.rem(x_me + shift, rows)
+        begin = pl.multiple_of(jnp.clip(target * frames - TAPS, 0, window - width), TAPS)
+        copies.append(pltpu.make_async_copy(sig_hbm.at[:, pl.ds(begin, width)], out_refs[shift], sems.at[shift]))
+    for copy in copies:
+        copy.start()
+    for copy in copies:
+        copy.wait()
+
+
+def pair_rows(s_ref, span, pair, x, cl):
+    halves = [s_ref[span, blk, x].reshape(-1, TAPS) for blk in (2 * pair, 2 * pair + 1)]
+    return jnp.concatenate(halves, axis=1)
 
 
 def group_rows(s_ref, g, pair, rows, cl):
-    halves = []
-    for blk in (2 * pair, 2 * pair + 1):
-        parts = [
-            s_ref[pl.ds(g * GROUP, GROUP), blk, x * cl : (x + 1) * cl, :].reshape(GROUP * cl, TAPS)
-            for x in range(rows)
-        ]
-        halves.append(jnp.concatenate(parts, axis=0))
-    return jnp.concatenate(halves, axis=1)
-
-
-def crossed(low, s_ref, core, out_ref, rows, subs, cl):
-    per_sub = GROUPS // subs
-    wide = GROUP * cl
-    for part in range(per_sub):
-        acc = jnp.zeros((low.shape[0], rows * wide), F32)
-        for pair in range(low.shape[1] // (2 * TAPS)):
-            cols = slice(2 * TAPS * pair, 2 * TAPS * (pair + 1))
-            spectra = group_rows(s_ref, core * per_sub + part, pair, rows, cl)
-            acc = acc + lax.dot_general(low[:, cols], spectra, NT, preferred_element_type=F32)
-        for x in range(rows):
-            out_ref[x, :, part * wide : (part + 1) * wide] = acc[:, x * wide : (x + 1) * wide]
+    span = slice(g * GROUP, (g + 1) * GROUP)
+    return jnp.concatenate([pair_rows(s_ref, span, pair, x, cl) for x in range(rows)], axis=0)
+
+
+def crossed(low, s_ref, x, core, subs, cl):
+    count = NF // subs
+    span = pl.ds(core * count, count)
+    acc = jnp.zeros((low.shape[0], count * cl), F32)
+    for pair in range(low.shape[1] // (2 * TAPS)):
+        cols = slice(2 * TAPS * pair, 2 * TAPS * (pair + 1))
+        acc = acc + lax.dot_general(
+            low[:, cols], pair_rows(s_ref, span, pair, x, cl), NT, preferred_element_type=F32
+        )
+    return acc
+
+
+def others_of(rows, subs):
+    return [(dx, dc) for dx in range(1, rows) for dc in range(1, subs)]
 
 
 def new_activations(old, gram, w_scr, num_scr, s_ref, h_out, h_gram_ref, msg_refs, rows, subs, cl):
@@ -107,48 +150,29 @@
     h_gram = lax.dot_general(new, new, NT, precision=HIGH, preferred_element_type=F32)
     h_gram_ref[...] = h_gram
     size = per_sub * GROUP * cl
-    c_me = lax.axis_index("sub")
-    for dc in range(1, subs):
-        ref = msg_refs[dc - 1]
-        crossed(new.astype(BF16), s_ref, lax.rem(c_me + dc, subs), ref, rows, subs, cl)
-        for x in range(rows):
-            ref[x, :, size:] = h_gram
-
-
-def own_kernel(rows, subs, cl, h_ref, s_ref, out_ref):
-    crossed(h_ref[...].astype(BF16), s_ref, lax.axis_index("sub"), out_ref, rows, subs, cl)
+    x_me, c_me = lax.axis_index("row"), lax.axis_index("sub")
+    for ref, (dx, dc) in zip(msg_refs, others_of(rows, subs)):
+        ref[:, :size] = crossed(
+            new.astype(BF16), s_ref, lax.rem(x_me + dx, rows), lax.rem(c_me + dc, subs), subs, cl
+        )
+        ref[:, size:] = h_gram
+
+
+def products_kernel(places, rows, subs, cl, h_ref, s_ref, *refs):
+    x_me, c_me = lax.axis_index("row"), lax.axis_index("sub")
+    low = h_ref[...].astype(BF16)
+    for ref, (dx, dc) in zip(refs[len(refs) - len(places) :], places):
+        ref[...] = crossed(low, s_ref, lax.rem(x_me + dx, rows), lax.rem(c_me + dc, subs), subs, cl)
 
 
 def spectra_kernel(rows, cl, blocks, *refs):
     refs = list(refs)
-    sig_hbm, h_hbm, w_hbm, tab_hbm, order_hbm = (refs.pop(0) for _ in range(5))
-    sig_refs = [refs.pop(0) for _ in range(rows - 1)]
+    sig_refs = [refs.pop(0) for _ in range(rows)]
     halo_refs = [refs.pop(0) for _ in range(rows)]
-    s_ref, old_ref, w_ref, order_ref = (refs.pop(0) for _ in range(4))
-    sig_scr, tab_scr, xp_scr, x_scr, sems, tab_sems = refs
-    frames = old_ref.shape[1]
-    window = sig_hbm.shape[1]
-    width = sig_scr.shape[1]
+    tab_ref, s_ref, xp_scr, x_scr = refs
+    frames = blocks * TAPS
+    width = sig_refs[0].shape[1]
     x_me = lax.axis_index("row")
-    depth = tab_scr.shape[0]
-
-    def tab_copy(g):
-        slot = lax.rem(g, depth)
-        return pltpu.make_async_copy(tab_hbm.at[pl.ds(g * GROUP, GROUP)], tab_scr.at[slot], tab_sems.at[slot])
-
-    begin = pl.multiple_of(jnp.clip(x_me * frames - TAPS, 0, window - width), TAPS)
-    sig_copy = pltpu.make_async_copy(sig_hbm.at[:, pl.ds(begin, width)], sig_scr, sems.at[0])
-    mine = pl.ds(pl.multiple_of(x_me * frames, TAPS), frames)
-    later = [
-        pltpu.make_async_copy(h_hbm.at[:, mine], old_ref, sems.at[1]),
-        pltpu.make_async_copy(w_hbm, w_ref, sems.at[2]),
-        pltpu.make_async_copy(order_hbm, order_ref, sems.at[3]),
-    ]
-    sig_copy.start()
-    for g in range(depth - 1):
-        tab_copy(g).start()
-    for copy in later:
-        copy.start()
 
     def place(source, owner):
         @pl.when(x_me == 0)
@@ -166,10 +190,8 @@
             def _():
                 xp_scr[owner] = source[:, HALF : HALF + frames + TAPS]
 
-    for shift in range(1, rows):
-        place(sig_refs[shift - 1], lax.rem(x_me + rows - shift, rows))
-    sig_copy.wait()
-    place(sig_scr, x_me)
+    for shift in range(rows):
+        place(sig_refs[shift], lax.rem(x_me + rows - shift, rows))
 
     @pl.when(x_me == 0)
     def _():
@@ -186,25 +208,17 @@
             x_scr[blk, x * cl : (x + 1) * cl, :] = xp_scr[x, :, blk * TAPS : (blk + 2) * TAPS]
 
     def convolve(g, carry):
-        tab_copy(g).wait()
-
-        @pl.when(g + depth - 1 < GROUPS)
-        def _():
-            tab_copy(g + depth - 1).start()
-
         for at in range(GROUP):
             co = jnp.dot(
                 x_scr[...].reshape(blocks * rows * cl, 2 * TAPS),
-                tab_scr[lax.rem(g, depth), at],
+                tab_ref[g * GROUP + at],
                 preferred_element_type=F32,
             )
             power = co[:, :TAPS] * co[:, :TAPS] + co[:, TAPS:] * co[:, TAPS:]
-            s_ref[g * GROUP + at] = power.astype(BF16).reshape(blocks, rows * cl, TAPS)
+            s_ref[g * GROUP + at] = power.astype(BF16).reshape(blocks, rows, cl, TAPS)
         return carry
 
     lax.fori_loop(0, GROUPS, convolve, 0)
-    for copy in later:
-        copy.wait()
 
 
 def first_kernel(rows, subs, cl, *refs):
@@ -213,7 +227,7 @@
     w_msgs = [refs.pop(0) for _ in range(rows - 1)]
     order_ref, h_ref, s_ref = (refs.pop(0) for _ in range(3))
     w_out, h_out, h_gram_ref = (refs.pop(0) for _ in range(3))
-    msg_refs, (w_scr, num_scr) = refs[: subs - 1], refs[subs - 1 :]
+    msg_refs, (w_scr, num_scr) = refs[:-2], refs[-2:]
     rank = h_ref.shape[0]
     per_sub = GROUPS // subs
     wide = GROUP * cl
@@ -250,7 +264,7 @@
     w_refs = [refs.pop(0) for _ in range(rows * subs)]
     h_ref, s_ref = refs.pop(0), refs.pop(0)
     h_out, h_gram_ref = (refs.pop(0) for _ in range(2))
-    msg_refs, (w_scr, num_scr) = refs[: subs - 1], refs[subs - 1 :]
+    msg_refs, (w_scr, num_scr) = refs[:-2], refs[-2:]
     rank = h_ref.shape[0]
     per_sub = GROUPS // subs
     wide = GROUP * cl
@@ -267,27 +281,28 @@
     new_activations(h_ref[...], gram, w_scr, num_scr, s_ref, h_out, h_gram_ref, msg_refs, rows, subs, cl)
 
 
-def core_kernel(rows, subs, *refs):
-    own_ref, own_gram_ref, *refs = refs
-    msg_refs, refs = refs[: subs - 1], refs[subs - 1 :]
-    out_ref, gram_ref, *out_msgs, scr = refs
-    size = own_ref.shape[2]
-    total, gram = own_ref[...], own_gram_ref[...]
-    for ref in msg_refs:
-        total = total + ref[:, :, :size]
-        gram = gram + ref[0, :, size:]
-    scr[...] = total
-    gram_ref[...] = gram
-    x_me = lax.axis_index("row")
-    out_ref[...] = scr[x_me]
-    for dx in range(1, rows):
-        pack(out_msgs[dx - 1], scr[lax.rem(x_me + dx, rows)], gram)
-
-
-def row_kernel(*refs):
-    own_ref, own_gram_ref, *msg_refs, out_ref = refs
+def core_kernel(count, rank, *refs):
+    own_refs, gram_ref, got_refs = refs[:count], refs[count], refs[count + 1 : -count - 1]
+    out_refs, total_ref = refs[-count - 1 : -1], refs[-1]
+    size = own_refs[0].shape[1]
+    each = len(got_refs) // count
+    gram = gram_ref[...]
+    for ref in got_refs[:each]:
+        gram = gram + ref[:, size:]
+    total_ref[...] = gram
+    for at in range(count):
+        total = own_refs[at][...]
+        for ref in got_refs[at * each : (at + 1) * each]:
+            total = total + ref[:, :size]
+        pack(out_refs[at], total, gram)
+
+
+def row_kernel(subs, own_ref, gram_ref, *refs):
+    core_refs, msg_refs, out_ref = refs[: subs - 1], refs[subs - 1 : -1], refs[-1]
     rank, size = own_ref.shape
-    total, gram = own_ref[...], own_gram_ref[...]
+    total, gram = own_ref[...], gram_ref[...]
+    for ref in core_refs:
+        total = total + ref[...]
     for ref in msg_refs:
         total = total + ref[:, :size].astype(F32)
         gram = gram + joined(ref, size, rank)
@@ -414,79 +429,86 @@
     def place(x, at):
         return (at // subs * rows + x) * subs + at % subs
 
-    def begin(target):
-        return jnp.clip(target * frames - TAPS, 0, window - width)
-
-    sig = [
-        row_shift(lax.dynamic_slice_in_dim(signal, begin((x_me + shift) % rows), width, 1), shift)
-        for shift in range(1, rows)
-    ]
-    tail, head = signal[:, window - TAPS :], signal[:, :TAPS]
+    edges = call(
+        functools.partial(cut_edges_kernel, rows),
+        [hbm(signal)],
+        [((cl, TAPS), BF16)] * rows,
+        [pltpu.SemaphoreType.DMA((rows,))],
+        in_specs=[anywhere],
+    )
     halos = [None] * rows
     for at in reversed(range(rows)):
         to_next = [(place(at, i), place(0, i + 1)) for i in range(line - 1)]
         to_prev = [(place(rows - 1 - at, i + 1), place(rows - 1, i)) for i in range(line - 1)]
-        halos[at] = lax.ppermute(jnp.where(x_me == at, tail, head), ("frm", "row", "sub"), to_next + to_prev)
-
-    w_cols = w_start.T
-    w_msg, w_gram = call(
-        prepare_kernel,
-        [w_cols] + sig,
-        [((rank, NF * cl + 2 * rank), BF16), ((rank, rank), F32)],
-        in_specs=[whole] + [anywhere] * len(sig),
-    )
-    w_msgs = [row_shift(w_msg, shift) for shift in range(1, rows)]
+        halos[at] = lax.ppermute(edges[at], ("frm", "row", "sub"), to_next + to_prev)
+    own_sig, *out_sigs = call(
+        functools.partial(cut_signal_kernel, rows, frames),
+        [hbm(signal)] + list(edges),
+        [((cl, width), BF16)] * rows,
+        [pltpu.SemaphoreType.DMA((rows,))],
+        in_specs=[anywhere] * (rows + 1),
+    )
+    sig = [own_sig] + [row_shift(part, shift + 1) for shift, part in enumerate(out_sigs)]
 
     msg = ((rank, size + 2 * rank), BF16)
     piece = ((rank, size), F32)
     update_outs = [((rank, frames), F32), ((rank, rank), F32)]
-    update_outs += [((rows, rank, size + rank), F32)] * (subs - 1)
+    update_outs += [((rank, size + rank), F32)] * ((rows - 1) * (subs - 1))
     update_scratch = [
         pltpu.VMEM((subs, GROUPS // subs, rows, rank, GROUP * cl), BF16),
         pltpu.VMEM((rank, frames), F32),
     ]
-    order = jnp.asarray(reorder(cl))
-    held = [hbm(signal), hbm(h_start), hbm(w_cols), hbm(jnp.asarray(toeplitz())), hbm(order)]
-    macs = NF * chans * frames * rank
-    spectra, old, w_own, order = call(
+    table, order = jnp.asarray(toeplitz()), jnp.asarray(reorder(cl))
+    w_own, old, table, order, w_msg, w_gram = call(
+        fetch_kernel,
+        [hbm(w_start.T), hbm(h_start), hbm(table), hbm(order), own_sig],
+        [
+            pltpu.VMEM((rank, NF * cl), F32),
+            pltpu.VMEM((rank, frames), F32),
+            pltpu.VMEM(table.shape, BF16),
+            pltpu.VMEM(order.shape, BF16),
+            ((rank, NF * cl + 2 * rank), BF16),
+            ((rank, rank), F32),
+        ],
+        [pltpu.SemaphoreType.DMA((4,))],
+        in_specs=[anywhere] * 5,
+        cost=2 * 10**9,
+    )
+    w_msgs = [row_shift(w_msg, shift) for shift in range(1, rows)]
+    order = vmem(order)
+    (spectra,) = call(
         functools.partial(spectra_kernel, rows, cl, blocks),
-        held + sig + halos,
-        [
-            pltpu.VMEM((NF, blocks, chans, TAPS), BF16),
-            pltpu.VMEM((rank, frames), F32),
-            pltpu.VMEM((rank, NF * cl), F32),
-            pltpu.VMEM(order.shape, BF16),
-        ],
-        [
-            pltpu.VMEM((cl, width), BF16),
-            pltpu.VMEM((3, GROUP, 2 * TAPS, 2 * TAPS), BF16),
-            pltpu.VMEM((rows, cl, frames + TAPS), BF16),
-            pltpu.VMEM((blocks, chans, 2 * TAPS), BF16),
-            pltpu.SemaphoreType.DMA((4,)),
-            pltpu.SemaphoreType.DMA((3,)),
-        ],
-        in_specs=[anywhere] * len(held) + [whole] * (len(sig) + len(halos)),
-        limit=12,
+        sig + halos + [vmem(table)],
+        [pltpu.VMEM((NF, blocks, rows, cl, TAPS), BF16)],
+        [pltpu.VMEM((rows, cl, frames + TAPS), BF16), pltpu.VMEM((blocks, chans, 2 * TAPS), BF16)],
+        limit=8,
         cost=2 * NF * chans * frames * 4 * TAPS,
     )
-    spectra, order = vmem(spectra), vmem(order)
+    spectra = vmem(spectra)
+
+    def products(places, activations, after):
+        return call(
+            functools.partial(products_kernel, places, rows, subs, cl),
+            [activations, spectra] + after,
+            [piece] * len(places),
+            in_specs=[whole] * 2 + [anywhere] * len(after),
+            cost=1 if after else 16 * NF * cl * frames * rank // subs * len(places),
+        )
 
     def gathered(activations, h_gram, msgs):
-        got = [sub_shift(m, dc + 1) for dc, m in enumerate(msgs)]
-        (own,) = call(
-            functools.partial(own_kernel, rows, subs, cl),
-            [activations, spectra],
-            [((rows,) + piece[0], F32)],
-            cost=16 * macs // subs,
+        got = [sub_shift(m, dc) for m, (_, dc) in zip(msgs, others_of(rows, subs))]
+        out_places = [(dx, 0) for dx in range(1, rows)]
+        own = products(out_places, activations, [])
+        *outs, gram = call(
+            functools.partial(core_kernel, rows - 1, rank),
+            list(own) + [h_gram] + got,
+            [msg] * (rows - 1) + [((rank, rank), F32)],
         )
-        part, gram, *outs = call(
-            functools.partial(core_kernel, rows, subs),
-            [own, h_gram] + got,
-            [piece, ((rank, rank), F32)] + [msg] * (rows - 1),
-            [pltpu.VMEM((rows,) + piece[0], F32)],
-        )
-        got = [row_shift(m, dx + 1) for dx, m in enumerate(outs)]
-        (part,) = call(row_kernel, [part, gram] + got, [msg])
+        from_rows = [row_shift(m, dx + 1) for dx, m in enumerate(outs)]
+        for_cores = products([(0, dc) for dc in range(1, subs)], activations, outs)
+        from_cores = [sub_shift(m, dc + 1) for dc, m in enumerate(for_cores)]
+        (own,) = products([(0, 0)], activations, list(for_cores))
+        (part,) = call(functools.partial(row_kernel, subs), [own, gram] + from_cores + from_rows, [msg])
         return [part] + [frm_shift(part, shift) for shift in range(1, frms)]
 
     w_piece, activations, h_gram, *msgs = call(

time: 69 us -> 68.9 us (level)
  Pallas kernels: 23.1 us -> 27.3 us
  local copies, waits for them, and re-layouts: 1.93 us -> 0 us
  starting transfers between devices: 23.6 us -> 22.8 us
  other arithmetic: 0.72 us -> 0 us
  waiting for transfers between devices: 18.6 us -> 17.9 us
    pallas_call x13 -> x19, Pallas kernels: 23.1 us -> 27.3 us  [call(): pl.pallas_call(kernel, out_shape=[jax.ShapeDtypeStruct(*out) if isinstanc...]
    ppermute x6, starting transfers between devices: 8.59 us -> 10.2 us  [row_shift(): lax.ppermute(value, 'row', [(i, (i + shift) % rows) for i in range(rows)])]
    ppermute x5 -> x7, starting transfers between devices: 2.32 us -> 0.81 us  [sub_shift(): lax.ppermute(value, 'sub', [(i, (i + shift) % subs) for i in range(subs)])]
    ppermute x6, waiting for transfers between devices: 8.62 us -> 7.2 us  [row_shift(): lax.ppermute(value, 'row', [(i, (i + shift) % rows) for i in range(rows)])]
    dynamic_slice x1 -> x0, local copies, waits for them, and re-layouts: 1.02 us -> none  [shards(): lax.dynamic_slice_in_dim(signal, begin((x_me + shift) % rows), width, 1)]
    ppermute x2, starting transfers between devices: 3.94 us -> 3.02 us  [shards(): lax.ppermute(edges[at], ('frm', 'row', 'sub'), to_next + to_prev)]
    unnamed x2 -> x0, local copies, waits for them, and re-layouts: 0.91 us -> none
    ppermute x5 -> x7, waiting for transfers between devices: 2.61 us -> 3.38 us  [sub_shift(): lax.ppermute(value, 'sub', [(i, (i + shift) % subs) for i in range(subs)])]
  transfers between devices with their start and end apart: 19 -> 21, of which waited for: 9 -> 12; matrix products, arithmetic and copies ran while one was open for 1% -> 0% of each run, Pallas kernels for 19% -> 24%
where the time goes in v4:
time: 68.9 us; the launch traced here: 68.7 us
  Pallas kernels  27.3 us (40%)
  starting transfers between devices  22.8 us (33%)
  waiting for transfers between devices  17.9 us (26%)
  between operations  0.75 us (1%)
    pallas_call x19, Pallas kernels, call(): pl.pallas_call(kernel, out_shape=[jax.ShapeDtypeStruct(*out) if isinstanc...  27.3 us
    ppermute x6, starting transfers between devices, row_shift(): lax.ppermute(value, 'row', [(i, (i + shift) % rows) for i in range(rows)])  10.2 us
    ppermute x6, starting transfers between devices, frm_shift(): lax.ppermute(value, 'frm', [(partner(i, shift, frms), i) for i in range(f...  8.78 us
    ppermute x6, waiting for transfers between devices, frm_shift(): lax.ppermute(value, 'frm', [(partner(i, shift, frms), i) for i in range(f...  7.27 us
    ppermute x6, waiting for transfers between devices, row_shift(): lax.ppermute(value, 'row', [(i, (i + shift) % rows) for i in range(rows)])  7.2 us
    ppermute x7, waiting for transfers between devices, sub_shift(): lax.ppermute(value, 'sub', [(i, (i + shift) % subs) for i in range(subs)])  3.38 us
    ppermute x2, starting transfers between devices, shards(): lax.ppermute(edges[at], ('frm', 'row', 'sub'), to_next + to_prev)  3.02 us
  transfers between devices with their start and end apart: 21, of which 12 were waited for; matrix products, arithmetic and copies ran while one was open for 0% of the time, Pallas kernels for 24%

profile of v4, /device:TPU:0, one launch (start us, length us, event | category | flops | bytes accessed | tf_op | source)
XLA Modules:
  0.0 68.7 jit_solution(13324772110906724568)
XLA Ops:
  0.6 0.7 %shard_map.68 = (bf16[32,128]{1,0:T(8,128)(2,1)S(1)}, bf16[32,128]{1,0:T(8,128)(2,1)S(1)}) custom-call(bf16[32,4096]{1,0:T(8,128)(2,1)} %sig_hbm.3), custom_call_target="tpu_custom_call" | custom-call | tf_op jit(solution)/shard_map/pallas_call | solution.py:382
  1.4 2.4 %collective-permute-start.2 = (bf16[32,128]{1,0:T(8,128)(2,1)S(1)}, bf16[32,128]{1,0:T(8,128)(2,1)S(1)}, u32[]{:S(2)}, u32[]{:S(2)}) collective-permute-start(bf16[32,128]{1,0:T(8,128)(2,1)S(1)} %get-tuple-element.29.refs_0_), channel_id=1, source_target_pairs={{0,1},{1,4},{4,5},{5,8},{8,9},{9,12},{12,13},{3,2},{6,3},{7,6},{10... | collective-permute-start | bytes 24584 | tf_op jit(solution)/shard_map/ppermute | solution.py:443
  3.7 0.7 collective-permute-start.3
  4.4 1.0 %shard_map.69 = (bf16[32,2176]{1,0:T(8,128)(2,1)S(1)}, bf16[32,2176]{1,0:T(8,128)(2,1)S(1)}) custom-call(bf16[32,4096]{1,0:T(8,128)(2,1)} %sig_hbm.3, bf16[32,128]{1,0:T(8,128)(2,1)S(1)} %get-tuple-element.29.refs_0_, bf16[32,128]{1,0:T(8,128)(2,1)S(1)} %get-tuple-element.30.refs_1_), custom_call_target="tpu_custom_call" | custom-call | tf_op jit(solution)/shard_map/pallas_call | solution.py:382
  5.4 5.6 %collective-permute-start.1 = (bf16[32,2176]{1,0:T(8,128)(2,1)S(1)}, bf16[32,2176]{1,0:T(8,128)(2,1)S(1)}, u32[]{:S(2)}, u32[]{:S(2)}) collective-permute-start(bf16[32,2176]{1,0:T(8,128)(2,1)S(1)} %get-tuple-element.37), channel_id=1, source_target_pairs={{0,2},{2,0},{1,3},{3,1},{4,6},{6,4},{5,7},{7,5},{8,10},{10,8},{9,1... | collective-permute-start | bytes 417800 | tf_op jit(solution)/shard_map/ppermute | solution.py:421
  11.1 3.7 %shard_map.70 = (f32[32,1280]{1,0:T(8,128)S(1)}, f32[32,2048]{1,0:T(8,128)S(1)}, bf16[40,256,256]{2,1,0:T(8,128)(2,1)S(1)}, bf16[1280,1280]{1,0:T(8,128)(2,1)S(1...) custom-call(f32[32,1280]{1,0:T(8,128)} %bitcast.2, f32[32,4096]{1,0:T(8,128)} %h_hbm.1, ...), custom_call_target="tpu_custom_call" | custom-call | flops 2000000000 | tf_op jit(solution)/shard_map/pallas_call | solution.py:382
  14.8 0.1 collective-permute-start
  14.8 0.0 collective-permute-done.2.refs_2_
  14.9 0.0 collective-permute-done.3.refs_3_
  14.9 0.2 collective-permute-done.1.refs_1_
  15.0 7.5 %shard_map.71.refs_5_.s_ref = bf16[40,16,2,32,128]{4,3,2,1,0:T(8,128)(2,1)S(1)} custom-call(bf16[32,2176]{1,0:T(8,128)(2,1)S(1)} %get-tuple-element.31.refs_0_, bf16[32,2176]{1,0:T(8,128)(2,1)S(1)} %collective-permute-done.1.refs_1_, bf16[32,128]{1,0:T(8,128)(2,1)S(1)} %collective-permute-done.2.refs_2_, bf16[32,128]{1,0:T(8,128)(2,1)S(1)} %collective-permute-done.3.refs_3_, ...), custom_call_target="tpu_custom_call" | custom-call | flops 5368709120 | tf_op jit(solution)/shard_map/pallas_call | solution.py:382
  22.5 0.0 collective-permute-done.refs_2_
  22.5 3.6 %shard_map.72 = (f32[32,640]{1,0:T(8,128)S(1)}, f32[32,2048]{1,0:T(8,128)S(1)}, f32[32,32]{1,0:T(8,128)S(1)}, f32[32,672]{1,0:T(8,128)S(1)}) custom-call(f32[32,1280]{1,0:T(8,128)S(1)} %get-tuple-element.32.refs_0_, f32[32,32]{1,0:T(8,128)S(1)} %get-tuple-element.33.refs_1_, bf16[32,1344]{1,0:T(8,128)(2,1)S(1)} %collective-permute-done.refs_2_, ...), custom_call_target="tpu_custom_call" | custom-call | tf_op jit(solution)/shard_map/pallas_call | solution.py:382
  26.2 0.1 collective-permute-start.4
  26.2 0.8 %shard_map.73.refs_0_ = f32[32,640]{1,0:T(8,128)S(1)} custom-call(f32[32,2048]{1,0:T(8,128)S(1)} %get-tuple-element.40.h_ref.refs_4_, bf16[40,16,2,32,128]{4,3,2,1,0:T(8,128)(2,1)S(1)} %shard_map.71.refs_5_.s_ref), custom_call_target="tpu_custom_call" | custom-call | flops 671088640 | tf_op jit(solution)/shard_map/pallas_call | solution.py:382
  27.1 0.4 collective-permute-done.4.refs_2_
  27.5 0.1 shard_map.74
  27.6 0.8 %shard_map.75.refs_0_ = f32[32,640]{1,0:T(8,128)S(1)} custom-call(f32[32,2048]{1,0:T(8,128)S(1)} %get-tuple-element.40.h_ref.refs_4_, bf16[40,16,2,32,128]{4,3,2,1,0:T(8,128)(2,1)S(1)} %shard_map.71.refs_5_.s_ref, bf16[32,704]{1,0:T(8,128)(2,1)S(1)} %get-tuple-element.43.refs_0_), custom_call_target="tpu_custom_call" | custom-call | flops 1 | tf_op jit(solution)/shard_map/pallas_call | solution.py:382
  28.4 0.2 collective-permute-start.5
  28.6 1.9 %collective-permute-start.6 = (bf16[32,704]{1,0:T(8,128)(2,1)S(1)}, bf16[32,704]{1,0:T(8,128)(2,1)S(1)}, u32[]{:S(2)}, u32[]{:S(2)}) collective-permute-start(bf16[32,704]{1,0:T(8,128)(2,1)S(1)} %get-tuple-element.43.refs_0_), channel_id=1, source_target_pairs={{0,2},{2,0},{1,3},{3,1},{4,6},{6,4},{5,7},{7,5},{8,10},{10,8},{9,1... | collective-permute-start | bytes 135176 | tf_op jit(solution)/shard_map/ppermute | solution.py:421
  30.5 0.8 %shard_map.76.own_ref = f32[32,640]{1,0:T(8,128)S(1)} custom-call(f32[32,2048]{1,0:T(8,128)S(1)} %get-tuple-element.40.h_ref.refs_4_, bf16[40,16,2,32,128]{4,3,2,1,0:T(8,128)(2,1)S(1)} %shard_map.71.refs_5_.s_ref, f32[32,640]{1,0:T(8,128)S(1)} %shard_map.75.refs_0_), custom_call_target="tpu_custom_call" | custom-call | flops 1 | tf_op jit(solution)/shard_map/pallas_call | solution.py:382
  31.3 1.4 %collective-permute-done.6.refs_1_ = bf16[32,704]{1,0:T(8,128)(2,1)S(1)} collective-permute-done((bf16[32,704]{1,0:T(8,128)(2,1)S(1)}, bf16[32,704]{1,0:T(8,128)(2,1)S(1)}, u32[]{:S(2)}, u32[]{:S(2)}) %collective-permute-start.6) | collective-permute-done | bytes 45088 | tf_op jit(solution)/shard_map/ppermute | solution.py:421
  32.8 0.0 collective-permute-done.5.refs_0_
  32.8 0.2 shard_map.77.refs_0_
  32.9 3.6 %collective-permute-start.9 = (bf16[32,704]{1,0:T(8,128)(2,1)S(1)}, bf16[32,704]{1,0:T(8,128)(2,1)S(1)}, u32[]{:S(2)}, u32[]{:S(2)}) collective-permute-start(bf16[32,704]{1,0:T(8,128)(2,1)S(1)} %shard_map.77.refs_0_), channel_id=1, source_target_pairs={{12,0},{8,4},{4,8},{0,12},{13,1},{9,5},{5,9},{1,13},{14,2},{10,6},... | collective-permute-start | bytes 135176 | tf_op jit(solution)/shard_map/ppermute | solution.py:427
  36.5 0.0 collective-permute-start.8
  36.5 0.8 %collective-permute-start.7 = (bf16[32,704]{1,0:T(8,128)(2,1)S(1)}, bf16[32,704]{1,0:T(8,128)(2,1)S(1)}, u32[]{:S(2)}, u32[]{:S(2)}) collective-permute-start(bf16[32,704]{1,0:T(8,128)(2,1)S(1)} %shard_map.77.refs_0_), channel_id=1, source_target_pairs={{4,0},{0,4},{12,8},{8,12},{5,1},{1,5},{13,9},{9,13},{6,2},{2,6},{1... | collective-permute-start | bytes 135176 | tf_op jit(solution)/shard_map/ppermute | solution.py:427
  37.3 1.8 %collective-permute-done.9.refs_3_ = bf16[32,704]{1,0:T(8,128)(2,1)S(1)} collective-permute-done((bf16[32,704]{1,0:T(8,128)(2,1)S(1)}, bf16[32,704]{1,0:T(8,128)(2,1)S(1)}, u32[]{:S(2)}, u32[]{:S(2)}) %collective-permute-start.9) | collective-permute-done | bytes 45088 | tf_op jit(solution)/shard_map/ppermute | solution.py:427
  39.1 2.4 %collective-permute-done.8.refs_2_ = bf16[32,704]{1,0:T(8,128)(2,1)S(1)} collective-permute-done((bf16[32,704]{1,0:T(8,128)(2,1)S(1)}, bf16[32,704]{1,0:T(8,128)(2,1)S(1)}, u32[]{:S(2)}, u32[]{:S(2)}) %collective-permute-start.8) | collective-permute-done | bytes 45088 | tf_op jit(solution)/shard_map/ppermute | solution.py:427
  41.5 0.0 collective-permute-done.7.refs_1_
  41.5 0.6 shard_map.78
  42.1 0.9 %collective-permute-start.11 = (bf16[32,704]{1,0:T(8,128)(2,1)S(1)}, bf16[32,704]{1,0:T(8,128)(2,1)S(1)}, u32[]{:S(2)}, u32[]{:S(2)}) collective-permute-start(bf16[32,704]{1,0:T(8,128)(2,1)S(1)} %get-tuple-element.45.refs_0_), channel_id=1, source_target_pairs={{0,2},{2,0},{1,3},{3,1},{4,6},{6,4},{5,7},{7,5},{8,10},{10,8},{9,1... | collective-permute-start | bytes 135176 | tf_op jit(solution)/shard_map/ppermute | solution.py:421
  43.0 0.0 collective-permute-start.10
  43.0 3.2 %collective-permute-done.11.refs_2_ = bf16[32,704]{1,0:T(8,128)(2,1)S(1)} collective-permute-done((bf16[32,704]{1,0:T(8,128)(2,1)S(1)}, bf16[32,704]{1,0:T(8,128)(2,1)S(1)}, u32[]{:S(2)}, u32[]{:S(2)}) %collective-permute-start.11) | collective-permute-done | bytes 45088 | tf_op jit(solution)/shard_map/ppermute | solution.py:421
  46.2 0.0 collective-permute-start.12
  46.2 0.0 collective-permute-done.10.refs_1_
  46.2 1.2 %collective-permute-done.12.refs_3_ = bf16[32,704]{1,0:T(8,128)(2,1)S(1)} collective-permute-done((bf16[32,704]{1,0:T(8,128)(2,1)S(1)}, bf16[32,704]{1,0:T(8,128)(2,1)S(1)}, u32[]{:S(2)}, u32[]{:S(2)}) %collective-permute-start.12) | collective-permute-done | bytes 45088 | tf_op jit(solution)/shard_map/ppermute | solution.py:424
  47.4 2.9 %shard_map.79 = (f32[32,2048]{1,0:T(8,128)S(1)}, f32[32,32]{1,0:T(8,128)S(1)}, f32[32,672]{1,0:T(8,128)S(1)}) custom-call(bf16[32,704]{1,0:T(8,128)(2,1)S(1)} %get-tuple-element.45.refs_0_, bf16[32,704]{1,0:T(8,128)(2,1)S(1)} %collective-permute-done.10.refs_1_, bf16[32,704]{1,0:T(8,128)(2,1)S(1)} %collective-permute-done.11.refs_2_, ...), custom_call_target="tpu_custom_call" | custom-call | tf_op jit(solution)/shard_map/pallas_call | solution.py:382
  50.3 0.2 collective-permute-start.13
  50.6 0.8 %shard_map.80.refs_0_ = f32[32,640]{1,0:T(8,128)S(1)} custom-call(f32[32,2048]{1,0:T(8,128)S(1)} %get-tuple-element.51.h_ref.refs_0_, bf16[40,16,2,32,128]{4,3,2,1,0:T(8,128)(2,1)S(1)} %shard_map.71.refs_5_.s_ref), custom_call_target="tpu_custom_call" | custom-call | flops 671088640 | tf_op jit(solution)/shard_map/pallas_call | solution.py:382
  51.4 0.3 collective-permute-done.13.refs_2_
  51.7 0.1 shard_map.81
  51.8 0.8 %shard_map.82.refs_0_ = f32[32,640]{1,0:T(8,128)S(1)} custom-call(f32[32,2048]{1,0:T(8,128)S(1)} %get-tuple-element.51.h_ref.refs_0_, bf16[40,16,2,32,128]{4,3,2,1,0:T(8,128)(2,1)S(1)} %shard_map.71.refs_5_.s_ref, bf16[32,704]{1,0:T(8,128)(2,1)S(1)} %get-tuple-element.49.refs_0_), custom_call_target="tpu_custom_call" | custom-call | flops 1 | tf_op jit(solution)/shard_map/pallas_call | solution.py:382
  52.6 0.2 collective-permute-start.14
  52.8 0.9 %collective-permute-start.15 = (bf16[32,704]{1,0:T(8,128)(2,1)S(1)}, bf16[32,704]{1,0:T(8,128)(2,1)S(1)}, u32[]{:S(2)}, u32[]{:S(2)}) collective-permute-start(bf16[32,704]{1,0:T(8,128)(2,1)S(1)} %get-tuple-element.49.refs_0_), channel_id=1, source_target_pairs={{0,2},{2,0},{1,3},{3,1},{4,6},{6,4},{5,7},{7,5},{8,10},{10,8},{9,1... | collective-permute-start | bytes 135176 | tf_op jit(solution)/shard_map/ppermute | solution.py:421
  53.7 0.8 %shard_map.83.own_ref = f32[32,640]{1,0:T(8,128)S(1)} custom-call(f32[32,2048]{1,0:T(8,128)S(1)} %get-tuple-element.51.h_ref.refs_0_, bf16[40,16,2,32,128]{4,3,2,1,0:T(8,128)(2,1)S(1)} %shard_map.71.refs_5_.s_ref, f32[32,640]{1,0:T(8,128)S(1)} %shard_map.82.refs_0_), custom_call_target="tpu_custom_call" | custom-call | flops 1 | tf_op jit(solution)/shard_map/pallas_call | solution.py:382
  54.5 2.4 %collective-permute-done.15.refs_1_ = bf16[32,704]{1,0:T(8,128)(2,1)S(1)} collective-permute-done((bf16[32,704]{1,0:T(8,128)(2,1)S(1)}, bf16[32,704]{1,0:T(8,128)(2,1)S(1)}, u32[]{:S(2)}, u32[]{:S(2)}) %collective-permute-start.15) | collective-permute-done | bytes 45088 | tf_op jit(solution)/shard_map/ppermute | solution.py:421
  56.9 0.0 collective-permute-done.14.refs_0_
  56.9 0.2 shard_map.84.refs_0_
  57.1 0.9 %collective-permute-start.16 = (f32[32,2048]{1,0:T(8,128)S(1)}, f32[32,2048]{1,0:T(8,128)S(1)}, u32[]{:S(2)}, u32[]{:S(2)}) collective-permute-start(f32[32,2048]{1,0:T(8,128)S(1)} %get-tuple-element.51.h_ref.refs_0_), channel_id=1, source_target_pairs={{0,2},{2,0},{1,3},{3,1},{4,6},{6,4},{5,7},{7,5},{8,10},{10,8},{9,1... | collective-permute-start | bytes 786440 | tf_op jit(solution)/shard_map/ppermute | solution.py:421
  58.0 2.4 %collective-permute-start.19 = (bf16[32,704]{1,0:T(8,128)(2,1)S(1)}, bf16[32,704]{1,0:T(8,128)(2,1)S(1)}, u32[]{:S(2)}, u32[]{:S(2)}) collective-permute-start(bf16[32,704]{1,0:T(8,128)(2,1)S(1)} %shard_map.84.refs_0_), channel_id=1, source_target_pairs={{12,0},{8,4},{4,8},{0,12},{13,1},{9,5},{5,9},{1,13},{14,2},{10,6},... | collective-permute-start | bytes 135176 | tf_op jit(solution)/shard_map/ppermute | solution.py:427
  60.3 0.0 collective-permute-start.18
  60.4 2.0 %collective-permute-start.17 = (bf16[32,704]{1,0:T(8,128)(2,1)S(1)}, bf16[32,704]{1,0:T(8,128)(2,1)S(1)}, u32[]{:S(2)}, u32[]{:S(2)}) collective-permute-start(bf16[32,704]{1,0:T(8,128)(2,1)S(1)} %shard_map.84.refs_0_), channel_id=1, source_target_pairs={{4,0},{0,4},{12,8},{8,12},{5,1},{1,5},{13,9},{9,13},{6,2},{2,6},{1... | collective-permute-start | bytes 135176 | tf_op jit(solution)/shard_map/ppermute | solution.py:427
  62.3 1.7 %collective-permute-done.19.refs_3_ = bf16[32,704]{1,0:T(8,128)(2,1)S(1)} collective-permute-done((bf16[32,704]{1,0:T(8,128)(2,1)S(1)}, bf16[32,704]{1,0:T(8,128)(2,1)S(1)}, u32[]{:S(2)}, u32[]{:S(2)}) %collective-permute-start.19) | collective-permute-done | bytes 45088 | tf_op jit(solution)/shard_map/ppermute | solution.py:427
  64.0 1.4 %collective-permute-done.18.refs_2_ = bf16[32,704]{1,0:T(8,128)(2,1)S(1)} collective-permute-done((bf16[32,704]{1,0:T(8,128)(2,1)S(1)}, bf16[32,704]{1,0:T(8,128)(2,1)S(1)}, u32[]{:S(2)}, u32[]{:S(2)}) %collective-permute-start.18) | collective-permute-done | bytes 45088 | tf_op jit(solution)/shard_map/ppermute | solution.py:427
  65.4 0.0 collective-permute-done.17.refs_1_
  65.4 0.9 %shard_map.85.refs_2_ = f32[32,1280]{1,0:T(8,128)S(1)} custom-call(f32[32,640]{1,0:T(8,128)S(1)} %get-tuple-element.52.w_ref, bf16[1280,1280]{1,0:T(8,128)(2,1)S(1)} %get-tuple-element.35.refs_3_.order_ref, bf16[32,704]{1,0:T(8,128)(2,1)S(1)} %shard_map.84.refs_0_, bf16[32,704]{1,0:T(8,128)(2,1)S(1)} %collective-permute-done.17.refs_1_, ...), custom_call_target="tpu_custom_call" | custom-call | tf_op jit(solution)/shard_map/pallas_call | solution.py:382
  66.3 0.1 collective-permute-start.20
  66.4 1.4 %collective-permute-done.20.refs_3_ = f32[32,1280]{1,0:T(8,128)S(1)} collective-permute-done((f32[32,1280]{1,0:T(8,128)S(1)}, f32[32,1280]{1,0:T(8,128)S(1)}, u32[]{:S(2)}, u32[]{:S(2)}) %collective-permute-start.20) | collective-permute-done | bytes 163872 | tf_op jit(solution)/shard_map/ppermute | solution.py:424
  67.8 0.0 collective-permute-done.16.refs_1_
  67.8 0.9 %shard_map.86 = (f32[32,1280]{1,0:T(8,128)}, f32[32,4096]{1,0:T(8,128)}) custom-call(f32[32,2048]{1,0:T(8,128)S(1)} %get-tuple-element.51.h_ref.refs_0_, f32[32,2048]{1,0:T(8,128)S(1)} %collective-permute-done.16.refs_1_, f32[32,1280]{1,0:T(8,128)S(1)} %shard_map.85.refs_2_, f32[32,1280]{1,0:T(8,128)S(1)} %collective-permute-done.20.refs_3_), custom_call_target="tpu_custom_call" | custom-call | tf_op jit(solution)/shard_map/pallas_call | solution.py:382
Async XLA Ops:
  1.4 13.5 %collective-permute-start.2 = (bf16[32,128]{1,0:T(8,128)(2,1)S(1)}, bf16[32,128]{1,0:T(8,128)(2,1)S(1)}, u32[]{:S(2)}, u32[]{:S(2)}) collective-permute-start(bf16[32,128]{1,0:T(8,128)(2,1)S(1)} %get-tuple-element.29.refs_0_), channel_id=1, source_target_pairs={{0,1},{1,4},{4,5},{5,8},{8,9},{9,12},{12,13},{3,2},{6,3},{7,6},{10... | collective-permute-start | bytes 24584 | tf_op jit(solution)/shard_map/ppermute | solution.py:443
  3.7 11.1 %collective-permute-start.3 = (bf16[32,128]{1,0:T(8,128)(2,1)S(1)}, bf16[32,128]{1,0:T(8,128)(2,1)S(1)}, u32[]{:S(2)}, u32[]{:S(2)}) collective-permute-start(bf16[32,128]{1,0:T(8,128)(2,1)S(1)} %get-tuple-element.30.refs_1_), channel_id=1, source_target_pairs={{2,1},{3,4},{6,5},{7,8},{10,9},{11,12},{14,13},{1,2},{4,3},{5,6},{... | collective-permute-start | bytes 24584 | tf_op jit(solution)/shard_map/ppermute | solution.py:443
  5.4 9.6 %collective-permute-start.1 = (bf16[32,2176]{1,0:T(8,128)(2,1)S(1)}, bf16[32,2176]{1,0:T(8,128)(2,1)S(1)}, u32[]{:S(2)}, u32[]{:S(2)}) collective-permute-start(bf16[32,2176]{1,0:T(8,128)(2,1)S(1)} %get-tuple-element.37), channel_id=1, source_target_pairs={{0,2},{2,0},{1,3},{3,1},{4,6},{6,4},{5,7},{7,5},{8,10},{10,8},{9,1... | collective-permute-start | bytes 417800 | tf_op jit(solution)/shard_map/ppermute | solution.py:421
  14.8 7.8 %collective-permute-start = (bf16[32,1344]{1,0:T(8,128)(2,1)S(1)}, bf16[32,1344]{1,0:T(8,128)(2,1)S(1)}, u32[]{:S(2)}, u32[]{:S(2)}) collective-permute-start(bf16[32,1344]{1,0:T(8,128)(2,1)S(1)} %get-tuple-element.34), channel_id=1, source_target_pairs={{0,2},{2,0},{1,3},{3,1},{4,6},{6,4},{5,7},{7,5},{8,10},{10,8},{9,1... | collective-permute-start | bytes 258056 | tf_op jit(solution)/shard_map/ppermute | solution.py:421
  26.2 1.4 %collective-permute-start.4 = (f32[32,672]{1,0:T(8,128)S(1)}, f32[32,672]{1,0:T(8,128)S(1)}, u32[]{:S(2)}, u32[]{:S(2)}) collective-permute-start(f32[32,672]{1,0:T(8,128)S(1)} %get-tuple-element.42), channel_id=1, source_target_pairs={{0,1},{1,0},{2,3},{3,2},{4,5},{5,4},{6,7},{7,6},{8,9},{9,8},{10,11... | collective-permute-start | bytes 258056 | tf_op jit(solution)/shard_map/ppermute | solution.py:424
  28.4 4.3 %collective-permute-start.5 = (f32[32,640]{1,0:T(8,128)S(1)}, f32[32,640]{1,0:T(8,128)S(1)}, u32[]{:S(2)}, u32[]{:S(2)}) collective-permute-start(f32[32,640]{1,0:T(8,128)S(1)} %shard_map.75.refs_0_), channel_id=1, source_target_pairs={{0,1},{1,0},{2,3},{3,2},{4,5},{5,4},{6,7},{7,6},{8,9},{9,8},{10,11... | collective-permute-start | bytes 245768 | tf_op jit(solution)/shard_map/ppermute | solution.py:424
  28.6 4.1 %collective-permute-start.6 = (bf16[32,704]{1,0:T(8,128)(2,1)S(1)}, bf16[32,704]{1,0:T(8,128)(2,1)S(1)}, u32[]{:S(2)}, u32[]{:S(2)}) collective-permute-start(bf16[32,704]{1,0:T(8,128)(2,1)S(1)} %get-tuple-element.43.refs_0_), channel_id=1, source_target_pairs={{0,2},{2,0},{1,3},{3,1},{4,6},{6,4},{5,7},{7,5},{8,10},{10,8},{9,1... | collective-permute-start | bytes 135176 | tf_op jit(solution)/shard_map/ppermute | solution.py:421
  32.9 6.2 %collective-permute-start.9 = (bf16[32,704]{1,0:T(8,128)(2,1)S(1)}, bf16[32,704]{1,0:T(8,128)(2,1)S(1)}, u32[]{:S(2)}, u32[]{:S(2)}) collective-permute-start(bf16[32,704]{1,0:T(8,128)(2,1)S(1)} %shard_map.77.refs_0_), channel_id=1, source_target_pairs={{12,0},{8,4},{4,8},{0,12},{13,1},{9,5},{5,9},{1,13},{14,2},{10,6},... | collective-permute-start | bytes 135176 | tf_op jit(solution)/shard_map/ppermute | solution.py:427
  36.5 5.0 %collective-permute-start.8 = (bf16[32,704]{1,0:T(8,128)(2,1)S(1)}, bf16[32,704]{1,0:T(8,128)(2,1)S(1)}, u32[]{:S(2)}, u32[]{:S(2)}) collective-permute-start(bf16[32,704]{1,0:T(8,128)(2,1)S(1)} %shard_map.77.refs_0_), channel_id=1, source_target_pairs={{8,0},{12,4},{0,8},{4,12},{9,1},{13,5},{1,9},{5,13},{10,2},{14,6},... | collective-permute-start | bytes 135176 | tf_op jit(solution)/shard_map/ppermute | solution.py:427
  36.5 5.0 %collective-permute-start.7 = (bf16[32,704]{1,0:T(8,128)(2,1)S(1)}, bf16[32,704]{1,0:T(8,128)(2,1)S(1)}, u32[]{:S(2)}, u32[]{:S(2)}) collective-permute-start(bf16[32,704]{1,0:T(8,128)(2,1)S(1)} %shard_map.77.refs_0_), channel_id=1, source_target_pairs={{4,0},{0,4},{12,8},{8,12},{5,1},{1,5},{13,9},{9,13},{6,2},{2,6},{1... | collective-permute-start | bytes 135176 | tf_op jit(solution)/shard_map/ppermute | solution.py:427
  42.1 4.1 %collective-permute-start.11 = (bf16[32,704]{1,0:T(8,128)(2,1)S(1)}, bf16[32,704]{1,0:T(8,128)(2,1)S(1)}, u32[]{:S(2)}, u32[]{:S(2)}) collective-permute-start(bf16[32,704]{1,0:T(8,128)(2,1)S(1)} %get-tuple-element.45.refs_0_), channel_id=1, source_target_pairs={{0,2},{2,0},{1,3},{3,1},{4,6},{6,4},{5,7},{7,5},{8,10},{10,8},{9,1... | collective-permute-start | bytes 135176 | tf_op jit(solution)/shard_map/ppermute | solution.py:421
  43.0 3.2 %collective-permute-start.10 = (bf16[32,704]{1,0:T(8,128)(2,1)S(1)}, bf16[32,704]{1,0:T(8,128)(2,1)S(1)}, u32[]{:S(2)}, u32[]{:S(2)}) collective-permute-start(bf16[32,704]{1,0:T(8,128)(2,1)S(1)} %get-tuple-element.45.refs_0_), channel_id=1, source_target_pairs={{0,1},{1,0},{2,3},{3,2},{4,5},{5,4},{6,7},{7,6},{8,9},{9,8},{10,11... | collective-permute-start | bytes 135176 | tf_op jit(solution)/shard_map/ppermute | solution.py:424
  46.2 1.2 %collective-permute-start.12 = (bf16[32,704]{1,0:T(8,128)(2,1)S(1)}, bf16[32,704]{1,0:T(8,128)(2,1)S(1)}, u32[]{:S(2)}, u32[]{:S(2)}) collective-permute-start(bf16[32,704]{1,0:T(8,128)(2,1)S(1)} %collective-permute-done.11.refs_2_), channel_id=1, source_target_pairs={{0,1},{1,0},{2,3},{3,2},{4,5},{5,4},{6,7},{7,6},{8,9},{9,8},{10,11... | collective-permute-start | bytes 135176 | tf_op jit(solution)/shard_map/ppermute | solution.py:424
  50.3 1.4 %collective-permute-start.13 = (f32[32,672]{1,0:T(8,128)S(1)}, f32[32,672]{1,0:T(8,128)S(1)}, u32[]{:S(2)}, u32[]{:S(2)}) collective-permute-start(f32[32,672]{1,0:T(8,128)S(1)} %get-tuple-element.48), channel_id=1, source_target_pairs={{0,1},{1,0},{2,3},{3,2},{4,5},{5,4},{6,7},{7,6},{8,9},{9,8},{10,11... | collective-permute-start | bytes 258056 | tf_op jit(solution)/shard_map/ppermute | solution.py:424
  52.6 4.3 %collective-permute-start.14 = (f32[32,640]{1,0:T(8,128)S(1)}, f32[32,640]{1,0:T(8,128)S(1)}, u32[]{:S(2)}, u32[]{:S(2)}) collective-permute-start(f32[32,640]{1,0:T(8,128)S(1)} %shard_map.82.refs_0_), channel_id=1, source_target_pairs={{0,1},{1,0},{2,3},{3,2},{4,5},{5,4},{6,7},{7,6},{8,9},{9,8},{10,11... | collective-permute-start | bytes 245768 | tf_op jit(solution)/shard_map/ppermute | solution.py:424
  52.8 4.1 %collective-permute-start.15 = (bf16[32,704]{1,0:T(8,128)(2,1)S(1)}, bf16[32,704]{1,0:T(8,128)(2,1)S(1)}, u32[]{:S(2)}, u32[]{:S(2)}) collective-permute-start(bf16[32,704]{1,0:T(8,128)(2,1)S(1)} %get-tuple-element.49.refs_0_), channel_id=1, source_target_pairs={{0,2},{2,0},{1,3},{3,1},{4,6},{6,4},{5,7},{7,5},{8,10},{10,8},{9,1... | collective-permute-start | bytes 135176 | tf_op jit(solution)/shard_map/ppermute | solution.py:421
  57.1 10.7 %collective-permute-start.16 = (f32[32,2048]{1,0:T(8,128)S(1)}, f32[32,2048]{1,0:T(8,128)S(1)}, u32[]{:S(2)}, u32[]{:S(2)}) collective-permute-start(f32[32,2048]{1,0:T(8,128)S(1)} %get-tuple-element.51.h_ref.refs_0_), channel_id=1, source_target_pairs={{0,2},{2,0},{1,3},{3,1},{4,6},{6,4},{5,7},{7,5},{8,10},{10,8},{9,1... | collective-permute-start | bytes 786440 | tf_op jit(solution)/shard_map/ppermute | solution.py:421
  58.0 6.1 %collective-permute-start.19 = (bf16[32,704]{1,0:T(8,128)(2,1)S(1)}, bf16[32,704]{1,0:T(8,128)(2,1)S(1)}, u32[]{:S(2)}, u32[]{:S(2)}) collective-permute-start(bf16[32,704]{1,0:T(8,128)(2,1)S(1)} %shard_map.84.refs_0_), channel_id=1, source_target_pairs={{12,0},{8,4},{4,8},{0,12},{13,1},{9,5},{5,9},{1,13},{14,2},{10,6},... | collective-permute-start | bytes 135176 | tf_op jit(solution)/shard_map/ppermute | solution.py:427
  60.3 5.1 %collective-permute-start.18 = (bf16[32,704]{1,0:T(8,128)(2,1)S(1)}, bf16[32,704]{1,0:T(8,128)(2,1)S(1)}, u32[]{:S(2)}, u32[]{:S(2)}) collective-permute-start(bf16[32,704]{1,0:T(8,128)(2,1)S(1)} %shard_map.84.refs_0_), channel_id=1, source_target_pairs={{8,0},{12,4},{0,8},{4,12},{9,1},{13,5},{1,9},{5,13},{10,2},{14,6},... | collective-permute-start | bytes 135176 | tf_op jit(solution)/shard_map/ppermute | solution.py:427
  60.4 5.1 %collective-permute-start.17 = (bf16[32,704]{1,0:T(8,128)(2,1)S(1)}, bf16[32,704]{1,0:T(8,128)(2,1)S(1)}, u32[]{:S(2)}, u32[]{:S(2)}) collective-permute-start(bf16[32,704]{1,0:T(8,128)(2,1)S(1)} %shard_map.84.refs_0_), channel_id=1, source_target_pairs={{4,0},{0,4},{12,8},{8,12},{5,1},{1,5},{13,9},{9,13},{6,2},{2,6},{1... | collective-permute-start | bytes 135176 | tf_op jit(solution)/shard_map/ppermute | solution.py:427
  66.3 1.5 %collective-permute-start.20 = (f32[32,1280]{1,0:T(8,128)S(1)}, f32[32,1280]{1,0:T(8,128)S(1)}, u32[]{:S(2)}, u32[]{:S(2)}) collective-permute-start(f32[32,1280]{1,0:T(8,128)S(1)} %shard_map.85.refs_2_), channel_id=1, source_target_pairs={{0,1},{1,0},{2,3},{3,2},{4,5},{5,4},{6,7},{7,6},{8,9},{9,8},{10,11... | collective-permute-start | bytes 491528 | tf_op jit(solution)/shard_map/ppermute | solution.py:424

commit v5 on v4

--- a/solution.py
+++ b/solution.py
@@ -61,38 +61,64 @@
     out_ref[:, size + rank : size + 2 * rank] = rest
 
 
-def fetch_kernel(w_hbm, h_hbm, tab_hbm, order_hbm, *refs):
-    w_ref, old_ref, tab_ref, order_ref, msg_ref, gram_ref, sems = refs[-7:]
+def fetch_kernel(w_hbm, h_hbm, order_hbm, *refs):
+    piece_ref, msg_ref, gram_ref, old_ref, order_ref, w_scr, sems = refs[-7:]
     frames = old_ref.shape[1]
+    size = piece_ref.shape[1]
     mine = pl.ds(pl.multiple_of(lax.axis_index("row") * frames, TAPS), frames)
     copies = [
-        pltpu.make_async_copy(w_hbm, w_ref, sems.at[0]),
-        pltpu.make_async_copy(tab_hbm, tab_ref, sems.at[1]),
+        pltpu.make_async_copy(w_hbm, w_scr, sems.at[0]),
+        pltpu.make_async_copy(order_hbm, order_ref, sems.at[1]),
         pltpu.make_async_copy(h_hbm.at[:, mine], old_ref, sems.at[2]),
-        pltpu.make_async_copy(order_hbm, order_ref, sems.at[3]),
     ]
     for copy in copies:
         copy.start()
     copies[0].wait()
-    w = w_ref[...]
+    w = w_scr[...]
+    rank = w.shape[0]
     gram = lax.dot_general(w, w, NT, precision=HIGH, preferred_element_type=F32)
     gram_ref[...] = gram
-    pack(msg_ref, w, gram)
-    for copy in copies[1:]:
-        copy.wait()
-
-
-def cut_edges_kernel(rows, sig_hbm, *refs):
-    out_refs, sems = refs[:rows], refs[rows]
-    window, x_me = sig_hbm.shape[1], lax.axis_index("row")
-    copies = []
-    for at in range(rows):
-        begin = pl.multiple_of(jnp.where(x_me == at, window - TAPS, 0), TAPS)
-        copies.append(pltpu.make_async_copy(sig_hbm.at[:, pl.ds(begin, TAPS)], out_refs[at], sems.at[at]))
-    for copy in copies:
-        copy.start()
-    for copy in copies:
-        copy.wait()
+    terms = three_terms(w)
+    copies[1].wait()
+    moved = jnp.dot(terms, order_ref[...], preferred_element_type=F32)
+    whole = moved[:rank] + (moved[rank : 2 * rank] + moved[2 * rank :])
+    for c in range(w.shape[1] // size):
+
+        @pl.when(lax.axis_index("sub") == c)
+        def _():
+            piece_ref[...] = whole[:, c * size : (c + 1) * size]
+
+    pack(msg_ref, whole, gram)
+    copies[2].wait()
+
+
+def table_kernel(tab_hbm, *refs):
+    tab_ref, sem = refs[-2:]
+    copy = pltpu.make_async_copy(tab_hbm, tab_ref, sem)
+    copy.start()
+    copy.wait()
+
+
+def three_terms(value):
+    top = value.astype(BF16)
+    rest = value - top.astype(F32)
+    middle = rest.astype(BF16)
+    return jnp.concatenate([top, middle, (rest - middle.astype(F32)).astype(BF16)], axis=0)
+
+
+def edges_kernel(rows, sig_ref, *refs):
+    got_refs, out_ref = refs[: rows - 1], refs[rows - 1]
+    cl, width = sig_ref.shape
+    x_me = lax.axis_index("row")
+    for at, ref in enumerate((sig_ref,) + tuple(got_refs)):
+
+        @pl.when(x_me == 0)
+        def _():
+            out_ref[at * cl : (at + 1) * cl, :] = ref[:, :TAPS]
+
+        @pl.when(x_me > 0)
+        def _():
+            out_ref[at * cl : (at + 1) * cl, :] = ref[:, width - TAPS :]
 
 
 def cut_signal_kernel(rows, frames, sig_hbm, *refs):
@@ -115,9 +141,12 @@
     return jnp.concatenate(halves, axis=1)
 
 
-def group_rows(s_ref, g, pair, rows, cl):
-    span = slice(g * GROUP, (g + 1) * GROUP)
-    return jnp.concatenate([pair_rows(s_ref, span, pair, x, cl) for x in range(rows)], axis=0)
+def numerators(parts, s_ref, num_ref, cl):
+    for pair in range(num_ref.shape[1] // (2 * TAPS)):
+        terms = [
+            jnp.dot(w, pair_rows(s_ref, slice(None), pair, x, cl), preferred_element_type=F32) for w, x in parts
+        ]
+        num_ref[:, 2 * TAPS * pair : 2 * TAPS * (pair + 1)] = functools.reduce(jnp.add, terms)
 
 
 def crossed(low, s_ref, x, core, subs, cl):
@@ -136,20 +165,12 @@
     return [(dx, dc) for dx in range(1, rows) for dc in range(1, subs)]
 
 
-def new_activations(old, gram, w_scr, num_scr, s_ref, h_out, h_gram_ref, msg_refs, rows, subs, cl):
-    rank, frames = old.shape
-    per_sub = GROUPS // subs
-    for pair in range(frames // (2 * TAPS)):
-        acc = jnp.zeros((rank, 2 * TAPS), F32)
-        for g in range(GROUPS):
-            wg = jnp.concatenate([w_scr[g // per_sub, g % per_sub, x] for x in range(rows)], axis=1)
-            acc = acc + jnp.dot(wg, group_rows(s_ref, g, pair, rows, cl), preferred_element_type=F32)
-        num_scr[:, 2 * TAPS * pair : 2 * TAPS * (pair + 1)] = acc
-    new = old * num_scr[...] / jnp.dot(gram, old, precision=HIGH, preferred_element_type=F32)
+def new_activations(old, gram, above, s_ref, h_out, h_gram_ref, msg_refs, rows, subs, cl):
+    new = old * above / jnp.dot(gram, old, precision=HIGH, preferred_element_type=F32)
     h_out[...] = new
     h_gram = lax.dot_general(new, new, NT, precision=HIGH, preferred_element_type=F32)
     h_gram_ref[...] = h_gram
-    size = per_sub * GROUP * cl
+    size = NF // subs * cl
     x_me, c_me = lax.axis_index("row"), lax.axis_index("sub")
     for ref, (dx, dc) in zip(msg_refs, others_of(rows, subs)):
         ref[:, :size] = crossed(
@@ -168,8 +189,7 @@
 def spectra_kernel(rows, cl, blocks, *refs):
     refs = list(refs)
     sig_refs = [refs.pop(0) for _ in range(rows)]
-    halo_refs = [refs.pop(0) for _ in range(rows)]
-    tab_ref, s_ref, xp_scr, x_scr = refs
+    halo_ref, tab_ref, s_ref, xp_scr, x_scr = refs
     frames = blocks * TAPS
     width = sig_refs[0].shape[1]
     x_me = lax.axis_index("row")
@@ -196,12 +216,12 @@
     @pl.when(x_me == 0)
     def _():
         for at in range(rows):
-            xp_scr[at, :, :HALF] = halo_refs[at][:, HALF:]
+            xp_scr[rows - 1 - at, :, :HALF] = halo_ref[at * cl : (at + 1) * cl, HALF:]
 
     @pl.when(x_me == rows - 1)
     def _():
         for at in range(rows):
-            xp_scr[rows - 1 - at, :, frames + HALF :] = halo_refs[at][:, :HALF]
+            xp_scr[(rows - at) % rows, :, frames + HALF :] = halo_ref[at * cl : (at + 1) * cl, :HALF]
 
     for blk in range(blocks):
         for x in range(rows):
@@ -223,62 +243,48 @@
 
 def first_kernel(rows, subs, cl, *refs):
     refs = list(refs)
-    w_ref, gram_ref = (refs.pop(0) for _ in range(2))
-    w_msgs = [refs.pop(0) for _ in range(rows - 1)]
-    order_ref, h_ref, s_ref = (refs.pop(0) for _ in range(3))
-    w_out, h_out, h_gram_ref = (refs.pop(0) for _ in range(3))
-    msg_refs, (w_scr, num_scr) = refs[:-2], refs[-2:]
-    rank = h_ref.shape[0]
-    per_sub = GROUPS // subs
-    wide = GROUP * cl
+    w_refs = [refs.pop(0) for _ in range(rows)]
+    h_ref, s_ref, h_out, h_gram_ref = (refs.pop(0) for _ in range(4))
+    msg_refs, num_scr = refs[:-1], refs[-1]
+    x_me = lax.axis_index("row")
+    parts, gram = [], jnp.zeros(h_gram_ref.shape, F32)
+    for shift, ref in enumerate(w_refs):
+        parts.append((ref[:, : NF * cl], lax.rem(x_me + rows - shift, rows)))
+        gram = gram + joined(ref, NF * cl, h_ref.shape[0])
+    numerators(parts, s_ref, num_scr, cl)
+    new_activations(h_ref[...], gram, num_scr[...], s_ref, h_out, h_gram_ref, msg_refs, rows, subs, cl)
+
+
+def row_parts(rows, subs, cl, w_refs, w_scr, shifts):
     x_me, c_me = lax.axis_index("row"), lax.axis_index("sub")
-    w = w_ref[...]
-    top = w.astype(BF16)
-    rest = w - top.astype(F32)
-    middle = rest.astype(BF16)
-    terms = [top, middle, (rest - middle.astype(F32)).astype(BF16)] + [ref[:, : NF * cl] for ref in w_msgs]
-    moved = jnp.dot(jnp.concatenate(terms, axis=0), order_ref[...], preferred_element_type=F32)
-    for at in range(GROUPS):
-        cols = slice(at * wide, (at + 1) * wide)
-        w_scr[at // per_sub, at % per_sub, x_me] = moved[:rank, cols].astype(BF16)
-        for shift in range(1, rows):
-            owner = lax.rem(x_me + rows - shift, rows)
-            line = (shift + 2) * rank
-            w_scr[at // per_sub, at % per_sub, owner] = moved[line : line + rank, cols].astype(BF16)
-    whole = moved[:rank] + (moved[rank : 2 * rank] + moved[2 * rank : 3 * rank])
-    size = per_sub * wide
-    for c in range(subs):
-
-        @pl.when(c_me == c)
-        def _():
-            w_out[...] = whole[:, c * size : (c + 1) * size]
-
-    gram = gram_ref[...]
-    for ref in w_msgs:
-        gram = gram + joined(ref, NF * cl, rank)
-    new_activations(h_ref[...], gram, w_scr, num_scr, s_ref, h_out, h_gram_ref, msg_refs, rows, subs, cl)
+    size = NF // subs * cl
+    parts = []
+    for line, dx in enumerate(shifts):
+        for dc in range(subs):
+            w_scr[line, lax.rem(c_me + subs - dc, subs)] = w_refs[line * subs + dc][:, :size]
+        w = jnp.concatenate([w_scr[line, c] for c in range(subs)], axis=1)
+        parts.append((w, lax.rem(x_me + rows - dx, rows)))
+    return parts
+
+
+def early_kernel(rows, subs, cl, *refs):
+    w_refs, (s_ref, num_ref, w_scr) = refs[:subs], refs[subs:]
+    numerators(row_parts(rows, subs, cl, w_refs, w_scr, [0]), s_ref, num_ref, cl)
 
 
 def later_kernel(rows, subs, cl, *refs):
     refs = list(refs)
     w_refs = [refs.pop(0) for _ in range(rows * subs)]
-    h_ref, s_ref = refs.pop(0), refs.pop(0)
-    h_out, h_gram_ref = (refs.pop(0) for _ in range(2))
+    early_ref, h_ref, s_ref, h_out, h_gram_ref = (refs.pop(0) for _ in range(5))
     msg_refs, (w_scr, num_scr) = refs[:-2], refs[-2:]
-    rank = h_ref.shape[0]
-    per_sub = GROUPS // subs
-    wide = GROUP * cl
-    x_me, c_me = lax.axis_index("row"), lax.axis_index("sub")
-    gram = jnp.zeros((rank, rank), F32)
-    at = 0
-    for dx in range(rows):
-        for dc in range(subs):
-            x_of, c_of = lax.rem(x_me + rows - dx, rows), lax.rem(c_me + subs - dc, subs)
-            for part in range(per_sub):
-                w_scr[c_of, part, x_of] = w_refs[at][:, part * wide : (part + 1) * wide]
-            gram = gram + joined(w_refs[at], per_sub * wide, rank)
-            at += 1
-    new_activations(h_ref[...], gram, w_scr, num_scr, s_ref, h_out, h_gram_ref, msg_refs, rows, subs, cl)
+    gram = jnp.zeros(h_gram_ref.shape, F32)
+    for ref in w_refs:
+        gram = gram + joined(ref, NF // subs * cl, h_ref.shape[0])
+    above = early_ref[...]
+    if rows > 1:
+        numerators(row_parts(rows, subs, cl, w_refs[subs:], w_scr, list(range(1, rows))), s_ref, num_scr, cl)
+        above = above + num_scr[...]
+    new_activations(h_ref[...], gram, above, s_ref, h_out, h_gram_ref, msg_refs, rows, subs, cl)
 
 
 def core_kernel(count, rank, *refs):
@@ -341,10 +347,7 @@
     total, gram = summed(lax.axis_index("frm"), count, msg_refs, scr, rank, size)
     w = w_ref[...]
     new = w * total / jnp.dot(gram, w, precision=HIGH, preferred_element_type=F32)
-    top = new.astype(BF16)
-    rest = new - top.astype(F32)
-    middle = rest.astype(BF16)
-    terms = jnp.concatenate([top, middle, (rest - middle.astype(F32)).astype(BF16)], axis=0)
+    terms = three_terms(new)
     for c in range(order_ref.shape[1] // size):
 
         @pl.when(lax.axis_index("sub") == c)
@@ -429,56 +432,50 @@
     def place(x, at):
         return (at // subs * rows + x) * subs + at % subs
 
-    edges = call(
-        functools.partial(cut_edges_kernel, rows),
+    own_sig, *out_sigs = call(
+        functools.partial(cut_signal_kernel, rows, frames),
         [hbm(signal)],
-        [((cl, TAPS), BF16)] * rows,
+        [((cl, width), BF16)] * rows,
         [pltpu.SemaphoreType.DMA((rows,))],
         in_specs=[anywhere],
     )
-    halos = [None] * rows
-    for at in reversed(range(rows)):
-        to_next = [(place(at, i), place(0, i + 1)) for i in range(line - 1)]
-        to_prev = [(place(rows - 1 - at, i + 1), place(rows - 1, i)) for i in range(line - 1)]
-        halos[at] = lax.ppermute(edges[at], ("frm", "row", "sub"), to_next + to_prev)
-    own_sig, *out_sigs = call(
-        functools.partial(cut_signal_kernel, rows, frames),
-        [hbm(signal)] + list(edges),
-        [((cl, width), BF16)] * rows,
-        [pltpu.SemaphoreType.DMA((rows,))],
-        in_specs=[anywhere] * (rows + 1),
-    )
     sig = [own_sig] + [row_shift(part, shift + 1) for shift, part in enumerate(out_sigs)]
+    (edge,) = call(functools.partial(edges_kernel, rows), sig, [((chans, TAPS), BF16)])
+    pairs = [(place(rows - 1, i), place(0, i + 1)) for i in range(line - 1)]
+    halo = lax.ppermute(edge, ("frm", "row", "sub"), pairs + [(b, a) for a, b in pairs])
 
     msg = ((rank, size + 2 * rank), BF16)
     piece = ((rank, size), F32)
     update_outs = [((rank, frames), F32), ((rank, rank), F32)]
     update_outs += [((rank, size + rank), F32)] * ((rows - 1) * (subs - 1))
-    update_scratch = [
-        pltpu.VMEM((subs, GROUPS // subs, rows, rank, GROUP * cl), BF16),
-        pltpu.VMEM((rank, frames), F32),
-    ]
     table, order = jnp.asarray(toeplitz()), jnp.asarray(reorder(cl))
-    w_own, old, table, order, w_msg, w_gram = call(
+    w_piece, w_msg, w_gram, old, order = call(
         fetch_kernel,
-        [hbm(w_start.T), hbm(h_start), hbm(table), hbm(order), own_sig],
+        [hbm(w_start.T), hbm(h_start), hbm(order), own_sig],
         [
-            pltpu.VMEM((rank, NF * cl), F32),
-            pltpu.VMEM((rank, frames), F32),
-            pltpu.VMEM(table.shape, BF16),
-            pltpu.VMEM(order.shape, BF16),
+            piece,
             ((rank, NF * cl + 2 * rank), BF16),
             ((rank, rank), F32),
+            pltpu.VMEM((rank, frames), F32),
+            pltpu.VMEM(order.shape, BF16),
         ],
-        [pltpu.SemaphoreType.DMA((4,))],
-        in_specs=[anywhere] * 5,
+        [pltpu.VMEM((rank, NF * cl), F32), pltpu.SemaphoreType.DMA((3,))],
+        in_specs=[anywhere] * 4,
         cost=2 * 10**9,
     )
-    w_msgs = [row_shift(w_msg, shift) for shift in range(1, rows)]
+    w_msgs = [w_msg] + [row_shift(w_msg, shift) for shift in range(1, rows)]
     order = vmem(order)
+    (table,) = call(
+        table_kernel,
+        [hbm(table), edge],
+        [pltpu.VMEM(table.shape, BF16)],
+        [pltpu.SemaphoreType.DMA],
+        in_specs=[anywhere] * 2,
+        cost=2 * 10**9,
+    )
     (spectra,) = call(
         functools.partial(spectra_kernel, rows, cl, blocks),
-        sig + halos + [vmem(table)],
+        sig + [halo, vmem(table)],
         [pltpu.VMEM((NF, blocks, rows, cl, TAPS), BF16)],
         [pltpu.VMEM((rows, cl, frames + TAPS), BF16), pltpu.VMEM((blocks, chans, 2 * TAPS), BF16)],
         limit=8,
@@ -497,25 +494,25 @@
 
     def gathered(activations, h_gram, msgs):
         got = [sub_shift(m, dc) for m, (_, dc) in zip(msgs, others_of(rows, subs))]
-        out_places = [(dx, 0) for dx in range(1, rows)]
-        own = products(out_places, activations, [])
+        places = [(dx, 0) for dx in range(1, rows)] + [(0, dc) for dc in range(1, subs)]
+        formed = products(places, activations, [])
+        for_rows, for_cores = formed[: rows - 1], formed[rows - 1 :]
+        from_cores = [sub_shift(m, dc + 1) for dc, m in enumerate(for_cores)]
         *outs, gram = call(
             functools.partial(core_kernel, rows - 1, rank),
-            list(own) + [h_gram] + got,
+            list(for_rows) + [h_gram] + got,
             [msg] * (rows - 1) + [((rank, rank), F32)],
         )
         from_rows = [row_shift(m, dx + 1) for dx, m in enumerate(outs)]
-        for_cores = products([(0, dc) for dc in range(1, subs)], activations, outs)
-        from_cores = [sub_shift(m, dc + 1) for dc, m in enumerate(for_cores)]
-        (own,) = products([(0, 0)], activations, list(for_cores))
+        (own,) = products([(0, 0)], activations, outs)
         (part,) = call(functools.partial(row_kernel, subs), [own, gram] + from_cores + from_rows, [msg])
         return [part] + [frm_shift(part, shift) for shift in range(1, frms)]
 
-    w_piece, activations, h_gram, *msgs = call(
+    activations, h_gram, *msgs = call(
         functools.partial(first_kernel, rows, subs, cl),
-        [vmem(w_own), w_gram] + w_msgs + [order, vmem(old), spectra],
-        [piece] + update_outs,
-        update_scratch,
+        w_msgs + [vmem(old), spectra],
+        update_outs,
+        [pltpu.VMEM((rank, frames), F32)],
         limit=8,
     )
     piled = [pltpu.VMEM((frms,) + msg[0], BF16)]
@@ -525,15 +522,24 @@
         [piece, msg],
         piled,
     )
-    w_msgs = []
-    for dx in range(rows):
-        base = row_shift(w_msg, dx) if dx else w_msg
+    w_msgs = [w_msg] + [sub_shift(w_msg, dc) for dc in range(1, subs)]
+    w_pieces = pltpu.VMEM((rows, subs, rank, size), BF16)
+    (early,) = call(
+        functools.partial(early_kernel, rows, subs, cl),
+        w_msgs + [spectra],
+        [((rank, frames), F32)],
+        [w_pieces],
+        cost=16 * NF * cl * frames * rank,
+    )
+    from_rows = [row_shift(w_msg, dx) for dx in range(1, rows)]
+    *from_rows, early = lax.optimization_barrier((*from_rows, early))
+    for base in from_rows:
         w_msgs += [base] + [sub_shift(base, dc) for dc in range(1, subs)]
     activations, h_gram, *msgs = call(
         functools.partial(later_kernel, rows, subs, cl),
-        w_msgs + [activations, spectra],
+        w_msgs + [early, activations, spectra],
         update_outs,
-        update_scratch,
+        [w_pieces, pltpu.VMEM((rank, frames), F32)],
         limit=8,
     )
     parts = gathered(activations, h_gram, msgs)

time: 68.9 us -> 68.1 us (0.988)
  starting transfers between devices: 22.8 us -> 20.1 us
  Pallas kernels: 27.3 us -> 28.4 us
  waiting for transfers between devices: 17.9 us -> 18.7 us
    ppermute x6, starting transfers between devices: 10.2 us -> 6.43 us  [row_shift(): lax.ppermute(value, 'row', [(i, (i + shift) % rows) for i in range(rows)])]
    ppermute x7, starting transfers between devices: 0.81 us -> 4.12 us  [sub_shift(): lax.ppermute(value, 'sub', [(i, (i + shift) % subs) for i in range(subs)])]
    ppermute x2 -> x1, starting transfers between devices: 3.02 us -> 0.65 us  [shards(): lax.ppermute(edge, ('frm', 'row', 'sub'), pairs + [(b, a) for a, b in pai...]
    ppermute x6, waiting for transfers between devices: 7.27 us -> 8.98 us  [frm_shift(): lax.ppermute(value, 'frm', [(partner(i, shift, frms), i) for i in range(f...]
    pallas_call x19, Pallas kernels: 27.3 us -> 28.4 us  [call(): pl.pallas_call(kernel, out_shape=[jax.ShapeDtypeStruct(*out) if isinstanc...]
    ppermute x6, waiting for transfers between devices: 7.2 us -> 6.49 us  [row_shift(): lax.ppermute(value, 'row', [(i, (i + shift) % rows) for i in range(rows)])]
  transfers between devices with their start and end apart: 21 -> 20, of which waited for: 12 -> 11; matrix products, arithmetic and copies ran while one was open for 0% -> 0% of each run, Pallas kernels for 24% -> 30%
where the time goes in v5:
time: 68.1 us; the launch traced here: 68 us
  Pallas kernels  28.4 us (42%)
  starting transfers between devices  20.1 us (30%)
  waiting for transfers between devices  18.7 us (27%)
  between operations  0.79 us (1%)
    pallas_call x19, Pallas kernels, call(): pl.pallas_call(kernel, out_shape=[jax.ShapeDtypeStruct(*out) if isinstanc...  28.4 us
    ppermute x6, waiting for transfers between devices, frm_shift(): lax.ppermute(value, 'frm', [(partner(i, shift, frms), i) for i in range(f...  8.98 us
    ppermute x6, starting transfers between devices, frm_shift(): lax.ppermute(value, 'frm', [(partner(i, shift, frms), i) for i in range(f...  8.91 us
    ppermute x6, waiting for transfers between devices, row_shift(): lax.ppermute(value, 'row', [(i, (i + shift) % rows) for i in range(rows)])  6.49 us
    ppermute x6, starting transfers between devices, row_shift(): lax.ppermute(value, 'row', [(i, (i + shift) % rows) for i in range(rows)])  6.43 us
    ppermute x7, starting transfers between devices, sub_shift(): lax.ppermute(value, 'sub', [(i, (i + shift) % subs) for i in range(subs)])  4.12 us
    ppermute x7, waiting for transfers between devices, sub_shift(): lax.ppermute(value, 'sub', [(i, (i + shift) % subs) for i in range(subs)])  3.19 us
  transfers between devices with their start and end apart: 20, of which 11 were waited for; matrix products, arithmetic and copies ran while one was open for 0% of the time, Pallas kernels for 30%

profile of v5, /device:TPU:0, one launch (start us, length us, event | category | flops | bytes accessed | tf_op | source)
XLA Modules:
  0.0 68.0 jit_solution(16281415881058369426)
XLA Ops:
  0.6 1.0 %shard_map.68 = (bf16[32,2176]{1,0:T(8,128)(2,1)S(1)}, bf16[32,2176]{1,0:T(8,128)(2,1)S(1)}) custom-call(bf16[32,4096]{1,0:T(8,128)(2,1)} %sig_hbm.1), custom_call_target="tpu_custom_call" | custom-call | tf_op jit(solution)/shard_map/pallas_call | solution.py:385
  1.7 3.0 %collective-permute-start.1 = (bf16[32,2176]{1,0:T(8,128)(2,1)S(1)}, bf16[32,2176]{1,0:T(8,128)(2,1)S(1)}, u32[]{:S(2)}, u32[]{:S(2)}) collective-permute-start(bf16[32,2176]{1,0:T(8,128)(2,1)S(1)} %get-tuple-element.34), channel_id=1, source_target_pairs={{0,2},{2,0},{1,3},{3,1},{4,6},{6,4},{5,7},{7,5},{8,10},{10,8},{9,1... | collective-permute-start | bytes 417800 | tf_op jit(solution)/shard_map/ppermute | solution.py:424
  4.7 3.5 %shard_map.69 = (f32[32,640]{1,0:T(8,128)S(1)}, bf16[32,1344]{1,0:T(8,128)(2,1)S(1)}, f32[32,32]{1,0:T(8,128)}, f32[32,2048]{1,0:T(8,128)S(1)}, bf16[1280,1280]{1,0:T(8,128)(2,1)S(1)}) custom-call(f32[32,1280]{1,0:T(8,128)} %bitcast.2, f32[32,4096]{1,0:T(8,128)} %h_hbm.1, bf16[1280,1280]{1,0:T(8,128)(2,1)} %constant.5.clone.order_hbm, ...), custom_call_target="tpu_custom_call" | custom-call | flops 2000000000 | tf_op jit(solution)/shard_map/pallas_call | solution.py:385
  8.1 0.1 collective-permute-start
  8.2 0.1 collective-permute-done.1.refs_0_.refs_1_
  8.3 0.7 collective-permute-start.2
  9.0 2.5 %shard_map.71.refs_3_ = bf16[40,256,256]{2,1,0:T(8,128)(2,1)S(1)} custom-call(bf16[40,256,256]{2,1,0:T(8,128)(2,1)} %constant.4.clone.tab_hbm, bf16[64,128]{1,0:T(8,128)(2,1)S(1)} %shard_map.70.refs_0_), custom_call_target="tpu_custom_call" | custom-call | flops 2000000000 | tf_op jit(solution)/shard_map/pallas_call | solution.py:385
  11.5 0.0 collective-permute-done.2.refs_2_
  11.5 7.5 %shard_map.72.refs_3_.s_ref.refs_2_.refs_6_ = bf16[40,16,2,32,128]{4,3,2,1,0:T(8,128)(2,1)S(1)} custom-call(bf16[32,2176]{1,0:T(8,128)(2,1)S(1)} %get-tuple-element.30.refs_0_.sig_ref, bf16[32,2176]{1,0:T(8,128)(2,1)S(1)} %collective-permute-done.1.refs_0_.refs_1_, bf16[64,128]{1,0:T(8,128)(2,1)S(1)} %collective-permute-done.2.refs_2_, ...), custom_call_target="tpu_custom_call" | custom-call | flops 5368709120 | tf_op jit(solution)/shard_map/pallas_call | solution.py:385
  19.0 0.0 collective-permute-done.refs_1_
  19.0 3.0 %shard_map.73 = (f32[32,2048]{1,0:T(8,128)S(1)}, f32[32,32]{1,0:T(8,128)S(1)}, f32[32,672]{1,0:T(8,128)S(1)}) custom-call(bf16[32,1344]{1,0:T(8,128)(2,1)S(1)} %get-tuple-element.32.refs_0_, bf16[32,1344]{1,0:T(8,128)(2,1)S(1)} %collective-permute-done.refs_1_, f32[32,2048]{1,0:T(8,128)S(1)} %get-tuple-element.33.refs_2_, ...), custom_call_target="tpu_custom_call" | custom-call | tf_op jit(solution)/shard_map/pallas_call | solution.py:385
  22.1 3.3 %collective-permute-start.3 = (f32[32,672]{1,0:T(8,128)S(1)}, f32[32,672]{1,0:T(8,128)S(1)}, u32[]{:S(2)}, u32[]{:S(2)}) collective-permute-start(f32[32,672]{1,0:T(8,128)S(1)} %get-tuple-element.38), channel_id=1, source_target_pairs={{0,1},{1,0},{2,3},{3,2},{4,5},{5,4},{6,7},{7,6},{8,9},{9,8},{10,11... | collective-permute-start | bytes 258056 | tf_op jit(solution)/shard_map/ppermute | solution.py:427
  25.4 1.6 %shard_map.74 = (f32[32,640]{1,0:T(8,128)S(1)}, f32[32,640]{1,0:T(8,128)S(1)}) custom-call(f32[32,2048]{1,0:T(8,128)S(1)} %get-tuple-element.35.h_ref.refs_5_, bf16[40,16,2,32,128]{4,3,2,1,0:T(8,128)(2,1)S(1)} %shard_map.72.refs_3_.s_ref.refs_2_.refs_6_), custom_call_target="tpu_custom_call" | custom-call | flops 1342177280 | tf_op jit(solution)/shard_map/pallas_call | solution.py:385
  27.0 0.1 collective-permute-start.4
  27.1 0.0 collective-permute-done.3.refs_2_
  27.1 0.1 shard_map.75
  27.2 1.6 %collective-permute-start.5 = (bf16[32,704]{1,0:T(8,128)(2,1)S(1)}, bf16[32,704]{1,0:T(8,128)(2,1)S(1)}, u32[]{:S(2)}, u32[]{:S(2)}) collective-permute-start(bf16[32,704]{1,0:T(8,128)(2,1)S(1)} %get-tuple-element.39.refs_0_), channel_id=1, source_target_pairs={{0,2},{2,0},{1,3},{3,1},{4,6},{6,4},{5,7},{7,5},{8,10},{10,8},{9,1... | collective-permute-start | bytes 135176 | tf_op jit(solution)/shard_map/ppermute | solution.py:424
  28.7 0.8 %shard_map.76.own_ref = f32[32,640]{1,0:T(8,128)S(1)} custom-call(f32[32,2048]{1,0:T(8,128)S(1)} %get-tuple-element.35.h_ref.refs_5_, bf16[40,16,2,32,128]{4,3,2,1,0:T(8,128)(2,1)S(1)} %shard_map.72.refs_3_.s_ref.refs_2_.refs_6_, bf16[32,704]{1,0:T(8,128)(2,1)S(1)} %get-tuple-element.39.refs_0_), custom_call_target="tpu_custom_call" | custom-call | flops 1 | tf_op jit(solution)/shard_map/pallas_call | solution.py:385
  29.6 0.0 collective-permute-done.4.refs_0_
  29.6 1.7 %collective-permute-done.5.refs_1_ = bf16[32,704]{1,0:T(8,128)(2,1)S(1)} collective-permute-done((bf16[32,704]{1,0:T(8,128)(2,1)S(1)}, bf16[32,704]{1,0:T(8,128)(2,1)S(1)}, u32[]{:S(2)}, u32[]{:S(2)}) %collective-permute-start.5) | collective-permute-done | bytes 45088 | tf_op jit(solution)/shard_map/ppermute | solution.py:424
  31.3 0.2 shard_map.77.refs_0_
  31.5 1.9 %collective-permute-start.6 = (bf16[32,704]{1,0:T(8,128)(2,1)S(1)}, bf16[32,704]{1,0:T(8,128)(2,1)S(1)}, u32[]{:S(2)}, u32[]{:S(2)}) collective-permute-start(bf16[32,704]{1,0:T(8,128)(2,1)S(1)} %shard_map.77.refs_0_), channel_id=1, source_target_pairs={{4,0},{0,4},{12,8},{8,12},{5,1},{1,5},{13,9},{9,13},{6,2},{2,6},{1... | collective-permute-start | bytes 135176 | tf_op jit(solution)/shard_map/ppermute | solution.py:430
  33.4 2.6 %collective-permute-start.7 = (bf16[32,704]{1,0:T(8,128)(2,1)S(1)}, bf16[32,704]{1,0:T(8,128)(2,1)S(1)}, u32[]{:S(2)}, u32[]{:S(2)}) collective-permute-start(bf16[32,704]{1,0:T(8,128)(2,1)S(1)} %shard_map.77.refs_0_), channel_id=1, source_target_pairs={{8,0},{12,4},{0,8},{4,12},{9,1},{13,5},{1,9},{5,13},{10,2},{14,6},... | collective-permute-start | bytes 135176 | tf_op jit(solution)/shard_map/ppermute | solution.py:430
  36.0 0.0 collective-permute-start.8
  36.0 0.0 collective-permute-done.6.refs_1_
  36.0 3.4 %collective-permute-done.7.refs_2_ = bf16[32,704]{1,0:T(8,128)(2,1)S(1)} collective-permute-done((bf16[32,704]{1,0:T(8,128)(2,1)S(1)}, bf16[32,704]{1,0:T(8,128)(2,1)S(1)}, u32[]{:S(2)}, u32[]{:S(2)}) %collective-permute-start.7) | collective-permute-done | bytes 45088 | tf_op jit(solution)/shard_map/ppermute | solution.py:430
  39.4 2.4 %collective-permute-done.8.refs_3_ = bf16[32,704]{1,0:T(8,128)(2,1)S(1)} collective-permute-done((bf16[32,704]{1,0:T(8,128)(2,1)S(1)}, bf16[32,704]{1,0:T(8,128)(2,1)S(1)}, u32[]{:S(2)}, u32[]{:S(2)}) %collective-permute-start.8) | collective-permute-done | bytes 45088 | tf_op jit(solution)/shard_map/ppermute | solution.py:430
  41.9 0.6 shard_map.78
  42.5 0.0 collective-permute-start.9
  42.5 0.6 collective-permute-start.10
  43.2 0.6 collective-permute-done.9.refs_1_
  43.7 1.0 %shard_map.79.refs_4_ = f32[32,2048]{1,0:T(8,128)S(1)} custom-call(bf16[32,704]{1,0:T(8,128)(2,1)S(1)} %get-tuple-element.42.refs_0_, bf16[32,704]{1,0:T(8,128)(2,1)S(1)} %collective-permute-done.9.refs_1_, bf16[40,16,2,32,128]{4,3,2,1,0:T(8,128)(2,1)S(1)} %shard_map.72.refs_3_.s_ref.refs_2_.refs_6_), custom_call_target="tpu_custom_call" | custom-call | flops 1342177280 | tf_op jit(solution)/shard_map/pallas_call | solution.py:385
  44.7 1.9 %collective-permute-done.10.refs_2_ = bf16[32,704]{1,0:T(8,128)(2,1)S(1)} collective-permute-done((bf16[32,704]{1,0:T(8,128)(2,1)S(1)}, bf16[32,704]{1,0:T(8,128)(2,1)S(1)}, u32[]{:S(2)}, u32[]{:S(2)}) %collective-permute-start.10) | collective-permute-done | bytes 45088 | tf_op jit(solution)/shard_map/ppermute | solution.py:424
  46.7 0.0 collective-permute-start.11
  46.7 1.2 %collective-permute-done.11.refs_3_ = bf16[32,704]{1,0:T(8,128)(2,1)S(1)} collective-permute-done((bf16[32,704]{1,0:T(8,128)(2,1)S(1)}, bf16[32,704]{1,0:T(8,128)(2,1)S(1)}, u32[]{:S(2)}, u32[]{:S(2)}) %collective-permute-start.11) | collective-permute-done | bytes 45088 | tf_op jit(solution)/shard_map/ppermute | solution.py:427
  47.9 2.1 %shard_map.80 = (f32[32,2048]{1,0:T(8,128)S(1)}, f32[32,32]{1,0:T(8,128)S(1)}, f32[32,672]{1,0:T(8,128)S(1)}) custom-call(bf16[32,704]{1,0:T(8,128)(2,1)S(1)} %get-tuple-element.42.refs_0_, bf16[32,704]{1,0:T(8,128)(2,1)S(1)} %collective-permute-done.9.refs_1_, bf16[32,704]{1,0:T(8,128)(2,1)S(1)} %collective-permute-done.10.refs_2_, ...), custom_call_target="tpu_custom_call" | custom-call | tf_op jit(solution)/shard_map/pallas_call | solution.py:385
  50.1 0.2 collective-permute-start.12
  50.3 1.6 %shard_map.81 = (f32[32,640]{1,0:T(8,128)S(1)}, f32[32,640]{1,0:T(8,128)S(1)}) custom-call(f32[32,2048]{1,0:T(8,128)S(1)} %get-tuple-element.52.h_ref.refs_0_, bf16[40,16,2,32,128]{4,3,2,1,0:T(8,128)(2,1)S(1)} %shard_map.72.refs_3_.s_ref.refs_2_.refs_6_), custom_call_target="tpu_custom_call" | custom-call | flops 1342177280 | tf_op jit(solution)/shard_map/pallas_call | solution.py:385
  51.9 0.4 collective-permute-start.13
  52.3 0.0 collective-permute-done.12.refs_2_
  52.3 0.1 shard_map.82
  52.4 0.6 collective-permute-start.14
  53.0 0.8 %shard_map.83.own_ref = f32[32,640]{1,0:T(8,128)S(1)} custom-call(f32[32,2048]{1,0:T(8,128)S(1)} %get-tuple-element.52.h_ref.refs_0_, bf16[40,16,2,32,128]{4,3,2,1,0:T(8,128)(2,1)S(1)} %shard_map.72.refs_3_.s_ref.refs_2_.refs_6_, bf16[32,704]{1,0:T(8,128)(2,1)S(1)} %get-tuple-element.49.refs_0_), custom_call_target="tpu_custom_call" | custom-call | flops 1 | tf_op jit(solution)/shard_map/pallas_call | solution.py:385
  53.8 0.0 collective-permute-done.13.refs_0_
  53.8 2.7 %collective-permute-done.14.refs_1_ = bf16[32,704]{1,0:T(8,128)(2,1)S(1)} collective-permute-done((bf16[32,704]{1,0:T(8,128)(2,1)S(1)}, bf16[32,704]{1,0:T(8,128)(2,1)S(1)}, u32[]{:S(2)}, u32[]{:S(2)}) %collective-permute-start.14) | collective-permute-done | bytes 45088 | tf_op jit(solution)/shard_map/ppermute | solution.py:424
  56.5 0.2 shard_map.84.refs_0_
  56.6 0.6 collective-permute-start.15
  57.2 0.0 collective-permute-start.16
  57.2 1.6 %collective-permute-start.17 = (bf16[32,704]{1,0:T(8,128)(2,1)S(1)}, bf16[32,704]{1,0:T(8,128)(2,1)S(1)}, u32[]{:S(2)}, u32[]{:S(2)}) collective-permute-start(bf16[32,704]{1,0:T(8,128)(2,1)S(1)} %shard_map.84.refs_0_), channel_id=1, source_target_pairs={{8,0},{12,4},{0,8},{4,12},{9,1},{13,5},{1,9},{5,13},{10,2},{14,6},... | collective-permute-start | bytes 135176 | tf_op jit(solution)/shard_map/ppermute | solution.py:430
  58.8 2.8 %collective-permute-start.18 = (bf16[32,704]{1,0:T(8,128)(2,1)S(1)}, bf16[32,704]{1,0:T(8,128)(2,1)S(1)}, u32[]{:S(2)}, u32[]{:S(2)}) collective-permute-start(bf16[32,704]{1,0:T(8,128)(2,1)S(1)} %shard_map.84.refs_0_), channel_id=1, source_target_pairs={{12,0},{8,4},{4,8},{0,12},{13,1},{9,5},{5,9},{1,13},{14,2},{10,6},... | collective-permute-start | bytes 135176 | tf_op jit(solution)/shard_map/ppermute | solution.py:430
  61.6 0.0 collective-permute-done.16.refs_1_
  61.6 1.0 %collective-permute-done.17.refs_2_ = bf16[32,704]{1,0:T(8,128)(2,1)S(1)} collective-permute-done((bf16[32,704]{1,0:T(8,128)(2,1)S(1)}, bf16[32,704]{1,0:T(8,128)(2,1)S(1)}, u32[]{:S(2)}, u32[]{:S(2)}) %collective-permute-start.17) | collective-permute-done | bytes 45088 | tf_op jit(solution)/shard_map/ppermute | solution.py:430
  62.6 2.1 %collective-permute-done.18.refs_3_ = bf16[32,704]{1,0:T(8,128)(2,1)S(1)} collective-permute-done((bf16[32,704]{1,0:T(8,128)(2,1)S(1)}, bf16[32,704]{1,0:T(8,128)(2,1)S(1)}, u32[]{:S(2)}, u32[]{:S(2)}) %collective-permute-start.18) | collective-permute-done | bytes 45088 | tf_op jit(solution)/shard_map/ppermute | solution.py:430
  64.7 0.9 %shard_map.85.refs_2_ = f32[32,1280]{1,0:T(8,128)S(1)} custom-call(f32[32,640]{1,0:T(8,128)S(1)} %get-tuple-element.53.w_ref, bf16[1280,1280]{1,0:T(8,128)(2,1)S(1)} %get-tuple-element.54.order_ref, bf16[32,704]{1,0:T(8,128)(2,1)S(1)} %shard_map.84.refs_0_, bf16[32,704]{1,0:T(8,128)(2,1)S(1)} %collective-permute-done.16.refs_1_, ...), custom_call_target="tpu_custom_call" | custom-call | tf_op jit(solution)/shard_map/pallas_call | solution.py:385
  65.6 0.1 collective-permute-start.19
  65.7 1.4 %collective-permute-done.19.refs_3_ = f32[32,1280]{1,0:T(8,128)S(1)} collective-permute-done((f32[32,1280]{1,0:T(8,128)S(1)}, f32[32,1280]{1,0:T(8,128)S(1)}, u32[]{:S(2)}, u32[]{:S(2)}) %collective-permute-start.19) | collective-permute-done | bytes 163872 | tf_op jit(solution)/shard_map/ppermute | solution.py:427
  67.1 0.0 collective-permute-done.15.refs_1_
  67.1 0.9 %shard_map.86 = (f32[32,1280]{1,0:T(8,128)}, f32[32,4096]{1,0:T(8,128)}) custom-call(f32[32,2048]{1,0:T(8,128)S(1)} %get-tuple-element.52.h_ref.refs_0_, f32[32,2048]{1,0:T(8,128)S(1)} %collective-permute-done.15.refs_1_, f32[32,1280]{1,0:T(8,128)S(1)} %shard_map.85.refs_2_, f32[32,1280]{1,0:T(8,128)S(1)} %collective-permute-done.19.refs_3_), custom_call_target="tpu_custom_call" | custom-call | tf_op jit(solution)/shard_map/pallas_call | solution.py:385
  (1 shorter events, 0.0 us)
Async XLA Ops:
  1.7 6.7 %collective-permute-start.1 = (bf16[32,2176]{1,0:T(8,128)(2,1)S(1)}, bf16[32,2176]{1,0:T(8,128)(2,1)S(1)}, u32[]{:S(2)}, u32[]{:S(2)}) collective-permute-start(bf16[32,2176]{1,0:T(8,128)(2,1)S(1)} %get-tuple-element.34), channel_id=1, source_target_pairs={{0,2},{2,0},{1,3},{3,1},{4,6},{6,4},{5,7},{7,5},{8,10},{10,8},{9,1... | collective-permute-start | bytes 417800 | tf_op jit(solution)/shard_map/ppermute | solution.py:424
  8.1 10.9 %collective-permute-start = (bf16[32,1344]{1,0:T(8,128)(2,1)S(1)}, bf16[32,1344]{1,0:T(8,128)(2,1)S(1)}, u32[]{:S(2)}, u32[]{:S(2)}) collective-permute-start(bf16[32,1344]{1,0:T(8,128)(2,1)S(1)} %get-tuple-element.32.refs_0_), channel_id=1, source_target_pairs={{0,2},{2,0},{1,3},{3,1},{4,6},{6,4},{5,7},{7,5},{8,10},{10,8},{9,1... | collective-permute-start | bytes 258056 | tf_op jit(solution)/shard_map/ppermute | solution.py:424
  8.3 3.2 %collective-permute-start.2 = (bf16[64,128]{1,0:T(8,128)(2,1)S(1)}, bf16[64,128]{1,0:T(8,128)(2,1)S(1)}, u32[]{:S(2)}, u32[]{:S(2)}) collective-permute-start(bf16[64,128]{1,0:T(8,128)(2,1)S(1)} %shard_map.70.refs_0_), channel_id=1, source_target_pairs={{2,1},{3,4},{6,5},{7,8},{10,9},{11,12},{14,13},{1,2},{4,3},{5,6},{... | collective-permute-start | bytes 49160 | tf_op jit(solution)/shard_map/ppermute | solution.py:445
  22.1 5.0 %collective-permute-start.3 = (f32[32,672]{1,0:T(8,128)S(1)}, f32[32,672]{1,0:T(8,128)S(1)}, u32[]{:S(2)}, u32[]{:S(2)}) collective-permute-start(f32[32,672]{1,0:T(8,128)S(1)} %get-tuple-element.38), channel_id=1, source_target_pairs={{0,1},{1,0},{2,3},{3,2},{4,5},{5,4},{6,7},{7,6},{8,9},{9,8},{10,11... | collective-permute-start | bytes 258056 | tf_op jit(solution)/shard_map/ppermute | solution.py:427
  27.0 2.6 %collective-permute-start.4 = (f32[32,640]{1,0:T(8,128)S(1)}, f32[32,640]{1,0:T(8,128)S(1)}, u32[]{:S(2)}, u32[]{:S(2)}) collective-permute-start(f32[32,640]{1,0:T(8,128)S(1)} %get-tuple-element.41), channel_id=1, source_target_pairs={{0,1},{1,0},{2,3},{3,2},{4,5},{5,4},{6,7},{7,6},{8,9},{9,8},{10,11... | collective-permute-start | bytes 245768 | tf_op jit(solution)/shard_map/ppermute | solution.py:427
  27.2 4.1 %collective-permute-start.5 = (bf16[32,704]{1,0:T(8,128)(2,1)S(1)}, bf16[32,704]{1,0:T(8,128)(2,1)S(1)}, u32[]{:S(2)}, u32[]{:S(2)}) collective-permute-start(bf16[32,704]{1,0:T(8,128)(2,1)S(1)} %get-tuple-element.39.refs_0_), channel_id=1, source_target_pairs={{0,2},{2,0},{1,3},{3,1},{4,6},{6,4},{5,7},{7,5},{8,10},{10,8},{9,1... | collective-permute-start | bytes 135176 | tf_op jit(solution)/shard_map/ppermute | solution.py:424
  31.5 4.5 %collective-permute-start.6 = (bf16[32,704]{1,0:T(8,128)(2,1)S(1)}, bf16[32,704]{1,0:T(8,128)(2,1)S(1)}, u32[]{:S(2)}, u32[]{:S(2)}) collective-permute-start(bf16[32,704]{1,0:T(8,128)(2,1)S(1)} %shard_map.77.refs_0_), channel_id=1, source_target_pairs={{4,0},{0,4},{12,8},{8,12},{5,1},{1,5},{13,9},{9,13},{6,2},{2,6},{1... | collective-permute-start | bytes 135176 | tf_op jit(solution)/shard_map/ppermute | solution.py:430
  33.4 6.0 %collective-permute-start.7 = (bf16[32,704]{1,0:T(8,128)(2,1)S(1)}, bf16[32,704]{1,0:T(8,128)(2,1)S(1)}, u32[]{:S(2)}, u32[]{:S(2)}) collective-permute-start(bf16[32,704]{1,0:T(8,128)(2,1)S(1)} %shard_map.77.refs_0_), channel_id=1, source_target_pairs={{8,0},{12,4},{0,8},{4,12},{9,1},{13,5},{1,9},{5,13},{10,2},{14,6},... | collective-permute-start | bytes 135176 | tf_op jit(solution)/shard_map/ppermute | solution.py:430
  36.0 5.9 %collective-permute-start.8 = (bf16[32,704]{1,0:T(8,128)(2,1)S(1)}, bf16[32,704]{1,0:T(8,128)(2,1)S(1)}, u32[]{:S(2)}, u32[]{:S(2)}) collective-permute-start(bf16[32,704]{1,0:T(8,128)(2,1)S(1)} %shard_map.77.refs_0_), channel_id=1, source_target_pairs={{12,0},{8,4},{4,8},{0,12},{13,1},{9,5},{5,9},{1,13},{14,2},{10,6},... | collective-permute-start | bytes 135176 | tf_op jit(solution)/shard_map/ppermute | solution.py:430
  42.5 1.2 %collective-permute-start.9 = (bf16[32,704]{1,0:T(8,128)(2,1)S(1)}, bf16[32,704]{1,0:T(8,128)(2,1)S(1)}, u32[]{:S(2)}, u32[]{:S(2)}) collective-permute-start(bf16[32,704]{1,0:T(8,128)(2,1)S(1)} %get-tuple-element.42.refs_0_), channel_id=1, source_target_pairs={{0,1},{1,0},{2,3},{3,2},{4,5},{5,4},{6,7},{7,6},{8,9},{9,8},{10,11... | collective-permute-start | bytes 135176 | tf_op jit(solution)/shard_map/ppermute | solution.py:427
  42.5 4.2 %collective-permute-start.10 = (bf16[32,704]{1,0:T(8,128)(2,1)S(1)}, bf16[32,704]{1,0:T(8,128)(2,1)S(1)}, u32[]{:S(2)}, u32[]{:S(2)}) collective-permute-start(bf16[32,704]{1,0:T(8,128)(2,1)S(1)} %get-tuple-element.42.refs_0_), channel_id=1, source_target_pairs={{0,2},{2,0},{1,3},{3,1},{4,6},{6,4},{5,7},{7,5},{8,10},{10,8},{9,1... | collective-permute-start | bytes 135176 | tf_op jit(solution)/shard_map/ppermute | solution.py:424
  46.7 1.2 %collective-permute-start.11 = (bf16[32,704]{1,0:T(8,128)(2,1)S(1)}, bf16[32,704]{1,0:T(8,128)(2,1)S(1)}, u32[]{:S(2)}, u32[]{:S(2)}) collective-permute-start(bf16[32,704]{1,0:T(8,128)(2,1)S(1)} %collective-permute-done.10.refs_2_), channel_id=1, source_target_pairs={{0,1},{1,0},{2,3},{3,2},{4,5},{5,4},{6,7},{7,6},{8,9},{9,8},{10,11... | collective-permute-start | bytes 135176 | tf_op jit(solution)/shard_map/ppermute | solution.py:427
  50.1 2.3 %collective-permute-start.12 = (f32[32,672]{1,0:T(8,128)S(1)}, f32[32,672]{1,0:T(8,128)S(1)}, u32[]{:S(2)}, u32[]{:S(2)}) collective-permute-start(f32[32,672]{1,0:T(8,128)S(1)} %get-tuple-element.48), channel_id=1, source_target_pairs={{0,1},{1,0},{2,3},{3,2},{4,5},{5,4},{6,7},{7,6},{8,9},{9,8},{10,11... | collective-permute-start | bytes 258056 | tf_op jit(solution)/shard_map/ppermute | solution.py:427
  51.9 1.9 %collective-permute-start.13 = (f32[32,640]{1,0:T(8,128)S(1)}, f32[32,640]{1,0:T(8,128)S(1)}, u32[]{:S(2)}, u32[]{:S(2)}) collective-permute-start(f32[32,640]{1,0:T(8,128)S(1)} %get-tuple-element.51), channel_id=1, source_target_pairs={{0,1},{1,0},{2,3},{3,2},{4,5},{5,4},{6,7},{7,6},{8,9},{9,8},{10,11... | collective-permute-start | bytes 245768 | tf_op jit(solution)/shard_map/ppermute | solution.py:427
  52.4 4.1 %collective-permute-start.14 = (bf16[32,704]{1,0:T(8,128)(2,1)S(1)}, bf16[32,704]{1,0:T(8,128)(2,1)S(1)}, u32[]{:S(2)}, u32[]{:S(2)}) collective-permute-start(bf16[32,704]{1,0:T(8,128)(2,1)S(1)} %get-tuple-element.49.refs_0_), channel_id=1, source_target_pairs={{0,2},{2,0},{1,3},{3,1},{4,6},{6,4},{5,7},{7,5},{8,10},{10,8},{9,1... | collective-permute-start | bytes 135176 | tf_op jit(solution)/shard_map/ppermute | solution.py:424
  56.6 10.4 %collective-permute-start.15 = (f32[32,2048]{1,0:T(8,128)S(1)}, f32[32,2048]{1,0:T(8,128)S(1)}, u32[]{:S(2)}, u32[]{:S(2)}) collective-permute-start(f32[32,2048]{1,0:T(8,128)S(1)} %get-tuple-element.52.h_ref.refs_0_), channel_id=1, source_target_pairs={{0,2},{2,0},{1,3},{3,1},{4,6},{6,4},{5,7},{7,5},{8,10},{10,8},{9,1... | collective-permute-start | bytes 786440 | tf_op jit(solution)/shard_map/ppermute | solution.py:424
  57.2 4.4 %collective-permute-start.16 = (bf16[32,704]{1,0:T(8,128)(2,1)S(1)}, bf16[32,704]{1,0:T(8,128)(2,1)S(1)}, u32[]{:S(2)}, u32[]{:S(2)}) collective-permute-start(bf16[32,704]{1,0:T(8,128)(2,1)S(1)} %shard_map.84.refs_0_), channel_id=1, source_target_pairs={{4,0},{0,4},{12,8},{8,12},{5,1},{1,5},{13,9},{9,13},{6,2},{2,6},{1... | collective-permute-start | bytes 135176 | tf_op jit(solution)/shard_map/ppermute | solution.py:430
  57.2 5.4 %collective-permute-start.17 = (bf16[32,704]{1,0:T(8,128)(2,1)S(1)}, bf16[32,704]{1,0:T(8,128)(2,1)S(1)}, u32[]{:S(2)}, u32[]{:S(2)}) collective-permute-start(bf16[32,704]{1,0:T(8,128)(2,1)S(1)} %shard_map.84.refs_0_), channel_id=1, source_target_pairs={{8,0},{12,4},{0,8},{4,12},{9,1},{13,5},{1,9},{5,13},{10,2},{14,6},... | collective-permute-start | bytes 135176 | tf_op jit(solution)/shard_map/ppermute | solution.py:430
  58.8 5.9 %collective-permute-start.18 = (bf16[32,704]{1,0:T(8,128)(2,1)S(1)}, bf16[32,704]{1,0:T(8,128)(2,1)S(1)}, u32[]{:S(2)}, u32[]{:S(2)}) collective-permute-start(bf16[32,704]{1,0:T(8,128)(2,1)S(1)} %shard_map.84.refs_0_), channel_id=1, source_target_pairs={{12,0},{8,4},{4,8},{0,12},{13,1},{9,5},{5,9},{1,13},{14,2},{10,6},... | collective-permute-start | bytes 135176 | tf_op jit(solution)/shard_map/ppermute | solution.py:430
  65.6 1.5 %collective-permute-start.19 = (f32[32,1280]{1,0:T(8,128)S(1)}, f32[32,1280]{1,0:T(8,128)S(1)}, u32[]{:S(2)}, u32[]{:S(2)}) collective-permute-start(f32[32,1280]{1,0:T(8,128)S(1)} %shard_map.85.refs_2_), channel_id=1, source_target_pairs={{0,1},{1,0},{2,3},{3,2},{4,5},{5,4},{6,7},{7,6},{8,9},{9,8},{10,11... | collective-permute-start | bytes 491528 | tf_op jit(solution)/shard_map/ppermute | solution.py:427

commit v6 on v5

--- a/solution.py
+++ b/solution.py
@@ -61,15 +61,16 @@
     out_ref[:, size + rank : size + 2 * rank] = rest
 
 
-def fetch_kernel(w_hbm, h_hbm, order_hbm, *refs):
-    piece_ref, msg_ref, gram_ref, old_ref, order_ref, w_scr, sems = refs[-7:]
+def fetch_kernel(w_hbm, h_hbm, order_hbm, tab_hbm, *refs):
+    piece_ref, whole_ref, gram_ref, old_ref, order_ref, tab_ref, w_scr, sems = refs[-8:]
     frames = old_ref.shape[1]
     size = piece_ref.shape[1]
     mine = pl.ds(pl.multiple_of(lax.axis_index("row") * frames, TAPS), frames)
     copies = [
         pltpu.make_async_copy(w_hbm, w_scr, sems.at[0]),
         pltpu.make_async_copy(order_hbm, order_ref, sems.at[1]),
-        pltpu.make_async_copy(h_hbm.at[:, mine], old_ref, sems.at[2]),
+        pltpu.make_async_copy(tab_hbm, tab_ref, sems.at[2]),
+        pltpu.make_async_copy(h_hbm.at[:, mine], old_ref, sems.at[3]),
     ]
     for copy in copies:
         copy.start()
@@ -88,15 +89,13 @@
         def _():
             piece_ref[...] = whole[:, c * size : (c + 1) * size]
 
-    pack(msg_ref, whole, gram)
+    whole_ref[...] = whole
     copies[2].wait()
-
-
-def table_kernel(tab_hbm, *refs):
-    tab_ref, sem = refs[-2:]
-    copy = pltpu.make_async_copy(tab_hbm, tab_ref, sem)
-    copy.start()
-    copy.wait()
+    copies[3].wait()
+
+
+def pack_kernel(w_ref, gram_ref, *refs):
+    pack(refs[-1], w_ref[...], gram_ref[...])
 
 
 def three_terms(value):
@@ -449,30 +448,29 @@
     update_outs = [((rank, frames), F32), ((rank, rank), F32)]
     update_outs += [((rank, size + rank), F32)] * ((rows - 1) * (subs - 1))
     table, order = jnp.asarray(toeplitz()), jnp.asarray(reorder(cl))
-    w_piece, w_msg, w_gram, old, order = call(
+    w_piece, w_whole, w_gram, old, order, table = call(
         fetch_kernel,
-        [hbm(w_start.T), hbm(h_start), hbm(order), own_sig],
+        [hbm(w_start.T), hbm(h_start), hbm(order), hbm(table), own_sig],
         [
             piece,
-            ((rank, NF * cl + 2 * rank), BF16),
+            ((rank, NF * cl), F32),
             ((rank, rank), F32),
             pltpu.VMEM((rank, frames), F32),
             pltpu.VMEM(order.shape, BF16),
+            pltpu.VMEM(table.shape, BF16),
         ],
-        [pltpu.VMEM((rank, NF * cl), F32), pltpu.SemaphoreType.DMA((3,))],
-        in_specs=[anywhere] * 4,
+        [pltpu.VMEM((rank, NF * cl), F32), pltpu.SemaphoreType.DMA((4,))],
+        in_specs=[anywhere] * 5,
         cost=2 * 10**9,
+    )
+    (w_msg,) = call(
+        pack_kernel,
+        [w_whole, w_gram, edge],
+        [((rank, NF * cl + 2 * rank), BF16)],
+        in_specs=[whole, whole, anywhere],
     )
     w_msgs = [w_msg] + [row_shift(w_msg, shift) for shift in range(1, rows)]
     order = vmem(order)
-    (table,) = call(
-        table_kernel,
-        [hbm(table), edge],
-        [pltpu.VMEM(table.shape, BF16)],
-        [pltpu.SemaphoreType.DMA],
-        in_specs=[anywhere] * 2,
-        cost=2 * 10**9,
-    )
     (spectra,) = call(
         functools.partial(spectra_kernel, rows, cl, blocks),
         sig + [halo, vmem(table)],

time: 68.1 us -> 68.5 us (level)
  Pallas kernels: 28.4 us -> 26.1 us
  waiting for transfers between devices: 18.7 us -> 20.4 us
  starting transfers between devices: 20.1 us -> 21.1 us
    ppermute x6, waiting for transfers between devices: 6.49 us -> 10.8 us  [row_shift(): lax.ppermute(value, 'row', [(i, (i + shift) % rows) for i in range(rows)])]
    ppermute x6, starting transfers between devices: 6.43 us -> 9.41 us  [row_shift(): lax.ppermute(value, 'row', [(i, (i + shift) % rows) for i in range(rows)])]
    pallas_call x19, Pallas kernels: 28.4 us -> 26.1 us  [call(): pl.pallas_call(kernel, out_shape=[jax.ShapeDtypeStruct(*out) if isinstanc...]
    ppermute x6, waiting for transfers between devices: 8.98 us -> 6.82 us  [frm_shift(): lax.ppermute(value, 'frm', [(partner(i, shift, frms), i) for i in range(f...]
    ppermute x7, starting transfers between devices: 4.12 us -> 2.23 us  [sub_shift(): lax.ppermute(value, 'sub', [(i, (i + shift) % subs) for i in range(subs)])]
  transfers between devices with their start and end apart: 20 -> 20, of which waited for: 11 -> 11; matrix products, arithmetic and copies ran while one was open for 0% -> 0% of each run, Pallas kernels for 30% -> 27%
where the time goes in v6:
time: 68.5 us; the launch traced here: 68.4 us
  Pallas kernels  26.1 us (38%)
  starting transfers between devices  21.1 us (31%)
  waiting for transfers between devices  20.4 us (30%)
  between operations  0.77 us (1%)
    pallas_call x19, Pallas kernels, call(): pl.pallas_call(kernel, out_shape=[jax.ShapeDtypeStruct(*out) if isinstanc...  26.1 us
    ppermute x6, waiting for transfers between devices, row_shift(): lax.ppermute(value, 'row', [(i, (i + shift) % rows) for i in range(rows)])  10.8 us
    ppermute x6, starting transfers between devices, row_shift(): lax.ppermute(value, 'row', [(i, (i + shift) % rows) for i in range(rows)])  9.41 us
    ppermute x6, starting transfers between devices, frm_shift(): lax.ppermute(value, 'frm', [(partner(i, shift, frms), i) for i in range(f...  8.78 us
    ppermute x6, waiting for transfers between devices, frm_shift(): lax.ppermute(value, 'frm', [(partner(i, shift, frms), i) for i in range(f...  6.82 us
    ppermute x7, waiting for transfers between devices, sub_shift(): lax.ppermute(value, 'sub', [(i, (i + shift) % subs) for i in range(subs)])  2.82 us
    ppermute x7, starting transfers between devices, sub_shift(): lax.ppermute(value, 'sub', [(i, (i + shift) % subs) for i in range(subs)])  2.23 us
  transfers between devices with their start and end apart: 20, of which 11 were waited for; matrix products, arithmetic and copies ran while one was open for 0% of the time, Pallas kernels for 27%

profile of v6, /device:TPU:0, one launch (start us, length us, event | category | flops | bytes accessed | tf_op | source)
XLA Modules:
  0.0 68.4 jit_solution(2086572763621733235)
XLA Ops:
  0.6 1.0 %shard_map.68 = (bf16[32,2176]{1,0:T(8,128)(2,1)S(1)}, bf16[32,2176]{1,0:T(8,128)(2,1)S(1)}) custom-call(bf16[32,4096]{1,0:T(8,128)(2,1)} %sig_hbm.1), custom_call_target="tpu_custom_call" | custom-call | tf_op jit(solution)/shard_map/pallas_call | solution.py:384
  1.7 3.0 %collective-permute-start = (bf16[32,2176]{1,0:T(8,128)(2,1)S(1)}, bf16[32,2176]{1,0:T(8,128)(2,1)S(1)}, u32[]{:S(2)}, u32[]{:S(2)}) collective-permute-start(bf16[32,2176]{1,0:T(8,128)(2,1)S(1)} %get-tuple-element.36), channel_id=1, source_target_pairs={{0,2},{2,0},{1,3},{3,1},{4,6},{6,4},{5,7},{7,5},{8,10},{10,8},{9,1... | collective-permute-start | bytes 417800 | tf_op jit(solution)/shard_map/ppermute | solution.py:423
  4.7 3.7 %collective-permute-done.refs_0_.refs_1_ = bf16[32,2176]{1,0:T(8,128)(2,1)S(1)} collective-permute-done((bf16[32,2176]{1,0:T(8,128)(2,1)S(1)}, bf16[32,2176]{1,0:T(8,128)(2,1)S(1)}, u32[]{:S(2)}, u32[]{:S(2)}) %collective-permute-start) | collective-permute-done | bytes 139296 | tf_op jit(solution)/shard_map/ppermute | solution.py:423
  8.3 0.7 collective-permute-start.2
  9.0 3.6 %shard_map.69 = (f32[32,640]{1,0:T(8,128)S(1)}, f32[32,1280]{1,0:T(8,128)S(1)}, f32[32,32]{1,0:T(8,128)S(1)}, f32[32,2048]{1,0:T(8,128)S(1)}, bf16[1280,1280]{1,...) custom-call(f32[32,1280]{1,0:T(8,128)} %bitcast.2, f32[32,4096]{1,0:T(8,128)} %h_hbm.1, ...), custom_call_target="tpu_custom_call" | custom-call | flops 2000000000 | tf_op jit(solution)/shard_map/pallas_call | solution.py:384
  12.6 0.1 shard_map.71.refs_0_
  12.7 3.0 %collective-permute-start.1 = (bf16[32,1344]{1,0:T(8,128)(2,1)S(1)}, bf16[32,1344]{1,0:T(8,128)(2,1)S(1)}, u32[]{:S(2)}, u32[]{:S(2)}) collective-permute-start(bf16[32,1344]{1,0:T(8,128)(2,1)S(1)} %shard_map.71.refs_0_), channel_id=1, source_target_pairs={{0,2},{2,0},{1,3},{3,1},{4,6},{6,4},{5,7},{7,5},{8,10},{10,8},{9,1... | collective-permute-start | bytes 258056 | tf_op jit(solution)/shard_map/ppermute | solution.py:423
  15.7 0.0 collective-permute-done.2.refs_2_
  15.7 7.5 %shard_map.72.refs_3_.s_ref.refs_2_.refs_6_ = bf16[40,16,2,32,128]{4,3,2,1,0:T(8,128)(2,1)S(1)} custom-call(bf16[32,2176]{1,0:T(8,128)(2,1)S(1)} %get-tuple-element.32.refs_0_.sig_ref, bf16[32,2176]{1,0:T(8,128)(2,1)S(1)} %collective-permute-done.refs_0_.refs_1_, bf16[64,128]{1,0:T(8,128)(2,1)S(1)} %collective-permute-done.2.refs_2_, ...), custom_call_target="tpu_custom_call" | custom-call | flops 5368709120 | tf_op jit(solution)/shard_map/pallas_call | solution.py:384
  23.2 0.0 collective-permute-done.1.refs_1_
  23.2 3.0 %shard_map.73 = (f32[32,2048]{1,0:T(8,128)S(1)}, f32[32,32]{1,0:T(8,128)S(1)}, f32[32,672]{1,0:T(8,128)S(1)}) custom-call(bf16[32,1344]{1,0:T(8,128)(2,1)S(1)} %shard_map.71.refs_0_, bf16[32,1344]{1,0:T(8,128)(2,1)S(1)} %collective-permute-done.1.refs_1_, f32[32,2048]{1,0:T(8,128)S(1)} %get-tuple-element.37.refs_2_, ...), custom_call_target="tpu_custom_call" | custom-call | tf_op jit(solution)/shard_map/pallas_call | solution.py:384
  26.3 1.4 %collective-permute-start.3 = (f32[32,672]{1,0:T(8,128)S(1)}, f32[32,672]{1,0:T(8,128)S(1)}, u32[]{:S(2)}, u32[]{:S(2)}) collective-permute-start(f32[32,672]{1,0:T(8,128)S(1)} %get-tuple-element.42), channel_id=1, source_target_pairs={{0,1},{1,0},{2,3},{3,2},{4,5},{5,4},{6,7},{7,6},{8,9},{9,8},{10,11... | collective-permute-start | bytes 258056 | tf_op jit(solution)/shard_map/ppermute | solution.py:426
  27.7 1.6 %shard_map.74 = (f32[32,640]{1,0:T(8,128)S(1)}, f32[32,640]{1,0:T(8,128)S(1)}) custom-call(f32[32,2048]{1,0:T(8,128)S(1)} %get-tuple-element.39.h_ref.refs_5_, bf16[40,16,2,32,128]{4,3,2,1,0:T(8,128)(2,1)S(1)} %shard_map.72.refs_3_.s_ref.refs_2_.refs_6_), custom_call_target="tpu_custom_call" | custom-call | flops 1342177280 | tf_op jit(solution)/shard_map/pallas_call | solution.py:384
  29.3 0.1 collective-permute-start.4
  29.4 0.0 collective-permute-done.3.refs_2_
  29.4 0.1 shard_map.75
  29.5 0.5 collective-permute-start.5
  30.0 0.8 %shard_map.76.own_ref = f32[32,640]{1,0:T(8,128)S(1)} custom-call(f32[32,2048]{1,0:T(8,128)S(1)} %get-tuple-element.39.h_ref.refs_5_, bf16[40,16,2,32,128]{4,3,2,1,0:T(8,128)(2,1)S(1)} %shard_map.72.refs_3_.s_ref.refs_2_.refs_6_, bf16[32,704]{1,0:T(8,128)(2,1)S(1)} %get-tuple-element.43.refs_0_), custom_call_target="tpu_custom_call" | custom-call | flops 1 | tf_op jit(solution)/shard_map/pallas_call | solution.py:384
  30.8 0.0 collective-permute-done.4.refs_0_
  30.8 2.8 %collective-permute-done.5.refs_1_ = bf16[32,704]{1,0:T(8,128)(2,1)S(1)} collective-permute-done((bf16[32,704]{1,0:T(8,128)(2,1)S(1)}, bf16[32,704]{1,0:T(8,128)(2,1)S(1)}, u32[]{:S(2)}, u32[]{:S(2)}) %collective-permute-start.5) | collective-permute-done | bytes 45088 | tf_op jit(solution)/shard_map/ppermute | solution.py:423
  33.6 0.2 shard_map.77.refs_0_
  33.8 2.7 %collective-permute-start.8 = (bf16[32,704]{1,0:T(8,128)(2,1)S(1)}, bf16[32,704]{1,0:T(8,128)(2,1)S(1)}, u32[]{:S(2)}, u32[]{:S(2)}) collective-permute-start(bf16[32,704]{1,0:T(8,128)(2,1)S(1)} %shard_map.77.refs_0_), channel_id=1, source_target_pairs={{12,0},{8,4},{4,8},{0,12},{13,1},{9,5},{5,9},{1,13},{14,2},{10,6},... | collective-permute-start | bytes 135176 | tf_op jit(solution)/shard_map/ppermute | solution.py:429
  36.5 0.4 collective-permute-start.7
  36.8 1.3 %collective-permute-start.6 = (bf16[32,704]{1,0:T(8,128)(2,1)S(1)}, bf16[32,704]{1,0:T(8,128)(2,1)S(1)}, u32[]{:S(2)}, u32[]{:S(2)}) collective-permute-start(bf16[32,704]{1,0:T(8,128)(2,1)S(1)} %shard_map.77.refs_0_), channel_id=1, source_target_pairs={{4,0},{0,4},{12,8},{8,12},{5,1},{1,5},{13,9},{9,13},{6,2},{2,6},{1... | collective-permute-start | bytes 135176 | tf_op jit(solution)/shard_map/ppermute | solution.py:429
  38.2 2.0 %collective-permute-done.8.refs_3_ = bf16[32,704]{1,0:T(8,128)(2,1)S(1)} collective-permute-done((bf16[32,704]{1,0:T(8,128)(2,1)S(1)}, bf16[32,704]{1,0:T(8,128)(2,1)S(1)}, u32[]{:S(2)}, u32[]{:S(2)}) %collective-permute-start.8) | collective-permute-done | bytes 45088 | tf_op jit(solution)/shard_map/ppermute | solution.py:429
  40.2 1.7 %collective-permute-done.7.refs_2_ = bf16[32,704]{1,0:T(8,128)(2,1)S(1)} collective-permute-done((bf16[32,704]{1,0:T(8,128)(2,1)S(1)}, bf16[32,704]{1,0:T(8,128)(2,1)S(1)}, u32[]{:S(2)}, u32[]{:S(2)}) %collective-permute-start.7) | collective-permute-done | bytes 45088 | tf_op jit(solution)/shard_map/ppermute | solution.py:429
  41.9 0.0 collective-permute-done.6.refs_1_
  41.9 0.6 shard_map.78
  42.5 0.0 collective-permute-start.9
  42.5 1.0 %collective-permute-start.10 = (bf16[32,704]{1,0:T(8,128)(2,1)S(1)}, bf16[32,704]{1,0:T(8,128)(2,1)S(1)}, u32[]{:S(2)}, u32[]{:S(2)}) collective-permute-start(bf16[32,704]{1,0:T(8,128)(2,1)S(1)} %get-tuple-element.46.refs_0_), channel_id=1, source_target_pairs={{0,2},{2,0},{1,3},{3,1},{4,6},{6,4},{5,7},{7,5},{8,10},{10,8},{9,1... | collective-permute-start | bytes 135176 | tf_op jit(solution)/shard_map/ppermute | solution.py:423
  43.5 0.2 collective-permute-done.9.refs_1_
  43.7 1.0 %shard_map.79.refs_4_ = f32[32,2048]{1,0:T(8,128)S(1)} custom-call(bf16[32,704]{1,0:T(8,128)(2,1)S(1)} %get-tuple-element.46.refs_0_, bf16[32,704]{1,0:T(8,128)(2,1)S(1)} %collective-permute-done.9.refs_1_, bf16[40,16,2,32,128]{4,3,2,1,0:T(8,128)(2,1)S(1)} %shard_map.72.refs_3_.s_ref.refs_2_.refs_6_), custom_call_target="tpu_custom_call" | custom-call | flops 1342177280 | tf_op jit(solution)/shard_map/pallas_call | solution.py:384
  44.7 1.9 %collective-permute-done.10.refs_2_ = bf16[32,704]{1,0:T(8,128)(2,1)S(1)} collective-permute-done((bf16[32,704]{1,0:T(8,128)(2,1)S(1)}, bf16[32,704]{1,0:T(8,128)(2,1)S(1)}, u32[]{:S(2)}, u32[]{:S(2)}) %collective-permute-start.10) | collective-permute-done | bytes 45088 | tf_op jit(solution)/shard_map/ppermute | solution.py:423
  46.7 0.0 collective-permute-start.11
  46.7 1.2 %collective-permute-done.11.refs_3_ = bf16[32,704]{1,0:T(8,128)(2,1)S(1)} collective-permute-done((bf16[32,704]{1,0:T(8,128)(2,1)S(1)}, bf16[32,704]{1,0:T(8,128)(2,1)S(1)}, u32[]{:S(2)}, u32[]{:S(2)}) %collective-permute-start.11) | collective-permute-done | bytes 45088 | tf_op jit(solution)/shard_map/ppermute | solution.py:426
  47.9 2.1 %shard_map.80 = (f32[32,2048]{1,0:T(8,128)S(1)}, f32[32,32]{1,0:T(8,128)S(1)}, f32[32,672]{1,0:T(8,128)S(1)}) custom-call(bf16[32,704]{1,0:T(8,128)(2,1)S(1)} %get-tuple-element.46.refs_0_, bf16[32,704]{1,0:T(8,128)(2,1)S(1)} %collective-permute-done.9.refs_1_, bf16[32,704]{1,0:T(8,128)(2,1)S(1)} %collective-permute-done.10.refs_2_, ...), custom_call_target="tpu_custom_call" | custom-call | tf_op jit(solution)/shard_map/pallas_call | solution.py:384
  50.1 0.2 collective-permute-start.12
  50.3 1.6 %shard_map.81 = (f32[32,640]{1,0:T(8,128)S(1)}, f32[32,640]{1,0:T(8,128)S(1)}) custom-call(f32[32,2048]{1,0:T(8,128)S(1)} %get-tuple-element.56.h_ref.refs_0_, bf16[40,16,2,32,128]{4,3,2,1,0:T(8,128)(2,1)S(1)} %shard_map.72.refs_3_.s_ref.refs_2_.refs_6_), custom_call_target="tpu_custom_call" | custom-call | flops 1342177280 | tf_op jit(solution)/shard_map/pallas_call | solution.py:384
  51.9 0.4 collective-permute-start.13
  52.3 0.0 collective-permute-done.12.refs_2_
  52.3 0.1 shard_map.82
  52.4 1.0 %collective-permute-start.14 = (bf16[32,704]{1,0:T(8,128)(2,1)S(1)}, bf16[32,704]{1,0:T(8,128)(2,1)S(1)}, u32[]{:S(2)}, u32[]{:S(2)}) collective-permute-start(bf16[32,704]{1,0:T(8,128)(2,1)S(1)} %get-tuple-element.53.refs_0_), channel_id=1, source_target_pairs={{0,2},{2,0},{1,3},{3,1},{4,6},{6,4},{5,7},{7,5},{8,10},{10,8},{9,1... | collective-permute-start | bytes 135176 | tf_op jit(solution)/shard_map/ppermute | solution.py:423
  53.4 0.8 %shard_map.83.own_ref = f32[32,640]{1,0:T(8,128)S(1)} custom-call(f32[32,2048]{1,0:T(8,128)S(1)} %get-tuple-element.56.h_ref.refs_0_, bf16[40,16,2,32,128]{4,3,2,1,0:T(8,128)(2,1)S(1)} %shard_map.72.refs_3_.s_ref.refs_2_.refs_6_, bf16[32,704]{1,0:T(8,128)(2,1)S(1)} %get-tuple-element.53.refs_0_), custom_call_target="tpu_custom_call" | custom-call | flops 1 | tf_op jit(solution)/shard_map/pallas_call | solution.py:384
  54.2 0.0 collective-permute-done.13.refs_0_
  54.2 2.3 %collective-permute-done.14.refs_1_ = bf16[32,704]{1,0:T(8,128)(2,1)S(1)} collective-permute-done((bf16[32,704]{1,0:T(8,128)(2,1)S(1)}, bf16[32,704]{1,0:T(8,128)(2,1)S(1)}, u32[]{:S(2)}, u32[]{:S(2)}) %collective-permute-start.14) | collective-permute-done | bytes 45088 | tf_op jit(solution)/shard_map/ppermute | solution.py:423
  56.5 0.2 shard_map.84.refs_0_
  56.7 0.9 %collective-permute-start.15 = (f32[32,2048]{1,0:T(8,128)S(1)}, f32[32,2048]{1,0:T(8,128)S(1)}, u32[]{:S(2)}, u32[]{:S(2)}) collective-permute-start(f32[32,2048]{1,0:T(8,128)S(1)} %get-tuple-element.56.h_ref.refs_0_), channel_id=1, source_target_pairs={{0,2},{2,0},{1,3},{3,1},{4,6},{6,4},{5,7},{7,5},{8,10},{10,8},{9,1... | collective-permute-start | bytes 786440 | tf_op jit(solution)/shard_map/ppermute | solution.py:423
  57.6 2.0 %collective-permute-start.18 = (bf16[32,704]{1,0:T(8,128)(2,1)S(1)}, bf16[32,704]{1,0:T(8,128)(2,1)S(1)}, u32[]{:S(2)}, u32[]{:S(2)}) collective-permute-start(bf16[32,704]{1,0:T(8,128)(2,1)S(1)} %shard_map.84.refs_0_), channel_id=1, source_target_pairs={{12,0},{8,4},{4,8},{0,12},{13,1},{9,5},{5,9},{1,13},{14,2},{10,6},... | collective-permute-start | bytes 135176 | tf_op jit(solution)/shard_map/ppermute | solution.py:429
  59.6 0.1 collective-permute-start.17
  59.6 2.4 %collective-permute-start.16 = (bf16[32,704]{1,0:T(8,128)(2,1)S(1)}, bf16[32,704]{1,0:T(8,128)(2,1)S(1)}, u32[]{:S(2)}, u32[]{:S(2)}) collective-permute-start(bf16[32,704]{1,0:T(8,128)(2,1)S(1)} %shard_map.84.refs_0_), channel_id=1, source_target_pairs={{4,0},{0,4},{12,8},{8,12},{5,1},{1,5},{13,9},{9,13},{6,2},{2,6},{1... | collective-permute-start | bytes 135176 | tf_op jit(solution)/shard_map/ppermute | solution.py:429
  62.0 1.8 %collective-permute-done.18.refs_3_ = bf16[32,704]{1,0:T(8,128)(2,1)S(1)} collective-permute-done((bf16[32,704]{1,0:T(8,128)(2,1)S(1)}, bf16[32,704]{1,0:T(8,128)(2,1)S(1)}, u32[]{:S(2)}, u32[]{:S(2)}) %collective-permute-start.18) | collective-permute-done | bytes 45088 | tf_op jit(solution)/shard_map/ppermute | solution.py:429
  63.8 1.3 %collective-permute-done.17.refs_2_ = bf16[32,704]{1,0:T(8,128)(2,1)S(1)} collective-permute-done((bf16[32,704]{1,0:T(8,128)(2,1)S(1)}, bf16[32,704]{1,0:T(8,128)(2,1)S(1)}, u32[]{:S(2)}, u32[]{:S(2)}) %collective-permute-start.17) | collective-permute-done | bytes 45088 | tf_op jit(solution)/shard_map/ppermute | solution.py:429
  65.1 0.0 collective-permute-done.16.refs_1_
  65.1 0.9 %shard_map.85.refs_2_ = f32[32,1280]{1,0:T(8,128)S(1)} custom-call(f32[32,640]{1,0:T(8,128)S(1)} %get-tuple-element.57.w_ref, bf16[1280,1280]{1,0:T(8,128)(2,1)S(1)} %get-tuple-element.58.order_ref, bf16[32,704]{1,0:T(8,128)(2,1)S(1)} %shard_map.84.refs_0_, bf16[32,704]{1,0:T(8,128)(2,1)S(1)} %collective-permute-done.16.refs_1_, ...), custom_call_target="tpu_custom_call" | custom-call | tf_op jit(solution)/shard_map/pallas_call | solution.py:384
  66.0 0.1 collective-permute-start.19
  66.1 1.4 %collective-permute-done.19.refs_3_ = f32[32,1280]{1,0:T(8,128)S(1)} collective-permute-done((f32[32,1280]{1,0:T(8,128)S(1)}, f32[32,1280]{1,0:T(8,128)S(1)}, u32[]{:S(2)}, u32[]{:S(2)}) %collective-permute-start.19) | collective-permute-done | bytes 163872 | tf_op jit(solution)/shard_map/ppermute | solution.py:426
  67.5 0.0 collective-permute-done.15.refs_1_
  67.5 0.9 %shard_map.86 = (f32[32,1280]{1,0:T(8,128)}, f32[32,4096]{1,0:T(8,128)}) custom-call(f32[32,2048]{1,0:T(8,128)S(1)} %get-tuple-element.56.h_ref.refs_0_, f32[32,2048]{1,0:T(8,128)S(1)} %collective-permute-done.15.refs_1_, f32[32,1280]{1,0:T(8,128)S(1)} %shard_map.85.refs_2_, f32[32,1280]{1,0:T(8,128)S(1)} %collective-permute-done.19.refs_3_), custom_call_target="tpu_custom_call" | custom-call | tf_op jit(solution)/shard_map/pallas_call | solution.py:384
  (1 shorter events, 0.0 us)
Async XLA Ops:
  1.7 6.7 %collective-permute-start = (bf16[32,2176]{1,0:T(8,128)(2,1)S(1)}, bf16[32,2176]{1,0:T(8,128)(2,1)S(1)}, u32[]{:S(2)}, u32[]{:S(2)}) collective-permute-start(bf16[32,2176]{1,0:T(8,128)(2,1)S(1)} %get-tuple-element.36), channel_id=1, source_target_pairs={{0,2},{2,0},{1,3},{3,1},{4,6},{6,4},{5,7},{7,5},{8,10},{10,8},{9,1... | collective-permute-start | bytes 417800 | tf_op jit(solution)/shard_map/ppermute | solution.py:423
  8.3 7.4 %collective-permute-start.2 = (bf16[64,128]{1,0:T(8,128)(2,1)S(1)}, bf16[64,128]{1,0:T(8,128)(2,1)S(1)}, u32[]{:S(2)}, u32[]{:S(2)}) collective-permute-start(bf16[64,128]{1,0:T(8,128)(2,1)S(1)} %shard_map.70.refs_0_), channel_id=1, source_target_pairs={{2,1},{3,4},{6,5},{7,8},{10,9},{11,12},{14,13},{1,2},{4,3},{5,6},{... | collective-permute-start | bytes 49160 | tf_op jit(solution)/shard_map/ppermute | solution.py:444
  12.7 10.5 %collective-permute-start.1 = (bf16[32,1344]{1,0:T(8,128)(2,1)S(1)}, bf16[32,1344]{1,0:T(8,128)(2,1)S(1)}, u32[]{:S(2)}, u32[]{:S(2)}) collective-permute-start(bf16[32,1344]{1,0:T(8,128)(2,1)S(1)} %shard_map.71.refs_0_), channel_id=1, source_target_pairs={{0,2},{2,0},{1,3},{3,1},{4,6},{6,4},{5,7},{7,5},{8,10},{10,8},{9,1... | collective-permute-start | bytes 258056 | tf_op jit(solution)/shard_map/ppermute | solution.py:423
  26.3 3.1 %collective-permute-start.3 = (f32[32,672]{1,0:T(8,128)S(1)}, f32[32,672]{1,0:T(8,128)S(1)}, u32[]{:S(2)}, u32[]{:S(2)}) collective-permute-start(f32[32,672]{1,0:T(8,128)S(1)} %get-tuple-element.42), channel_id=1, source_target_pairs={{0,1},{1,0},{2,3},{3,2},{4,5},{5,4},{6,7},{7,6},{8,9},{9,8},{10,11... | collective-permute-start | bytes 258056 | tf_op jit(solution)/shard_map/ppermute | solution.py:426
  29.3 1.5 %collective-permute-start.4 = (f32[32,640]{1,0:T(8,128)S(1)}, f32[32,640]{1,0:T(8,128)S(1)}, u32[]{:S(2)}, u32[]{:S(2)}) collective-permute-start(f32[32,640]{1,0:T(8,128)S(1)} %get-tuple-element.45), channel_id=1, source_target_pairs={{0,1},{1,0},{2,3},{3,2},{4,5},{5,4},{6,7},{7,6},{8,9},{9,8},{10,11... | collective-permute-start | bytes 245768 | tf_op jit(solution)/shard_map/ppermute | solution.py:426
  29.5 4.1 %collective-permute-start.5 = (bf16[32,704]{1,0:T(8,128)(2,1)S(1)}, bf16[32,704]{1,0:T(8,128)(2,1)S(1)}, u32[]{:S(2)}, u32[]{:S(2)}) collective-permute-start(bf16[32,704]{1,0:T(8,128)(2,1)S(1)} %get-tuple-element.43.refs_0_), channel_id=1, source_target_pairs={{0,2},{2,0},{1,3},{3,1},{4,6},{6,4},{5,7},{7,5},{8,10},{10,8},{9,1... | collective-permute-start | bytes 135176 | tf_op jit(solution)/shard_map/ppermute | solution.py:423
  33.8 6.4 %collective-permute-start.8 = (bf16[32,704]{1,0:T(8,128)(2,1)S(1)}, bf16[32,704]{1,0:T(8,128)(2,1)S(1)}, u32[]{:S(2)}, u32[]{:S(2)}) collective-permute-start(bf16[32,704]{1,0:T(8,128)(2,1)S(1)} %shard_map.77.refs_0_), channel_id=1, source_target_pairs={{12,0},{8,4},{4,8},{0,12},{13,1},{9,5},{5,9},{1,13},{14,2},{10,6},... | collective-permute-start | bytes 135176 | tf_op jit(solution)/shard_map/ppermute | solution.py:429
  36.5 5.4 %collective-permute-start.7 = (bf16[32,704]{1,0:T(8,128)(2,1)S(1)}, bf16[32,704]{1,0:T(8,128)(2,1)S(1)}, u32[]{:S(2)}, u32[]{:S(2)}) collective-permute-start(bf16[32,704]{1,0:T(8,128)(2,1)S(1)} %shard_map.77.refs_0_), channel_id=1, source_target_pairs={{8,0},{12,4},{0,8},{4,12},{9,1},{13,5},{1,9},{5,13},{10,2},{14,6},... | collective-permute-start | bytes 135176 | tf_op jit(solution)/shard_map/ppermute | solution.py:429
  36.8 5.1 %collective-permute-start.6 = (bf16[32,704]{1,0:T(8,128)(2,1)S(1)}, bf16[32,704]{1,0:T(8,128)(2,1)S(1)}, u32[]{:S(2)}, u32[]{:S(2)}) collective-permute-start(bf16[32,704]{1,0:T(8,128)(2,1)S(1)} %shard_map.77.refs_0_), channel_id=1, source_target_pairs={{4,0},{0,4},{12,8},{8,12},{5,1},{1,5},{13,9},{9,13},{6,2},{2,6},{1... | collective-permute-start | bytes 135176 | tf_op jit(solution)/shard_map/ppermute | solution.py:429
  42.5 1.2 %collective-permute-start.9 = (bf16[32,704]{1,0:T(8,128)(2,1)S(1)}, bf16[32,704]{1,0:T(8,128)(2,1)S(1)}, u32[]{:S(2)}, u32[]{:S(2)}) collective-permute-start(bf16[32,704]{1,0:T(8,128)(2,1)S(1)} %get-tuple-element.46.refs_0_), channel_id=1, source_target_pairs={{0,1},{1,0},{2,3},{3,2},{4,5},{5,4},{6,7},{7,6},{8,9},{9,8},{10,11... | collective-permute-start | bytes 135176 | tf_op jit(solution)/shard_map/ppermute | solution.py:426
  42.5 4.2 %collective-permute-start.10 = (bf16[32,704]{1,0:T(8,128)(2,1)S(1)}, bf16[32,704]{1,0:T(8,128)(2,1)S(1)}, u32[]{:S(2)}, u32[]{:S(2)}) collective-permute-start(bf16[32,704]{1,0:T(8,128)(2,1)S(1)} %get-tuple-element.46.refs_0_), channel_id=1, source_target_pairs={{0,2},{2,0},{1,3},{3,1},{4,6},{6,4},{5,7},{7,5},{8,10},{10,8},{9,1... | collective-permute-start | bytes 135176 | tf_op jit(solution)/shard_map/ppermute | solution.py:423
  46.7 1.2 %collective-permute-start.11 = (bf16[32,704]{1,0:T(8,128)(2,1)S(1)}, bf16[32,704]{1,0:T(8,128)(2,1)S(1)}, u32[]{:S(2)}, u32[]{:S(2)}) collective-permute-start(bf16[32,704]{1,0:T(8,128)(2,1)S(1)} %collective-permute-done.10.refs_2_), channel_id=1, source_target_pairs={{0,1},{1,0},{2,3},{3,2},{4,5},{5,4},{6,7},{7,6},{8,9},{9,8},{10,11... | collective-permute-start | bytes 135176 | tf_op jit(solution)/shard_map/ppermute | solution.py:426
  50.1 2.3 %collective-permute-start.12 = (f32[32,672]{1,0:T(8,128)S(1)}, f32[32,672]{1,0:T(8,128)S(1)}, u32[]{:S(2)}, u32[]{:S(2)}) collective-permute-start(f32[32,672]{1,0:T(8,128)S(1)} %get-tuple-element.52), channel_id=1, source_target_pairs={{0,1},{1,0},{2,3},{3,2},{4,5},{5,4},{6,7},{7,6},{8,9},{9,8},{10,11... | collective-permute-start | bytes 258056 | tf_op jit(solution)/shard_map/ppermute | solution.py:426
  51.9 2.3 %collective-permute-start.13 = (f32[32,640]{1,0:T(8,128)S(1)}, f32[32,640]{1,0:T(8,128)S(1)}, u32[]{:S(2)}, u32[]{:S(2)}) collective-permute-start(f32[32,640]{1,0:T(8,128)S(1)} %get-tuple-element.55), channel_id=1, source_target_pairs={{0,1},{1,0},{2,3},{3,2},{4,5},{5,4},{6,7},{7,6},{8,9},{9,8},{10,11... | collective-permute-start | bytes 245768 | tf_op jit(solution)/shard_map/ppermute | solution.py:426
  52.4 4.1 %collective-permute-start.14 = (bf16[32,704]{1,0:T(8,128)(2,1)S(1)}, bf16[32,704]{1,0:T(8,128)(2,1)S(1)}, u32[]{:S(2)}, u32[]{:S(2)}) collective-permute-start(bf16[32,704]{1,0:T(8,128)(2,1)S(1)} %get-tuple-element.53.refs_0_), channel_id=1, source_target_pairs={{0,2},{2,0},{1,3},{3,1},{4,6},{6,4},{5,7},{7,5},{8,10},{10,8},{9,1... | collective-permute-start | bytes 135176 | tf_op jit(solution)/shard_map/ppermute | solution.py:423
  56.7 10.8 %collective-permute-start.15 = (f32[32,2048]{1,0:T(8,128)S(1)}, f32[32,2048]{1,0:T(8,128)S(1)}, u32[]{:S(2)}, u32[]{:S(2)}) collective-permute-start(f32[32,2048]{1,0:T(8,128)S(1)} %get-tuple-element.56.h_ref.refs_0_), channel_id=1, source_target_pairs={{0,2},{2,0},{1,3},{3,1},{4,6},{6,4},{5,7},{7,5},{8,10},{10,8},{9,1... | collective-permute-start | bytes 786440 | tf_op jit(solution)/shard_map/ppermute | solution.py:423
  57.6 6.2 %collective-permute-start.18 = (bf16[32,704]{1,0:T(8,128)(2,1)S(1)}, bf16[32,704]{1,0:T(8,128)(2,1)S(1)}, u32[]{:S(2)}, u32[]{:S(2)}) collective-permute-start(bf16[32,704]{1,0:T(8,128)(2,1)S(1)} %shard_map.84.refs_0_), channel_id=1, source_target_pairs={{12,0},{8,4},{4,8},{0,12},{13,1},{9,5},{5,9},{1,13},{14,2},{10,6},... | collective-permute-start | bytes 135176 | tf_op jit(solution)/shard_map/ppermute | solution.py:429
  59.6 5.5 %collective-permute-start.17 = (bf16[32,704]{1,0:T(8,128)(2,1)S(1)}, bf16[32,704]{1,0:T(8,128)(2,1)S(1)}, u32[]{:S(2)}, u32[]{:S(2)}) collective-permute-start(bf16[32,704]{1,0:T(8,128)(2,1)S(1)} %shard_map.84.refs_0_), channel_id=1, source_target_pairs={{8,0},{12,4},{0,8},{4,12},{9,1},{13,5},{1,9},{5,13},{10,2},{14,6},... | collective-permute-start | bytes 135176 | tf_op jit(solution)/shard_map/ppermute | solution.py:429
  59.6 5.5 %collective-permute-start.16 = (bf16[32,704]{1,0:T(8,128)(2,1)S(1)}, bf16[32,704]{1,0:T(8,128)(2,1)S(1)}, u32[]{:S(2)}, u32[]{:S(2)}) collective-permute-start(bf16[32,704]{1,0:T(8,128)(2,1)S(1)} %shard_map.84.refs_0_), channel_id=1, source_target_pairs={{4,0},{0,4},{12,8},{8,12},{5,1},{1,5},{13,9},{9,13},{6,2},{2,6},{1... | collective-permute-start | bytes 135176 | tf_op jit(solution)/shard_map/ppermute | solution.py:429
  66.0 1.5 %collective-permute-start.19 = (f32[32,1280]{1,0:T(8,128)S(1)}, f32[32,1280]{1,0:T(8,128)S(1)}, u32[]{:S(2)}, u32[]{:S(2)}) collective-permute-start(f32[32,1280]{1,0:T(8,128)S(1)} %shard_map.85.refs_2_), channel_id=1, source_target_pairs={{0,1},{1,0},{2,3},{3,2},{4,5},{5,4},{6,7},{7,6},{8,9},{9,8},{10,11... | collective-permute-start | bytes 491528 | tf_op jit(solution)/shard_map/ppermute | solution.py:426

commit v7 on v6

--- a/solution.py
+++ b/solution.py
@@ -61,27 +61,12 @@
     out_ref[:, size + rank : size + 2 * rank] = rest
 
 
-def fetch_kernel(w_hbm, h_hbm, order_hbm, tab_hbm, *refs):
-    piece_ref, whole_ref, gram_ref, old_ref, order_ref, tab_ref, w_scr, sems = refs[-8:]
-    frames = old_ref.shape[1]
-    size = piece_ref.shape[1]
-    mine = pl.ds(pl.multiple_of(lax.axis_index("row") * frames, TAPS), frames)
-    copies = [
-        pltpu.make_async_copy(w_hbm, w_scr, sems.at[0]),
-        pltpu.make_async_copy(order_hbm, order_ref, sems.at[1]),
-        pltpu.make_async_copy(tab_hbm, tab_ref, sems.at[2]),
-        pltpu.make_async_copy(h_hbm.at[:, mine], old_ref, sems.at[3]),
-    ]
-    for copy in copies:
-        copy.start()
-    copies[0].wait()
-    w = w_scr[...]
-    rank = w.shape[0]
+def reorder_kernel(w_ref, order_ref, *refs):
+    piece_ref, msg_ref = refs[-2:]
+    w = w_ref[...]
+    rank, size = piece_ref.shape
     gram = lax.dot_general(w, w, NT, precision=HIGH, preferred_element_type=F32)
-    gram_ref[...] = gram
-    terms = three_terms(w)
-    copies[1].wait()
-    moved = jnp.dot(terms, order_ref[...], preferred_element_type=F32)
+    moved = jnp.dot(three_terms(w), order_ref[...], preferred_element_type=F32)
     whole = moved[:rank] + (moved[rank : 2 * rank] + moved[2 * rank :])
     for c in range(w.shape[1] // size):
 
@@ -89,13 +74,7 @@
         def _():
             piece_ref[...] = whole[:, c * size : (c + 1) * size]
 
-    whole_ref[...] = whole
-    copies[2].wait()
-    copies[3].wait()
-
-
-def pack_kernel(w_ref, gram_ref, *refs):
-    pack(refs[-1], w_ref[...], gram_ref[...])
+    pack(msg_ref, whole, gram)
 
 
 def three_terms(value):
@@ -106,7 +85,7 @@
 
 
 def edges_kernel(rows, sig_ref, *refs):
-    got_refs, out_ref = refs[: rows - 1], refs[rows - 1]
+    got_refs, out_ref = refs[: rows - 1], refs[-1]
     cl, width = sig_ref.shape
     x_me = lax.axis_index("row")
     for at, ref in enumerate((sig_ref,) + tuple(got_refs)):
@@ -185,32 +164,76 @@
         ref[...] = crossed(low, s_ref, lax.rem(x_me + dx, rows), lax.rem(c_me + dc, subs), subs, cl)
 
 
-def spectra_kernel(rows, cl, blocks, *refs):
-    refs = list(refs)
-    sig_refs = [refs.pop(0) for _ in range(rows)]
-    halo_ref, tab_ref, s_ref, xp_scr, x_scr = refs
+def place_signal(source, target, rows, frames):
+    x_me = lax.axis_index("row")
+    width = source.shape[1]
+
+    @pl.when(x_me == 0)
+    def _():
+        target[:, HALF:] = source[:, : frames + HALF]
+
+    @pl.when(x_me == rows - 1)
+    def _():
+        target[:, : frames + HALF] = source[:, width - frames - HALF :]
+
+    if rows > 2:
+
+        @pl.when((x_me > 0) & (x_me < rows - 1))
+        def _():
+            target[...] = source[:, HALF : HALF + frames + TAPS]
+
+
+def power_of(x_ref, table):
+    co = jnp.dot(x_ref[...], table, preferred_element_type=F32)
+    return (co[:, :TAPS] * co[:, :TAPS] + co[:, TAPS:] * co[:, TAPS:]).astype(BF16)
+
+
+def own_spectra_kernel(rows, sig_ref, w_hbm, h_hbm, order_hbm, tab_hbm, *refs):
+    s_ref, w_ref, old_ref, order_ref, tab_ref, xp_scr, x_scr, sems, tab_sems = refs
+    _, blocks, _, cl, _ = s_ref.shape
     frames = blocks * TAPS
-    width = sig_refs[0].shape[1]
     x_me = lax.axis_index("row")
-
-    def place(source, owner):
-        @pl.when(x_me == 0)
-        def _():
-            xp_scr[owner, :, HALF:] = source[:, : frames + HALF]
-
-        @pl.when(x_me == rows - 1)
-        def _():
-            skip = width - frames - HALF
-            xp_scr[owner, :, : frames + HALF] = source[:, skip:]
-
-        if rows > 2:
-
-            @pl.when((x_me > 0) & (x_me < rows - 1))
-            def _():
-                xp_scr[owner] = source[:, HALF : HALF + frames + TAPS]
-
+    mine = pl.ds(pl.multiple_of(x_me * frames, TAPS), frames)
+
+    def tab_copy(g):
+        span = pl.ds(g * GROUP, GROUP)
+        return pltpu.make_async_copy(tab_hbm.at[span], tab_ref.at[span], tab_sems.at[g])
+
+    later = [
+        pltpu.make_async_copy(w_hbm, w_ref, sems.at[0]),
+        pltpu.make_async_copy(order_hbm, order_ref, sems.at[1]),
+        pltpu.make_async_copy(h_hbm.at[:, mine], old_ref, sems.at[2]),
+    ]
+    for g in range(GROUPS):
+        tab_copy(g).start()
+    for copy in later:
+        copy.start()
+    place_signal(sig_ref, xp_scr, rows, frames)
+    first = jnp.where(x_me == 0, 1, 0)
+    for at in range(blocks - 1):
+        begin = pl.multiple_of((first + at) * TAPS, TAPS)
+        x_scr[at * cl : (at + 1) * cl, :] = xp_scr[:, pl.ds(begin, 2 * TAPS)]
+
+    def convolve(g, carry):
+        tab_copy(g).wait()
+        for at in range(GROUP):
+            f = g * GROUP + at
+            s_ref[f, pl.ds(first, blocks - 1), x_me] = power_of(x_scr, tab_ref[f]).reshape(blocks - 1, cl, TAPS)
+        return carry
+
+    lax.fori_loop(0, GROUPS, convolve, 0)
+    for copy in later:
+        copy.wait()
+
+
+def other_spectra_kernel(rows, halo_ref, tab_ref, *refs):
+    sig_refs, (_, s_ref, xp_scr, x_scr) = refs[:rows], refs[rows:]
+    _, blocks, _, cl, _ = s_ref.shape
+    frames = blocks * TAPS
+    x_me = lax.axis_index("row")
+    owners = [lax.rem(x_me + rows - shift, rows) for shift in range(rows)]
     for shift in range(rows):
-        place(sig_refs[shift], lax.rem(x_me + rows - shift, rows))
+        place_signal(sig_refs[shift], xp_scr.at[owners[shift]], rows, frames)
 
     @pl.when(x_me == 0)
     def _():
@@ -222,19 +245,22 @@
         for at in range(rows):
             xp_scr[(rows - at) % rows, :, frames + HALF :] = halo_ref[at * cl : (at + 1) * cl, :HALF]
 
-    for blk in range(blocks):
-        for x in range(rows):
-            x_scr[blk, x * cl : (x + 1) * cl, :] = xp_scr[x, :, blk * TAPS : (blk + 2) * TAPS]
+    outer = jnp.where(x_me == 0, 0, blocks - 1)
+    begin = pl.multiple_of(outer * TAPS, TAPS)
+    x_scr[:cl, :] = xp_scr[x_me, :, pl.ds(begin, 2 * TAPS)]
+    for shift in range(1, rows):
+        for blk in range(blocks):
+            at = cl * (1 + (shift - 1) * blocks + blk)
+            x_scr[at : at + cl, :] = xp_scr[owners[shift], :, blk * TAPS : (blk + 2) * TAPS]
 
     def convolve(g, carry):
         for at in range(GROUP):
-            co = jnp.dot(
-                x_scr[...].reshape(blocks * rows * cl, 2 * TAPS),
-                tab_ref[g * GROUP + at],
-                preferred_element_type=F32,
-            )
-            power = co[:, :TAPS] * co[:, :TAPS] + co[:, TAPS:] * co[:, TAPS:]
-            s_ref[g * GROUP + at] = power.astype(BF16).reshape(blocks, rows, cl, TAPS)
+            f = g * GROUP + at
+            power = power_of(x_scr, tab_ref[f])
+            s_ref[f, outer, x_me] = power[:cl]
+            for shift in range(1, rows):
+                line = cl * (1 + (shift - 1) * blocks)
+                s_ref[f, :, owners[shift]] = power[line : line + blocks * cl].reshape(blocks, cl, TAPS)
         return carry
 
     lax.fori_loop(0, GROUPS, convolve, 0)
@@ -377,7 +403,7 @@
         copy.wait()
 
 
-def call(kernel, args, outs, scratch=(), in_specs=None, out_specs=None, limit=4, cost=None):
+def call(kernel, args, outs, scratch=(), in_specs=None, out_specs=None, limit=4, cost=None, aliases=None):
     whole = pl.BlockSpec(memory_space=pltpu.VMEM)
     if cost is not None:
         cost = pl.CostEstimate(flops=cost, bytes_accessed=0, transcendentals=0)
@@ -389,6 +415,7 @@
         scratch_shapes=list(scratch),
         compiler_params=pltpu.CompilerParams(vmem_limit_bytes=limit * MIB),
         cost_estimate=cost,
+        input_output_aliases=aliases or {},
     )(*args)
 
 
@@ -439,45 +466,59 @@
         in_specs=[anywhere],
     )
     sig = [own_sig] + [row_shift(part, shift + 1) for shift, part in enumerate(out_sigs)]
-    (edge,) = call(functools.partial(edges_kernel, rows), sig, [((chans, TAPS), BF16)])
-    pairs = [(place(rows - 1, i), place(0, i + 1)) for i in range(line - 1)]
-    halo = lax.ppermute(edge, ("frm", "row", "sub"), pairs + [(b, a) for a, b in pairs])
-
     msg = ((rank, size + 2 * rank), BF16)
     piece = ((rank, size), F32)
     update_outs = [((rank, frames), F32), ((rank, rank), F32)]
     update_outs += [((rank, size + rank), F32)] * ((rows - 1) * (subs - 1))
     table, order = jnp.asarray(toeplitz()), jnp.asarray(reorder(cl))
-    w_piece, w_whole, w_gram, old, order, table = call(
-        fetch_kernel,
-        [hbm(w_start.T), hbm(h_start), hbm(order), hbm(table), own_sig],
+    half_done, w_own, old, order, table = call(
+        functools.partial(own_spectra_kernel, rows),
+        [own_sig, hbm(w_start.T), hbm(h_start), hbm(order), hbm(table)],
         [
-            piece,
-            ((rank, NF * cl), F32),
-            ((rank, rank), F32),
+            pltpu.VMEM((NF, blocks, rows, cl, TAPS), BF16),
+            pltpu.VMEM((rank, NF * cl), F32),
             pltpu.VMEM((rank, frames), F32),
             pltpu.VMEM(order.shape, BF16),
             pltpu.VMEM(table.shape, BF16),
         ],
-        [pltpu.VMEM((rank, NF * cl), F32), pltpu.SemaphoreType.DMA((4,))],
-        in_specs=[anywhere] * 5,
-        cost=2 * 10**9,
-    )
-    (w_msg,) = call(
-        pack_kernel,
-        [w_whole, w_gram, edge],
-        [((rank, NF * cl + 2 * rank), BF16)],
+        [
+            pltpu.VMEM((cl, frames + TAPS), BF16),
+            pltpu.VMEM(((blocks - 1) * cl, 2 * TAPS), BF16),
+            pltpu.SemaphoreType.DMA((3,)),
+            pltpu.SemaphoreType.DMA((GROUPS,)),
+        ],
+        in_specs=[whole] + [anywhere] * 4,
+        limit=8,
+        cost=2 * NF * cl * frames * 4 * TAPS,
+    )
+    order = vmem(order)
+    (edge,) = call(
+        functools.partial(edges_kernel, rows),
+        sig + [vmem(half_done)],
+        [((chans, TAPS), BF16)],
+        in_specs=[whole] * rows + [anywhere],
+    )
+    pairs = [(place(rows - 1, i), place(0, i + 1)) for i in range(line - 1)]
+    halo = lax.ppermute(edge, ("frm", "row", "sub"), pairs + [(b, a) for a, b in pairs])
+    w_piece, w_msg = call(
+        reorder_kernel,
+        [vmem(w_own), order, edge],
+        [piece, ((rank, NF * cl + 2 * rank), BF16)],
         in_specs=[whole, whole, anywhere],
     )
     w_msgs = [w_msg] + [row_shift(w_msg, shift) for shift in range(1, rows)]
-    order = vmem(order)
     (spectra,) = call(
-        functools.partial(spectra_kernel, rows, cl, blocks),
-        sig + [halo, vmem(table)],
+        functools.partial(other_spectra_kernel, rows),
+        [halo, vmem(table)] + sig + [vmem(half_done)],
         [pltpu.VMEM((NF, blocks, rows, cl, TAPS), BF16)],
-        [pltpu.VMEM((rows, cl, frames + TAPS), BF16), pltpu.VMEM((blocks, chans, 2 * TAPS), BF16)],
+        [
+            pltpu.VMEM((rows, cl, frames + TAPS), BF16),
+            pltpu.VMEM((((rows - 1) * blocks + 1) * cl, 2 * TAPS), BF16),
+        ],
+        in_specs=[whole] * (rows + 2) + [anywhere],
         limit=8,
         cost=2 * NF * chans * frames * 4 * TAPS,
+        aliases={rows + 2: 0},
     )
     spectra = vmem(spectra)
 

time: 68.5 us -> 65 us (0.949)
  waiting for transfers between devices: 20.4 us -> 18.2 us
  starting transfers between devices: 21.1 us -> 19.6 us
    ppermute x6, waiting for transfers between devices: 10.8 us -> 7.37 us  [row_shift(): lax.ppermute(value, 'row', [(i, (i + shift) % rows) for i in range(rows)])]
    ppermute x6, starting transfers between devices: 9.41 us -> 6.99 us  [row_shift(): lax.ppermute(value, 'row', [(i, (i + shift) % rows) for i in range(rows)])]
    ppermute x7, waiting for transfers between devices: 2.82 us -> 3.72 us  [sub_shift(): lax.ppermute(value, 'sub', [(i, (i + shift) % subs) for i in range(subs)])]
  transfers between devices with their start and end apart: 20 -> 20, of which waited for: 11 -> 10; matrix products, arithmetic and copies ran while one was open for 0% -> 0% of each run, Pallas kernels for 27% -> 28%
where the time goes in v7:
time: 65 us; the launch traced here: 64.9 us
  Pallas kernels  26.3 us (40%)
  starting transfers between devices  19.6 us (30%)
  waiting for transfers between devices  18.2 us (28%)
  between operations  0.79 us (1%)
    pallas_call x19, Pallas kernels, call(): pl.pallas_call(kernel, out_shape=[jax.ShapeDtypeStruct(*out) if isinstanc...  26.3 us
    ppermute x6, starting transfers between devices, frm_shift(): lax.ppermute(value, 'frm', [(partner(i, shift, frms), i) for i in range(f...  9.38 us
    ppermute x6, waiting for transfers between devices, row_shift(): lax.ppermute(value, 'row', [(i, (i + shift) % rows) for i in range(rows)])  7.37 us
    ppermute x6, waiting for transfers between devices, frm_shift(): lax.ppermute(value, 'frm', [(partner(i, shift, frms), i) for i in range(f...  7.14 us
    ppermute x6, starting transfers between devices, row_shift(): lax.ppermute(value, 'row', [(i, (i + shift) % rows) for i in range(rows)])  6.99 us
    ppermute x7, waiting for transfers between devices, sub_shift(): lax.ppermute(value, 'sub', [(i, (i + shift) % subs) for i in range(subs)])  3.72 us
    ppermute x7, starting transfers between devices, sub_shift(): lax.ppermute(value, 'sub', [(i, (i + shift) % subs) for i in range(subs)])  2.55 us
  transfers between devices with their start and end apart: 20, of which 10 were waited for; matrix products, arithmetic and copies ran while one was open for 0% of the time, Pallas kernels for 28%

profile of v7, /device:TPU:0, one launch (start us, length us, event | category | flops | bytes accessed | tf_op | source)
XLA Modules:
  0.0 64.9 jit_solution(11006818155593402237)
XLA Ops:
  0.6 1.0 %shard_map.68 = (bf16[32,2176]{1,0:T(8,128)(2,1)S(1)}, bf16[32,2176]{1,0:T(8,128)(2,1)S(1)}) custom-call(bf16[32,4096]{1,0:T(8,128)(2,1)} %sig_hbm.1), custom_call_target="tpu_custom_call" | custom-call | tf_op jit(solution)/shard_map/pallas_call | solution.py:410
  1.7 3.0 %collective-permute-start = (bf16[32,2176]{1,0:T(8,128)(2,1)S(1)}, bf16[32,2176]{1,0:T(8,128)(2,1)S(1)}, u32[]{:S(2)}, u32[]{:S(2)}) collective-permute-start(bf16[32,2176]{1,0:T(8,128)(2,1)S(1)} %get-tuple-element.36), channel_id=1, source_target_pairs={{0,2},{2,0},{1,3},{3,1},{4,6},{6,4},{5,7},{7,5},{8,10},{10,8},{9,1... | collective-permute-start | bytes 417800 | tf_op jit(solution)/shard_map/ppermute | solution.py:450
  4.7 5.5 %shard_map.69 = (bf16[40,16,2,32,128]{4,3,2,1,0:T(8,128)(2,1)S(1)}, f32[32,1280]{1,0:T(8,128)S(1)}, f32[32,2048]{1,0:T(8,128)S(1)}, bf16[1280,1280]{1,0:T(8,128)(2,1)S(1)}, bf16[40,256,256]{2,1,0:T(8,128)(2,1)S(1)}) custom-call(bf16[32,2176]{1,0:T(8,128)(2,1)S(1)} %get-tuple-element.33.sig_ref.refs_0_, f32[32,1280]{1,0:T(8,128)} %bitcast.2, ...), custom_call_target="tpu_custom_call" | custom-call | flops 2684354560 | tf_op jit(solution)/shard_map/pallas_call | solution.py:410
  10.1 0.0 collective-permute-done.refs_0_.refs_1_
  10.2 0.7 %collective-permute-start.2 = (bf16[64,128]{1,0:T(8,128)(2,1)S(1)}, bf16[64,128]{1,0:T(8,128)(2,1)S(1)}, u32[]{:S(2)}, u32[]{:S(2)}) collective-permute-start(bf16[64,128]{1,0:T(8,128)(2,1)S(1)} %shard_map.70.refs_0_), channel_id=1, source_target_pairs={{2,1},{3,4},{6,5},{7,8},{10,9},{11,12},{14,13},{1,2},{4,3},{5,6},{... | collective-permute-start | bytes 49160 | tf_op jit(solution)/shard_map/ppermute | solution.py:502
  10.8 0.8 %shard_map.71 = (f32[32,640]{1,0:T(8,128)S(1)}, bf16[32,1344]{1,0:T(8,128)(2,1)S(1)}) custom-call(f32[32,1280]{1,0:T(8,128)S(1)} %get-tuple-element.34.w_ref, bf16[1280,1280]{1,0:T(8,128)(2,1)S(1)} %get-tuple-element.35.order_ref, bf16[64,128]{1,0:T(8,128)(2,1)S(1)} %shard_map.70.refs_0_), custom_call_target="tpu_custom_call" | custom-call | tf_op jit(solution)/shard_map/pallas_call | solution.py:410
  11.7 2.4 %collective-permute-start.1 = (bf16[32,1344]{1,0:T(8,128)(2,1)S(1)}, bf16[32,1344]{1,0:T(8,128)(2,1)S(1)}, u32[]{:S(2)}, u32[]{:S(2)}) collective-permute-start(bf16[32,1344]{1,0:T(8,128)(2,1)S(1)} %get-tuple-element.39.refs_0_), channel_id=1, source_target_pairs={{0,2},{2,0},{1,3},{3,1},{4,6},{6,4},{5,7},{7,5},{8,10},{10,8},{9,1... | collective-permute-start | bytes 258056 | tf_op jit(solution)/shard_map/ppermute | solution.py:450
  14.1 0.0 collective-permute-done.2.halo_ref
  14.1 5.0 %shard_map.72.refs_3_.s_ref.refs_2_.refs_6_ = bf16[40,16,2,32,128]{4,3,2,1,0:T(8,128)(2,1)S(1)} custom-call(bf16[64,128]{1,0:T(8,128)(2,1)S(1)} %collective-permute-done.2.halo_ref, bf16[40,256,256]{2,1,0:T(8,128)(2,1)S(1)} %get-tuple-element.41.tab_ref, bf16[32,2176]{1,0:T(8,128)(2,1)S(1)} %get-tuple-element.33.sig_ref.refs_0_, ...), custom_call_target="tpu_custom_call", output_to_operand_aliasing={{}: (4, {})} | custom-call | flops 5368709120 | tf_op jit(solution)/shard_map/pallas_call | solution.py:410
  19.2 0.0 collective-permute-done.1.refs_1_
  19.2 3.0 %shard_map.73 = (f32[32,2048]{1,0:T(8,128)S(1)}, f32[32,32]{1,0:T(8,128)S(1)}, f32[32,672]{1,0:T(8,128)S(1)}) custom-call(bf16[32,1344]{1,0:T(8,128)(2,1)S(1)} %get-tuple-element.39.refs_0_, bf16[32,1344]{1,0:T(8,128)(2,1)S(1)} %collective-permute-done.1.refs_1_, f32[32,2048]{1,0:T(8,128)S(1)} %get-tuple-element.40.refs_2_, ...), custom_call_target="tpu_custom_call" | custom-call | tf_op jit(solution)/shard_map/pallas_call | solution.py:410
  22.2 1.8 %collective-permute-start.3 = (f32[32,672]{1,0:T(8,128)S(1)}, f32[32,672]{1,0:T(8,128)S(1)}, u32[]{:S(2)}, u32[]{:S(2)}) collective-permute-start(f32[32,672]{1,0:T(8,128)S(1)} %get-tuple-element.45), channel_id=1, source_target_pairs={{0,1},{1,0},{2,3},{3,2},{4,5},{5,4},{6,7},{7,6},{8,9},{9,8},{10,11... | collective-permute-start | bytes 258056 | tf_op jit(solution)/shard_map/ppermute | solution.py:453
  24.0 1.6 %shard_map.74 = (f32[32,640]{1,0:T(8,128)S(1)}, f32[32,640]{1,0:T(8,128)S(1)}) custom-call(f32[32,2048]{1,0:T(8,128)S(1)} %get-tuple-element.42.h_ref.refs_5_, bf16[40,16,2,32,128]{4,3,2,1,0:T(8,128)(2,1)S(1)} %shard_map.72.refs_3_.s_ref.refs_2_.refs_6_), custom_call_target="tpu_custom_call" | custom-call | flops 1342177280 | tf_op jit(solution)/shard_map/pallas_call | solution.py:410
  25.6 0.1 collective-permute-start.4
  25.7 0.0 collective-permute-done.3.refs_2_
  25.7 0.1 shard_map.75
  25.8 0.8 %collective-permute-start.5 = (bf16[32,704]{1,0:T(8,128)(2,1)S(1)}, bf16[32,704]{1,0:T(8,128)(2,1)S(1)}, u32[]{:S(2)}, u32[]{:S(2)}) collective-permute-start(bf16[32,704]{1,0:T(8,128)(2,1)S(1)} %get-tuple-element.46.refs_0_), channel_id=1, source_target_pairs={{0,2},{2,0},{1,3},{3,1},{4,6},{6,4},{5,7},{7,5},{8,10},{10,8},{9,1... | collective-permute-start | bytes 135176 | tf_op jit(solution)/shard_map/ppermute | solution.py:450
  26.6 0.8 %shard_map.76.own_ref = f32[32,640]{1,0:T(8,128)S(1)} custom-call(f32[32,2048]{1,0:T(8,128)S(1)} %get-tuple-element.42.h_ref.refs_5_, bf16[40,16,2,32,128]{4,3,2,1,0:T(8,128)(2,1)S(1)} %shard_map.72.refs_3_.s_ref.refs_2_.refs_6_, bf16[32,704]{1,0:T(8,128)(2,1)S(1)} %get-tuple-element.46.refs_0_), custom_call_target="tpu_custom_call" | custom-call | flops 1 | tf_op jit(solution)/shard_map/pallas_call | solution.py:410
  27.4 0.0 collective-permute-done.4.refs_0_
  27.5 2.5 %collective-permute-done.5.refs_1_ = bf16[32,704]{1,0:T(8,128)(2,1)S(1)} collective-permute-done((bf16[32,704]{1,0:T(8,128)(2,1)S(1)}, bf16[32,704]{1,0:T(8,128)(2,1)S(1)}, u32[]{:S(2)}, u32[]{:S(2)}) %collective-permute-start.5) | collective-permute-done | bytes 45088 | tf_op jit(solution)/shard_map/ppermute | solution.py:450
  29.9 0.2 shard_map.77.refs_0_
  30.1 4.4 %collective-permute-start.8 = (bf16[32,704]{1,0:T(8,128)(2,1)S(1)}, bf16[32,704]{1,0:T(8,128)(2,1)S(1)}, u32[]{:S(2)}, u32[]{:S(2)}) collective-permute-start(bf16[32,704]{1,0:T(8,128)(2,1)S(1)} %shard_map.77.refs_0_), channel_id=1, source_target_pairs={{12,0},{8,4},{4,8},{0,12},{13,1},{9,5},{5,9},{1,13},{14,2},{10,6},... | collective-permute-start | bytes 135176 | tf_op jit(solution)/shard_map/ppermute | solution.py:456
  34.4 0.0 collective-permute-start.7
  34.4 0.6 collective-permute-start.6
  35.1 1.6 %collective-permute-done.8.refs_3_ = bf16[32,704]{1,0:T(8,128)(2,1)S(1)} collective-permute-done((bf16[32,704]{1,0:T(8,128)(2,1)S(1)}, bf16[32,704]{1,0:T(8,128)(2,1)S(1)}, u32[]{:S(2)}, u32[]{:S(2)}) %collective-permute-start.8) | collective-permute-done | bytes 45088 | tf_op jit(solution)/shard_map/ppermute | solution.py:456
  36.7 2.7 %collective-permute-done.7.refs_2_ = bf16[32,704]{1,0:T(8,128)(2,1)S(1)} collective-permute-done((bf16[32,704]{1,0:T(8,128)(2,1)S(1)}, bf16[32,704]{1,0:T(8,128)(2,1)S(1)}, u32[]{:S(2)}, u32[]{:S(2)}) %collective-permute-start.7) | collective-permute-done | bytes 45088 | tf_op jit(solution)/shard_map/ppermute | solution.py:456
  39.4 0.0 collective-permute-done.6.refs_1_
  39.4 0.6 shard_map.78
  40.0 0.0 collective-permute-start.9
  40.0 0.1 collective-permute-start.10
  40.2 1.1 %collective-permute-done.9.refs_1_ = bf16[32,704]{1,0:T(8,128)(2,1)S(1)} collective-permute-done((bf16[32,704]{1,0:T(8,128)(2,1)S(1)}, bf16[32,704]{1,0:T(8,128)(2,1)S(1)}, u32[]{:S(2)}, u32[]{:S(2)}) %collective-permute-start.9) | collective-permute-done | bytes 45088 | tf_op jit(solution)/shard_map/ppermute | solution.py:453
  41.3 1.0 %shard_map.79.refs_4_ = f32[32,2048]{1,0:T(8,128)S(1)} custom-call(bf16[32,704]{1,0:T(8,128)(2,1)S(1)} %get-tuple-element.49.refs_0_, bf16[32,704]{1,0:T(8,128)(2,1)S(1)} %collective-permute-done.9.refs_1_, bf16[40,16,2,32,128]{4,3,2,1,0:T(8,128)(2,1)S(1)} %shard_map.72.refs_3_.s_ref.refs_2_.refs_6_), custom_call_target="tpu_custom_call" | custom-call | flops 1342177280 | tf_op jit(solution)/shard_map/pallas_call | solution.py:410
  42.3 1.9 %collective-permute-done.10.refs_2_ = bf16[32,704]{1,0:T(8,128)(2,1)S(1)} collective-permute-done((bf16[32,704]{1,0:T(8,128)(2,1)S(1)}, bf16[32,704]{1,0:T(8,128)(2,1)S(1)}, u32[]{:S(2)}, u32[]{:S(2)}) %collective-permute-start.10) | collective-permute-done | bytes 45088 | tf_op jit(solution)/shard_map/ppermute | solution.py:450
  44.2 0.0 collective-permute-start.11
  44.2 1.2 %collective-permute-done.11.refs_3_ = bf16[32,704]{1,0:T(8,128)(2,1)S(1)} collective-permute-done((bf16[32,704]{1,0:T(8,128)(2,1)S(1)}, bf16[32,704]{1,0:T(8,128)(2,1)S(1)}, u32[]{:S(2)}, u32[]{:S(2)}) %collective-permute-start.11) | collective-permute-done | bytes 45088 | tf_op jit(solution)/shard_map/ppermute | solution.py:453
  45.4 2.1 %shard_map.80 = (f32[32,2048]{1,0:T(8,128)S(1)}, f32[32,32]{1,0:T(8,128)S(1)}, f32[32,672]{1,0:T(8,128)S(1)}) custom-call(bf16[32,704]{1,0:T(8,128)(2,1)S(1)} %get-tuple-element.49.refs_0_, bf16[32,704]{1,0:T(8,128)(2,1)S(1)} %collective-permute-done.9.refs_1_, bf16[32,704]{1,0:T(8,128)(2,1)S(1)} %collective-permute-done.10.refs_2_, ...), custom_call_target="tpu_custom_call" | custom-call | tf_op jit(solution)/shard_map/pallas_call | solution.py:410
  47.6 0.2 collective-permute-start.12
  47.8 1.6 %shard_map.81 = (f32[32,640]{1,0:T(8,128)S(1)}, f32[32,640]{1,0:T(8,128)S(1)}) custom-call(f32[32,2048]{1,0:T(8,128)S(1)} %get-tuple-element.59.h_ref.refs_0_, bf16[40,16,2,32,128]{4,3,2,1,0:T(8,128)(2,1)S(1)} %shard_map.72.refs_3_.s_ref.refs_2_.refs_6_), custom_call_target="tpu_custom_call" | custom-call | flops 1342177280 | tf_op jit(solution)/shard_map/pallas_call | solution.py:410
  49.4 0.4 collective-permute-start.13
  49.8 0.0 collective-permute-done.12.refs_2_
  49.8 0.1 shard_map.82
  49.9 0.3 collective-permute-start.14
  50.2 0.8 %shard_map.83.own_ref = f32[32,640]{1,0:T(8,128)S(1)} custom-call(f32[32,2048]{1,0:T(8,128)S(1)} %get-tuple-element.59.h_ref.refs_0_, bf16[40,16,2,32,128]{4,3,2,1,0:T(8,128)(2,1)S(1)} %shard_map.72.refs_3_.s_ref.refs_2_.refs_6_, bf16[32,704]{1,0:T(8,128)(2,1)S(1)} %get-tuple-element.56.refs_0_), custom_call_target="tpu_custom_call" | custom-call | flops 1 | tf_op jit(solution)/shard_map/pallas_call | solution.py:410
  51.0 0.0 collective-permute-done.13.refs_0_
  51.0 3.0 %collective-permute-done.14.refs_1_ = bf16[32,704]{1,0:T(8,128)(2,1)S(1)} collective-permute-done((bf16[32,704]{1,0:T(8,128)(2,1)S(1)}, bf16[32,704]{1,0:T(8,128)(2,1)S(1)}, u32[]{:S(2)}, u32[]{:S(2)}) %collective-permute-start.14) | collective-permute-done | bytes 45088 | tf_op jit(solution)/shard_map/ppermute | solution.py:450
  54.0 0.2 shard_map.84.refs_0_
  54.2 0.3 collective-permute-start.15
  54.4 1.7 %collective-permute-start.18 = (bf16[32,704]{1,0:T(8,128)(2,1)S(1)}, bf16[32,704]{1,0:T(8,128)(2,1)S(1)}, u32[]{:S(2)}, u32[]{:S(2)}) collective-permute-start(bf16[32,704]{1,0:T(8,128)(2,1)S(1)} %shard_map.84.refs_0_), channel_id=1, source_target_pairs={{12,0},{8,4},{4,8},{0,12},{13,1},{9,5},{5,9},{1,13},{14,2},{10,6},... | collective-permute-start | bytes 135176 | tf_op jit(solution)/shard_map/ppermute | solution.py:456
  56.1 0.4 collective-permute-start.17
  56.5 2.4 %collective-permute-start.16 = (bf16[32,704]{1,0:T(8,128)(2,1)S(1)}, bf16[32,704]{1,0:T(8,128)(2,1)S(1)}, u32[]{:S(2)}, u32[]{:S(2)}) collective-permute-start(bf16[32,704]{1,0:T(8,128)(2,1)S(1)} %shard_map.84.refs_0_), channel_id=1, source_target_pairs={{4,0},{0,4},{12,8},{8,12},{5,1},{1,5},{13,9},{9,13},{6,2},{2,6},{1... | collective-permute-start | bytes 135176 | tf_op jit(solution)/shard_map/ppermute | solution.py:456
  58.8 1.5 %collective-permute-done.18.refs_3_ = bf16[32,704]{1,0:T(8,128)(2,1)S(1)} collective-permute-done((bf16[32,704]{1,0:T(8,128)(2,1)S(1)}, bf16[32,704]{1,0:T(8,128)(2,1)S(1)}, u32[]{:S(2)}, u32[]{:S(2)}) %collective-permute-start.18) | collective-permute-done | bytes 45088 | tf_op jit(solution)/shard_map/ppermute | solution.py:456
  60.3 1.3 %collective-permute-done.17.refs_2_ = bf16[32,704]{1,0:T(8,128)(2,1)S(1)} collective-permute-done((bf16[32,704]{1,0:T(8,128)(2,1)S(1)}, bf16[32,704]{1,0:T(8,128)(2,1)S(1)}, u32[]{:S(2)}, u32[]{:S(2)}) %collective-permute-start.17) | collective-permute-done | bytes 45088 | tf_op jit(solution)/shard_map/ppermute | solution.py:456
  61.6 0.0 collective-permute-done.16.refs_1_
  61.6 0.9 %shard_map.85.refs_2_ = f32[32,1280]{1,0:T(8,128)S(1)} custom-call(f32[32,640]{1,0:T(8,128)S(1)} %get-tuple-element.60.w_ref, bf16[1280,1280]{1,0:T(8,128)(2,1)S(1)} %get-tuple-element.35.order_ref, bf16[32,704]{1,0:T(8,128)(2,1)S(1)} %shard_map.84.refs_0_, bf16[32,704]{1,0:T(8,128)(2,1)S(1)} %collective-permute-done.16.refs_1_, ...), custom_call_target="tpu_custom_call" | custom-call | tf_op jit(solution)/shard_map/pallas_call | solution.py:410
  62.5 0.1 collective-permute-start.19
  62.6 1.4 %collective-permute-done.19.refs_3_ = f32[32,1280]{1,0:T(8,128)S(1)} collective-permute-done((f32[32,1280]{1,0:T(8,128)S(1)}, f32[32,1280]{1,0:T(8,128)S(1)}, u32[]{:S(2)}, u32[]{:S(2)}) %collective-permute-start.19) | collective-permute-done | bytes 163872 | tf_op jit(solution)/shard_map/ppermute | solution.py:453
  64.0 0.0 collective-permute-done.15.refs_1_
  64.0 0.9 %shard_map.86 = (f32[32,1280]{1,0:T(8,128)}, f32[32,4096]{1,0:T(8,128)}) custom-call(f32[32,2048]{1,0:T(8,128)S(1)} %get-tuple-element.59.h_ref.refs_0_, f32[32,2048]{1,0:T(8,128)S(1)} %collective-permute-done.15.refs_1_, f32[32,1280]{1,0:T(8,128)S(1)} %shard_map.85.refs_2_, f32[32,1280]{1,0:T(8,128)S(1)} %collective-permute-done.19.refs_3_), custom_call_target="tpu_custom_call" | custom-call | tf_op jit(solution)/shard_map/pallas_call | solution.py:410
  (1 shorter events, 0.0 us)
Async XLA Ops:
  1.7 8.5 %collective-permute-start = (bf16[32,2176]{1,0:T(8,128)(2,1)S(1)}, bf16[32,2176]{1,0:T(8,128)(2,1)S(1)}, u32[]{:S(2)}, u32[]{:S(2)}) collective-permute-start(bf16[32,2176]{1,0:T(8,128)(2,1)S(1)} %get-tuple-element.36), channel_id=1, source_target_pairs={{0,2},{2,0},{1,3},{3,1},{4,6},{6,4},{5,7},{7,5},{8,10},{10,8},{9,1... | collective-permute-start | bytes 417800 | tf_op jit(solution)/shard_map/ppermute | solution.py:450
  10.2 4.0 %collective-permute-start.2 = (bf16[64,128]{1,0:T(8,128)(2,1)S(1)}, bf16[64,128]{1,0:T(8,128)(2,1)S(1)}, u32[]{:S(2)}, u32[]{:S(2)}) collective-permute-start(bf16[64,128]{1,0:T(8,128)(2,1)S(1)} %shard_map.70.refs_0_), channel_id=1, source_target_pairs={{2,1},{3,4},{6,5},{7,8},{10,9},{11,12},{14,13},{1,2},{4,3},{5,6},{... | collective-permute-start | bytes 49160 | tf_op jit(solution)/shard_map/ppermute | solution.py:502
  11.7 7.5 %collective-permute-start.1 = (bf16[32,1344]{1,0:T(8,128)(2,1)S(1)}, bf16[32,1344]{1,0:T(8,128)(2,1)S(1)}, u32[]{:S(2)}, u32[]{:S(2)}) collective-permute-start(bf16[32,1344]{1,0:T(8,128)(2,1)S(1)} %get-tuple-element.39.refs_0_), channel_id=1, source_target_pairs={{0,2},{2,0},{1,3},{3,1},{4,6},{6,4},{5,7},{7,5},{8,10},{10,8},{9,1... | collective-permute-start | bytes 258056 | tf_op jit(solution)/shard_map/ppermute | solution.py:450
  22.2 3.5 %collective-permute-start.3 = (f32[32,672]{1,0:T(8,128)S(1)}, f32[32,672]{1,0:T(8,128)S(1)}, u32[]{:S(2)}, u32[]{:S(2)}) collective-permute-start(f32[32,672]{1,0:T(8,128)S(1)} %get-tuple-element.45), channel_id=1, source_target_pairs={{0,1},{1,0},{2,3},{3,2},{4,5},{5,4},{6,7},{7,6},{8,9},{9,8},{10,11... | collective-permute-start | bytes 258056 | tf_op jit(solution)/shard_map/ppermute | solution.py:453
  25.6 1.8 %collective-permute-start.4 = (f32[32,640]{1,0:T(8,128)S(1)}, f32[32,640]{1,0:T(8,128)S(1)}, u32[]{:S(2)}, u32[]{:S(2)}) collective-permute-start(f32[32,640]{1,0:T(8,128)S(1)} %get-tuple-element.48), channel_id=1, source_target_pairs={{0,1},{1,0},{2,3},{3,2},{4,5},{5,4},{6,7},{7,6},{8,9},{9,8},{10,11... | collective-permute-start | bytes 245768 | tf_op jit(solution)/shard_map/ppermute | solution.py:453
  25.8 4.1 %collective-permute-start.5 = (bf16[32,704]{1,0:T(8,128)(2,1)S(1)}, bf16[32,704]{1,0:T(8,128)(2,1)S(1)}, u32[]{:S(2)}, u32[]{:S(2)}) collective-permute-start(bf16[32,704]{1,0:T(8,128)(2,1)S(1)} %get-tuple-element.46.refs_0_), channel_id=1, source_target_pairs={{0,2},{2,0},{1,3},{3,1},{4,6},{6,4},{5,7},{7,5},{8,10},{10,8},{9,1... | collective-permute-start | bytes 135176 | tf_op jit(solution)/shard_map/ppermute | solution.py:450
  30.1 6.6 %collective-permute-start.8 = (bf16[32,704]{1,0:T(8,128)(2,1)S(1)}, bf16[32,704]{1,0:T(8,128)(2,1)S(1)}, u32[]{:S(2)}, u32[]{:S(2)}) collective-permute-start(bf16[32,704]{1,0:T(8,128)(2,1)S(1)} %shard_map.77.refs_0_), channel_id=1, source_target_pairs={{12,0},{8,4},{4,8},{0,12},{13,1},{9,5},{5,9},{1,13},{14,2},{10,6},... | collective-permute-start | bytes 135176 | tf_op jit(solution)/shard_map/ppermute | solution.py:456
  34.4 5.0 %collective-permute-start.7 = (bf16[32,704]{1,0:T(8,128)(2,1)S(1)}, bf16[32,704]{1,0:T(8,128)(2,1)S(1)}, u32[]{:S(2)}, u32[]{:S(2)}) collective-permute-start(bf16[32,704]{1,0:T(8,128)(2,1)S(1)} %shard_map.77.refs_0_), channel_id=1, source_target_pairs={{8,0},{12,4},{0,8},{4,12},{9,1},{13,5},{1,9},{5,13},{10,2},{14,6},... | collective-permute-start | bytes 135176 | tf_op jit(solution)/shard_map/ppermute | solution.py:456
  34.4 5.0 %collective-permute-start.6 = (bf16[32,704]{1,0:T(8,128)(2,1)S(1)}, bf16[32,704]{1,0:T(8,128)(2,1)S(1)}, u32[]{:S(2)}, u32[]{:S(2)}) collective-permute-start(bf16[32,704]{1,0:T(8,128)(2,1)S(1)} %shard_map.77.refs_0_), channel_id=1, source_target_pairs={{4,0},{0,4},{12,8},{8,12},{5,1},{1,5},{13,9},{9,13},{6,2},{2,6},{1... | collective-permute-start | bytes 135176 | tf_op jit(solution)/shard_map/ppermute | solution.py:456
  40.0 1.2 %collective-permute-start.9 = (bf16[32,704]{1,0:T(8,128)(2,1)S(1)}, bf16[32,704]{1,0:T(8,128)(2,1)S(1)}, u32[]{:S(2)}, u32[]{:S(2)}) collective-permute-start(bf16[32,704]{1,0:T(8,128)(2,1)S(1)} %get-tuple-element.49.refs_0_), channel_id=1, source_target_pairs={{0,1},{1,0},{2,3},{3,2},{4,5},{5,4},{6,7},{7,6},{8,9},{9,8},{10,11... | collective-permute-start | bytes 135176 | tf_op jit(solution)/shard_map/ppermute | solution.py:453
  40.0 4.2 %collective-permute-start.10 = (bf16[32,704]{1,0:T(8,128)(2,1)S(1)}, bf16[32,704]{1,0:T(8,128)(2,1)S(1)}, u32[]{:S(2)}, u32[]{:S(2)}) collective-permute-start(bf16[32,704]{1,0:T(8,128)(2,1)S(1)} %get-tuple-element.49.refs_0_), channel_id=1, source_target_pairs={{0,2},{2,0},{1,3},{3,1},{4,6},{6,4},{5,7},{7,5},{8,10},{10,8},{9,1... | collective-permute-start | bytes 135176 | tf_op jit(solution)/shard_map/ppermute | solution.py:450
  44.2 1.2 %collective-permute-start.11 = (bf16[32,704]{1,0:T(8,128)(2,1)S(1)}, bf16[32,704]{1,0:T(8,128)(2,1)S(1)}, u32[]{:S(2)}, u32[]{:S(2)}) collective-permute-start(bf16[32,704]{1,0:T(8,128)(2,1)S(1)} %collective-permute-done.10.refs_2_), channel_id=1, source_target_pairs={{0,1},{1,0},{2,3},{3,2},{4,5},{5,4},{6,7},{7,6},{8,9},{9,8},{10,11... | collective-permute-start | bytes 135176 | tf_op jit(solution)/shard_map/ppermute | solution.py:453
  47.6 2.3 %collective-permute-start.12 = (f32[32,672]{1,0:T(8,128)S(1)}, f32[32,672]{1,0:T(8,128)S(1)}, u32[]{:S(2)}, u32[]{:S(2)}) collective-permute-start(f32[32,672]{1,0:T(8,128)S(1)} %get-tuple-element.55), channel_id=1, source_target_pairs={{0,1},{1,0},{2,3},{3,2},{4,5},{5,4},{6,7},{7,6},{8,9},{9,8},{10,11... | collective-permute-start | bytes 258056 | tf_op jit(solution)/shard_map/ppermute | solution.py:453
  49.4 1.6 %collective-permute-start.13 = (f32[32,640]{1,0:T(8,128)S(1)}, f32[32,640]{1,0:T(8,128)S(1)}, u32[]{:S(2)}, u32[]{:S(2)}) collective-permute-start(f32[32,640]{1,0:T(8,128)S(1)} %get-tuple-element.58), channel_id=1, source_target_pairs={{0,1},{1,0},{2,3},{3,2},{4,5},{5,4},{6,7},{7,6},{8,9},{9,8},{10,11... | collective-permute-start | bytes 245768 | tf_op jit(solution)/shard_map/ppermute | solution.py:453
  49.9 4.1 %collective-permute-start.14 = (bf16[32,704]{1,0:T(8,128)(2,1)S(1)}, bf16[32,704]{1,0:T(8,128)(2,1)S(1)}, u32[]{:S(2)}, u32[]{:S(2)}) collective-permute-start(bf16[32,704]{1,0:T(8,128)(2,1)S(1)} %get-tuple-element.56.refs_0_), channel_id=1, source_target_pairs={{0,2},{2,0},{1,3},{3,1},{4,6},{6,4},{5,7},{7,5},{8,10},{10,8},{9,1... | collective-permute-start | bytes 135176 | tf_op jit(solution)/shard_map/ppermute | solution.py:450
  54.2 9.8 %collective-permute-start.15 = (f32[32,2048]{1,0:T(8,128)S(1)}, f32[32,2048]{1,0:T(8,128)S(1)}, u32[]{:S(2)}, u32[]{:S(2)}) collective-permute-start(f32[32,2048]{1,0:T(8,128)S(1)} %get-tuple-element.59.h_ref.refs_0_), channel_id=1, source_target_pairs={{0,2},{2,0},{1,3},{3,1},{4,6},{6,4},{5,7},{7,5},{8,10},{10,8},{9,1... | collective-permute-start | bytes 786440 | tf_op jit(solution)/shard_map/ppermute | solution.py:450
  54.4 5.9 %collective-permute-start.18 = (bf16[32,704]{1,0:T(8,128)(2,1)S(1)}, bf16[32,704]{1,0:T(8,128)(2,1)S(1)}, u32[]{:S(2)}, u32[]{:S(2)}) collective-permute-start(bf16[32,704]{1,0:T(8,128)(2,1)S(1)} %shard_map.84.refs_0_), channel_id=1, source_target_pairs={{12,0},{8,4},{4,8},{0,12},{13,1},{9,5},{5,9},{1,13},{14,2},{10,6},... | collective-permute-start | bytes 135176 | tf_op jit(solution)/shard_map/ppermute | solution.py:456
  56.1 5.5 %collective-permute-start.17 = (bf16[32,704]{1,0:T(8,128)(2,1)S(1)}, bf16[32,704]{1,0:T(8,128)(2,1)S(1)}, u32[]{:S(2)}, u32[]{:S(2)}) collective-permute-start(bf16[32,704]{1,0:T(8,128)(2,1)S(1)} %shard_map.84.refs_0_), channel_id=1, source_target_pairs={{8,0},{12,4},{0,8},{4,12},{9,1},{13,5},{1,9},{5,13},{10,2},{14,6},... | collective-permute-start | bytes 135176 | tf_op jit(solution)/shard_map/ppermute | solution.py:456
  56.5 5.1 %collective-permute-start.16 = (bf16[32,704]{1,0:T(8,128)(2,1)S(1)}, bf16[32,704]{1,0:T(8,128)(2,1)S(1)}, u32[]{:S(2)}, u32[]{:S(2)}) collective-permute-start(bf16[32,704]{1,0:T(8,128)(2,1)S(1)} %shard_map.84.refs_0_), channel_id=1, source_target_pairs={{4,0},{0,4},{12,8},{8,12},{5,1},{1,5},{13,9},{9,13},{6,2},{2,6},{1... | collective-permute-start | bytes 135176 | tf_op jit(solution)/shard_map/ppermute | solution.py:456
  62.5 1.5 %collective-permute-start.19 = (f32[32,1280]{1,0:T(8,128)S(1)}, f32[32,1280]{1,0:T(8,128)S(1)}, u32[]{:S(2)}, u32[]{:S(2)}) collective-permute-start(f32[32,1280]{1,0:T(8,128)S(1)} %shard_map.85.refs_2_), channel_id=1, source_target_pairs={{0,1},{1,0},{2,3},{3,2},{4,5},{5,4},{6,7},{7,6},{8,9},{9,8},{10,11... | collective-permute-start | bytes 491528 | tf_op jit(solution)/shard_map/ppermute | solution.py:453

commit v8 on v7

--- a/solution.py
+++ b/solution.py
@@ -13,7 +13,7 @@
 NF = 40
 TAPS = 128
 HALF = TAPS // 2
-GROUP = 4
+GROUP = 8
 GROUPS = NF // GROUP
 F32 = jnp.float32
 BF16 = jnp.bfloat16
@@ -127,14 +127,14 @@
         num_ref[:, 2 * TAPS * pair : 2 * TAPS * (pair + 1)] = functools.reduce(jnp.add, terms)
 
 
-def crossed(low, s_ref, x, core, subs, cl):
+def crossed(low, s_ref, places, subs, cl):
     count = NF // subs
-    span = pl.ds(core * count, count)
-    acc = jnp.zeros((low.shape[0], count * cl), F32)
+    acc = jnp.zeros((low.shape[0], len(places) * count * cl), F32)
     for pair in range(low.shape[1] // (2 * TAPS)):
         cols = slice(2 * TAPS * pair, 2 * TAPS * (pair + 1))
+        parts = [pair_rows(s_ref, pl.ds(core * count, count), pair, x, cl) for x, core in places]
         acc = acc + lax.dot_general(
-            low[:, cols], pair_rows(s_ref, span, pair, x, cl), NT, preferred_element_type=F32
+            low[:, cols], jnp.concatenate(parts, axis=0), NT, preferred_element_type=F32
         )
     return acc
 
@@ -151,17 +151,19 @@
     size = NF // subs * cl
     x_me, c_me = lax.axis_index("row"), lax.axis_index("sub")
     for ref, (dx, dc) in zip(msg_refs, others_of(rows, subs)):
-        ref[:, :size] = crossed(
-            new.astype(BF16), s_ref, lax.rem(x_me + dx, rows), lax.rem(c_me + dc, subs), subs, cl
-        )
+        target = (lax.rem(x_me + dx, rows), lax.rem(c_me + dc, subs))
+        ref[:, :size] = crossed(new.astype(BF16), s_ref, [target], subs, cl)
         ref[:, size:] = h_gram
 
 
 def products_kernel(places, rows, subs, cl, h_ref, s_ref, *refs):
     x_me, c_me = lax.axis_index("row"), lax.axis_index("sub")
     low = h_ref[...].astype(BF16)
-    for ref, (dx, dc) in zip(refs[len(refs) - len(places) :], places):
-        ref[...] = crossed(low, s_ref, lax.rem(x_me + dx, rows), lax.rem(c_me + dc, subs), subs, cl)
+    targets = [(lax.rem(x_me + dx, rows), lax.rem(c_me + dc, subs)) for dx, dc in places]
+    acc = crossed(low, s_ref, targets, subs, cl)
+    size = acc.shape[1] // len(places)
+    for at, ref in enumerate(refs[len(refs) - len(places) :]):
+        ref[...] = acc[:, at * size : (at + 1) * size]
 
 
 def place_signal(source, target, rows, frames):
@@ -383,8 +385,8 @@
             out_ref[...] = moved[:rank] + (moved[rank : 2 * rank] + moved[2 * rank :])
 
 
-def join_kernel(rows, subs, *refs):
-    act_refs, parts, (syn_ref, out_ref, scr, sems) = refs[:rows], refs[rows : rows + subs], refs[rows + subs :]
+def join_kernel(rows, *refs):
+    act_refs, (out_ref, sems) = refs[:rows], refs[rows:]
     frames = act_refs[0].shape[1]
     x_me = lax.axis_index("row")
     copies = []
@@ -393,14 +395,19 @@
         copies.append(pltpu.make_async_copy(act_refs[shift], out_ref.at[:, pl.ds(begin, frames)], sems.at[shift]))
     for copy in copies:
         copy.start()
+    for copy in copies:
+        copy.wait()
+
+
+def sum_kernel(*refs):
+    parts, (out_ref, scr, sem) = refs[:-3], refs[-3:]
     total = parts[0][...]
     for part in parts[1:]:
         total = total + part[...]
     scr[...] = total
-    copies.append(pltpu.make_async_copy(scr, syn_ref, sems.at[rows]))
-    copies[-1].start()
-    for copy in copies:
-        copy.wait()
+    copy = pltpu.make_async_copy(scr, out_ref, sem)
+    copy.start()
+    copy.wait()
 
 
 def call(kernel, args, outs, scratch=(), in_specs=None, out_specs=None, limit=4, cost=None, aliases=None):
@@ -587,13 +594,20 @@
     (part,) = call(
         functools.partial(last_kernel, frms), [w_piece, order] + parts, [((rank, NF * cl), F32)], piled
     )
-    synergies, wide = call(
-        functools.partial(join_kernel, rows, subs),
-        sides + [part] + [sub_shift(part, dc) for dc in range(1, subs)],
-        [pltpu.HBM((rank, NF * cl), F32), pltpu.HBM((rank, window), F32)],
-        [pltpu.VMEM((rank, NF * cl), F32), pltpu.SemaphoreType.DMA((rows + 1,))],
-        in_specs=[anywhere] * rows + [whole] * subs,
-        out_specs=[anywhere] * 2,
+    (wide,) = call(
+        functools.partial(join_kernel, rows),
+        sides,
+        [pltpu.HBM((rank, window), F32)],
+        [pltpu.SemaphoreType.DMA((rows,))],
+        in_specs=[anywhere] * rows,
+        out_specs=[anywhere],
+    )
+    (synergies,) = call(
+        sum_kernel,
+        [part] + [sub_shift(part, dc) for dc in range(1, subs)],
+        [pltpu.HBM((rank, NF * cl), F32)],
+        [pltpu.VMEM((rank, NF * cl), F32), pltpu.SemaphoreType.DMA],
+        out_specs=[anywhere],
     )
     return (synergies.T, wide)
 

time: 65 us -> 64.1 us (0.986)
  Pallas kernels: 26.3 us -> 25.3 us
    pallas_call x19 -> x20, Pallas kernels: 26.3 us -> 25.3 us  [call(): pl.pallas_call(kernel, out_shape=[jax.ShapeDtypeStruct(*out) if isinstanc...]
  transfers between devices with their start and end apart: 20 -> 20, of which waited for: 10 -> 10; matrix products, arithmetic and copies ran while one was open for 0% -> 0% of each run, Pallas kernels for 28% -> 27%
where the time goes in v8:
time: 64.1 us; the launch traced here: 63.9 us
  Pallas kernels  25.3 us (39%)
  starting transfers between devices  19.6 us (31%)
  waiting for transfers between devices  18.2 us (28%)
  between operations  0.8 us (1%)
    pallas_call x20, Pallas kernels, call(): pl.pallas_call(kernel, out_shape=[jax.ShapeDtypeStruct(*out) if isinstanc...  25.3 us
    ppermute x6, starting transfers between devices, frm_shift(): lax.ppermute(value, 'frm', [(partner(i, shift, frms), i) for i in range(f...  9.37 us
    ppermute x6, waiting for transfers between devices, row_shift(): lax.ppermute(value, 'row', [(i, (i + shift) % rows) for i in range(rows)])  7.37 us
    ppermute x6, waiting for transfers between devices, frm_shift(): lax.ppermute(value, 'frm', [(partner(i, shift, frms), i) for i in range(f...  7.15 us
    ppermute x6, starting transfers between devices, row_shift(): lax.ppermute(value, 'row', [(i, (i + shift) % rows) for i in range(rows)])  6.99 us
    ppermute x7, waiting for transfers between devices, sub_shift(): lax.ppermute(value, 'sub', [(i, (i + shift) % subs) for i in range(subs)])  3.71 us
    ppermute x7, starting transfers between devices, sub_shift(): lax.ppermute(value, 'sub', [(i, (i + shift) % subs) for i in range(subs)])  2.55 us
  transfers between devices with their start and end apart: 20, of which 10 were waited for; matrix products, arithmetic and copies ran while one was open for 0% of the time, Pallas kernels for 27%

profile of v8, /device:TPU:0, one launch (start us, length us, event | category | flops | bytes accessed | tf_op | source)
XLA Modules:
  0.0 63.9 jit_solution(12497516644525071398)
XLA Ops:
  0.6 1.0 %shard_map.68 = (bf16[32,2176]{1,0:T(8,128)(2,1)S(1)}, bf16[32,2176]{1,0:T(8,128)(2,1)S(1)}) custom-call(bf16[32,4096]{1,0:T(8,128)(2,1)} %sig_hbm.1), custom_call_target="tpu_custom_call" | custom-call | tf_op jit(solution)/shard_map/pallas_call | solution.py:417
  1.7 3.0 %collective-permute-start = (bf16[32,2176]{1,0:T(8,128)(2,1)S(1)}, bf16[32,2176]{1,0:T(8,128)(2,1)S(1)}, u32[]{:S(2)}, u32[]{:S(2)}) collective-permute-start(bf16[32,2176]{1,0:T(8,128)(2,1)S(1)} %get-tuple-element.34), channel_id=1, source_target_pairs={{0,2},{2,0},{1,3},{3,1},{4,6},{6,4},{5,7},{7,5},{8,10},{10,8},{9,1... | collective-permute-start | bytes 417800 | tf_op jit(solution)/shard_map/ppermute | solution.py:457
  4.7 4.7 %shard_map.69 = (bf16[40,16,2,32,128]{4,3,2,1,0:T(8,128)(2,1)S(1)}, f32[32,1280]{1,0:T(8,128)S(1)}, f32[32,2048]{1,0:T(8,128)S(1)}, bf16[1280,1280]{1,0:T(8,128)(2,1)S(1)}, bf16[40,256,256]{2,1,0:T(8,128)(2,1)S(1)}) custom-call(bf16[32,2176]{1,0:T(8,128)(2,1)S(1)} %get-tuple-element.31.sig_ref.refs_0_, f32[32,1280]{1,0:T(8,128)} %bitcast.3, ...), custom_call_target="tpu_custom_call" | custom-call | flops 2684354560 | tf_op jit(solution)/shard_map/pallas_call | solution.py:417
  9.4 0.0 collective-permute-done.refs_0_.refs_1_
  9.4 0.7 %collective-permute-start.2 = (bf16[64,128]{1,0:T(8,128)(2,1)S(1)}, bf16[64,128]{1,0:T(8,128)(2,1)S(1)}, u32[]{:S(2)}, u32[]{:S(2)}) collective-permute-start(bf16[64,128]{1,0:T(8,128)(2,1)S(1)} %shard_map.70.refs_0_), channel_id=1, source_target_pairs={{2,1},{3,4},{6,5},{7,8},{10,9},{11,12},{14,13},{1,2},{4,3},{5,6},{... | collective-permute-start | bytes 49160 | tf_op jit(solution)/shard_map/ppermute | solution.py:509
  10.1 0.8 %shard_map.71 = (f32[32,640]{1,0:T(8,128)S(1)}, bf16[32,1344]{1,0:T(8,128)(2,1)S(1)}) custom-call(f32[32,1280]{1,0:T(8,128)S(1)} %get-tuple-element.32.w_ref, bf16[1280,1280]{1,0:T(8,128)(2,1)S(1)} %get-tuple-element.33.order_ref, bf16[64,128]{1,0:T(8,128)(2,1)S(1)} %shard_map.70.refs_0_), custom_call_target="tpu_custom_call" | custom-call | tf_op jit(solution)/shard_map/pallas_call | solution.py:417
  11.0 2.4 %collective-permute-start.1 = (bf16[32,1344]{1,0:T(8,128)(2,1)S(1)}, bf16[32,1344]{1,0:T(8,128)(2,1)S(1)}, u32[]{:S(2)}, u32[]{:S(2)}) collective-permute-start(bf16[32,1344]{1,0:T(8,128)(2,1)S(1)} %get-tuple-element.37.refs_0_), channel_id=1, source_target_pairs={{0,2},{2,0},{1,3},{3,1},{4,6},{6,4},{5,7},{7,5},{8,10},{10,8},{9,1... | collective-permute-start | bytes 258056 | tf_op jit(solution)/shard_map/ppermute | solution.py:457
  13.4 0.0 collective-permute-done.2.halo_ref
  13.4 4.1 %shard_map.72.refs_3_.s_ref.refs_2_.refs_6_ = bf16[40,16,2,32,128]{4,3,2,1,0:T(8,128)(2,1)S(1)} custom-call(bf16[64,128]{1,0:T(8,128)(2,1)S(1)} %collective-permute-done.2.halo_ref, bf16[40,256,256]{2,1,0:T(8,128)(2,1)S(1)} %get-tuple-element.39.tab_ref, bf16[32,2176]{1,0:T(8,128)(2,1)S(1)} %get-tuple-element.31.sig_ref.refs_0_, ...), custom_call_target="tpu_custom_call", output_to_operand_aliasing={{}: (4, {})} | custom-call | flops 5368709120 | tf_op jit(solution)/shard_map/pallas_call | solution.py:417
  17.5 0.0 collective-permute-done.1.refs_1_
  17.6 3.0 %shard_map.73 = (f32[32,2048]{1,0:T(8,128)S(1)}, f32[32,32]{1,0:T(8,128)S(1)}, f32[32,672]{1,0:T(8,128)S(1)}) custom-call(bf16[32,1344]{1,0:T(8,128)(2,1)S(1)} %get-tuple-element.37.refs_0_, bf16[32,1344]{1,0:T(8,128)(2,1)S(1)} %collective-permute-done.1.refs_1_, f32[32,2048]{1,0:T(8,128)S(1)} %get-tuple-element.38.refs_2_, ...), custom_call_target="tpu_custom_call" | custom-call | tf_op jit(solution)/shard_map/pallas_call | solution.py:417
  20.6 1.8 %collective-permute-start.3 = (f32[32,672]{1,0:T(8,128)S(1)}, f32[32,672]{1,0:T(8,128)S(1)}, u32[]{:S(2)}, u32[]{:S(2)}) collective-permute-start(f32[32,672]{1,0:T(8,128)S(1)} %get-tuple-element.43), channel_id=1, source_target_pairs={{0,1},{1,0},{2,3},{3,2},{4,5},{5,4},{6,7},{7,6},{8,9},{9,8},{10,11... | collective-permute-start | bytes 258056 | tf_op jit(solution)/shard_map/ppermute | solution.py:460
  22.4 1.6 %shard_map.74 = (f32[32,640]{1,0:T(8,128)S(1)}, f32[32,640]{1,0:T(8,128)S(1)}) custom-call(f32[32,2048]{1,0:T(8,128)S(1)} %get-tuple-element.40.h_ref.refs_5_, bf16[40,16,2,32,128]{4,3,2,1,0:T(8,128)(2,1)S(1)} %shard_map.72.refs_3_.s_ref.refs_2_.refs_6_), custom_call_target="tpu_custom_call" | custom-call | flops 1342177280 | tf_op jit(solution)/shard_map/pallas_call | solution.py:417
  24.0 0.1 collective-permute-start.4
  24.1 0.0 collective-permute-done.3.refs_2_
  24.1 0.1 shard_map.75
  24.1 0.8 %collective-permute-start.5 = (bf16[32,704]{1,0:T(8,128)(2,1)S(1)}, bf16[32,704]{1,0:T(8,128)(2,1)S(1)}, u32[]{:S(2)}, u32[]{:S(2)}) collective-permute-start(bf16[32,704]{1,0:T(8,128)(2,1)S(1)} %get-tuple-element.44.refs_0_), channel_id=1, source_target_pairs={{0,2},{2,0},{1,3},{3,1},{4,6},{6,4},{5,7},{7,5},{8,10},{10,8},{9,1... | collective-permute-start | bytes 135176 | tf_op jit(solution)/shard_map/ppermute | solution.py:457
  25.0 0.8 %shard_map.76.own_ref = f32[32,640]{1,0:T(8,128)S(1)} custom-call(f32[32,2048]{1,0:T(8,128)S(1)} %get-tuple-element.40.h_ref.refs_5_, bf16[40,16,2,32,128]{4,3,2,1,0:T(8,128)(2,1)S(1)} %shard_map.72.refs_3_.s_ref.refs_2_.refs_6_, bf16[32,704]{1,0:T(8,128)(2,1)S(1)} %get-tuple-element.44.refs_0_), custom_call_target="tpu_custom_call" | custom-call | flops 1 | tf_op jit(solution)/shard_map/pallas_call | solution.py:417
  25.8 0.0 collective-permute-done.4.refs_0_
  25.8 2.5 %collective-permute-done.5.refs_1_ = bf16[32,704]{1,0:T(8,128)(2,1)S(1)} collective-permute-done((bf16[32,704]{1,0:T(8,128)(2,1)S(1)}, bf16[32,704]{1,0:T(8,128)(2,1)S(1)}, u32[]{:S(2)}, u32[]{:S(2)}) %collective-permute-start.5) | collective-permute-done | bytes 45088 | tf_op jit(solution)/shard_map/ppermute | solution.py:457
  28.3 0.2 shard_map.77.refs_0_
  28.4 4.3 %collective-permute-start.8 = (bf16[32,704]{1,0:T(8,128)(2,1)S(1)}, bf16[32,704]{1,0:T(8,128)(2,1)S(1)}, u32[]{:S(2)}, u32[]{:S(2)}) collective-permute-start(bf16[32,704]{1,0:T(8,128)(2,1)S(1)} %shard_map.77.refs_0_), channel_id=1, source_target_pairs={{12,0},{8,4},{4,8},{0,12},{13,1},{9,5},{5,9},{1,13},{14,2},{10,6},... | collective-permute-start | bytes 135176 | tf_op jit(solution)/shard_map/ppermute | solution.py:463
  32.8 0.0 collective-permute-start.7
  32.8 0.6 collective-permute-start.6
  33.4 1.6 %collective-permute-done.8.refs_3_ = bf16[32,704]{1,0:T(8,128)(2,1)S(1)} collective-permute-done((bf16[32,704]{1,0:T(8,128)(2,1)S(1)}, bf16[32,704]{1,0:T(8,128)(2,1)S(1)}, u32[]{:S(2)}, u32[]{:S(2)}) %collective-permute-start.8) | collective-permute-done | bytes 45088 | tf_op jit(solution)/shard_map/ppermute | solution.py:463
  35.0 2.7 %collective-permute-done.7.refs_2_ = bf16[32,704]{1,0:T(8,128)(2,1)S(1)} collective-permute-done((bf16[32,704]{1,0:T(8,128)(2,1)S(1)}, bf16[32,704]{1,0:T(8,128)(2,1)S(1)}, u32[]{:S(2)}, u32[]{:S(2)}) %collective-permute-start.7) | collective-permute-done | bytes 45088 | tf_op jit(solution)/shard_map/ppermute | solution.py:463
  37.8 0.0 collective-permute-done.6.refs_1_
  37.8 0.6 shard_map.78
  38.4 0.0 collective-permute-start.9
  38.4 0.1 collective-permute-start.10
  38.5 1.1 %collective-permute-done.9.refs_1_ = bf16[32,704]{1,0:T(8,128)(2,1)S(1)} collective-permute-done((bf16[32,704]{1,0:T(8,128)(2,1)S(1)}, bf16[32,704]{1,0:T(8,128)(2,1)S(1)}, u32[]{:S(2)}, u32[]{:S(2)}) %collective-permute-start.9) | collective-permute-done | bytes 45088 | tf_op jit(solution)/shard_map/ppermute | solution.py:460
  39.6 1.0 %shard_map.79.refs_4_ = f32[32,2048]{1,0:T(8,128)S(1)} custom-call(bf16[32,704]{1,0:T(8,128)(2,1)S(1)} %get-tuple-element.48.refs_0_, bf16[32,704]{1,0:T(8,128)(2,1)S(1)} %collective-permute-done.9.refs_1_, bf16[40,16,2,32,128]{4,3,2,1,0:T(8,128)(2,1)S(1)} %shard_map.72.refs_3_.s_ref.refs_2_.refs_6_), custom_call_target="tpu_custom_call" | custom-call | flops 1342177280 | tf_op jit(solution)/shard_map/pallas_call | solution.py:417
  40.6 1.9 %collective-permute-done.10.refs_2_ = bf16[32,704]{1,0:T(8,128)(2,1)S(1)} collective-permute-done((bf16[32,704]{1,0:T(8,128)(2,1)S(1)}, bf16[32,704]{1,0:T(8,128)(2,1)S(1)}, u32[]{:S(2)}, u32[]{:S(2)}) %collective-permute-start.10) | collective-permute-done | bytes 45088 | tf_op jit(solution)/shard_map/ppermute | solution.py:457
  42.6 0.0 collective-permute-start.11
  42.6 1.2 %collective-permute-done.11.refs_3_ = bf16[32,704]{1,0:T(8,128)(2,1)S(1)} collective-permute-done((bf16[32,704]{1,0:T(8,128)(2,1)S(1)}, bf16[32,704]{1,0:T(8,128)(2,1)S(1)}, u32[]{:S(2)}, u32[]{:S(2)}) %collective-permute-start.11) | collective-permute-done | bytes 45088 | tf_op jit(solution)/shard_map/ppermute | solution.py:460
  43.8 2.1 %shard_map.80 = (f32[32,2048]{1,0:T(8,128)S(1)}, f32[32,32]{1,0:T(8,128)S(1)}, f32[32,672]{1,0:T(8,128)S(1)}) custom-call(bf16[32,704]{1,0:T(8,128)(2,1)S(1)} %get-tuple-element.48.refs_0_, bf16[32,704]{1,0:T(8,128)(2,1)S(1)} %collective-permute-done.9.refs_1_, bf16[32,704]{1,0:T(8,128)(2,1)S(1)} %collective-permute-done.10.refs_2_, ...), custom_call_target="tpu_custom_call" | custom-call | tf_op jit(solution)/shard_map/pallas_call | solution.py:417
  45.9 0.2 collective-permute-start.12
  46.2 1.6 %shard_map.81 = (f32[32,640]{1,0:T(8,128)S(1)}, f32[32,640]{1,0:T(8,128)S(1)}) custom-call(f32[32,2048]{1,0:T(8,128)S(1)} %get-tuple-element.59.h_ref.refs_0_, bf16[40,16,2,32,128]{4,3,2,1,0:T(8,128)(2,1)S(1)} %shard_map.72.refs_3_.s_ref.refs_2_.refs_6_), custom_call_target="tpu_custom_call" | custom-call | flops 1342177280 | tf_op jit(solution)/shard_map/pallas_call | solution.py:417
  47.8 0.4 collective-permute-start.13
  48.2 0.0 collective-permute-done.12.refs_2_
  48.2 0.1 shard_map.82
  48.3 0.3 collective-permute-start.14
  48.6 0.8 %shard_map.83.own_ref = f32[32,640]{1,0:T(8,128)S(1)} custom-call(f32[32,2048]{1,0:T(8,128)S(1)} %get-tuple-element.59.h_ref.refs_0_, bf16[40,16,2,32,128]{4,3,2,1,0:T(8,128)(2,1)S(1)} %shard_map.72.refs_3_.s_ref.refs_2_.refs_6_, bf16[32,704]{1,0:T(8,128)(2,1)S(1)} %get-tuple-element.55.refs_0_), custom_call_target="tpu_custom_call" | custom-call | flops 1 | tf_op jit(solution)/shard_map/pallas_call | solution.py:417
  49.4 0.0 collective-permute-done.13.refs_0_
  49.4 3.0 %collective-permute-done.14.refs_1_ = bf16[32,704]{1,0:T(8,128)(2,1)S(1)} collective-permute-done((bf16[32,704]{1,0:T(8,128)(2,1)S(1)}, bf16[32,704]{1,0:T(8,128)(2,1)S(1)}, u32[]{:S(2)}, u32[]{:S(2)}) %collective-permute-start.14) | collective-permute-done | bytes 45088 | tf_op jit(solution)/shard_map/ppermute | solution.py:457
  52.4 0.2 shard_map.84.refs_0_
  52.5 0.3 collective-permute-start.19
  52.8 1.7 %collective-permute-start.17 = (bf16[32,704]{1,0:T(8,128)(2,1)S(1)}, bf16[32,704]{1,0:T(8,128)(2,1)S(1)}, u32[]{:S(2)}, u32[]{:S(2)}) collective-permute-start(bf16[32,704]{1,0:T(8,128)(2,1)S(1)} %shard_map.84.refs_0_), channel_id=1, source_target_pairs={{12,0},{8,4},{4,8},{0,12},{13,1},{9,5},{5,9},{1,13},{14,2},{10,6},... | collective-permute-start | bytes 135176 | tf_op jit(solution)/shard_map/ppermute | solution.py:463
  54.5 0.4 collective-permute-start.16
  54.8 2.4 %collective-permute-start.15 = (bf16[32,704]{1,0:T(8,128)(2,1)S(1)}, bf16[32,704]{1,0:T(8,128)(2,1)S(1)}, u32[]{:S(2)}, u32[]{:S(2)}) collective-permute-start(bf16[32,704]{1,0:T(8,128)(2,1)S(1)} %shard_map.84.refs_0_), channel_id=1, source_target_pairs={{4,0},{0,4},{12,8},{8,12},{5,1},{1,5},{13,9},{9,13},{6,2},{2,6},{1... | collective-permute-start | bytes 135176 | tf_op jit(solution)/shard_map/ppermute | solution.py:463
  57.2 1.5 %collective-permute-done.17.refs_3_ = bf16[32,704]{1,0:T(8,128)(2,1)S(1)} collective-permute-done((bf16[32,704]{1,0:T(8,128)(2,1)S(1)}, bf16[32,704]{1,0:T(8,128)(2,1)S(1)}, u32[]{:S(2)}, u32[]{:S(2)}) %collective-permute-start.17) | collective-permute-done | bytes 45088 | tf_op jit(solution)/shard_map/ppermute | solution.py:463
  58.7 1.3 %collective-permute-done.16.refs_2_ = bf16[32,704]{1,0:T(8,128)(2,1)S(1)} collective-permute-done((bf16[32,704]{1,0:T(8,128)(2,1)S(1)}, bf16[32,704]{1,0:T(8,128)(2,1)S(1)}, u32[]{:S(2)}, u32[]{:S(2)}) %collective-permute-start.16) | collective-permute-done | bytes 45088 | tf_op jit(solution)/shard_map/ppermute | solution.py:463
  60.0 0.0 collective-permute-done.15.refs_1_
  60.0 0.9 %shard_map.85.refs_0_ = f32[32,1280]{1,0:T(8,128)S(1)} custom-call(f32[32,640]{1,0:T(8,128)S(1)} %get-tuple-element.47.w_ref, bf16[1280,1280]{1,0:T(8,128)(2,1)S(1)} %get-tuple-element.33.order_ref, bf16[32,704]{1,0:T(8,128)(2,1)S(1)} %shard_map.84.refs_0_, bf16[32,704]{1,0:T(8,128)(2,1)S(1)} %collective-permute-done.15.refs_1_, ...), custom_call_target="tpu_custom_call" | custom-call | tf_op jit(solution)/shard_map/pallas_call | solution.py:417
  60.9 0.1 collective-permute-start.18
  61.0 1.4 %collective-permute-done.18.refs_1_ = f32[32,1280]{1,0:T(8,128)S(1)} collective-permute-done((f32[32,1280]{1,0:T(8,128)S(1)}, f32[32,1280]{1,0:T(8,128)S(1)}, u32[]{:S(2)}, u32[]{:S(2)}) %collective-permute-start.18) | collective-permute-done | bytes 163872 | tf_op jit(solution)/shard_map/ppermute | solution.py:460
  62.4 0.7 %shard_map.86 = f32[32,1280]{1,0:T(8,128)} custom-call(f32[32,1280]{1,0:T(8,128)S(1)} %shard_map.85.refs_0_, f32[32,1280]{1,0:T(8,128)S(1)} %collective-permute-done.18.refs_1_), custom_call_target="tpu_custom_call" | custom-call | tf_op jit(solution)/shard_map/pallas_call | solution.py:417
  63.1 0.0 collective-permute-done.19.refs_1_
  63.1 0.8 %shard_map.87 = f32[32,4096]{1,0:T(8,128)} custom-call(f32[32,2048]{1,0:T(8,128)S(1)} %get-tuple-element.59.h_ref.refs_0_, f32[32,2048]{1,0:T(8,128)S(1)} %collective-permute-done.19.refs_1_), custom_call_target="tpu_custom_call" | custom-call | tf_op jit(solution)/shard_map/pallas_call | solution.py:417
  (1 shorter events, 0.0 us)
Async XLA Ops:
  1.7 7.8 %collective-permute-start = (bf16[32,2176]{1,0:T(8,128)(2,1)S(1)}, bf16[32,2176]{1,0:T(8,128)(2,1)S(1)}, u32[]{:S(2)}, u32[]{:S(2)}) collective-permute-start(bf16[32,2176]{1,0:T(8,128)(2,1)S(1)} %get-tuple-element.34), channel_id=1, source_target_pairs={{0,2},{2,0},{1,3},{3,1},{4,6},{6,4},{5,7},{7,5},{8,10},{10,8},{9,1... | collective-permute-start | bytes 417800 | tf_op jit(solution)/shard_map/ppermute | solution.py:457
  9.4 4.0 %collective-permute-start.2 = (bf16[64,128]{1,0:T(8,128)(2,1)S(1)}, bf16[64,128]{1,0:T(8,128)(2,1)S(1)}, u32[]{:S(2)}, u32[]{:S(2)}) collective-permute-start(bf16[64,128]{1,0:T(8,128)(2,1)S(1)} %shard_map.70.refs_0_), channel_id=1, source_target_pairs={{2,1},{3,4},{6,5},{7,8},{10,9},{11,12},{14,13},{1,2},{4,3},{5,6},{... | collective-permute-start | bytes 49160 | tf_op jit(solution)/shard_map/ppermute | solution.py:509
  11.0 6.6 %collective-permute-start.1 = (bf16[32,1344]{1,0:T(8,128)(2,1)S(1)}, bf16[32,1344]{1,0:T(8,128)(2,1)S(1)}, u32[]{:S(2)}, u32[]{:S(2)}) collective-permute-start(bf16[32,1344]{1,0:T(8,128)(2,1)S(1)} %get-tuple-element.37.refs_0_), channel_id=1, source_target_pairs={{0,2},{2,0},{1,3},{3,1},{4,6},{6,4},{5,7},{7,5},{8,10},{10,8},{9,1... | collective-permute-start | bytes 258056 | tf_op jit(solution)/shard_map/ppermute | solution.py:457
  20.6 3.5 %collective-permute-start.3 = (f32[32,672]{1,0:T(8,128)S(1)}, f32[32,672]{1,0:T(8,128)S(1)}, u32[]{:S(2)}, u32[]{:S(2)}) collective-permute-start(f32[32,672]{1,0:T(8,128)S(1)} %get-tuple-element.43), channel_id=1, source_target_pairs={{0,1},{1,0},{2,3},{3,2},{4,5},{5,4},{6,7},{7,6},{8,9},{9,8},{10,11... | collective-permute-start | bytes 258056 | tf_op jit(solution)/shard_map/ppermute | solution.py:460
  24.0 1.8 %collective-permute-start.4 = (f32[32,640]{1,0:T(8,128)S(1)}, f32[32,640]{1,0:T(8,128)S(1)}, u32[]{:S(2)}, u32[]{:S(2)}) collective-permute-start(f32[32,640]{1,0:T(8,128)S(1)} %get-tuple-element.46), channel_id=1, source_target_pairs={{0,1},{1,0},{2,3},{3,2},{4,5},{5,4},{6,7},{7,6},{8,9},{9,8},{10,11... | collective-permute-start | bytes 245768 | tf_op jit(solution)/shard_map/ppermute | solution.py:460
  24.1 4.1 %collective-permute-start.5 = (bf16[32,704]{1,0:T(8,128)(2,1)S(1)}, bf16[32,704]{1,0:T(8,128)(2,1)S(1)}, u32[]{:S(2)}, u32[]{:S(2)}) collective-permute-start(bf16[32,704]{1,0:T(8,128)(2,1)S(1)} %get-tuple-element.44.refs_0_), channel_id=1, source_target_pairs={{0,2},{2,0},{1,3},{3,1},{4,6},{6,4},{5,7},{7,5},{8,10},{10,8},{9,1... | collective-permute-start | bytes 135176 | tf_op jit(solution)/shard_map/ppermute | solution.py:457
  28.4 6.6 %collective-permute-start.8 = (bf16[32,704]{1,0:T(8,128)(2,1)S(1)}, bf16[32,704]{1,0:T(8,128)(2,1)S(1)}, u32[]{:S(2)}, u32[]{:S(2)}) collective-permute-start(bf16[32,704]{1,0:T(8,128)(2,1)S(1)} %shard_map.77.refs_0_), channel_id=1, source_target_pairs={{12,0},{8,4},{4,8},{0,12},{13,1},{9,5},{5,9},{1,13},{14,2},{10,6},... | collective-permute-start | bytes 135176 | tf_op jit(solution)/shard_map/ppermute | solution.py:463
  32.8 5.0 %collective-permute-start.7 = (bf16[32,704]{1,0:T(8,128)(2,1)S(1)}, bf16[32,704]{1,0:T(8,128)(2,1)S(1)}, u32[]{:S(2)}, u32[]{:S(2)}) collective-permute-start(bf16[32,704]{1,0:T(8,128)(2,1)S(1)} %shard_map.77.refs_0_), channel_id=1, source_target_pairs={{8,0},{12,4},{0,8},{4,12},{9,1},{13,5},{1,9},{5,13},{10,2},{14,6},... | collective-permute-start | bytes 135176 | tf_op jit(solution)/shard_map/ppermute | solution.py:463
  32.8 5.0 %collective-permute-start.6 = (bf16[32,704]{1,0:T(8,128)(2,1)S(1)}, bf16[32,704]{1,0:T(8,128)(2,1)S(1)}, u32[]{:S(2)}, u32[]{:S(2)}) collective-permute-start(bf16[32,704]{1,0:T(8,128)(2,1)S(1)} %shard_map.77.refs_0_), channel_id=1, source_target_pairs={{4,0},{0,4},{12,8},{8,12},{5,1},{1,5},{13,9},{9,13},{6,2},{2,6},{1... | collective-permute-start | bytes 135176 | tf_op jit(solution)/shard_map/ppermute | solution.py:463
  38.4 1.2 %collective-permute-start.9 = (bf16[32,704]{1,0:T(8,128)(2,1)S(1)}, bf16[32,704]{1,0:T(8,128)(2,1)S(1)}, u32[]{:S(2)}, u32[]{:S(2)}) collective-permute-start(bf16[32,704]{1,0:T(8,128)(2,1)S(1)} %get-tuple-element.48.refs_0_), channel_id=1, source_target_pairs={{0,1},{1,0},{2,3},{3,2},{4,5},{5,4},{6,7},{7,6},{8,9},{9,8},{10,11... | collective-permute-start | bytes 135176 | tf_op jit(solution)/shard_map/ppermute | solution.py:460
  38.4 4.2 %collective-permute-start.10 = (bf16[32,704]{1,0:T(8,128)(2,1)S(1)}, bf16[32,704]{1,0:T(8,128)(2,1)S(1)}, u32[]{:S(2)}, u32[]{:S(2)}) collective-permute-start(bf16[32,704]{1,0:T(8,128)(2,1)S(1)} %get-tuple-element.48.refs_0_), channel_id=1, source_target_pairs={{0,2},{2,0},{1,3},{3,1},{4,6},{6,4},{5,7},{7,5},{8,10},{10,8},{9,1... | collective-permute-start | bytes 135176 | tf_op jit(solution)/shard_map/ppermute | solution.py:457
  42.6 1.2 %collective-permute-start.11 = (bf16[32,704]{1,0:T(8,128)(2,1)S(1)}, bf16[32,704]{1,0:T(8,128)(2,1)S(1)}, u32[]{:S(2)}, u32[]{:S(2)}) collective-permute-start(bf16[32,704]{1,0:T(8,128)(2,1)S(1)} %collective-permute-done.10.refs_2_), channel_id=1, source_target_pairs={{0,1},{1,0},{2,3},{3,2},{4,5},{5,4},{6,7},{7,6},{8,9},{9,8},{10,11... | collective-permute-start | bytes 135176 | tf_op jit(solution)/shard_map/ppermute | solution.py:460
  45.9 2.2 %collective-permute-start.12 = (f32[32,672]{1,0:T(8,128)S(1)}, f32[32,672]{1,0:T(8,128)S(1)}, u32[]{:S(2)}, u32[]{:S(2)}) collective-permute-start(f32[32,672]{1,0:T(8,128)S(1)} %get-tuple-element.54), channel_id=1, source_target_pairs={{0,1},{1,0},{2,3},{3,2},{4,5},{5,4},{6,7},{7,6},{8,9},{9,8},{10,11... | collective-permute-start | bytes 258056 | tf_op jit(solution)/shard_map/ppermute | solution.py:460
  47.8 1.6 %collective-permute-start.13 = (f32[32,640]{1,0:T(8,128)S(1)}, f32[32,640]{1,0:T(8,128)S(1)}, u32[]{:S(2)}, u32[]{:S(2)}) collective-permute-start(f32[32,640]{1,0:T(8,128)S(1)} %get-tuple-element.57), channel_id=1, source_target_pairs={{0,1},{1,0},{2,3},{3,2},{4,5},{5,4},{6,7},{7,6},{8,9},{9,8},{10,11... | collective-permute-start | bytes 245768 | tf_op jit(solution)/shard_map/ppermute | solution.py:460
  48.3 4.1 %collective-permute-start.14 = (bf16[32,704]{1,0:T(8,128)(2,1)S(1)}, bf16[32,704]{1,0:T(8,128)(2,1)S(1)}, u32[]{:S(2)}, u32[]{:S(2)}) collective-permute-start(bf16[32,704]{1,0:T(8,128)(2,1)S(1)} %get-tuple-element.55.refs_0_), channel_id=1, source_target_pairs={{0,2},{2,0},{1,3},{3,1},{4,6},{6,4},{5,7},{7,5},{8,10},{10,8},{9,1... | collective-permute-start | bytes 135176 | tf_op jit(solution)/shard_map/ppermute | solution.py:457
  52.5 10.6 %collective-permute-start.19 = (f32[32,2048]{1,0:T(8,128)S(1)}, f32[32,2048]{1,0:T(8,128)S(1)}, u32[]{:S(2)}, u32[]{:S(2)}) collective-permute-start(f32[32,2048]{1,0:T(8,128)S(1)} %get-tuple-element.59.h_ref.refs_0_), channel_id=1, source_target_pairs={{0,2},{2,0},{1,3},{3,1},{4,6},{6,4},{5,7},{7,5},{8,10},{10,8},{9,1... | collective-permute-start | bytes 786440 | tf_op jit(solution)/shard_map/ppermute | solution.py:457
  52.8 5.9 %collective-permute-start.17 = (bf16[32,704]{1,0:T(8,128)(2,1)S(1)}, bf16[32,704]{1,0:T(8,128)(2,1)S(1)}, u32[]{:S(2)}, u32[]{:S(2)}) collective-permute-start(bf16[32,704]{1,0:T(8,128)(2,1)S(1)} %shard_map.84.refs_0_), channel_id=1, source_target_pairs={{12,0},{8,4},{4,8},{0,12},{13,1},{9,5},{5,9},{1,13},{14,2},{10,6},... | collective-permute-start | bytes 135176 | tf_op jit(solution)/shard_map/ppermute | solution.py:463
  54.5 5.5 %collective-permute-start.16 = (bf16[32,704]{1,0:T(8,128)(2,1)S(1)}, bf16[32,704]{1,0:T(8,128)(2,1)S(1)}, u32[]{:S(2)}, u32[]{:S(2)}) collective-permute-start(bf16[32,704]{1,0:T(8,128)(2,1)S(1)} %shard_map.84.refs_0_), channel_id=1, source_target_pairs={{8,0},{12,4},{0,8},{4,12},{9,1},{13,5},{1,9},{5,13},{10,2},{14,6},... | collective-permute-start | bytes 135176 | tf_op jit(solution)/shard_map/ppermute | solution.py:463
  54.8 5.2 %collective-permute-start.15 = (bf16[32,704]{1,0:T(8,128)(2,1)S(1)}, bf16[32,704]{1,0:T(8,128)(2,1)S(1)}, u32[]{:S(2)}, u32[]{:S(2)}) collective-permute-start(bf16[32,704]{1,0:T(8,128)(2,1)S(1)} %shard_map.84.refs_0_), channel_id=1, source_target_pairs={{4,0},{0,4},{12,8},{8,12},{5,1},{1,5},{13,9},{9,13},{6,2},{2,6},{1... | collective-permute-start | bytes 135176 | tf_op jit(solution)/shard_map/ppermute | solution.py:463
  60.9 1.5 %collective-permute-start.18 = (f32[32,1280]{1,0:T(8,128)S(1)}, f32[32,1280]{1,0:T(8,128)S(1)}, u32[]{:S(2)}, u32[]{:S(2)}) collective-permute-start(f32[32,1280]{1,0:T(8,128)S(1)} %shard_map.85.refs_0_), channel_id=1, source_target_pairs={{0,1},{1,0},{2,3},{3,2},{4,5},{5,4},{6,7},{7,6},{8,9},{9,8},{10,11... | collective-permute-start | bytes 491528 | tf_op jit(solution)/shard_map/ppermute | solution.py:460

commit v9 on v8

--- a/solution.py
+++ b/solution.py
@@ -216,14 +216,10 @@
         begin = pl.multiple_of((first + at) * TAPS, TAPS)
         x_scr[at * cl : (at + 1) * cl, :] = xp_scr[:, pl.ds(begin, 2 * TAPS)]
 
-    def convolve(g, carry):
-        tab_copy(g).wait()
-        for at in range(GROUP):
-            f = g * GROUP + at
-            s_ref[f, pl.ds(first, blocks - 1), x_me] = power_of(x_scr, tab_ref[f]).reshape(blocks - 1, cl, TAPS)
-        return carry
-
-    lax.fori_loop(0, GROUPS, convolve, 0)
+    for f in range(NF):
+        if f % GROUP == 0:
+            tab_copy(f // GROUP).wait()
+        s_ref[f, pl.ds(first, blocks - 1), x_me] = power_of(x_scr, tab_ref[f]).reshape(blocks - 1, cl, TAPS)
     for copy in later:
         copy.wait()
 
@@ -255,17 +251,12 @@
             at = cl * (1 + (shift - 1) * blocks + blk)
             x_scr[at : at + cl, :] = xp_scr[owners[shift], :, blk * TAPS : (blk + 2) * TAPS]
 
-    def convolve(g, carry):
-        for at in range(GROUP):
-            f = g * GROUP + at
-            power = power_of(x_scr, tab_ref[f])
-            s_ref[f, outer, x_me] = power[:cl]
-            for shift in range(1, rows):
-                line = cl * (1 + (shift - 1) * blocks)
-                s_ref[f, :, owners[shift]] = power[line : line + blocks * cl].reshape(blocks, cl, TAPS)
-        return carry
-
-    lax.fori_loop(0, GROUPS, convolve, 0)
+    for f in range(NF):
+        power = power_of(x_scr, tab_ref[f])
+        s_ref[f, outer, x_me] = power[:cl]
+        for shift in range(1, rows):
+            line = cl * (1 + (shift - 1) * blocks)
+            s_ref[f, :, owners[shift]] = power[line : line + blocks * cl].reshape(blocks, cl, TAPS)
 
 
 def first_kernel(rows, subs, cl, *refs):
@@ -399,7 +390,7 @@
         copy.wait()
 
 
-def sum_kernel(*refs):
+def sum_kernel(_, *refs):
     parts, (out_ref, scr, sem) = refs[:-3], refs[-3:]
     total = parts[0][...]
     for part in parts[1:]:
@@ -604,9 +595,10 @@
     )
     (synergies,) = call(
         sum_kernel,
-        [part] + [sub_shift(part, dc) for dc in range(1, subs)],
+        [wide, part] + [sub_shift(part, dc) for dc in range(1, subs)],
         [pltpu.HBM((rank, NF * cl), F32)],
         [pltpu.VMEM((rank, NF * cl), F32), pltpu.SemaphoreType.DMA],
+        in_specs=[anywhere] + [whole] * subs,
         out_specs=[anywhere],
     )
     return (synergies.T, wide)

time: 64.1 us -> 63.9 us (level)
  local copies, waits for them, and re-layouts: 0 us -> 1.04 us
  waiting for transfers between devices: 18.2 us -> 17.3 us
    unnamed x0 -> x2, local copies, waits for them, and re-layouts: none -> 1.04 us
    ppermute x7, waiting for transfers between devices: 3.71 us -> 2.88 us  [sub_shift(): lax.ppermute(value, 'sub', [(i, (i + shift) % subs) for i in range(subs)])]
where the time goes in v9:
time: 63.9 us; the launch traced here: 63.7 us
  Pallas kernels  24.7 us (39%)
  starting transfers between devices  19.6 us (31%)
  waiting for transfers between devices  17.3 us (27%)
  local copies, waits for them, and re-layouts  1.04 us (2%)
  between operations  0.96 us (2%)
    pallas_call x20, Pallas kernels, call(): pl.pallas_call(kernel, out_shape=[jax.ShapeDtypeStruct(*out) if isinstanc...  24.7 us
    ppermute x6, starting transfers between devices, frm_shift(): lax.ppermute(value, 'frm', [(partner(i, shift, frms), i) for i in range(f...  9.41 us
    ppermute x6, waiting for transfers between devices, row_shift(): lax.ppermute(value, 'row', [(i, (i + shift) % rows) for i in range(rows)])  7.36 us
    ppermute x6, waiting for transfers between devices, frm_shift(): lax.ppermute(value, 'frm', [(partner(i, shift, frms), i) for i in range(f...  7.1 us
    ppermute x6, starting transfers between devices, row_shift(): lax.ppermute(value, 'row', [(i, (i + shift) % rows) for i in range(rows)])  6.99 us
    ppermute x7, waiting for transfers between devices, sub_shift(): lax.ppermute(value, 'sub', [(i, (i + shift) % subs) for i in range(subs)])  2.88 us
    ppermute x7, starting transfers between devices, sub_shift(): lax.ppermute(value, 'sub', [(i, (i + shift) % subs) for i in range(subs)])  2.54 us
  transfers between devices with their start and end apart: 20, of which 10 were waited for; matrix products, arithmetic and copies ran while one was open for 0% of the time, Pallas kernels for 27%

profile of v9, /device:TPU:0, one launch (start us, length us, event | category | flops | bytes accessed | tf_op | source)
XLA Modules:
  0.0 63.7 jit_solution(14476568680896116242)
XLA Ops:
  0.6 1.0 %shard_map.68 = (bf16[32,2176]{1,0:T(8,128)(2,1)S(1)}, bf16[32,2176]{1,0:T(8,128)(2,1)S(1)}) custom-call(bf16[32,4096]{1,0:T(8,128)(2,1)} %sig_hbm.1), custom_call_target="tpu_custom_call" | custom-call | tf_op jit(solution)/shard_map/pallas_call | solution.py:408
  1.7 3.0 %collective-permute-start = (bf16[32,2176]{1,0:T(8,128)(2,1)S(1)}, bf16[32,2176]{1,0:T(8,128)(2,1)S(1)}, u32[]{:S(2)}, u32[]{:S(2)}) collective-permute-start(bf16[32,2176]{1,0:T(8,128)(2,1)S(1)} %get-tuple-element.34), channel_id=1, source_target_pairs={{0,2},{2,0},{1,3},{3,1},{4,6},{6,4},{5,7},{7,5},{8,10},{10,8},{9,1... | collective-permute-start | bytes 417800 | tf_op jit(solution)/shard_map/ppermute | solution.py:448
  4.7 4.8 %shard_map.69 = (bf16[40,16,2,32,128]{4,3,2,1,0:T(8,128)(2,1)S(1)}, f32[32,1280]{1,0:T(8,128)S(1)}, f32[32,2048]{1,0:T(8,128)S(1)}, bf16[1280,1280]{1,0:T(8,128)(2,1)S(1)}, bf16[40,256,256]{2,1,0:T(8,128)(2,1)S(1)}) custom-call(bf16[32,2176]{1,0:T(8,128)(2,1)S(1)} %get-tuple-element.31.sig_ref.refs_0_, f32[32,1280]{1,0:T(8,128)} %bitcast.3, ...), custom_call_target="tpu_custom_call" | custom-call | flops 2684354560 | tf_op jit(solution)/shard_map/pallas_call | solution.py:408
  9.5 0.0 collective-permute-done.refs_0_.refs_1_
  9.5 0.7 %collective-permute-start.2 = (bf16[64,128]{1,0:T(8,128)(2,1)S(1)}, bf16[64,128]{1,0:T(8,128)(2,1)S(1)}, u32[]{:S(2)}, u32[]{:S(2)}) collective-permute-start(bf16[64,128]{1,0:T(8,128)(2,1)S(1)} %shard_map.70.refs_0_), channel_id=1, source_target_pairs={{2,1},{3,4},{6,5},{7,8},{10,9},{11,12},{14,13},{1,2},{4,3},{5,6},{... | collective-permute-start | bytes 49160 | tf_op jit(solution)/shard_map/ppermute | solution.py:500
  10.2 0.8 %shard_map.71 = (f32[32,640]{1,0:T(8,128)S(1)}, bf16[32,1344]{1,0:T(8,128)(2,1)S(1)}) custom-call(f32[32,1280]{1,0:T(8,128)S(1)} %get-tuple-element.32.w_ref, bf16[1280,1280]{1,0:T(8,128)(2,1)S(1)} %get-tuple-element.33.order_ref, bf16[64,128]{1,0:T(8,128)(2,1)S(1)} %shard_map.70.refs_0_), custom_call_target="tpu_custom_call" | custom-call | tf_op jit(solution)/shard_map/pallas_call | solution.py:408
  11.0 2.4 %collective-permute-start.1 = (bf16[32,1344]{1,0:T(8,128)(2,1)S(1)}, bf16[32,1344]{1,0:T(8,128)(2,1)S(1)}, u32[]{:S(2)}, u32[]{:S(2)}) collective-permute-start(bf16[32,1344]{1,0:T(8,128)(2,1)S(1)} %get-tuple-element.37.refs_0_), channel_id=1, source_target_pairs={{0,2},{2,0},{1,3},{3,1},{4,6},{6,4},{5,7},{7,5},{8,10},{10,8},{9,1... | collective-permute-start | bytes 258056 | tf_op jit(solution)/shard_map/ppermute | solution.py:448
  13.5 0.0 collective-permute-done.2.halo_ref
  13.5 3.5 %shard_map.72.refs_3_.s_ref.refs_2_.refs_6_ = bf16[40,16,2,32,128]{4,3,2,1,0:T(8,128)(2,1)S(1)} custom-call(bf16[64,128]{1,0:T(8,128)(2,1)S(1)} %collective-permute-done.2.halo_ref, bf16[40,256,256]{2,1,0:T(8,128)(2,1)S(1)} %get-tuple-element.39.tab_ref, bf16[32,2176]{1,0:T(8,128)(2,1)S(1)} %get-tuple-element.31.sig_ref.refs_0_, ...), custom_call_target="tpu_custom_call", output_to_operand_aliasing={{}: (4, {})} | custom-call | flops 5368709120 | tf_op jit(solution)/shard_map/pallas_call | solution.py:408
  17.0 0.0 collective-permute-done.1.refs_1_
  17.0 3.0 %shard_map.73 = (f32[32,2048]{1,0:T(8,128)S(1)}, f32[32,32]{1,0:T(8,128)S(1)}, f32[32,672]{1,0:T(8,128)S(1)}) custom-call(bf16[32,1344]{1,0:T(8,128)(2,1)S(1)} %get-tuple-element.37.refs_0_, bf16[32,1344]{1,0:T(8,128)(2,1)S(1)} %collective-permute-done.1.refs_1_, f32[32,2048]{1,0:T(8,128)S(1)} %get-tuple-element.38.refs_2_, ...), custom_call_target="tpu_custom_call" | custom-call | tf_op jit(solution)/shard_map/pallas_call | solution.py:408
  20.0 1.8 %collective-permute-start.3 = (f32[32,672]{1,0:T(8,128)S(1)}, f32[32,672]{1,0:T(8,128)S(1)}, u32[]{:S(2)}, u32[]{:S(2)}) collective-permute-start(f32[32,672]{1,0:T(8,128)S(1)} %get-tuple-element.43), channel_id=1, source_target_pairs={{0,1},{1,0},{2,3},{3,2},{4,5},{5,4},{6,7},{7,6},{8,9},{9,8},{10,11... | collective-permute-start | bytes 258056 | tf_op jit(solution)/shard_map/ppermute | solution.py:451
  21.8 1.6 %shard_map.74 = (f32[32,640]{1,0:T(8,128)S(1)}, f32[32,640]{1,0:T(8,128)S(1)}) custom-call(f32[32,2048]{1,0:T(8,128)S(1)} %get-tuple-element.40.h_ref.refs_5_, bf16[40,16,2,32,128]{4,3,2,1,0:T(8,128)(2,1)S(1)} %shard_map.72.refs_3_.s_ref.refs_2_.refs_6_), custom_call_target="tpu_custom_call" | custom-call | flops 1342177280 | tf_op jit(solution)/shard_map/pallas_call | solution.py:408
  23.4 0.1 collective-permute-start.4
  23.5 0.0 collective-permute-done.3.refs_2_
  23.5 0.1 shard_map.75
  23.6 0.8 %collective-permute-start.5 = (bf16[32,704]{1,0:T(8,128)(2,1)S(1)}, bf16[32,704]{1,0:T(8,128)(2,1)S(1)}, u32[]{:S(2)}, u32[]{:S(2)}) collective-permute-start(bf16[32,704]{1,0:T(8,128)(2,1)S(1)} %get-tuple-element.44.refs_0_), channel_id=1, source_target_pairs={{0,2},{2,0},{1,3},{3,1},{4,6},{6,4},{5,7},{7,5},{8,10},{10,8},{9,1... | collective-permute-start | bytes 135176 | tf_op jit(solution)/shard_map/ppermute | solution.py:448
  24.4 0.8 %shard_map.76.own_ref = f32[32,640]{1,0:T(8,128)S(1)} custom-call(f32[32,2048]{1,0:T(8,128)S(1)} %get-tuple-element.40.h_ref.refs_5_, bf16[40,16,2,32,128]{4,3,2,1,0:T(8,128)(2,1)S(1)} %shard_map.72.refs_3_.s_ref.refs_2_.refs_6_, bf16[32,704]{1,0:T(8,128)(2,1)S(1)} %get-tuple-element.44.refs_0_), custom_call_target="tpu_custom_call" | custom-call | flops 1 | tf_op jit(solution)/shard_map/pallas_call | solution.py:408
  25.2 0.0 collective-permute-done.4.refs_0_
  25.3 2.4 %collective-permute-done.5.refs_1_ = bf16[32,704]{1,0:T(8,128)(2,1)S(1)} collective-permute-done((bf16[32,704]{1,0:T(8,128)(2,1)S(1)}, bf16[32,704]{1,0:T(8,128)(2,1)S(1)}, u32[]{:S(2)}, u32[]{:S(2)}) %collective-permute-start.5) | collective-permute-done | bytes 45088 | tf_op jit(solution)/shard_map/ppermute | solution.py:448
  27.7 0.2 shard_map.77.refs_0_
  27.9 4.4 %collective-permute-start.8 = (bf16[32,704]{1,0:T(8,128)(2,1)S(1)}, bf16[32,704]{1,0:T(8,128)(2,1)S(1)}, u32[]{:S(2)}, u32[]{:S(2)}) collective-permute-start(bf16[32,704]{1,0:T(8,128)(2,1)S(1)} %shard_map.77.refs_0_), channel_id=1, source_target_pairs={{12,0},{8,4},{4,8},{0,12},{13,1},{9,5},{5,9},{1,13},{14,2},{10,6},... | collective-permute-start | bytes 135176 | tf_op jit(solution)/shard_map/ppermute | solution.py:454
  32.2 0.0 collective-permute-start.7
  32.2 0.6 collective-permute-start.6
  32.9 1.6 %collective-permute-done.8.refs_3_ = bf16[32,704]{1,0:T(8,128)(2,1)S(1)} collective-permute-done((bf16[32,704]{1,0:T(8,128)(2,1)S(1)}, bf16[32,704]{1,0:T(8,128)(2,1)S(1)}, u32[]{:S(2)}, u32[]{:S(2)}) %collective-permute-start.8) | collective-permute-done | bytes 45088 | tf_op jit(solution)/shard_map/ppermute | solution.py:454
  34.5 2.7 %collective-permute-done.7.refs_2_ = bf16[32,704]{1,0:T(8,128)(2,1)S(1)} collective-permute-done((bf16[32,704]{1,0:T(8,128)(2,1)S(1)}, bf16[32,704]{1,0:T(8,128)(2,1)S(1)}, u32[]{:S(2)}, u32[]{:S(2)}) %collective-permute-start.7) | collective-permute-done | bytes 45088 | tf_op jit(solution)/shard_map/ppermute | solution.py:454
  37.2 0.0 collective-permute-done.6.refs_1_
  37.2 0.6 shard_map.78
  37.8 0.0 collective-permute-start.9
  37.9 0.1 collective-permute-start.10
  38.0 1.1 %collective-permute-done.9.refs_1_ = bf16[32,704]{1,0:T(8,128)(2,1)S(1)} collective-permute-done((bf16[32,704]{1,0:T(8,128)(2,1)S(1)}, bf16[32,704]{1,0:T(8,128)(2,1)S(1)}, u32[]{:S(2)}, u32[]{:S(2)}) %collective-permute-start.9) | collective-permute-done | bytes 45088 | tf_op jit(solution)/shard_map/ppermute | solution.py:451
  39.1 1.0 %shard_map.79.refs_4_ = f32[32,2048]{1,0:T(8,128)S(1)} custom-call(bf16[32,704]{1,0:T(8,128)(2,1)S(1)} %get-tuple-element.47.refs_0_, bf16[32,704]{1,0:T(8,128)(2,1)S(1)} %collective-permute-done.9.refs_1_, bf16[40,16,2,32,128]{4,3,2,1,0:T(8,128)(2,1)S(1)} %shard_map.72.refs_3_.s_ref.refs_2_.refs_6_), custom_call_target="tpu_custom_call" | custom-call | flops 1342177280 | tf_op jit(solution)/shard_map/pallas_call | solution.py:408
  40.1 1.9 %collective-permute-done.10.refs_2_ = bf16[32,704]{1,0:T(8,128)(2,1)S(1)} collective-permute-done((bf16[32,704]{1,0:T(8,128)(2,1)S(1)}, bf16[32,704]{1,0:T(8,128)(2,1)S(1)}, u32[]{:S(2)}, u32[]{:S(2)}) %collective-permute-start.10) | collective-permute-done | bytes 45088 | tf_op jit(solution)/shard_map/ppermute | solution.py:448
  42.0 0.0 collective-permute-start.11
  42.0 1.2 %collective-permute-done.11.refs_3_ = bf16[32,704]{1,0:T(8,128)(2,1)S(1)} collective-permute-done((bf16[32,704]{1,0:T(8,128)(2,1)S(1)}, bf16[32,704]{1,0:T(8,128)(2,1)S(1)}, u32[]{:S(2)}, u32[]{:S(2)}) %collective-permute-start.11) | collective-permute-done | bytes 45088 | tf_op jit(solution)/shard_map/ppermute | solution.py:451
  43.3 2.1 %shard_map.80 = (f32[32,2048]{1,0:T(8,128)S(1)}, f32[32,32]{1,0:T(8,128)S(1)}, f32[32,672]{1,0:T(8,128)S(1)}) custom-call(bf16[32,704]{1,0:T(8,128)(2,1)S(1)} %get-tuple-element.47.refs_0_, bf16[32,704]{1,0:T(8,128)(2,1)S(1)} %collective-permute-done.9.refs_1_, bf16[32,704]{1,0:T(8,128)(2,1)S(1)} %collective-permute-done.10.refs_2_, ...), custom_call_target="tpu_custom_call" | custom-call | tf_op jit(solution)/shard_map/pallas_call | solution.py:408
  45.4 0.2 collective-permute-start.12
  45.6 1.6 %shard_map.81 = (f32[32,640]{1,0:T(8,128)S(1)}, f32[32,640]{1,0:T(8,128)S(1)}) custom-call(f32[32,2048]{1,0:T(8,128)S(1)} %get-tuple-element.57.h_ref.refs_0_, bf16[40,16,2,32,128]{4,3,2,1,0:T(8,128)(2,1)S(1)} %shard_map.72.refs_3_.s_ref.refs_2_.refs_6_), custom_call_target="tpu_custom_call" | custom-call | flops 1342177280 | tf_op jit(solution)/shard_map/pallas_call | solution.py:408
  47.2 0.4 collective-permute-start.13
  47.6 0.0 collective-permute-done.12.refs_2_
  47.6 0.1 shard_map.82
  47.7 0.3 collective-permute-start.14
  48.0 0.8 %shard_map.83.own_ref = f32[32,640]{1,0:T(8,128)S(1)} custom-call(f32[32,2048]{1,0:T(8,128)S(1)} %get-tuple-element.57.h_ref.refs_0_, bf16[40,16,2,32,128]{4,3,2,1,0:T(8,128)(2,1)S(1)} %shard_map.72.refs_3_.s_ref.refs_2_.refs_6_, bf16[32,704]{1,0:T(8,128)(2,1)S(1)} %get-tuple-element.54.refs_0_), custom_call_target="tpu_custom_call" | custom-call | flops 1 | tf_op jit(solution)/shard_map/pallas_call | solution.py:408
  48.8 0.0 collective-permute-done.13.refs_0_
  48.8 3.0 %collective-permute-done.14.refs_1_ = bf16[32,704]{1,0:T(8,128)(2,1)S(1)} collective-permute-done((bf16[32,704]{1,0:T(8,128)(2,1)S(1)}, bf16[32,704]{1,0:T(8,128)(2,1)S(1)}, u32[]{:S(2)}, u32[]{:S(2)}) %collective-permute-start.14) | collective-permute-done | bytes 45088 | tf_op jit(solution)/shard_map/ppermute | solution.py:448
  51.8 0.2 shard_map.84.refs_0_
  52.0 0.3 collective-permute-start.15
  52.3 1.6 %collective-permute-start.18 = (bf16[32,704]{1,0:T(8,128)(2,1)S(1)}, bf16[32,704]{1,0:T(8,128)(2,1)S(1)}, u32[]{:S(2)}, u32[]{:S(2)}) collective-permute-start(bf16[32,704]{1,0:T(8,128)(2,1)S(1)} %shard_map.84.refs_0_), channel_id=1, source_target_pairs={{12,0},{8,4},{4,8},{0,12},{13,1},{9,5},{5,9},{1,13},{14,2},{10,6},... | collective-permute-start | bytes 135176 | tf_op jit(solution)/shard_map/ppermute | solution.py:454
  53.9 0.4 collective-permute-start.17
  54.3 2.4 %collective-permute-start.16 = (bf16[32,704]{1,0:T(8,128)(2,1)S(1)}, bf16[32,704]{1,0:T(8,128)(2,1)S(1)}, u32[]{:S(2)}, u32[]{:S(2)}) collective-permute-start(bf16[32,704]{1,0:T(8,128)(2,1)S(1)} %shard_map.84.refs_0_), channel_id=1, source_target_pairs={{4,0},{0,4},{12,8},{8,12},{5,1},{1,5},{13,9},{9,13},{6,2},{2,6},{1... | collective-permute-start | bytes 135176 | tf_op jit(solution)/shard_map/ppermute | solution.py:454
  56.6 1.5 %collective-permute-done.18.refs_3_ = bf16[32,704]{1,0:T(8,128)(2,1)S(1)} collective-permute-done((bf16[32,704]{1,0:T(8,128)(2,1)S(1)}, bf16[32,704]{1,0:T(8,128)(2,1)S(1)}, u32[]{:S(2)}, u32[]{:S(2)}) %collective-permute-start.18) | collective-permute-done | bytes 45088 | tf_op jit(solution)/shard_map/ppermute | solution.py:454
  58.1 1.2 %collective-permute-done.17.refs_2_ = bf16[32,704]{1,0:T(8,128)(2,1)S(1)} collective-permute-done((bf16[32,704]{1,0:T(8,128)(2,1)S(1)}, bf16[32,704]{1,0:T(8,128)(2,1)S(1)}, u32[]{:S(2)}, u32[]{:S(2)}) %collective-permute-start.17) | collective-permute-done | bytes 45088 | tf_op jit(solution)/shard_map/ppermute | solution.py:454
  59.4 0.0 collective-permute-done.16.refs_1_
  59.4 0.9 %shard_map.86.refs_0_ = f32[32,1280]{1,0:T(8,128)S(1)} custom-call(f32[32,640]{1,0:T(8,128)S(1)} %get-tuple-element.58.w_ref, bf16[1280,1280]{1,0:T(8,128)(2,1)S(1)} %get-tuple-element.33.order_ref, bf16[32,704]{1,0:T(8,128)(2,1)S(1)} %shard_map.84.refs_0_, bf16[32,704]{1,0:T(8,128)(2,1)S(1)} %collective-permute-done.16.refs_1_, ...), custom_call_target="tpu_custom_call" | custom-call | tf_op jit(solution)/shard_map/pallas_call | solution.py:408
  60.3 0.1 collective-permute-start.19
  60.4 0.0 collective-permute-done.15.refs_1_
  60.4 0.8 %shard_map.85._ = f32[32,4096]{1,0:T(8,128)} custom-call(f32[32,2048]{1,0:T(8,128)S(1)} %get-tuple-element.57.h_ref.refs_0_, f32[32,2048]{1,0:T(8,128)S(1)} %collective-permute-done.15.refs_1_), custom_call_target="tpu_custom_call" | custom-call | tf_op jit(solution)/shard_map/pallas_call | solution.py:408
  61.2 0.5 collective-permute-done.19.refs_1_
  61.8 0.0 copy-start
  61.8 1.0 %copy-done = f32[32,4096]{1,0:T(8,128)S(1)} copy-done((f32[32,4096]{1,0:T(8,128)S(1)}, f32[32,4096]{1,0:T(8,128)}, u32[]{:S(2)}) %copy-start) | copy-done | bytes 524312
  62.8 0.7 %shard_map.87 = f32[32,1280]{1,0:T(8,128)} custom-call(f32[32,4096]{1,0:T(8,128)S(1)} %copy-done, f32[32,1280]{1,0:T(8,128)S(1)} %shard_map.86.refs_0_, f32[32,1280]{1,0:T(8,128)S(1)} %collective-permute-done.19.refs_1_), custom_call_target="tpu_custom_call" | custom-call | tf_op jit(solution)/shard_map/pallas_call | solution.py:408
  (1 shorter events, 0.0 us)
Async XLA Ops:
  1.7 7.8 %collective-permute-start = (bf16[32,2176]{1,0:T(8,128)(2,1)S(1)}, bf16[32,2176]{1,0:T(8,128)(2,1)S(1)}, u32[]{:S(2)}, u32[]{:S(2)}) collective-permute-start(bf16[32,2176]{1,0:T(8,128)(2,1)S(1)} %get-tuple-element.34), channel_id=1, source_target_pairs={{0,2},{2,0},{1,3},{3,1},{4,6},{6,4},{5,7},{7,5},{8,10},{10,8},{9,1... | collective-permute-start | bytes 417800 | tf_op jit(solution)/shard_map/ppermute | solution.py:448
  9.5 4.0 %collective-permute-start.2 = (bf16[64,128]{1,0:T(8,128)(2,1)S(1)}, bf16[64,128]{1,0:T(8,128)(2,1)S(1)}, u32[]{:S(2)}, u32[]{:S(2)}) collective-permute-start(bf16[64,128]{1,0:T(8,128)(2,1)S(1)} %shard_map.70.refs_0_), channel_id=1, source_target_pairs={{2,1},{3,4},{6,5},{7,8},{10,9},{11,12},{14,13},{1,2},{4,3},{5,6},{... | collective-permute-start | bytes 49160 | tf_op jit(solution)/shard_map/ppermute | solution.py:500
  11.0 6.0 %collective-permute-start.1 = (bf16[32,1344]{1,0:T(8,128)(2,1)S(1)}, bf16[32,1344]{1,0:T(8,128)(2,1)S(1)}, u32[]{:S(2)}, u32[]{:S(2)}) collective-permute-start(bf16[32,1344]{1,0:T(8,128)(2,1)S(1)} %get-tuple-element.37.refs_0_), channel_id=1, source_target_pairs={{0,2},{2,0},{1,3},{3,1},{4,6},{6,4},{5,7},{7,5},{8,10},{10,8},{9,1... | collective-permute-start | bytes 258056 | tf_op jit(solution)/shard_map/ppermute | solution.py:448
  20.0 3.4 %collective-permute-start.3 = (f32[32,672]{1,0:T(8,128)S(1)}, f32[32,672]{1,0:T(8,128)S(1)}, u32[]{:S(2)}, u32[]{:S(2)}) collective-permute-start(f32[32,672]{1,0:T(8,128)S(1)} %get-tuple-element.43), channel_id=1, source_target_pairs={{0,1},{1,0},{2,3},{3,2},{4,5},{5,4},{6,7},{7,6},{8,9},{9,8},{10,11... | collective-permute-start | bytes 258056 | tf_op jit(solution)/shard_map/ppermute | solution.py:451
  23.4 1.8 %collective-permute-start.4 = (f32[32,640]{1,0:T(8,128)S(1)}, f32[32,640]{1,0:T(8,128)S(1)}, u32[]{:S(2)}, u32[]{:S(2)}) collective-permute-start(f32[32,640]{1,0:T(8,128)S(1)} %get-tuple-element.46), channel_id=1, source_target_pairs={{0,1},{1,0},{2,3},{3,2},{4,5},{5,4},{6,7},{7,6},{8,9},{9,8},{10,11... | collective-permute-start | bytes 245768 | tf_op jit(solution)/shard_map/ppermute | solution.py:451
  23.6 4.1 %collective-permute-start.5 = (bf16[32,704]{1,0:T(8,128)(2,1)S(1)}, bf16[32,704]{1,0:T(8,128)(2,1)S(1)}, u32[]{:S(2)}, u32[]{:S(2)}) collective-permute-start(bf16[32,704]{1,0:T(8,128)(2,1)S(1)} %get-tuple-element.44.refs_0_), channel_id=1, source_target_pairs={{0,2},{2,0},{1,3},{3,1},{4,6},{6,4},{5,7},{7,5},{8,10},{10,8},{9,1... | collective-permute-start | bytes 135176 | tf_op jit(solution)/shard_map/ppermute | solution.py:448
  27.9 6.6 %collective-permute-start.8 = (bf16[32,704]{1,0:T(8,128)(2,1)S(1)}, bf16[32,704]{1,0:T(8,128)(2,1)S(1)}, u32[]{:S(2)}, u32[]{:S(2)}) collective-permute-start(bf16[32,704]{1,0:T(8,128)(2,1)S(1)} %shard_map.77.refs_0_), channel_id=1, source_target_pairs={{12,0},{8,4},{4,8},{0,12},{13,1},{9,5},{5,9},{1,13},{14,2},{10,6},... | collective-permute-start | bytes 135176 | tf_op jit(solution)/shard_map/ppermute | solution.py:454
  32.2 5.0 %collective-permute-start.7 = (bf16[32,704]{1,0:T(8,128)(2,1)S(1)}, bf16[32,704]{1,0:T(8,128)(2,1)S(1)}, u32[]{:S(2)}, u32[]{:S(2)}) collective-permute-start(bf16[32,704]{1,0:T(8,128)(2,1)S(1)} %shard_map.77.refs_0_), channel_id=1, source_target_pairs={{8,0},{12,4},{0,8},{4,12},{9,1},{13,5},{1,9},{5,13},{10,2},{14,6},... | collective-permute-start | bytes 135176 | tf_op jit(solution)/shard_map/ppermute | solution.py:454
  32.2 5.0 %collective-permute-start.6 = (bf16[32,704]{1,0:T(8,128)(2,1)S(1)}, bf16[32,704]{1,0:T(8,128)(2,1)S(1)}, u32[]{:S(2)}, u32[]{:S(2)}) collective-permute-start(bf16[32,704]{1,0:T(8,128)(2,1)S(1)} %shard_map.77.refs_0_), channel_id=1, source_target_pairs={{4,0},{0,4},{12,8},{8,12},{5,1},{1,5},{13,9},{9,13},{6,2},{2,6},{1... | collective-permute-start | bytes 135176 | tf_op jit(solution)/shard_map/ppermute | solution.py:454
  37.8 1.2 %collective-permute-start.9 = (bf16[32,704]{1,0:T(8,128)(2,1)S(1)}, bf16[32,704]{1,0:T(8,128)(2,1)S(1)}, u32[]{:S(2)}, u32[]{:S(2)}) collective-permute-start(bf16[32,704]{1,0:T(8,128)(2,1)S(1)} %get-tuple-element.47.refs_0_), channel_id=1, source_target_pairs={{0,1},{1,0},{2,3},{3,2},{4,5},{5,4},{6,7},{7,6},{8,9},{9,8},{10,11... | collective-permute-start | bytes 135176 | tf_op jit(solution)/shard_map/ppermute | solution.py:451
  37.9 4.2 %collective-permute-start.10 = (bf16[32,704]{1,0:T(8,128)(2,1)S(1)}, bf16[32,704]{1,0:T(8,128)(2,1)S(1)}, u32[]{:S(2)}, u32[]{:S(2)}) collective-permute-start(bf16[32,704]{1,0:T(8,128)(2,1)S(1)} %get-tuple-element.47.refs_0_), channel_id=1, source_target_pairs={{0,2},{2,0},{1,3},{3,1},{4,6},{6,4},{5,7},{7,5},{8,10},{10,8},{9,1... | collective-permute-start | bytes 135176 | tf_op jit(solution)/shard_map/ppermute | solution.py:448
  42.0 1.2 %collective-permute-start.11 = (bf16[32,704]{1,0:T(8,128)(2,1)S(1)}, bf16[32,704]{1,0:T(8,128)(2,1)S(1)}, u32[]{:S(2)}, u32[]{:S(2)}) collective-permute-start(bf16[32,704]{1,0:T(8,128)(2,1)S(1)} %collective-permute-done.10.refs_2_), channel_id=1, source_target_pairs={{0,1},{1,0},{2,3},{3,2},{4,5},{5,4},{6,7},{7,6},{8,9},{9,8},{10,11... | collective-permute-start | bytes 135176 | tf_op jit(solution)/shard_map/ppermute | solution.py:451
  45.4 2.2 %collective-permute-start.12 = (f32[32,672]{1,0:T(8,128)S(1)}, f32[32,672]{1,0:T(8,128)S(1)}, u32[]{:S(2)}, u32[]{:S(2)}) collective-permute-start(f32[32,672]{1,0:T(8,128)S(1)} %get-tuple-element.53), channel_id=1, source_target_pairs={{0,1},{1,0},{2,3},{3,2},{4,5},{5,4},{6,7},{7,6},{8,9},{9,8},{10,11... | collective-permute-start | bytes 258056 | tf_op jit(solution)/shard_map/ppermute | solution.py:451
  47.2 1.6 %collective-permute-start.13 = (f32[32,640]{1,0:T(8,128)S(1)}, f32[32,640]{1,0:T(8,128)S(1)}, u32[]{:S(2)}, u32[]{:S(2)}) collective-permute-start(f32[32,640]{1,0:T(8,128)S(1)} %get-tuple-element.56), channel_id=1, source_target_pairs={{0,1},{1,0},{2,3},{3,2},{4,5},{5,4},{6,7},{7,6},{8,9},{9,8},{10,11... | collective-permute-start | bytes 245768 | tf_op jit(solution)/shard_map/ppermute | solution.py:451
  47.7 4.1 %collective-permute-start.14 = (bf16[32,704]{1,0:T(8,128)(2,1)S(1)}, bf16[32,704]{1,0:T(8,128)(2,1)S(1)}, u32[]{:S(2)}, u32[]{:S(2)}) collective-permute-start(bf16[32,704]{1,0:T(8,128)(2,1)S(1)} %get-tuple-element.54.refs_0_), channel_id=1, source_target_pairs={{0,2},{2,0},{1,3},{3,1},{4,6},{6,4},{5,7},{7,5},{8,10},{10,8},{9,1... | collective-permute-start | bytes 135176 | tf_op jit(solution)/shard_map/ppermute | solution.py:448
  52.0 8.4 %collective-permute-start.15 = (f32[32,2048]{1,0:T(8,128)S(1)}, f32[32,2048]{1,0:T(8,128)S(1)}, u32[]{:S(2)}, u32[]{:S(2)}) collective-permute-start(f32[32,2048]{1,0:T(8,128)S(1)} %get-tuple-element.57.h_ref.refs_0_), channel_id=1, source_target_pairs={{0,2},{2,0},{1,3},{3,1},{4,6},{6,4},{5,7},{7,5},{8,10},{10,8},{9,1... | collective-permute-start | bytes 786440 | tf_op jit(solution)/shard_map/ppermute | solution.py:448
  52.3 5.9 %collective-permute-start.18 = (bf16[32,704]{1,0:T(8,128)(2,1)S(1)}, bf16[32,704]{1,0:T(8,128)(2,1)S(1)}, u32[]{:S(2)}, u32[]{:S(2)}) collective-permute-start(bf16[32,704]{1,0:T(8,128)(2,1)S(1)} %shard_map.84.refs_0_), channel_id=1, source_target_pairs={{12,0},{8,4},{4,8},{0,12},{13,1},{9,5},{5,9},{1,13},{14,2},{10,6},... | collective-permute-start | bytes 135176 | tf_op jit(solution)/shard_map/ppermute | solution.py:454
  53.9 5.5 %collective-permute-start.17 = (bf16[32,704]{1,0:T(8,128)(2,1)S(1)}, bf16[32,704]{1,0:T(8,128)(2,1)S(1)}, u32[]{:S(2)}, u32[]{:S(2)}) collective-permute-start(bf16[32,704]{1,0:T(8,128)(2,1)S(1)} %shard_map.84.refs_0_), channel_id=1, source_target_pairs={{8,0},{12,4},{0,8},{4,12},{9,1},{13,5},{1,9},{5,13},{10,2},{14,6},... | collective-permute-start | bytes 135176 | tf_op jit(solution)/shard_map/ppermute | solution.py:454
  54.3 5.1 %collective-permute-start.16 = (bf16[32,704]{1,0:T(8,128)(2,1)S(1)}, bf16[32,704]{1,0:T(8,128)(2,1)S(1)}, u32[]{:S(2)}, u32[]{:S(2)}) collective-permute-start(bf16[32,704]{1,0:T(8,128)(2,1)S(1)} %shard_map.84.refs_0_), channel_id=1, source_target_pairs={{4,0},{0,4},{12,8},{8,12},{5,1},{1,5},{13,9},{9,13},{6,2},{2,6},{1... | collective-permute-start | bytes 135176 | tf_op jit(solution)/shard_map/ppermute | solution.py:454
  60.3 1.5 %collective-permute-start.19 = (f32[32,1280]{1,0:T(8,128)S(1)}, f32[32,1280]{1,0:T(8,128)S(1)}, u32[]{:S(2)}, u32[]{:S(2)}) collective-permute-start(f32[32,1280]{1,0:T(8,128)S(1)} %shard_map.86.refs_0_), channel_id=1, source_target_pairs={{0,1},{1,0},{2,3},{3,2},{4,5},{5,4},{6,7},{7,6},{8,9},{9,8},{10,11... | collective-permute-start | bytes 491528 | tf_op jit(solution)/shard_map/ppermute | solution.py:451
  61.8 1.0 %copy-start = (f32[32,4096]{1,0:T(8,128)S(1)}, f32[32,4096]{1,0:T(8,128)}, u32[]{:S(2)}) copy-start(f32[32,4096]{1,0:T(8,128)} %shard_map.85._) | copy-start | bytes 1572868

commit v10 on v9

--- a/solution.py
+++ b/solution.py
@@ -13,8 +13,8 @@
 NF = 40
 TAPS = 128
 HALF = TAPS // 2
-GROUP = 8
-GROUPS = NF // GROUP
+LANES = 128
+CUTS = (0, 2, 8, 16, 24, 32, NF)
 F32 = jnp.float32
 BF16 = jnp.bfloat16
 HIGH = lax.Precision.HIGHEST
@@ -49,16 +49,36 @@
     return top, (value - top.astype(F32)).astype(BF16)
 
 
-def joined(message, at, rank):
-    return message[:, at : at + rank].astype(F32) + message[:, at + rank : at + 2 * rank].astype(F32)
+def message(rank, size):
+    return (rank * -(-size // LANES) + rank // 2, LANES)
 
 
 def pack(out_ref, main, gram):
     rank, size = main.shape
+    half = rank // 2
+    for at in range(0, size, LANES):
+        line = at // LANES * rank
+        width = min(LANES, size - at)
+        out_ref[line : line + rank, :width] = main[:, at : at + width].astype(BF16)
     top, rest = split_two(gram)
-    out_ref[:, :size] = main.astype(BF16)
-    out_ref[:, size : size + rank] = top
-    out_ref[:, size + rank : size + 2 * rank] = rest
+    terms = [top[:half], top[half:], rest[:half], rest[half:]]
+    line = out_ref.shape[0] - half
+    for at, term in enumerate(terms):
+        out_ref[line:, at * rank : (at + 1) * rank] = term
+
+
+def body(value, rank, size):
+    parts = []
+    for at in range(0, size, LANES):
+        line = at // LANES * rank
+        parts.append(value[line : line + rank, : min(LANES, size - at)])
+    return jnp.concatenate(parts, axis=1)
+
+
+def gram_of(value, rank):
+    last = value[value.shape[0] - rank // 2 :, :].astype(F32)
+    total = last[:, : 2 * rank] + last[:, 2 * rank : 4 * rank]
+    return jnp.concatenate([total[:, :rank], total[:, rank:]], axis=0)
 
 
 def reorder_kernel(w_ref, order_ref, *refs):
@@ -197,18 +217,16 @@
     x_me = lax.axis_index("row")
     mine = pl.ds(pl.multiple_of(x_me * frames, TAPS), frames)
 
-    def tab_copy(g):
-        span = pl.ds(g * GROUP, GROUP)
-        return pltpu.make_async_copy(tab_hbm.at[span], tab_ref.at[span], tab_sems.at[g])
-
+    table = [
+        pltpu.make_async_copy(tab_hbm.at[begin:end], tab_ref.at[begin:end], tab_sems.at[at])
+        for at, (begin, end) in enumerate(zip(CUTS, CUTS[1:]))
+    ]
     later = [
         pltpu.make_async_copy(w_hbm, w_ref, sems.at[0]),
         pltpu.make_async_copy(order_hbm, order_ref, sems.at[1]),
         pltpu.make_async_copy(h_hbm.at[:, mine], old_ref, sems.at[2]),
     ]
-    for g in range(GROUPS):
-        tab_copy(g).start()
-    for copy in later:
+    for copy in table:
         copy.start()
     place_signal(sig_ref, xp_scr, rows, frames)
     first = jnp.where(x_me == 0, 1, 0)
@@ -217,8 +235,11 @@
         x_scr[at * cl : (at + 1) * cl, :] = xp_scr[:, pl.ds(begin, 2 * TAPS)]
 
     for f in range(NF):
-        if f % GROUP == 0:
-            tab_copy(f // GROUP).wait()
+        if f in CUTS:
+            table[CUTS.index(f)].wait()
+        if f == CUTS[3]:
+            for copy in later:
+                copy.start()
         s_ref[f, pl.ds(first, blocks - 1), x_me] = power_of(x_scr, tab_ref[f]).reshape(blocks - 1, cl, TAPS)
     for copy in later:
         copy.wait()
@@ -267,8 +288,8 @@
     x_me = lax.axis_index("row")
     parts, gram = [], jnp.zeros(h_gram_ref.shape, F32)
     for shift, ref in enumerate(w_refs):
-        parts.append((ref[:, : NF * cl], lax.rem(x_me + rows - shift, rows)))
-        gram = gram + joined(ref, NF * cl, h_ref.shape[0])
+        parts.append((body(ref[...], h_ref.shape[0], NF * cl), lax.rem(x_me + rows - shift, rows)))
+        gram = gram + gram_of(ref[...], h_ref.shape[0])
     numerators(parts, s_ref, num_scr, cl)
     new_activations(h_ref[...], gram, num_scr[...], s_ref, h_out, h_gram_ref, msg_refs, rows, subs, cl)
 
@@ -279,7 +300,8 @@
     parts = []
     for line, dx in enumerate(shifts):
         for dc in range(subs):
-            w_scr[line, lax.rem(c_me + subs - dc, subs)] = w_refs[line * subs + dc][:, :size]
+            piece = body(w_refs[line * subs + dc][...], w_scr.shape[2], size)
+            w_scr[line, lax.rem(c_me + subs - dc, subs)] = piece
         w = jnp.concatenate([w_scr[line, c] for c in range(subs)], axis=1)
         parts.append((w, lax.rem(x_me + rows - dx, rows)))
     return parts
@@ -297,7 +319,7 @@
     msg_refs, (w_scr, num_scr) = refs[:-2], refs[-2:]
     gram = jnp.zeros(h_gram_ref.shape, F32)
     for ref in w_refs:
-        gram = gram + joined(ref, NF // subs * cl, h_ref.shape[0])
+        gram = gram + gram_of(ref[...], h_ref.shape[0])
     above = early_ref[...]
     if rows > 1:
         numerators(row_parts(rows, subs, cl, w_refs[subs:], w_scr, list(range(1, rows))), s_ref, num_scr, cl)
@@ -328,18 +350,18 @@
     for ref in core_refs:
         total = total + ref[...]
     for ref in msg_refs:
-        total = total + ref[:, :size].astype(F32)
-        gram = gram + joined(ref, size, rank)
+        total = total + body(ref[...], rank, size).astype(F32)
+        gram = gram + gram_of(ref[...], rank)
     pack(out_ref, total, gram)
 
 
 def summed(z_me, count, msg_refs, scr, rank, size):
     for shift in range(count):
         scr[partner(z_me, shift, count)] = msg_refs[shift][...]
-    total, gram = scr[0, :, :size].astype(F32), joined(scr[0], size, rank)
+    total, gram = body(scr[0], rank, size).astype(F32), gram_of(scr[0], rank)
     for at in range(1, count):
-        total = total + scr[at, :, :size].astype(F32)
-        gram = gram + joined(scr[at], size, rank)
+        total = total + body(scr[at], rank, size).astype(F32)
+        gram = gram + gram_of(scr[at], rank)
     return total, gram
 
 
@@ -464,7 +486,7 @@
         in_specs=[anywhere],
     )
     sig = [own_sig] + [row_shift(part, shift + 1) for shift, part in enumerate(out_sigs)]
-    msg = ((rank, size + 2 * rank), BF16)
+    msg = (message(rank, size), BF16)
     piece = ((rank, size), F32)
     update_outs = [((rank, frames), F32), ((rank, rank), F32)]
     update_outs += [((rank, size + rank), F32)] * ((rows - 1) * (subs - 1))
@@ -483,7 +505,7 @@
             pltpu.VMEM((cl, frames + TAPS), BF16),
             pltpu.VMEM(((blocks - 1) * cl, 2 * TAPS), BF16),
             pltpu.SemaphoreType.DMA((3,)),
-            pltpu.SemaphoreType.DMA((GROUPS,)),
+            pltpu.SemaphoreType.DMA((len(CUTS) - 1,)),
         ],
         in_specs=[whole] + [anywhere] * 4,
         limit=8,
@@ -501,7 +523,7 @@
     w_piece, w_msg = call(
         reorder_kernel,
         [vmem(w_own), order, edge],
-        [piece, ((rank, NF * cl + 2 * rank), BF16)],
+        [piece, (message(rank, NF * cl), BF16)],
         in_specs=[whole, whole, anywhere],
     )
     w_msgs = [w_msg] + [row_shift(w_msg, shift) for shift in range(1, rows)]
@@ -595,7 +617,7 @@
     )
     (synergies,) = call(
         sum_kernel,
-        [wide, part] + [sub_shift(part, dc) for dc in range(1, subs)],
+        [hbm(wide), part] + [sub_shift(part, dc) for dc in range(1, subs)],
         [pltpu.HBM((rank, NF * cl), F32)],
         [pltpu.VMEM((rank, NF * cl), F32), pltpu.SemaphoreType.DMA],
         in_specs=[anywhere] + [whole] * subs,

time: 63.9 us -> 62.5 us (0.978)
  local copies, waits for them, and re-layouts: 1.04 us -> 0 us
    unnamed x2 -> x0, local copies, waits for them, and re-layouts: 1.04 us -> none
  transfers between devices with their start and end apart: 20 -> 20, of which waited for: 10 -> 11; matrix products, arithmetic and copies ran while one was open for 0% -> 0% of each run, Pallas kernels for 27% -> 27%
where the time goes in v10:
time: 62.5 us; the launch traced here: 62.3 us
  Pallas kernels  24.9 us (40%)
  starting transfers between devices  19.5 us (31%)
  waiting for transfers between devices  17 us (27%)
  between operations  0.97 us (2%)
    pallas_call x20, Pallas kernels, call(): pl.pallas_call(kernel, out_shape=[jax.ShapeDtypeStruct(*out) if isinstanc...  24.9 us
    ppermute x6, starting transfers between devices, frm_shift(): lax.ppermute(value, 'frm', [(partner(i, shift, frms), i) for i in range(f...  9.44 us
    ppermute x6, waiting for transfers between devices, row_shift(): lax.ppermute(value, 'row', [(i, (i + shift) % rows) for i in range(rows)])  7.27 us
    ppermute x6, starting transfers between devices, row_shift(): lax.ppermute(value, 'row', [(i, (i + shift) % rows) for i in range(rows)])  6.84 us
    ppermute x6, waiting for transfers between devices, frm_shift(): lax.ppermute(value, 'frm', [(partner(i, shift, frms), i) for i in range(f...  6.79 us
    ppermute x7, waiting for transfers between devices, sub_shift(): lax.ppermute(value, 'sub', [(i, (i + shift) % subs) for i in range(subs)])  2.91 us
    ppermute x7, starting transfers between devices, sub_shift(): lax.ppermute(value, 'sub', [(i, (i + shift) % subs) for i in range(subs)])  2.52 us
  transfers between devices with their start and end apart: 20, of which 11 were waited for; matrix products, arithmetic and copies ran while one was open for 0% of the time, Pallas kernels for 27%

profile of v10, /device:TPU:0, one launch (start us, length us, event | category | flops | bytes accessed | tf_op | source)
XLA Modules:
  0.0 62.3 jit_solution(4625177649173271555)
XLA Ops:
  0.6 1.0 %shard_map.68 = (bf16[32,2176]{1,0:T(8,128)(2,1)S(1)}, bf16[32,2176]{1,0:T(8,128)(2,1)S(1)}) custom-call(bf16[32,4096]{1,0:T(8,128)(2,1)} %sig_hbm.1), custom_call_target="tpu_custom_call" | custom-call | tf_op jit(solution)/shard_map/pallas_call | solution.py:430
  1.7 3.0 %collective-permute-start = (bf16[32,2176]{1,0:T(8,128)(2,1)S(1)}, bf16[32,2176]{1,0:T(8,128)(2,1)S(1)}, u32[]{:S(2)}, u32[]{:S(2)}) collective-permute-start(bf16[32,2176]{1,0:T(8,128)(2,1)S(1)} %get-tuple-element.34), channel_id=1, source_target_pairs={{0,2},{2,0},{1,3},{3,1},{4,6},{6,4},{5,7},{7,5},{8,10},{10,8},{9,1... | collective-permute-start | bytes 417800 | tf_op jit(solution)/shard_map/ppermute | solution.py:470
  4.7 4.7 %shard_map.69 = (bf16[40,16,2,32,128]{4,3,2,1,0:T(8,128)(2,1)S(1)}, f32[32,1280]{1,0:T(8,128)S(1)}, f32[32,2048]{1,0:T(8,128)S(1)}, bf16[1280,1280]{1,0:T(8,128)(2,1)S(1)}, bf16[40,256,256]{2,1,0:T(8,128)(2,1)S(1)}) custom-call(bf16[32,2176]{1,0:T(8,128)(2,1)S(1)} %get-tuple-element.31.sig_ref.refs_0_, f32[32,1280]{1,0:T(8,128)} %bitcast.3, ...), custom_call_target="tpu_custom_call" | custom-call | flops 2684354560 | tf_op jit(solution)/shard_map/pallas_call | solution.py:430
  9.4 0.0 collective-permute-done.refs_0_.refs_1_
  9.4 0.7 %collective-permute-start.2 = (bf16[64,128]{1,0:T(8,128)(2,1)S(1)}, bf16[64,128]{1,0:T(8,128)(2,1)S(1)}, u32[]{:S(2)}, u32[]{:S(2)}) collective-permute-start(bf16[64,128]{1,0:T(8,128)(2,1)S(1)} %shard_map.70.refs_0_), channel_id=1, source_target_pairs={{2,1},{3,4},{6,5},{7,8},{10,9},{11,12},{14,13},{1,2},{4,3},{5,6},{... | collective-permute-start | bytes 49160 | tf_op jit(solution)/shard_map/ppermute | solution.py:522
  10.1 0.8 %shard_map.71 = (f32[32,640]{1,0:T(8,128)S(1)}, bf16[336,128]{1,0:T(8,128)(2,1)S(1)}) custom-call(f32[32,1280]{1,0:T(8,128)S(1)} %get-tuple-element.32.w_ref, bf16[1280,1280]{1,0:T(8,128)(2,1)S(1)} %get-tuple-element.33.order_ref, bf16[64,128]{1,0:T(8,128)(2,1)S(1)} %shard_map.70.refs_0_), custom_call_target="tpu_custom_call" | custom-call | tf_op jit(solution)/shard_map/pallas_call | solution.py:430
  10.9 2.4 %collective-permute-start.1 = (bf16[336,128]{1,0:T(8,128)(2,1)S(1)}, bf16[336,128]{1,0:T(8,128)(2,1)S(1)}, u32[]{:S(2)}, u32[]{:S(2)}) collective-permute-start(bf16[336,128]{1,0:T(8,128)(2,1)S(1)} %get-tuple-element.37.refs_0_), channel_id=1, source_target_pairs={{0,2},{2,0},{1,3},{3,1},{4,6},{6,4},{5,7},{7,5},{8,10},{10,8},{9,1... | collective-permute-start | bytes 258056 | tf_op jit(solution)/shard_map/ppermute | solution.py:470
  13.4 0.0 collective-permute-done.2.halo_ref
  13.4 3.5 %shard_map.72.refs_3_.s_ref.refs_2_.refs_6_ = bf16[40,16,2,32,128]{4,3,2,1,0:T(8,128)(2,1)S(1)} custom-call(bf16[64,128]{1,0:T(8,128)(2,1)S(1)} %collective-permute-done.2.halo_ref, bf16[40,256,256]{2,1,0:T(8,128)(2,1)S(1)} %get-tuple-element.39.tab_ref, bf16[32,2176]{1,0:T(8,128)(2,1)S(1)} %get-tuple-element.31.sig_ref.refs_0_, ...), custom_call_target="tpu_custom_call", output_to_operand_aliasing={{}: (4, {})} | custom-call | flops 5368709120 | tf_op jit(solution)/shard_map/pallas_call | solution.py:430
  16.9 0.0 collective-permute-done.1.refs_1_
  16.9 3.0 %shard_map.73 = (f32[32,2048]{1,0:T(8,128)S(1)}, f32[32,32]{1,0:T(8,128)S(1)}, f32[32,672]{1,0:T(8,128)S(1)}) custom-call(bf16[336,128]{1,0:T(8,128)(2,1)S(1)} %get-tuple-element.37.refs_0_, bf16[336,128]{1,0:T(8,128)(2,1)S(1)} %collective-permute-done.1.refs_1_, f32[32,2048]{1,0:T(8,128)S(1)} %get-tuple-element.38.refs_2_, ...), custom_call_target="tpu_custom_call" | custom-call | tf_op jit(solution)/shard_map/pallas_call | solution.py:430
  20.0 1.7 %collective-permute-start.3 = (f32[32,672]{1,0:T(8,128)S(1)}, f32[32,672]{1,0:T(8,128)S(1)}, u32[]{:S(2)}, u32[]{:S(2)}) collective-permute-start(f32[32,672]{1,0:T(8,128)S(1)} %get-tuple-element.43), channel_id=1, source_target_pairs={{0,1},{1,0},{2,3},{3,2},{4,5},{5,4},{6,7},{7,6},{8,9},{9,8},{10,11... | collective-permute-start | bytes 258056 | tf_op jit(solution)/shard_map/ppermute | solution.py:473
  21.7 1.6 %shard_map.74 = (f32[32,640]{1,0:T(8,128)S(1)}, f32[32,640]{1,0:T(8,128)S(1)}) custom-call(f32[32,2048]{1,0:T(8,128)S(1)} %get-tuple-element.40.h_ref.refs_5_, bf16[40,16,2,32,128]{4,3,2,1,0:T(8,128)(2,1)S(1)} %shard_map.72.refs_3_.s_ref.refs_2_.refs_6_), custom_call_target="tpu_custom_call" | custom-call | flops 1342177280 | tf_op jit(solution)/shard_map/pallas_call | solution.py:430
  23.3 0.1 collective-permute-start.4
  23.4 0.0 collective-permute-done.3.refs_2_
  23.4 0.1 shard_map.75
  23.5 0.8 %collective-permute-start.5 = (bf16[176,128]{1,0:T(8,128)(2,1)S(1)}, bf16[176,128]{1,0:T(8,128)(2,1)S(1)}, u32[]{:S(2)}, u32[]{:S(2)}) collective-permute-start(bf16[176,128]{1,0:T(8,128)(2,1)S(1)} %get-tuple-element.44.refs_0_), channel_id=1, source_target_pairs={{0,2},{2,0},{1,3},{3,1},{4,6},{6,4},{5,7},{7,5},{8,10},{10,8},{9,1... | collective-permute-start | bytes 135176 | tf_op jit(solution)/shard_map/ppermute | solution.py:470
  24.3 0.8 %shard_map.76.own_ref = f32[32,640]{1,0:T(8,128)S(1)} custom-call(f32[32,2048]{1,0:T(8,128)S(1)} %get-tuple-element.40.h_ref.refs_5_, bf16[40,16,2,32,128]{4,3,2,1,0:T(8,128)(2,1)S(1)} %shard_map.72.refs_3_.s_ref.refs_2_.refs_6_, bf16[176,128]{1,0:T(8,128)(2,1)S(1)} %get-tuple-element.44.refs_0_), custom_call_target="tpu_custom_call" | custom-call | flops 1 | tf_op jit(solution)/shard_map/pallas_call | solution.py:430
  25.1 0.0 collective-permute-done.4.refs_0_
  25.1 2.4 %collective-permute-done.5.refs_1_ = bf16[176,128]{1,0:T(8,128)(2,1)S(1)} collective-permute-done((bf16[176,128]{1,0:T(8,128)(2,1)S(1)}, bf16[176,128]{1,0:T(8,128)(2,1)S(1)}, u32[]{:S(2)}, u32[]{:S(2)}) %collective-permute-start.5) | collective-permute-done | bytes 45088 | tf_op jit(solution)/shard_map/ppermute | solution.py:470
  27.5 0.2 shard_map.77.refs_0_
  27.7 4.4 %collective-permute-start.8 = (bf16[176,128]{1,0:T(8,128)(2,1)S(1)}, bf16[176,128]{1,0:T(8,128)(2,1)S(1)}, u32[]{:S(2)}, u32[]{:S(2)}) collective-permute-start(bf16[176,128]{1,0:T(8,128)(2,1)S(1)} %shard_map.77.refs_0_), channel_id=1, source_target_pairs={{12,0},{8,4},{4,8},{0,12},{13,1},{9,5},{5,9},{1,13},{14,2},{10,6},... | collective-permute-start | bytes 135176 | tf_op jit(solution)/shard_map/ppermute | solution.py:476
  32.2 0.0 collective-permute-start.7
  32.2 0.6 %collective-permute-start.6 = (bf16[176,128]{1,0:T(8,128)(2,1)S(1)}, bf16[176,128]{1,0:T(8,128)(2,1)S(1)}, u32[]{:S(2)}, u32[]{:S(2)}) collective-permute-start(bf16[176,128]{1,0:T(8,128)(2,1)S(1)} %shard_map.77.refs_0_), channel_id=1, source_target_pairs={{4,0},{0,4},{12,8},{8,12},{5,1},{1,5},{13,9},{9,13},{6,2},{2,6},{1... | collective-permute-start | bytes 135176 | tf_op jit(solution)/shard_map/ppermute | solution.py:476
  32.8 1.5 %collective-permute-done.8.refs_3_ = bf16[176,128]{1,0:T(8,128)(2,1)S(1)} collective-permute-done((bf16[176,128]{1,0:T(8,128)(2,1)S(1)}, bf16[176,128]{1,0:T(8,128)(2,1)S(1)}, u32[]{:S(2)}, u32[]{:S(2)}) %collective-permute-start.8) | collective-permute-done | bytes 45088 | tf_op jit(solution)/shard_map/ppermute | solution.py:476
  34.3 2.8 %collective-permute-done.7.refs_2_ = bf16[176,128]{1,0:T(8,128)(2,1)S(1)} collective-permute-done((bf16[176,128]{1,0:T(8,128)(2,1)S(1)}, bf16[176,128]{1,0:T(8,128)(2,1)S(1)}, u32[]{:S(2)}, u32[]{:S(2)}) %collective-permute-start.7) | collective-permute-done | bytes 45088 | tf_op jit(solution)/shard_map/ppermute | solution.py:476
  37.1 0.0 collective-permute-done.6.refs_1_
  37.1 0.7 %shard_map.78 = (f32[32,640]{1,0:T(8,128)S(1)}, bf16[176,128]{1,0:T(8,128)(2,1)S(1)}) custom-call(f32[32,640]{1,0:T(8,128)S(1)} %get-tuple-element.36.w_ref, bf16[176,128]{1,0:T(8,128)(2,1)S(1)} %shard_map.77.refs_0_, bf16[176,128]{1,0:T(8,128)(2,1)S(1)} %collective-permute-done.6.refs_1_, bf16[176,128]{1,0:T(8,128)(2,1)S(1)} %collective-permute-done.7.refs_2_, ...), custom_call_target="tpu_custom_call" | custom-call | tf_op jit(solution)/shard_map/pallas_call | solution.py:430
  37.8 0.0 collective-permute-start.9
  37.8 0.1 collective-permute-start.10
  37.9 1.1 %collective-permute-done.9.refs_1_ = bf16[176,128]{1,0:T(8,128)(2,1)S(1)} collective-permute-done((bf16[176,128]{1,0:T(8,128)(2,1)S(1)}, bf16[176,128]{1,0:T(8,128)(2,1)S(1)}, u32[]{:S(2)}, u32[]{:S(2)}) %collective-permute-start.9) | collective-permute-done | bytes 45088 | tf_op jit(solution)/shard_map/ppermute | solution.py:473
  39.0 1.0 %shard_map.79.refs_4_ = f32[32,2048]{1,0:T(8,128)S(1)} custom-call(bf16[176,128]{1,0:T(8,128)(2,1)S(1)} %get-tuple-element.47.refs_0_, bf16[176,128]{1,0:T(8,128)(2,1)S(1)} %collective-permute-done.9.refs_1_, bf16[40,16,2,32,128]{4,3,2,1,0:T(8,128)(2,1)S(1)} %shard_map.72.refs_3_.s_ref.refs_2_.refs_6_), custom_call_target="tpu_custom_call" | custom-call | flops 1342177280 | tf_op jit(solution)/shard_map/pallas_call | solution.py:430
  40.0 1.9 %collective-permute-done.10.refs_2_ = bf16[176,128]{1,0:T(8,128)(2,1)S(1)} collective-permute-done((bf16[176,128]{1,0:T(8,128)(2,1)S(1)}, bf16[176,128]{1,0:T(8,128)(2,1)S(1)}, u32[]{:S(2)}, u32[]{:S(2)}) %collective-permute-start.10) | collective-permute-done | bytes 45088 | tf_op jit(solution)/shard_map/ppermute | solution.py:470
  41.9 0.0 collective-permute-start.11
  41.9 1.2 %collective-permute-done.11.refs_3_ = bf16[176,128]{1,0:T(8,128)(2,1)S(1)} collective-permute-done((bf16[176,128]{1,0:T(8,128)(2,1)S(1)}, bf16[176,128]{1,0:T(8,128)(2,1)S(1)}, u32[]{:S(2)}, u32[]{:S(2)}) %collective-permute-start.11) | collective-permute-done | bytes 45088 | tf_op jit(solution)/shard_map/ppermute | solution.py:473
  43.1 2.1 %shard_map.80 = (f32[32,2048]{1,0:T(8,128)S(1)}, f32[32,32]{1,0:T(8,128)S(1)}, f32[32,672]{1,0:T(8,128)S(1)}) custom-call(bf16[176,128]{1,0:T(8,128)(2,1)S(1)} %get-tuple-element.47.refs_0_, bf16[176,128]{1,0:T(8,128)(2,1)S(1)} %collective-permute-done.9.refs_1_, bf16[176,128]{1,0:T(8,128)(2,1)S(1)} %collective-permute-done.10.refs_2_, ...), custom_call_target="tpu_custom_call" | custom-call | tf_op jit(solution)/shard_map/pallas_call | solution.py:430
  45.3 0.2 collective-permute-start.12
  45.5 1.6 %shard_map.81 = (f32[32,640]{1,0:T(8,128)S(1)}, f32[32,640]{1,0:T(8,128)S(1)}) custom-call(f32[32,2048]{1,0:T(8,128)S(1)} %get-tuple-element.57.h_ref.refs_0_, bf16[40,16,2,32,128]{4,3,2,1,0:T(8,128)(2,1)S(1)} %shard_map.72.refs_3_.s_ref.refs_2_.refs_6_), custom_call_target="tpu_custom_call" | custom-call | flops 1342177280 | tf_op jit(solution)/shard_map/pallas_call | solution.py:430
  47.1 0.4 collective-permute-start.13
  47.5 0.0 collective-permute-done.12.refs_2_
  47.5 0.1 shard_map.82
  47.6 0.2 collective-permute-start.14
  47.9 0.8 %shard_map.83.own_ref = f32[32,640]{1,0:T(8,128)S(1)} custom-call(f32[32,2048]{1,0:T(8,128)S(1)} %get-tuple-element.57.h_ref.refs_0_, bf16[40,16,2,32,128]{4,3,2,1,0:T(8,128)(2,1)S(1)} %shard_map.72.refs_3_.s_ref.refs_2_.refs_6_, bf16[176,128]{1,0:T(8,128)(2,1)S(1)} %get-tuple-element.54.refs_0_), custom_call_target="tpu_custom_call" | custom-call | flops 1 | tf_op jit(solution)/shard_map/pallas_call | solution.py:430
  48.7 0.0 collective-permute-done.13.refs_0_
  48.7 3.0 %collective-permute-done.14.refs_1_ = bf16[176,128]{1,0:T(8,128)(2,1)S(1)} collective-permute-done((bf16[176,128]{1,0:T(8,128)(2,1)S(1)}, bf16[176,128]{1,0:T(8,128)(2,1)S(1)}, u32[]{:S(2)}, u32[]{:S(2)}) %collective-permute-start.14) | collective-permute-done | bytes 45088 | tf_op jit(solution)/shard_map/ppermute | solution.py:470
  51.7 0.2 shard_map.84.refs_0_
  51.9 0.2 collective-permute-start.15
  52.1 1.4 %collective-permute-start.18 = (bf16[176,128]{1,0:T(8,128)(2,1)S(1)}, bf16[176,128]{1,0:T(8,128)(2,1)S(1)}, u32[]{:S(2)}, u32[]{:S(2)}) collective-permute-start(bf16[176,128]{1,0:T(8,128)(2,1)S(1)} %shard_map.84.refs_0_), channel_id=1, source_target_pairs={{12,0},{8,4},{4,8},{0,12},{13,1},{9,5},{5,9},{1,13},{14,2},{10,6},... | collective-permute-start | bytes 135176 | tf_op jit(solution)/shard_map/ppermute | solution.py:476
  53.6 0.6 collective-permute-start.17
  54.1 2.4 %collective-permute-start.16 = (bf16[176,128]{1,0:T(8,128)(2,1)S(1)}, bf16[176,128]{1,0:T(8,128)(2,1)S(1)}, u32[]{:S(2)}, u32[]{:S(2)}) collective-permute-start(bf16[176,128]{1,0:T(8,128)(2,1)S(1)} %shard_map.84.refs_0_), channel_id=1, source_target_pairs={{4,0},{0,4},{12,8},{8,12},{5,1},{1,5},{13,9},{9,13},{6,2},{2,6},{1... | collective-permute-start | bytes 135176 | tf_op jit(solution)/shard_map/ppermute | solution.py:476
  56.5 1.5 %collective-permute-done.18.refs_3_ = bf16[176,128]{1,0:T(8,128)(2,1)S(1)} collective-permute-done((bf16[176,128]{1,0:T(8,128)(2,1)S(1)}, bf16[176,128]{1,0:T(8,128)(2,1)S(1)}, u32[]{:S(2)}, u32[]{:S(2)}) %collective-permute-start.18) | collective-permute-done | bytes 45088 | tf_op jit(solution)/shard_map/ppermute | solution.py:476
  58.0 0.6 collective-permute-done.17.refs_2_
  58.6 0.4 collective-permute-done.16.refs_1_
  59.0 1.0 %shard_map.86.refs_0_ = f32[32,1280]{1,0:T(8,128)S(1)} custom-call(f32[32,640]{1,0:T(8,128)S(1)} %get-tuple-element.58.w_ref, bf16[1280,1280]{1,0:T(8,128)(2,1)S(1)} %get-tuple-element.33.order_ref, bf16[176,128]{1,0:T(8,128)(2,1)S(1)} %shard_map.84.refs_0_, bf16[176,128]{1,0:T(8,128)(2,1)S(1)} %collective-permute-done.16.refs_1_, ...), custom_call_target="tpu_custom_call" | custom-call | tf_op jit(solution)/shard_map/pallas_call | solution.py:430
  60.0 0.1 collective-permute-start.19
  60.1 0.0 collective-permute-done.15.refs_1_
  60.1 0.8 %shard_map.85._ = f32[32,4096]{1,0:T(8,128)} custom-call(f32[32,2048]{1,0:T(8,128)S(1)} %get-tuple-element.57.h_ref.refs_0_, f32[32,2048]{1,0:T(8,128)S(1)} %collective-permute-done.15.refs_1_), custom_call_target="tpu_custom_call" | custom-call | tf_op jit(solution)/shard_map/pallas_call | solution.py:430
  60.9 0.5 collective-permute-done.19.refs_1_
  61.4 0.7 %shard_map.87 = f32[32,1280]{1,0:T(8,128)} custom-call(f32[32,4096]{1,0:T(8,128)} %shard_map.85._, f32[32,1280]{1,0:T(8,128)S(1)} %shard_map.86.refs_0_, f32[32,1280]{1,0:T(8,128)S(1)} %collective-permute-done.19.refs_1_), custom_call_target="tpu_custom_call" | custom-call | tf_op jit(solution)/shard_map/pallas_call | solution.py:430
  (1 shorter events, 0.0 us)
Async XLA Ops:
  1.7 7.7 %collective-permute-start = (bf16[32,2176]{1,0:T(8,128)(2,1)S(1)}, bf16[32,2176]{1,0:T(8,128)(2,1)S(1)}, u32[]{:S(2)}, u32[]{:S(2)}) collective-permute-start(bf16[32,2176]{1,0:T(8,128)(2,1)S(1)} %get-tuple-element.34), channel_id=1, source_target_pairs={{0,2},{2,0},{1,3},{3,1},{4,6},{6,4},{5,7},{7,5},{8,10},{10,8},{9,1... | collective-permute-start | bytes 417800 | tf_op jit(solution)/shard_map/ppermute | solution.py:470
  9.4 4.0 %collective-permute-start.2 = (bf16[64,128]{1,0:T(8,128)(2,1)S(1)}, bf16[64,128]{1,0:T(8,128)(2,1)S(1)}, u32[]{:S(2)}, u32[]{:S(2)}) collective-permute-start(bf16[64,128]{1,0:T(8,128)(2,1)S(1)} %shard_map.70.refs_0_), channel_id=1, source_target_pairs={{2,1},{3,4},{6,5},{7,8},{10,9},{11,12},{14,13},{1,2},{4,3},{5,6},{... | collective-permute-start | bytes 49160 | tf_op jit(solution)/shard_map/ppermute | solution.py:522
  10.9 6.0 %collective-permute-start.1 = (bf16[336,128]{1,0:T(8,128)(2,1)S(1)}, bf16[336,128]{1,0:T(8,128)(2,1)S(1)}, u32[]{:S(2)}, u32[]{:S(2)}) collective-permute-start(bf16[336,128]{1,0:T(8,128)(2,1)S(1)} %get-tuple-element.37.refs_0_), channel_id=1, source_target_pairs={{0,2},{2,0},{1,3},{3,1},{4,6},{6,4},{5,7},{7,5},{8,10},{10,8},{9,1... | collective-permute-start | bytes 258056 | tf_op jit(solution)/shard_map/ppermute | solution.py:470
  20.0 3.4 %collective-permute-start.3 = (f32[32,672]{1,0:T(8,128)S(1)}, f32[32,672]{1,0:T(8,128)S(1)}, u32[]{:S(2)}, u32[]{:S(2)}) collective-permute-start(f32[32,672]{1,0:T(8,128)S(1)} %get-tuple-element.43), channel_id=1, source_target_pairs={{0,1},{1,0},{2,3},{3,2},{4,5},{5,4},{6,7},{7,6},{8,9},{9,8},{10,11... | collective-permute-start | bytes 258056 | tf_op jit(solution)/shard_map/ppermute | solution.py:473
  23.3 1.8 %collective-permute-start.4 = (f32[32,640]{1,0:T(8,128)S(1)}, f32[32,640]{1,0:T(8,128)S(1)}, u32[]{:S(2)}, u32[]{:S(2)}) collective-permute-start(f32[32,640]{1,0:T(8,128)S(1)} %get-tuple-element.46), channel_id=1, source_target_pairs={{0,1},{1,0},{2,3},{3,2},{4,5},{5,4},{6,7},{7,6},{8,9},{9,8},{10,11... | collective-permute-start | bytes 245768 | tf_op jit(solution)/shard_map/ppermute | solution.py:473
  23.5 4.1 %collective-permute-start.5 = (bf16[176,128]{1,0:T(8,128)(2,1)S(1)}, bf16[176,128]{1,0:T(8,128)(2,1)S(1)}, u32[]{:S(2)}, u32[]{:S(2)}) collective-permute-start(bf16[176,128]{1,0:T(8,128)(2,1)S(1)} %get-tuple-element.44.refs_0_), channel_id=1, source_target_pairs={{0,2},{2,0},{1,3},{3,1},{4,6},{6,4},{5,7},{7,5},{8,10},{10,8},{9,1... | collective-permute-start | bytes 135176 | tf_op jit(solution)/shard_map/ppermute | solution.py:470
  27.7 6.6 %collective-permute-start.8 = (bf16[176,128]{1,0:T(8,128)(2,1)S(1)}, bf16[176,128]{1,0:T(8,128)(2,1)S(1)}, u32[]{:S(2)}, u32[]{:S(2)}) collective-permute-start(bf16[176,128]{1,0:T(8,128)(2,1)S(1)} %shard_map.77.refs_0_), channel_id=1, source_target_pairs={{12,0},{8,4},{4,8},{0,12},{13,1},{9,5},{5,9},{1,13},{14,2},{10,6},... | collective-permute-start | bytes 135176 | tf_op jit(solution)/shard_map/ppermute | solution.py:476
  32.2 4.9 %collective-permute-start.7 = (bf16[176,128]{1,0:T(8,128)(2,1)S(1)}, bf16[176,128]{1,0:T(8,128)(2,1)S(1)}, u32[]{:S(2)}, u32[]{:S(2)}) collective-permute-start(bf16[176,128]{1,0:T(8,128)(2,1)S(1)} %shard_map.77.refs_0_), channel_id=1, source_target_pairs={{8,0},{12,4},{0,8},{4,12},{9,1},{13,5},{1,9},{5,13},{10,2},{14,6},... | collective-permute-start | bytes 135176 | tf_op jit(solution)/shard_map/ppermute | solution.py:476
  32.2 4.9 %collective-permute-start.6 = (bf16[176,128]{1,0:T(8,128)(2,1)S(1)}, bf16[176,128]{1,0:T(8,128)(2,1)S(1)}, u32[]{:S(2)}, u32[]{:S(2)}) collective-permute-start(bf16[176,128]{1,0:T(8,128)(2,1)S(1)} %shard_map.77.refs_0_), channel_id=1, source_target_pairs={{4,0},{0,4},{12,8},{8,12},{5,1},{1,5},{13,9},{9,13},{6,2},{2,6},{1... | collective-permute-start | bytes 135176 | tf_op jit(solution)/shard_map/ppermute | solution.py:476
  37.8 1.2 %collective-permute-start.9 = (bf16[176,128]{1,0:T(8,128)(2,1)S(1)}, bf16[176,128]{1,0:T(8,128)(2,1)S(1)}, u32[]{:S(2)}, u32[]{:S(2)}) collective-permute-start(bf16[176,128]{1,0:T(8,128)(2,1)S(1)} %get-tuple-element.47.refs_0_), channel_id=1, source_target_pairs={{0,1},{1,0},{2,3},{3,2},{4,5},{5,4},{6,7},{7,6},{8,9},{9,8},{10,11... | collective-permute-start | bytes 135176 | tf_op jit(solution)/shard_map/ppermute | solution.py:473
  37.8 4.1 %collective-permute-start.10 = (bf16[176,128]{1,0:T(8,128)(2,1)S(1)}, bf16[176,128]{1,0:T(8,128)(2,1)S(1)}, u32[]{:S(2)}, u32[]{:S(2)}) collective-permute-start(bf16[176,128]{1,0:T(8,128)(2,1)S(1)} %get-tuple-element.47.refs_0_), channel_id=1, source_target_pairs={{0,2},{2,0},{1,3},{3,1},{4,6},{6,4},{5,7},{7,5},{8,10},{10,8},{9,1... | collective-permute-start | bytes 135176 | tf_op jit(solution)/shard_map/ppermute | solution.py:470
  41.9 1.2 %collective-permute-start.11 = (bf16[176,128]{1,0:T(8,128)(2,1)S(1)}, bf16[176,128]{1,0:T(8,128)(2,1)S(1)}, u32[]{:S(2)}, u32[]{:S(2)}) collective-permute-start(bf16[176,128]{1,0:T(8,128)(2,1)S(1)} %collective-permute-done.10.refs_2_), channel_id=1, source_target_pairs={{0,1},{1,0},{2,3},{3,2},{4,5},{5,4},{6,7},{7,6},{8,9},{9,8},{10,11... | collective-permute-start | bytes 135176 | tf_op jit(solution)/shard_map/ppermute | solution.py:473
  45.3 2.2 %collective-permute-start.12 = (f32[32,672]{1,0:T(8,128)S(1)}, f32[32,672]{1,0:T(8,128)S(1)}, u32[]{:S(2)}, u32[]{:S(2)}) collective-permute-start(f32[32,672]{1,0:T(8,128)S(1)} %get-tuple-element.53), channel_id=1, source_target_pairs={{0,1},{1,0},{2,3},{3,2},{4,5},{5,4},{6,7},{7,6},{8,9},{9,8},{10,11... | collective-permute-start | bytes 258056 | tf_op jit(solution)/shard_map/ppermute | solution.py:473
  47.1 1.6 %collective-permute-start.13 = (f32[32,640]{1,0:T(8,128)S(1)}, f32[32,640]{1,0:T(8,128)S(1)}, u32[]{:S(2)}, u32[]{:S(2)}) collective-permute-start(f32[32,640]{1,0:T(8,128)S(1)} %get-tuple-element.56), channel_id=1, source_target_pairs={{0,1},{1,0},{2,3},{3,2},{4,5},{5,4},{6,7},{7,6},{8,9},{9,8},{10,11... | collective-permute-start | bytes 245768 | tf_op jit(solution)/shard_map/ppermute | solution.py:473
  47.6 4.1 %collective-permute-start.14 = (bf16[176,128]{1,0:T(8,128)(2,1)S(1)}, bf16[176,128]{1,0:T(8,128)(2,1)S(1)}, u32[]{:S(2)}, u32[]{:S(2)}) collective-permute-start(bf16[176,128]{1,0:T(8,128)(2,1)S(1)} %get-tuple-element.54.refs_0_), channel_id=1, source_target_pairs={{0,2},{2,0},{1,3},{3,1},{4,6},{6,4},{5,7},{7,5},{8,10},{10,8},{9,1... | collective-permute-start | bytes 135176 | tf_op jit(solution)/shard_map/ppermute | solution.py:470
  51.9 8.2 %collective-permute-start.15 = (f32[32,2048]{1,0:T(8,128)S(1)}, f32[32,2048]{1,0:T(8,128)S(1)}, u32[]{:S(2)}, u32[]{:S(2)}) collective-permute-start(f32[32,2048]{1,0:T(8,128)S(1)} %get-tuple-element.57.h_ref.refs_0_), channel_id=1, source_target_pairs={{0,2},{2,0},{1,3},{3,1},{4,6},{6,4},{5,7},{7,5},{8,10},{10,8},{9,1... | collective-permute-start | bytes 786440 | tf_op jit(solution)/shard_map/ppermute | solution.py:470
  52.1 5.8 %collective-permute-start.18 = (bf16[176,128]{1,0:T(8,128)(2,1)S(1)}, bf16[176,128]{1,0:T(8,128)(2,1)S(1)}, u32[]{:S(2)}, u32[]{:S(2)}) collective-permute-start(bf16[176,128]{1,0:T(8,128)(2,1)S(1)} %shard_map.84.refs_0_), channel_id=1, source_target_pairs={{12,0},{8,4},{4,8},{0,12},{13,1},{9,5},{5,9},{1,13},{14,2},{10,6},... | collective-permute-start | bytes 135176 | tf_op jit(solution)/shard_map/ppermute | solution.py:476
  53.6 5.0 %collective-permute-start.17 = (bf16[176,128]{1,0:T(8,128)(2,1)S(1)}, bf16[176,128]{1,0:T(8,128)(2,1)S(1)}, u32[]{:S(2)}, u32[]{:S(2)}) collective-permute-start(bf16[176,128]{1,0:T(8,128)(2,1)S(1)} %shard_map.84.refs_0_), channel_id=1, source_target_pairs={{8,0},{12,4},{0,8},{4,12},{9,1},{13,5},{1,9},{5,13},{10,2},{14,6},... | collective-permute-start | bytes 135176 | tf_op jit(solution)/shard_map/ppermute | solution.py:476
  54.1 4.9 %collective-permute-start.16 = (bf16[176,128]{1,0:T(8,128)(2,1)S(1)}, bf16[176,128]{1,0:T(8,128)(2,1)S(1)}, u32[]{:S(2)}, u32[]{:S(2)}) collective-permute-start(bf16[176,128]{1,0:T(8,128)(2,1)S(1)} %shard_map.84.refs_0_), channel_id=1, source_target_pairs={{4,0},{0,4},{12,8},{8,12},{5,1},{1,5},{13,9},{9,13},{6,2},{2,6},{1... | collective-permute-start | bytes 135176 | tf_op jit(solution)/shard_map/ppermute | solution.py:476
  60.0 1.5 %collective-permute-start.19 = (f32[32,1280]{1,0:T(8,128)S(1)}, f32[32,1280]{1,0:T(8,128)S(1)}, u32[]{:S(2)}, u32[]{:S(2)}) collective-permute-start(f32[32,1280]{1,0:T(8,128)S(1)} %shard_map.86.refs_0_), channel_id=1, source_target_pairs={{0,1},{1,0},{2,3},{3,2},{4,5},{5,4},{6,7},{7,6},{8,9},{9,8},{10,11... | collective-permute-start | bytes 491528 | tf_op jit(solution)/shard_map/ppermute | solution.py:473

commit v11 on v10

--- a/solution.py
+++ b/solution.py
@@ -14,7 +14,8 @@
 TAPS = 128
 HALF = TAPS // 2
 LANES = 128
-CUTS = (0, 2, 8, 16, 24, 32, NF)
+CUTS = (8, 16, 24, 32, NF)
+AHEAD = CUTS[0]
 F32 = jnp.float32
 BF16 = jnp.bfloat16
 HIGH = lax.Precision.HIGHEST
@@ -119,15 +120,16 @@
             out_ref[at * cl : (at + 1) * cl, :] = ref[:, width - TAPS :]
 
 
-def cut_signal_kernel(rows, frames, sig_hbm, *refs):
-    out_refs, sems = refs[-rows - 1 : -1], refs[-1]
+def cut_kernel(rows, frames, sig_hbm, tab_hbm, *refs):
+    out_refs, (tab_ref, sems) = refs[:rows], refs[rows:]
     window, x_me = sig_hbm.shape[1], lax.axis_index("row")
     width = out_refs[0].shape[1]
     copies = []
-    for shift in range(rows):
+    for shift in reversed(range(rows)):
         target = lax.rem(x_me + shift, rows)
         begin = pl.multiple_of(jnp.clip(target * frames - TAPS, 0, window - width), TAPS)
         copies.append(pltpu.make_async_copy(sig_hbm.at[:, pl.ds(begin, width)], out_refs[shift], sems.at[shift]))
+    copies.append(pltpu.make_async_copy(tab_hbm.at[:AHEAD], tab_ref, sems.at[rows]))
     for copy in copies:
         copy.start()
     for copy in copies:
@@ -210,7 +212,11 @@
     return (co[:, :TAPS] * co[:, :TAPS] + co[:, TAPS:] * co[:, TAPS:]).astype(BF16)
 
 
-def own_spectra_kernel(rows, sig_ref, w_hbm, h_hbm, order_hbm, tab_hbm, *refs):
+def table_at(f, ahead_ref, tab_ref):
+    return ahead_ref[f] if f < AHEAD else tab_ref[f - AHEAD]
+
+
+def own_spectra_kernel(rows, sig_ref, ahead_ref, w_hbm, h_hbm, order_hbm, tab_hbm, *refs):
     s_ref, w_ref, old_ref, order_ref, tab_ref, xp_scr, x_scr, sems, tab_sems = refs
     _, blocks, _, cl, _ = s_ref.shape
     frames = blocks * TAPS
@@ -218,7 +224,7 @@
     mine = pl.ds(pl.multiple_of(x_me * frames, TAPS), frames)
 
     table = [
-        pltpu.make_async_copy(tab_hbm.at[begin:end], tab_ref.at[begin:end], tab_sems.at[at])
+        pltpu.make_async_copy(tab_hbm.at[begin:end], tab_ref.at[begin - AHEAD : end - AHEAD], tab_sems.at[at])
         for at, (begin, end) in enumerate(zip(CUTS, CUTS[1:]))
     ]
     later = [
@@ -237,16 +243,17 @@
     for f in range(NF):
         if f in CUTS:
             table[CUTS.index(f)].wait()
-        if f == CUTS[3]:
+        if f == CUTS[1]:
             for copy in later:
                 copy.start()
-        s_ref[f, pl.ds(first, blocks - 1), x_me] = power_of(x_scr, tab_ref[f]).reshape(blocks - 1, cl, TAPS)
+        power = power_of(x_scr, table_at(f, ahead_ref, tab_ref))
+        s_ref[f, pl.ds(first, blocks - 1), x_me] = power.reshape(blocks - 1, cl, TAPS)
     for copy in later:
         copy.wait()
 
 
-def other_spectra_kernel(rows, halo_ref, tab_ref, *refs):
-    sig_refs, (_, s_ref, xp_scr, x_scr) = refs[:rows], refs[rows:]
+def other_spectra_kernel(rows, halo_ref, ahead_ref, tab_ref, *refs):
+    sig_refs, (s_ref, xp_scr, x_scr) = refs[:rows], refs[-3:]
     _, blocks, _, cl, _ = s_ref.shape
     frames = blocks * TAPS
     x_me = lax.axis_index("row")
@@ -273,25 +280,54 @@
             x_scr[at : at + cl, :] = xp_scr[owners[shift], :, blk * TAPS : (blk + 2) * TAPS]
 
     for f in range(NF):
-        power = power_of(x_scr, tab_ref[f])
+        power = power_of(x_scr, table_at(f, ahead_ref, tab_ref))
         s_ref[f, outer, x_me] = power[:cl]
         for shift in range(1, rows):
             line = cl * (1 + (shift - 1) * blocks)
             s_ref[f, :, owners[shift]] = power[line : line + blocks * cl].reshape(blocks, cl, TAPS)
 
 
+def outer_pair(pairs):
+    return jnp.where(lax.axis_index("row") == 0, 0, pairs - 1)
+
+
+def pair_columns(pair):
+    return pl.ds(pl.multiple_of(pair * 2 * TAPS, 2 * TAPS), 2 * TAPS)
+
+
+def first_early_kernel(cl, w_ref, s_ref, num_ref):
+    rank, frames = num_ref.shape
+    pairs = frames // (2 * TAPS)
+    x_me = lax.axis_index("row")
+    w = body(w_ref[...], rank, NF * cl)
+    num_ref[:, pair_columns(outer_pair(pairs))] = jnp.zeros((rank, 2 * TAPS), F32)
+    for at in range(pairs - 1):
+        pair = at + jnp.where(x_me == 0, 1, 0)
+        rows_of = pair_rows(s_ref, slice(None), pair, x_me, cl)
+        num_ref[:, pair_columns(pair)] = jnp.dot(w, rows_of, preferred_element_type=F32)
+
+
 def first_kernel(rows, subs, cl, *refs):
     refs = list(refs)
     w_refs = [refs.pop(0) for _ in range(rows)]
-    h_ref, s_ref, h_out, h_gram_ref = (refs.pop(0) for _ in range(4))
+    early_ref, h_ref, s_ref, h_out, h_gram_ref = (refs.pop(0) for _ in range(5))
     msg_refs, num_scr = refs[:-1], refs[-1]
+    rank, frames = h_ref.shape
     x_me = lax.axis_index("row")
     parts, gram = [], jnp.zeros(h_gram_ref.shape, F32)
     for shift, ref in enumerate(w_refs):
-        parts.append((body(ref[...], h_ref.shape[0], NF * cl), lax.rem(x_me + rows - shift, rows)))
-        gram = gram + gram_of(ref[...], h_ref.shape[0])
-    numerators(parts, s_ref, num_scr, cl)
-    new_activations(h_ref[...], gram, num_scr[...], s_ref, h_out, h_gram_ref, msg_refs, rows, subs, cl)
+        parts.append((body(ref[...], rank, NF * cl), lax.rem(x_me + rows - shift, rows)))
+        gram = gram + gram_of(ref[...], rank)
+    if rows > 1:
+        numerators(parts[1:], s_ref, num_scr, cl)
+    else:
+        num_scr[...] = jnp.zeros_like(num_scr)
+    outer = outer_pair(frames // (2 * TAPS))
+    num_scr[:, pair_columns(outer)] += jnp.dot(
+        parts[0][0], pair_rows(s_ref, slice(None), outer, x_me, cl), preferred_element_type=F32
+    )
+    above = early_ref[...] + num_scr[...]
+    new_activations(h_ref[...], gram, above, s_ref, h_out, h_gram_ref, msg_refs, rows, subs, cl)
 
 
 def row_parts(rows, subs, cl, w_refs, w_scr, shifts):
@@ -478,28 +514,30 @@
     def place(x, at):
         return (at // subs * rows + x) * subs + at % subs
 
-    own_sig, *out_sigs = call(
-        functools.partial(cut_signal_kernel, rows, frames),
-        [hbm(signal)],
-        [((cl, width), BF16)] * rows,
-        [pltpu.SemaphoreType.DMA((rows,))],
-        in_specs=[anywhere],
-    )
+    table, order = hbm(jnp.asarray(toeplitz())), jnp.asarray(reorder(cl))
+    *cuts, ahead = call(
+        functools.partial(cut_kernel, rows, frames),
+        [hbm(signal), table],
+        [((cl, width), BF16)] * rows + [pltpu.VMEM((AHEAD,) + table.shape[1:], BF16)],
+        [pltpu.SemaphoreType.DMA((rows + 1,))],
+        in_specs=[anywhere] * 2,
+    )
+    own_sig, *out_sigs = cuts
+    ahead = vmem(ahead)
     sig = [own_sig] + [row_shift(part, shift + 1) for shift, part in enumerate(out_sigs)]
     msg = (message(rank, size), BF16)
     piece = ((rank, size), F32)
     update_outs = [((rank, frames), F32), ((rank, rank), F32)]
     update_outs += [((rank, size + rank), F32)] * ((rows - 1) * (subs - 1))
-    table, order = jnp.asarray(toeplitz()), jnp.asarray(reorder(cl))
     half_done, w_own, old, order, table = call(
         functools.partial(own_spectra_kernel, rows),
-        [own_sig, hbm(w_start.T), hbm(h_start), hbm(order), hbm(table)],
+        [own_sig, ahead, hbm(w_start.T), hbm(h_start), hbm(order), table],
         [
             pltpu.VMEM((NF, blocks, rows, cl, TAPS), BF16),
             pltpu.VMEM((rank, NF * cl), F32),
             pltpu.VMEM((rank, frames), F32),
             pltpu.VMEM(order.shape, BF16),
-            pltpu.VMEM(table.shape, BF16),
+            pltpu.VMEM((NF - AHEAD,) + table.shape[1:], BF16),
         ],
         [
             pltpu.VMEM((cl, frames + TAPS), BF16),
@@ -507,7 +545,7 @@
             pltpu.SemaphoreType.DMA((3,)),
             pltpu.SemaphoreType.DMA((len(CUTS) - 1,)),
         ],
-        in_specs=[whole] + [anywhere] * 4,
+        in_specs=[whole] * 2 + [anywhere] * 4,
         limit=8,
         cost=2 * NF * cl * frames * 4 * TAPS,
     )
@@ -527,18 +565,24 @@
         in_specs=[whole, whole, anywhere],
     )
     w_msgs = [w_msg] + [row_shift(w_msg, shift) for shift in range(1, rows)]
+    (early,) = call(
+        functools.partial(first_early_kernel, cl),
+        [w_msg, vmem(half_done)],
+        [((rank, frames), F32)],
+        cost=16 * NF * cl * frames * rank,
+    )
     (spectra,) = call(
         functools.partial(other_spectra_kernel, rows),
-        [halo, vmem(table)] + sig + [vmem(half_done)],
+        [halo, ahead, vmem(table)] + sig + [vmem(half_done), early],
         [pltpu.VMEM((NF, blocks, rows, cl, TAPS), BF16)],
         [
             pltpu.VMEM((rows, cl, frames + TAPS), BF16),
             pltpu.VMEM((((rows - 1) * blocks + 1) * cl, 2 * TAPS), BF16),
         ],
-        in_specs=[whole] * (rows + 2) + [anywhere],
+        in_specs=[whole] * (rows + 3) + [anywhere] * 2,
         limit=8,
         cost=2 * NF * chans * frames * 4 * TAPS,
-        aliases={rows + 2: 0},
+        aliases={rows + 3: 0},
     )
     spectra = vmem(spectra)
 
@@ -569,7 +613,7 @@
 
     activations, h_gram, *msgs = call(
         functools.partial(first_kernel, rows, subs, cl),
-        w_msgs + [vmem(old), spectra],
+        w_msgs + [early, vmem(old), spectra],
         update_outs,
         [pltpu.VMEM((rank, frames), F32)],
         limit=8,

time: 62.5 us -> 63.1 us (level)
  waiting for transfers between devices: 17 us -> 18.1 us
    ppermute x6, waiting for transfers between devices: 6.79 us -> 8.01 us  [frm_shift(): lax.ppermute(value, 'frm', [(partner(i, shift, frms), i) for i in range(f...]
    ppermute x6, starting transfers between devices: 9.44 us -> 8.78 us  [frm_shift(): lax.ppermute(value, 'frm', [(partner(i, shift, frms), i) for i in range(f...]
    pallas_call x20 -> x21, Pallas kernels: 24.9 us -> 24.8 us  [call(): pl.pallas_call(kernel, out_shape=[jax.ShapeDtypeStruct(*out) if isinstanc...]
  transfers between devices with their start and end apart: 20 -> 20, of which waited for: 11 -> 10; matrix products, arithmetic and copies ran while one was open for 0% -> 0% of each run, Pallas kernels for 27% -> 27%
where the time goes in v11:
time: 63.1 us; the launch traced here: 62.9 us
  Pallas kernels  24.8 us (39%)
  starting transfers between devices  19.1 us (30%)
  waiting for transfers between devices  18.1 us (29%)
  between operations  0.94 us (1%)
    pallas_call x21, Pallas kernels, call(): pl.pallas_call(kernel, out_shape=[jax.ShapeDtypeStruct(*out) if isinstanc...  24.8 us
    ppermute x6, starting transfers between devices, frm_shift(): lax.ppermute(value, 'frm', [(partner(i, shift, frms), i) for i in range(f...  8.78 us
    ppermute x6, waiting for transfers between devices, frm_shift(): lax.ppermute(value, 'frm', [(partner(i, shift, frms), i) for i in range(f...  8.01 us
    ppermute x6, waiting for transfers between devices, row_shift(): lax.ppermute(value, 'row', [(i, (i + shift) % rows) for i in range(rows)])  7.58 us
    ppermute x6, starting transfers between devices, row_shift(): lax.ppermute(value, 'row', [(i, (i + shift) % rows) for i in range(rows)])  7.24 us
    ppermute x7, waiting for transfers between devices, sub_shift(): lax.ppermute(value, 'sub', [(i, (i + shift) % subs) for i in range(subs)])  2.51 us
    ppermute x7, starting transfers between devices, sub_shift(): lax.ppermute(value, 'sub', [(i, (i + shift) % subs) for i in range(subs)])  2.45 us
  transfers between devices with their start and end apart: 20, of which 10 were waited for; matrix products, arithmetic and copies ran while one was open for 0% of the time, Pallas kernels for 27%

profile of v11, /device:TPU:0, one launch (start us, length us, event | category | flops | bytes accessed | tf_op | source)
XLA Modules:
  0.0 62.9 jit_solution(450257694999809076)
XLA Ops:
  0.6 1.4 %shard_map.68 = (bf16[32,2176]{1,0:T(8,128)(2,1)S(1)}, bf16[32,2176]{1,0:T(8,128)(2,1)S(1)}, bf16[8,256,256]{2,1,0:T(8,128)(2,1)S(1)}) custom-call(bf16[32,4096]{1,0:T(8,128)(2,1)} %sig_hbm.1, bf16[40,256,256]{2,1,0:T(8,128)(2,1)} %constant.4.clone.tab_hbm), custom_call_target="tpu_custom_call" | custom-call | tf_op jit(solution)/shard_map/pallas_call | solution.py:466
  2.1 3.0 %collective-permute-start = (bf16[32,2176]{1,0:T(8,128)(2,1)S(1)}, bf16[32,2176]{1,0:T(8,128)(2,1)S(1)}, u32[]{:S(2)}, u32[]{:S(2)}) collective-permute-start(bf16[32,2176]{1,0:T(8,128)(2,1)S(1)} %get-tuple-element.36), channel_id=1, source_target_pairs={{0,2},{2,0},{1,3},{3,1},{4,6},{6,4},{5,7},{7,5},{8,10},{10,8},{9,1... | collective-permute-start | bytes 417800 | tf_op jit(solution)/shard_map/ppermute | solution.py:506
  5.1 4.1 %shard_map.69 = (bf16[40,16,2,32,128]{4,3,2,1,0:T(8,128)(2,1)S(1)}, f32[32,1280]{1,0:T(8,128)S(1)}, f32[32,2048]{1,0:T(8,128)S(1)}, bf16[1280,1280]{1,0:T(8,128)(2,1)S(1)}, bf16[32,256,256]{2,1,0:T(8,128)(2,1)S(1)}) custom-call(bf16[32,2176]{1,0:T(8,128)(2,1)S(1)} %get-tuple-element.32.sig_ref.refs_0_, bf16[8,256,256]{2,1,0:T(8,128)(2,1)S(1)} %get-tuple-element.33.ahead_ref, ...), custom_call_target="tpu_custom_call" | custom-call | flops 2684354560 | tf_op jit(solution)/shard_map/pallas_call | solution.py:466
  9.2 0.0 collective-permute-done.refs_0_.refs_1_
  9.2 0.7 %collective-permute-start.2 = (bf16[64,128]{1,0:T(8,128)(2,1)S(1)}, bf16[64,128]{1,0:T(8,128)(2,1)S(1)}, u32[]{:S(2)}, u32[]{:S(2)}) collective-permute-start(bf16[64,128]{1,0:T(8,128)(2,1)S(1)} %shard_map.70.refs_0_), channel_id=1, source_target_pairs={{2,1},{3,4},{6,5},{7,8},{10,9},{11,12},{14,13},{1,2},{4,3},{5,6},{... | collective-permute-start | bytes 49160 | tf_op jit(solution)/shard_map/ppermute | solution.py:560
  9.9 0.8 %shard_map.71 = (f32[32,640]{1,0:T(8,128)S(1)}, bf16[336,128]{1,0:T(8,128)(2,1)S(1)}) custom-call(f32[32,1280]{1,0:T(8,128)S(1)} %get-tuple-element.34.w_ref, bf16[1280,1280]{1,0:T(8,128)(2,1)S(1)} %get-tuple-element.35.order_ref, bf16[64,128]{1,0:T(8,128)(2,1)S(1)} %shard_map.70.refs_0_), custom_call_target="tpu_custom_call" | custom-call | tf_op jit(solution)/shard_map/pallas_call | solution.py:466
  10.7 0.9 %shard_map.72.refs_3_.refs_2_ = f32[32,2048]{1,0:T(8,128)S(1)} custom-call(bf16[336,128]{1,0:T(8,128)(2,1)S(1)} %get-tuple-element.39.w_ref.refs_0_, bf16[40,16,2,32,128]{4,3,2,1,0:T(8,128)(2,1)S(1)} %get-tuple-element.37.refs_1_.s_ref.refs_2_), custom_call_target="tpu_custom_call" | custom-call | flops 1342177280 | tf_op jit(solution)/shard_map/pallas_call | solution.py:466
  11.6 2.6 %collective-permute-start.1 = (bf16[336,128]{1,0:T(8,128)(2,1)S(1)}, bf16[336,128]{1,0:T(8,128)(2,1)S(1)}, u32[]{:S(2)}, u32[]{:S(2)}) collective-permute-start(bf16[336,128]{1,0:T(8,128)(2,1)S(1)} %get-tuple-element.39.w_ref.refs_0_), channel_id=1, source_target_pairs={{0,2},{2,0},{1,3},{3,1},{4,6},{6,4},{5,7},{7,5},{8,10},{10,8},{9,1... | collective-permute-start | bytes 258056 | tf_op jit(solution)/shard_map/ppermute | solution.py:506
  14.2 0.0 collective-permute-done.2.halo_ref
  14.2 3.5 %shard_map.73.refs_4_.s_ref.refs_2_.refs_6_ = bf16[40,16,2,32,128]{4,3,2,1,0:T(8,128)(2,1)S(1)} custom-call(bf16[64,128]{1,0:T(8,128)(2,1)S(1)} %collective-permute-done.2.halo_ref, bf16[8,256,256]{2,1,0:T(8,128)(2,1)S(1)} %get-tuple-element.33.ahead_ref, bf16[32,256,256]{2,1,0:T(8,128)(2,1)S(1)} %get-tuple-element.41.tab_ref, ...), custom_call_target="tpu_custom_call", output_to_operand_aliasing={{}: (5, {})} | custom-call | flops 5368709120 | tf_op jit(solution)/shard_map/pallas_call | solution.py:466
  17.7 0.0 collective-permute-done.1.refs_1_
  17.7 2.2 %shard_map.74 = (f32[32,2048]{1,0:T(8,128)S(1)}, f32[32,32]{1,0:T(8,128)S(1)}, f32[32,672]{1,0:T(8,128)S(1)}) custom-call(bf16[336,128]{1,0:T(8,128)(2,1)S(1)} %get-tuple-element.39.w_ref.refs_0_, bf16[336,128]{1,0:T(8,128)(2,1)S(1)} %collective-permute-done.1.refs_1_, f32[32,2048]{1,0:T(8,128)S(1)} %shard_map.72.refs_3_.refs_2_, ...), custom_call_target="tpu_custom_call" | custom-call | tf_op jit(solution)/shard_map/pallas_call | solution.py:466
  19.9 1.7 %collective-permute-start.3 = (f32[32,672]{1,0:T(8,128)S(1)}, f32[32,672]{1,0:T(8,128)S(1)}, u32[]{:S(2)}, u32[]{:S(2)}) collective-permute-start(f32[32,672]{1,0:T(8,128)S(1)} %get-tuple-element.45), channel_id=1, source_target_pairs={{0,1},{1,0},{2,3},{3,2},{4,5},{5,4},{6,7},{7,6},{8,9},{9,8},{10,11... | collective-permute-start | bytes 258056 | tf_op jit(solution)/shard_map/ppermute | solution.py:509
  21.6 1.6 %shard_map.75 = (f32[32,640]{1,0:T(8,128)S(1)}, f32[32,640]{1,0:T(8,128)S(1)}) custom-call(f32[32,2048]{1,0:T(8,128)S(1)} %get-tuple-element.42.h_ref.refs_5_, bf16[40,16,2,32,128]{4,3,2,1,0:T(8,128)(2,1)S(1)} %shard_map.73.refs_4_.s_ref.refs_2_.refs_6_), custom_call_target="tpu_custom_call" | custom-call | flops 1342177280 | tf_op jit(solution)/shard_map/pallas_call | solution.py:466
  23.2 0.1 collective-permute-start.4
  23.3 0.0 collective-permute-done.3.refs_2_
  23.3 0.1 shard_map.76
  23.4 0.3 collective-permute-start.5
  23.7 0.8 %shard_map.77.own_ref = f32[32,640]{1,0:T(8,128)S(1)} custom-call(f32[32,2048]{1,0:T(8,128)S(1)} %get-tuple-element.42.h_ref.refs_5_, bf16[40,16,2,32,128]{4,3,2,1,0:T(8,128)(2,1)S(1)} %shard_map.73.refs_4_.s_ref.refs_2_.refs_6_, bf16[176,128]{1,0:T(8,128)(2,1)S(1)} %get-tuple-element.46.refs_0_), custom_call_target="tpu_custom_call" | custom-call | flops 1 | tf_op jit(solution)/shard_map/pallas_call | solution.py:466
  24.5 0.0 collective-permute-done.4.refs_0_
  24.5 2.9 %collective-permute-done.5.refs_1_ = bf16[176,128]{1,0:T(8,128)(2,1)S(1)} collective-permute-done((bf16[176,128]{1,0:T(8,128)(2,1)S(1)}, bf16[176,128]{1,0:T(8,128)(2,1)S(1)}, u32[]{:S(2)}, u32[]{:S(2)}) %collective-permute-start.5) | collective-permute-done | bytes 45088 | tf_op jit(solution)/shard_map/ppermute | solution.py:506
  27.4 0.2 shard_map.78.refs_0_
  27.6 1.6 %collective-permute-start.6 = (bf16[176,128]{1,0:T(8,128)(2,1)S(1)}, bf16[176,128]{1,0:T(8,128)(2,1)S(1)}, u32[]{:S(2)}, u32[]{:S(2)}) collective-permute-start(bf16[176,128]{1,0:T(8,128)(2,1)S(1)} %shard_map.78.refs_0_), channel_id=1, source_target_pairs={{4,0},{0,4},{12,8},{8,12},{5,1},{1,5},{13,9},{9,13},{6,2},{2,6},{1... | collective-permute-start | bytes 135176 | tf_op jit(solution)/shard_map/ppermute | solution.py:512
  29.2 2.4 %collective-permute-start.7 = (bf16[176,128]{1,0:T(8,128)(2,1)S(1)}, bf16[176,128]{1,0:T(8,128)(2,1)S(1)}, u32[]{:S(2)}, u32[]{:S(2)}) collective-permute-start(bf16[176,128]{1,0:T(8,128)(2,1)S(1)} %shard_map.78.refs_0_), channel_id=1, source_target_pairs={{8,0},{12,4},{0,8},{4,12},{9,1},{13,5},{1,9},{5,13},{10,2},{14,6},... | collective-permute-start | bytes 135176 | tf_op jit(solution)/shard_map/ppermute | solution.py:512
  31.7 0.4 collective-permute-start.8
  32.0 0.0 collective-permute-done.6.refs_1_
  32.0 3.1 %collective-permute-done.7.refs_2_ = bf16[176,128]{1,0:T(8,128)(2,1)S(1)} collective-permute-done((bf16[176,128]{1,0:T(8,128)(2,1)S(1)}, bf16[176,128]{1,0:T(8,128)(2,1)S(1)}, u32[]{:S(2)}, u32[]{:S(2)}) %collective-permute-start.7) | collective-permute-done | bytes 45088 | tf_op jit(solution)/shard_map/ppermute | solution.py:512
  35.2 2.4 %collective-permute-done.8.refs_3_ = bf16[176,128]{1,0:T(8,128)(2,1)S(1)} collective-permute-done((bf16[176,128]{1,0:T(8,128)(2,1)S(1)}, bf16[176,128]{1,0:T(8,128)(2,1)S(1)}, u32[]{:S(2)}, u32[]{:S(2)}) %collective-permute-start.8) | collective-permute-done | bytes 45088 | tf_op jit(solution)/shard_map/ppermute | solution.py:512
  37.5 0.7 %shard_map.79 = (f32[32,640]{1,0:T(8,128)S(1)}, bf16[176,128]{1,0:T(8,128)(2,1)S(1)}) custom-call(f32[32,640]{1,0:T(8,128)S(1)} %get-tuple-element.38.w_ref, bf16[176,128]{1,0:T(8,128)(2,1)S(1)} %shard_map.78.refs_0_, bf16[176,128]{1,0:T(8,128)(2,1)S(1)} %collective-permute-done.6.refs_1_, bf16[176,128]{1,0:T(8,128)(2,1)S(1)} %collective-permute-done.7.refs_2_, ...), custom_call_target="tpu_custom_call" | custom-call | tf_op jit(solution)/shard_map/pallas_call | solution.py:466
  38.2 0.0 collective-permute-start.9
  38.2 0.5 collective-permute-start.10
  38.7 0.7 %collective-permute-done.9.refs_1_ = bf16[176,128]{1,0:T(8,128)(2,1)S(1)} collective-permute-done((bf16[176,128]{1,0:T(8,128)(2,1)S(1)}, bf16[176,128]{1,0:T(8,128)(2,1)S(1)}, u32[]{:S(2)}, u32[]{:S(2)}) %collective-permute-start.9) | collective-permute-done | bytes 45088 | tf_op jit(solution)/shard_map/ppermute | solution.py:509
  39.4 1.0 %shard_map.80.refs_4_ = f32[32,2048]{1,0:T(8,128)S(1)} custom-call(bf16[176,128]{1,0:T(8,128)(2,1)S(1)} %get-tuple-element.49.refs_0_, bf16[176,128]{1,0:T(8,128)(2,1)S(1)} %collective-permute-done.9.refs_1_, bf16[40,16,2,32,128]{4,3,2,1,0:T(8,128)(2,1)S(1)} %shard_map.73.refs_4_.s_ref.refs_2_.refs_6_), custom_call_target="tpu_custom_call" | custom-call | flops 1342177280 | tf_op jit(solution)/shard_map/pallas_call | solution.py:466
  40.4 1.9 %collective-permute-done.10.refs_2_ = bf16[176,128]{1,0:T(8,128)(2,1)S(1)} collective-permute-done((bf16[176,128]{1,0:T(8,128)(2,1)S(1)}, bf16[176,128]{1,0:T(8,128)(2,1)S(1)}, u32[]{:S(2)}, u32[]{:S(2)}) %collective-permute-start.10) | collective-permute-done | bytes 45088 | tf_op jit(solution)/shard_map/ppermute | solution.py:506
  42.3 0.0 collective-permute-start.11
  42.3 1.2 %collective-permute-done.11.refs_3_ = bf16[176,128]{1,0:T(8,128)(2,1)S(1)} collective-permute-done((bf16[176,128]{1,0:T(8,128)(2,1)S(1)}, bf16[176,128]{1,0:T(8,128)(2,1)S(1)}, u32[]{:S(2)}, u32[]{:S(2)}) %collective-permute-start.11) | collective-permute-done | bytes 45088 | tf_op jit(solution)/shard_map/ppermute | solution.py:509
  43.6 2.1 %shard_map.81 = (f32[32,2048]{1,0:T(8,128)S(1)}, f32[32,32]{1,0:T(8,128)S(1)}, f32[32,672]{1,0:T(8,128)S(1)}) custom-call(bf16[176,128]{1,0:T(8,128)(2,1)S(1)} %get-tuple-element.49.refs_0_, bf16[176,128]{1,0:T(8,128)(2,1)S(1)} %collective-permute-done.9.refs_1_, bf16[176,128]{1,0:T(8,128)(2,1)S(1)} %collective-permute-done.10.refs_2_, ...), custom_call_target="tpu_custom_call" | custom-call | tf_op jit(solution)/shard_map/pallas_call | solution.py:466
  45.7 0.2 collective-permute-start.12
  45.9 1.6 %shard_map.82 = (f32[32,640]{1,0:T(8,128)S(1)}, f32[32,640]{1,0:T(8,128)S(1)}) custom-call(f32[32,2048]{1,0:T(8,128)S(1)} %get-tuple-element.59.h_ref.refs_0_, bf16[40,16,2,32,128]{4,3,2,1,0:T(8,128)(2,1)S(1)} %shard_map.73.refs_4_.s_ref.refs_2_.refs_6_), custom_call_target="tpu_custom_call" | custom-call | flops 1342177280 | tf_op jit(solution)/shard_map/pallas_call | solution.py:466
  47.6 0.4 collective-permute-start.13
  47.9 0.0 collective-permute-done.12.refs_2_
  47.9 0.1 shard_map.83
  48.0 0.4 collective-permute-start.14
  48.5 0.8 %shard_map.84.own_ref = f32[32,640]{1,0:T(8,128)S(1)} custom-call(f32[32,2048]{1,0:T(8,128)S(1)} %get-tuple-element.59.h_ref.refs_0_, bf16[40,16,2,32,128]{4,3,2,1,0:T(8,128)(2,1)S(1)} %shard_map.73.refs_4_.s_ref.refs_2_.refs_6_, bf16[176,128]{1,0:T(8,128)(2,1)S(1)} %get-tuple-element.56.refs_0_), custom_call_target="tpu_custom_call" | custom-call | flops 1 | tf_op jit(solution)/shard_map/pallas_call | solution.py:466
  49.3 0.0 collective-permute-done.13.refs_0_
  49.3 2.8 %collective-permute-done.14.refs_1_ = bf16[176,128]{1,0:T(8,128)(2,1)S(1)} collective-permute-done((bf16[176,128]{1,0:T(8,128)(2,1)S(1)}, bf16[176,128]{1,0:T(8,128)(2,1)S(1)}, u32[]{:S(2)}, u32[]{:S(2)}) %collective-permute-start.14) | collective-permute-done | bytes 45088 | tf_op jit(solution)/shard_map/ppermute | solution.py:506
  52.1 0.2 shard_map.85.refs_0_
  52.3 0.4 collective-permute-start.15
  52.7 0.0 collective-permute-start.16
  52.7 1.1 %collective-permute-start.17 = (bf16[176,128]{1,0:T(8,128)(2,1)S(1)}, bf16[176,128]{1,0:T(8,128)(2,1)S(1)}, u32[]{:S(2)}, u32[]{:S(2)}) collective-permute-start(bf16[176,128]{1,0:T(8,128)(2,1)S(1)} %shard_map.85.refs_0_), channel_id=1, source_target_pairs={{8,0},{12,4},{0,8},{4,12},{9,1},{13,5},{1,9},{5,13},{10,2},{14,6},... | collective-permute-start | bytes 135176 | tf_op jit(solution)/shard_map/ppermute | solution.py:512
  53.8 3.3 %collective-permute-start.18 = (bf16[176,128]{1,0:T(8,128)(2,1)S(1)}, bf16[176,128]{1,0:T(8,128)(2,1)S(1)}, u32[]{:S(2)}, u32[]{:S(2)}) collective-permute-start(bf16[176,128]{1,0:T(8,128)(2,1)S(1)} %shard_map.85.refs_0_), channel_id=1, source_target_pairs={{12,0},{8,4},{4,8},{0,12},{13,1},{9,5},{5,9},{1,13},{14,2},{10,6},... | collective-permute-start | bytes 135176 | tf_op jit(solution)/shard_map/ppermute | solution.py:512
  57.1 0.6 collective-permute-done.16.refs_1_
  57.7 0.0 collective-permute-done.17.refs_2_
  57.7 1.9 %collective-permute-done.18.refs_3_ = bf16[176,128]{1,0:T(8,128)(2,1)S(1)} collective-permute-done((bf16[176,128]{1,0:T(8,128)(2,1)S(1)}, bf16[176,128]{1,0:T(8,128)(2,1)S(1)}, u32[]{:S(2)}, u32[]{:S(2)}) %collective-permute-start.18) | collective-permute-done | bytes 45088 | tf_op jit(solution)/shard_map/ppermute | solution.py:512
  59.7 1.0 %shard_map.87.refs_0_ = f32[32,1280]{1,0:T(8,128)S(1)} custom-call(f32[32,640]{1,0:T(8,128)S(1)} %get-tuple-element.60.w_ref, bf16[1280,1280]{1,0:T(8,128)(2,1)S(1)} %get-tuple-element.35.order_ref, bf16[176,128]{1,0:T(8,128)(2,1)S(1)} %shard_map.85.refs_0_, bf16[176,128]{1,0:T(8,128)(2,1)S(1)} %collective-permute-done.16.refs_1_, ...), custom_call_target="tpu_custom_call" | custom-call | tf_op jit(solution)/shard_map/pallas_call | solution.py:466
  60.6 0.1 collective-permute-start.19
  60.7 0.0 collective-permute-done.15.refs_1_
  60.7 0.8 %shard_map.86._ = f32[32,4096]{1,0:T(8,128)} custom-call(f32[32,2048]{1,0:T(8,128)S(1)} %get-tuple-element.59.h_ref.refs_0_, f32[32,2048]{1,0:T(8,128)S(1)} %collective-permute-done.15.refs_1_), custom_call_target="tpu_custom_call" | custom-call | tf_op jit(solution)/shard_map/pallas_call | solution.py:466
  61.5 0.5 collective-permute-done.19.refs_1_
  62.1 0.7 %shard_map.88 = f32[32,1280]{1,0:T(8,128)} custom-call(f32[32,4096]{1,0:T(8,128)} %shard_map.86._, f32[32,1280]{1,0:T(8,128)S(1)} %shard_map.87.refs_0_, f32[32,1280]{1,0:T(8,128)S(1)} %collective-permute-done.19.refs_1_), custom_call_target="tpu_custom_call" | custom-call | tf_op jit(solution)/shard_map/pallas_call | solution.py:466
  (1 shorter events, 0.0 us)
Async XLA Ops:
  2.1 7.1 %collective-permute-start = (bf16[32,2176]{1,0:T(8,128)(2,1)S(1)}, bf16[32,2176]{1,0:T(8,128)(2,1)S(1)}, u32[]{:S(2)}, u32[]{:S(2)}) collective-permute-start(bf16[32,2176]{1,0:T(8,128)(2,1)S(1)} %get-tuple-element.36), channel_id=1, source_target_pairs={{0,2},{2,0},{1,3},{3,1},{4,6},{6,4},{5,7},{7,5},{8,10},{10,8},{9,1... | collective-permute-start | bytes 417800 | tf_op jit(solution)/shard_map/ppermute | solution.py:506
  9.2 5.0 %collective-permute-start.2 = (bf16[64,128]{1,0:T(8,128)(2,1)S(1)}, bf16[64,128]{1,0:T(8,128)(2,1)S(1)}, u32[]{:S(2)}, u32[]{:S(2)}) collective-permute-start(bf16[64,128]{1,0:T(8,128)(2,1)S(1)} %shard_map.70.refs_0_), channel_id=1, source_target_pairs={{2,1},{3,4},{6,5},{7,8},{10,9},{11,12},{14,13},{1,2},{4,3},{5,6},{... | collective-permute-start | bytes 49160 | tf_op jit(solution)/shard_map/ppermute | solution.py:560
  11.6 6.1 %collective-permute-start.1 = (bf16[336,128]{1,0:T(8,128)(2,1)S(1)}, bf16[336,128]{1,0:T(8,128)(2,1)S(1)}, u32[]{:S(2)}, u32[]{:S(2)}) collective-permute-start(bf16[336,128]{1,0:T(8,128)(2,1)S(1)} %get-tuple-element.39.w_ref.refs_0_), channel_id=1, source_target_pairs={{0,2},{2,0},{1,3},{3,1},{4,6},{6,4},{5,7},{7,5},{8,10},{10,8},{9,1... | collective-permute-start | bytes 258056 | tf_op jit(solution)/shard_map/ppermute | solution.py:506
  19.9 3.4 %collective-permute-start.3 = (f32[32,672]{1,0:T(8,128)S(1)}, f32[32,672]{1,0:T(8,128)S(1)}, u32[]{:S(2)}, u32[]{:S(2)}) collective-permute-start(f32[32,672]{1,0:T(8,128)S(1)} %get-tuple-element.45), channel_id=1, source_target_pairs={{0,1},{1,0},{2,3},{3,2},{4,5},{5,4},{6,7},{7,6},{8,9},{9,8},{10,11... | collective-permute-start | bytes 258056 | tf_op jit(solution)/shard_map/ppermute | solution.py:509
  23.2 1.3 %collective-permute-start.4 = (f32[32,640]{1,0:T(8,128)S(1)}, f32[32,640]{1,0:T(8,128)S(1)}, u32[]{:S(2)}, u32[]{:S(2)}) collective-permute-start(f32[32,640]{1,0:T(8,128)S(1)} %get-tuple-element.48), channel_id=1, source_target_pairs={{0,1},{1,0},{2,3},{3,2},{4,5},{5,4},{6,7},{7,6},{8,9},{9,8},{10,11... | collective-permute-start | bytes 245768 | tf_op jit(solution)/shard_map/ppermute | solution.py:509
  23.4 4.1 %collective-permute-start.5 = (bf16[176,128]{1,0:T(8,128)(2,1)S(1)}, bf16[176,128]{1,0:T(8,128)(2,1)S(1)}, u32[]{:S(2)}, u32[]{:S(2)}) collective-permute-start(bf16[176,128]{1,0:T(8,128)(2,1)S(1)} %get-tuple-element.46.refs_0_), channel_id=1, source_target_pairs={{0,2},{2,0},{1,3},{3,1},{4,6},{6,4},{5,7},{7,5},{8,10},{10,8},{9,1... | collective-permute-start | bytes 135176 | tf_op jit(solution)/shard_map/ppermute | solution.py:506
  27.6 4.4 %collective-permute-start.6 = (bf16[176,128]{1,0:T(8,128)(2,1)S(1)}, bf16[176,128]{1,0:T(8,128)(2,1)S(1)}, u32[]{:S(2)}, u32[]{:S(2)}) collective-permute-start(bf16[176,128]{1,0:T(8,128)(2,1)S(1)} %shard_map.78.refs_0_), channel_id=1, source_target_pairs={{4,0},{0,4},{12,8},{8,12},{5,1},{1,5},{13,9},{9,13},{6,2},{2,6},{1... | collective-permute-start | bytes 135176 | tf_op jit(solution)/shard_map/ppermute | solution.py:512
  29.2 5.9 %collective-permute-start.7 = (bf16[176,128]{1,0:T(8,128)(2,1)S(1)}, bf16[176,128]{1,0:T(8,128)(2,1)S(1)}, u32[]{:S(2)}, u32[]{:S(2)}) collective-permute-start(bf16[176,128]{1,0:T(8,128)(2,1)S(1)} %shard_map.78.refs_0_), channel_id=1, source_target_pairs={{8,0},{12,4},{0,8},{4,12},{9,1},{13,5},{1,9},{5,13},{10,2},{14,6},... | collective-permute-start | bytes 135176 | tf_op jit(solution)/shard_map/ppermute | solution.py:512
  31.7 5.8 %collective-permute-start.8 = (bf16[176,128]{1,0:T(8,128)(2,1)S(1)}, bf16[176,128]{1,0:T(8,128)(2,1)S(1)}, u32[]{:S(2)}, u32[]{:S(2)}) collective-permute-start(bf16[176,128]{1,0:T(8,128)(2,1)S(1)} %shard_map.78.refs_0_), channel_id=1, source_target_pairs={{12,0},{8,4},{4,8},{0,12},{13,1},{9,5},{5,9},{1,13},{14,2},{10,6},... | collective-permute-start | bytes 135176 | tf_op jit(solution)/shard_map/ppermute | solution.py:512
  38.2 1.2 %collective-permute-start.9 = (bf16[176,128]{1,0:T(8,128)(2,1)S(1)}, bf16[176,128]{1,0:T(8,128)(2,1)S(1)}, u32[]{:S(2)}, u32[]{:S(2)}) collective-permute-start(bf16[176,128]{1,0:T(8,128)(2,1)S(1)} %get-tuple-element.49.refs_0_), channel_id=1, source_target_pairs={{0,1},{1,0},{2,3},{3,2},{4,5},{5,4},{6,7},{7,6},{8,9},{9,8},{10,11... | collective-permute-start | bytes 135176 | tf_op jit(solution)/shard_map/ppermute | solution.py:509
  38.2 4.1 %collective-permute-start.10 = (bf16[176,128]{1,0:T(8,128)(2,1)S(1)}, bf16[176,128]{1,0:T(8,128)(2,1)S(1)}, u32[]{:S(2)}, u32[]{:S(2)}) collective-permute-start(bf16[176,128]{1,0:T(8,128)(2,1)S(1)} %get-tuple-element.49.refs_0_), channel_id=1, source_target_pairs={{0,2},{2,0},{1,3},{3,1},{4,6},{6,4},{5,7},{7,5},{8,10},{10,8},{9,1... | collective-permute-start | bytes 135176 | tf_op jit(solution)/shard_map/ppermute | solution.py:506
  42.3 1.2 %collective-permute-start.11 = (bf16[176,128]{1,0:T(8,128)(2,1)S(1)}, bf16[176,128]{1,0:T(8,128)(2,1)S(1)}, u32[]{:S(2)}, u32[]{:S(2)}) collective-permute-start(bf16[176,128]{1,0:T(8,128)(2,1)S(1)} %collective-permute-done.10.refs_2_), channel_id=1, source_target_pairs={{0,1},{1,0},{2,3},{3,2},{4,5},{5,4},{6,7},{7,6},{8,9},{9,8},{10,11... | collective-permute-start | bytes 135176 | tf_op jit(solution)/shard_map/ppermute | solution.py:509
  45.7 2.2 %collective-permute-start.12 = (f32[32,672]{1,0:T(8,128)S(1)}, f32[32,672]{1,0:T(8,128)S(1)}, u32[]{:S(2)}, u32[]{:S(2)}) collective-permute-start(f32[32,672]{1,0:T(8,128)S(1)} %get-tuple-element.55), channel_id=1, source_target_pairs={{0,1},{1,0},{2,3},{3,2},{4,5},{5,4},{6,7},{7,6},{8,9},{9,8},{10,11... | collective-permute-start | bytes 258056 | tf_op jit(solution)/shard_map/ppermute | solution.py:509
  47.6 1.7 %collective-permute-start.13 = (f32[32,640]{1,0:T(8,128)S(1)}, f32[32,640]{1,0:T(8,128)S(1)}, u32[]{:S(2)}, u32[]{:S(2)}) collective-permute-start(f32[32,640]{1,0:T(8,128)S(1)} %get-tuple-element.58), channel_id=1, source_target_pairs={{0,1},{1,0},{2,3},{3,2},{4,5},{5,4},{6,7},{7,6},{8,9},{9,8},{10,11... | collective-permute-start | bytes 245768 | tf_op jit(solution)/shard_map/ppermute | solution.py:509
  48.0 4.1 %collective-permute-start.14 = (bf16[176,128]{1,0:T(8,128)(2,1)S(1)}, bf16[176,128]{1,0:T(8,128)(2,1)S(1)}, u32[]{:S(2)}, u32[]{:S(2)}) collective-permute-start(bf16[176,128]{1,0:T(8,128)(2,1)S(1)} %get-tuple-element.56.refs_0_), channel_id=1, source_target_pairs={{0,2},{2,0},{1,3},{3,1},{4,6},{6,4},{5,7},{7,5},{8,10},{10,8},{9,1... | collective-permute-start | bytes 135176 | tf_op jit(solution)/shard_map/ppermute | solution.py:506
  52.3 8.4 %collective-permute-start.15 = (f32[32,2048]{1,0:T(8,128)S(1)}, f32[32,2048]{1,0:T(8,128)S(1)}, u32[]{:S(2)}, u32[]{:S(2)}) collective-permute-start(f32[32,2048]{1,0:T(8,128)S(1)} %get-tuple-element.59.h_ref.refs_0_), channel_id=1, source_target_pairs={{0,2},{2,0},{1,3},{3,1},{4,6},{6,4},{5,7},{7,5},{8,10},{10,8},{9,1... | collective-permute-start | bytes 786440 | tf_op jit(solution)/shard_map/ppermute | solution.py:506
  52.7 5.0 %collective-permute-start.16 = (bf16[176,128]{1,0:T(8,128)(2,1)S(1)}, bf16[176,128]{1,0:T(8,128)(2,1)S(1)}, u32[]{:S(2)}, u32[]{:S(2)}) collective-permute-start(bf16[176,128]{1,0:T(8,128)(2,1)S(1)} %shard_map.85.refs_0_), channel_id=1, source_target_pairs={{4,0},{0,4},{12,8},{8,12},{5,1},{1,5},{13,9},{9,13},{6,2},{2,6},{1... | collective-permute-start | bytes 135176 | tf_op jit(solution)/shard_map/ppermute | solution.py:512
  52.7 5.0 %collective-permute-start.17 = (bf16[176,128]{1,0:T(8,128)(2,1)S(1)}, bf16[176,128]{1,0:T(8,128)(2,1)S(1)}, u32[]{:S(2)}, u32[]{:S(2)}) collective-permute-start(bf16[176,128]{1,0:T(8,128)(2,1)S(1)} %shard_map.85.refs_0_), channel_id=1, source_target_pairs={{8,0},{12,4},{0,8},{4,12},{9,1},{13,5},{1,9},{5,13},{10,2},{14,6},... | collective-permute-start | bytes 135176 | tf_op jit(solution)/shard_map/ppermute | solution.py:512
  53.8 5.8 %collective-permute-start.18 = (bf16[176,128]{1,0:T(8,128)(2,1)S(1)}, bf16[176,128]{1,0:T(8,128)(2,1)S(1)}, u32[]{:S(2)}, u32[]{:S(2)}) collective-permute-start(bf16[176,128]{1,0:T(8,128)(2,1)S(1)} %shard_map.85.refs_0_), channel_id=1, source_target_pairs={{12,0},{8,4},{4,8},{0,12},{13,1},{9,5},{5,9},{1,13},{14,2},{10,6},... | collective-permute-start | bytes 135176 | tf_op jit(solution)/shard_map/ppermute | solution.py:512
  60.6 1.5 %collective-permute-start.19 = (f32[32,1280]{1,0:T(8,128)S(1)}, f32[32,1280]{1,0:T(8,128)S(1)}, u32[]{:S(2)}, u32[]{:S(2)}) collective-permute-start(f32[32,1280]{1,0:T(8,128)S(1)} %shard_map.87.refs_0_), channel_id=1, source_target_pairs={{0,1},{1,0},{2,3},{3,2},{4,5},{5,4},{6,7},{7,6},{8,9},{9,8},{10,11... | collective-permute-start | bytes 491528 | tf_op jit(solution)/shard_map/ppermute | solution.py:509

commit v12 on v11

--- a/solution.py
+++ b/solution.py
@@ -392,8 +392,8 @@
 
 
 def summed(z_me, count, msg_refs, scr, rank, size):
-    for shift in range(count):
-        scr[partner(z_me, shift, count)] = msg_refs[shift][...]
+    for at, shift in enumerate([0, *reversed(range(1, count))]):
+        scr[partner(z_me, shift, count)] = msg_refs[at][...]
     total, gram = body(scr[0], rank, size).astype(F32), gram_of(scr[0], rank)
     for at in range(1, count):
         total = total + body(scr[at], rank, size).astype(F32)
@@ -609,7 +609,7 @@
         from_rows = [row_shift(m, dx + 1) for dx, m in enumerate(outs)]
         (own,) = products([(0, 0)], activations, outs)
         (part,) = call(functools.partial(row_kernel, subs), [own, gram] + from_cores + from_rows, [msg])
-        return [part] + [frm_shift(part, shift) for shift in range(1, frms)]
+        return [part] + [frm_shift(part, shift) for shift in reversed(range(1, frms))]
 
     activations, h_gram, *msgs = call(
         functools.partial(first_kernel, rows, subs, cl),

time: 63.1 us -> 61.6 us (0.976)
  waiting for transfers between devices: 18.1 us -> 16.6 us
    ppermute x6, waiting for transfers between devices: 8.01 us -> 6.52 us  [frm_shift(): lax.ppermute(value, 'frm', [(partner(i, shift, frms), i) for i in range(f...]
  transfers between devices with their start and end apart: 20 -> 20, of which waited for: 10 -> 11; matrix products, arithmetic and copies ran while one was open for 0% -> 0% of each run, Pallas kernels for 27% -> 28%
where the time goes in v12:
time: 61.6 us; the launch traced here: 61.5 us
  Pallas kernels  24.8 us (40%)
  starting transfers between devices  19.1 us (31%)
  waiting for transfers between devices  16.6 us (27%)
  between operations  0.94 us (2%)
    pallas_call x21, Pallas kernels, call(): pl.pallas_call(kernel, out_shape=[jax.ShapeDtypeStruct(*out) if isinstanc...  24.8 us
    ppermute x6, starting transfers between devices, frm_shift(): lax.ppermute(value, 'frm', [(partner(i, shift, frms), i) for i in range(f...  8.78 us
    ppermute x6, waiting for transfers between devices, row_shift(): lax.ppermute(value, 'row', [(i, (i + shift) % rows) for i in range(rows)])  7.58 us
    ppermute x6, starting transfers between devices, row_shift(): lax.ppermute(value, 'row', [(i, (i + shift) % rows) for i in range(rows)])  7.24 us
    ppermute x6, waiting for transfers between devices, frm_shift(): lax.ppermute(value, 'frm', [(partner(i, shift, frms), i) for i in range(f...  6.52 us
    ppermute x7, waiting for transfers between devices, sub_shift(): lax.ppermute(value, 'sub', [(i, (i + shift) % subs) for i in range(subs)])  2.51 us
    ppermute x7, starting transfers between devices, sub_shift(): lax.ppermute(value, 'sub', [(i, (i + shift) % subs) for i in range(subs)])  2.44 us
  transfers between devices with their start and end apart: 20, of which 11 were waited for; matrix products, arithmetic and copies ran while one was open for 0% of the time, Pallas kernels for 28%

profile of v12, /device:TPU:0, one launch (start us, length us, event | category | flops | bytes accessed | tf_op | source)
XLA Modules:
  0.0 61.5 jit_solution(11623096173326780944)
XLA Ops:
  0.6 1.4 %shard_map.68 = (bf16[32,2176]{1,0:T(8,128)(2,1)S(1)}, bf16[32,2176]{1,0:T(8,128)(2,1)S(1)}, bf16[8,256,256]{2,1,0:T(8,128)(2,1)S(1)}) custom-call(bf16[32,4096]{1,0:T(8,128)(2,1)} %sig_hbm.1, bf16[40,256,256]{2,1,0:T(8,128)(2,1)} %constant.4.clone.tab_hbm), custom_call_target="tpu_custom_call" | custom-call | tf_op jit(solution)/shard_map/pallas_call | solution.py:466
  2.1 3.0 %collective-permute-start = (bf16[32,2176]{1,0:T(8,128)(2,1)S(1)}, bf16[32,2176]{1,0:T(8,128)(2,1)S(1)}, u32[]{:S(2)}, u32[]{:S(2)}) collective-permute-start(bf16[32,2176]{1,0:T(8,128)(2,1)S(1)} %get-tuple-element.36), channel_id=1, source_target_pairs={{0,2},{2,0},{1,3},{3,1},{4,6},{6,4},{5,7},{7,5},{8,10},{10,8},{9,1... | collective-permute-start | bytes 417800 | tf_op jit(solution)/shard_map/ppermute | solution.py:506
  5.1 4.1 %shard_map.69 = (bf16[40,16,2,32,128]{4,3,2,1,0:T(8,128)(2,1)S(1)}, f32[32,1280]{1,0:T(8,128)S(1)}, f32[32,2048]{1,0:T(8,128)S(1)}, bf16[1280,1280]{1,0:T(8,128)(2,1)S(1)}, bf16[32,256,256]{2,1,0:T(8,128)(2,1)S(1)}) custom-call(bf16[32,2176]{1,0:T(8,128)(2,1)S(1)} %get-tuple-element.32.sig_ref.refs_0_, bf16[8,256,256]{2,1,0:T(8,128)(2,1)S(1)} %get-tuple-element.33.ahead_ref, ...), custom_call_target="tpu_custom_call" | custom-call | flops 2684354560 | tf_op jit(solution)/shard_map/pallas_call | solution.py:466
  9.2 0.0 collective-permute-done.refs_0_.refs_1_
  9.2 0.7 %collective-permute-start.2 = (bf16[64,128]{1,0:T(8,128)(2,1)S(1)}, bf16[64,128]{1,0:T(8,128)(2,1)S(1)}, u32[]{:S(2)}, u32[]{:S(2)}) collective-permute-start(bf16[64,128]{1,0:T(8,128)(2,1)S(1)} %shard_map.70.refs_0_), channel_id=1, source_target_pairs={{2,1},{3,4},{6,5},{7,8},{10,9},{11,12},{14,13},{1,2},{4,3},{5,6},{... | collective-permute-start | bytes 49160 | tf_op jit(solution)/shard_map/ppermute | solution.py:560
  9.9 0.8 %shard_map.71 = (f32[32,640]{1,0:T(8,128)S(1)}, bf16[336,128]{1,0:T(8,128)(2,1)S(1)}) custom-call(f32[32,1280]{1,0:T(8,128)S(1)} %get-tuple-element.34.w_ref, bf16[1280,1280]{1,0:T(8,128)(2,1)S(1)} %get-tuple-element.35.order_ref, bf16[64,128]{1,0:T(8,128)(2,1)S(1)} %shard_map.70.refs_0_), custom_call_target="tpu_custom_call" | custom-call | tf_op jit(solution)/shard_map/pallas_call | solution.py:466
  10.7 0.9 %shard_map.72.refs_3_.refs_2_ = f32[32,2048]{1,0:T(8,128)S(1)} custom-call(bf16[336,128]{1,0:T(8,128)(2,1)S(1)} %get-tuple-element.39.w_ref.refs_0_, bf16[40,16,2,32,128]{4,3,2,1,0:T(8,128)(2,1)S(1)} %get-tuple-element.37.refs_1_.s_ref.refs_2_), custom_call_target="tpu_custom_call" | custom-call | flops 1342177280 | tf_op jit(solution)/shard_map/pallas_call | solution.py:466
  11.6 2.6 %collective-permute-start.1 = (bf16[336,128]{1,0:T(8,128)(2,1)S(1)}, bf16[336,128]{1,0:T(8,128)(2,1)S(1)}, u32[]{:S(2)}, u32[]{:S(2)}) collective-permute-start(bf16[336,128]{1,0:T(8,128)(2,1)S(1)} %get-tuple-element.39.w_ref.refs_0_), channel_id=1, source_target_pairs={{0,2},{2,0},{1,3},{3,1},{4,6},{6,4},{5,7},{7,5},{8,10},{10,8},{9,1... | collective-permute-start | bytes 258056 | tf_op jit(solution)/shard_map/ppermute | solution.py:506
  14.2 0.0 collective-permute-done.2.halo_ref
  14.2 3.5 %shard_map.73.refs_4_.s_ref.refs_2_.refs_6_ = bf16[40,16,2,32,128]{4,3,2,1,0:T(8,128)(2,1)S(1)} custom-call(bf16[64,128]{1,0:T(8,128)(2,1)S(1)} %collective-permute-done.2.halo_ref, bf16[8,256,256]{2,1,0:T(8,128)(2,1)S(1)} %get-tuple-element.33.ahead_ref, bf16[32,256,256]{2,1,0:T(8,128)(2,1)S(1)} %get-tuple-element.41.tab_ref, ...), custom_call_target="tpu_custom_call", output_to_operand_aliasing={{}: (5, {})} | custom-call | flops 5368709120 | tf_op jit(solution)/shard_map/pallas_call | solution.py:466
  17.7 0.0 collective-permute-done.1.refs_1_
  17.7 2.2 %shard_map.74 = (f32[32,2048]{1,0:T(8,128)S(1)}, f32[32,32]{1,0:T(8,128)S(1)}, f32[32,672]{1,0:T(8,128)S(1)}) custom-call(bf16[336,128]{1,0:T(8,128)(2,1)S(1)} %get-tuple-element.39.w_ref.refs_0_, bf16[336,128]{1,0:T(8,128)(2,1)S(1)} %collective-permute-done.1.refs_1_, f32[32,2048]{1,0:T(8,128)S(1)} %shard_map.72.refs_3_.refs_2_, ...), custom_call_target="tpu_custom_call" | custom-call | tf_op jit(solution)/shard_map/pallas_call | solution.py:466
  19.9 1.7 %collective-permute-start.3 = (f32[32,672]{1,0:T(8,128)S(1)}, f32[32,672]{1,0:T(8,128)S(1)}, u32[]{:S(2)}, u32[]{:S(2)}) collective-permute-start(f32[32,672]{1,0:T(8,128)S(1)} %get-tuple-element.45), channel_id=1, source_target_pairs={{0,1},{1,0},{2,3},{3,2},{4,5},{5,4},{6,7},{7,6},{8,9},{9,8},{10,11... | collective-permute-start | bytes 258056 | tf_op jit(solution)/shard_map/ppermute | solution.py:509
  21.6 1.6 %shard_map.75 = (f32[32,640]{1,0:T(8,128)S(1)}, f32[32,640]{1,0:T(8,128)S(1)}) custom-call(f32[32,2048]{1,0:T(8,128)S(1)} %get-tuple-element.42.h_ref.refs_5_, bf16[40,16,2,32,128]{4,3,2,1,0:T(8,128)(2,1)S(1)} %shard_map.73.refs_4_.s_ref.refs_2_.refs_6_), custom_call_target="tpu_custom_call" | custom-call | flops 1342177280 | tf_op jit(solution)/shard_map/pallas_call | solution.py:466
  23.2 0.1 collective-permute-start.4
  23.3 0.0 collective-permute-done.3.refs_2_
  23.3 0.1 shard_map.76
  23.4 0.3 collective-permute-start.5
  23.7 0.8 %shard_map.77.own_ref = f32[32,640]{1,0:T(8,128)S(1)} custom-call(f32[32,2048]{1,0:T(8,128)S(1)} %get-tuple-element.42.h_ref.refs_5_, bf16[40,16,2,32,128]{4,3,2,1,0:T(8,128)(2,1)S(1)} %shard_map.73.refs_4_.s_ref.refs_2_.refs_6_, bf16[176,128]{1,0:T(8,128)(2,1)S(1)} %get-tuple-element.46.refs_0_), custom_call_target="tpu_custom_call" | custom-call | flops 1 | tf_op jit(solution)/shard_map/pallas_call | solution.py:466
  24.5 0.0 collective-permute-done.4.refs_0_
  24.5 2.9 %collective-permute-done.5.refs_1_ = bf16[176,128]{1,0:T(8,128)(2,1)S(1)} collective-permute-done((bf16[176,128]{1,0:T(8,128)(2,1)S(1)}, bf16[176,128]{1,0:T(8,128)(2,1)S(1)}, u32[]{:S(2)}, u32[]{:S(2)}) %collective-permute-start.5) | collective-permute-done | bytes 45088 | tf_op jit(solution)/shard_map/ppermute | solution.py:506
  27.4 0.2 shard_map.78.refs_0_
  27.6 3.5 %collective-permute-start.6 = (bf16[176,128]{1,0:T(8,128)(2,1)S(1)}, bf16[176,128]{1,0:T(8,128)(2,1)S(1)}, u32[]{:S(2)}, u32[]{:S(2)}) collective-permute-start(bf16[176,128]{1,0:T(8,128)(2,1)S(1)} %shard_map.78.refs_0_), channel_id=1, source_target_pairs={{12,0},{8,4},{4,8},{0,12},{13,1},{9,5},{5,9},{1,13},{14,2},{10,6},... | collective-permute-start | bytes 135176 | tf_op jit(solution)/shard_map/ppermute | solution.py:512
  31.1 0.0 collective-permute-start.7
  31.1 0.9 %collective-permute-start.8 = (bf16[176,128]{1,0:T(8,128)(2,1)S(1)}, bf16[176,128]{1,0:T(8,128)(2,1)S(1)}, u32[]{:S(2)}, u32[]{:S(2)}) collective-permute-start(bf16[176,128]{1,0:T(8,128)(2,1)S(1)} %shard_map.78.refs_0_), channel_id=1, source_target_pairs={{4,0},{0,4},{12,8},{8,12},{5,1},{1,5},{13,9},{9,13},{6,2},{2,6},{1... | collective-permute-start | bytes 135176 | tf_op jit(solution)/shard_map/ppermute | solution.py:512
  32.0 1.8 %collective-permute-done.6.refs_1_ = bf16[176,128]{1,0:T(8,128)(2,1)S(1)} collective-permute-done((bf16[176,128]{1,0:T(8,128)(2,1)S(1)}, bf16[176,128]{1,0:T(8,128)(2,1)S(1)}, u32[]{:S(2)}, u32[]{:S(2)}) %collective-permute-start.6) | collective-permute-done | bytes 45088 | tf_op jit(solution)/shard_map/ppermute | solution.py:512
  33.8 2.2 %collective-permute-done.7.refs_2_ = bf16[176,128]{1,0:T(8,128)(2,1)S(1)} collective-permute-done((bf16[176,128]{1,0:T(8,128)(2,1)S(1)}, bf16[176,128]{1,0:T(8,128)(2,1)S(1)}, u32[]{:S(2)}, u32[]{:S(2)}) %collective-permute-start.7) | collective-permute-done | bytes 45088 | tf_op jit(solution)/shard_map/ppermute | solution.py:512
  36.1 0.0 collective-permute-done.8.refs_3_
  36.1 0.7 %shard_map.79 = (f32[32,640]{1,0:T(8,128)S(1)}, bf16[176,128]{1,0:T(8,128)(2,1)S(1)}) custom-call(f32[32,640]{1,0:T(8,128)S(1)} %get-tuple-element.38.w_ref, bf16[176,128]{1,0:T(8,128)(2,1)S(1)} %shard_map.78.refs_0_, bf16[176,128]{1,0:T(8,128)(2,1)S(1)} %collective-permute-done.6.refs_1_, bf16[176,128]{1,0:T(8,128)(2,1)S(1)} %collective-permute-done.7.refs_2_, ...), custom_call_target="tpu_custom_call" | custom-call | tf_op jit(solution)/shard_map/pallas_call | solution.py:466
  36.7 0.0 collective-permute-start.9
  36.8 0.5 collective-permute-start.10
  37.2 0.7 %collective-permute-done.9.refs_1_ = bf16[176,128]{1,0:T(8,128)(2,1)S(1)} collective-permute-done((bf16[176,128]{1,0:T(8,128)(2,1)S(1)}, bf16[176,128]{1,0:T(8,128)(2,1)S(1)}, u32[]{:S(2)}, u32[]{:S(2)}) %collective-permute-start.9) | collective-permute-done | bytes 45088 | tf_op jit(solution)/shard_map/ppermute | solution.py:509
  38.0 1.0 %shard_map.80.refs_4_ = f32[32,2048]{1,0:T(8,128)S(1)} custom-call(bf16[176,128]{1,0:T(8,128)(2,1)S(1)} %get-tuple-element.49.refs_0_, bf16[176,128]{1,0:T(8,128)(2,1)S(1)} %collective-permute-done.9.refs_1_, bf16[40,16,2,32,128]{4,3,2,1,0:T(8,128)(2,1)S(1)} %shard_map.73.refs_4_.s_ref.refs_2_.refs_6_), custom_call_target="tpu_custom_call" | custom-call | flops 1342177280 | tf_op jit(solution)/shard_map/pallas_call | solution.py:466
  39.0 1.9 %collective-permute-done.10.refs_2_ = bf16[176,128]{1,0:T(8,128)(2,1)S(1)} collective-permute-done((bf16[176,128]{1,0:T(8,128)(2,1)S(1)}, bf16[176,128]{1,0:T(8,128)(2,1)S(1)}, u32[]{:S(2)}, u32[]{:S(2)}) %collective-permute-start.10) | collective-permute-done | bytes 45088 | tf_op jit(solution)/shard_map/ppermute | solution.py:506
  40.9 0.0 collective-permute-start.11
  40.9 1.2 %collective-permute-done.11.refs_3_ = bf16[176,128]{1,0:T(8,128)(2,1)S(1)} collective-permute-done((bf16[176,128]{1,0:T(8,128)(2,1)S(1)}, bf16[176,128]{1,0:T(8,128)(2,1)S(1)}, u32[]{:S(2)}, u32[]{:S(2)}) %collective-permute-start.11) | collective-permute-done | bytes 45088 | tf_op jit(solution)/shard_map/ppermute | solution.py:509
  42.1 2.1 %shard_map.81 = (f32[32,2048]{1,0:T(8,128)S(1)}, f32[32,32]{1,0:T(8,128)S(1)}, f32[32,672]{1,0:T(8,128)S(1)}) custom-call(bf16[176,128]{1,0:T(8,128)(2,1)S(1)} %get-tuple-element.49.refs_0_, bf16[176,128]{1,0:T(8,128)(2,1)S(1)} %collective-permute-done.9.refs_1_, bf16[176,128]{1,0:T(8,128)(2,1)S(1)} %collective-permute-done.10.refs_2_, ...), custom_call_target="tpu_custom_call" | custom-call | tf_op jit(solution)/shard_map/pallas_call | solution.py:466
  44.2 0.2 collective-permute-start.12
  44.5 1.6 %shard_map.82 = (f32[32,640]{1,0:T(8,128)S(1)}, f32[32,640]{1,0:T(8,128)S(1)}) custom-call(f32[32,2048]{1,0:T(8,128)S(1)} %get-tuple-element.59.h_ref.refs_0_, bf16[40,16,2,32,128]{4,3,2,1,0:T(8,128)(2,1)S(1)} %shard_map.73.refs_4_.s_ref.refs_2_.refs_6_), custom_call_target="tpu_custom_call" | custom-call | flops 1342177280 | tf_op jit(solution)/shard_map/pallas_call | solution.py:466
  46.1 0.4 collective-permute-start.13
  46.5 0.0 collective-permute-done.12.refs_2_
  46.5 0.1 shard_map.83
  46.6 0.4 collective-permute-start.14
  47.0 0.8 %shard_map.84.own_ref = f32[32,640]{1,0:T(8,128)S(1)} custom-call(f32[32,2048]{1,0:T(8,128)S(1)} %get-tuple-element.59.h_ref.refs_0_, bf16[40,16,2,32,128]{4,3,2,1,0:T(8,128)(2,1)S(1)} %shard_map.73.refs_4_.s_ref.refs_2_.refs_6_, bf16[176,128]{1,0:T(8,128)(2,1)S(1)} %get-tuple-element.56.refs_0_), custom_call_target="tpu_custom_call" | custom-call | flops 1 | tf_op jit(solution)/shard_map/pallas_call | solution.py:466
  47.8 0.0 collective-permute-done.13.refs_0_
  47.8 2.8 %collective-permute-done.14.refs_1_ = bf16[176,128]{1,0:T(8,128)(2,1)S(1)} collective-permute-done((bf16[176,128]{1,0:T(8,128)(2,1)S(1)}, bf16[176,128]{1,0:T(8,128)(2,1)S(1)}, u32[]{:S(2)}, u32[]{:S(2)}) %collective-permute-start.14) | collective-permute-done | bytes 45088 | tf_op jit(solution)/shard_map/ppermute | solution.py:506
  50.6 0.2 shard_map.85.refs_0_
  50.8 0.4 collective-permute-start.15
  51.3 1.5 %collective-permute-start.16 = (bf16[176,128]{1,0:T(8,128)(2,1)S(1)}, bf16[176,128]{1,0:T(8,128)(2,1)S(1)}, u32[]{:S(2)}, u32[]{:S(2)}) collective-permute-start(bf16[176,128]{1,0:T(8,128)(2,1)S(1)} %shard_map.85.refs_0_), channel_id=1, source_target_pairs={{12,0},{8,4},{4,8},{0,12},{13,1},{9,5},{5,9},{1,13},{14,2},{10,6},... | collective-permute-start | bytes 135176 | tf_op jit(solution)/shard_map/ppermute | solution.py:512
  52.7 0.6 collective-permute-start.17
  53.3 2.4 %collective-permute-start.18 = (bf16[176,128]{1,0:T(8,128)(2,1)S(1)}, bf16[176,128]{1,0:T(8,128)(2,1)S(1)}, u32[]{:S(2)}, u32[]{:S(2)}) collective-permute-start(bf16[176,128]{1,0:T(8,128)(2,1)S(1)} %shard_map.85.refs_0_), channel_id=1, source_target_pairs={{4,0},{0,4},{12,8},{8,12},{5,1},{1,5},{13,9},{9,13},{6,2},{2,6},{1... | collective-permute-start | bytes 135176 | tf_op jit(solution)/shard_map/ppermute | solution.py:512
  55.7 1.5 %collective-permute-done.16.refs_1_ = bf16[176,128]{1,0:T(8,128)(2,1)S(1)} collective-permute-done((bf16[176,128]{1,0:T(8,128)(2,1)S(1)}, bf16[176,128]{1,0:T(8,128)(2,1)S(1)}, u32[]{:S(2)}, u32[]{:S(2)}) %collective-permute-start.16) | collective-permute-done | bytes 45088 | tf_op jit(solution)/shard_map/ppermute | solution.py:512
  57.1 0.6 collective-permute-done.17.refs_2_
  57.7 0.4 collective-permute-done.18.refs_3_
  58.2 1.0 %shard_map.87.refs_0_ = f32[32,1280]{1,0:T(8,128)S(1)} custom-call(f32[32,640]{1,0:T(8,128)S(1)} %get-tuple-element.60.w_ref, bf16[1280,1280]{1,0:T(8,128)(2,1)S(1)} %get-tuple-element.35.order_ref, bf16[176,128]{1,0:T(8,128)(2,1)S(1)} %shard_map.85.refs_0_, bf16[176,128]{1,0:T(8,128)(2,1)S(1)} %collective-permute-done.16.refs_1_, ...), custom_call_target="tpu_custom_call" | custom-call | tf_op jit(solution)/shard_map/pallas_call | solution.py:466
  59.1 0.1 collective-permute-start.19
  59.2 0.0 collective-permute-done.15.refs_1_
  59.2 0.8 %shard_map.86._ = f32[32,4096]{1,0:T(8,128)} custom-call(f32[32,2048]{1,0:T(8,128)S(1)} %get-tuple-element.59.h_ref.refs_0_, f32[32,2048]{1,0:T(8,128)S(1)} %collective-permute-done.15.refs_1_), custom_call_target="tpu_custom_call" | custom-call | tf_op jit(solution)/shard_map/pallas_call | solution.py:466
  60.1 0.5 collective-permute-done.19.refs_1_
  60.6 0.7 %shard_map.88 = f32[32,1280]{1,0:T(8,128)} custom-call(f32[32,4096]{1,0:T(8,128)} %shard_map.86._, f32[32,1280]{1,0:T(8,128)S(1)} %shard_map.87.refs_0_, f32[32,1280]{1,0:T(8,128)S(1)} %collective-permute-done.19.refs_1_), custom_call_target="tpu_custom_call" | custom-call | tf_op jit(solution)/shard_map/pallas_call | solution.py:466
  (1 shorter events, 0.0 us)
Async XLA Ops:
  2.1 7.1 %collective-permute-start = (bf16[32,2176]{1,0:T(8,128)(2,1)S(1)}, bf16[32,2176]{1,0:T(8,128)(2,1)S(1)}, u32[]{:S(2)}, u32[]{:S(2)}) collective-permute-start(bf16[32,2176]{1,0:T(8,128)(2,1)S(1)} %get-tuple-element.36), channel_id=1, source_target_pairs={{0,2},{2,0},{1,3},{3,1},{4,6},{6,4},{5,7},{7,5},{8,10},{10,8},{9,1... | collective-permute-start | bytes 417800 | tf_op jit(solution)/shard_map/ppermute | solution.py:506
  9.2 5.0 %collective-permute-start.2 = (bf16[64,128]{1,0:T(8,128)(2,1)S(1)}, bf16[64,128]{1,0:T(8,128)(2,1)S(1)}, u32[]{:S(2)}, u32[]{:S(2)}) collective-permute-start(bf16[64,128]{1,0:T(8,128)(2,1)S(1)} %shard_map.70.refs_0_), channel_id=1, source_target_pairs={{2,1},{3,4},{6,5},{7,8},{10,9},{11,12},{14,13},{1,2},{4,3},{5,6},{... | collective-permute-start | bytes 49160 | tf_op jit(solution)/shard_map/ppermute | solution.py:560
  11.6 6.1 %collective-permute-start.1 = (bf16[336,128]{1,0:T(8,128)(2,1)S(1)}, bf16[336,128]{1,0:T(8,128)(2,1)S(1)}, u32[]{:S(2)}, u32[]{:S(2)}) collective-permute-start(bf16[336,128]{1,0:T(8,128)(2,1)S(1)} %get-tuple-element.39.w_ref.refs_0_), channel_id=1, source_target_pairs={{0,2},{2,0},{1,3},{3,1},{4,6},{6,4},{5,7},{7,5},{8,10},{10,8},{9,1... | collective-permute-start | bytes 258056 | tf_op jit(solution)/shard_map/ppermute | solution.py:506
  19.9 3.4 %collective-permute-start.3 = (f32[32,672]{1,0:T(8,128)S(1)}, f32[32,672]{1,0:T(8,128)S(1)}, u32[]{:S(2)}, u32[]{:S(2)}) collective-permute-start(f32[32,672]{1,0:T(8,128)S(1)} %get-tuple-element.45), channel_id=1, source_target_pairs={{0,1},{1,0},{2,3},{3,2},{4,5},{5,4},{6,7},{7,6},{8,9},{9,8},{10,11... | collective-permute-start | bytes 258056 | tf_op jit(solution)/shard_map/ppermute | solution.py:509
  23.2 1.3 %collective-permute-start.4 = (f32[32,640]{1,0:T(8,128)S(1)}, f32[32,640]{1,0:T(8,128)S(1)}, u32[]{:S(2)}, u32[]{:S(2)}) collective-permute-start(f32[32,640]{1,0:T(8,128)S(1)} %get-tuple-element.48), channel_id=1, source_target_pairs={{0,1},{1,0},{2,3},{3,2},{4,5},{5,4},{6,7},{7,6},{8,9},{9,8},{10,11... | collective-permute-start | bytes 245768 | tf_op jit(solution)/shard_map/ppermute | solution.py:509
  23.4 4.1 %collective-permute-start.5 = (bf16[176,128]{1,0:T(8,128)(2,1)S(1)}, bf16[176,128]{1,0:T(8,128)(2,1)S(1)}, u32[]{:S(2)}, u32[]{:S(2)}) collective-permute-start(bf16[176,128]{1,0:T(8,128)(2,1)S(1)} %get-tuple-element.46.refs_0_), channel_id=1, source_target_pairs={{0,2},{2,0},{1,3},{3,1},{4,6},{6,4},{5,7},{7,5},{8,10},{10,8},{9,1... | collective-permute-start | bytes 135176 | tf_op jit(solution)/shard_map/ppermute | solution.py:506
  27.6 6.2 %collective-permute-start.6 = (bf16[176,128]{1,0:T(8,128)(2,1)S(1)}, bf16[176,128]{1,0:T(8,128)(2,1)S(1)}, u32[]{:S(2)}, u32[]{:S(2)}) collective-permute-start(bf16[176,128]{1,0:T(8,128)(2,1)S(1)} %shard_map.78.refs_0_), channel_id=1, source_target_pairs={{12,0},{8,4},{4,8},{0,12},{13,1},{9,5},{5,9},{1,13},{14,2},{10,6},... | collective-permute-start | bytes 135176 | tf_op jit(solution)/shard_map/ppermute | solution.py:512
  31.1 4.9 %collective-permute-start.7 = (bf16[176,128]{1,0:T(8,128)(2,1)S(1)}, bf16[176,128]{1,0:T(8,128)(2,1)S(1)}, u32[]{:S(2)}, u32[]{:S(2)}) collective-permute-start(bf16[176,128]{1,0:T(8,128)(2,1)S(1)} %shard_map.78.refs_0_), channel_id=1, source_target_pairs={{8,0},{12,4},{0,8},{4,12},{9,1},{13,5},{1,9},{5,13},{10,2},{14,6},... | collective-permute-start | bytes 135176 | tf_op jit(solution)/shard_map/ppermute | solution.py:512
  31.1 4.9 %collective-permute-start.8 = (bf16[176,128]{1,0:T(8,128)(2,1)S(1)}, bf16[176,128]{1,0:T(8,128)(2,1)S(1)}, u32[]{:S(2)}, u32[]{:S(2)}) collective-permute-start(bf16[176,128]{1,0:T(8,128)(2,1)S(1)} %shard_map.78.refs_0_), channel_id=1, source_target_pairs={{4,0},{0,4},{12,8},{8,12},{5,1},{1,5},{13,9},{9,13},{6,2},{2,6},{1... | collective-permute-start | bytes 135176 | tf_op jit(solution)/shard_map/ppermute | solution.py:512
  36.7 1.2 %collective-permute-start.9 = (bf16[176,128]{1,0:T(8,128)(2,1)S(1)}, bf16[176,128]{1,0:T(8,128)(2,1)S(1)}, u32[]{:S(2)}, u32[]{:S(2)}) collective-permute-start(bf16[176,128]{1,0:T(8,128)(2,1)S(1)} %get-tuple-element.49.refs_0_), channel_id=1, source_target_pairs={{0,1},{1,0},{2,3},{3,2},{4,5},{5,4},{6,7},{7,6},{8,9},{9,8},{10,11... | collective-permute-start | bytes 135176 | tf_op jit(solution)/shard_map/ppermute | solution.py:509
  36.8 4.1 %collective-permute-start.10 = (bf16[176,128]{1,0:T(8,128)(2,1)S(1)}, bf16[176,128]{1,0:T(8,128)(2,1)S(1)}, u32[]{:S(2)}, u32[]{:S(2)}) collective-permute-start(bf16[176,128]{1,0:T(8,128)(2,1)S(1)} %get-tuple-element.49.refs_0_), channel_id=1, source_target_pairs={{0,2},{2,0},{1,3},{3,1},{4,6},{6,4},{5,7},{7,5},{8,10},{10,8},{9,1... | collective-permute-start | bytes 135176 | tf_op jit(solution)/shard_map/ppermute | solution.py:506
  40.9 1.2 %collective-permute-start.11 = (bf16[176,128]{1,0:T(8,128)(2,1)S(1)}, bf16[176,128]{1,0:T(8,128)(2,1)S(1)}, u32[]{:S(2)}, u32[]{:S(2)}) collective-permute-start(bf16[176,128]{1,0:T(8,128)(2,1)S(1)} %collective-permute-done.10.refs_2_), channel_id=1, source_target_pairs={{0,1},{1,0},{2,3},{3,2},{4,5},{5,4},{6,7},{7,6},{8,9},{9,8},{10,11... | collective-permute-start | bytes 135176 | tf_op jit(solution)/shard_map/ppermute | solution.py:509
  44.2 2.2 %collective-permute-start.12 = (f32[32,672]{1,0:T(8,128)S(1)}, f32[32,672]{1,0:T(8,128)S(1)}, u32[]{:S(2)}, u32[]{:S(2)}) collective-permute-start(f32[32,672]{1,0:T(8,128)S(1)} %get-tuple-element.55), channel_id=1, source_target_pairs={{0,1},{1,0},{2,3},{3,2},{4,5},{5,4},{6,7},{7,6},{8,9},{9,8},{10,11... | collective-permute-start | bytes 258056 | tf_op jit(solution)/shard_map/ppermute | solution.py:509
  46.1 1.7 %collective-permute-start.13 = (f32[32,640]{1,0:T(8,128)S(1)}, f32[32,640]{1,0:T(8,128)S(1)}, u32[]{:S(2)}, u32[]{:S(2)}) collective-permute-start(f32[32,640]{1,0:T(8,128)S(1)} %get-tuple-element.58), channel_id=1, source_target_pairs={{0,1},{1,0},{2,3},{3,2},{4,5},{5,4},{6,7},{7,6},{8,9},{9,8},{10,11... | collective-permute-start | bytes 245768 | tf_op jit(solution)/shard_map/ppermute | solution.py:509
  46.6 4.1 %collective-permute-start.14 = (bf16[176,128]{1,0:T(8,128)(2,1)S(1)}, bf16[176,128]{1,0:T(8,128)(2,1)S(1)}, u32[]{:S(2)}, u32[]{:S(2)}) collective-permute-start(bf16[176,128]{1,0:T(8,128)(2,1)S(1)} %get-tuple-element.56.refs_0_), channel_id=1, source_target_pairs={{0,2},{2,0},{1,3},{3,1},{4,6},{6,4},{5,7},{7,5},{8,10},{10,8},{9,1... | collective-permute-start | bytes 135176 | tf_op jit(solution)/shard_map/ppermute | solution.py:506
  50.8 8.4 %collective-permute-start.15 = (f32[32,2048]{1,0:T(8,128)S(1)}, f32[32,2048]{1,0:T(8,128)S(1)}, u32[]{:S(2)}, u32[]{:S(2)}) collective-permute-start(f32[32,2048]{1,0:T(8,128)S(1)} %get-tuple-element.59.h_ref.refs_0_), channel_id=1, source_target_pairs={{0,2},{2,0},{1,3},{3,1},{4,6},{6,4},{5,7},{7,5},{8,10},{10,8},{9,1... | collective-permute-start | bytes 786440 | tf_op jit(solution)/shard_map/ppermute | solution.py:506
  51.3 5.8 %collective-permute-start.16 = (bf16[176,128]{1,0:T(8,128)(2,1)S(1)}, bf16[176,128]{1,0:T(8,128)(2,1)S(1)}, u32[]{:S(2)}, u32[]{:S(2)}) collective-permute-start(bf16[176,128]{1,0:T(8,128)(2,1)S(1)} %shard_map.85.refs_0_), channel_id=1, source_target_pairs={{12,0},{8,4},{4,8},{0,12},{13,1},{9,5},{5,9},{1,13},{14,2},{10,6},... | collective-permute-start | bytes 135176 | tf_op jit(solution)/shard_map/ppermute | solution.py:512
  52.7 5.0 %collective-permute-start.17 = (bf16[176,128]{1,0:T(8,128)(2,1)S(1)}, bf16[176,128]{1,0:T(8,128)(2,1)S(1)}, u32[]{:S(2)}, u32[]{:S(2)}) collective-permute-start(bf16[176,128]{1,0:T(8,128)(2,1)S(1)} %shard_map.85.refs_0_), channel_id=1, source_target_pairs={{8,0},{12,4},{0,8},{4,12},{9,1},{13,5},{1,9},{5,13},{10,2},{14,6},... | collective-permute-start | bytes 135176 | tf_op jit(solution)/shard_map/ppermute | solution.py:512
  53.3 4.9 %collective-permute-start.18 = (bf16[176,128]{1,0:T(8,128)(2,1)S(1)}, bf16[176,128]{1,0:T(8,128)(2,1)S(1)}, u32[]{:S(2)}, u32[]{:S(2)}) collective-permute-start(bf16[176,128]{1,0:T(8,128)(2,1)S(1)} %shard_map.85.refs_0_), channel_id=1, source_target_pairs={{4,0},{0,4},{12,8},{8,12},{5,1},{1,5},{13,9},{9,13},{6,2},{2,6},{1... | collective-permute-start | bytes 135176 | tf_op jit(solution)/shard_map/ppermute | solution.py:512
  59.1 1.5 %collective-permute-start.19 = (f32[32,1280]{1,0:T(8,128)S(1)}, f32[32,1280]{1,0:T(8,128)S(1)}, u32[]{:S(2)}, u32[]{:S(2)}) collective-permute-start(f32[32,1280]{1,0:T(8,128)S(1)} %shard_map.87.refs_0_), channel_id=1, source_target_pairs={{0,1},{1,0},{2,3},{3,2},{4,5},{5,4},{6,7},{7,6},{8,9},{9,8},{10,11... | collective-permute-start | bytes 491528 | tf_op jit(solution)/shard_map/ppermute | solution.py:509

commit v13 on v12

--- a/solution.py
+++ b/solution.py
@@ -348,19 +348,40 @@
     numerators(row_parts(rows, subs, cl, w_refs, w_scr, [0]), s_ref, num_ref, cl)
 
 
+def add_pieces(base_ref, pieces, s_ref, out_ref, rows, subs, cl):
+    rank, frames = out_ref.shape
+    count = NF // subs
+    x_me, c_me = lax.axis_index("row"), lax.axis_index("sub")
+    terms = []
+    for ref, dx, dc in pieces:
+        core = lax.rem(c_me + subs - dc, subs)
+        terms.append((body(ref[...], rank, count * cl), lax.rem(x_me + rows - dx, rows), core))
+    for pair in range(frames // (2 * TAPS)):
+        cols = slice(2 * TAPS * pair, 2 * TAPS * (pair + 1))
+        acc = base_ref[:, cols]
+        for w, x, core in terms:
+            spectra = pair_rows(s_ref, pl.ds(core * count, count), pair, x, cl)
+            acc = acc + jnp.dot(w, spectra, preferred_element_type=F32)
+        out_ref[:, cols] = acc
+
+
+def middle_kernel(rows, subs, cl, *refs):
+    w_refs, (base_ref, s_ref, out_ref) = refs[:-3], refs[-3:]
+    pieces = [(ref, dx + 1, 0) for dx, ref in enumerate(w_refs)]
+    add_pieces(base_ref, pieces, s_ref, out_ref, rows, subs, cl)
+
+
 def later_kernel(rows, subs, cl, *refs):
     refs = list(refs)
     w_refs = [refs.pop(0) for _ in range(rows * subs)]
-    early_ref, h_ref, s_ref, h_out, h_gram_ref = (refs.pop(0) for _ in range(5))
-    msg_refs, (w_scr, num_scr) = refs[:-2], refs[-2:]
+    middle_ref, h_ref, s_ref, h_out, h_gram_ref = (refs.pop(0) for _ in range(5))
+    msg_refs, num_scr = refs[:-1], refs[-1]
     gram = jnp.zeros(h_gram_ref.shape, F32)
     for ref in w_refs:
         gram = gram + gram_of(ref[...], h_ref.shape[0])
-    above = early_ref[...]
-    if rows > 1:
-        numerators(row_parts(rows, subs, cl, w_refs[subs:], w_scr, list(range(1, rows))), s_ref, num_scr, cl)
-        above = above + num_scr[...]
-    new_activations(h_ref[...], gram, above, s_ref, h_out, h_gram_ref, msg_refs, rows, subs, cl)
+    pieces = [(w_refs[dx * subs + dc], dx, dc) for dx in range(1, rows) for dc in range(1, subs)]
+    add_pieces(middle_ref, pieces, s_ref, num_scr, rows, subs, cl)
+    new_activations(h_ref[...], gram, num_scr[...], s_ref, h_out, h_gram_ref, msg_refs, rows, subs, cl)
 
 
 def core_kernel(count, rank, *refs):
@@ -626,7 +647,7 @@
         piled,
     )
     w_msgs = [w_msg] + [sub_shift(w_msg, dc) for dc in range(1, subs)]
-    w_pieces = pltpu.VMEM((rows, subs, rank, size), BF16)
+    w_pieces = pltpu.VMEM((1, subs, rank, size), BF16)
     (early,) = call(
         functools.partial(early_kernel, rows, subs, cl),
         w_msgs + [spectra],
@@ -636,13 +657,19 @@
     )
     from_rows = [row_shift(w_msg, dx) for dx in range(1, rows)]
     *from_rows, early = lax.optimization_barrier((*from_rows, early))
+    (middle,) = call(
+        functools.partial(middle_kernel, rows, subs, cl),
+        from_rows + [early, spectra],
+        [((rank, frames), F32)],
+        cost=16 * NF * cl * frames * rank // subs,
+    )
     for base in from_rows:
         w_msgs += [base] + [sub_shift(base, dc) for dc in range(1, subs)]
     activations, h_gram, *msgs = call(
         functools.partial(later_kernel, rows, subs, cl),
-        w_msgs + [early, activations, spectra],
+        w_msgs + [middle, activations, spectra],
         update_outs,
-        [w_pieces, pltpu.VMEM((rank, frames), F32)],
+        [pltpu.VMEM((rank, frames), F32)],
         limit=8,
     )
     parts = gathered(activations, h_gram, msgs)

time: 61.6 us -> 61.2 us (level)
    pallas_call x21 -> x22, Pallas kernels: 24.8 us -> 24.9 us  [call(): pl.pallas_call(kernel, out_shape=[jax.ShapeDtypeStruct(*out) if isinstanc...]
  transfers between devices with their start and end apart: 20 -> 20, of which waited for: 11 -> 11; matrix products, arithmetic and copies ran while one was open for 0% -> 0% of each run, Pallas kernels for 28% -> 29%
where the time goes in v13:
time: 61.2 us; the launch traced here: 61 us
  Pallas kernels  24.9 us (41%)
  starting transfers between devices  19.1 us (31%)
  waiting for transfers between devices  16 us (26%)
  between operations  0.94 us (2%)
    pallas_call x22, Pallas kernels, call(): pl.pallas_call(kernel, out_shape=[jax.ShapeDtypeStruct(*out) if isinstanc...  24.9 us
    ppermute x6, starting transfers between devices, frm_shift(): lax.ppermute(value, 'frm', [(partner(i, shift, frms), i) for i in range(f...  8.78 us
    ppermute x6, waiting for transfers between devices, row_shift(): lax.ppermute(value, 'row', [(i, (i + shift) % rows) for i in range(rows)])  7.59 us
    ppermute x6, starting transfers between devices, row_shift(): lax.ppermute(value, 'row', [(i, (i + shift) % rows) for i in range(rows)])  7.22 us
    ppermute x6, waiting for transfers between devices, frm_shift(): lax.ppermute(value, 'frm', [(partner(i, shift, frms), i) for i in range(f...  6.5 us
    ppermute x7, starting transfers between devices, sub_shift(): lax.ppermute(value, 'sub', [(i, (i + shift) % subs) for i in range(subs)])  2.45 us
    ppermute x7, waiting for transfers between devices, sub_shift(): lax.ppermute(value, 'sub', [(i, (i + shift) % subs) for i in range(subs)])  1.95 us
  transfers between devices with their start and end apart: 20, of which 11 were waited for; matrix products, arithmetic and copies ran while one was open for 0% of the time, Pallas kernels for 29%

profile of v13, /device:TPU:0, one launch (start us, length us, event | category | flops | bytes accessed | tf_op | source)
XLA Modules:
  0.0 61.0 jit_solution(16236169218337805678)
XLA Ops:
  0.6 1.4 %shard_map.68 = (bf16[32,2176]{1,0:T(8,128)(2,1)S(1)}, bf16[32,2176]{1,0:T(8,128)(2,1)S(1)}, bf16[8,256,256]{2,1,0:T(8,128)(2,1)S(1)}) custom-call(bf16[32,4096]{1,0:T(8,128)(2,1)} %sig_hbm.1, bf16[40,256,256]{2,1,0:T(8,128)(2,1)} %constant.4.clone.tab_hbm), custom_call_target="tpu_custom_call" | custom-call | tf_op jit(solution)/shard_map/pallas_call | solution.py:487
  2.1 3.0 %collective-permute-start = (bf16[32,2176]{1,0:T(8,128)(2,1)S(1)}, bf16[32,2176]{1,0:T(8,128)(2,1)S(1)}, u32[]{:S(2)}, u32[]{:S(2)}) collective-permute-start(bf16[32,2176]{1,0:T(8,128)(2,1)S(1)} %get-tuple-element.36), channel_id=1, source_target_pairs={{0,2},{2,0},{1,3},{3,1},{4,6},{6,4},{5,7},{7,5},{8,10},{10,8},{9,1... | collective-permute-start | bytes 417800 | tf_op jit(solution)/shard_map/ppermute | solution.py:527
  5.1 4.1 %shard_map.69 = (bf16[40,16,2,32,128]{4,3,2,1,0:T(8,128)(2,1)S(1)}, f32[32,1280]{1,0:T(8,128)S(1)}, f32[32,2048]{1,0:T(8,128)S(1)}, bf16[1280,1280]{1,0:T(8,128)(2,1)S(1)}, bf16[32,256,256]{2,1,0:T(8,128)(2,1)S(1)}) custom-call(bf16[32,2176]{1,0:T(8,128)(2,1)S(1)} %get-tuple-element.32.sig_ref.refs_0_, bf16[8,256,256]{2,1,0:T(8,128)(2,1)S(1)} %get-tuple-element.33.ahead_ref, ...), custom_call_target="tpu_custom_call" | custom-call | flops 2684354560 | tf_op jit(solution)/shard_map/pallas_call | solution.py:487
  9.2 0.0 collective-permute-done.refs_0_.refs_1_
  9.2 0.7 %collective-permute-start.2 = (bf16[64,128]{1,0:T(8,128)(2,1)S(1)}, bf16[64,128]{1,0:T(8,128)(2,1)S(1)}, u32[]{:S(2)}, u32[]{:S(2)}) collective-permute-start(bf16[64,128]{1,0:T(8,128)(2,1)S(1)} %shard_map.70.refs_0_), channel_id=1, source_target_pairs={{2,1},{3,4},{6,5},{7,8},{10,9},{11,12},{14,13},{1,2},{4,3},{5,6},{... | collective-permute-start | bytes 49160 | tf_op jit(solution)/shard_map/ppermute | solution.py:581
  9.9 0.8 %shard_map.71 = (f32[32,640]{1,0:T(8,128)S(1)}, bf16[336,128]{1,0:T(8,128)(2,1)S(1)}) custom-call(f32[32,1280]{1,0:T(8,128)S(1)} %get-tuple-element.34.w_ref, bf16[1280,1280]{1,0:T(8,128)(2,1)S(1)} %get-tuple-element.35.order_ref, bf16[64,128]{1,0:T(8,128)(2,1)S(1)} %shard_map.70.refs_0_), custom_call_target="tpu_custom_call" | custom-call | tf_op jit(solution)/shard_map/pallas_call | solution.py:487
  10.7 0.9 %shard_map.72.refs_3_.refs_2_ = f32[32,2048]{1,0:T(8,128)S(1)} custom-call(bf16[336,128]{1,0:T(8,128)(2,1)S(1)} %get-tuple-element.39.w_ref.refs_0_, bf16[40,16,2,32,128]{4,3,2,1,0:T(8,128)(2,1)S(1)} %get-tuple-element.37.refs_1_.s_ref.refs_2_), custom_call_target="tpu_custom_call" | custom-call | flops 1342177280 | tf_op jit(solution)/shard_map/pallas_call | solution.py:487
  11.6 2.6 %collective-permute-start.1 = (bf16[336,128]{1,0:T(8,128)(2,1)S(1)}, bf16[336,128]{1,0:T(8,128)(2,1)S(1)}, u32[]{:S(2)}, u32[]{:S(2)}) collective-permute-start(bf16[336,128]{1,0:T(8,128)(2,1)S(1)} %get-tuple-element.39.w_ref.refs_0_), channel_id=1, source_target_pairs={{0,2},{2,0},{1,3},{3,1},{4,6},{6,4},{5,7},{7,5},{8,10},{10,8},{9,1... | collective-permute-start | bytes 258056 | tf_op jit(solution)/shard_map/ppermute | solution.py:527
  14.2 0.0 collective-permute-done.2.halo_ref
  14.2 3.5 %shard_map.73.refs_4_.s_ref.refs_2_.refs_6_ = bf16[40,16,2,32,128]{4,3,2,1,0:T(8,128)(2,1)S(1)} custom-call(bf16[64,128]{1,0:T(8,128)(2,1)S(1)} %collective-permute-done.2.halo_ref, bf16[8,256,256]{2,1,0:T(8,128)(2,1)S(1)} %get-tuple-element.33.ahead_ref, bf16[32,256,256]{2,1,0:T(8,128)(2,1)S(1)} %get-tuple-element.41.tab_ref, ...), custom_call_target="tpu_custom_call", output_to_operand_aliasing={{}: (5, {})} | custom-call | flops 5368709120 | tf_op jit(solution)/shard_map/pallas_call | solution.py:487
  17.7 0.0 collective-permute-done.1.refs_1_
  17.7 2.2 %shard_map.74 = (f32[32,2048]{1,0:T(8,128)S(1)}, f32[32,32]{1,0:T(8,128)S(1)}, f32[32,672]{1,0:T(8,128)S(1)}) custom-call(bf16[336,128]{1,0:T(8,128)(2,1)S(1)} %get-tuple-element.39.w_ref.refs_0_, bf16[336,128]{1,0:T(8,128)(2,1)S(1)} %collective-permute-done.1.refs_1_, f32[32,2048]{1,0:T(8,128)S(1)} %shard_map.72.refs_3_.refs_2_, ...), custom_call_target="tpu_custom_call" | custom-call | tf_op jit(solution)/shard_map/pallas_call | solution.py:487
  20.0 1.7 %collective-permute-start.3 = (f32[32,672]{1,0:T(8,128)S(1)}, f32[32,672]{1,0:T(8,128)S(1)}, u32[]{:S(2)}, u32[]{:S(2)}) collective-permute-start(f32[32,672]{1,0:T(8,128)S(1)} %get-tuple-element.45), channel_id=1, source_target_pairs={{0,1},{1,0},{2,3},{3,2},{4,5},{5,4},{6,7},{7,6},{8,9},{9,8},{10,11... | collective-permute-start | bytes 258056 | tf_op jit(solution)/shard_map/ppermute | solution.py:530
  21.6 1.6 %shard_map.75 = (f32[32,640]{1,0:T(8,128)S(1)}, f32[32,640]{1,0:T(8,128)S(1)}) custom-call(f32[32,2048]{1,0:T(8,128)S(1)} %get-tuple-element.42.h_ref.refs_5_, bf16[40,16,2,32,128]{4,3,2,1,0:T(8,128)(2,1)S(1)} %shard_map.73.refs_4_.s_ref.refs_2_.refs_6_), custom_call_target="tpu_custom_call" | custom-call | flops 1342177280 | tf_op jit(solution)/shard_map/pallas_call | solution.py:487
  23.2 0.1 collective-permute-start.4
  23.3 0.0 collective-permute-done.3.refs_2_
  23.3 0.1 shard_map.76
  23.4 0.3 collective-permute-start.5
  23.7 0.8 %shard_map.77.own_ref = f32[32,640]{1,0:T(8,128)S(1)} custom-call(f32[32,2048]{1,0:T(8,128)S(1)} %get-tuple-element.42.h_ref.refs_5_, bf16[40,16,2,32,128]{4,3,2,1,0:T(8,128)(2,1)S(1)} %shard_map.73.refs_4_.s_ref.refs_2_.refs_6_, bf16[176,128]{1,0:T(8,128)(2,1)S(1)} %get-tuple-element.46.refs_0_), custom_call_target="tpu_custom_call" | custom-call | flops 1 | tf_op jit(solution)/shard_map/pallas_call | solution.py:487
  24.5 0.0 collective-permute-done.4.refs_0_
  24.6 2.9 %collective-permute-done.5.refs_1_ = bf16[176,128]{1,0:T(8,128)(2,1)S(1)} collective-permute-done((bf16[176,128]{1,0:T(8,128)(2,1)S(1)}, bf16[176,128]{1,0:T(8,128)(2,1)S(1)}, u32[]{:S(2)}, u32[]{:S(2)}) %collective-permute-start.5) | collective-permute-done | bytes 45088 | tf_op jit(solution)/shard_map/ppermute | solution.py:527
  27.5 0.2 shard_map.78.refs_0_
  27.7 3.5 %collective-permute-start.6 = (bf16[176,128]{1,0:T(8,128)(2,1)S(1)}, bf16[176,128]{1,0:T(8,128)(2,1)S(1)}, u32[]{:S(2)}, u32[]{:S(2)}) collective-permute-start(bf16[176,128]{1,0:T(8,128)(2,1)S(1)} %shard_map.78.refs_0_), channel_id=1, source_target_pairs={{12,0},{8,4},{4,8},{0,12},{13,1},{9,5},{5,9},{1,13},{14,2},{10,6},... | collective-permute-start | bytes 135176 | tf_op jit(solution)/shard_map/ppermute | solution.py:533
  31.1 0.0 collective-permute-start.7
  31.1 0.9 %collective-permute-start.8 = (bf16[176,128]{1,0:T(8,128)(2,1)S(1)}, bf16[176,128]{1,0:T(8,128)(2,1)S(1)}, u32[]{:S(2)}, u32[]{:S(2)}) collective-permute-start(bf16[176,128]{1,0:T(8,128)(2,1)S(1)} %shard_map.78.refs_0_), channel_id=1, source_target_pairs={{4,0},{0,4},{12,8},{8,12},{5,1},{1,5},{13,9},{9,13},{6,2},{2,6},{1... | collective-permute-start | bytes 135176 | tf_op jit(solution)/shard_map/ppermute | solution.py:533
  32.1 1.8 %collective-permute-done.6.refs_1_ = bf16[176,128]{1,0:T(8,128)(2,1)S(1)} collective-permute-done((bf16[176,128]{1,0:T(8,128)(2,1)S(1)}, bf16[176,128]{1,0:T(8,128)(2,1)S(1)}, u32[]{:S(2)}, u32[]{:S(2)}) %collective-permute-start.6) | collective-permute-done | bytes 45088 | tf_op jit(solution)/shard_map/ppermute | solution.py:533
  33.8 2.2 %collective-permute-done.7.refs_2_ = bf16[176,128]{1,0:T(8,128)(2,1)S(1)} collective-permute-done((bf16[176,128]{1,0:T(8,128)(2,1)S(1)}, bf16[176,128]{1,0:T(8,128)(2,1)S(1)}, u32[]{:S(2)}, u32[]{:S(2)}) %collective-permute-start.7) | collective-permute-done | bytes 45088 | tf_op jit(solution)/shard_map/ppermute | solution.py:533
  36.1 0.0 collective-permute-done.8.refs_3_
  36.1 0.7 %shard_map.79 = (f32[32,640]{1,0:T(8,128)S(1)}, bf16[176,128]{1,0:T(8,128)(2,1)S(1)}) custom-call(f32[32,640]{1,0:T(8,128)S(1)} %get-tuple-element.38.w_ref, bf16[176,128]{1,0:T(8,128)(2,1)S(1)} %shard_map.78.refs_0_, bf16[176,128]{1,0:T(8,128)(2,1)S(1)} %collective-permute-done.6.refs_1_, bf16[176,128]{1,0:T(8,128)(2,1)S(1)} %collective-permute-done.7.refs_2_, ...), custom_call_target="tpu_custom_call" | custom-call | tf_op jit(solution)/shard_map/pallas_call | solution.py:487
  36.7 0.0 collective-permute-start.9
  36.8 0.5 collective-permute-start.10
  37.2 0.7 %collective-permute-done.9.refs_1_ = bf16[176,128]{1,0:T(8,128)(2,1)S(1)} collective-permute-done((bf16[176,128]{1,0:T(8,128)(2,1)S(1)}, bf16[176,128]{1,0:T(8,128)(2,1)S(1)}, u32[]{:S(2)}, u32[]{:S(2)}) %collective-permute-start.9) | collective-permute-done | bytes 45088 | tf_op jit(solution)/shard_map/ppermute | solution.py:530
  38.0 1.0 %shard_map.80.refs_1_ = f32[32,2048]{1,0:T(8,128)S(1)} custom-call(bf16[176,128]{1,0:T(8,128)(2,1)S(1)} %get-tuple-element.49.refs_0_, bf16[176,128]{1,0:T(8,128)(2,1)S(1)} %collective-permute-done.9.refs_1_, bf16[40,16,2,32,128]{4,3,2,1,0:T(8,128)(2,1)S(1)} %shard_map.73.refs_4_.s_ref.refs_2_.refs_6_), custom_call_target="tpu_custom_call" | custom-call | flops 1342177280 | tf_op jit(solution)/shard_map/pallas_call | solution.py:487
  39.0 1.9 %collective-permute-done.10.refs_0_.refs_2_ = bf16[176,128]{1,0:T(8,128)(2,1)S(1)} collective-permute-done((bf16[176,128]{1,0:T(8,128)(2,1)S(1)}, bf16[176,128]{1,0:T(8,128)(2,1)S(1)}, u32[]{:S(2)}, u32[]{:S(2)}) %collective-permute-start.10) | collective-permute-done | bytes 45088 | tf_op jit(solution)/shard_map/ppermute | solution.py:527
  40.9 0.0 collective-permute-start.11
  40.9 0.6 shard_map.81.refs_4_
  41.4 0.7 %collective-permute-done.11.refs_3_ = bf16[176,128]{1,0:T(8,128)(2,1)S(1)} collective-permute-done((bf16[176,128]{1,0:T(8,128)(2,1)S(1)}, bf16[176,128]{1,0:T(8,128)(2,1)S(1)}, u32[]{:S(2)}, u32[]{:S(2)}) %collective-permute-start.11) | collective-permute-done | bytes 45088 | tf_op jit(solution)/shard_map/ppermute | solution.py:530
  42.1 1.7 %shard_map.82 = (f32[32,2048]{1,0:T(8,128)S(1)}, f32[32,32]{1,0:T(8,128)S(1)}, f32[32,672]{1,0:T(8,128)S(1)}) custom-call(bf16[176,128]{1,0:T(8,128)(2,1)S(1)} %get-tuple-element.49.refs_0_, bf16[176,128]{1,0:T(8,128)(2,1)S(1)} %collective-permute-done.9.refs_1_, bf16[176,128]{1,0:T(8,128)(2,1)S(1)} %collective-permute-done.10.refs_0_.refs_2_, ...), custom_call_target="tpu_custom_call" | custom-call | tf_op jit(solution)/shard_map/pallas_call | solution.py:487
  43.8 0.2 collective-permute-start.12
  44.0 1.6 %shard_map.83 = (f32[32,640]{1,0:T(8,128)S(1)}, f32[32,640]{1,0:T(8,128)S(1)}) custom-call(f32[32,2048]{1,0:T(8,128)S(1)} %get-tuple-element.59.h_ref.refs_0_, bf16[40,16,2,32,128]{4,3,2,1,0:T(8,128)(2,1)S(1)} %shard_map.73.refs_4_.s_ref.refs_2_.refs_6_), custom_call_target="tpu_custom_call" | custom-call | flops 1342177280 | tf_op jit(solution)/shard_map/pallas_call | solution.py:487
  45.6 0.4 collective-permute-start.13
  46.0 0.0 collective-permute-done.12.refs_2_
  46.0 0.1 shard_map.84
  46.1 0.4 collective-permute-start.14
  46.5 0.8 %shard_map.85.own_ref = f32[32,640]{1,0:T(8,128)S(1)} custom-call(f32[32,2048]{1,0:T(8,128)S(1)} %get-tuple-element.59.h_ref.refs_0_, bf16[40,16,2,32,128]{4,3,2,1,0:T(8,128)(2,1)S(1)} %shard_map.73.refs_4_.s_ref.refs_2_.refs_6_, bf16[176,128]{1,0:T(8,128)(2,1)S(1)} %get-tuple-element.56.refs_0_), custom_call_target="tpu_custom_call" | custom-call | flops 1 | tf_op jit(solution)/shard_map/pallas_call | solution.py:487
  47.4 0.0 collective-permute-done.13.refs_0_
  47.4 2.8 %collective-permute-done.14.refs_1_ = bf16[176,128]{1,0:T(8,128)(2,1)S(1)} collective-permute-done((bf16[176,128]{1,0:T(8,128)(2,1)S(1)}, bf16[176,128]{1,0:T(8,128)(2,1)S(1)}, u32[]{:S(2)}, u32[]{:S(2)}) %collective-permute-start.14) | collective-permute-done | bytes 45088 | tf_op jit(solution)/shard_map/ppermute | solution.py:527
  50.2 0.2 shard_map.86.refs_0_
  50.4 0.4 collective-permute-start.15
  50.8 1.5 %collective-permute-start.16 = (bf16[176,128]{1,0:T(8,128)(2,1)S(1)}, bf16[176,128]{1,0:T(8,128)(2,1)S(1)}, u32[]{:S(2)}, u32[]{:S(2)}) collective-permute-start(bf16[176,128]{1,0:T(8,128)(2,1)S(1)} %shard_map.86.refs_0_), channel_id=1, source_target_pairs={{12,0},{8,4},{4,8},{0,12},{13,1},{9,5},{5,9},{1,13},{14,2},{10,6},... | collective-permute-start | bytes 135176 | tf_op jit(solution)/shard_map/ppermute | solution.py:533
  52.3 0.6 collective-permute-start.17
  52.8 2.4 %collective-permute-start.18 = (bf16[176,128]{1,0:T(8,128)(2,1)S(1)}, bf16[176,128]{1,0:T(8,128)(2,1)S(1)}, u32[]{:S(2)}, u32[]{:S(2)}) collective-permute-start(bf16[176,128]{1,0:T(8,128)(2,1)S(1)} %shard_map.86.refs_0_), channel_id=1, source_target_pairs={{4,0},{0,4},{12,8},{8,12},{5,1},{1,5},{13,9},{9,13},{6,2},{2,6},{1... | collective-permute-start | bytes 135176 | tf_op jit(solution)/shard_map/ppermute | solution.py:533
  55.2 1.5 %collective-permute-done.16.refs_1_ = bf16[176,128]{1,0:T(8,128)(2,1)S(1)} collective-permute-done((bf16[176,128]{1,0:T(8,128)(2,1)S(1)}, bf16[176,128]{1,0:T(8,128)(2,1)S(1)}, u32[]{:S(2)}, u32[]{:S(2)}) %collective-permute-start.16) | collective-permute-done | bytes 45088 | tf_op jit(solution)/shard_map/ppermute | solution.py:533
  56.7 0.6 %collective-permute-done.17.refs_2_ = bf16[176,128]{1,0:T(8,128)(2,1)S(1)} collective-permute-done((bf16[176,128]{1,0:T(8,128)(2,1)S(1)}, bf16[176,128]{1,0:T(8,128)(2,1)S(1)}, u32[]{:S(2)}, u32[]{:S(2)}) %collective-permute-start.17) | collective-permute-done | bytes 45088 | tf_op jit(solution)/shard_map/ppermute | solution.py:533
  57.3 0.4 collective-permute-done.18.refs_3_
  57.7 1.0 %shard_map.88.refs_0_ = f32[32,1280]{1,0:T(8,128)S(1)} custom-call(f32[32,640]{1,0:T(8,128)S(1)} %get-tuple-element.60.w_ref, bf16[1280,1280]{1,0:T(8,128)(2,1)S(1)} %get-tuple-element.35.order_ref, bf16[176,128]{1,0:T(8,128)(2,1)S(1)} %shard_map.86.refs_0_, bf16[176,128]{1,0:T(8,128)(2,1)S(1)} %collective-permute-done.16.refs_1_, ...), custom_call_target="tpu_custom_call" | custom-call | tf_op jit(solution)/shard_map/pallas_call | solution.py:487
  58.7 0.1 collective-permute-start.19
  58.8 0.0 collective-permute-done.15.refs_1_
  58.8 0.8 %shard_map.87._ = f32[32,4096]{1,0:T(8,128)} custom-call(f32[32,2048]{1,0:T(8,128)S(1)} %get-tuple-element.59.h_ref.refs_0_, f32[32,2048]{1,0:T(8,128)S(1)} %collective-permute-done.15.refs_1_), custom_call_target="tpu_custom_call" | custom-call | tf_op jit(solution)/shard_map/pallas_call | solution.py:487
  59.6 0.5 collective-permute-done.19.refs_1_
  60.1 0.7 %shard_map.89 = f32[32,1280]{1,0:T(8,128)} custom-call(f32[32,4096]{1,0:T(8,128)} %shard_map.87._, f32[32,1280]{1,0:T(8,128)S(1)} %shard_map.88.refs_0_, f32[32,1280]{1,0:T(8,128)S(1)} %collective-permute-done.19.refs_1_), custom_call_target="tpu_custom_call" | custom-call | tf_op jit(solution)/shard_map/pallas_call | solution.py:487
  (1 shorter events, 0.0 us)
Async XLA Ops:
  2.1 7.1 %collective-permute-start = (bf16[32,2176]{1,0:T(8,128)(2,1)S(1)}, bf16[32,2176]{1,0:T(8,128)(2,1)S(1)}, u32[]{:S(2)}, u32[]{:S(2)}) collective-permute-start(bf16[32,2176]{1,0:T(8,128)(2,1)S(1)} %get-tuple-element.36), channel_id=1, source_target_pairs={{0,2},{2,0},{1,3},{3,1},{4,6},{6,4},{5,7},{7,5},{8,10},{10,8},{9,1... | collective-permute-start | bytes 417800 | tf_op jit(solution)/shard_map/ppermute | solution.py:527
  9.2 5.0 %collective-permute-start.2 = (bf16[64,128]{1,0:T(8,128)(2,1)S(1)}, bf16[64,128]{1,0:T(8,128)(2,1)S(1)}, u32[]{:S(2)}, u32[]{:S(2)}) collective-permute-start(bf16[64,128]{1,0:T(8,128)(2,1)S(1)} %shard_map.70.refs_0_), channel_id=1, source_target_pairs={{2,1},{3,4},{6,5},{7,8},{10,9},{11,12},{14,13},{1,2},{4,3},{5,6},{... | collective-permute-start | bytes 49160 | tf_op jit(solution)/shard_map/ppermute | solution.py:581
  11.6 6.1 %collective-permute-start.1 = (bf16[336,128]{1,0:T(8,128)(2,1)S(1)}, bf16[336,128]{1,0:T(8,128)(2,1)S(1)}, u32[]{:S(2)}, u32[]{:S(2)}) collective-permute-start(bf16[336,128]{1,0:T(8,128)(2,1)S(1)} %get-tuple-element.39.w_ref.refs_0_), channel_id=1, source_target_pairs={{0,2},{2,0},{1,3},{3,1},{4,6},{6,4},{5,7},{7,5},{8,10},{10,8},{9,1... | collective-permute-start | bytes 258056 | tf_op jit(solution)/shard_map/ppermute | solution.py:527
  20.0 3.4 %collective-permute-start.3 = (f32[32,672]{1,0:T(8,128)S(1)}, f32[32,672]{1,0:T(8,128)S(1)}, u32[]{:S(2)}, u32[]{:S(2)}) collective-permute-start(f32[32,672]{1,0:T(8,128)S(1)} %get-tuple-element.45), channel_id=1, source_target_pairs={{0,1},{1,0},{2,3},{3,2},{4,5},{5,4},{6,7},{7,6},{8,9},{9,8},{10,11... | collective-permute-start | bytes 258056 | tf_op jit(solution)/shard_map/ppermute | solution.py:530
  23.2 1.3 %collective-permute-start.4 = (f32[32,640]{1,0:T(8,128)S(1)}, f32[32,640]{1,0:T(8,128)S(1)}, u32[]{:S(2)}, u32[]{:S(2)}) collective-permute-start(f32[32,640]{1,0:T(8,128)S(1)} %get-tuple-element.48), channel_id=1, source_target_pairs={{0,1},{1,0},{2,3},{3,2},{4,5},{5,4},{6,7},{7,6},{8,9},{9,8},{10,11... | collective-permute-start | bytes 245768 | tf_op jit(solution)/shard_map/ppermute | solution.py:530
  23.4 4.1 %collective-permute-start.5 = (bf16[176,128]{1,0:T(8,128)(2,1)S(1)}, bf16[176,128]{1,0:T(8,128)(2,1)S(1)}, u32[]{:S(2)}, u32[]{:S(2)}) collective-permute-start(bf16[176,128]{1,0:T(8,128)(2,1)S(1)} %get-tuple-element.46.refs_0_), channel_id=1, source_target_pairs={{0,2},{2,0},{1,3},{3,1},{4,6},{6,4},{5,7},{7,5},{8,10},{10,8},{9,1... | collective-permute-start | bytes 135176 | tf_op jit(solution)/shard_map/ppermute | solution.py:527
  27.7 6.2 %collective-permute-start.6 = (bf16[176,128]{1,0:T(8,128)(2,1)S(1)}, bf16[176,128]{1,0:T(8,128)(2,1)S(1)}, u32[]{:S(2)}, u32[]{:S(2)}) collective-permute-start(bf16[176,128]{1,0:T(8,128)(2,1)S(1)} %shard_map.78.refs_0_), channel_id=1, source_target_pairs={{12,0},{8,4},{4,8},{0,12},{13,1},{9,5},{5,9},{1,13},{14,2},{10,6},... | collective-permute-start | bytes 135176 | tf_op jit(solution)/shard_map/ppermute | solution.py:533
  31.1 4.9 %collective-permute-start.7 = (bf16[176,128]{1,0:T(8,128)(2,1)S(1)}, bf16[176,128]{1,0:T(8,128)(2,1)S(1)}, u32[]{:S(2)}, u32[]{:S(2)}) collective-permute-start(bf16[176,128]{1,0:T(8,128)(2,1)S(1)} %shard_map.78.refs_0_), channel_id=1, source_target_pairs={{8,0},{12,4},{0,8},{4,12},{9,1},{13,5},{1,9},{5,13},{10,2},{14,6},... | collective-permute-start | bytes 135176 | tf_op jit(solution)/shard_map/ppermute | solution.py:533
  31.1 4.9 %collective-permute-start.8 = (bf16[176,128]{1,0:T(8,128)(2,1)S(1)}, bf16[176,128]{1,0:T(8,128)(2,1)S(1)}, u32[]{:S(2)}, u32[]{:S(2)}) collective-permute-start(bf16[176,128]{1,0:T(8,128)(2,1)S(1)} %shard_map.78.refs_0_), channel_id=1, source_target_pairs={{4,0},{0,4},{12,8},{8,12},{5,1},{1,5},{13,9},{9,13},{6,2},{2,6},{1... | collective-permute-start | bytes 135176 | tf_op jit(solution)/shard_map/ppermute | solution.py:533
  36.7 1.2 %collective-permute-start.9 = (bf16[176,128]{1,0:T(8,128)(2,1)S(1)}, bf16[176,128]{1,0:T(8,128)(2,1)S(1)}, u32[]{:S(2)}, u32[]{:S(2)}) collective-permute-start(bf16[176,128]{1,0:T(8,128)(2,1)S(1)} %get-tuple-element.49.refs_0_), channel_id=1, source_target_pairs={{0,1},{1,0},{2,3},{3,2},{4,5},{5,4},{6,7},{7,6},{8,9},{9,8},{10,11... | collective-permute-start | bytes 135176 | tf_op jit(solution)/shard_map/ppermute | solution.py:530
  36.8 4.1 %collective-permute-start.10 = (bf16[176,128]{1,0:T(8,128)(2,1)S(1)}, bf16[176,128]{1,0:T(8,128)(2,1)S(1)}, u32[]{:S(2)}, u32[]{:S(2)}) collective-permute-start(bf16[176,128]{1,0:T(8,128)(2,1)S(1)} %get-tuple-element.49.refs_0_), channel_id=1, source_target_pairs={{0,2},{2,0},{1,3},{3,1},{4,6},{6,4},{5,7},{7,5},{8,10},{10,8},{9,1... | collective-permute-start | bytes 135176 | tf_op jit(solution)/shard_map/ppermute | solution.py:527
  40.9 1.2 %collective-permute-start.11 = (bf16[176,128]{1,0:T(8,128)(2,1)S(1)}, bf16[176,128]{1,0:T(8,128)(2,1)S(1)}, u32[]{:S(2)}, u32[]{:S(2)}) collective-permute-start(bf16[176,128]{1,0:T(8,128)(2,1)S(1)} %collective-permute-done.10.refs_0_.refs_2_), channel_id=1, source_target_pairs={{0,1},{1,0},{2,3},{3,2},{4,5},{5,4},{6,7},{7,6},{8,9},{9,8},{10,11... | collective-permute-start | bytes 135176 | tf_op jit(solution)/shard_map/ppermute | solution.py:530
  43.8 2.2 %collective-permute-start.12 = (f32[32,672]{1,0:T(8,128)S(1)}, f32[32,672]{1,0:T(8,128)S(1)}, u32[]{:S(2)}, u32[]{:S(2)}) collective-permute-start(f32[32,672]{1,0:T(8,128)S(1)} %get-tuple-element.55), channel_id=1, source_target_pairs={{0,1},{1,0},{2,3},{3,2},{4,5},{5,4},{6,7},{7,6},{8,9},{9,8},{10,11... | collective-permute-start | bytes 258056 | tf_op jit(solution)/shard_map/ppermute | solution.py:530
  45.6 1.7 %collective-permute-start.13 = (f32[32,640]{1,0:T(8,128)S(1)}, f32[32,640]{1,0:T(8,128)S(1)}, u32[]{:S(2)}, u32[]{:S(2)}) collective-permute-start(f32[32,640]{1,0:T(8,128)S(1)} %get-tuple-element.58), channel_id=1, source_target_pairs={{0,1},{1,0},{2,3},{3,2},{4,5},{5,4},{6,7},{7,6},{8,9},{9,8},{10,11... | collective-permute-start | bytes 245768 | tf_op jit(solution)/shard_map/ppermute | solution.py:530
  46.1 4.1 %collective-permute-start.14 = (bf16[176,128]{1,0:T(8,128)(2,1)S(1)}, bf16[176,128]{1,0:T(8,128)(2,1)S(1)}, u32[]{:S(2)}, u32[]{:S(2)}) collective-permute-start(bf16[176,128]{1,0:T(8,128)(2,1)S(1)} %get-tuple-element.56.refs_0_), channel_id=1, source_target_pairs={{0,2},{2,0},{1,3},{3,1},{4,6},{6,4},{5,7},{7,5},{8,10},{10,8},{9,1... | collective-permute-start | bytes 135176 | tf_op jit(solution)/shard_map/ppermute | solution.py:527
  50.4 8.4 %collective-permute-start.15 = (f32[32,2048]{1,0:T(8,128)S(1)}, f32[32,2048]{1,0:T(8,128)S(1)}, u32[]{:S(2)}, u32[]{:S(2)}) collective-permute-start(f32[32,2048]{1,0:T(8,128)S(1)} %get-tuple-element.59.h_ref.refs_0_), channel_id=1, source_target_pairs={{0,2},{2,0},{1,3},{3,1},{4,6},{6,4},{5,7},{7,5},{8,10},{10,8},{9,1... | collective-permute-start | bytes 786440 | tf_op jit(solution)/shard_map/ppermute | solution.py:527
  50.8 5.8 %collective-permute-start.16 = (bf16[176,128]{1,0:T(8,128)(2,1)S(1)}, bf16[176,128]{1,0:T(8,128)(2,1)S(1)}, u32[]{:S(2)}, u32[]{:S(2)}) collective-permute-start(bf16[176,128]{1,0:T(8,128)(2,1)S(1)} %shard_map.86.refs_0_), channel_id=1, source_target_pairs={{12,0},{8,4},{4,8},{0,12},{13,1},{9,5},{5,9},{1,13},{14,2},{10,6},... | collective-permute-start | bytes 135176 | tf_op jit(solution)/shard_map/ppermute | solution.py:533
  52.3 5.0 %collective-permute-start.17 = (bf16[176,128]{1,0:T(8,128)(2,1)S(1)}, bf16[176,128]{1,0:T(8,128)(2,1)S(1)}, u32[]{:S(2)}, u32[]{:S(2)}) collective-permute-start(bf16[176,128]{1,0:T(8,128)(2,1)S(1)} %shard_map.86.refs_0_), channel_id=1, source_target_pairs={{8,0},{12,4},{0,8},{4,12},{9,1},{13,5},{1,9},{5,13},{10,2},{14,6},... | collective-permute-start | bytes 135176 | tf_op jit(solution)/shard_map/ppermute | solution.py:533
  52.8 4.9 %collective-permute-start.18 = (bf16[176,128]{1,0:T(8,128)(2,1)S(1)}, bf16[176,128]{1,0:T(8,128)(2,1)S(1)}, u32[]{:S(2)}, u32[]{:S(2)}) collective-permute-start(bf16[176,128]{1,0:T(8,128)(2,1)S(1)} %shard_map.86.refs_0_), channel_id=1, source_target_pairs={{4,0},{0,4},{12,8},{8,12},{5,1},{1,5},{13,9},{9,13},{6,2},{2,6},{1... | collective-permute-start | bytes 135176 | tf_op jit(solution)/shard_map/ppermute | solution.py:533
  58.7 1.5 %collective-permute-start.19 = (f32[32,1280]{1,0:T(8,128)S(1)}, f32[32,1280]{1,0:T(8,128)S(1)}, u32[]{:S(2)}, u32[]{:S(2)}) collective-permute-start(f32[32,1280]{1,0:T(8,128)S(1)} %shard_map.88.refs_0_), channel_id=1, source_target_pairs={{0,1},{1,0},{2,3},{3,2},{4,5},{5,4},{6,7},{7,6},{8,9},{9,8},{10,11... | collective-permute-start | bytes 491528 | tf_op jit(solution)/shard_map/ppermute | solution.py:530

commit v14 on v13

--- a/solution.py
+++ b/solution.py
@@ -14,8 +14,7 @@
 TAPS = 128
 HALF = TAPS // 2
 LANES = 128
-CUTS = (8, 16, 24, 32, NF)
-AHEAD = CUTS[0]
+CUTS = (0, 2, 8, 16, 24, 32, NF)
 F32 = jnp.float32
 BF16 = jnp.bfloat16
 HIGH = lax.Precision.HIGHEST
@@ -120,16 +119,17 @@
             out_ref[at * cl : (at + 1) * cl, :] = ref[:, width - TAPS :]
 
 
-def cut_kernel(rows, frames, sig_hbm, tab_hbm, *refs):
-    out_refs, (tab_ref, sems) = refs[:rows], refs[rows:]
-    window, x_me = sig_hbm.shape[1], lax.axis_index("row")
-    width = out_refs[0].shape[1]
+def window_of(shift, rows, frames, width, window):
+    target = lax.rem(lax.axis_index("row") + shift, rows)
+    return pl.ds(pl.multiple_of(jnp.clip(target * frames - TAPS, 0, window - width), TAPS), width)
+
+
+def cut_kernel(rows, frames, sig_hbm, *refs):
+    out_refs, sems = refs[:-1], refs[-1]
     copies = []
-    for shift in reversed(range(rows)):
-        target = lax.rem(x_me + shift, rows)
-        begin = pl.multiple_of(jnp.clip(target * frames - TAPS, 0, window - width), TAPS)
-        copies.append(pltpu.make_async_copy(sig_hbm.at[:, pl.ds(begin, width)], out_refs[shift], sems.at[shift]))
-    copies.append(pltpu.make_async_copy(tab_hbm.at[:AHEAD], tab_ref, sems.at[rows]))
+    for at, ref in enumerate(out_refs):
+        span = window_of(at + 1, rows, frames, ref.shape[1], sig_hbm.shape[1])
+        copies.append(pltpu.make_async_copy(sig_hbm.at[:, span], ref, sems.at[at]))
     for copy in copies:
         copy.start()
     for copy in copies:
@@ -212,19 +212,15 @@
     return (co[:, :TAPS] * co[:, :TAPS] + co[:, TAPS:] * co[:, TAPS:]).astype(BF16)
 
 
-def table_at(f, ahead_ref, tab_ref):
-    return ahead_ref[f] if f < AHEAD else tab_ref[f - AHEAD]
-
-
-def own_spectra_kernel(rows, sig_ref, ahead_ref, w_hbm, h_hbm, order_hbm, tab_hbm, *refs):
-    s_ref, w_ref, old_ref, order_ref, tab_ref, xp_scr, x_scr, sems, tab_sems = refs
+def own_spectra_kernel(rows, sig_hbm, w_hbm, h_hbm, order_hbm, tab_hbm, *refs):
+    s_ref, sig_ref, w_ref, old_ref, order_ref, tab_ref, xp_scr, x_scr, sems, tab_sems = refs
     _, blocks, _, cl, _ = s_ref.shape
     frames = blocks * TAPS
     x_me = lax.axis_index("row")
     mine = pl.ds(pl.multiple_of(x_me * frames, TAPS), frames)
 
     table = [
-        pltpu.make_async_copy(tab_hbm.at[begin:end], tab_ref.at[begin - AHEAD : end - AHEAD], tab_sems.at[at])
+        pltpu.make_async_copy(tab_hbm.at[begin:end], tab_ref.at[begin:end], tab_sems.at[at])
         for at, (begin, end) in enumerate(zip(CUTS, CUTS[1:]))
     ]
     later = [
@@ -232,8 +228,12 @@
         pltpu.make_async_copy(order_hbm, order_ref, sems.at[1]),
         pltpu.make_async_copy(h_hbm.at[:, mine], old_ref, sems.at[2]),
     ]
+    own_span = window_of(0, rows, frames, sig_ref.shape[1], sig_hbm.shape[1])
+    own_copy = pltpu.make_async_copy(sig_hbm.at[:, own_span], sig_ref, sems.at[3])
+    own_copy.start()
     for copy in table:
         copy.start()
+    own_copy.wait()
     place_signal(sig_ref, xp_scr, rows, frames)
     first = jnp.where(x_me == 0, 1, 0)
     for at in range(blocks - 1):
@@ -243,16 +243,16 @@
     for f in range(NF):
         if f in CUTS:
             table[CUTS.index(f)].wait()
-        if f == CUTS[1]:
+        if f == CUTS[3]:
             for copy in later:
                 copy.start()
-        power = power_of(x_scr, table_at(f, ahead_ref, tab_ref))
+        power = power_of(x_scr, tab_ref[f])
         s_ref[f, pl.ds(first, blocks - 1), x_me] = power.reshape(blocks - 1, cl, TAPS)
     for copy in later:
         copy.wait()
 
 
-def other_spectra_kernel(rows, halo_ref, ahead_ref, tab_ref, *refs):
+def other_spectra_kernel(rows, halo_ref, tab_ref, *refs):
     sig_refs, (s_ref, xp_scr, x_scr) = refs[:rows], refs[-3:]
     _, blocks, _, cl, _ = s_ref.shape
     frames = blocks * TAPS
@@ -280,7 +280,7 @@
             x_scr[at : at + cl, :] = xp_scr[owners[shift], :, blk * TAPS : (blk + 2) * TAPS]
 
     for f in range(NF):
-        power = power_of(x_scr, table_at(f, ahead_ref, tab_ref))
+        power = power_of(x_scr, tab_ref[f])
         s_ref[f, outer, x_me] = power[:cl]
         for shift in range(1, rows):
             line = cl * (1 + (shift - 1) * blocks)
@@ -536,41 +536,41 @@
         return (at // subs * rows + x) * subs + at % subs
 
     table, order = hbm(jnp.asarray(toeplitz())), jnp.asarray(reorder(cl))
-    *cuts, ahead = call(
+    cuts = call(
         functools.partial(cut_kernel, rows, frames),
-        [hbm(signal), table],
-        [((cl, width), BF16)] * rows + [pltpu.VMEM((AHEAD,) + table.shape[1:], BF16)],
-        [pltpu.SemaphoreType.DMA((rows + 1,))],
-        in_specs=[anywhere] * 2,
-    )
-    own_sig, *out_sigs = cuts
-    ahead = vmem(ahead)
-    sig = [own_sig] + [row_shift(part, shift + 1) for shift, part in enumerate(out_sigs)]
+        [hbm(signal)],
+        [((cl, width), BF16)] * (rows - 1),
+        [pltpu.SemaphoreType.DMA((rows,))],
+        in_specs=[anywhere],
+    )
+    sig = [row_shift(part, shift + 1) for shift, part in enumerate(cuts)]
+
     msg = (message(rank, size), BF16)
     piece = ((rank, size), F32)
     update_outs = [((rank, frames), F32), ((rank, rank), F32)]
     update_outs += [((rank, size + rank), F32)] * ((rows - 1) * (subs - 1))
-    half_done, w_own, old, order, table = call(
+    half_done, own_sig, w_own, old, order, table = call(
         functools.partial(own_spectra_kernel, rows),
-        [own_sig, ahead, hbm(w_start.T), hbm(h_start), hbm(order), table],
+        [hbm(signal), hbm(w_start.T), hbm(h_start), hbm(order), table],
         [
             pltpu.VMEM((NF, blocks, rows, cl, TAPS), BF16),
+            pltpu.VMEM((cl, width), BF16),
             pltpu.VMEM((rank, NF * cl), F32),
             pltpu.VMEM((rank, frames), F32),
             pltpu.VMEM(order.shape, BF16),
-            pltpu.VMEM((NF - AHEAD,) + table.shape[1:], BF16),
+            pltpu.VMEM(table.shape, BF16),
         ],
         [
             pltpu.VMEM((cl, frames + TAPS), BF16),
             pltpu.VMEM(((blocks - 1) * cl, 2 * TAPS), BF16),
-            pltpu.SemaphoreType.DMA((3,)),
+            pltpu.SemaphoreType.DMA((4,)),
             pltpu.SemaphoreType.DMA((len(CUTS) - 1,)),
         ],
-        in_specs=[whole] * 2 + [anywhere] * 4,
+        in_specs=[anywhere] * 5,
         limit=8,
         cost=2 * NF * cl * frames * 4 * TAPS,
     )
-    order = vmem(order)
+    order, sig = vmem(order), [vmem(own_sig)] + sig
     (edge,) = call(
         functools.partial(edges_kernel, rows),
         sig + [vmem(half_done)],
@@ -594,16 +594,16 @@
     )
     (spectra,) = call(
         functools.partial(other_spectra_kernel, rows),
-        [halo, ahead, vmem(table)] + sig + [vmem(half_done), early],
+        [halo, vmem(table)] + sig + [vmem(half_done), early],
         [pltpu.VMEM((NF, blocks, rows, cl, TAPS), BF16)],
         [
             pltpu.VMEM((rows, cl, frames + TAPS), BF16),
             pltpu.VMEM((((rows - 1) * blocks + 1) * cl, 2 * TAPS), BF16),
         ],
-        in_specs=[whole] * (rows + 3) + [anywhere] * 2,
+        in_specs=[whole] * (rows + 2) + [anywhere] * 2,
         limit=8,
         cost=2 * NF * chans * frames * 4 * TAPS,
-        aliases={rows + 3: 0},
+        aliases={rows + 2: 0},
     )
     spectra = vmem(spectra)
 

time: 61.2 us -> 62.8 us (1.026)
  Pallas kernels: 24.9 us -> 26.7 us
  starting transfers between devices: 19.1 us -> 18.4 us
    pallas_call x22, Pallas kernels: 24.9 us -> 26.7 us  [call(): pl.pallas_call(kernel, out_shape=[jax.ShapeDtypeStruct(*out) if isinstanc...]
    ppermute x6, starting transfers between devices: 7.22 us -> 6.44 us  [row_shift(): lax.ppermute(value, 'row', [(i, (i + shift) % rows) for i in range(rows)])]
  transfers between devices with their start and end apart: 20 -> 20, of which waited for: 11 -> 11; matrix products, arithmetic and copies ran while one was open for 0% -> 0% of each run, Pallas kernels for 29% -> 32%
where the time goes in v14:
time: 62.8 us; the launch traced here: 62.6 us
  Pallas kernels  26.7 us (43%)
  starting transfers between devices  18.4 us (29%)
  waiting for transfers between devices  16.6 us (26%)
  between operations  0.94 us (1%)
    pallas_call x22, Pallas kernels, call(): pl.pallas_call(kernel, out_shape=[jax.ShapeDtypeStruct(*out) if isinstanc...  26.7 us
    ppermute x6, starting transfers between devices, frm_shift(): lax.ppermute(value, 'frm', [(partner(i, shift, frms), i) for i in range(f...  8.78 us
    ppermute x6, waiting for transfers between devices, row_shift(): lax.ppermute(value, 'row', [(i, (i + shift) % rows) for i in range(rows)])  7.74 us
    ppermute x6, waiting for transfers between devices, frm_shift(): lax.ppermute(value, 'frm', [(partner(i, shift, frms), i) for i in range(f...  6.51 us
    ppermute x6, starting transfers between devices, row_shift(): lax.ppermute(value, 'row', [(i, (i + shift) % rows) for i in range(rows)])  6.44 us
    ppermute x7, starting transfers between devices, sub_shift(): lax.ppermute(value, 'sub', [(i, (i + shift) % subs) for i in range(subs)])  2.56 us
    ppermute x7, waiting for transfers between devices, sub_shift(): lax.ppermute(value, 'sub', [(i, (i + shift) % subs) for i in range(subs)])  2.3 us
  transfers between devices with their start and end apart: 20, of which 11 were waited for; matrix products, arithmetic and copies ran while one was open for 0% of the time, Pallas kernels for 32%

profile of v14, /device:TPU:0, one launch (start us, length us, event | category | flops | bytes accessed | tf_op | source)
XLA Modules:
  0.0 62.6 jit_solution(6407555466030118672)
XLA Ops:
  0.6 0.9 %shard_map.69 = bf16[32,2176]{1,0:T(8,128)(2,1)S(1)} custom-call(bf16[32,4096]{1,0:T(8,128)(2,1)} %sig_hbm.3), custom_call_target="tpu_custom_call" | custom-call | tf_op jit(solution)/shard_map/pallas_call | solution.py:487
  1.6 3.0 %collective-permute-start = (bf16[32,2176]{1,0:T(8,128)(2,1)S(1)}, bf16[32,2176]{1,0:T(8,128)(2,1)S(1)}, u32[]{:S(2)}, u32[]{:S(2)}) collective-permute-start(bf16[32,2176]{1,0:T(8,128)(2,1)S(1)} %shard_map.69), channel_id=1, source_target_pairs={{0,2},{2,0},{1,3},{3,1},{4,6},{6,4},{5,7},{7,5},{8,10},{10,8},{9,1... | collective-permute-start | bytes 417800 | tf_op jit(solution)/shard_map/ppermute | solution.py:527
  4.6 6.3 %shard_map.68 = (bf16[40,16,2,32,128]{4,3,2,1,0:T(8,128)(2,1)S(1)}, bf16[32,2176]{1,0:T(8,128)(2,1)S(1)}, f32[32,1280]{1,0:T(8,128)S(1)}, f32[32,2048]{1,0:T(8,1...) custom-call(bf16[32,4096]{1,0:T(8,128)(2,1)} %sig_hbm.3, f32[32,1280]{1,0:T(8,128)} %bitcast.3, ...), custom_call_target="tpu_custom_call" | custom-call | flops 2684354560 | tf_op jit(solution)/shard_map/pallas_call | solution.py:487
  10.9 0.0 collective-permute-done.refs_0_.refs_1_
  11.0 0.7 %collective-permute-start.2 = (bf16[64,128]{1,0:T(8,128)(2,1)S(1)}, bf16[64,128]{1,0:T(8,128)(2,1)S(1)}, u32[]{:S(2)}, u32[]{:S(2)}) collective-permute-start(bf16[64,128]{1,0:T(8,128)(2,1)S(1)} %shard_map.70.refs_0_), channel_id=1, source_target_pairs={{2,1},{3,4},{6,5},{7,8},{10,9},{11,12},{14,13},{1,2},{4,3},{5,6},{... | collective-permute-start | bytes 49160 | tf_op jit(solution)/shard_map/ppermute | solution.py:581
  11.6 0.8 %shard_map.71 = (f32[32,640]{1,0:T(8,128)S(1)}, bf16[336,128]{1,0:T(8,128)(2,1)S(1)}) custom-call(f32[32,1280]{1,0:T(8,128)S(1)} %get-tuple-element.30.w_ref, bf16[1280,1280]{1,0:T(8,128)(2,1)S(1)} %get-tuple-element.31.order_ref, bf16[64,128]{1,0:T(8,128)(2,1)S(1)} %shard_map.70.refs_0_), custom_call_target="tpu_custom_call" | custom-call | tf_op jit(solution)/shard_map/pallas_call | solution.py:487
  12.5 0.9 %shard_map.72.refs_3_.refs_2_ = f32[32,2048]{1,0:T(8,128)S(1)} custom-call(bf16[336,128]{1,0:T(8,128)(2,1)S(1)} %get-tuple-element.35.w_ref.refs_0_, bf16[40,16,2,32,128]{4,3,2,1,0:T(8,128)(2,1)S(1)} %get-tuple-element.33.refs_1_.s_ref.refs_2_), custom_call_target="tpu_custom_call" | custom-call | flops 1342177280 | tf_op jit(solution)/shard_map/pallas_call | solution.py:487
  13.4 2.5 %collective-permute-start.1 = (bf16[336,128]{1,0:T(8,128)(2,1)S(1)}, bf16[336,128]{1,0:T(8,128)(2,1)S(1)}, u32[]{:S(2)}, u32[]{:S(2)}) collective-permute-start(bf16[336,128]{1,0:T(8,128)(2,1)S(1)} %get-tuple-element.35.w_ref.refs_0_), channel_id=1, source_target_pairs={{0,2},{2,0},{1,3},{3,1},{4,6},{6,4},{5,7},{7,5},{8,10},{10,8},{9,1... | collective-permute-start | bytes 258056 | tf_op jit(solution)/shard_map/ppermute | solution.py:527
  15.9 0.0 collective-permute-done.2.halo_ref
  15.9 3.5 %shard_map.73.refs_4_.s_ref.refs_2_.refs_6_ = bf16[40,16,2,32,128]{4,3,2,1,0:T(8,128)(2,1)S(1)} custom-call(bf16[64,128]{1,0:T(8,128)(2,1)S(1)} %collective-permute-done.2.halo_ref, bf16[40,256,256]{2,1,0:T(8,128)(2,1)S(1)} %get-tuple-element.37.tab_ref, bf16[32,2176]{1,0:T(8,128)(2,1)S(1)} %get-tuple-element.32.sig_ref.refs_0_, ...), custom_call_target="tpu_custom_call", output_to_operand_aliasing={{}: (4, {})} | custom-call | flops 5368709120 | tf_op jit(solution)/shard_map/pallas_call | solution.py:487
  19.4 0.0 collective-permute-done.1.refs_1_
  19.4 2.2 %shard_map.74 = (f32[32,2048]{1,0:T(8,128)S(1)}, f32[32,32]{1,0:T(8,128)S(1)}, f32[32,672]{1,0:T(8,128)S(1)}) custom-call(bf16[336,128]{1,0:T(8,128)(2,1)S(1)} %get-tuple-element.35.w_ref.refs_0_, bf16[336,128]{1,0:T(8,128)(2,1)S(1)} %collective-permute-done.1.refs_1_, f32[32,2048]{1,0:T(8,128)S(1)} %shard_map.72.refs_3_.refs_2_, ...), custom_call_target="tpu_custom_call" | custom-call | tf_op jit(solution)/shard_map/pallas_call | solution.py:487
  21.6 1.8 %collective-permute-start.3 = (f32[32,672]{1,0:T(8,128)S(1)}, f32[32,672]{1,0:T(8,128)S(1)}, u32[]{:S(2)}, u32[]{:S(2)}) collective-permute-start(f32[32,672]{1,0:T(8,128)S(1)} %get-tuple-element.41), channel_id=1, source_target_pairs={{0,1},{1,0},{2,3},{3,2},{4,5},{5,4},{6,7},{7,6},{8,9},{9,8},{10,11... | collective-permute-start | bytes 258056 | tf_op jit(solution)/shard_map/ppermute | solution.py:530
  23.4 1.6 %shard_map.75 = (f32[32,640]{1,0:T(8,128)S(1)}, f32[32,640]{1,0:T(8,128)S(1)}) custom-call(f32[32,2048]{1,0:T(8,128)S(1)} %get-tuple-element.38.h_ref.refs_5_, bf16[40,16,2,32,128]{4,3,2,1,0:T(8,128)(2,1)S(1)} %shard_map.73.refs_4_.s_ref.refs_2_.refs_6_), custom_call_target="tpu_custom_call" | custom-call | flops 1342177280 | tf_op jit(solution)/shard_map/pallas_call | solution.py:487
  25.0 0.1 collective-permute-start.4
  25.1 0.0 collective-permute-done.3.refs_2_
  25.1 0.1 shard_map.76
  25.2 0.3 collective-permute-start.5
  25.5 0.8 %shard_map.77.own_ref = f32[32,640]{1,0:T(8,128)S(1)} custom-call(f32[32,2048]{1,0:T(8,128)S(1)} %get-tuple-element.38.h_ref.refs_5_, bf16[40,16,2,32,128]{4,3,2,1,0:T(8,128)(2,1)S(1)} %shard_map.73.refs_4_.s_ref.refs_2_.refs_6_, bf16[176,128]{1,0:T(8,128)(2,1)S(1)} %get-tuple-element.42.refs_0_), custom_call_target="tpu_custom_call" | custom-call | flops 1 | tf_op jit(solution)/shard_map/pallas_call | solution.py:487
  26.4 0.0 collective-permute-done.4.refs_0_
  26.4 2.9 %collective-permute-done.5.refs_1_ = bf16[176,128]{1,0:T(8,128)(2,1)S(1)} collective-permute-done((bf16[176,128]{1,0:T(8,128)(2,1)S(1)}, bf16[176,128]{1,0:T(8,128)(2,1)S(1)}, u32[]{:S(2)}, u32[]{:S(2)}) %collective-permute-start.5) | collective-permute-done | bytes 45088 | tf_op jit(solution)/shard_map/ppermute | solution.py:527
  29.2 0.2 shard_map.78.refs_0_
  29.5 3.5 %collective-permute-start.6 = (bf16[176,128]{1,0:T(8,128)(2,1)S(1)}, bf16[176,128]{1,0:T(8,128)(2,1)S(1)}, u32[]{:S(2)}, u32[]{:S(2)}) collective-permute-start(bf16[176,128]{1,0:T(8,128)(2,1)S(1)} %shard_map.78.refs_0_), channel_id=1, source_target_pairs={{12,0},{8,4},{4,8},{0,12},{13,1},{9,5},{5,9},{1,13},{14,2},{10,6},... | collective-permute-start | bytes 135176 | tf_op jit(solution)/shard_map/ppermute | solution.py:533
  32.9 0.0 collective-permute-start.7
  32.9 0.9 %collective-permute-start.8 = (bf16[176,128]{1,0:T(8,128)(2,1)S(1)}, bf16[176,128]{1,0:T(8,128)(2,1)S(1)}, u32[]{:S(2)}, u32[]{:S(2)}) collective-permute-start(bf16[176,128]{1,0:T(8,128)(2,1)S(1)} %shard_map.78.refs_0_), channel_id=1, source_target_pairs={{4,0},{0,4},{12,8},{8,12},{5,1},{1,5},{13,9},{9,13},{6,2},{2,6},{1... | collective-permute-start | bytes 135176 | tf_op jit(solution)/shard_map/ppermute | solution.py:533
  33.9 1.8 %collective-permute-done.6.refs_1_ = bf16[176,128]{1,0:T(8,128)(2,1)S(1)} collective-permute-done((bf16[176,128]{1,0:T(8,128)(2,1)S(1)}, bf16[176,128]{1,0:T(8,128)(2,1)S(1)}, u32[]{:S(2)}, u32[]{:S(2)}) %collective-permute-start.6) | collective-permute-done | bytes 45088 | tf_op jit(solution)/shard_map/ppermute | solution.py:533
  35.6 2.2 %collective-permute-done.7.refs_2_ = bf16[176,128]{1,0:T(8,128)(2,1)S(1)} collective-permute-done((bf16[176,128]{1,0:T(8,128)(2,1)S(1)}, bf16[176,128]{1,0:T(8,128)(2,1)S(1)}, u32[]{:S(2)}, u32[]{:S(2)}) %collective-permute-start.7) | collective-permute-done | bytes 45088 | tf_op jit(solution)/shard_map/ppermute | solution.py:533
  37.9 0.0 collective-permute-done.8.refs_3_
  37.9 0.7 %shard_map.79 = (f32[32,640]{1,0:T(8,128)S(1)}, bf16[176,128]{1,0:T(8,128)(2,1)S(1)}) custom-call(f32[32,640]{1,0:T(8,128)S(1)} %get-tuple-element.34.w_ref, bf16[176,128]{1,0:T(8,128)(2,1)S(1)} %shard_map.78.refs_0_, bf16[176,128]{1,0:T(8,128)(2,1)S(1)} %collective-permute-done.6.refs_1_, bf16[176,128]{1,0:T(8,128)(2,1)S(1)} %collective-permute-done.7.refs_2_, ...), custom_call_target="tpu_custom_call" | custom-call | tf_op jit(solution)/shard_map/pallas_call | solution.py:487
  38.5 0.0 collective-permute-start.9
  38.6 0.1 collective-permute-start.10
  38.7 1.1 %collective-permute-done.9.refs_1_ = bf16[176,128]{1,0:T(8,128)(2,1)S(1)} collective-permute-done((bf16[176,128]{1,0:T(8,128)(2,1)S(1)}, bf16[176,128]{1,0:T(8,128)(2,1)S(1)}, u32[]{:S(2)}, u32[]{:S(2)}) %collective-permute-start.9) | collective-permute-done | bytes 45088 | tf_op jit(solution)/shard_map/ppermute | solution.py:530
  39.8 1.0 %shard_map.80.refs_1_ = f32[32,2048]{1,0:T(8,128)S(1)} custom-call(bf16[176,128]{1,0:T(8,128)(2,1)S(1)} %get-tuple-element.45.refs_0_, bf16[176,128]{1,0:T(8,128)(2,1)S(1)} %collective-permute-done.9.refs_1_, bf16[40,16,2,32,128]{4,3,2,1,0:T(8,128)(2,1)S(1)} %shard_map.73.refs_4_.s_ref.refs_2_.refs_6_), custom_call_target="tpu_custom_call" | custom-call | flops 1342177280 | tf_op jit(solution)/shard_map/pallas_call | solution.py:487
  40.8 1.9 %collective-permute-done.10.refs_0_.refs_2_ = bf16[176,128]{1,0:T(8,128)(2,1)S(1)} collective-permute-done((bf16[176,128]{1,0:T(8,128)(2,1)S(1)}, bf16[176,128]{1,0:T(8,128)(2,1)S(1)}, u32[]{:S(2)}, u32[]{:S(2)}) %collective-permute-start.10) | collective-permute-done | bytes 45088 | tf_op jit(solution)/shard_map/ppermute | solution.py:527
  42.7 0.0 collective-permute-start.11
  42.7 0.6 shard_map.81.refs_4_
  43.2 0.7 %collective-permute-done.11.refs_3_ = bf16[176,128]{1,0:T(8,128)(2,1)S(1)} collective-permute-done((bf16[176,128]{1,0:T(8,128)(2,1)S(1)}, bf16[176,128]{1,0:T(8,128)(2,1)S(1)}, u32[]{:S(2)}, u32[]{:S(2)}) %collective-permute-start.11) | collective-permute-done | bytes 45088 | tf_op jit(solution)/shard_map/ppermute | solution.py:530
  43.9 1.7 %shard_map.82 = (f32[32,2048]{1,0:T(8,128)S(1)}, f32[32,32]{1,0:T(8,128)S(1)}, f32[32,672]{1,0:T(8,128)S(1)}) custom-call(bf16[176,128]{1,0:T(8,128)(2,1)S(1)} %get-tuple-element.45.refs_0_, bf16[176,128]{1,0:T(8,128)(2,1)S(1)} %collective-permute-done.9.refs_1_, bf16[176,128]{1,0:T(8,128)(2,1)S(1)} %collective-permute-done.10.refs_0_.refs_2_, ...), custom_call_target="tpu_custom_call" | custom-call | tf_op jit(solution)/shard_map/pallas_call | solution.py:487
  45.6 0.2 collective-permute-start.12
  45.8 1.6 %shard_map.83 = (f32[32,640]{1,0:T(8,128)S(1)}, f32[32,640]{1,0:T(8,128)S(1)}) custom-call(f32[32,2048]{1,0:T(8,128)S(1)} %get-tuple-element.55.h_ref.refs_0_, bf16[40,16,2,32,128]{4,3,2,1,0:T(8,128)(2,1)S(1)} %shard_map.73.refs_4_.s_ref.refs_2_.refs_6_), custom_call_target="tpu_custom_call" | custom-call | flops 1342177280 | tf_op jit(solution)/shard_map/pallas_call | solution.py:487
  47.4 0.4 collective-permute-start.13
  47.8 0.0 collective-permute-done.12.refs_2_
  47.8 0.1 shard_map.84
  47.9 0.3 collective-permute-start.14
  48.2 0.8 %shard_map.85.own_ref = f32[32,640]{1,0:T(8,128)S(1)} custom-call(f32[32,2048]{1,0:T(8,128)S(1)} %get-tuple-element.55.h_ref.refs_0_, bf16[40,16,2,32,128]{4,3,2,1,0:T(8,128)(2,1)S(1)} %shard_map.73.refs_4_.s_ref.refs_2_.refs_6_, bf16[176,128]{1,0:T(8,128)(2,1)S(1)} %get-tuple-element.52.refs_0_), custom_call_target="tpu_custom_call" | custom-call | flops 1 | tf_op jit(solution)/shard_map/pallas_call | solution.py:487
  49.0 0.0 collective-permute-done.13.refs_0_
  49.0 3.0 %collective-permute-done.14.refs_1_ = bf16[176,128]{1,0:T(8,128)(2,1)S(1)} collective-permute-done((bf16[176,128]{1,0:T(8,128)(2,1)S(1)}, bf16[176,128]{1,0:T(8,128)(2,1)S(1)}, u32[]{:S(2)}, u32[]{:S(2)}) %collective-permute-start.14) | collective-permute-done | bytes 45088 | tf_op jit(solution)/shard_map/ppermute | solution.py:527
  52.0 0.2 shard_map.86.refs_0_
  52.2 0.3 collective-permute-start.15
  52.4 1.5 %collective-permute-start.16 = (bf16[176,128]{1,0:T(8,128)(2,1)S(1)}, bf16[176,128]{1,0:T(8,128)(2,1)S(1)}, u32[]{:S(2)}, u32[]{:S(2)}) collective-permute-start(bf16[176,128]{1,0:T(8,128)(2,1)S(1)} %shard_map.86.refs_0_), channel_id=1, source_target_pairs={{12,0},{8,4},{4,8},{0,12},{13,1},{9,5},{5,9},{1,13},{14,2},{10,6},... | collective-permute-start | bytes 135176 | tf_op jit(solution)/shard_map/ppermute | solution.py:533
  53.9 0.6 collective-permute-start.17
  54.4 2.4 %collective-permute-start.18 = (bf16[176,128]{1,0:T(8,128)(2,1)S(1)}, bf16[176,128]{1,0:T(8,128)(2,1)S(1)}, u32[]{:S(2)}, u32[]{:S(2)}) collective-permute-start(bf16[176,128]{1,0:T(8,128)(2,1)S(1)} %shard_map.86.refs_0_), channel_id=1, source_target_pairs={{4,0},{0,4},{12,8},{8,12},{5,1},{1,5},{13,9},{9,13},{6,2},{2,6},{1... | collective-permute-start | bytes 135176 | tf_op jit(solution)/shard_map/ppermute | solution.py:533
  56.8 1.5 %collective-permute-done.16.refs_1_ = bf16[176,128]{1,0:T(8,128)(2,1)S(1)} collective-permute-done((bf16[176,128]{1,0:T(8,128)(2,1)S(1)}, bf16[176,128]{1,0:T(8,128)(2,1)S(1)}, u32[]{:S(2)}, u32[]{:S(2)}) %collective-permute-start.16) | collective-permute-done | bytes 45088 | tf_op jit(solution)/shard_map/ppermute | solution.py:533
  58.3 0.6 collective-permute-done.17.refs_2_
  58.9 0.4 collective-permute-done.18.refs_3_
  59.3 1.0 %shard_map.88.refs_0_ = f32[32,1280]{1,0:T(8,128)S(1)} custom-call(f32[32,640]{1,0:T(8,128)S(1)} %get-tuple-element.56.w_ref, bf16[1280,1280]{1,0:T(8,128)(2,1)S(1)} %get-tuple-element.31.order_ref, bf16[176,128]{1,0:T(8,128)(2,1)S(1)} %shard_map.86.refs_0_, bf16[176,128]{1,0:T(8,128)(2,1)S(1)} %collective-permute-done.16.refs_1_, ...), custom_call_target="tpu_custom_call" | custom-call | tf_op jit(solution)/shard_map/pallas_call | solution.py:487
  60.3 0.1 collective-permute-start.19
  60.4 0.0 collective-permute-done.15.refs_1_
  60.4 0.8 %shard_map.87._ = f32[32,4096]{1,0:T(8,128)} custom-call(f32[32,2048]{1,0:T(8,128)S(1)} %get-tuple-element.55.h_ref.refs_0_, f32[32,2048]{1,0:T(8,128)S(1)} %collective-permute-done.15.refs_1_), custom_call_target="tpu_custom_call" | custom-call | tf_op jit(solution)/shard_map/pallas_call | solution.py:487
  61.2 0.5 collective-permute-done.19.refs_1_
  61.8 0.7 %shard_map.89 = f32[32,1280]{1,0:T(8,128)} custom-call(f32[32,4096]{1,0:T(8,128)} %shard_map.87._, f32[32,1280]{1,0:T(8,128)S(1)} %shard_map.88.refs_0_, f32[32,1280]{1,0:T(8,128)S(1)} %collective-permute-done.19.refs_1_), custom_call_target="tpu_custom_call" | custom-call | tf_op jit(solution)/shard_map/pallas_call | solution.py:487
  (1 shorter events, 0.0 us)
Async XLA Ops:
  1.6 9.3 %collective-permute-start = (bf16[32,2176]{1,0:T(8,128)(2,1)S(1)}, bf16[32,2176]{1,0:T(8,128)(2,1)S(1)}, u32[]{:S(2)}, u32[]{:S(2)}) collective-permute-start(bf16[32,2176]{1,0:T(8,128)(2,1)S(1)} %shard_map.69), channel_id=1, source_target_pairs={{0,2},{2,0},{1,3},{3,1},{4,6},{6,4},{5,7},{7,5},{8,10},{10,8},{9,1... | collective-permute-start | bytes 417800 | tf_op jit(solution)/shard_map/ppermute | solution.py:527
  11.0 4.9 %collective-permute-start.2 = (bf16[64,128]{1,0:T(8,128)(2,1)S(1)}, bf16[64,128]{1,0:T(8,128)(2,1)S(1)}, u32[]{:S(2)}, u32[]{:S(2)}) collective-permute-start(bf16[64,128]{1,0:T(8,128)(2,1)S(1)} %shard_map.70.refs_0_), channel_id=1, source_target_pairs={{2,1},{3,4},{6,5},{7,8},{10,9},{11,12},{14,13},{1,2},{4,3},{5,6},{... | collective-permute-start | bytes 49160 | tf_op jit(solution)/shard_map/ppermute | solution.py:581
  13.4 6.0 %collective-permute-start.1 = (bf16[336,128]{1,0:T(8,128)(2,1)S(1)}, bf16[336,128]{1,0:T(8,128)(2,1)S(1)}, u32[]{:S(2)}, u32[]{:S(2)}) collective-permute-start(bf16[336,128]{1,0:T(8,128)(2,1)S(1)} %get-tuple-element.35.w_ref.refs_0_), channel_id=1, source_target_pairs={{0,2},{2,0},{1,3},{3,1},{4,6},{6,4},{5,7},{7,5},{8,10},{10,8},{9,1... | collective-permute-start | bytes 258056 | tf_op jit(solution)/shard_map/ppermute | solution.py:527
  21.6 3.5 %collective-permute-start.3 = (f32[32,672]{1,0:T(8,128)S(1)}, f32[32,672]{1,0:T(8,128)S(1)}, u32[]{:S(2)}, u32[]{:S(2)}) collective-permute-start(f32[32,672]{1,0:T(8,128)S(1)} %get-tuple-element.41), channel_id=1, source_target_pairs={{0,1},{1,0},{2,3},{3,2},{4,5},{5,4},{6,7},{7,6},{8,9},{9,8},{10,11... | collective-permute-start | bytes 258056 | tf_op jit(solution)/shard_map/ppermute | solution.py:530
  25.0 1.3 %collective-permute-start.4 = (f32[32,640]{1,0:T(8,128)S(1)}, f32[32,640]{1,0:T(8,128)S(1)}, u32[]{:S(2)}, u32[]{:S(2)}) collective-permute-start(f32[32,640]{1,0:T(8,128)S(1)} %get-tuple-element.44), channel_id=1, source_target_pairs={{0,1},{1,0},{2,3},{3,2},{4,5},{5,4},{6,7},{7,6},{8,9},{9,8},{10,11... | collective-permute-start | bytes 245768 | tf_op jit(solution)/shard_map/ppermute | solution.py:530
  25.2 4.1 %collective-permute-start.5 = (bf16[176,128]{1,0:T(8,128)(2,1)S(1)}, bf16[176,128]{1,0:T(8,128)(2,1)S(1)}, u32[]{:S(2)}, u32[]{:S(2)}) collective-permute-start(bf16[176,128]{1,0:T(8,128)(2,1)S(1)} %get-tuple-element.42.refs_0_), channel_id=1, source_target_pairs={{0,2},{2,0},{1,3},{3,1},{4,6},{6,4},{5,7},{7,5},{8,10},{10,8},{9,1... | collective-permute-start | bytes 135176 | tf_op jit(solution)/shard_map/ppermute | solution.py:527
  29.5 6.2 %collective-permute-start.6 = (bf16[176,128]{1,0:T(8,128)(2,1)S(1)}, bf16[176,128]{1,0:T(8,128)(2,1)S(1)}, u32[]{:S(2)}, u32[]{:S(2)}) collective-permute-start(bf16[176,128]{1,0:T(8,128)(2,1)S(1)} %shard_map.78.refs_0_), channel_id=1, source_target_pairs={{12,0},{8,4},{4,8},{0,12},{13,1},{9,5},{5,9},{1,13},{14,2},{10,6},... | collective-permute-start | bytes 135176 | tf_op jit(solution)/shard_map/ppermute | solution.py:533
  32.9 4.9 %collective-permute-start.7 = (bf16[176,128]{1,0:T(8,128)(2,1)S(1)}, bf16[176,128]{1,0:T(8,128)(2,1)S(1)}, u32[]{:S(2)}, u32[]{:S(2)}) collective-permute-start(bf16[176,128]{1,0:T(8,128)(2,1)S(1)} %shard_map.78.refs_0_), channel_id=1, source_target_pairs={{8,0},{12,4},{0,8},{4,12},{9,1},{13,5},{1,9},{5,13},{10,2},{14,6},... | collective-permute-start | bytes 135176 | tf_op jit(solution)/shard_map/ppermute | solution.py:533
  32.9 4.9 %collective-permute-start.8 = (bf16[176,128]{1,0:T(8,128)(2,1)S(1)}, bf16[176,128]{1,0:T(8,128)(2,1)S(1)}, u32[]{:S(2)}, u32[]{:S(2)}) collective-permute-start(bf16[176,128]{1,0:T(8,128)(2,1)S(1)} %shard_map.78.refs_0_), channel_id=1, source_target_pairs={{4,0},{0,4},{12,8},{8,12},{5,1},{1,5},{13,9},{9,13},{6,2},{2,6},{1... | collective-permute-start | bytes 135176 | tf_op jit(solution)/shard_map/ppermute | solution.py:533
  38.5 1.2 %collective-permute-start.9 = (bf16[176,128]{1,0:T(8,128)(2,1)S(1)}, bf16[176,128]{1,0:T(8,128)(2,1)S(1)}, u32[]{:S(2)}, u32[]{:S(2)}) collective-permute-start(bf16[176,128]{1,0:T(8,128)(2,1)S(1)} %get-tuple-element.45.refs_0_), channel_id=1, source_target_pairs={{0,1},{1,0},{2,3},{3,2},{4,5},{5,4},{6,7},{7,6},{8,9},{9,8},{10,11... | collective-permute-start | bytes 135176 | tf_op jit(solution)/shard_map/ppermute | solution.py:530
  38.6 4.1 %collective-permute-start.10 = (bf16[176,128]{1,0:T(8,128)(2,1)S(1)}, bf16[176,128]{1,0:T(8,128)(2,1)S(1)}, u32[]{:S(2)}, u32[]{:S(2)}) collective-permute-start(bf16[176,128]{1,0:T(8,128)(2,1)S(1)} %get-tuple-element.45.refs_0_), channel_id=1, source_target_pairs={{0,2},{2,0},{1,3},{3,1},{4,6},{6,4},{5,7},{7,5},{8,10},{10,8},{9,1... | collective-permute-start | bytes 135176 | tf_op jit(solution)/shard_map/ppermute | solution.py:527
  42.7 1.2 %collective-permute-start.11 = (bf16[176,128]{1,0:T(8,128)(2,1)S(1)}, bf16[176,128]{1,0:T(8,128)(2,1)S(1)}, u32[]{:S(2)}, u32[]{:S(2)}) collective-permute-start(bf16[176,128]{1,0:T(8,128)(2,1)S(1)} %collective-permute-done.10.refs_0_.refs_2_), channel_id=1, source_target_pairs={{0,1},{1,0},{2,3},{3,2},{4,5},{5,4},{6,7},{7,6},{8,9},{9,8},{10,11... | collective-permute-start | bytes 135176 | tf_op jit(solution)/shard_map/ppermute | solution.py:530
  45.6 2.2 %collective-permute-start.12 = (f32[32,672]{1,0:T(8,128)S(1)}, f32[32,672]{1,0:T(8,128)S(1)}, u32[]{:S(2)}, u32[]{:S(2)}) collective-permute-start(f32[32,672]{1,0:T(8,128)S(1)} %get-tuple-element.51), channel_id=1, source_target_pairs={{0,1},{1,0},{2,3},{3,2},{4,5},{5,4},{6,7},{7,6},{8,9},{9,8},{10,11... | collective-permute-start | bytes 258056 | tf_op jit(solution)/shard_map/ppermute | solution.py:530
  47.4 1.6 %collective-permute-start.13 = (f32[32,640]{1,0:T(8,128)S(1)}, f32[32,640]{1,0:T(8,128)S(1)}, u32[]{:S(2)}, u32[]{:S(2)}) collective-permute-start(f32[32,640]{1,0:T(8,128)S(1)} %get-tuple-element.54), channel_id=1, source_target_pairs={{0,1},{1,0},{2,3},{3,2},{4,5},{5,4},{6,7},{7,6},{8,9},{9,8},{10,11... | collective-permute-start | bytes 245768 | tf_op jit(solution)/shard_map/ppermute | solution.py:530
  47.9 4.1 %collective-permute-start.14 = (bf16[176,128]{1,0:T(8,128)(2,1)S(1)}, bf16[176,128]{1,0:T(8,128)(2,1)S(1)}, u32[]{:S(2)}, u32[]{:S(2)}) collective-permute-start(bf16[176,128]{1,0:T(8,128)(2,1)S(1)} %get-tuple-element.52.refs_0_), channel_id=1, source_target_pairs={{0,2},{2,0},{1,3},{3,1},{4,6},{6,4},{5,7},{7,5},{8,10},{10,8},{9,1... | collective-permute-start | bytes 135176 | tf_op jit(solution)/shard_map/ppermute | solution.py:527
  52.2 8.2 %collective-permute-start.15 = (f32[32,2048]{1,0:T(8,128)S(1)}, f32[32,2048]{1,0:T(8,128)S(1)}, u32[]{:S(2)}, u32[]{:S(2)}) collective-permute-start(f32[32,2048]{1,0:T(8,128)S(1)} %get-tuple-element.55.h_ref.refs_0_), channel_id=1, source_target_pairs={{0,2},{2,0},{1,3},{3,1},{4,6},{6,4},{5,7},{7,5},{8,10},{10,8},{9,1... | collective-permute-start | bytes 786440 | tf_op jit(solution)/shard_map/ppermute | solution.py:527
  52.4 5.8 %collective-permute-start.16 = (bf16[176,128]{1,0:T(8,128)(2,1)S(1)}, bf16[176,128]{1,0:T(8,128)(2,1)S(1)}, u32[]{:S(2)}, u32[]{:S(2)}) collective-permute-start(bf16[176,128]{1,0:T(8,128)(2,1)S(1)} %shard_map.86.refs_0_), channel_id=1, source_target_pairs={{12,0},{8,4},{4,8},{0,12},{13,1},{9,5},{5,9},{1,13},{14,2},{10,6},... | collective-permute-start | bytes 135176 | tf_op jit(solution)/shard_map/ppermute | solution.py:533
  53.9 5.0 %collective-permute-start.17 = (bf16[176,128]{1,0:T(8,128)(2,1)S(1)}, bf16[176,128]{1,0:T(8,128)(2,1)S(1)}, u32[]{:S(2)}, u32[]{:S(2)}) collective-permute-start(bf16[176,128]{1,0:T(8,128)(2,1)S(1)} %shard_map.86.refs_0_), channel_id=1, source_target_pairs={{8,0},{12,4},{0,8},{4,12},{9,1},{13,5},{1,9},{5,13},{10,2},{14,6},... | collective-permute-start | bytes 135176 | tf_op jit(solution)/shard_map/ppermute | solution.py:533
  54.4 4.9 %collective-permute-start.18 = (bf16[176,128]{1,0:T(8,128)(2,1)S(1)}, bf16[176,128]{1,0:T(8,128)(2,1)S(1)}, u32[]{:S(2)}, u32[]{:S(2)}) collective-permute-start(bf16[176,128]{1,0:T(8,128)(2,1)S(1)} %shard_map.86.refs_0_), channel_id=1, source_target_pairs={{4,0},{0,4},{12,8},{8,12},{5,1},{1,5},{13,9},{9,13},{6,2},{2,6},{1... | collective-permute-start | bytes 135176 | tf_op jit(solution)/shard_map/ppermute | solution.py:533
  60.3 1.5 %collective-permute-start.19 = (f32[32,1280]{1,0:T(8,128)S(1)}, f32[32,1280]{1,0:T(8,128)S(1)}, u32[]{:S(2)}, u32[]{:S(2)}) collective-permute-start(f32[32,1280]{1,0:T(8,128)S(1)} %shard_map.88.refs_0_), channel_id=1, source_target_pairs={{0,1},{1,0},{2,3},{3,2},{4,5},{5,4},{6,7},{7,6},{8,9},{9,8},{10,11... | collective-permute-start | bytes 491528 | tf_op jit(solution)/shard_map/ppermute | solution.py:530

commit v15 on v13

--- a/solution.py
+++ b/solution.py
@@ -14,7 +14,7 @@
 TAPS = 128
 HALF = TAPS // 2
 LANES = 128
-CUTS = (8, 16, 24, 32, NF)
+CUTS = (4, 8, 16, 24, 32, NF)
 AHEAD = CUTS[0]
 F32 = jnp.float32
 BF16 = jnp.bfloat16
@@ -243,7 +243,7 @@
     for f in range(NF):
         if f in CUTS:
             table[CUTS.index(f)].wait()
-        if f == CUTS[1]:
+        if f == CUTS[2]:
             for copy in later:
                 copy.start()
         power = power_of(x_scr, table_at(f, ahead_ref, tab_ref))
@@ -470,14 +470,18 @@
 
 
 def sum_kernel(_, *refs):
-    parts, (out_ref, scr, sem) = refs[:-3], refs[-3:]
-    total = parts[0][...]
-    for part in parts[1:]:
-        total = total + part[...]
-    scr[...] = total
-    copy = pltpu.make_async_copy(scr, out_ref, sem)
-    copy.start()
-    copy.wait()
+    parts, (out_ref, scr, sems) = refs[:-3], refs[-3:]
+    copies = []
+    for at in range(0, scr.shape[0], 8):
+        lines = slice(at, at + 8)
+        total = parts[0][lines, :]
+        for part in parts[1:]:
+            total = total + part[lines, :]
+        scr[lines, :] = total
+        copies.append(pltpu.make_async_copy(scr.at[lines], out_ref.at[lines], sems.at[at // 8]))
+        copies[-1].start()
+    for copy in copies:
+        copy.wait()
 
 
 def call(kernel, args, outs, scratch=(), in_specs=None, out_specs=None, limit=4, cost=None, aliases=None):
@@ -690,7 +694,7 @@
         sum_kernel,
         [hbm(wide), part] + [sub_shift(part, dc) for dc in range(1, subs)],
         [pltpu.HBM((rank, NF * cl), F32)],
-        [pltpu.VMEM((rank, NF * cl), F32), pltpu.SemaphoreType.DMA],
+        [pltpu.VMEM((rank, NF * cl), F32), pltpu.SemaphoreType.DMA((rank // 8,))],
         in_specs=[anywhere] + [whole] * subs,
         out_specs=[anywhere],
     )

time: 61.2 us -> 61.1 us (level)
  transfers between devices with their start and end apart: 20 -> 20, of which waited for: 11 -> 11; matrix products, arithmetic and copies ran while one was open for 0% -> 0% of each run, Pallas kernels for 29% -> 30%
where the time goes in v15:
time: 61.1 us; the launch traced here: 61 us
  Pallas kernels  25 us (41%)
  starting transfers between devices  18.8 us (31%)
  waiting for transfers between devices  16.3 us (27%)
  between operations  0.94 us (2%)
    pallas_call x22, Pallas kernels, call(): pl.pallas_call(kernel, out_shape=[jax.ShapeDtypeStruct(*out) if isinstanc...  25 us
    ppermute x6, starting transfers between devices, frm_shift(): lax.ppermute(value, 'frm', [(partner(i, shift, frms), i) for i in range(f...  8.78 us
    ppermute x6, waiting for transfers between devices, row_shift(): lax.ppermute(value, 'row', [(i, (i + shift) % rows) for i in range(rows)])  7.7 us
    ppermute x6, starting transfers between devices, row_shift(): lax.ppermute(value, 'row', [(i, (i + shift) % rows) for i in range(rows)])  6.8 us
    ppermute x6, waiting for transfers between devices, frm_shift(): lax.ppermute(value, 'frm', [(partner(i, shift, frms), i) for i in range(f...  6.51 us
    ppermute x7, starting transfers between devices, sub_shift(): lax.ppermute(value, 'sub', [(i, (i + shift) % subs) for i in range(subs)])  2.53 us
    ppermute x7, waiting for transfers between devices, sub_shift(): lax.ppermute(value, 'sub', [(i, (i + shift) % subs) for i in range(subs)])  2.06 us
  transfers between devices with their start and end apart: 20, of which 11 were waited for; matrix products, arithmetic and copies ran while one was open for 0% of the time, Pallas kernels for 30%

profile of v15, /device:TPU:0, one launch (start us, length us, event | category | flops | bytes accessed | tf_op | source)
XLA Modules:
  0.0 61.0 jit_solution(7162223524690108784)
XLA Ops:
  0.6 1.2 %shard_map.68 = (bf16[32,2176]{1,0:T(8,128)(2,1)S(1)}, bf16[32,2176]{1,0:T(8,128)(2,1)S(1)}, bf16[4,256,256]{2,1,0:T(8,128)(2,1)S(1)}) custom-call(bf16[32,4096]{1,0:T(8,128)(2,1)} %sig_hbm.1, bf16[40,256,256]{2,1,0:T(8,128)(2,1)} %constant.4.clone.tab_hbm), custom_call_target="tpu_custom_call" | custom-call | tf_op jit(solution)/shard_map/pallas_call | solution.py:491
  1.9 3.0 %collective-permute-start = (bf16[32,2176]{1,0:T(8,128)(2,1)S(1)}, bf16[32,2176]{1,0:T(8,128)(2,1)S(1)}, u32[]{:S(2)}, u32[]{:S(2)}) collective-permute-start(bf16[32,2176]{1,0:T(8,128)(2,1)S(1)} %get-tuple-element.36), channel_id=1, source_target_pairs={{0,2},{2,0},{1,3},{3,1},{4,6},{6,4},{5,7},{7,5},{8,10},{10,8},{9,1... | collective-permute-start | bytes 417800 | tf_op jit(solution)/shard_map/ppermute | solution.py:531
  4.9 4.3 %shard_map.69 = (bf16[40,16,2,32,128]{4,3,2,1,0:T(8,128)(2,1)S(1)}, f32[32,1280]{1,0:T(8,128)S(1)}, f32[32,2048]{1,0:T(8,128)S(1)}, bf16[1280,1280]{1,0:T(8,128)(2,1)S(1)}, bf16[36,256,256]{2,1,0:T(8,128)(2,1)S(1)}) custom-call(bf16[32,2176]{1,0:T(8,128)(2,1)S(1)} %get-tuple-element.32.sig_ref.refs_0_, bf16[4,256,256]{2,1,0:T(8,128)(2,1)S(1)} %get-tuple-element.33.ahead_ref, ...), custom_call_target="tpu_custom_call" | custom-call | flops 2684354560 | tf_op jit(solution)/shard_map/pallas_call | solution.py:491
  9.2 0.0 collective-permute-done.refs_0_.refs_1_
  9.3 0.7 %collective-permute-start.2 = (bf16[64,128]{1,0:T(8,128)(2,1)S(1)}, bf16[64,128]{1,0:T(8,128)(2,1)S(1)}, u32[]{:S(2)}, u32[]{:S(2)}) collective-permute-start(bf16[64,128]{1,0:T(8,128)(2,1)S(1)} %shard_map.70.refs_0_), channel_id=1, source_target_pairs={{2,1},{3,4},{6,5},{7,8},{10,9},{11,12},{14,13},{1,2},{4,3},{5,6},{... | collective-permute-start | bytes 49160 | tf_op jit(solution)/shard_map/ppermute | solution.py:585
  9.9 0.8 %shard_map.71 = (f32[32,640]{1,0:T(8,128)S(1)}, bf16[336,128]{1,0:T(8,128)(2,1)S(1)}) custom-call(f32[32,1280]{1,0:T(8,128)S(1)} %get-tuple-element.34.w_ref, bf16[1280,1280]{1,0:T(8,128)(2,1)S(1)} %get-tuple-element.35.order_ref, bf16[64,128]{1,0:T(8,128)(2,1)S(1)} %shard_map.70.refs_0_), custom_call_target="tpu_custom_call" | custom-call | tf_op jit(solution)/shard_map/pallas_call | solution.py:491
  10.8 0.9 %shard_map.72.refs_3_.refs_2_ = f32[32,2048]{1,0:T(8,128)S(1)} custom-call(bf16[336,128]{1,0:T(8,128)(2,1)S(1)} %get-tuple-element.39.w_ref.refs_0_, bf16[40,16,2,32,128]{4,3,2,1,0:T(8,128)(2,1)S(1)} %get-tuple-element.37.refs_1_.s_ref.refs_2_), custom_call_target="tpu_custom_call" | custom-call | flops 1342177280 | tf_op jit(solution)/shard_map/pallas_call | solution.py:491
  11.7 2.5 %collective-permute-start.1 = (bf16[336,128]{1,0:T(8,128)(2,1)S(1)}, bf16[336,128]{1,0:T(8,128)(2,1)S(1)}, u32[]{:S(2)}, u32[]{:S(2)}) collective-permute-start(bf16[336,128]{1,0:T(8,128)(2,1)S(1)} %get-tuple-element.39.w_ref.refs_0_), channel_id=1, source_target_pairs={{0,2},{2,0},{1,3},{3,1},{4,6},{6,4},{5,7},{7,5},{8,10},{10,8},{9,1... | collective-permute-start | bytes 258056 | tf_op jit(solution)/shard_map/ppermute | solution.py:531
  14.2 0.0 collective-permute-done.2.halo_ref
  14.2 3.5 %shard_map.73.refs_4_.s_ref.refs_2_.refs_6_ = bf16[40,16,2,32,128]{4,3,2,1,0:T(8,128)(2,1)S(1)} custom-call(bf16[64,128]{1,0:T(8,128)(2,1)S(1)} %collective-permute-done.2.halo_ref, bf16[4,256,256]{2,1,0:T(8,128)(2,1)S(1)} %get-tuple-element.33.ahead_ref, bf16[36,256,256]{2,1,0:T(8,128)(2,1)S(1)} %get-tuple-element.41.tab_ref, ...), custom_call_target="tpu_custom_call", output_to_operand_aliasing={{}: (5, {})} | custom-call | flops 5368709120 | tf_op jit(solution)/shard_map/pallas_call | solution.py:491
  17.7 0.0 collective-permute-done.1.refs_1_
  17.7 2.2 %shard_map.74 = (f32[32,2048]{1,0:T(8,128)S(1)}, f32[32,32]{1,0:T(8,128)S(1)}, f32[32,672]{1,0:T(8,128)S(1)}) custom-call(bf16[336,128]{1,0:T(8,128)(2,1)S(1)} %get-tuple-element.39.w_ref.refs_0_, bf16[336,128]{1,0:T(8,128)(2,1)S(1)} %collective-permute-done.1.refs_1_, f32[32,2048]{1,0:T(8,128)S(1)} %shard_map.72.refs_3_.refs_2_, ...), custom_call_target="tpu_custom_call" | custom-call | tf_op jit(solution)/shard_map/pallas_call | solution.py:491
  20.0 1.7 %collective-permute-start.3 = (f32[32,672]{1,0:T(8,128)S(1)}, f32[32,672]{1,0:T(8,128)S(1)}, u32[]{:S(2)}, u32[]{:S(2)}) collective-permute-start(f32[32,672]{1,0:T(8,128)S(1)} %get-tuple-element.45), channel_id=1, source_target_pairs={{0,1},{1,0},{2,3},{3,2},{4,5},{5,4},{6,7},{7,6},{8,9},{9,8},{10,11... | collective-permute-start | bytes 258056 | tf_op jit(solution)/shard_map/ppermute | solution.py:534
  21.7 1.6 %shard_map.75 = (f32[32,640]{1,0:T(8,128)S(1)}, f32[32,640]{1,0:T(8,128)S(1)}) custom-call(f32[32,2048]{1,0:T(8,128)S(1)} %get-tuple-element.42.h_ref.refs_5_, bf16[40,16,2,32,128]{4,3,2,1,0:T(8,128)(2,1)S(1)} %shard_map.73.refs_4_.s_ref.refs_2_.refs_6_), custom_call_target="tpu_custom_call" | custom-call | flops 1342177280 | tf_op jit(solution)/shard_map/pallas_call | solution.py:491
  23.3 0.1 collective-permute-start.4
  23.4 0.0 collective-permute-done.3.refs_2_
  23.4 0.1 shard_map.76
  23.5 0.3 collective-permute-start.5
  23.8 0.8 %shard_map.77.own_ref = f32[32,640]{1,0:T(8,128)S(1)} custom-call(f32[32,2048]{1,0:T(8,128)S(1)} %get-tuple-element.42.h_ref.refs_5_, bf16[40,16,2,32,128]{4,3,2,1,0:T(8,128)(2,1)S(1)} %shard_map.73.refs_4_.s_ref.refs_2_.refs_6_, bf16[176,128]{1,0:T(8,128)(2,1)S(1)} %get-tuple-element.46.refs_0_), custom_call_target="tpu_custom_call" | custom-call | flops 1 | tf_op jit(solution)/shard_map/pallas_call | solution.py:491
  24.6 0.0 collective-permute-done.4.refs_0_
  24.6 2.9 %collective-permute-done.5.refs_1_ = bf16[176,128]{1,0:T(8,128)(2,1)S(1)} collective-permute-done((bf16[176,128]{1,0:T(8,128)(2,1)S(1)}, bf16[176,128]{1,0:T(8,128)(2,1)S(1)}, u32[]{:S(2)}, u32[]{:S(2)}) %collective-permute-start.5) | collective-permute-done | bytes 45088 | tf_op jit(solution)/shard_map/ppermute | solution.py:531
  27.5 0.2 shard_map.78.refs_0_
  27.7 3.5 %collective-permute-start.6 = (bf16[176,128]{1,0:T(8,128)(2,1)S(1)}, bf16[176,128]{1,0:T(8,128)(2,1)S(1)}, u32[]{:S(2)}, u32[]{:S(2)}) collective-permute-start(bf16[176,128]{1,0:T(8,128)(2,1)S(1)} %shard_map.78.refs_0_), channel_id=1, source_target_pairs={{12,0},{8,4},{4,8},{0,12},{13,1},{9,5},{5,9},{1,13},{14,2},{10,6},... | collective-permute-start | bytes 135176 | tf_op jit(solution)/shard_map/ppermute | solution.py:537
  31.2 0.0 collective-permute-start.7
  31.2 0.9 %collective-permute-start.8 = (bf16[176,128]{1,0:T(8,128)(2,1)S(1)}, bf16[176,128]{1,0:T(8,128)(2,1)S(1)}, u32[]{:S(2)}, u32[]{:S(2)}) collective-permute-start(bf16[176,128]{1,0:T(8,128)(2,1)S(1)} %shard_map.78.refs_0_), channel_id=1, source_target_pairs={{4,0},{0,4},{12,8},{8,12},{5,1},{1,5},{13,9},{9,13},{6,2},{2,6},{1... | collective-permute-start | bytes 135176 | tf_op jit(solution)/shard_map/ppermute | solution.py:537
  32.1 1.8 %collective-permute-done.6.refs_1_ = bf16[176,128]{1,0:T(8,128)(2,1)S(1)} collective-permute-done((bf16[176,128]{1,0:T(8,128)(2,1)S(1)}, bf16[176,128]{1,0:T(8,128)(2,1)S(1)}, u32[]{:S(2)}, u32[]{:S(2)}) %collective-permute-start.6) | collective-permute-done | bytes 45088 | tf_op jit(solution)/shard_map/ppermute | solution.py:537
  33.9 2.2 %collective-permute-done.7.refs_2_ = bf16[176,128]{1,0:T(8,128)(2,1)S(1)} collective-permute-done((bf16[176,128]{1,0:T(8,128)(2,1)S(1)}, bf16[176,128]{1,0:T(8,128)(2,1)S(1)}, u32[]{:S(2)}, u32[]{:S(2)}) %collective-permute-start.7) | collective-permute-done | bytes 45088 | tf_op jit(solution)/shard_map/ppermute | solution.py:537
  36.1 0.0 collective-permute-done.8.refs_3_
  36.1 0.7 %shard_map.79 = (f32[32,640]{1,0:T(8,128)S(1)}, bf16[176,128]{1,0:T(8,128)(2,1)S(1)}) custom-call(f32[32,640]{1,0:T(8,128)S(1)} %get-tuple-element.38.w_ref, bf16[176,128]{1,0:T(8,128)(2,1)S(1)} %shard_map.78.refs_0_, bf16[176,128]{1,0:T(8,128)(2,1)S(1)} %collective-permute-done.6.refs_1_, bf16[176,128]{1,0:T(8,128)(2,1)S(1)} %collective-permute-done.7.refs_2_, ...), custom_call_target="tpu_custom_call" | custom-call | tf_op jit(solution)/shard_map/pallas_call | solution.py:491
  36.8 0.0 collective-permute-start.9
  36.8 0.4 collective-permute-start.10
  37.2 0.8 %collective-permute-done.9.refs_1_ = bf16[176,128]{1,0:T(8,128)(2,1)S(1)} collective-permute-done((bf16[176,128]{1,0:T(8,128)(2,1)S(1)}, bf16[176,128]{1,0:T(8,128)(2,1)S(1)}, u32[]{:S(2)}, u32[]{:S(2)}) %collective-permute-start.9) | collective-permute-done | bytes 45088 | tf_op jit(solution)/shard_map/ppermute | solution.py:534
  38.0 1.0 %shard_map.80.refs_1_ = f32[32,2048]{1,0:T(8,128)S(1)} custom-call(bf16[176,128]{1,0:T(8,128)(2,1)S(1)} %get-tuple-element.49.refs_0_, bf16[176,128]{1,0:T(8,128)(2,1)S(1)} %collective-permute-done.9.refs_1_, bf16[40,16,2,32,128]{4,3,2,1,0:T(8,128)(2,1)S(1)} %shard_map.73.refs_4_.s_ref.refs_2_.refs_6_), custom_call_target="tpu_custom_call" | custom-call | flops 1342177280 | tf_op jit(solution)/shard_map/pallas_call | solution.py:491
  39.1 1.9 %collective-permute-done.10.refs_0_.refs_2_ = bf16[176,128]{1,0:T(8,128)(2,1)S(1)} collective-permute-done((bf16[176,128]{1,0:T(8,128)(2,1)S(1)}, bf16[176,128]{1,0:T(8,128)(2,1)S(1)}, u32[]{:S(2)}, u32[]{:S(2)}) %collective-permute-start.10) | collective-permute-done | bytes 45088 | tf_op jit(solution)/shard_map/ppermute | solution.py:531
  40.9 0.0 collective-permute-start.11
  41.0 0.6 shard_map.81.refs_4_
  41.5 0.7 %collective-permute-done.11.refs_3_ = bf16[176,128]{1,0:T(8,128)(2,1)S(1)} collective-permute-done((bf16[176,128]{1,0:T(8,128)(2,1)S(1)}, bf16[176,128]{1,0:T(8,128)(2,1)S(1)}, u32[]{:S(2)}, u32[]{:S(2)}) %collective-permute-start.11) | collective-permute-done | bytes 45088 | tf_op jit(solution)/shard_map/ppermute | solution.py:534
  42.2 1.7 %shard_map.82 = (f32[32,2048]{1,0:T(8,128)S(1)}, f32[32,32]{1,0:T(8,128)S(1)}, f32[32,672]{1,0:T(8,128)S(1)}) custom-call(bf16[176,128]{1,0:T(8,128)(2,1)S(1)} %get-tuple-element.49.refs_0_, bf16[176,128]{1,0:T(8,128)(2,1)S(1)} %collective-permute-done.9.refs_1_, bf16[176,128]{1,0:T(8,128)(2,1)S(1)} %collective-permute-done.10.refs_0_.refs_2_, ...), custom_call_target="tpu_custom_call" | custom-call | tf_op jit(solution)/shard_map/pallas_call | solution.py:491
  43.9 0.2 collective-permute-start.12
  44.1 1.6 %shard_map.83 = (f32[32,640]{1,0:T(8,128)S(1)}, f32[32,640]{1,0:T(8,128)S(1)}) custom-call(f32[32,2048]{1,0:T(8,128)S(1)} %get-tuple-element.59.h_ref.refs_0_, bf16[40,16,2,32,128]{4,3,2,1,0:T(8,128)(2,1)S(1)} %shard_map.73.refs_4_.s_ref.refs_2_.refs_6_), custom_call_target="tpu_custom_call" | custom-call | flops 1342177280 | tf_op jit(solution)/shard_map/pallas_call | solution.py:491
  45.7 0.4 collective-permute-start.13
  46.1 0.0 collective-permute-done.12.refs_2_
  46.1 0.1 shard_map.84
  46.2 0.3 collective-permute-start.14
  46.5 0.8 %shard_map.85.own_ref = f32[32,640]{1,0:T(8,128)S(1)} custom-call(f32[32,2048]{1,0:T(8,128)S(1)} %get-tuple-element.59.h_ref.refs_0_, bf16[40,16,2,32,128]{4,3,2,1,0:T(8,128)(2,1)S(1)} %shard_map.73.refs_4_.s_ref.refs_2_.refs_6_, bf16[176,128]{1,0:T(8,128)(2,1)S(1)} %get-tuple-element.56.refs_0_), custom_call_target="tpu_custom_call" | custom-call | flops 1 | tf_op jit(solution)/shard_map/pallas_call | solution.py:491
  47.3 0.0 collective-permute-done.13.refs_0_
  47.3 2.9 %collective-permute-done.14.refs_1_ = bf16[176,128]{1,0:T(8,128)(2,1)S(1)} collective-permute-done((bf16[176,128]{1,0:T(8,128)(2,1)S(1)}, bf16[176,128]{1,0:T(8,128)(2,1)S(1)}, u32[]{:S(2)}, u32[]{:S(2)}) %collective-permute-start.14) | collective-permute-done | bytes 45088 | tf_op jit(solution)/shard_map/ppermute | solution.py:531
  50.2 0.2 shard_map.86.refs_0_
  50.5 0.3 collective-permute-start.15
  50.8 1.5 %collective-permute-start.16 = (bf16[176,128]{1,0:T(8,128)(2,1)S(1)}, bf16[176,128]{1,0:T(8,128)(2,1)S(1)}, u32[]{:S(2)}, u32[]{:S(2)}) collective-permute-start(bf16[176,128]{1,0:T(8,128)(2,1)S(1)} %shard_map.86.refs_0_), channel_id=1, source_target_pairs={{12,0},{8,4},{4,8},{0,12},{13,1},{9,5},{5,9},{1,13},{14,2},{10,6},... | collective-permute-start | bytes 135176 | tf_op jit(solution)/shard_map/ppermute | solution.py:537
  52.3 0.4 collective-permute-start.17
  52.7 2.4 %collective-permute-start.18 = (bf16[176,128]{1,0:T(8,128)(2,1)S(1)}, bf16[176,128]{1,0:T(8,128)(2,1)S(1)}, u32[]{:S(2)}, u32[]{:S(2)}) collective-permute-start(bf16[176,128]{1,0:T(8,128)(2,1)S(1)} %shard_map.86.refs_0_), channel_id=1, source_target_pairs={{4,0},{0,4},{12,8},{8,12},{5,1},{1,5},{13,9},{9,13},{6,2},{2,6},{1... | collective-permute-start | bytes 135176 | tf_op jit(solution)/shard_map/ppermute | solution.py:537
  55.2 1.5 %collective-permute-done.16.refs_1_ = bf16[176,128]{1,0:T(8,128)(2,1)S(1)} collective-permute-done((bf16[176,128]{1,0:T(8,128)(2,1)S(1)}, bf16[176,128]{1,0:T(8,128)(2,1)S(1)}, u32[]{:S(2)}, u32[]{:S(2)}) %collective-permute-start.16) | collective-permute-done | bytes 45088 | tf_op jit(solution)/shard_map/ppermute | solution.py:537
  56.6 0.7 %collective-permute-done.17.refs_2_ = bf16[176,128]{1,0:T(8,128)(2,1)S(1)} collective-permute-done((bf16[176,128]{1,0:T(8,128)(2,1)S(1)}, bf16[176,128]{1,0:T(8,128)(2,1)S(1)}, u32[]{:S(2)}, u32[]{:S(2)}) %collective-permute-start.17) | collective-permute-done | bytes 45088 | tf_op jit(solution)/shard_map/ppermute | solution.py:537
  57.4 0.3 collective-permute-done.18.refs_3_
  57.7 1.0 %shard_map.88.refs_0_ = f32[32,1280]{1,0:T(8,128)S(1)} custom-call(f32[32,640]{1,0:T(8,128)S(1)} %get-tuple-element.60.w_ref, bf16[1280,1280]{1,0:T(8,128)(2,1)S(1)} %get-tuple-element.35.order_ref, bf16[176,128]{1,0:T(8,128)(2,1)S(1)} %shard_map.86.refs_0_, bf16[176,128]{1,0:T(8,128)(2,1)S(1)} %collective-permute-done.16.refs_1_, ...), custom_call_target="tpu_custom_call" | custom-call | tf_op jit(solution)/shard_map/pallas_call | solution.py:491
  58.7 0.1 collective-permute-start.19
  58.7 0.0 collective-permute-done.15.refs_1_
  58.7 0.8 %shard_map.87._ = f32[32,4096]{1,0:T(8,128)} custom-call(f32[32,2048]{1,0:T(8,128)S(1)} %get-tuple-element.59.h_ref.refs_0_, f32[32,2048]{1,0:T(8,128)S(1)} %collective-permute-done.15.refs_1_), custom_call_target="tpu_custom_call" | custom-call | tf_op jit(solution)/shard_map/pallas_call | solution.py:491
  59.6 0.5 collective-permute-done.19.refs_1_
  60.1 0.7 %shard_map.89 = f32[32,1280]{1,0:T(8,128)} custom-call(f32[32,4096]{1,0:T(8,128)} %shard_map.87._, f32[32,1280]{1,0:T(8,128)S(1)} %shard_map.88.refs_0_, f32[32,1280]{1,0:T(8,128)S(1)} %collective-permute-done.19.refs_1_), custom_call_target="tpu_custom_call" | custom-call | tf_op jit(solution)/shard_map/pallas_call | solution.py:491
  (1 shorter events, 0.0 us)
Async XLA Ops:
  1.9 7.4 %collective-permute-start = (bf16[32,2176]{1,0:T(8,128)(2,1)S(1)}, bf16[32,2176]{1,0:T(8,128)(2,1)S(1)}, u32[]{:S(2)}, u32[]{:S(2)}) collective-permute-start(bf16[32,2176]{1,0:T(8,128)(2,1)S(1)} %get-tuple-element.36), channel_id=1, source_target_pairs={{0,2},{2,0},{1,3},{3,1},{4,6},{6,4},{5,7},{7,5},{8,10},{10,8},{9,1... | collective-permute-start | bytes 417800 | tf_op jit(solution)/shard_map/ppermute | solution.py:531
  9.3 4.9 %collective-permute-start.2 = (bf16[64,128]{1,0:T(8,128)(2,1)S(1)}, bf16[64,128]{1,0:T(8,128)(2,1)S(1)}, u32[]{:S(2)}, u32[]{:S(2)}) collective-permute-start(bf16[64,128]{1,0:T(8,128)(2,1)S(1)} %shard_map.70.refs_0_), channel_id=1, source_target_pairs={{2,1},{3,4},{6,5},{7,8},{10,9},{11,12},{14,13},{1,2},{4,3},{5,6},{... | collective-permute-start | bytes 49160 | tf_op jit(solution)/shard_map/ppermute | solution.py:585
  11.7 6.0 %collective-permute-start.1 = (bf16[336,128]{1,0:T(8,128)(2,1)S(1)}, bf16[336,128]{1,0:T(8,128)(2,1)S(1)}, u32[]{:S(2)}, u32[]{:S(2)}) collective-permute-start(bf16[336,128]{1,0:T(8,128)(2,1)S(1)} %get-tuple-element.39.w_ref.refs_0_), channel_id=1, source_target_pairs={{0,2},{2,0},{1,3},{3,1},{4,6},{6,4},{5,7},{7,5},{8,10},{10,8},{9,1... | collective-permute-start | bytes 258056 | tf_op jit(solution)/shard_map/ppermute | solution.py:531
  20.0 3.4 %collective-permute-start.3 = (f32[32,672]{1,0:T(8,128)S(1)}, f32[32,672]{1,0:T(8,128)S(1)}, u32[]{:S(2)}, u32[]{:S(2)}) collective-permute-start(f32[32,672]{1,0:T(8,128)S(1)} %get-tuple-element.45), channel_id=1, source_target_pairs={{0,1},{1,0},{2,3},{3,2},{4,5},{5,4},{6,7},{7,6},{8,9},{9,8},{10,11... | collective-permute-start | bytes 258056 | tf_op jit(solution)/shard_map/ppermute | solution.py:534
  23.3 1.3 %collective-permute-start.4 = (f32[32,640]{1,0:T(8,128)S(1)}, f32[32,640]{1,0:T(8,128)S(1)}, u32[]{:S(2)}, u32[]{:S(2)}) collective-permute-start(f32[32,640]{1,0:T(8,128)S(1)} %get-tuple-element.48), channel_id=1, source_target_pairs={{0,1},{1,0},{2,3},{3,2},{4,5},{5,4},{6,7},{7,6},{8,9},{9,8},{10,11... | collective-permute-start | bytes 245768 | tf_op jit(solution)/shard_map/ppermute | solution.py:534
  23.5 4.1 %collective-permute-start.5 = (bf16[176,128]{1,0:T(8,128)(2,1)S(1)}, bf16[176,128]{1,0:T(8,128)(2,1)S(1)}, u32[]{:S(2)}, u32[]{:S(2)}) collective-permute-start(bf16[176,128]{1,0:T(8,128)(2,1)S(1)} %get-tuple-element.46.refs_0_), channel_id=1, source_target_pairs={{0,2},{2,0},{1,3},{3,1},{4,6},{6,4},{5,7},{7,5},{8,10},{10,8},{9,1... | collective-permute-start | bytes 135176 | tf_op jit(solution)/shard_map/ppermute | solution.py:531
  27.7 6.2 %collective-permute-start.6 = (bf16[176,128]{1,0:T(8,128)(2,1)S(1)}, bf16[176,128]{1,0:T(8,128)(2,1)S(1)}, u32[]{:S(2)}, u32[]{:S(2)}) collective-permute-start(bf16[176,128]{1,0:T(8,128)(2,1)S(1)} %shard_map.78.refs_0_), channel_id=1, source_target_pairs={{12,0},{8,4},{4,8},{0,12},{13,1},{9,5},{5,9},{1,13},{14,2},{10,6},... | collective-permute-start | bytes 135176 | tf_op jit(solution)/shard_map/ppermute | solution.py:537
  31.2 4.9 %collective-permute-start.7 = (bf16[176,128]{1,0:T(8,128)(2,1)S(1)}, bf16[176,128]{1,0:T(8,128)(2,1)S(1)}, u32[]{:S(2)}, u32[]{:S(2)}) collective-permute-start(bf16[176,128]{1,0:T(8,128)(2,1)S(1)} %shard_map.78.refs_0_), channel_id=1, source_target_pairs={{8,0},{12,4},{0,8},{4,12},{9,1},{13,5},{1,9},{5,13},{10,2},{14,6},... | collective-permute-start | bytes 135176 | tf_op jit(solution)/shard_map/ppermute | solution.py:537
  31.2 4.9 %collective-permute-start.8 = (bf16[176,128]{1,0:T(8,128)(2,1)S(1)}, bf16[176,128]{1,0:T(8,128)(2,1)S(1)}, u32[]{:S(2)}, u32[]{:S(2)}) collective-permute-start(bf16[176,128]{1,0:T(8,128)(2,1)S(1)} %shard_map.78.refs_0_), channel_id=1, source_target_pairs={{4,0},{0,4},{12,8},{8,12},{5,1},{1,5},{13,9},{9,13},{6,2},{2,6},{1... | collective-permute-start | bytes 135176 | tf_op jit(solution)/shard_map/ppermute | solution.py:537
  36.8 1.2 %collective-permute-start.9 = (bf16[176,128]{1,0:T(8,128)(2,1)S(1)}, bf16[176,128]{1,0:T(8,128)(2,1)S(1)}, u32[]{:S(2)}, u32[]{:S(2)}) collective-permute-start(bf16[176,128]{1,0:T(8,128)(2,1)S(1)} %get-tuple-element.49.refs_0_), channel_id=1, source_target_pairs={{0,1},{1,0},{2,3},{3,2},{4,5},{5,4},{6,7},{7,6},{8,9},{9,8},{10,11... | collective-permute-start | bytes 135176 | tf_op jit(solution)/shard_map/ppermute | solution.py:534
  36.8 4.1 %collective-permute-start.10 = (bf16[176,128]{1,0:T(8,128)(2,1)S(1)}, bf16[176,128]{1,0:T(8,128)(2,1)S(1)}, u32[]{:S(2)}, u32[]{:S(2)}) collective-permute-start(bf16[176,128]{1,0:T(8,128)(2,1)S(1)} %get-tuple-element.49.refs_0_), channel_id=1, source_target_pairs={{0,2},{2,0},{1,3},{3,1},{4,6},{6,4},{5,7},{7,5},{8,10},{10,8},{9,1... | collective-permute-start | bytes 135176 | tf_op jit(solution)/shard_map/ppermute | solution.py:531
  40.9 1.2 %collective-permute-start.11 = (bf16[176,128]{1,0:T(8,128)(2,1)S(1)}, bf16[176,128]{1,0:T(8,128)(2,1)S(1)}, u32[]{:S(2)}, u32[]{:S(2)}) collective-permute-start(bf16[176,128]{1,0:T(8,128)(2,1)S(1)} %collective-permute-done.10.refs_0_.refs_2_), channel_id=1, source_target_pairs={{0,1},{1,0},{2,3},{3,2},{4,5},{5,4},{6,7},{7,6},{8,9},{9,8},{10,11... | collective-permute-start | bytes 135176 | tf_op jit(solution)/shard_map/ppermute | solution.py:534
  43.9 2.2 %collective-permute-start.12 = (f32[32,672]{1,0:T(8,128)S(1)}, f32[32,672]{1,0:T(8,128)S(1)}, u32[]{:S(2)}, u32[]{:S(2)}) collective-permute-start(f32[32,672]{1,0:T(8,128)S(1)} %get-tuple-element.55), channel_id=1, source_target_pairs={{0,1},{1,0},{2,3},{3,2},{4,5},{5,4},{6,7},{7,6},{8,9},{9,8},{10,11... | collective-permute-start | bytes 258056 | tf_op jit(solution)/shard_map/ppermute | solution.py:534
  45.7 1.6 %collective-permute-start.13 = (f32[32,640]{1,0:T(8,128)S(1)}, f32[32,640]{1,0:T(8,128)S(1)}, u32[]{:S(2)}, u32[]{:S(2)}) collective-permute-start(f32[32,640]{1,0:T(8,128)S(1)} %get-tuple-element.58), channel_id=1, source_target_pairs={{0,1},{1,0},{2,3},{3,2},{4,5},{5,4},{6,7},{7,6},{8,9},{9,8},{10,11... | collective-permute-start | bytes 245768 | tf_op jit(solution)/shard_map/ppermute | solution.py:534
  46.2 4.1 %collective-permute-start.14 = (bf16[176,128]{1,0:T(8,128)(2,1)S(1)}, bf16[176,128]{1,0:T(8,128)(2,1)S(1)}, u32[]{:S(2)}, u32[]{:S(2)}) collective-permute-start(bf16[176,128]{1,0:T(8,128)(2,1)S(1)} %get-tuple-element.56.refs_0_), channel_id=1, source_target_pairs={{0,2},{2,0},{1,3},{3,1},{4,6},{6,4},{5,7},{7,5},{8,10},{10,8},{9,1... | collective-permute-start | bytes 135176 | tf_op jit(solution)/shard_map/ppermute | solution.py:531
  50.5 8.3 %collective-permute-start.15 = (f32[32,2048]{1,0:T(8,128)S(1)}, f32[32,2048]{1,0:T(8,128)S(1)}, u32[]{:S(2)}, u32[]{:S(2)}) collective-permute-start(f32[32,2048]{1,0:T(8,128)S(1)} %get-tuple-element.59.h_ref.refs_0_), channel_id=1, source_target_pairs={{0,2},{2,0},{1,3},{3,1},{4,6},{6,4},{5,7},{7,5},{8,10},{10,8},{9,1... | collective-permute-start | bytes 786440 | tf_op jit(solution)/shard_map/ppermute | solution.py:531
  50.8 5.8 %collective-permute-start.16 = (bf16[176,128]{1,0:T(8,128)(2,1)S(1)}, bf16[176,128]{1,0:T(8,128)(2,1)S(1)}, u32[]{:S(2)}, u32[]{:S(2)}) collective-permute-start(bf16[176,128]{1,0:T(8,128)(2,1)S(1)} %shard_map.86.refs_0_), channel_id=1, source_target_pairs={{12,0},{8,4},{4,8},{0,12},{13,1},{9,5},{5,9},{1,13},{14,2},{10,6},... | collective-permute-start | bytes 135176 | tf_op jit(solution)/shard_map/ppermute | solution.py:537
  52.3 5.1 %collective-permute-start.17 = (bf16[176,128]{1,0:T(8,128)(2,1)S(1)}, bf16[176,128]{1,0:T(8,128)(2,1)S(1)}, u32[]{:S(2)}, u32[]{:S(2)}) collective-permute-start(bf16[176,128]{1,0:T(8,128)(2,1)S(1)} %shard_map.86.refs_0_), channel_id=1, source_target_pairs={{8,0},{12,4},{0,8},{4,12},{9,1},{13,5},{1,9},{5,13},{10,2},{14,6},... | collective-permute-start | bytes 135176 | tf_op jit(solution)/shard_map/ppermute | solution.py:537
  52.7 4.9 %collective-permute-start.18 = (bf16[176,128]{1,0:T(8,128)(2,1)S(1)}, bf16[176,128]{1,0:T(8,128)(2,1)S(1)}, u32[]{:S(2)}, u32[]{:S(2)}) collective-permute-start(bf16[176,128]{1,0:T(8,128)(2,1)S(1)} %shard_map.86.refs_0_), channel_id=1, source_target_pairs={{4,0},{0,4},{12,8},{8,12},{5,1},{1,5},{13,9},{9,13},{6,2},{2,6},{1... | collective-permute-start | bytes 135176 | tf_op jit(solution)/shard_map/ppermute | solution.py:537
  58.7 1.5 %collective-permute-start.19 = (f32[32,1280]{1,0:T(8,128)S(1)}, f32[32,1280]{1,0:T(8,128)S(1)}, u32[]{:S(2)}, u32[]{:S(2)}) collective-permute-start(f32[32,1280]{1,0:T(8,128)S(1)} %shard_map.88.refs_0_), channel_id=1, source_target_pairs={{0,1},{1,0},{2,3},{3,2},{4,5},{5,4},{6,7},{7,6},{8,9},{9,8},{10,11... | collective-permute-start | bytes 491528 | tf_op jit(solution)/shard_map/ppermute | solution.py:534

commit v16 on v15

--- a/solution.py
+++ b/solution.py
@@ -165,10 +165,27 @@
     return [(dx, dc) for dx in range(1, rows) for dc in range(1, subs)]
 
 
+def two_term_dot(left, right):
+    top, rest = split_two(left)
+    right_top, right_rest = split_two(right)
+    return jnp.dot(
+        jnp.concatenate([top, rest, top], axis=1),
+        jnp.concatenate([right_top, right_top, right_rest], axis=0),
+        preferred_element_type=F32,
+    )
+
+
+def two_term_gram(value):
+    rank = value.shape[0]
+    both = jnp.concatenate(split_two(value), axis=0)
+    full = lax.dot_general(both, both, NT, preferred_element_type=F32)
+    return full[:rank, :rank] + (full[:rank, rank:] + full[rank:, :rank]) + full[rank:, rank:]
+
+
 def new_activations(old, gram, above, s_ref, h_out, h_gram_ref, msg_refs, rows, subs, cl):
-    new = old * above / jnp.dot(gram, old, precision=HIGH, preferred_element_type=F32)
+    new = old * above / two_term_dot(gram, old)
     h_out[...] = new
-    h_gram = lax.dot_general(new, new, NT, precision=HIGH, preferred_element_type=F32)
+    h_gram = two_term_gram(new)
     h_gram_ref[...] = h_gram
     size = NF // subs * cl
     x_me, c_me = lax.axis_index("row"), lax.axis_index("sub")

time: 61.1 us -> 60.6 us (level)
  no operation moved by 1% of the time
where the time goes in v16:
time: 60.6 us; the launch traced here: 60.5 us
  Pallas kernels  24.6 us (41%)
  starting transfers between devices  18.7 us (31%)
  waiting for transfers between devices  16.3 us (27%)
  between operations  0.93 us (2%)
    pallas_call x22, Pallas kernels, call(): pl.pallas_call(kernel, out_shape=[jax.ShapeDtypeStruct(*out) if isinstanc...  24.6 us
    ppermute x6, starting transfers between devices, frm_shift(): lax.ppermute(value, 'frm', [(partner(i, shift, frms), i) for i in range(f...  8.78 us
    ppermute x6, waiting for transfers between devices, row_shift(): lax.ppermute(value, 'row', [(i, (i + shift) % rows) for i in range(rows)])  7.7 us
    ppermute x6, starting transfers between devices, row_shift(): lax.ppermute(value, 'row', [(i, (i + shift) % rows) for i in range(rows)])  6.79 us
    ppermute x6, waiting for transfers between devices, frm_shift(): lax.ppermute(value, 'frm', [(partner(i, shift, frms), i) for i in range(f...  6.51 us
    ppermute x7, starting transfers between devices, sub_shift(): lax.ppermute(value, 'sub', [(i, (i + shift) % subs) for i in range(subs)])  2.44 us
    ppermute x7, waiting for transfers between devices, sub_shift(): lax.ppermute(value, 'sub', [(i, (i + shift) % subs) for i in range(subs)])  2.06 us
  transfers between devices with their start and end apart: 20, of which 11 were waited for; matrix products, arithmetic and copies ran while one was open for 0% of the time, Pallas kernels for 30%

profile of v16, /device:TPU:0, one launch (start us, length us, event | category | flops | bytes accessed | tf_op | source)
XLA Modules:
  0.0 60.5 jit_solution(2969244230182703829)
XLA Ops:
  0.6 1.2 %shard_map.68 = (bf16[32,2176]{1,0:T(8,128)(2,1)S(1)}, bf16[32,2176]{1,0:T(8,128)(2,1)S(1)}, bf16[4,256,256]{2,1,0:T(8,128)(2,1)S(1)}) custom-call(bf16[32,4096]{1,0:T(8,128)(2,1)} %sig_hbm.1, bf16[40,256,256]{2,1,0:T(8,128)(2,1)} %constant.4.clone.tab_hbm), custom_call_target="tpu_custom_call" | custom-call | tf_op jit(solution)/shard_map/pallas_call | solution.py:508
  1.9 3.0 %collective-permute-start = (bf16[32,2176]{1,0:T(8,128)(2,1)S(1)}, bf16[32,2176]{1,0:T(8,128)(2,1)S(1)}, u32[]{:S(2)}, u32[]{:S(2)}) collective-permute-start(bf16[32,2176]{1,0:T(8,128)(2,1)S(1)} %get-tuple-element.36), channel_id=1, source_target_pairs={{0,2},{2,0},{1,3},{3,1},{4,6},{6,4},{5,7},{7,5},{8,10},{10,8},{9,1... | collective-permute-start | bytes 417800 | tf_op jit(solution)/shard_map/ppermute | solution.py:548
  4.9 4.3 %shard_map.69 = (bf16[40,16,2,32,128]{4,3,2,1,0:T(8,128)(2,1)S(1)}, f32[32,1280]{1,0:T(8,128)S(1)}, f32[32,2048]{1,0:T(8,128)S(1)}, bf16[1280,1280]{1,0:T(8,128)(2,1)S(1)}, bf16[36,256,256]{2,1,0:T(8,128)(2,1)S(1)}) custom-call(bf16[32,2176]{1,0:T(8,128)(2,1)S(1)} %get-tuple-element.32.sig_ref.refs_0_, bf16[4,256,256]{2,1,0:T(8,128)(2,1)S(1)} %get-tuple-element.33.ahead_ref, ...), custom_call_target="tpu_custom_call" | custom-call | flops 2684354560 | tf_op jit(solution)/shard_map/pallas_call | solution.py:508
  9.2 0.0 collective-permute-done.refs_0_.refs_1_
  9.3 0.7 %collective-permute-start.2 = (bf16[64,128]{1,0:T(8,128)(2,1)S(1)}, bf16[64,128]{1,0:T(8,128)(2,1)S(1)}, u32[]{:S(2)}, u32[]{:S(2)}) collective-permute-start(bf16[64,128]{1,0:T(8,128)(2,1)S(1)} %shard_map.70.refs_0_), channel_id=1, source_target_pairs={{2,1},{3,4},{6,5},{7,8},{10,9},{11,12},{14,13},{1,2},{4,3},{5,6},{... | collective-permute-start | bytes 49160 | tf_op jit(solution)/shard_map/ppermute | solution.py:602
  9.9 0.8 %shard_map.71 = (f32[32,640]{1,0:T(8,128)S(1)}, bf16[336,128]{1,0:T(8,128)(2,1)S(1)}) custom-call(f32[32,1280]{1,0:T(8,128)S(1)} %get-tuple-element.34.w_ref, bf16[1280,1280]{1,0:T(8,128)(2,1)S(1)} %get-tuple-element.35.order_ref, bf16[64,128]{1,0:T(8,128)(2,1)S(1)} %shard_map.70.refs_0_), custom_call_target="tpu_custom_call" | custom-call | tf_op jit(solution)/shard_map/pallas_call | solution.py:508
  10.8 0.9 %shard_map.72.refs_3_.refs_2_ = f32[32,2048]{1,0:T(8,128)S(1)} custom-call(bf16[336,128]{1,0:T(8,128)(2,1)S(1)} %get-tuple-element.39.w_ref.refs_0_, bf16[40,16,2,32,128]{4,3,2,1,0:T(8,128)(2,1)S(1)} %get-tuple-element.37.refs_1_.s_ref.refs_2_), custom_call_target="tpu_custom_call" | custom-call | flops 1342177280 | tf_op jit(solution)/shard_map/pallas_call | solution.py:508
  11.7 2.5 %collective-permute-start.1 = (bf16[336,128]{1,0:T(8,128)(2,1)S(1)}, bf16[336,128]{1,0:T(8,128)(2,1)S(1)}, u32[]{:S(2)}, u32[]{:S(2)}) collective-permute-start(bf16[336,128]{1,0:T(8,128)(2,1)S(1)} %get-tuple-element.39.w_ref.refs_0_), channel_id=1, source_target_pairs={{0,2},{2,0},{1,3},{3,1},{4,6},{6,4},{5,7},{7,5},{8,10},{10,8},{9,1... | collective-permute-start | bytes 258056 | tf_op jit(solution)/shard_map/ppermute | solution.py:548
  14.2 0.0 collective-permute-done.2.halo_ref
  14.2 3.5 %shard_map.73.refs_4_.s_ref.refs_2_.refs_6_ = bf16[40,16,2,32,128]{4,3,2,1,0:T(8,128)(2,1)S(1)} custom-call(bf16[64,128]{1,0:T(8,128)(2,1)S(1)} %collective-permute-done.2.halo_ref, bf16[4,256,256]{2,1,0:T(8,128)(2,1)S(1)} %get-tuple-element.33.ahead_ref, bf16[36,256,256]{2,1,0:T(8,128)(2,1)S(1)} %get-tuple-element.41.tab_ref, ...), custom_call_target="tpu_custom_call", output_to_operand_aliasing={{}: (5, {})} | custom-call | flops 5368709120 | tf_op jit(solution)/shard_map/pallas_call | solution.py:508
  17.7 0.0 collective-permute-done.1.refs_1_
  17.7 2.1 %shard_map.74 = (f32[32,2048]{1,0:T(8,128)S(1)}, f32[32,32]{1,0:T(8,128)S(1)}, f32[32,672]{1,0:T(8,128)S(1)}) custom-call(bf16[336,128]{1,0:T(8,128)(2,1)S(1)} %get-tuple-element.39.w_ref.refs_0_, bf16[336,128]{1,0:T(8,128)(2,1)S(1)} %collective-permute-done.1.refs_1_, f32[32,2048]{1,0:T(8,128)S(1)} %shard_map.72.refs_3_.refs_2_, ...), custom_call_target="tpu_custom_call" | custom-call | tf_op jit(solution)/shard_map/pallas_call | solution.py:508
  19.8 1.7 %collective-permute-start.3 = (f32[32,672]{1,0:T(8,128)S(1)}, f32[32,672]{1,0:T(8,128)S(1)}, u32[]{:S(2)}, u32[]{:S(2)}) collective-permute-start(f32[32,672]{1,0:T(8,128)S(1)} %get-tuple-element.45), channel_id=1, source_target_pairs={{0,1},{1,0},{2,3},{3,2},{4,5},{5,4},{6,7},{7,6},{8,9},{9,8},{10,11... | collective-permute-start | bytes 258056 | tf_op jit(solution)/shard_map/ppermute | solution.py:551
  21.5 1.6 %shard_map.75 = (f32[32,640]{1,0:T(8,128)S(1)}, f32[32,640]{1,0:T(8,128)S(1)}) custom-call(f32[32,2048]{1,0:T(8,128)S(1)} %get-tuple-element.42.h_ref.refs_5_, bf16[40,16,2,32,128]{4,3,2,1,0:T(8,128)(2,1)S(1)} %shard_map.73.refs_4_.s_ref.refs_2_.refs_6_), custom_call_target="tpu_custom_call" | custom-call | flops 1342177280 | tf_op jit(solution)/shard_map/pallas_call | solution.py:508
  23.1 0.1 collective-permute-start.4
  23.2 0.0 collective-permute-done.3.refs_2_
  23.2 0.1 shard_map.76
  23.2 0.3 collective-permute-start.5
  23.6 0.8 %shard_map.77.own_ref = f32[32,640]{1,0:T(8,128)S(1)} custom-call(f32[32,2048]{1,0:T(8,128)S(1)} %get-tuple-element.42.h_ref.refs_5_, bf16[40,16,2,32,128]{4,3,2,1,0:T(8,128)(2,1)S(1)} %shard_map.73.refs_4_.s_ref.refs_2_.refs_6_, bf16[176,128]{1,0:T(8,128)(2,1)S(1)} %get-tuple-element.46.refs_0_), custom_call_target="tpu_custom_call" | custom-call | flops 1 | tf_op jit(solution)/shard_map/pallas_call | solution.py:508
  24.4 0.0 collective-permute-done.4.refs_0_
  24.4 2.9 %collective-permute-done.5.refs_1_ = bf16[176,128]{1,0:T(8,128)(2,1)S(1)} collective-permute-done((bf16[176,128]{1,0:T(8,128)(2,1)S(1)}, bf16[176,128]{1,0:T(8,128)(2,1)S(1)}, u32[]{:S(2)}, u32[]{:S(2)}) %collective-permute-start.5) | collective-permute-done | bytes 45088 | tf_op jit(solution)/shard_map/ppermute | solution.py:548
  27.3 0.2 shard_map.78.refs_0_
  27.5 3.5 %collective-permute-start.6 = (bf16[176,128]{1,0:T(8,128)(2,1)S(1)}, bf16[176,128]{1,0:T(8,128)(2,1)S(1)}, u32[]{:S(2)}, u32[]{:S(2)}) collective-permute-start(bf16[176,128]{1,0:T(8,128)(2,1)S(1)} %shard_map.78.refs_0_), channel_id=1, source_target_pairs={{12,0},{8,4},{4,8},{0,12},{13,1},{9,5},{5,9},{1,13},{14,2},{10,6},... | collective-permute-start | bytes 135176 | tf_op jit(solution)/shard_map/ppermute | solution.py:554
  31.0 0.0 collective-permute-start.7
  31.0 0.9 %collective-permute-start.8 = (bf16[176,128]{1,0:T(8,128)(2,1)S(1)}, bf16[176,128]{1,0:T(8,128)(2,1)S(1)}, u32[]{:S(2)}, u32[]{:S(2)}) collective-permute-start(bf16[176,128]{1,0:T(8,128)(2,1)S(1)} %shard_map.78.refs_0_), channel_id=1, source_target_pairs={{4,0},{0,4},{12,8},{8,12},{5,1},{1,5},{13,9},{9,13},{6,2},{2,6},{1... | collective-permute-start | bytes 135176 | tf_op jit(solution)/shard_map/ppermute | solution.py:554
  31.9 1.8 %collective-permute-done.6.refs_1_ = bf16[176,128]{1,0:T(8,128)(2,1)S(1)} collective-permute-done((bf16[176,128]{1,0:T(8,128)(2,1)S(1)}, bf16[176,128]{1,0:T(8,128)(2,1)S(1)}, u32[]{:S(2)}, u32[]{:S(2)}) %collective-permute-start.6) | collective-permute-done | bytes 45088 | tf_op jit(solution)/shard_map/ppermute | solution.py:554
  33.7 2.2 %collective-permute-done.7.refs_2_ = bf16[176,128]{1,0:T(8,128)(2,1)S(1)} collective-permute-done((bf16[176,128]{1,0:T(8,128)(2,1)S(1)}, bf16[176,128]{1,0:T(8,128)(2,1)S(1)}, u32[]{:S(2)}, u32[]{:S(2)}) %collective-permute-start.7) | collective-permute-done | bytes 45088 | tf_op jit(solution)/shard_map/ppermute | solution.py:554
  35.9 0.0 collective-permute-done.8.refs_3_
  35.9 0.7 %shard_map.79 = (f32[32,640]{1,0:T(8,128)S(1)}, bf16[176,128]{1,0:T(8,128)(2,1)S(1)}) custom-call(f32[32,640]{1,0:T(8,128)S(1)} %get-tuple-element.38.w_ref, bf16[176,128]{1,0:T(8,128)(2,1)S(1)} %shard_map.78.refs_0_, bf16[176,128]{1,0:T(8,128)(2,1)S(1)} %collective-permute-done.6.refs_1_, bf16[176,128]{1,0:T(8,128)(2,1)S(1)} %collective-permute-done.7.refs_2_, ...), custom_call_target="tpu_custom_call" | custom-call | tf_op jit(solution)/shard_map/pallas_call | solution.py:508
  36.6 0.0 collective-permute-start.9
  36.6 0.4 collective-permute-start.10
  37.0 0.8 %collective-permute-done.9.refs_1_ = bf16[176,128]{1,0:T(8,128)(2,1)S(1)} collective-permute-done((bf16[176,128]{1,0:T(8,128)(2,1)S(1)}, bf16[176,128]{1,0:T(8,128)(2,1)S(1)}, u32[]{:S(2)}, u32[]{:S(2)}) %collective-permute-start.9) | collective-permute-done | bytes 45088 | tf_op jit(solution)/shard_map/ppermute | solution.py:551
  37.8 1.0 %shard_map.80.refs_1_ = f32[32,2048]{1,0:T(8,128)S(1)} custom-call(bf16[176,128]{1,0:T(8,128)(2,1)S(1)} %get-tuple-element.49.refs_0_, bf16[176,128]{1,0:T(8,128)(2,1)S(1)} %collective-permute-done.9.refs_1_, bf16[40,16,2,32,128]{4,3,2,1,0:T(8,128)(2,1)S(1)} %shard_map.73.refs_4_.s_ref.refs_2_.refs_6_), custom_call_target="tpu_custom_call" | custom-call | flops 1342177280 | tf_op jit(solution)/shard_map/pallas_call | solution.py:508
  38.8 1.9 %collective-permute-done.10.refs_0_.refs_2_ = bf16[176,128]{1,0:T(8,128)(2,1)S(1)} collective-permute-done((bf16[176,128]{1,0:T(8,128)(2,1)S(1)}, bf16[176,128]{1,0:T(8,128)(2,1)S(1)}, u32[]{:S(2)}, u32[]{:S(2)}) %collective-permute-start.10) | collective-permute-done | bytes 45088 | tf_op jit(solution)/shard_map/ppermute | solution.py:548
  40.7 0.0 collective-permute-start.11
  40.7 0.6 shard_map.81.refs_4_
  41.3 0.7 %collective-permute-done.11.refs_3_ = bf16[176,128]{1,0:T(8,128)(2,1)S(1)} collective-permute-done((bf16[176,128]{1,0:T(8,128)(2,1)S(1)}, bf16[176,128]{1,0:T(8,128)(2,1)S(1)}, u32[]{:S(2)}, u32[]{:S(2)}) %collective-permute-start.11) | collective-permute-done | bytes 45088 | tf_op jit(solution)/shard_map/ppermute | solution.py:551
  42.0 1.5 %shard_map.82 = (f32[32,2048]{1,0:T(8,128)S(1)}, f32[32,32]{1,0:T(8,128)S(1)}, f32[32,672]{1,0:T(8,128)S(1)}) custom-call(bf16[176,128]{1,0:T(8,128)(2,1)S(1)} %get-tuple-element.49.refs_0_, bf16[176,128]{1,0:T(8,128)(2,1)S(1)} %collective-permute-done.9.refs_1_, bf16[176,128]{1,0:T(8,128)(2,1)S(1)} %collective-permute-done.10.refs_0_.refs_2_, ...), custom_call_target="tpu_custom_call" | custom-call | tf_op jit(solution)/shard_map/pallas_call | solution.py:508
  43.4 0.2 collective-permute-start.12
  43.6 1.6 %shard_map.83 = (f32[32,640]{1,0:T(8,128)S(1)}, f32[32,640]{1,0:T(8,128)S(1)}) custom-call(f32[32,2048]{1,0:T(8,128)S(1)} %get-tuple-element.59.h_ref.refs_0_, bf16[40,16,2,32,128]{4,3,2,1,0:T(8,128)(2,1)S(1)} %shard_map.73.refs_4_.s_ref.refs_2_.refs_6_), custom_call_target="tpu_custom_call" | custom-call | flops 1342177280 | tf_op jit(solution)/shard_map/pallas_call | solution.py:508
  45.2 0.4 collective-permute-start.13
  45.6 0.0 collective-permute-done.12.refs_2_
  45.6 0.1 shard_map.84
  45.7 0.3 collective-permute-start.14
  46.0 0.8 %shard_map.85.own_ref = f32[32,640]{1,0:T(8,128)S(1)} custom-call(f32[32,2048]{1,0:T(8,128)S(1)} %get-tuple-element.59.h_ref.refs_0_, bf16[40,16,2,32,128]{4,3,2,1,0:T(8,128)(2,1)S(1)} %shard_map.73.refs_4_.s_ref.refs_2_.refs_6_, bf16[176,128]{1,0:T(8,128)(2,1)S(1)} %get-tuple-element.56.refs_0_), custom_call_target="tpu_custom_call" | custom-call | flops 1 | tf_op jit(solution)/shard_map/pallas_call | solution.py:508
  46.8 0.0 collective-permute-done.13.refs_0_
  46.9 2.9 %collective-permute-done.14.refs_1_ = bf16[176,128]{1,0:T(8,128)(2,1)S(1)} collective-permute-done((bf16[176,128]{1,0:T(8,128)(2,1)S(1)}, bf16[176,128]{1,0:T(8,128)(2,1)S(1)}, u32[]{:S(2)}, u32[]{:S(2)}) %collective-permute-start.14) | collective-permute-done | bytes 45088 | tf_op jit(solution)/shard_map/ppermute | solution.py:548
  49.8 0.2 shard_map.86.refs_0_
  50.0 0.3 collective-permute-start.15
  50.3 1.5 %collective-permute-start.16 = (bf16[176,128]{1,0:T(8,128)(2,1)S(1)}, bf16[176,128]{1,0:T(8,128)(2,1)S(1)}, u32[]{:S(2)}, u32[]{:S(2)}) collective-permute-start(bf16[176,128]{1,0:T(8,128)(2,1)S(1)} %shard_map.86.refs_0_), channel_id=1, source_target_pairs={{12,0},{8,4},{4,8},{0,12},{13,1},{9,5},{5,9},{1,13},{14,2},{10,6},... | collective-permute-start | bytes 135176 | tf_op jit(solution)/shard_map/ppermute | solution.py:554
  51.8 0.4 collective-permute-start.17
  52.3 2.4 %collective-permute-start.18 = (bf16[176,128]{1,0:T(8,128)(2,1)S(1)}, bf16[176,128]{1,0:T(8,128)(2,1)S(1)}, u32[]{:S(2)}, u32[]{:S(2)}) collective-permute-start(bf16[176,128]{1,0:T(8,128)(2,1)S(1)} %shard_map.86.refs_0_), channel_id=1, source_target_pairs={{4,0},{0,4},{12,8},{8,12},{5,1},{1,5},{13,9},{9,13},{6,2},{2,6},{1... | collective-permute-start | bytes 135176 | tf_op jit(solution)/shard_map/ppermute | solution.py:554
  54.7 1.5 %collective-permute-done.16.refs_1_ = bf16[176,128]{1,0:T(8,128)(2,1)S(1)} collective-permute-done((bf16[176,128]{1,0:T(8,128)(2,1)S(1)}, bf16[176,128]{1,0:T(8,128)(2,1)S(1)}, u32[]{:S(2)}, u32[]{:S(2)}) %collective-permute-start.16) | collective-permute-done | bytes 45088 | tf_op jit(solution)/shard_map/ppermute | solution.py:554
  56.1 0.7 %collective-permute-done.17.refs_2_ = bf16[176,128]{1,0:T(8,128)(2,1)S(1)} collective-permute-done((bf16[176,128]{1,0:T(8,128)(2,1)S(1)}, bf16[176,128]{1,0:T(8,128)(2,1)S(1)}, u32[]{:S(2)}, u32[]{:S(2)}) %collective-permute-start.17) | collective-permute-done | bytes 45088 | tf_op jit(solution)/shard_map/ppermute | solution.py:554
  56.9 0.3 collective-permute-done.18.refs_3_
  57.2 1.0 %shard_map.88.refs_0_ = f32[32,1280]{1,0:T(8,128)S(1)} custom-call(f32[32,640]{1,0:T(8,128)S(1)} %get-tuple-element.60.w_ref, bf16[1280,1280]{1,0:T(8,128)(2,1)S(1)} %get-tuple-element.35.order_ref, bf16[176,128]{1,0:T(8,128)(2,1)S(1)} %shard_map.86.refs_0_, bf16[176,128]{1,0:T(8,128)(2,1)S(1)} %collective-permute-done.16.refs_1_, ...), custom_call_target="tpu_custom_call" | custom-call | tf_op jit(solution)/shard_map/pallas_call | solution.py:508
  58.2 0.1 collective-permute-start.19
  58.2 0.0 collective-permute-done.15.refs_1_
  58.3 0.8 %shard_map.87._ = f32[32,4096]{1,0:T(8,128)} custom-call(f32[32,2048]{1,0:T(8,128)S(1)} %get-tuple-element.59.h_ref.refs_0_, f32[32,2048]{1,0:T(8,128)S(1)} %collective-permute-done.15.refs_1_), custom_call_target="tpu_custom_call" | custom-call | tf_op jit(solution)/shard_map/pallas_call | solution.py:508
  59.1 0.5 collective-permute-done.19.refs_1_
  59.6 0.7 %shard_map.89 = f32[32,1280]{1,0:T(8,128)} custom-call(f32[32,4096]{1,0:T(8,128)} %shard_map.87._, f32[32,1280]{1,0:T(8,128)S(1)} %shard_map.88.refs_0_, f32[32,1280]{1,0:T(8,128)S(1)} %collective-permute-done.19.refs_1_), custom_call_target="tpu_custom_call" | custom-call | tf_op jit(solution)/shard_map/pallas_call | solution.py:508
  (1 shorter events, 0.0 us)
Async XLA Ops:
  1.9 7.4 %collective-permute-start = (bf16[32,2176]{1,0:T(8,128)(2,1)S(1)}, bf16[32,2176]{1,0:T(8,128)(2,1)S(1)}, u32[]{:S(2)}, u32[]{:S(2)}) collective-permute-start(bf16[32,2176]{1,0:T(8,128)(2,1)S(1)} %get-tuple-element.36), channel_id=1, source_target_pairs={{0,2},{2,0},{1,3},{3,1},{4,6},{6,4},{5,7},{7,5},{8,10},{10,8},{9,1... | collective-permute-start | bytes 417800 | tf_op jit(solution)/shard_map/ppermute | solution.py:548
  9.3 4.9 %collective-permute-start.2 = (bf16[64,128]{1,0:T(8,128)(2,1)S(1)}, bf16[64,128]{1,0:T(8,128)(2,1)S(1)}, u32[]{:S(2)}, u32[]{:S(2)}) collective-permute-start(bf16[64,128]{1,0:T(8,128)(2,1)S(1)} %shard_map.70.refs_0_), channel_id=1, source_target_pairs={{2,1},{3,4},{6,5},{7,8},{10,9},{11,12},{14,13},{1,2},{4,3},{5,6},{... | collective-permute-start | bytes 49160 | tf_op jit(solution)/shard_map/ppermute | solution.py:602
  11.7 6.0 %collective-permute-start.1 = (bf16[336,128]{1,0:T(8,128)(2,1)S(1)}, bf16[336,128]{1,0:T(8,128)(2,1)S(1)}, u32[]{:S(2)}, u32[]{:S(2)}) collective-permute-start(bf16[336,128]{1,0:T(8,128)(2,1)S(1)} %get-tuple-element.39.w_ref.refs_0_), channel_id=1, source_target_pairs={{0,2},{2,0},{1,3},{3,1},{4,6},{6,4},{5,7},{7,5},{8,10},{10,8},{9,1... | collective-permute-start | bytes 258056 | tf_op jit(solution)/shard_map/ppermute | solution.py:548
  19.8 3.4 %collective-permute-start.3 = (f32[32,672]{1,0:T(8,128)S(1)}, f32[32,672]{1,0:T(8,128)S(1)}, u32[]{:S(2)}, u32[]{:S(2)}) collective-permute-start(f32[32,672]{1,0:T(8,128)S(1)} %get-tuple-element.45), channel_id=1, source_target_pairs={{0,1},{1,0},{2,3},{3,2},{4,5},{5,4},{6,7},{7,6},{8,9},{9,8},{10,11... | collective-permute-start | bytes 258056 | tf_op jit(solution)/shard_map/ppermute | solution.py:551
  23.1 1.3 %collective-permute-start.4 = (f32[32,640]{1,0:T(8,128)S(1)}, f32[32,640]{1,0:T(8,128)S(1)}, u32[]{:S(2)}, u32[]{:S(2)}) collective-permute-start(f32[32,640]{1,0:T(8,128)S(1)} %get-tuple-element.48), channel_id=1, source_target_pairs={{0,1},{1,0},{2,3},{3,2},{4,5},{5,4},{6,7},{7,6},{8,9},{9,8},{10,11... | collective-permute-start | bytes 245768 | tf_op jit(solution)/shard_map/ppermute | solution.py:551
  23.2 4.1 %collective-permute-start.5 = (bf16[176,128]{1,0:T(8,128)(2,1)S(1)}, bf16[176,128]{1,0:T(8,128)(2,1)S(1)}, u32[]{:S(2)}, u32[]{:S(2)}) collective-permute-start(bf16[176,128]{1,0:T(8,128)(2,1)S(1)} %get-tuple-element.46.refs_0_), channel_id=1, source_target_pairs={{0,2},{2,0},{1,3},{3,1},{4,6},{6,4},{5,7},{7,5},{8,10},{10,8},{9,1... | collective-permute-start | bytes 135176 | tf_op jit(solution)/shard_map/ppermute | solution.py:548
  27.5 6.2 %collective-permute-start.6 = (bf16[176,128]{1,0:T(8,128)(2,1)S(1)}, bf16[176,128]{1,0:T(8,128)(2,1)S(1)}, u32[]{:S(2)}, u32[]{:S(2)}) collective-permute-start(bf16[176,128]{1,0:T(8,128)(2,1)S(1)} %shard_map.78.refs_0_), channel_id=1, source_target_pairs={{12,0},{8,4},{4,8},{0,12},{13,1},{9,5},{5,9},{1,13},{14,2},{10,6},... | collective-permute-start | bytes 135176 | tf_op jit(solution)/shard_map/ppermute | solution.py:554
  31.0 4.9 %collective-permute-start.7 = (bf16[176,128]{1,0:T(8,128)(2,1)S(1)}, bf16[176,128]{1,0:T(8,128)(2,1)S(1)}, u32[]{:S(2)}, u32[]{:S(2)}) collective-permute-start(bf16[176,128]{1,0:T(8,128)(2,1)S(1)} %shard_map.78.refs_0_), channel_id=1, source_target_pairs={{8,0},{12,4},{0,8},{4,12},{9,1},{13,5},{1,9},{5,13},{10,2},{14,6},... | collective-permute-start | bytes 135176 | tf_op jit(solution)/shard_map/ppermute | solution.py:554
  31.0 4.9 %collective-permute-start.8 = (bf16[176,128]{1,0:T(8,128)(2,1)S(1)}, bf16[176,128]{1,0:T(8,128)(2,1)S(1)}, u32[]{:S(2)}, u32[]{:S(2)}) collective-permute-start(bf16[176,128]{1,0:T(8,128)(2,1)S(1)} %shard_map.78.refs_0_), channel_id=1, source_target_pairs={{4,0},{0,4},{12,8},{8,12},{5,1},{1,5},{13,9},{9,13},{6,2},{2,6},{1... | collective-permute-start | bytes 135176 | tf_op jit(solution)/shard_map/ppermute | solution.py:554
  36.6 1.2 %collective-permute-start.9 = (bf16[176,128]{1,0:T(8,128)(2,1)S(1)}, bf16[176,128]{1,0:T(8,128)(2,1)S(1)}, u32[]{:S(2)}, u32[]{:S(2)}) collective-permute-start(bf16[176,128]{1,0:T(8,128)(2,1)S(1)} %get-tuple-element.49.refs_0_), channel_id=1, source_target_pairs={{0,1},{1,0},{2,3},{3,2},{4,5},{5,4},{6,7},{7,6},{8,9},{9,8},{10,11... | collective-permute-start | bytes 135176 | tf_op jit(solution)/shard_map/ppermute | solution.py:551
  36.6 4.1 %collective-permute-start.10 = (bf16[176,128]{1,0:T(8,128)(2,1)S(1)}, bf16[176,128]{1,0:T(8,128)(2,1)S(1)}, u32[]{:S(2)}, u32[]{:S(2)}) collective-permute-start(bf16[176,128]{1,0:T(8,128)(2,1)S(1)} %get-tuple-element.49.refs_0_), channel_id=1, source_target_pairs={{0,2},{2,0},{1,3},{3,1},{4,6},{6,4},{5,7},{7,5},{8,10},{10,8},{9,1... | collective-permute-start | bytes 135176 | tf_op jit(solution)/shard_map/ppermute | solution.py:548
  40.7 1.2 %collective-permute-start.11 = (bf16[176,128]{1,0:T(8,128)(2,1)S(1)}, bf16[176,128]{1,0:T(8,128)(2,1)S(1)}, u32[]{:S(2)}, u32[]{:S(2)}) collective-permute-start(bf16[176,128]{1,0:T(8,128)(2,1)S(1)} %collective-permute-done.10.refs_0_.refs_2_), channel_id=1, source_target_pairs={{0,1},{1,0},{2,3},{3,2},{4,5},{5,4},{6,7},{7,6},{8,9},{9,8},{10,11... | collective-permute-start | bytes 135176 | tf_op jit(solution)/shard_map/ppermute | solution.py:551
  43.4 2.2 %collective-permute-start.12 = (f32[32,672]{1,0:T(8,128)S(1)}, f32[32,672]{1,0:T(8,128)S(1)}, u32[]{:S(2)}, u32[]{:S(2)}) collective-permute-start(f32[32,672]{1,0:T(8,128)S(1)} %get-tuple-element.55), channel_id=1, source_target_pairs={{0,1},{1,0},{2,3},{3,2},{4,5},{5,4},{6,7},{7,6},{8,9},{9,8},{10,11... | collective-permute-start | bytes 258056 | tf_op jit(solution)/shard_map/ppermute | solution.py:551
  45.2 1.6 %collective-permute-start.13 = (f32[32,640]{1,0:T(8,128)S(1)}, f32[32,640]{1,0:T(8,128)S(1)}, u32[]{:S(2)}, u32[]{:S(2)}) collective-permute-start(f32[32,640]{1,0:T(8,128)S(1)} %get-tuple-element.58), channel_id=1, source_target_pairs={{0,1},{1,0},{2,3},{3,2},{4,5},{5,4},{6,7},{7,6},{8,9},{9,8},{10,11... | collective-permute-start | bytes 245768 | tf_op jit(solution)/shard_map/ppermute | solution.py:551
  45.7 4.1 %collective-permute-start.14 = (bf16[176,128]{1,0:T(8,128)(2,1)S(1)}, bf16[176,128]{1,0:T(8,128)(2,1)S(1)}, u32[]{:S(2)}, u32[]{:S(2)}) collective-permute-start(bf16[176,128]{1,0:T(8,128)(2,1)S(1)} %get-tuple-element.56.refs_0_), channel_id=1, source_target_pairs={{0,2},{2,0},{1,3},{3,1},{4,6},{6,4},{5,7},{7,5},{8,10},{10,8},{9,1... | collective-permute-start | bytes 135176 | tf_op jit(solution)/shard_map/ppermute | solution.py:548
  50.0 8.3 %collective-permute-start.15 = (f32[32,2048]{1,0:T(8,128)S(1)}, f32[32,2048]{1,0:T(8,128)S(1)}, u32[]{:S(2)}, u32[]{:S(2)}) collective-permute-start(f32[32,2048]{1,0:T(8,128)S(1)} %get-tuple-element.59.h_ref.refs_0_), channel_id=1, source_target_pairs={{0,2},{2,0},{1,3},{3,1},{4,6},{6,4},{5,7},{7,5},{8,10},{10,8},{9,1... | collective-permute-start | bytes 786440 | tf_op jit(solution)/shard_map/ppermute | solution.py:548
  50.3 5.8 %collective-permute-start.16 = (bf16[176,128]{1,0:T(8,128)(2,1)S(1)}, bf16[176,128]{1,0:T(8,128)(2,1)S(1)}, u32[]{:S(2)}, u32[]{:S(2)}) collective-permute-start(bf16[176,128]{1,0:T(8,128)(2,1)S(1)} %shard_map.86.refs_0_), channel_id=1, source_target_pairs={{12,0},{8,4},{4,8},{0,12},{13,1},{9,5},{5,9},{1,13},{14,2},{10,6},... | collective-permute-start | bytes 135176 | tf_op jit(solution)/shard_map/ppermute | solution.py:554
  51.8 5.1 %collective-permute-start.17 = (bf16[176,128]{1,0:T(8,128)(2,1)S(1)}, bf16[176,128]{1,0:T(8,128)(2,1)S(1)}, u32[]{:S(2)}, u32[]{:S(2)}) collective-permute-start(bf16[176,128]{1,0:T(8,128)(2,1)S(1)} %shard_map.86.refs_0_), channel_id=1, source_target_pairs={{8,0},{12,4},{0,8},{4,12},{9,1},{13,5},{1,9},{5,13},{10,2},{14,6},... | collective-permute-start | bytes 135176 | tf_op jit(solution)/shard_map/ppermute | solution.py:554
  52.3 4.9 %collective-permute-start.18 = (bf16[176,128]{1,0:T(8,128)(2,1)S(1)}, bf16[176,128]{1,0:T(8,128)(2,1)S(1)}, u32[]{:S(2)}, u32[]{:S(2)}) collective-permute-start(bf16[176,128]{1,0:T(8,128)(2,1)S(1)} %shard_map.86.refs_0_), channel_id=1, source_target_pairs={{4,0},{0,4},{12,8},{8,12},{5,1},{1,5},{13,9},{9,13},{6,2},{2,6},{1... | collective-permute-start | bytes 135176 | tf_op jit(solution)/shard_map/ppermute | solution.py:554
  58.2 1.5 %collective-permute-start.19 = (f32[32,1280]{1,0:T(8,128)S(1)}, f32[32,1280]{1,0:T(8,128)S(1)}, u32[]{:S(2)}, u32[]{:S(2)}) collective-permute-start(f32[32,1280]{1,0:T(8,128)S(1)} %shard_map.88.refs_0_), channel_id=1, source_target_pairs={{0,1},{1,0},{2,3},{3,2},{4,5},{5,4},{6,7},{7,6},{8,9},{9,8},{10,11... | collective-permute-start | bytes 491528 | tf_op jit(solution)/shard_map/ppermute | solution.py:551

commit v17 on v16

--- a/solution.py
+++ b/solution.py
@@ -18,7 +18,6 @@
 AHEAD = CUTS[0]
 F32 = jnp.float32
 BF16 = jnp.bfloat16
-HIGH = lax.Precision.HIGHEST
 NT = (((1,), (1,)), ((), ()))
 MIB = 1024 * 1024
 
@@ -86,7 +85,7 @@
     piece_ref, msg_ref = refs[-2:]
     w = w_ref[...]
     rank, size = piece_ref.shape
-    gram = lax.dot_general(w, w, NT, precision=HIGH, preferred_element_type=F32)
+    gram = two_term_gram(w)
     moved = jnp.dot(three_terms(w), order_ref[...], preferred_element_type=F32)
     whole = moved[:rank] + (moved[rank : 2 * rank] + moved[2 * rank :])
     for c in range(w.shape[1] // size):
@@ -450,9 +449,9 @@
     rank, size = new_ref.shape
     total, gram = summed(lax.axis_index("frm"), count, msg_refs, scr, rank, size)
     w = w_ref[...]
-    new = w * total / jnp.dot(gram, w, precision=HIGH, preferred_element_type=F32)
+    new = w * total / two_term_dot(gram, w)
     new_ref[...] = new
-    pack(out_ref, new, lax.dot_general(new, new, NT, precision=HIGH, preferred_element_type=F32))
+    pack(out_ref, new, two_term_gram(new))
 
 
 def last_kernel(count, w_ref, order_ref, *refs):
@@ -460,7 +459,7 @@
     rank, size = w_ref.shape
     total, gram = summed(lax.axis_index("frm"), count, msg_refs, scr, rank, size)
     w = w_ref[...]
-    new = w * total / jnp.dot(gram, w, precision=HIGH, preferred_element_type=F32)
+    new = w * total / two_term_dot(gram, w)
     terms = three_terms(new)
     for c in range(order_ref.shape[1] // size):
 

time: 60.6 us -> 60.7 us (level)
  no operation moved by 1% of the time
where the time goes in v17:
time: 60.7 us; the launch traced here: 60.5 us
  Pallas kernels  24.6 us (41%)
  starting transfers between devices  18.4 us (30%)
  waiting for transfers between devices  16.6 us (27%)
  between operations  0.93 us (2%)
    pallas_call x22, Pallas kernels, call(): pl.pallas_call(kernel, out_shape=[jax.ShapeDtypeStruct(*out) if isinstanc...  24.6 us
    ppermute x6, starting transfers between devices, frm_shift(): lax.ppermute(value, 'frm', [(partner(i, shift, frms), i) for i in range(f...  8.78 us
    ppermute x6, waiting for transfers between devices, row_shift(): lax.ppermute(value, 'row', [(i, (i + shift) % rows) for i in range(rows)])  7.77 us
    ppermute x6, waiting for transfers between devices, frm_shift(): lax.ppermute(value, 'frm', [(partner(i, shift, frms), i) for i in range(f...  6.64 us
    ppermute x6, starting transfers between devices, row_shift(): lax.ppermute(value, 'row', [(i, (i + shift) % rows) for i in range(rows)])  6.54 us
    ppermute x7, starting transfers between devices, sub_shift(): lax.ppermute(value, 'sub', [(i, (i + shift) % subs) for i in range(subs)])  2.44 us
    ppermute x7, waiting for transfers between devices, sub_shift(): lax.ppermute(value, 'sub', [(i, (i + shift) % subs) for i in range(subs)])  2.16 us
  transfers between devices with their start and end apart: 20, of which 11 were waited for; matrix products, arithmetic and copies ran while one was open for 0% of the time, Pallas kernels for 30%

profile of v17, /device:TPU:0, one launch (start us, length us, event | category | flops | bytes accessed | tf_op | source)
XLA Modules:
  0.0 60.5 jit_solution(1388037375858751012)
XLA Ops:
  0.6 1.2 %shard_map.68 = (bf16[32,2176]{1,0:T(8,128)(2,1)S(1)}, bf16[32,2176]{1,0:T(8,128)(2,1)S(1)}, bf16[4,256,256]{2,1,0:T(8,128)(2,1)S(1)}) custom-call(bf16[32,4096]{1,0:T(8,128)(2,1)} %sig_hbm.1, bf16[40,256,256]{2,1,0:T(8,128)(2,1)} %constant.4.clone.tab_hbm), custom_call_target="tpu_custom_call" | custom-call | tf_op jit(solution)/shard_map/pallas_call | solution.py:507
  1.9 3.0 %collective-permute-start = (bf16[32,2176]{1,0:T(8,128)(2,1)S(1)}, bf16[32,2176]{1,0:T(8,128)(2,1)S(1)}, u32[]{:S(2)}, u32[]{:S(2)}) collective-permute-start(bf16[32,2176]{1,0:T(8,128)(2,1)S(1)} %get-tuple-element.36), channel_id=1, source_target_pairs={{0,2},{2,0},{1,3},{3,1},{4,6},{6,4},{5,7},{7,5},{8,10},{10,8},{9,1... | collective-permute-start | bytes 417800 | tf_op jit(solution)/shard_map/ppermute | solution.py:547
  4.9 4.3 %shard_map.69 = (bf16[40,16,2,32,128]{4,3,2,1,0:T(8,128)(2,1)S(1)}, f32[32,1280]{1,0:T(8,128)S(1)}, f32[32,2048]{1,0:T(8,128)S(1)}, bf16[1280,1280]{1,0:T(8,128)(2,1)S(1)}, bf16[36,256,256]{2,1,0:T(8,128)(2,1)S(1)}) custom-call(bf16[32,2176]{1,0:T(8,128)(2,1)S(1)} %get-tuple-element.32.sig_ref.refs_0_, bf16[4,256,256]{2,1,0:T(8,128)(2,1)S(1)} %get-tuple-element.33.ahead_ref, ...), custom_call_target="tpu_custom_call" | custom-call | flops 2684354560 | tf_op jit(solution)/shard_map/pallas_call | solution.py:507
  9.2 0.0 collective-permute-done.refs_0_.refs_1_
  9.3 0.7 %collective-permute-start.2 = (bf16[64,128]{1,0:T(8,128)(2,1)S(1)}, bf16[64,128]{1,0:T(8,128)(2,1)S(1)}, u32[]{:S(2)}, u32[]{:S(2)}) collective-permute-start(bf16[64,128]{1,0:T(8,128)(2,1)S(1)} %shard_map.70.refs_0_), channel_id=1, source_target_pairs={{2,1},{3,4},{6,5},{7,8},{10,9},{11,12},{14,13},{1,2},{4,3},{5,6},{... | collective-permute-start | bytes 49160 | tf_op jit(solution)/shard_map/ppermute | solution.py:601
  9.9 0.7 %shard_map.71 = (f32[32,640]{1,0:T(8,128)S(1)}, bf16[336,128]{1,0:T(8,128)(2,1)S(1)}) custom-call(f32[32,1280]{1,0:T(8,128)S(1)} %get-tuple-element.34.w_ref, bf16[1280,1280]{1,0:T(8,128)(2,1)S(1)} %get-tuple-element.35.order_ref, bf16[64,128]{1,0:T(8,128)(2,1)S(1)} %shard_map.70.refs_0_), custom_call_target="tpu_custom_call" | custom-call | tf_op jit(solution)/shard_map/pallas_call | solution.py:507
  10.7 0.9 %shard_map.72.refs_3_.refs_2_ = f32[32,2048]{1,0:T(8,128)S(1)} custom-call(bf16[336,128]{1,0:T(8,128)(2,1)S(1)} %get-tuple-element.39.w_ref.refs_0_, bf16[40,16,2,32,128]{4,3,2,1,0:T(8,128)(2,1)S(1)} %get-tuple-element.37.refs_1_.s_ref.refs_2_), custom_call_target="tpu_custom_call" | custom-call | flops 1342177280 | tf_op jit(solution)/shard_map/pallas_call | solution.py:507
  11.6 2.5 %collective-permute-start.1 = (bf16[336,128]{1,0:T(8,128)(2,1)S(1)}, bf16[336,128]{1,0:T(8,128)(2,1)S(1)}, u32[]{:S(2)}, u32[]{:S(2)}) collective-permute-start(bf16[336,128]{1,0:T(8,128)(2,1)S(1)} %get-tuple-element.39.w_ref.refs_0_), channel_id=1, source_target_pairs={{0,2},{2,0},{1,3},{3,1},{4,6},{6,4},{5,7},{7,5},{8,10},{10,8},{9,1... | collective-permute-start | bytes 258056 | tf_op jit(solution)/shard_map/ppermute | solution.py:547
  14.0 0.0 collective-permute-done.2.halo_ref
  14.0 3.5 %shard_map.73.refs_4_.s_ref.refs_2_.refs_6_ = bf16[40,16,2,32,128]{4,3,2,1,0:T(8,128)(2,1)S(1)} custom-call(bf16[64,128]{1,0:T(8,128)(2,1)S(1)} %collective-permute-done.2.halo_ref, bf16[4,256,256]{2,1,0:T(8,128)(2,1)S(1)} %get-tuple-element.33.ahead_ref, bf16[36,256,256]{2,1,0:T(8,128)(2,1)S(1)} %get-tuple-element.41.tab_ref, ...), custom_call_target="tpu_custom_call", output_to_operand_aliasing={{}: (5, {})} | custom-call | flops 5368709120 | tf_op jit(solution)/shard_map/pallas_call | solution.py:507
  17.6 0.0 collective-permute-done.1.refs_1_
  17.6 2.1 %shard_map.74 = (f32[32,2048]{1,0:T(8,128)S(1)}, f32[32,32]{1,0:T(8,128)S(1)}, f32[32,672]{1,0:T(8,128)S(1)}) custom-call(bf16[336,128]{1,0:T(8,128)(2,1)S(1)} %get-tuple-element.39.w_ref.refs_0_, bf16[336,128]{1,0:T(8,128)(2,1)S(1)} %collective-permute-done.1.refs_1_, f32[32,2048]{1,0:T(8,128)S(1)} %shard_map.72.refs_3_.refs_2_, ...), custom_call_target="tpu_custom_call" | custom-call | tf_op jit(solution)/shard_map/pallas_call | solution.py:507
  19.6 1.7 %collective-permute-start.3 = (f32[32,672]{1,0:T(8,128)S(1)}, f32[32,672]{1,0:T(8,128)S(1)}, u32[]{:S(2)}, u32[]{:S(2)}) collective-permute-start(f32[32,672]{1,0:T(8,128)S(1)} %get-tuple-element.45), channel_id=1, source_target_pairs={{0,1},{1,0},{2,3},{3,2},{4,5},{5,4},{6,7},{7,6},{8,9},{9,8},{10,11... | collective-permute-start | bytes 258056 | tf_op jit(solution)/shard_map/ppermute | solution.py:550
  21.3 1.6 %shard_map.75 = (f32[32,640]{1,0:T(8,128)S(1)}, f32[32,640]{1,0:T(8,128)S(1)}) custom-call(f32[32,2048]{1,0:T(8,128)S(1)} %get-tuple-element.42.h_ref.refs_5_, bf16[40,16,2,32,128]{4,3,2,1,0:T(8,128)(2,1)S(1)} %shard_map.73.refs_4_.s_ref.refs_2_.refs_6_), custom_call_target="tpu_custom_call" | custom-call | flops 1342177280 | tf_op jit(solution)/shard_map/pallas_call | solution.py:507
  23.0 0.1 collective-permute-start.4
  23.0 0.0 collective-permute-done.3.refs_2_
  23.0 0.1 shard_map.76
  23.1 0.3 collective-permute-start.5
  23.4 0.8 %shard_map.77.own_ref = f32[32,640]{1,0:T(8,128)S(1)} custom-call(f32[32,2048]{1,0:T(8,128)S(1)} %get-tuple-element.42.h_ref.refs_5_, bf16[40,16,2,32,128]{4,3,2,1,0:T(8,128)(2,1)S(1)} %shard_map.73.refs_4_.s_ref.refs_2_.refs_6_, bf16[176,128]{1,0:T(8,128)(2,1)S(1)} %get-tuple-element.46.refs_0_), custom_call_target="tpu_custom_call" | custom-call | flops 1 | tf_op jit(solution)/shard_map/pallas_call | solution.py:507
  24.3 0.0 collective-permute-done.4.refs_0_
  24.3 2.9 %collective-permute-done.5.refs_1_ = bf16[176,128]{1,0:T(8,128)(2,1)S(1)} collective-permute-done((bf16[176,128]{1,0:T(8,128)(2,1)S(1)}, bf16[176,128]{1,0:T(8,128)(2,1)S(1)}, u32[]{:S(2)}, u32[]{:S(2)}) %collective-permute-start.5) | collective-permute-done | bytes 45088 | tf_op jit(solution)/shard_map/ppermute | solution.py:547
  27.2 0.2 shard_map.78.refs_0_
  27.4 3.6 %collective-permute-start.6 = (bf16[176,128]{1,0:T(8,128)(2,1)S(1)}, bf16[176,128]{1,0:T(8,128)(2,1)S(1)}, u32[]{:S(2)}, u32[]{:S(2)}) collective-permute-start(bf16[176,128]{1,0:T(8,128)(2,1)S(1)} %shard_map.78.refs_0_), channel_id=1, source_target_pairs={{12,0},{8,4},{4,8},{0,12},{13,1},{9,5},{5,9},{1,13},{14,2},{10,6},... | collective-permute-start | bytes 135176 | tf_op jit(solution)/shard_map/ppermute | solution.py:553
  31.0 0.0 collective-permute-start.7
  31.0 0.8 %collective-permute-start.8 = (bf16[176,128]{1,0:T(8,128)(2,1)S(1)}, bf16[176,128]{1,0:T(8,128)(2,1)S(1)}, u32[]{:S(2)}, u32[]{:S(2)}) collective-permute-start(bf16[176,128]{1,0:T(8,128)(2,1)S(1)} %shard_map.78.refs_0_), channel_id=1, source_target_pairs={{4,0},{0,4},{12,8},{8,12},{5,1},{1,5},{13,9},{9,13},{6,2},{2,6},{1... | collective-permute-start | bytes 135176 | tf_op jit(solution)/shard_map/ppermute | solution.py:553
  31.8 1.8 %collective-permute-done.6.refs_1_ = bf16[176,128]{1,0:T(8,128)(2,1)S(1)} collective-permute-done((bf16[176,128]{1,0:T(8,128)(2,1)S(1)}, bf16[176,128]{1,0:T(8,128)(2,1)S(1)}, u32[]{:S(2)}, u32[]{:S(2)}) %collective-permute-start.6) | collective-permute-done | bytes 45088 | tf_op jit(solution)/shard_map/ppermute | solution.py:553
  33.5 2.4 %collective-permute-done.7.refs_2_ = bf16[176,128]{1,0:T(8,128)(2,1)S(1)} collective-permute-done((bf16[176,128]{1,0:T(8,128)(2,1)S(1)}, bf16[176,128]{1,0:T(8,128)(2,1)S(1)}, u32[]{:S(2)}, u32[]{:S(2)}) %collective-permute-start.7) | collective-permute-done | bytes 45088 | tf_op jit(solution)/shard_map/ppermute | solution.py:553
  35.9 0.0 collective-permute-done.8.refs_3_
  35.9 0.7 %shard_map.79 = (f32[32,640]{1,0:T(8,128)S(1)}, bf16[176,128]{1,0:T(8,128)(2,1)S(1)}) custom-call(f32[32,640]{1,0:T(8,128)S(1)} %get-tuple-element.38.w_ref, bf16[176,128]{1,0:T(8,128)(2,1)S(1)} %shard_map.78.refs_0_, bf16[176,128]{1,0:T(8,128)(2,1)S(1)} %collective-permute-done.6.refs_1_, bf16[176,128]{1,0:T(8,128)(2,1)S(1)} %collective-permute-done.7.refs_2_, ...), custom_call_target="tpu_custom_call" | custom-call | tf_op jit(solution)/shard_map/pallas_call | solution.py:507
  36.7 0.0 collective-permute-start.9
  36.7 0.3 collective-permute-start.10
  37.0 0.9 %collective-permute-done.9.refs_1_ = bf16[176,128]{1,0:T(8,128)(2,1)S(1)} collective-permute-done((bf16[176,128]{1,0:T(8,128)(2,1)S(1)}, bf16[176,128]{1,0:T(8,128)(2,1)S(1)}, u32[]{:S(2)}, u32[]{:S(2)}) %collective-permute-start.9) | collective-permute-done | bytes 45088 | tf_op jit(solution)/shard_map/ppermute | solution.py:550
  37.9 1.0 %shard_map.80.refs_1_ = f32[32,2048]{1,0:T(8,128)S(1)} custom-call(bf16[176,128]{1,0:T(8,128)(2,1)S(1)} %get-tuple-element.49.refs_0_, bf16[176,128]{1,0:T(8,128)(2,1)S(1)} %collective-permute-done.9.refs_1_, bf16[40,16,2,32,128]{4,3,2,1,0:T(8,128)(2,1)S(1)} %shard_map.73.refs_4_.s_ref.refs_2_.refs_6_), custom_call_target="tpu_custom_call" | custom-call | flops 1342177280 | tf_op jit(solution)/shard_map/pallas_call | solution.py:507
  38.9 1.9 %collective-permute-done.10.refs_0_.refs_2_ = bf16[176,128]{1,0:T(8,128)(2,1)S(1)} collective-permute-done((bf16[176,128]{1,0:T(8,128)(2,1)S(1)}, bf16[176,128]{1,0:T(8,128)(2,1)S(1)}, u32[]{:S(2)}, u32[]{:S(2)}) %collective-permute-start.10) | collective-permute-done | bytes 45088 | tf_op jit(solution)/shard_map/ppermute | solution.py:547
  40.8 0.0 collective-permute-start.11
  40.8 0.6 shard_map.81.refs_4_
  41.4 0.7 %collective-permute-done.11.refs_3_ = bf16[176,128]{1,0:T(8,128)(2,1)S(1)} collective-permute-done((bf16[176,128]{1,0:T(8,128)(2,1)S(1)}, bf16[176,128]{1,0:T(8,128)(2,1)S(1)}, u32[]{:S(2)}, u32[]{:S(2)}) %collective-permute-start.11) | collective-permute-done | bytes 45088 | tf_op jit(solution)/shard_map/ppermute | solution.py:550
  42.0 1.5 %shard_map.82 = (f32[32,2048]{1,0:T(8,128)S(1)}, f32[32,32]{1,0:T(8,128)S(1)}, f32[32,672]{1,0:T(8,128)S(1)}) custom-call(bf16[176,128]{1,0:T(8,128)(2,1)S(1)} %get-tuple-element.49.refs_0_, bf16[176,128]{1,0:T(8,128)(2,1)S(1)} %collective-permute-done.9.refs_1_, bf16[176,128]{1,0:T(8,128)(2,1)S(1)} %collective-permute-done.10.refs_0_.refs_2_, ...), custom_call_target="tpu_custom_call" | custom-call | tf_op jit(solution)/shard_map/pallas_call | solution.py:507
  43.5 0.2 collective-permute-start.12
  43.7 1.6 %shard_map.83 = (f32[32,640]{1,0:T(8,128)S(1)}, f32[32,640]{1,0:T(8,128)S(1)}) custom-call(f32[32,2048]{1,0:T(8,128)S(1)} %get-tuple-element.59.h_ref.refs_0_, bf16[40,16,2,32,128]{4,3,2,1,0:T(8,128)(2,1)S(1)} %shard_map.73.refs_4_.s_ref.refs_2_.refs_6_), custom_call_target="tpu_custom_call" | custom-call | flops 1342177280 | tf_op jit(solution)/shard_map/pallas_call | solution.py:507
  45.3 0.4 collective-permute-start.13
  45.7 0.0 collective-permute-done.12.refs_2_
  45.7 0.1 shard_map.84
  45.8 0.2 collective-permute-start.14
  46.0 0.8 %shard_map.85.own_ref = f32[32,640]{1,0:T(8,128)S(1)} custom-call(f32[32,2048]{1,0:T(8,128)S(1)} %get-tuple-element.59.h_ref.refs_0_, bf16[40,16,2,32,128]{4,3,2,1,0:T(8,128)(2,1)S(1)} %shard_map.73.refs_4_.s_ref.refs_2_.refs_6_, bf16[176,128]{1,0:T(8,128)(2,1)S(1)} %get-tuple-element.56.refs_0_), custom_call_target="tpu_custom_call" | custom-call | flops 1 | tf_op jit(solution)/shard_map/pallas_call | solution.py:507
  46.9 0.0 collective-permute-done.13.refs_0_
  46.9 3.0 %collective-permute-done.14.refs_1_ = bf16[176,128]{1,0:T(8,128)(2,1)S(1)} collective-permute-done((bf16[176,128]{1,0:T(8,128)(2,1)S(1)}, bf16[176,128]{1,0:T(8,128)(2,1)S(1)}, u32[]{:S(2)}, u32[]{:S(2)}) %collective-permute-start.14) | collective-permute-done | bytes 45088 | tf_op jit(solution)/shard_map/ppermute | solution.py:547
  49.8 0.2 shard_map.86.refs_0_
  50.1 0.2 collective-permute-start.15
  50.3 1.5 %collective-permute-start.16 = (bf16[176,128]{1,0:T(8,128)(2,1)S(1)}, bf16[176,128]{1,0:T(8,128)(2,1)S(1)}, u32[]{:S(2)}, u32[]{:S(2)}) collective-permute-start(bf16[176,128]{1,0:T(8,128)(2,1)S(1)} %shard_map.86.refs_0_), channel_id=1, source_target_pairs={{12,0},{8,4},{4,8},{0,12},{13,1},{9,5},{5,9},{1,13},{14,2},{10,6},... | collective-permute-start | bytes 135176 | tf_op jit(solution)/shard_map/ppermute | solution.py:553
  51.8 0.5 collective-permute-start.17
  52.3 2.4 %collective-permute-start.18 = (bf16[176,128]{1,0:T(8,128)(2,1)S(1)}, bf16[176,128]{1,0:T(8,128)(2,1)S(1)}, u32[]{:S(2)}, u32[]{:S(2)}) collective-permute-start(bf16[176,128]{1,0:T(8,128)(2,1)S(1)} %shard_map.86.refs_0_), channel_id=1, source_target_pairs={{4,0},{0,4},{12,8},{8,12},{5,1},{1,5},{13,9},{9,13},{6,2},{2,6},{1... | collective-permute-start | bytes 135176 | tf_op jit(solution)/shard_map/ppermute | solution.py:553
  54.7 1.5 %collective-permute-done.16.refs_1_ = bf16[176,128]{1,0:T(8,128)(2,1)S(1)} collective-permute-done((bf16[176,128]{1,0:T(8,128)(2,1)S(1)}, bf16[176,128]{1,0:T(8,128)(2,1)S(1)}, u32[]{:S(2)}, u32[]{:S(2)}) %collective-permute-start.16) | collective-permute-done | bytes 45088 | tf_op jit(solution)/shard_map/ppermute | solution.py:553
  56.1 0.7 %collective-permute-done.17.refs_2_ = bf16[176,128]{1,0:T(8,128)(2,1)S(1)} collective-permute-done((bf16[176,128]{1,0:T(8,128)(2,1)S(1)}, bf16[176,128]{1,0:T(8,128)(2,1)S(1)}, u32[]{:S(2)}, u32[]{:S(2)}) %collective-permute-start.17) | collective-permute-done | bytes 45088 | tf_op jit(solution)/shard_map/ppermute | solution.py:553
  56.8 0.3 collective-permute-done.18.refs_3_
  57.2 1.0 %shard_map.88.refs_0_ = f32[32,1280]{1,0:T(8,128)S(1)} custom-call(f32[32,640]{1,0:T(8,128)S(1)} %get-tuple-element.60.w_ref, bf16[1280,1280]{1,0:T(8,128)(2,1)S(1)} %get-tuple-element.35.order_ref, bf16[176,128]{1,0:T(8,128)(2,1)S(1)} %shard_map.86.refs_0_, bf16[176,128]{1,0:T(8,128)(2,1)S(1)} %collective-permute-done.16.refs_1_, ...), custom_call_target="tpu_custom_call" | custom-call | tf_op jit(solution)/shard_map/pallas_call | solution.py:507
  58.2 0.1 collective-permute-start.19
  58.3 0.0 collective-permute-done.15.refs_1_
  58.3 0.8 %shard_map.87._ = f32[32,4096]{1,0:T(8,128)} custom-call(f32[32,2048]{1,0:T(8,128)S(1)} %get-tuple-element.59.h_ref.refs_0_, f32[32,2048]{1,0:T(8,128)S(1)} %collective-permute-done.15.refs_1_), custom_call_target="tpu_custom_call" | custom-call | tf_op jit(solution)/shard_map/pallas_call | solution.py:507
  59.1 0.5 collective-permute-done.19.refs_1_
  59.6 0.7 %shard_map.89 = f32[32,1280]{1,0:T(8,128)} custom-call(f32[32,4096]{1,0:T(8,128)} %shard_map.87._, f32[32,1280]{1,0:T(8,128)S(1)} %shard_map.88.refs_0_, f32[32,1280]{1,0:T(8,128)S(1)} %collective-permute-done.19.refs_1_), custom_call_target="tpu_custom_call" | custom-call | tf_op jit(solution)/shard_map/pallas_call | solution.py:507
  (1 shorter events, 0.0 us)
Async XLA Ops:
  1.9 7.4 %collective-permute-start = (bf16[32,2176]{1,0:T(8,128)(2,1)S(1)}, bf16[32,2176]{1,0:T(8,128)(2,1)S(1)}, u32[]{:S(2)}, u32[]{:S(2)}) collective-permute-start(bf16[32,2176]{1,0:T(8,128)(2,1)S(1)} %get-tuple-element.36), channel_id=1, source_target_pairs={{0,2},{2,0},{1,3},{3,1},{4,6},{6,4},{5,7},{7,5},{8,10},{10,8},{9,1... | collective-permute-start | bytes 417800 | tf_op jit(solution)/shard_map/ppermute | solution.py:547
  9.3 4.8 %collective-permute-start.2 = (bf16[64,128]{1,0:T(8,128)(2,1)S(1)}, bf16[64,128]{1,0:T(8,128)(2,1)S(1)}, u32[]{:S(2)}, u32[]{:S(2)}) collective-permute-start(bf16[64,128]{1,0:T(8,128)(2,1)S(1)} %shard_map.70.refs_0_), channel_id=1, source_target_pairs={{2,1},{3,4},{6,5},{7,8},{10,9},{11,12},{14,13},{1,2},{4,3},{5,6},{... | collective-permute-start | bytes 49160 | tf_op jit(solution)/shard_map/ppermute | solution.py:601
  11.6 6.0 %collective-permute-start.1 = (bf16[336,128]{1,0:T(8,128)(2,1)S(1)}, bf16[336,128]{1,0:T(8,128)(2,1)S(1)}, u32[]{:S(2)}, u32[]{:S(2)}) collective-permute-start(bf16[336,128]{1,0:T(8,128)(2,1)S(1)} %get-tuple-element.39.w_ref.refs_0_), channel_id=1, source_target_pairs={{0,2},{2,0},{1,3},{3,1},{4,6},{6,4},{5,7},{7,5},{8,10},{10,8},{9,1... | collective-permute-start | bytes 258056 | tf_op jit(solution)/shard_map/ppermute | solution.py:547
  19.6 3.4 %collective-permute-start.3 = (f32[32,672]{1,0:T(8,128)S(1)}, f32[32,672]{1,0:T(8,128)S(1)}, u32[]{:S(2)}, u32[]{:S(2)}) collective-permute-start(f32[32,672]{1,0:T(8,128)S(1)} %get-tuple-element.45), channel_id=1, source_target_pairs={{0,1},{1,0},{2,3},{3,2},{4,5},{5,4},{6,7},{7,6},{8,9},{9,8},{10,11... | collective-permute-start | bytes 258056 | tf_op jit(solution)/shard_map/ppermute | solution.py:550
  23.0 1.3 %collective-permute-start.4 = (f32[32,640]{1,0:T(8,128)S(1)}, f32[32,640]{1,0:T(8,128)S(1)}, u32[]{:S(2)}, u32[]{:S(2)}) collective-permute-start(f32[32,640]{1,0:T(8,128)S(1)} %get-tuple-element.48), channel_id=1, source_target_pairs={{0,1},{1,0},{2,3},{3,2},{4,5},{5,4},{6,7},{7,6},{8,9},{9,8},{10,11... | collective-permute-start | bytes 245768 | tf_op jit(solution)/shard_map/ppermute | solution.py:550
  23.1 4.1 %collective-permute-start.5 = (bf16[176,128]{1,0:T(8,128)(2,1)S(1)}, bf16[176,128]{1,0:T(8,128)(2,1)S(1)}, u32[]{:S(2)}, u32[]{:S(2)}) collective-permute-start(bf16[176,128]{1,0:T(8,128)(2,1)S(1)} %get-tuple-element.46.refs_0_), channel_id=1, source_target_pairs={{0,2},{2,0},{1,3},{3,1},{4,6},{6,4},{5,7},{7,5},{8,10},{10,8},{9,1... | collective-permute-start | bytes 135176 | tf_op jit(solution)/shard_map/ppermute | solution.py:547
  27.4 6.2 %collective-permute-start.6 = (bf16[176,128]{1,0:T(8,128)(2,1)S(1)}, bf16[176,128]{1,0:T(8,128)(2,1)S(1)}, u32[]{:S(2)}, u32[]{:S(2)}) collective-permute-start(bf16[176,128]{1,0:T(8,128)(2,1)S(1)} %shard_map.78.refs_0_), channel_id=1, source_target_pairs={{12,0},{8,4},{4,8},{0,12},{13,1},{9,5},{5,9},{1,13},{14,2},{10,6},... | collective-permute-start | bytes 135176 | tf_op jit(solution)/shard_map/ppermute | solution.py:553
  31.0 4.9 %collective-permute-start.7 = (bf16[176,128]{1,0:T(8,128)(2,1)S(1)}, bf16[176,128]{1,0:T(8,128)(2,1)S(1)}, u32[]{:S(2)}, u32[]{:S(2)}) collective-permute-start(bf16[176,128]{1,0:T(8,128)(2,1)S(1)} %shard_map.78.refs_0_), channel_id=1, source_target_pairs={{8,0},{12,4},{0,8},{4,12},{9,1},{13,5},{1,9},{5,13},{10,2},{14,6},... | collective-permute-start | bytes 135176 | tf_op jit(solution)/shard_map/ppermute | solution.py:553
  31.0 4.9 %collective-permute-start.8 = (bf16[176,128]{1,0:T(8,128)(2,1)S(1)}, bf16[176,128]{1,0:T(8,128)(2,1)S(1)}, u32[]{:S(2)}, u32[]{:S(2)}) collective-permute-start(bf16[176,128]{1,0:T(8,128)(2,1)S(1)} %shard_map.78.refs_0_), channel_id=1, source_target_pairs={{4,0},{0,4},{12,8},{8,12},{5,1},{1,5},{13,9},{9,13},{6,2},{2,6},{1... | collective-permute-start | bytes 135176 | tf_op jit(solution)/shard_map/ppermute | solution.py:553
  36.7 1.2 %collective-permute-start.9 = (bf16[176,128]{1,0:T(8,128)(2,1)S(1)}, bf16[176,128]{1,0:T(8,128)(2,1)S(1)}, u32[]{:S(2)}, u32[]{:S(2)}) collective-permute-start(bf16[176,128]{1,0:T(8,128)(2,1)S(1)} %get-tuple-element.49.refs_0_), channel_id=1, source_target_pairs={{0,1},{1,0},{2,3},{3,2},{4,5},{5,4},{6,7},{7,6},{8,9},{9,8},{10,11... | collective-permute-start | bytes 135176 | tf_op jit(solution)/shard_map/ppermute | solution.py:550
  36.7 4.1 %collective-permute-start.10 = (bf16[176,128]{1,0:T(8,128)(2,1)S(1)}, bf16[176,128]{1,0:T(8,128)(2,1)S(1)}, u32[]{:S(2)}, u32[]{:S(2)}) collective-permute-start(bf16[176,128]{1,0:T(8,128)(2,1)S(1)} %get-tuple-element.49.refs_0_), channel_id=1, source_target_pairs={{0,2},{2,0},{1,3},{3,1},{4,6},{6,4},{5,7},{7,5},{8,10},{10,8},{9,1... | collective-permute-start | bytes 135176 | tf_op jit(solution)/shard_map/ppermute | solution.py:547
  40.8 1.2 %collective-permute-start.11 = (bf16[176,128]{1,0:T(8,128)(2,1)S(1)}, bf16[176,128]{1,0:T(8,128)(2,1)S(1)}, u32[]{:S(2)}, u32[]{:S(2)}) collective-permute-start(bf16[176,128]{1,0:T(8,128)(2,1)S(1)} %collective-permute-done.10.refs_0_.refs_2_), channel_id=1, source_target_pairs={{0,1},{1,0},{2,3},{3,2},{4,5},{5,4},{6,7},{7,6},{8,9},{9,8},{10,11... | collective-permute-start | bytes 135176 | tf_op jit(solution)/shard_map/ppermute | solution.py:550
  43.5 2.2 %collective-permute-start.12 = (f32[32,672]{1,0:T(8,128)S(1)}, f32[32,672]{1,0:T(8,128)S(1)}, u32[]{:S(2)}, u32[]{:S(2)}) collective-permute-start(f32[32,672]{1,0:T(8,128)S(1)} %get-tuple-element.55), channel_id=1, source_target_pairs={{0,1},{1,0},{2,3},{3,2},{4,5},{5,4},{6,7},{7,6},{8,9},{9,8},{10,11... | collective-permute-start | bytes 258056 | tf_op jit(solution)/shard_map/ppermute | solution.py:550
  45.3 1.6 %collective-permute-start.13 = (f32[32,640]{1,0:T(8,128)S(1)}, f32[32,640]{1,0:T(8,128)S(1)}, u32[]{:S(2)}, u32[]{:S(2)}) collective-permute-start(f32[32,640]{1,0:T(8,128)S(1)} %get-tuple-element.58), channel_id=1, source_target_pairs={{0,1},{1,0},{2,3},{3,2},{4,5},{5,4},{6,7},{7,6},{8,9},{9,8},{10,11... | collective-permute-start | bytes 245768 | tf_op jit(solution)/shard_map/ppermute | solution.py:550
  45.8 4.1 %collective-permute-start.14 = (bf16[176,128]{1,0:T(8,128)(2,1)S(1)}, bf16[176,128]{1,0:T(8,128)(2,1)S(1)}, u32[]{:S(2)}, u32[]{:S(2)}) collective-permute-start(bf16[176,128]{1,0:T(8,128)(2,1)S(1)} %get-tuple-element.56.refs_0_), channel_id=1, source_target_pairs={{0,2},{2,0},{1,3},{3,1},{4,6},{6,4},{5,7},{7,5},{8,10},{10,8},{9,1... | collective-permute-start | bytes 135176 | tf_op jit(solution)/shard_map/ppermute | solution.py:547
  50.1 8.2 %collective-permute-start.15 = (f32[32,2048]{1,0:T(8,128)S(1)}, f32[32,2048]{1,0:T(8,128)S(1)}, u32[]{:S(2)}, u32[]{:S(2)}) collective-permute-start(f32[32,2048]{1,0:T(8,128)S(1)} %get-tuple-element.59.h_ref.refs_0_), channel_id=1, source_target_pairs={{0,2},{2,0},{1,3},{3,1},{4,6},{6,4},{5,7},{7,5},{8,10},{10,8},{9,1... | collective-permute-start | bytes 786440 | tf_op jit(solution)/shard_map/ppermute | solution.py:547
  50.3 5.8 %collective-permute-start.16 = (bf16[176,128]{1,0:T(8,128)(2,1)S(1)}, bf16[176,128]{1,0:T(8,128)(2,1)S(1)}, u32[]{:S(2)}, u32[]{:S(2)}) collective-permute-start(bf16[176,128]{1,0:T(8,128)(2,1)S(1)} %shard_map.86.refs_0_), channel_id=1, source_target_pairs={{12,0},{8,4},{4,8},{0,12},{13,1},{9,5},{5,9},{1,13},{14,2},{10,6},... | collective-permute-start | bytes 135176 | tf_op jit(solution)/shard_map/ppermute | solution.py:553
  51.8 5.1 %collective-permute-start.17 = (bf16[176,128]{1,0:T(8,128)(2,1)S(1)}, bf16[176,128]{1,0:T(8,128)(2,1)S(1)}, u32[]{:S(2)}, u32[]{:S(2)}) collective-permute-start(bf16[176,128]{1,0:T(8,128)(2,1)S(1)} %shard_map.86.refs_0_), channel_id=1, source_target_pairs={{8,0},{12,4},{0,8},{4,12},{9,1},{13,5},{1,9},{5,13},{10,2},{14,6},... | collective-permute-start | bytes 135176 | tf_op jit(solution)/shard_map/ppermute | solution.py:553
  52.3 4.9 %collective-permute-start.18 = (bf16[176,128]{1,0:T(8,128)(2,1)S(1)}, bf16[176,128]{1,0:T(8,128)(2,1)S(1)}, u32[]{:S(2)}, u32[]{:S(2)}) collective-permute-start(bf16[176,128]{1,0:T(8,128)(2,1)S(1)} %shard_map.86.refs_0_), channel_id=1, source_target_pairs={{4,0},{0,4},{12,8},{8,12},{5,1},{1,5},{13,9},{9,13},{6,2},{2,6},{1... | collective-permute-start | bytes 135176 | tf_op jit(solution)/shard_map/ppermute | solution.py:553
  58.2 1.5 %collective-permute-start.19 = (f32[32,1280]{1,0:T(8,128)S(1)}, f32[32,1280]{1,0:T(8,128)S(1)}, u32[]{:S(2)}, u32[]{:S(2)}) collective-permute-start(f32[32,1280]{1,0:T(8,128)S(1)} %shard_map.88.refs_0_), channel_id=1, source_target_pairs={{0,1},{1,0},{2,3},{3,2},{4,5},{5,4},{6,7},{7,6},{8,9},{9,8},{10,11... | collective-permute-start | bytes 491528 | tf_op jit(solution)/shard_map/ppermute | solution.py:550
